TPU v7x, 32 devices: a whole 2x2x4 slice. The times are simulated.
32 devices in a mesh: seq: 8 (over z, x), req: 4 (over y, core).
Axes of the slice: x: 2, y: 2, z: 4, core: 2. Of those that a mesh axis runs over, the one named last changes fastest.
Arguments:
- tokens: bfloat16 [32, 4, 2048], P('req'), may hold values from -6 to 6
- lengths: int32 [32], P('req'), may hold values from 1 to 508, as said below
- cache_keys: bfloat16 [32, 512, 2048], P('req', 'seq'), may hold values from -120 to 120
- cache_values: bfloat16 [32, 512, 2048], P('req', 'seq'), may hold values from -6 to 6
- norm1_gain: float32 [2048], replicated, may hold values from 0.5 to 1.5
- norm1_bias: float32 [2048], replicated, may hold values from -1.75 to 1.75
- w_query: bfloat16 [2048, 2048], P('req', 'seq'), may hold values from -0.125 to 0.125
- b_query: float32 [2048], P('seq'), may hold values from -3 to 3
- w_key: bfloat16 [2048, 2048], P('req', 'seq'), may hold values from -0.125 to 0.125
- b_key: float32 [2048], P('seq'), may hold values from -3 to 3
- w_value: bfloat16 [2048, 2048], P('req', 'seq'), may hold values from -0.125 to 0.125
- b_value: float32 [2048], P('seq'), may hold values from -3 to 3
- w_out: bfloat16 [2048, 2048], P('req', 'seq'), may hold values from -0.125 to 0.125
- b_out: float32 [2048], P('seq'), may hold values from -3 to 3
- norm2_gain: float32 [2048], replicated, may hold values from 0.5 to 1.5
- norm2_bias: float32 [2048], replicated, may hold values from -1.75 to 1.75
- w_up: bfloat16 [2048, 8192], P('req', 'seq'), may hold values from -0.125 to 0.125
- b_up: float32 [8192], P('seq'), may hold values from -3 to 3
- w_down: bfloat16 [8192, 2048], P('seq', 'req'), may hold values from -0.0625 to 0.0625
- b_down: float32 [2048], replicated, may hold values from -3 to 3
Outputs:
- hidden_out: bfloat16 [32, 4, 2048], P('req')
- new_keys: bfloat16 [32, 512, 2048], P('req', 'seq')
- new_values: bfloat16 [32, 512, 2048], P('req', 'seq')
Inputs may be any that keep to these rules, and one draw needn't show every extreme that they name: `lengths`: one request has exactly 508 cached positions.
All inputs are finite; a program needn't handle non-finite values.
Results may differ from a plain program's by a relative error of at most 0.033.
Values may be sent and summed in bfloat16 or wider, within the bound.
No kernel may reach another device: no remote copies, remote signals or barrier semaphores. Data moves between devices by JAX's collectives and lax.ppermute only.
A program may use at most 64 MiB of HBM per device.

v0:
```python
import jax
import jax.numpy as jnp
from jax import lax
from jax.sharding import PartitionSpec as P

HEADS = 16
HEAD = 128


def merged(x, axis, combine):
    everything = jax.tree.map(
        lambda part, kind: lax.all_gather(part.astype(kind), axis),
        x,
        (jnp.bfloat16, jnp.bfloat16, jnp.bfloat16),
    )

    def take(k):
        return jax.tree.map(lambda part, own: part[k].astype(own.dtype), everything, x)

    return lax.fori_loop(
        1, lax.axis_size(axis), lambda k, so_far: combine(so_far, take(k)), take(0)
    )


def layer_norm(values, gain, shift):
    center = values - jnp.mean(values, axis=-1, keepdims=True)
    spread = jnp.mean(center * center, axis=-1, keepdims=True)
    return center * lax.rsqrt(spread + 1e-05) * gain + shift


def combine(first, second):
    peak_a, total_a, part_a = first
    peak_b, total_b, part_b = second
    peak = jnp.maximum(peak_a, peak_b)
    scale_a = jnp.exp(peak_a - peak)
    scale_b = jnp.exp(peak_b - peak)
    total = total_a * scale_a + total_b * scale_b
    part = part_a * scale_a[..., None] + part_b * scale_b[..., None]
    return (peak, total, part)


def body(
    tokens,
    lengths,
    cache_keys,
    cache_values,
    norm1_gain,
    norm1_bias,
    w_query,
    b_query,
    w_key,
    b_key,
    w_value,
    b_value,
    w_out,
    b_out,
    norm2_gain,
    norm2_bias,
    w_up,
    b_up,
    w_down,
    b_down,
):
    group = tokens.shape[0]
    residual = tokens.astype(jnp.float32)
    normed = layer_norm(residual, norm1_gain, norm1_bias).astype(jnp.bfloat16)
    full_query, full_key, full_value, full_out, full_up = (
        lax.all_gather(w_query, "req", axis=0, tiled=True),
        lax.all_gather(w_key, "req", axis=0, tiled=True),
        lax.all_gather(w_value, "req", axis=0, tiled=True),
        lax.all_gather(w_out, "req", axis=0, tiled=True),
        lax.all_gather(w_up, "req", axis=0, tiled=True),
    )
    query_cols = (jnp.dot(normed, full_query, preferred_element_type=jnp.float32) + b_query).astype(
        jnp.bfloat16
    )
    key_cols = (jnp.dot(normed, full_key, preferred_element_type=jnp.float32) + b_key).astype(
        jnp.bfloat16
    )
    value_cols = (jnp.dot(normed, full_value, preferred_element_type=jnp.float32) + b_value).astype(
        jnp.bfloat16
    )
    query, key_rows, value_rows = (
        lax.all_gather(query_cols, "seq", axis=2, tiled=True),
        lax.all_gather(key_cols, "seq", axis=2, tiled=True),
        lax.all_gather(value_cols, "seq", axis=2, tiled=True),
    )
    steps, width = (query.shape[1], query.shape[2])
    slots = cache_keys.shape[1]
    position = lax.axis_index("seq") * slots + jnp.arange(slots, dtype=jnp.int32)
    new_keys = cache_keys
    new_values = cache_values
    for step in range(steps):
        hit = (position[None, :] == lengths[:, None] + step)[:, :, None]
        new_keys = jnp.where(hit, key_rows[:, step][:, None, :], new_keys)
        new_values = jnp.where(hit, value_rows[:, step][:, None, :], new_values)
    query_heads = query.reshape(group, steps, HEADS, HEAD)
    key_heads = new_keys.reshape(group, slots, HEADS, HEAD)
    value_heads = new_values.reshape(group, slots, HEADS, HEAD)
    scores = jnp.einsum(
        "rthd,rshd->rths", query_heads, key_heads, preferred_element_type=jnp.float32
    ) * HEAD ** (-0.5)
    limit = lengths[:, None] + jnp.arange(steps, dtype=jnp.int32)[None, :]
    valid = position[None, None, None, :] <= limit[:, :, None, None]
    masked = jnp.where(valid, scores, -1e30)
    peak = jnp.max(masked, axis=-1)
    expo = jnp.where(valid, jnp.exp(masked - peak[..., None]), 0.0)
    total = jnp.sum(expo, axis=-1)
    partial_value = jnp.einsum(
        "rths,rshd->rthd",
        expo.astype(jnp.bfloat16),
        value_heads,
        preferred_element_type=jnp.float32,
    )
    peak, total, partial_value = merged((peak, total, partial_value), "seq", combine)
    attn = (partial_value / total[..., None]).reshape(group, steps, width).astype(jnp.bfloat16)
    out_part = (jnp.dot(attn, full_out, preferred_element_type=jnp.float32) + b_out).astype(
        jnp.bfloat16
    )
    projected = lax.all_gather(out_part, "seq", axis=2, tiled=True)
    mid = residual + projected.astype(jnp.float32)
    normed2 = layer_norm(mid, norm2_gain, norm2_bias).astype(jnp.bfloat16)
    hidden = jax.nn.gelu(
        jnp.dot(normed2, full_up, preferred_element_type=jnp.float32) + b_up, approximate=False
    ).astype(jnp.bfloat16)
    feed = jnp.dot(
        hidden,
        lax.all_gather(w_down, "req", axis=1, tiled=True),
        preferred_element_type=jnp.float32,
    )
    summed = lax.psum(feed.astype(jnp.bfloat16), "seq").astype(jnp.float32)
    hidden_out = (mid + summed + b_down).astype(jnp.bfloat16)
    return (hidden_out, new_keys, new_values)


def solution(mesh):
    in_specs = (
        P("req", None, None),
        P("req"),
        P("req", "seq", None),
        P("req", "seq", None),
        P(),
        P(),
        P("req", "seq"),
        P("seq"),
        P("req", "seq"),
        P("seq"),
        P("req", "seq"),
        P("seq"),
        P("req", "seq"),
        P("seq"),
        P(),
        P(),
        P("req", "seq"),
        P("seq"),
        P("seq", "req"),
        P(),
    )
    out_specs = (P("req", None, None), P("req", "seq", None), P("req", "seq", None))
    return jax.shard_map(body, mesh=mesh, in_specs=in_specs, out_specs=out_specs, check_vma=False)
```

profile of v0, /device:TPU:0, one launch (start us, length us, event | category | flops | bytes accessed | tf_op | source)
XLA Modules:
  0.0 343.2 jit_solution(5678637516577500098)
XLA Ops:
  10.2 0.7 iota_add_fusion
  10.9 1.0 convert_reduce_fusion
  11.9 1.1 fusion.44
  13.1 0.7 broadcast_compare_fusion.4
  13.9 15.2 %all-gather.15.cloned.1.call-done = bf16[2048,256]{1,0:T(8,128)(2,1)} async-done(((bf16[512,256]{1,0:T(8,128)(2,1)}), bf16[2048,256]{1,0:T(8,128)(2,1)}) %all-gather.15.cloned.1.call-update) | async-done | bytes 1048592 | tf_op jit(solution)/shard_map/all_gather | solution.py:70
  29.1 1.7 fusion.36
  30.8 30.7 %all_gather.51 = bf16[8,4,2048]{2,0,1:T(8,128)(2,1)S(1)} all-gather(bf16[8,4,256]{2,0,1:T(8,128)(2,1)S(1)} %fusion.72), channel_id=1, replica_groups=mesh['seq'=8,'req'=4] {'seq'}, dimensions={2}, use_global_device_ids=true | all-gather | bytes 147456 | tf_op jit(solution)/shard_map/all_gather | solution.py:86
  61.6 1.6 fusion.40
  63.2 30.5 %all_gather.45 = bf16[8,4,2048]{2,0,1:T(8,128)(2,1)S(1)} all-gather(bf16[8,4,256]{2,0,1:T(8,128)(2,1)S(1)} %fusion.74), channel_id=1, replica_groups=mesh['seq'=8,'req'=4] {'seq'}, dimensions={2}, use_global_device_ids=true | all-gather | bytes 147456 | tf_op jit(solution)/shard_map/all_gather | solution.py:85
  93.8 1.6 fusion.38
  95.4 30.5 %all_gather.47 = bf16[8,4,2048]{2,0,1:T(8,128)(2,1)S(1)} all-gather(bf16[8,4,256]{2,0,1:T(8,128)(2,1)S(1)} %fusion.73), channel_id=1, replica_groups=mesh['seq'=8,'req'=4] {'seq'}, dimensions={2}, use_global_device_ids=true | all-gather | bytes 147456 | tf_op jit(solution)/shard_map/all_gather | solution.py:84
  125.9 2.7 select_select_fusion
  128.6 1.3 fusion.80
  129.9 0.7 fusion.31
  134.0 30.6 %all-gather.1 = bf16[64,4,16]{2,1,0:T(4,128)(2,1)S(1)} all-gather(bf16[8,4,16]{2,1,0:T(4,128)(2,1)S(1)} %copy.48), channel_id=3, replica_groups=mesh['seq'=8,'req'=4] {'seq'}, dimensions={0}, use_global_device_ids=true | all-gather | bytes 9216 | tf_op jit(solution)/shard_map/all_gather | solution.py:12
  164.6 30.5 %all-gather = bf16[64,4,16]{2,1,0:T(4,128)(2,1)S(1)} all-gather(bf16[8,4,16]{2,1,0:T(4,128)(2,1)S(1)} %copy.46), channel_id=2, replica_groups=mesh['seq'=8,'req'=4] {'seq'}, dimensions={0}, use_global_device_ids=true | all-gather | bytes 9216 | tf_op jit(solution)/shard_map/all_gather | solution.py:12
  195.2 0.9 slice_convert_fusion
  196.1 8.8 %while.19 = (s32[]{:T(128)}, f32[8,4,16]{2,1,0:T(4,128)S(1)}, f32[8,4,16]{2,1,0:T(4,128)S(1)}, f32[8,4,16,128]{3,2,1,0:T(8,128)S(1)}, bf16[8,8,4,16]{3,2,1,0:T(4...) while((s32[]{:T(128)}, f32[8,4,16]{2,1,0:T(4,128)S(1)}, ...), condition=%wide.region_5.6_spmd, body=%wide.region_4.5_spmd.sunk | while | flops 266245 | bytes 673943 | solution.py:20
  196.2 1.2 fusion.87
  197.4 1.2 fusion.87
  198.7 1.2 fusion.87
  200.0 1.2 fusion.87
  201.3 1.2 fusion.87
  202.5 1.2 fusion.87
  203.7 1.2 fusion.87
  205.2 1.5 fusion.34
  206.7 26.1 %all_gather.55 = bf16[8,4,2048]{2,1,0:T(4,128)(2,1)S(1)} all-gather(bf16[8,4,256]{2,1,0:T(4,128)(2,1)S(1)} %fusion.34), channel_id=1, replica_groups=mesh['seq'=8,'req'=4] {'seq'}, dimensions={2}, use_global_device_ids=true | all-gather | bytes 147456 | tf_op jit(solution)/shard_map/all_gather | solution.py:120
  233.5 3.8 %fusion.54 = bf16[8,4,1024]{2,0,1:T(8,128)(2,1)S(1)} fusion(bf16[2048,1024]{1,0:T(8,128)(2,1)} %all-gather.19.cloned.1.call-done, bf16[8,4,2048]{2,1,0:T(4,128)(2,1)S(1)} %add_convert_fusion.1, f32[1024]{0:T(1024)S(1)} %copy-done.12), kind=kOutput, calls=%fused_computation.56 | convolution fusion | flops 136380416 | bytes 4395008 | tf_op jit(solution)/shard_map/dot_general | solution.py:124
  237.2 23.8 %all-gather.21.cloned.1.call-done = bf16[1024,2048]{1,0:T(8,128)(2,1)} async-done(((bf16[1024,512]{1,0:T(8,128)(2,1)}), bf16[1024,2048]{1,0:T(8,128)(2,1)}) %all-gather.21.cloned.1.call-update) | async-done | bytes 4194320 | tf_op jit(solution)/shard_map/all_gather | solution.py:128
  261.0 3.6 %fusion.7 = bf16[8,4,2048]{2,1,0:T(4,128)(2,1)} fusion(bf16[1024,2048]{1,0:T(8,128)(2,1)} %all-gather.21.cloned.1.call-done, bf16[8,4,1024]{2,0,1:T(8,128)(2,1)S(1)} %fusion.54), kind=kOutput, calls=%fused_computation.12 | convolution fusion | flops 134283264 | bytes 4390912 | tf_op jit(solution)/shard_map/dot_general | solution.py:126
  264.7 70.0 %all-reduce.2.cloned.1.call-done = bf16[8,4,2048]{2,1,0:T(4,128)(2,1)} async-done(((bf16[8,4,2048]{2,1,0:T(4,128)(2,1)}), bf16[8,4,2048]{2,1,0:T(4,128)(2,1)}) %all-reduce.2.cloned.1.call-update) | async-done | bytes 131088 | tf_op jit(solution)/shard_map/psum | solution.py:131
  334.7 1.7 add_convert_fusion
  (81 shorter events, 7.6 us)
Async XLA Ops:
  7.2 54.4 %copy-start = (bf16[8,4,2048]{2,1,0:T(4,128)(2,1)S(1)}, bf16[8,4,2048]{2,1,0:T(4,128)(2,1)}, u32[]{:S(2)}) copy-start(bf16[8,4,2048]{2,1,0:T(4,128)(2,1)} %param.22) | copy-start | bytes 393220
  7.2 54.4 %copy-start.11 = (f32[2048]{0:T(1024)S(1)}, f32[2048]{0:T(1024)}, u32[]{:S(2)}) copy-start(f32[2048]{0:T(1024)} %param.26) | copy-start | bytes 24580
  7.2 54.4 %copy-start.10 = (f32[2048]{0:T(1024)S(1)}, f32[2048]{0:T(1024)}, u32[]{:S(2)}) copy-start(f32[2048]{0:T(1024)} %param.27) | copy-start | bytes 24580
  7.2 23.6 %copy-start.7 = (f32[256]{0:T(256)S(1)}, f32[256]{0:T(256)}, u32[]{:S(2)}) copy-start(f32[256]{0:T(256)} %param.33) | copy-start | bytes 3076
  7.2 55.9 %copy-start.8 = (f32[256]{0:T(256)S(1)}, f32[256]{0:T(256)}, u32[]{:S(2)}) copy-start(f32[256]{0:T(256)} %param.31) | copy-start | bytes 3076
  7.2 21.9 %all-gather.15.cloned.1.call-start = ((), (), s32[]{:S(2)}) async-start(), calls=%async_computation.2 | async-start | bytes 1310720 | tf_op jit(solution)/shard_map/all_gather | solution.py:70
  8.0 53.6 %all-gather.11.cloned.1.call-start = ((), (), s32[]{:S(2)}) async-start(), calls=%async_computation | async-start | bytes 1310720 | tf_op jit(solution)/shard_map/all_gather | solution.py:69
  8.7 85.0 %all-gather.13.cloned.1.call-start = ((), (), s32[]{:S(2)}) async-start(), calls=%async_computation.1 | async-start | bytes 1310720 | tf_op jit(solution)/shard_map/all_gather | solution.py:68
  9.4 185.7 %all-gather.23.cloned.1.call-start = ((), (), s32[]{:S(2)}) async-start(), calls=%async_computation.7 | async-start | bytes 1179648 | tf_op jit(solution)/shard_map/all_gather | solution.py:12
  30.8 64.6 %copy-start.9 = (f32[256]{0:T(256)S(1)}, f32[256]{0:T(256)}, u32[]{:S(2)}) copy-start(f32[256]{0:T(256)} %param.29) | copy-start | bytes 3076
  30.8 95.1 %copy-start.1 = (bf16[8,64,2048]{2,1,0:T(8,128)(2,1)S(1)}, bf16[8,64,2048]{2,1,0:T(8,128)(2,1)}, u32[]{:S(2)}) copy-start(bf16[8,64,2048]{2,1,0:T(8,128)(2,1)} %param.25) | copy-start | bytes 6291460
  128.6 2.0 copy-start.2
  128.6 2.0 copy-start.3
  131.3 73.8 %all-gather.17.cloned.1.call-start = ((), (), s32[]{:S(2)}) async-start(), calls=%async_computation.3 | async-start | bytes 1310720 | tf_op jit(solution)/shard_map/all_gather | solution.py:71
  131.9 101.5 %all-gather.19.cloned.1.call-start = ((), (), s32[]{:S(2)}) async-start(), calls=%async_computation.4 | async-start | bytes 5242880 | tf_op jit(solution)/shard_map/all_gather | solution.py:72
  132.5 128.5 %all-gather.21.cloned.1.call-start = ((), (), s32[]{:S(2)}) async-start(), calls=%async_computation.5 | async-start | bytes 5242880 | tf_op jit(solution)/shard_map/all_gather | solution.py:128
  133.3 201.4 %all-reduce.2.cloned.1.call-start = ((), (), s32[]{:S(2)}) async-start(), calls=%async_computation.6 | async-start | bytes 262144 | tf_op jit(solution)/shard_map/psum | solution.py:131
  196.1 9.0 %copy-start.13 = (f32[256]{0:T(256)S(1)}, f32[256]{0:T(256)}, u32[]{:S(2)}) copy-start(f32[256]{0:T(256)} %param.35) | copy-start | bytes 3076
  204.9 28.3 %copy-start.5 = (f32[2048]{0:T(1024)S(1)}, f32[2048]{0:T(1024)}, u32[]{:S(2)}) copy-start(f32[2048]{0:T(1024)} %param.37) | copy-start | bytes 24580
  204.9 28.3 %copy-start.6 = (f32[2048]{0:T(1024)S(1)}, f32[2048]{0:T(1024)}, u32[]{:S(2)}) copy-start(f32[2048]{0:T(1024)} %param.36) | copy-start | bytes 24580
  204.9 28.5 %copy-start.12 = (f32[1024]{0:T(1024)S(1)}, f32[1024]{0:T(1024)}, u32[]{:S(2)}) copy-start(f32[1024]{0:T(1024)} %param.39) | copy-start | bytes 12292
  237.2 97.5 %copy-start.4 = (f32[2048]{0:T(1024)S(1)}, f32[2048]{0:T(1024)}, u32[]{:S(2)}) copy-start(f32[2048]{0:T(1024)} %param.41) | copy-start | bytes 24580
Sparse Core Ops, SparseCore 0:
  9.6 19.4 all-gather.14
  30.6 16.7 all-gather.10
  49.0 16.7 all-gather.12
  131.5 40.6 all-gather.22
  173.5 15.3 all-gather.16
  190.4 34.5 all-gather.18
  226.5 34.4 all-gather.20
  264.9 69.6 all-reduce.1
where the time goes:
time: 344 us; the launch traced here: 343 us
  blocking collectives  179 us (52%)
  waiting for transfers between devices  113 us (33%)
  other arithmetic  19.5 us (6%)
  matrix products  15.7 us (5%)
  between operations  14.5 us (4%)
    psum x1, waiting for transfers between devices, body(): summed = lax.psum(feed.astype(jnp.bfloat16), 'seq').astype(jnp.float32)  70 us
    all_gather x2, blocking collectives, merged(): lax.all_gather(part.astype(kind), axis)  61.1 us
    all_gather x1, blocking collectives, body(): lax.all_gather(value_cols, 'seq', axis=2, tiled=True)  30.7 us
    all_gather x1, blocking collectives, body(): lax.all_gather(key_cols, 'seq', axis=2, tiled=True)  30.5 us
    all_gather x1, blocking collectives, body(): lax.all_gather(query_cols, 'seq', axis=2, tiled=True)  30.5 us
    all_gather x1, blocking collectives, body(): projected = lax.all_gather(out_part, 'seq', axis=2, tiled=True)  26.1 us
    all_gather x1, waiting for transfers between devices, body(): lax.all_gather(w_down, 'req', axis=1, tiled=True)  23.8 us
    all_gather x1, waiting for transfers between devices, body(): lax.all_gather(w_value, 'req', axis=0, tiled=True)  15.2 us
  transfers between devices with their start and end apart: 8, of which 3 were waited for; matrix products, arithmetic and copies ran while one was open for 7% of the time, Pallas kernels for 0%

commit v1 on v0

v1 whole, which is shorter than its diff:
```python
import jax
import jax.numpy as jnp
from jax import lax
from jax.sharding import PartitionSpec as P

HEAD = 128
BF16 = jnp.bfloat16
F32 = jnp.float32


def layer_norm(values, gain, shift):
    center = values - jnp.mean(values, axis=-1, keepdims=True)
    spread = jnp.mean(center * center, axis=-1, keepdims=True)
    return center * lax.rsqrt(spread + 1e-05) * gain + shift


def gather_blocks(x, axis):
    n = lax.axis_size(axis)
    me = lax.axis_index(axis)
    parts = [x]
    for k in range(1, n):
        parts.append(lax.ppermute(x, axis, [(i, (i - k) % n) for i in range(n)]))
    stacked = jnp.stack(parts)
    return jnp.roll(stacked, me, axis=0)


def columns(blocks):
    n, rows, c = blocks.shape
    return blocks.transpose(1, 0, 2).reshape(rows, n * c)


def swap(x, axis):
    return lax.all_to_all(x, axis, 0, 0, tiled=False)


def project(x, weight):
    parts = lax.axis_size("req")
    rows, depth = x.shape
    sent = x.reshape(rows, parts, depth // parts).transpose(1, 0, 2)
    mine = swap(sent, "req").reshape(parts * rows, depth // parts)
    partial = jnp.dot(mine, weight, preferred_element_type=F32)
    back = swap(partial.reshape(parts, rows, weight.shape[1]), "req")
    return jnp.sum(back, axis=0)


def body(
    tokens,
    lengths,
    cache_keys,
    cache_values,
    norm1_gain,
    norm1_bias,
    w_query,
    b_query,
    w_key,
    b_key,
    w_value,
    b_value,
    w_out,
    b_out,
    norm2_gain,
    norm2_bias,
    w_up,
    b_up,
    w_down,
    b_down,
):
    seqs = lax.axis_size("seq")
    reqs = lax.axis_size("req")
    seq = lax.axis_index("seq")
    group, steps, width = tokens.shape
    slots = cache_keys.shape[1]
    rows = group * steps
    heads = width // HEAD
    cols = width // seqs

    residual = tokens.reshape(rows, width).astype(F32)
    normed = layer_norm(residual, norm1_gain, norm1_bias).astype(BF16)
    w_qkv = jnp.concatenate([w_query, w_key, w_value], axis=1)
    b_qkv = jnp.concatenate([b_query, b_key, b_value])
    qkv = (project(normed, w_qkv) + b_qkv).astype(BF16)
    every = gather_blocks(qkv, "seq").reshape(seqs, rows, 3, cols)
    query = columns(every[:, :, 0]).reshape(group, steps, width)
    key_rows = columns(every[:, :, 1]).reshape(group, steps, width)
    value_rows = columns(every[:, :, 2]).reshape(group, steps, width)

    position = seq * slots + jnp.arange(slots, dtype=jnp.int32)
    new_keys = cache_keys
    new_values = cache_values
    for step in range(steps):
        hit = (position[None, :] == lengths[:, None] + step)[:, :, None]
        new_keys = jnp.where(hit, key_rows[:, step][:, None, :], new_keys)
        new_values = jnp.where(hit, value_rows[:, step][:, None, :], new_values)
    scores = (
        jnp.einsum(
            "rthd,rshd->rths",
            query.reshape(group, steps, heads, HEAD),
            new_keys.reshape(group, slots, heads, HEAD),
            preferred_element_type=F32,
        )
        * HEAD ** (-0.5)
    )
    limit = lengths[:, None] + jnp.arange(steps, dtype=jnp.int32)[None, :]
    valid = position[None, None, None, :] <= limit[:, :, None, None]
    masked = jnp.where(valid, scores, -1e30)
    peak = jnp.max(masked, axis=-1)
    expo = jnp.where(valid, jnp.exp(masked - peak[..., None]), 0.0)
    total = jnp.sum(expo, axis=-1)
    part = jnp.einsum(
        "rths,rshd->rthd",
        expo.astype(BF16),
        new_values.reshape(group, slots, heads, HEAD),
        preferred_element_type=F32,
    )
    stats = jnp.concatenate([peak, total], axis=-1).reshape(rows, 2 * heads)
    stats = jnp.pad(stats, ((0, 0), (0, HEAD - 2 * heads)))
    blocks = part.reshape(rows, seqs, cols).transpose(1, 0, 2)
    message = jnp.concatenate([blocks, jnp.broadcast_to(stats[None], (seqs, rows, HEAD))], axis=-1)
    got = swap(message, "seq")
    peaks = got[:, :, cols : cols + heads]
    totals = got[:, :, cols + heads : cols + 2 * heads]
    scale = jnp.exp(peaks - jnp.max(peaks, axis=0, keepdims=True))
    whole = jnp.sum(totals * scale, axis=0)
    factor = scale / whole
    head_of = (seq * cols + jnp.arange(cols)) // HEAD
    attn = jnp.sum(got[:, :, :cols] * jnp.take(factor, head_of, axis=2), axis=0).astype(BF16)

    attn = columns(gather_blocks(attn, "seq"))
    out_part = (project(attn, w_out) + b_out).astype(BF16)
    projected = columns(gather_blocks(out_part, "seq"))
    mid = residual + projected.astype(F32)
    normed2 = layer_norm(mid, norm2_gain, norm2_bias).astype(BF16)
    hidden = jax.nn.gelu(project(normed2, w_up) + b_up, approximate=False).astype(BF16)

    everyone = gather_blocks(hidden, "req").reshape(reqs * rows, hidden.shape[1])
    feed = jnp.dot(everyone, w_down, preferred_element_type=F32)
    ncols = feed.shape[1]
    share = rows * reqs // seqs
    own = jnp.sum(swap(feed.reshape(seqs, share, ncols), "seq"), axis=0).astype(BF16)
    pieces = lax.all_gather(own, "req")
    full = pieces.transpose(1, 0, 2).reshape(share, width)
    spread = gather_blocks(full, "seq").reshape(reqs, rows, width)
    summed = lax.dynamic_index_in_dim(spread, lax.axis_index("req"), 0, keepdims=False)
    out = (mid + summed.astype(F32) + b_down).astype(BF16)
    return (out.reshape(group, steps, width), new_keys, new_values)


def solution(mesh):
    in_specs = (
        P("req", None, None),
        P("req"),
        P("req", "seq", None),
        P("req", "seq", None),
        P(),
        P(),
        P("req", "seq"),
        P("seq"),
        P("req", "seq"),
        P("seq"),
        P("req", "seq"),
        P("seq"),
        P("req", "seq"),
        P("seq"),
        P(),
        P(),
        P("req", "seq"),
        P("seq"),
        P("seq", "req"),
        P(),
    )
    out_specs = (P("req", None, None), P("req", "seq", None), P("req", "seq", None))
    return jax.shard_map(body, mesh=mesh, in_specs=in_specs, out_specs=out_specs, check_vma=False)
```

time: 344 us -> 215 us (0.62)
  blocking collectives: 179 us -> 19.3 us
  starting transfers between devices: 0.31 us -> 86 us
  waiting for transfers between devices: 113 us -> 66.8 us
  local copies, waits for them, and re-layouts: 1.08 us -> 18 us
  between operations: 14.5 us -> 1.7 us
  matrix products: 15.7 us -> 7.1 us
  other arithmetic: 19.5 us -> 13.5 us
    all_gather x6 -> x1, blocking collectives: 179 us -> 5.25 us  [body(): pieces = lax.all_gather(own, 'req')]
    psum x1 -> x0, waiting for transfers between devices: 70 us -> none  [body(): summed = lax.psum(feed.astype(jnp.bfloat16), 'seq').astype(jnp.float32)]
    ppermute x0 -> x31, starting transfers between devices: none -> 54.4 us  [gather_blocks(): parts.append(lax.ppermute(x, axis, [(i, (i - k) % n) for i in range(n)]))]
    all_to_all x0 -> x6, waiting for transfers between devices: none -> 40.1 us  [swap(): return lax.all_to_all(x, axis, 0, 0, tiled=False)]
    all_gather x7 -> x0, waiting for transfers between devices: 39.1 us -> none  [the longest x1 23.8 us: body(): lax.all_gather(w_down, 'req', axis=1, tiled=True)]
    all_to_all x0 -> x6, starting transfers between devices: none -> 31.6 us  [swap(): return lax.all_to_all(x, axis, 0, 0, tiled=False)]
    ppermute x0 -> x31, waiting for transfers between devices: none -> 26.6 us  [gather_blocks(): parts.append(lax.ppermute(x, axis, [(i, (i - k) % n) for i in range(n)]))]
    all_to_all x0 -> x2, blocking collectives: none -> 14 us  [swap(): return lax.all_to_all(x, axis, 0, 0, tiled=False)]
  transfers between devices with their start and end apart: 8 -> 37, of which waited for: 3 -> 20; matrix products, arithmetic and copies ran while one was open for 7% -> 2% of each run, Pallas kernels for 0% -> 0%
where the time goes in v1:
time: 215 us; the launch traced here: 212 us
  starting transfers between devices  86 us (40%)
  waiting for transfers between devices  66.8 us (31%)
  blocking collectives  19.3 us (9%)
  local copies, waits for them, and re-layouts  18 us (8%)
  other arithmetic  13.5 us (6%)
  matrix products  7.1 us (3%)
    ppermute x31, starting transfers between devices, gather_blocks(): parts.append(lax.ppermute(x, axis, [(i, (i - k) % n) for i in range(n)]))  54.4 us
    all_to_all x6, waiting for transfers between devices, swap(): return lax.all_to_all(x, axis, 0, 0, tiled=False)  40.1 us
    all_to_all x6, starting transfers between devices, swap(): return lax.all_to_all(x, axis, 0, 0, tiled=False)  31.6 us
    ppermute x31, waiting for transfers between devices, gather_blocks(): parts.append(lax.ppermute(x, axis, [(i, (i - k) % n) for i in range(n)]))  26.6 us
    all_to_all x2, blocking collectives, swap(): return lax.all_to_all(x, axis, 0, 0, tiled=False)  14 us
    all_gather x1, blocking collectives, body(): pieces = lax.all_gather(own, 'req')  5.25 us
  transfers between devices with their start and end apart: 37, of which 20 were waited for; matrix products, arithmetic and copies ran while one was open for 2% of the time, Pallas kernels for 0%

profile of v1, /device:TPU:0, one launch (start us, length us, event | category | flops | bytes accessed | tf_op | source)
XLA Modules:
  0.0 212.2 jit_solution(11938823178978505291)
XLA Ops:
  6.3 4.2 %all-to-all-start = ((bf16[4,32,512]{2,1,0:T(8,128)(2,1)}), bf16[4,32,512]{2,1,0:T(8,128)(2,1)S(1)}, u32[]{:S(2)}, u32[]{:S(2)}) async-start(bf16[4,32,512]{2,1,0:T(8,128)(2,1)} %fusion.46), calls=%async_computation | async-start | bytes 262144 | tf_op jit(solution)/shard_map/all_to_all | solution.py:33
  15.2 2.1 %fusion.25 = f32[4,32,768]{2,1,0:T(8,128)} fusion(bf16[4,32,512]{2,1,0:T(8,128)(2,1)S(1)} %all-to-all-done, bf16[512,256]{1,0:T(8,128)(2,1)} %param.32, bf16[512,256]{1,0:T(8,128)(2,1)} %param.30, bf16[512,256]{1,0:T(8,128)(2,1)} %param.28), kind=kOutput, calls=%fused_computation.22 | convolution fusion | flops 103022592 | bytes 1310720 | tf_op jit(solution)/shard_map/dot_general | solution.py:41
  17.3 3.5 %all-to-all-start.1 = ((f32[4,32,768]{2,1,0:T(8,128)}), f32[4,32,768]{2,1,0:T(8,128)S(1)}, u32[]{:S(2)}, u32[]{:S(2)}) async-start(f32[4,32,768]{2,1,0:T(8,128)} %fusion.25), calls=%async_computation.1 | async-start | bytes 786432 | tf_op jit(solution)/shard_map/all_to_all | solution.py:33
  20.9 7.3 %all-to-all-done.1 = f32[4,32,768]{2,1,0:T(8,128)S(1)} async-done(((f32[4,32,768]{2,1,0:T(8,128)}), f32[4,32,768]{2,1,0:T(8,128)S(1)}, u32[]{:S(2)}, u32[]{:S(2)}) %all-to-all-start.1) | async-done | bytes 393248 | tf_op jit(solution)/shard_map/all_to_all | solution.py:33
  31.9 2.6 %collective-permute-start.4 = (bf16[32,768]{1,0:T(8,128)(2,1)S(1)}, bf16[32,768]{1,0:T(8,128)(2,1)S(1)}, u32[]{:S(2)}, u32[]{:S(2)}) collective-permute-start(bf16[32,768]{1,0:T(8,128)(2,1)S(1)} %add_convert_fusion.2), channel_id=1, source_target_pairs={{0,12},{4,16},{8,20},{12,24},{16,28},{20,0},{24,4},{28,8},{1,13},{... | collective-permute-start | bytes 147464 | tf_op jit(solution)/shard_map/ppermute | solution.py:22
  35.7 2.3 %collective-permute-start = (bf16[32,768]{1,0:T(8,128)(2,1)S(1)}, bf16[32,768]{1,0:T(8,128)(2,1)S(1)}, u32[]{:S(2)}, u32[]{:S(2)}) collective-permute-start(bf16[32,768]{1,0:T(8,128)(2,1)S(1)} %add_convert_fusion.2), channel_id=1, source_target_pairs={{0,28},{4,0},{8,4},{12,8},{16,12},{20,16},{24,20},{28,24},{1,29},{... | collective-permute-start | bytes 147464 | tf_op jit(solution)/shard_map/ppermute | solution.py:22
  41.5 2.5 %collective-permute-done.1 = bf16[32,768]{1,0:T(8,128)(2,1)S(1)} collective-permute-done((bf16[32,768]{1,0:T(8,128)(2,1)S(1)}, bf16[32,768]{1,0:T(8,128)(2,1)S(1)}, u32[]{:S(2)}, u32[]{:S(2)}) %collective-permute-start.1) | collective-permute-done | bytes 49184 | tf_op jit(solution)/shard_map/ppermute | solution.py:22
  44.0 3.5 %collective-permute-start.2 = (bf16[32,768]{1,0:T(8,128)(2,1)S(1)}, bf16[32,768]{1,0:T(8,128)(2,1)S(1)}, u32[]{:S(2)}, u32[]{:S(2)}) collective-permute-start(bf16[32,768]{1,0:T(8,128)(2,1)S(1)} %add_convert_fusion.2), channel_id=1, source_target_pairs={{0,20},{4,24},{8,28},{12,0},{16,4},{20,8},{24,12},{28,16},{1,21},{... | collective-permute-start | bytes 147464 | tf_op jit(solution)/shard_map/ppermute | solution.py:22
  59.6 2.8 %select_select_fusion.1 = (bf16[8,64,2048]{2,1,0:T(8,128)(2,1)S(1)}, bf16[8,64,2048]{2,1,0:T(8,128)(2,1)S(1)}) fusion(bf16[8,64,2048]{2,1,0:T(8,128)(2,1)S(1)} %copy-done.2, pred[8,64]{1,0:T(8,128)(4,1)} %get-tuple-element.23, pred[8,64]{1,0:T(8,128)(4,1)S(1)} %get-tuple-element.22, pred[8,64]{1,0:T(8,128)(4,1)S(1)} %get-tuple-element.21, ...), kind=kLoop, calls=%fused_computation.9 | loop fusion | flops 8388608 | bytes 8652800 | tf_op jit(solution)/shard_map/jit(_where)/select_n | solution.py:93
  65.9 8.5 %all-to-all-start.2 = ((f32[8,32,384]{2,1,0:T(8,128)}), f32[8,32,384]{2,1,0:T(8,128)S(1)}, u32[]{:S(2)}, u32[]{:S(2)}) async-start(f32[8,32,384]{2,1,0:T(8,128)} %pad_maximum_fusion), calls=%async_computation.2 | async-start | bytes 786432 | tf_op jit(solution)/shard_map/all_to_all | solution.py:33
  74.5 9.2 %all-to-all-done.2 = f32[8,32,384]{2,1,0:T(8,128)S(1)} async-done(((f32[8,32,384]{2,1,0:T(8,128)}), f32[8,32,384]{2,1,0:T(8,128)S(1)}, u32[]{:S(2)}, u32[]{:S(2)}) %all-to-all-start.2) | async-done | bytes 393248 | tf_op jit(solution)/shard_map/all_to_all | solution.py:33
  87.8 3.8 %collective-permute-start.10 = (bf16[32,256]{0,1:T(8,128)(2,1)S(1)}, bf16[32,256]{0,1:T(8,128)(2,1)S(1)}, u32[]{:S(2)}, u32[]{:S(2)}) collective-permute-start(bf16[32,256]{0,1:T(8,128)(2,1)S(1)} %fusion.24), channel_id=1, source_target_pairs={{0,16},{4,20},{8,24},{12,28},{16,0},{20,4},{24,8},{28,12},{1,17},{... | collective-permute-start | bytes 49160 | tf_op jit(solution)/shard_map/ppermute | solution.py:22
  91.7 2.7 %collective-permute-start.8 = (bf16[32,256]{0,1:T(8,128)(2,1)S(1)}, bf16[32,256]{0,1:T(8,128)(2,1)S(1)}, u32[]{:S(2)}, u32[]{:S(2)}) collective-permute-start(bf16[32,256]{0,1:T(8,128)(2,1)S(1)} %fusion.24), channel_id=1, source_target_pairs={{0,24},{4,28},{8,0},{12,4},{16,8},{20,12},{24,16},{28,20},{1,25},{... | collective-permute-start | bytes 49160 | tf_op jit(solution)/shard_map/ppermute | solution.py:22
  98.9 4.4 %collective-permute-done.13 = bf16[32,256]{0,1:T(8,128)(2,1)S(1)} collective-permute-done((bf16[32,256]{0,1:T(8,128)(2,1)S(1)}, bf16[32,256]{0,1:T(8,128)(2,1)S(1)}, u32[]{:S(2)}, u32[]{:S(2)}) %collective-permute-start.13) | collective-permute-done | bytes 16416 | tf_op jit(solution)/shard_map/ppermute | solution.py:22
  103.6 7.0 %all_to_all.40 = bf16[4,32,512]{2,1,0:T(8,128)(2,1)S(1)} all-to-all(bf16[4,32,512]{2,1,0:T(8,128)(2,1)S(1)} %bitcast.211), channel_id=1, replica_groups=mesh['seq'=8,'req'=4] {'req'}, dimensions={0} | all-to-all | bytes 262144 | tf_op jit(solution)/shard_map/all_to_all | solution.py:33
  111.5 3.3 %all-to-all-start.4 = ((f32[4,32,256]{2,1,0:T(8,128)}), f32[4,32,256]{2,1,0:T(8,128)S(1)}, u32[]{:S(2)}, u32[]{:S(2)}) async-start(f32[4,32,256]{2,1,0:T(8,128)} %fusion.30), calls=%async_computation.4 | async-start | bytes 262144 | tf_op jit(solution)/shard_map/all_to_all | solution.py:33
  114.9 4.6 %all-to-all-done.4 = f32[4,32,256]{2,1,0:T(8,128)S(1)} async-done(((f32[4,32,256]{2,1,0:T(8,128)}), f32[4,32,256]{2,1,0:T(8,128)S(1)}, u32[]{:S(2)}, u32[]{:S(2)}) %all-to-all-start.4) | async-done | bytes 131104 | tf_op jit(solution)/shard_map/all_to_all | solution.py:33
  121.3 3.5 %collective-permute-start.17 = (bf16[32,256]{1,0:T(8,128)(2,1)S(1)}, bf16[32,256]{1,0:T(8,128)(2,1)S(1)}, u32[]{:S(2)}, u32[]{:S(2)}) collective-permute-start(bf16[32,256]{1,0:T(8,128)(2,1)S(1)} %add_convert_fusion.3), channel_id=1, source_target_pairs={{0,16},{4,20},{8,24},{12,28},{16,0},{20,4},{24,8},{28,12},{1,17},{... | collective-permute-start | bytes 49160 | tf_op jit(solution)/shard_map/ppermute | solution.py:22
  124.8 2.4 %collective-permute-start.14 = (bf16[32,256]{1,0:T(8,128)(2,1)S(1)}, bf16[32,256]{1,0:T(8,128)(2,1)S(1)}, u32[]{:S(2)}, u32[]{:S(2)}) collective-permute-start(bf16[32,256]{1,0:T(8,128)(2,1)S(1)} %add_convert_fusion.3), channel_id=1, source_target_pairs={{0,28},{4,0},{8,4},{12,8},{16,12},{20,16},{24,20},{28,24},{1,29},{... | collective-permute-start | bytes 49160 | tf_op jit(solution)/shard_map/ppermute | solution.py:22
  128.7 2.8 %collective-permute-start.15 = (bf16[32,256]{1,0:T(8,128)(2,1)S(1)}, bf16[32,256]{1,0:T(8,128)(2,1)S(1)}, u32[]{:S(2)}, u32[]{:S(2)}) collective-permute-start(bf16[32,256]{1,0:T(8,128)(2,1)S(1)} %add_convert_fusion.3), channel_id=1, source_target_pairs={{0,24},{4,28},{8,0},{12,4},{16,8},{20,12},{24,16},{28,20},{1,25},{... | collective-permute-start | bytes 49160 | tf_op jit(solution)/shard_map/ppermute | solution.py:22
  132.9 3.0 %collective-permute-start.16 = (bf16[32,256]{1,0:T(8,128)(2,1)S(1)}, bf16[32,256]{1,0:T(8,128)(2,1)S(1)}, u32[]{:S(2)}, u32[]{:S(2)}) collective-permute-start(bf16[32,256]{1,0:T(8,128)(2,1)S(1)} %add_convert_fusion.3), channel_id=1, source_target_pairs={{0,20},{4,24},{8,28},{12,0},{16,4},{20,8},{24,12},{28,16},{1,21},{... | collective-permute-start | bytes 49160 | tf_op jit(solution)/shard_map/ppermute | solution.py:22
  138.9 7.0 %all_to_all.41 = bf16[4,32,512]{2,1,0:T(8,128)(2,1)S(1)} all-to-all(bf16[4,32,512]{2,1,0:T(8,128)(2,1)S(1)} %fusion.47), channel_id=1, replica_groups=mesh['seq'=8,'req'=4] {'req'}, dimensions={0} | all-to-all | bytes 262144 | tf_op jit(solution)/shard_map/all_to_all | solution.py:33
  147.1 3.6 %all-to-all-start.6 = ((f32[4,32,1024]{2,1,0:T(8,128)}), f32[4,32,1024]{2,1,0:T(8,128)S(1)}, u32[]{:S(2)}, u32[]{:S(2)}) async-start(f32[4,32,1024]{2,1,0:T(8,128)} %fusion.22), calls=%async_computation.6 | async-start | bytes 1048576 | tf_op jit(solution)/shard_map/all_to_all | solution.py:33
  150.7 8.8 %all-to-all-done.6 = f32[4,32,1024]{2,1,0:T(8,128)S(1)} async-done(((f32[4,32,1024]{2,1,0:T(8,128)}), f32[4,32,1024]{2,1,0:T(8,128)S(1)}, u32[]{:S(2)}, u32[]{:S(2)}) %all-to-all-start.6) | async-done | bytes 524320 | tf_op jit(solution)/shard_map/all_to_all | solution.py:33
  166.3 8.5 %all-to-all-start.7 = ((f32[8,16,512]{2,1,0:T(8,128)}), f32[8,16,512]{2,1,0:T(8,128)S(1)}, u32[]{:S(2)}, u32[]{:S(2)}) async-start(f32[8,16,512]{2,1,0:T(8,128)} %fusion.20), calls=%async_computation.7 | async-start | bytes 524288 | tf_op jit(solution)/shard_map/all_to_all | solution.py:33
  174.8 9.7 %all-to-all-done.7 = f32[8,16,512]{2,1,0:T(8,128)S(1)} async-done(((f32[8,16,512]{2,1,0:T(8,128)}), f32[8,16,512]{2,1,0:T(8,128)S(1)}, u32[]{:S(2)}, u32[]{:S(2)}) %all-to-all-start.7) | async-done | bytes 262176 | tf_op jit(solution)/shard_map/all_to_all | solution.py:33
  184.5 5.2 %all-gather = bf16[64,512]{1,0:T(8,128)(2,1)S(1)} all-gather(bf16[16,512]{1,0:T(8,128)(2,1)S(1)} %reduce_sum.118), channel_id=2, replica_groups=mesh['seq'=8,'req'=4] {'req'}, dimensions={0}, use_global_device_ids=true | all-gather | bytes 81920 | tf_op jit(solution)/shard_map/all_gather | solution.py:140
  192.9 3.2 %collective-permute-start.27 = (bf16[16,2048]{1,0:T(8,128)(2,1)S(1)}, bf16[16,2048]{1,0:T(8,128)(2,1)S(1)}, u32[]{:S(2)}, u32[]{:S(2)}) collective-permute-start(bf16[16,2048]{1,0:T(8,128)(2,1)S(1)} %bitcast.227), channel_id=1, source_target_pairs={{0,16},{4,20},{8,24},{12,28},{16,0},{20,4},{24,8},{28,12},{1,17},{... | collective-permute-start | bytes 196616 | tf_op jit(solution)/shard_map/ppermute | solution.py:22
  196.1 2.7 %collective-permute-start.24 = (bf16[16,2048]{1,0:T(8,128)(2,1)S(1)}, bf16[16,2048]{1,0:T(8,128)(2,1)S(1)}, u32[]{:S(2)}, u32[]{:S(2)}) collective-permute-start(bf16[16,2048]{1,0:T(8,128)(2,1)S(1)} %bitcast.228), channel_id=1, source_target_pairs={{0,28},{4,0},{8,4},{12,8},{16,12},{20,16},{24,20},{28,24},{1,29},{... | collective-permute-start | bytes 196616 | tf_op jit(solution)/shard_map/ppermute | solution.py:22
  202.3 2.7 %collective-permute-done.25 = bf16[16,2048]{1,0:T(8,128)(2,1)S(1)} collective-permute-done((bf16[16,2048]{1,0:T(8,128)(2,1)S(1)}, bf16[16,2048]{1,0:T(8,128)(2,1)S(1)}, u32[]{:S(2)}, u32[]{:S(2)}) %collective-permute-start.25) | collective-permute-done | bytes 65568 | tf_op jit(solution)/shard_map/ppermute | solution.py:22
  205.0 3.7 %collective-permute-start.26 = (bf16[16,2048]{1,0:T(8,128)(2,1)S(1)}, bf16[16,2048]{1,0:T(8,128)(2,1)S(1)}, u32[]{:S(2)}, u32[]{:S(2)}) collective-permute-start(bf16[16,2048]{1,0:T(8,128)(2,1)S(1)} %bitcast.230), channel_id=1, source_target_pairs={{0,20},{4,24},{8,28},{12,0},{16,4},{20,8},{24,12},{28,16},{1,21},{... | collective-permute-start | bytes 196616 | tf_op jit(solution)/shard_map/ppermute | solution.py:22
  208.7 2.3 %collective-permute-done.26 = bf16[16,2048]{1,0:T(8,128)(2,1)S(1)} collective-permute-done((bf16[16,2048]{1,0:T(8,128)(2,1)S(1)}, bf16[16,2048]{1,0:T(8,128)(2,1)S(1)}, u32[]{:S(2)}, u32[]{:S(2)}) %collective-permute-start.26) | collective-permute-done | bytes 65568 | tf_op jit(solution)/shard_map/ppermute | solution.py:22
  (232 shorter events, 67.1 us)
Async XLA Ops:
  6.3 8.9 %all-to-all-start = ((bf16[4,32,512]{2,1,0:T(8,128)(2,1)}), bf16[4,32,512]{2,1,0:T(8,128)(2,1)S(1)}, u32[]{:S(2)}, u32[]{:S(2)}) async-start(bf16[4,32,512]{2,1,0:T(8,128)(2,1)} %fusion.46), calls=%async_computation | async-start | bytes 262144 | tf_op jit(solution)/shard_map/all_to_all | solution.py:33
  17.3 10.9 %all-to-all-start.1 = ((f32[4,32,768]{2,1,0:T(8,128)}), f32[4,32,768]{2,1,0:T(8,128)S(1)}, u32[]{:S(2)}, u32[]{:S(2)}) async-start(f32[4,32,768]{2,1,0:T(8,128)} %fusion.25), calls=%async_computation.1 | async-start | bytes 786432 | tf_op jit(solution)/shard_map/all_to_all | solution.py:33
  28.2 21.1 %collective-permute-start.6 = (bf16[32,768]{1,0:T(8,128)(2,1)S(1)}, bf16[32,768]{1,0:T(8,128)(2,1)S(1)}, u32[]{:S(2)}, u32[]{:S(2)}) collective-permute-start(bf16[32,768]{1,0:T(8,128)(2,1)S(1)} %add_convert_fusion.2), channel_id=1, source_target_pairs={{0,4},{4,8},{8,12},{12,16},{16,20},{20,24},{24,28},{28,0},{1,5},{5... | collective-permute-start | bytes 147464 | tf_op jit(solution)/shard_map/ppermute | solution.py:22
  30.3 19.0 %collective-permute-start.5 = (bf16[32,768]{1,0:T(8,128)(2,1)S(1)}, bf16[32,768]{1,0:T(8,128)(2,1)S(1)}, u32[]{:S(2)}, u32[]{:S(2)}) collective-permute-start(bf16[32,768]{1,0:T(8,128)(2,1)S(1)} %add_convert_fusion.2), channel_id=1, source_target_pairs={{0,8},{4,12},{8,16},{12,20},{16,24},{20,28},{24,0},{28,4},{1,9},{5... | collective-permute-start | bytes 147464 | tf_op jit(solution)/shard_map/ppermute | solution.py:22
  31.9 17.4 %collective-permute-start.4 = (bf16[32,768]{1,0:T(8,128)(2,1)S(1)}, bf16[32,768]{1,0:T(8,128)(2,1)S(1)}, u32[]{:S(2)}, u32[]{:S(2)}) collective-permute-start(bf16[32,768]{1,0:T(8,128)(2,1)S(1)} %add_convert_fusion.2), channel_id=1, source_target_pairs={{0,12},{4,16},{8,20},{12,24},{16,28},{20,0},{24,4},{28,8},{1,13},{... | collective-permute-start | bytes 147464 | tf_op jit(solution)/shard_map/ppermute | solution.py:22
  34.4 14.8 %collective-permute-start.3 = (bf16[32,768]{1,0:T(8,128)(2,1)S(1)}, bf16[32,768]{1,0:T(8,128)(2,1)S(1)}, u32[]{:S(2)}, u32[]{:S(2)}) collective-permute-start(bf16[32,768]{1,0:T(8,128)(2,1)S(1)} %add_convert_fusion.2), channel_id=1, source_target_pairs={{0,16},{4,20},{8,24},{12,28},{16,0},{20,4},{24,8},{28,12},{1,17},{... | collective-permute-start | bytes 147464 | tf_op jit(solution)/shard_map/ppermute | solution.py:22
  35.7 4.3 %collective-permute-start = (bf16[32,768]{1,0:T(8,128)(2,1)S(1)}, bf16[32,768]{1,0:T(8,128)(2,1)S(1)}, u32[]{:S(2)}, u32[]{:S(2)}) collective-permute-start(bf16[32,768]{1,0:T(8,128)(2,1)S(1)} %add_convert_fusion.2), channel_id=1, source_target_pairs={{0,28},{4,0},{8,4},{12,8},{16,12},{20,16},{24,20},{28,24},{1,29},{... | collective-permute-start | bytes 147464 | tf_op jit(solution)/shard_map/ppermute | solution.py:22
  44.0 5.2 %collective-permute-start.2 = (bf16[32,768]{1,0:T(8,128)(2,1)S(1)}, bf16[32,768]{1,0:T(8,128)(2,1)S(1)}, u32[]{:S(2)}, u32[]{:S(2)}) collective-permute-start(bf16[32,768]{1,0:T(8,128)(2,1)S(1)} %add_convert_fusion.2), channel_id=1, source_target_pairs={{0,20},{4,24},{8,28},{12,0},{16,4},{20,8},{24,12},{28,16},{1,21},{... | collective-permute-start | bytes 147464 | tf_op jit(solution)/shard_map/ppermute | solution.py:22
  65.9 17.7 %all-to-all-start.2 = ((f32[8,32,384]{2,1,0:T(8,128)}), f32[8,32,384]{2,1,0:T(8,128)S(1)}, u32[]{:S(2)}, u32[]{:S(2)}) async-start(f32[8,32,384]{2,1,0:T(8,128)} %pad_maximum_fusion), calls=%async_computation.2 | async-start | bytes 786432 | tf_op jit(solution)/shard_map/all_to_all | solution.py:33
  86.6 7.8 %collective-permute-start.12 = (bf16[32,256]{0,1:T(8,128)(2,1)S(1)}, bf16[32,256]{0,1:T(8,128)(2,1)S(1)}, u32[]{:S(2)}, u32[]{:S(2)}) collective-permute-start(bf16[32,256]{0,1:T(8,128)(2,1)S(1)} %fusion.24), channel_id=1, source_target_pairs={{0,8},{4,12},{8,16},{12,20},{16,24},{20,28},{24,0},{28,4},{1,9},{5... | collective-permute-start | bytes 49160 | tf_op jit(solution)/shard_map/ppermute | solution.py:22
  86.8 9.4 %collective-permute-start.11 = (bf16[32,256]{0,1:T(8,128)(2,1)S(1)}, bf16[32,256]{0,1:T(8,128)(2,1)S(1)}, u32[]{:S(2)}, u32[]{:S(2)}) collective-permute-start(bf16[32,256]{0,1:T(8,128)(2,1)S(1)} %fusion.24), channel_id=1, source_target_pairs={{0,12},{4,16},{8,20},{12,24},{16,28},{20,0},{24,4},{28,8},{1,13},{... | collective-permute-start | bytes 49160 | tf_op jit(solution)/shard_map/ppermute | solution.py:22
  87.8 8.9 %collective-permute-start.10 = (bf16[32,256]{0,1:T(8,128)(2,1)S(1)}, bf16[32,256]{0,1:T(8,128)(2,1)S(1)}, u32[]{:S(2)}, u32[]{:S(2)}) collective-permute-start(bf16[32,256]{0,1:T(8,128)(2,1)S(1)} %fusion.24), channel_id=1, source_target_pairs={{0,16},{4,20},{8,24},{12,28},{16,0},{20,4},{24,8},{28,12},{1,17},{... | collective-permute-start | bytes 49160 | tf_op jit(solution)/shard_map/ppermute | solution.py:22
  91.7 5.2 %collective-permute-start.9 = (bf16[32,256]{0,1:T(8,128)(2,1)S(1)}, bf16[32,256]{0,1:T(8,128)(2,1)S(1)}, u32[]{:S(2)}, u32[]{:S(2)}) collective-permute-start(bf16[32,256]{0,1:T(8,128)(2,1)S(1)} %fusion.24), channel_id=1, source_target_pairs={{0,20},{4,24},{8,28},{12,0},{16,4},{20,8},{24,12},{28,16},{1,21},{... | collective-permute-start | bytes 49160 | tf_op jit(solution)/shard_map/ppermute | solution.py:22
  91.7 5.5 %collective-permute-start.8 = (bf16[32,256]{0,1:T(8,128)(2,1)S(1)}, bf16[32,256]{0,1:T(8,128)(2,1)S(1)}, u32[]{:S(2)}, u32[]{:S(2)}) collective-permute-start(bf16[32,256]{0,1:T(8,128)(2,1)S(1)} %fusion.24), channel_id=1, source_target_pairs={{0,24},{4,28},{8,0},{12,4},{16,8},{20,12},{24,16},{28,20},{1,25},{... | collective-permute-start | bytes 49160 | tf_op jit(solution)/shard_map/ppermute | solution.py:22
  94.4 4.3 %collective-permute-start.7 = (bf16[32,256]{0,1:T(8,128)(2,1)S(1)}, bf16[32,256]{0,1:T(8,128)(2,1)S(1)}, u32[]{:S(2)}, u32[]{:S(2)}) collective-permute-start(bf16[32,256]{0,1:T(8,128)(2,1)S(1)} %fusion.24), channel_id=1, source_target_pairs={{0,28},{4,0},{8,4},{12,8},{16,12},{20,16},{24,20},{28,24},{1,29},{... | collective-permute-start | bytes 49160 | tf_op jit(solution)/shard_map/ppermute | solution.py:22
  96.2 7.0 %collective-permute-start.13 = (bf16[32,256]{0,1:T(8,128)(2,1)S(1)}, bf16[32,256]{0,1:T(8,128)(2,1)S(1)}, u32[]{:S(2)}, u32[]{:S(2)}) collective-permute-start(bf16[32,256]{0,1:T(8,128)(2,1)S(1)} %fusion.24), channel_id=1, source_target_pairs={{0,4},{4,8},{8,12},{12,16},{16,20},{20,24},{24,28},{28,0},{1,5},{5... | collective-permute-start | bytes 49160 | tf_op jit(solution)/shard_map/ppermute | solution.py:22
  111.5 7.9 %all-to-all-start.4 = ((f32[4,32,256]{2,1,0:T(8,128)}), f32[4,32,256]{2,1,0:T(8,128)S(1)}, u32[]{:S(2)}, u32[]{:S(2)}) async-start(f32[4,32,256]{2,1,0:T(8,128)} %fusion.30), calls=%async_computation.4 | async-start | bytes 262144 | tf_op jit(solution)/shard_map/all_to_all | solution.py:33
  119.5 18.1 %collective-permute-start.20 = (bf16[32,256]{1,0:T(8,128)(2,1)S(1)}, bf16[32,256]{1,0:T(8,128)(2,1)S(1)}, u32[]{:S(2)}, u32[]{:S(2)}) collective-permute-start(bf16[32,256]{1,0:T(8,128)(2,1)S(1)} %add_convert_fusion.3), channel_id=1, source_target_pairs={{0,4},{4,8},{8,12},{12,16},{16,20},{20,24},{24,28},{28,0},{1,5},{5... | collective-permute-start | bytes 49160 | tf_op jit(solution)/shard_map/ppermute | solution.py:22
  119.5 18.1 %collective-permute-start.19 = (bf16[32,256]{1,0:T(8,128)(2,1)S(1)}, bf16[32,256]{1,0:T(8,128)(2,1)S(1)}, u32[]{:S(2)}, u32[]{:S(2)}) collective-permute-start(bf16[32,256]{1,0:T(8,128)(2,1)S(1)} %add_convert_fusion.3), channel_id=1, source_target_pairs={{0,8},{4,12},{8,16},{12,20},{16,24},{20,28},{24,0},{28,4},{1,9},{5... | collective-permute-start | bytes 49160 | tf_op jit(solution)/shard_map/ppermute | solution.py:22
  119.6 18.0 %collective-permute-start.18 = (bf16[32,256]{1,0:T(8,128)(2,1)S(1)}, bf16[32,256]{1,0:T(8,128)(2,1)S(1)}, u32[]{:S(2)}, u32[]{:S(2)}) collective-permute-start(bf16[32,256]{1,0:T(8,128)(2,1)S(1)} %add_convert_fusion.3), channel_id=1, source_target_pairs={{0,12},{4,16},{8,20},{12,24},{16,28},{20,0},{24,4},{28,8},{1,13},{... | collective-permute-start | bytes 49160 | tf_op jit(solution)/shard_map/ppermute | solution.py:22
  121.3 16.3 %collective-permute-start.17 = (bf16[32,256]{1,0:T(8,128)(2,1)S(1)}, bf16[32,256]{1,0:T(8,128)(2,1)S(1)}, u32[]{:S(2)}, u32[]{:S(2)}) collective-permute-start(bf16[32,256]{1,0:T(8,128)(2,1)S(1)} %add_convert_fusion.3), channel_id=1, source_target_pairs={{0,16},{4,20},{8,24},{12,28},{16,0},{20,4},{24,8},{28,12},{1,17},{... | collective-permute-start | bytes 49160 | tf_op jit(solution)/shard_map/ppermute | solution.py:22
  132.9 4.6 %collective-permute-start.16 = (bf16[32,256]{1,0:T(8,128)(2,1)S(1)}, bf16[32,256]{1,0:T(8,128)(2,1)S(1)}, u32[]{:S(2)}, u32[]{:S(2)}) collective-permute-start(bf16[32,256]{1,0:T(8,128)(2,1)S(1)} %add_convert_fusion.3), channel_id=1, source_target_pairs={{0,20},{4,24},{8,28},{12,0},{16,4},{20,8},{24,12},{28,16},{1,21},{... | collective-permute-start | bytes 49160 | tf_op jit(solution)/shard_map/ppermute | solution.py:22
  147.1 12.4 %all-to-all-start.6 = ((f32[4,32,1024]{2,1,0:T(8,128)}), f32[4,32,1024]{2,1,0:T(8,128)S(1)}, u32[]{:S(2)}, u32[]{:S(2)}) async-start(f32[4,32,1024]{2,1,0:T(8,128)} %fusion.22), calls=%async_computation.6 | async-start | bytes 1048576 | tf_op jit(solution)/shard_map/all_to_all | solution.py:33
  159.8 5.1 %collective-permute-start.23 = (bf16[32,1024]{1,0:T(8,128)(2,1)S(1)}, bf16[32,1024]{1,0:T(8,128)(2,1)S(1)}, u32[]{:S(2)}, u32[]{:S(2)}) collective-permute-start(bf16[32,1024]{1,0:T(8,128)(2,1)S(1)} %fusion.45), channel_id=1, source_target_pairs={{0,1},{1,2},{2,3},{3,0},{4,5},{5,6},{6,7},{7,4},{8,9},{9,10},{10,1... | collective-permute-start | bytes 196616 | tf_op jit(solution)/shard_map/ppermute | solution.py:22
  159.9 5.0 %collective-permute-start.22 = (bf16[32,1024]{1,0:T(8,128)(2,1)S(1)}, bf16[32,1024]{1,0:T(8,128)(2,1)S(1)}, u32[]{:S(2)}, u32[]{:S(2)}) collective-permute-start(bf16[32,1024]{1,0:T(8,128)(2,1)S(1)} %fusion.45), channel_id=1, source_target_pairs={{0,2},{1,3},{2,0},{3,1},{4,6},{5,7},{6,4},{7,5},{8,10},{9,11},{10,... | collective-permute-start | bytes 196616 | tf_op jit(solution)/shard_map/ppermute | solution.py:22
  166.3 18.2 %all-to-all-start.7 = ((f32[8,16,512]{2,1,0:T(8,128)}), f32[8,16,512]{2,1,0:T(8,128)S(1)}, u32[]{:S(2)}, u32[]{:S(2)}) async-start(f32[8,16,512]{2,1,0:T(8,128)} %fusion.20), calls=%async_computation.7 | async-start | bytes 524288 | tf_op jit(solution)/shard_map/all_to_all | solution.py:33
  189.8 21.4 %collective-permute-start.30 = (bf16[16,2048]{1,0:T(8,128)(2,1)S(1)}, bf16[16,2048]{1,0:T(8,128)(2,1)S(1)}, u32[]{:S(2)}, u32[]{:S(2)}) collective-permute-start(bf16[16,2048]{1,0:T(8,128)(2,1)S(1)} %bitcast.224), channel_id=1, source_target_pairs={{0,4},{4,8},{8,12},{12,16},{16,20},{20,24},{24,28},{28,0},{1,5},{5... | collective-permute-start | bytes 196616 | tf_op jit(solution)/shard_map/ppermute | solution.py:22
  191.2 19.9 %collective-permute-start.29 = (bf16[16,2048]{1,0:T(8,128)(2,1)S(1)}, bf16[16,2048]{1,0:T(8,128)(2,1)S(1)}, u32[]{:S(2)}, u32[]{:S(2)}) collective-permute-start(bf16[16,2048]{1,0:T(8,128)(2,1)S(1)} %bitcast.225), channel_id=1, source_target_pairs={{0,8},{4,12},{8,16},{12,20},{16,24},{20,28},{24,0},{28,4},{1,9},{5... | collective-permute-start | bytes 196616 | tf_op jit(solution)/shard_map/ppermute | solution.py:22
  191.3 19.8 %collective-permute-start.28 = (bf16[16,2048]{1,0:T(8,128)(2,1)S(1)}, bf16[16,2048]{1,0:T(8,128)(2,1)S(1)}, u32[]{:S(2)}, u32[]{:S(2)}) collective-permute-start(bf16[16,2048]{1,0:T(8,128)(2,1)S(1)} %bitcast.226), channel_id=1, source_target_pairs={{0,12},{4,16},{8,20},{12,24},{16,28},{20,0},{24,4},{28,8},{1,13},{... | collective-permute-start | bytes 196616 | tf_op jit(solution)/shard_map/ppermute | solution.py:22
  192.9 18.1 %collective-permute-start.27 = (bf16[16,2048]{1,0:T(8,128)(2,1)S(1)}, bf16[16,2048]{1,0:T(8,128)(2,1)S(1)}, u32[]{:S(2)}, u32[]{:S(2)}) collective-permute-start(bf16[16,2048]{1,0:T(8,128)(2,1)S(1)} %bitcast.227), channel_id=1, source_target_pairs={{0,16},{4,20},{8,24},{12,28},{16,0},{20,4},{24,8},{28,12},{1,17},{... | collective-permute-start | bytes 196616 | tf_op jit(solution)/shard_map/ppermute | solution.py:22
  196.1 4.6 %collective-permute-start.24 = (bf16[16,2048]{1,0:T(8,128)(2,1)S(1)}, bf16[16,2048]{1,0:T(8,128)(2,1)S(1)}, u32[]{:S(2)}, u32[]{:S(2)}) collective-permute-start(bf16[16,2048]{1,0:T(8,128)(2,1)S(1)} %bitcast.228), channel_id=1, source_target_pairs={{0,28},{4,0},{8,4},{12,8},{16,12},{20,16},{24,20},{28,24},{1,29},{... | collective-permute-start | bytes 196616 | tf_op jit(solution)/shard_map/ppermute | solution.py:22
  205.0 6.0 %collective-permute-start.26 = (bf16[16,2048]{1,0:T(8,128)(2,1)S(1)}, bf16[16,2048]{1,0:T(8,128)(2,1)S(1)}, u32[]{:S(2)}, u32[]{:S(2)}) collective-permute-start(bf16[16,2048]{1,0:T(8,128)(2,1)S(1)} %bitcast.230), channel_id=1, source_target_pairs={{0,20},{4,24},{8,28},{12,0},{16,4},{20,8},{24,12},{28,16},{1,21},{... | collective-permute-start | bytes 196616 | tf_op jit(solution)/shard_map/ppermute | solution.py:22
  (19 other events, 399.6 us)

commit v2 on v0

v2 whole, which is shorter than its diff:
```python
import functools

import jax
import jax.numpy as jnp
from jax import lax
from jax.experimental import pallas as pl
from jax.experimental.pallas import tpu as pltpu
from jax.sharding import PartitionSpec as P

HEAD = 128
LANES = 128
CORES = 2
BF16 = jnp.bfloat16
F32 = jnp.float32
VMEM = pl.BlockSpec(memory_space=pltpu.VMEM)
SMEM = pl.BlockSpec(memory_space=pltpu.SMEM)
ANY = pl.BlockSpec(memory_space=pl.ANY)


class Place:
    def __init__(self, seqs, reqs):
        self.ny = reqs // CORES
        self.nx = self.ny if seqs % self.ny == 0 else 1
        self.nz = seqs // self.nx
        self.seqs = seqs

    def x(self):
        return lax.rem(lax.axis_index("seq"), self.nx)

    def y(self):
        return lax.div(lax.axis_index("req"), CORES)

    def core(self):
        return lax.rem(lax.axis_index("req"), CORES)

    def x_before(self, dx):
        return lax.rem(self.x() + self.nx - dx, self.nx)

    def x_after(self, dx):
        return lax.rem(self.x() + dx, self.nx)

    def y_before(self, dy):
        return lax.rem(self.y() + self.ny - dy, self.ny)

    def z_before(self, dz):
        return lax.rem(lax.div(lax.axis_index("seq"), self.nx) + self.nz - dz, self.nz)

    def move(self, value, dx=0, dy=0, dc=0, dz=0):
        pairs = []
        for z in range(self.nz):
            for x in range(self.nx):
                for y in range(self.ny):
                    for c in range(CORES):
                        to_x, to_y, to_c = (x + dx) % self.nx, (y + dy) % self.ny, (c + dc) % CORES
                        to_z = (z + dz) % self.nz
                        pairs.append(
                            (
                                ((z * self.nx + x) * self.ny + y) * CORES + c,
                                ((to_z * self.nx + to_x) * self.ny + to_y) * CORES + to_c,
                            )
                        )
        return lax.ppermute(value, ("seq", "req"), pairs)

    def gather_z(self, value):
        return [value] + [self.move(value, dz=dz) for dz in range(1, self.nz)]


def layer_norm(values, gain, shift):
    center = values - jnp.mean(values, axis=-1, keepdims=True)
    spread = jnp.mean(center * center, axis=-1, keepdims=True)
    return center * lax.rsqrt(spread + 1e-05) * gain + shift


def dot(a, b):
    return jnp.dot(a, b, preferred_element_type=F32)


def at(index, size):
    return pl.ds(pl.multiple_of(index * size, size), size)


def call(kernel, name, ins, outs, in_specs=None, out_specs=None, scratch=()):
    single = not isinstance(outs, (list, tuple))
    specs = out_specs or (VMEM if single else [VMEM] * len(outs))
    return pl.pallas_call(
        kernel,
        name=name,
        out_shape=outs,
        in_specs=in_specs or [VMEM] * len(ins),
        out_specs=specs,
        scratch_shapes=list(scratch),
        compiler_params=pltpu.CompilerParams(vmem_limit_bytes=20 * 1024 * 1024),
    )(*ins)


def side_by_side(blocks, start, size):
    return jnp.concatenate(
        [blocks[x, :, start : start + size].astype(F32) for x in range(blocks.shape[0])], axis=1
    )


def two_halves(rows_by_k, own, sibling):
    depth = own.shape[0]
    req = lax.axis_index("req")
    other = req + 1 - 2 * lax.rem(req, CORES)
    return dot(rows_by_k[:, at(req, depth)], own[...]) + dot(
        rows_by_k[:, at(other, depth)], sibling[...]
    )


def qkv_kernel(place, *refs):
    ny = place.ny
    toks = refs[:ny]
    gain, shift, own, sibling, bias = refs[ny : ny + 5]
    outs = refs[ny + 5 : 2 * ny + 5]
    flat, normed = refs[2 * ny + 5 :]
    group, steps, _ = toks[0].shape
    rows = group * steps
    for j in range(ny):
        for i in range(group):
            flat[j * rows + i * steps : j * rows + (i + 1) * steps, :] = toks[j][i].astype(F32)
    normed[...] = layer_norm(flat[...], gain[...], shift[...]).astype(BF16)
    acc = two_halves(normed, own, sibling)
    for j in range(ny):
        part = acc[j * rows : (j + 1) * rows]
        if j == 0:
            part = part + bias[...]
        outs[(ny - j) % ny][...] = part.astype(BF16)


def add_columns_kernel(place, *refs):
    out = refs[-1]
    for dx in range(place.nx):
        total = refs[dx * place.ny][...].astype(F32)
        for dy in range(1, place.ny):
            total = total + refs[dx * place.ny + dy][...].astype(F32)
        out[place.x_before(dx)] = total.astype(BF16)


def split_three(value):
    first = value.astype(BF16).astype(F32)
    rest = value - first
    second = rest.astype(BF16).astype(F32)
    return first, second, rest - second


def turn(value, by):
    return pltpu.roll(value, by % LANES, 1)


def attention_kernel(place, heads, *refs):
    nx, nz = place.nx, place.nz
    gathered = refs[:nz]
    lengths, keys_in, values_in, keys_out, values_out = refs[nz : nz + 5]
    messages = refs[nz + 5 : nz + 5 + nx]
    qs, ks, vs, part, stats, flat, flat_stats, mask, keys, values, in_sems, out_sems = refs[
        nz + 5 + nx :
    ]
    group, slots, width = keys.shape
    steps = qs.shape[1]
    cols = width // place.seqs
    seq = lax.axis_index("seq")

    def copy_in(i, source, target, which):
        return pltpu.make_async_copy(source.at[i], target.at[i], in_sems.at[which, i])

    def copy_out(i, source, target, which):
        return pltpu.make_async_copy(source.at[i], target.at[i], out_sems.at[which, i])

    for i in range(group):
        copy_in(i, keys_in, keys, 0).start()
        copy_in(i, values_in, values, 1).start()
    for dz in range(nz):
        span = at(place.z_before(dz), nx * cols)
        for k, target in enumerate((qs, ks, vs)):
            block = side_by_side(gathered[dz], k * cols, cols)
            for i in range(group):
                target[i, :, span] = block[i * steps : (i + 1) * steps]
    across = steps * heads
    row_head = lax.rem(lax.broadcasted_iota(jnp.int32, (across, width), 0), heads)
    column_head = lax.div(lax.broadcasted_iota(jnp.int32, (across, width), 1), HEAD)
    mask[...] = (row_head == column_head).astype(F32)

    def one(i, carry):
        length = lengths[i]
        base = length - seq * slots
        copy_in(i, keys_in, keys, 0).wait()
        copy_in(i, values_in, values, 1).wait()

        @pl.when((base > -steps) & (base < slots))
        def _():
            slot = lax.broadcasted_iota(jnp.int32, (slots, width), 0)
            new_k = ks[i]
            new_v = vs[i]
            k = keys[i].astype(F32)
            v = values[i].astype(F32)
            for t in range(steps):
                k = jnp.where(slot == base + t, new_k[t : t + 1], k)
                v = jnp.where(slot == base + t, new_v[t : t + 1], v)
            keys[i] = k.astype(BF16)
            values[i] = v.astype(BF16)

        copy_out(i, keys, keys_out, 0).start()
        copy_out(i, values, values_out, 1).start()
        query = qs[i]
        query = jnp.broadcast_to(query[:, None, :], (steps, heads, width)).reshape(across, width)
        query = (query * mask[...]).astype(BF16)
        scores = lax.dot_general(
            query, keys[i], (((1,), (1,)), ((), ())), preferred_element_type=F32
        ) * HEAD ** (-0.5)
        position = seq * slots + lax.broadcasted_iota(jnp.int32, (across, slots), 1)
        step = lax.div(lax.broadcasted_iota(jnp.int32, (across, slots), 0), heads)
        valid = position <= length + step
        masked = jnp.where(valid, scores, -1e30)
        peak = jnp.max(masked, axis=-1, keepdims=True)
        expo = jnp.where(valid, jnp.exp(masked - peak), 0.0)
        total = jnp.sum(expo, axis=-1, keepdims=True)
        mixed = dot(expo.astype(BF16), values[i]) * mask[...]
        part[i] = jnp.sum(mixed.reshape(steps, heads, width), axis=1)
        lane = lax.broadcasted_iota(jnp.int32, (across, LANES), 1)
        head = lax.rem(lax.broadcasted_iota(jnp.int32, (across, LANES), 0), heads)
        pieces = split_three(peak) + split_three(total)[:2]
        tile = jnp.zeros((across, LANES), F32)
        for k, piece in enumerate(pieces):
            tile = jnp.where(lane == head + k * heads, piece, tile)
        stats[i] = jnp.sum(tile.reshape(steps, heads, LANES), axis=1)
        return carry

    lax.fori_loop(0, group, one, 0)
    for i in range(group):
        flat[i * steps : (i + 1) * steps, :] = part[i]
        flat_stats[i * steps : (i + 1) * steps, :] = stats[i]
    share = width // nx
    for dx in range(nx):
        to = place.x_after(dx)
        messages[dx][:, :share] = flat[:, at(to, share)].astype(BF16)
        messages[dx][:, share:] = pltpu.roll(
            flat_stats[...], lax.rem(LANES - to * (heads // nx), LANES), 1
        ).astype(BF16)
    for i in range(group):
        copy_out(i, keys, keys_out, 0).wait()
        copy_out(i, values, values_out, 1).wait()


def expand(factor, count):
    rows = factor.shape[0]
    return jnp.concatenate(
        [jnp.broadcast_to(factor[:, h : h + 1], (rows, HEAD)) for h in range(count)], axis=1
    )


def merge(messages, heads, share):
    peaks, totals = [], []
    for message in messages:
        stats = message[:, share:].astype(F32)
        peaks.append(stats + turn(stats, -heads) + turn(stats, -2 * heads))
        totals.append(turn(stats, -3 * heads) + turn(stats, -4 * heads))
    peak = functools.reduce(jnp.maximum, peaks)
    scales = [jnp.exp(p - peak) for p in peaks]
    total = sum(t * s for t, s in zip(totals, scales))
    return peak, total, scales


def merge_x_kernel(place, heads, *refs):
    share = refs[0].shape[1] - LANES
    count = share // HEAD
    out = refs[-1]
    messages = [r[...] for r in refs[:-1]]
    peak, total, scales = merge(messages, heads, share)
    out[:, :share] = sum(
        m[:, :share].astype(F32) * expand(s, count) for m, s in zip(messages, scales)
    ).astype(BF16)
    lane = lax.broadcasted_iota(jnp.int32, peak.shape, 1)
    tile = jnp.zeros_like(peak)
    for k, piece in enumerate(split_three(peak) + split_three(total)[:2]):
        tile = tile + turn(jnp.where(lane < count, piece, 0.0), k * heads)
    out[:, share:] = tile.astype(BF16)


def merge_z_kernel(place, heads, *refs):
    share = refs[0].shape[1] - LANES
    count = share // HEAD
    out = refs[-1]
    messages = [r[...] for r in refs[:-1]]
    _, total, scales = merge(messages, heads, share)
    out[...] = sum(
        m[:, :share].astype(F32) * expand(s / total, count) for m, s in zip(messages, scales)
    ).astype(BF16)


def out_kernel(place, *refs):
    nx, ny = place.nx, place.ny
    parts = refs[: nx * ny]
    own, sibling, bias, out, full = refs[nx * ny :]
    rows, share = parts[0].shape
    for dx in range(nx):
        for dy in range(ny):
            full[at(place.y_before(dy), rows), at(place.x_before(dx), share)] = parts[dx * ny + dy][...]
    first = (place.y() == 0).astype(F32)
    out[...] = (two_halves(full, own, sibling) + bias[...] * first).astype(BF16)


def up_kernel(place, *refs):
    ny, nz = place.ny, place.nz
    toks = refs[:ny]
    gathered = refs[ny : ny + nz]
    gain, shift, own, sibling, bias, out, mid_out, proj, normed, flat = refs[ny + nz :]
    group, steps, _ = toks[0].shape
    rows = group * steps
    cols = gathered[0].shape[2]
    for dz in range(nz):
        proj[:, at(place.z_before(dz), place.nx * cols)] = side_by_side(gathered[dz], 0, cols)
    for j in range(ny):
        here = at(place.y_before(j), rows)
        for i in range(group):
            flat[i * steps : (i + 1) * steps, :] = toks[j][i].astype(F32)
        mid = flat[...] + proj[here, :]
        if j == 0:
            mid_out[...] = mid
        normed[here, :] = layer_norm(mid, gain[...], shift[...]).astype(BF16)
    first = (place.y() == 0).astype(F32)
    out[...] = (two_halves(normed, own, sibling) + bias[...] * first).astype(BF16)


def down_kernel(place, *refs):
    nx, ny = place.nx, place.ny
    parts = refs[:ny]
    own, sibling = refs[ny : ny + 2]
    outs = refs[ny + 2 : ny + 2 + nx]
    feed = refs[-1]
    total = sum(p[...].astype(F32) for p in parts)
    hidden = (0.5 * total * (1.0 + lax.erf(total * 0.5**0.5))).astype(BF16)
    ncols = own.shape[1]
    feed[:, at(place.core(), ncols)] = dot(hidden, own[...])
    feed[:, at(1 - place.core(), ncols)] = dot(hidden, sibling[...])
    width = outs[0].shape[1]
    for dx in range(nx):
        outs[dx][...] = feed[:, at(place.x_after(dx), width)].astype(BF16)


def add_x_kernel(place, *refs):
    refs[-1][...] = sum(r[...].astype(F32) for r in refs[:-1]).astype(BF16)


def add_z_kernel(place, *refs):
    outs, total = refs[place.nz : -1], refs[-1]
    total[...] = sum(r[...].astype(F32) for r in refs[: place.nz])
    rows = outs[0].shape[0]
    for dy in range(place.ny):
        outs[dy][...] = total[at(lax.rem(place.y() + dy, place.ny), rows), :].astype(BF16)


def last_kernel(place, *refs):
    nx, ny = place.nx, place.ny
    parts = refs[: nx * ny]
    mid, bias, out, full = refs[nx * ny :]
    group, steps, _ = out.shape
    width = parts[0].shape[1]
    for dx in range(nx):
        for dy in range(ny):
            block = place.y_before(dy) * nx + place.x_before(dx)
            full[:, at(block, width)] = parts[dx * ny + dy][...].astype(F32)
    result = mid[...] + full[...] + bias[...]
    for i in range(group):
        out[i] = result[i * steps : (i + 1) * steps].astype(BF16)


def shape(sizes, kind=BF16):
    return jax.ShapeDtypeStruct(tuple(sizes), kind)


def body(
    tokens,
    lengths,
    cache_keys,
    cache_values,
    norm1_gain,
    norm1_bias,
    w_query,
    b_query,
    w_key,
    b_key,
    w_value,
    b_value,
    w_out,
    b_out,
    norm2_gain,
    norm2_bias,
    w_up,
    b_up,
    w_down,
    b_down,
):
    place = Place(lax.axis_size("seq"), lax.axis_size("req"))
    nx, ny = place.nx, place.ny
    group, steps, width = tokens.shape
    slots = cache_keys.shape[1]
    rows = group * steps
    heads = width // HEAD
    share = width // nx
    bind = functools.partial

    def row(vector):
        return vector.reshape(1, -1)

    def spread(by_dy):
        return [
            by_dy[dy] if dx == 0 and dy == 0 else place.move(by_dy[dy], dx, dy)
            for dx in range(nx)
            for dy in range(ny)
        ]

    toks = [tokens] + [place.move(tokens, dy=dy) for dy in range(1, ny)]
    w_qkv = jnp.concatenate([w_query, w_key, w_value], axis=1)
    w_qkv_sibling = place.move(w_qkv, dc=1)
    b_qkv = jnp.concatenate([b_query, b_key, b_value])
    parts = call(
        bind(qkv_kernel, place),
        "norm_qkv",
        [*toks, row(norm1_gain), row(norm1_bias), w_qkv, w_qkv_sibling, row(b_qkv)],
        [shape((rows, w_qkv.shape[1]))] * ny,
        scratch=[pltpu.VMEM((ny * rows, width), F32), pltpu.VMEM((ny * rows, width), BF16)],
    )
    w_out_sibling = place.move(w_out, dc=1)
    w_up_sibling = place.move(w_up, dc=1)
    w_down_sibling = place.move(w_down, dc=1)
    qkv = call(
        bind(add_columns_kernel, place), "add_qkv", spread(parts), shape((nx, rows, w_qkv.shape[1]))
    )
    new_keys, new_values, *messages = call(
        bind(attention_kernel, place, heads),
        "attention",
        [*place.gather_z(qkv), lengths, cache_keys, cache_values],
        [shape(cache_keys.shape), shape(cache_values.shape)] + [shape((rows, share + LANES))] * nx,
        in_specs=[VMEM] * place.nz + [SMEM, ANY, ANY],
        out_specs=[ANY, ANY] + [VMEM] * nx,
        scratch=[
            pltpu.VMEM((group, steps, width), F32),
            pltpu.VMEM((group, steps, width), F32),
            pltpu.VMEM((group, steps, width), F32),
            pltpu.VMEM((group, steps, width), F32),
            pltpu.VMEM((group, steps, LANES), F32),
            pltpu.VMEM((rows, width), F32),
            pltpu.VMEM((rows, LANES), F32),
            pltpu.VMEM((steps * heads, width), F32),
            pltpu.VMEM((group, slots, width), BF16),
            pltpu.VMEM((group, slots, width), BF16),
            pltpu.SemaphoreType.DMA((2, group)),
            pltpu.SemaphoreType.DMA((2, group)),
        ],
    )
    messages = [messages[0]] + [place.move(messages[dx], dx=dx) for dx in range(1, nx)]
    merged = call(
        bind(merge_x_kernel, place, heads), "merge_x", messages, shape((rows, share + LANES))
    )
    attn = call(
        bind(merge_z_kernel, place, heads), "merge_z", place.gather_z(merged), shape((rows, share))
    )
    out_part = call(
        bind(out_kernel, place),
        "out",
        [*spread([attn] * ny), w_out, w_out_sibling, row(b_out)],
        shape((ny * rows, w_out.shape[1])),
        scratch=[pltpu.VMEM((ny * rows, width), BF16)],
    )
    projected = call(
        bind(add_columns_kernel, place),
        "add_out",
        spread([out_part] * ny),
        shape((nx, ny * rows, w_out.shape[1])),
    )
    up_part, mid = call(
        bind(up_kernel, place),
        "norm_up",
        [
            *toks,
            *place.gather_z(projected),
            row(norm2_gain),
            row(norm2_bias),
            w_up,
            w_up_sibling,
            row(b_up),
        ],
        [shape((ny * rows, w_up.shape[1])), shape((rows, width), F32)],
        scratch=[
            pltpu.VMEM((ny * rows, width), F32),
            pltpu.VMEM((ny * rows, width), BF16),
            pltpu.VMEM((rows, width), F32),
        ],
    )
    up_parts = [up_part] + [place.move(up_part, dy=dy) for dy in range(1, ny)]
    piece = CORES * w_down.shape[1] // nx
    feeds = call(
        bind(down_kernel, place),
        "gelu_down",
        [*up_parts, w_down, w_down_sibling],
        [shape((ny * rows, piece))] * nx,
        scratch=[pltpu.VMEM((ny * rows, CORES * w_down.shape[1]), F32)],
    )
    feeds = [feeds[0]] + [place.move(feeds[dx], dx=dx) for dx in range(1, nx)]
    feed = call(bind(add_x_kernel, place), "add_x", feeds, shape((ny * rows, piece)))
    summed = call(
        bind(add_z_kernel, place),
        "add_z",
        place.gather_z(feed),
        [shape((rows, piece))] * ny,
        scratch=[pltpu.VMEM((ny * rows, piece), F32)],
    )
    hidden_out = call(
        bind(last_kernel, place),
        "last",
        [*spread(summed), mid, row(b_down)],
        shape(tokens.shape),
        scratch=[pltpu.VMEM((rows, width), F32)],
    )
    return (hidden_out, new_keys, new_values)


def solution(mesh):
    in_specs = (
        P("req", None, None),
        P("req"),
        P("req", "seq", None),
        P("req", "seq", None),
        P(),
        P(),
        P("req", "seq"),
        P("seq"),
        P("req", "seq"),
        P("seq"),
        P("req", "seq"),
        P("seq"),
        P("req", "seq"),
        P("seq"),
        P(),
        P(),
        P("req", "seq"),
        P("seq"),
        P("seq", "req"),
        P(),
    )
    out_specs = (P("req", None, None), P("req", "seq", None), P("req", "seq", None))
    return jax.shard_map(body, mesh=mesh, in_specs=in_specs, out_specs=out_specs, check_vma=False)
```

time: 344 us -> 107 us (0.31)
  blocking collectives: 179 us -> 0 us
  waiting for transfers between devices: 113 us -> 50.5 us
  starting transfers between devices: 0.31 us -> 37.1 us
  other arithmetic: 19.5 us -> 0.72 us
  matrix products: 15.7 us -> 0 us
  between operations: 14.5 us -> 0.82 us
  Pallas kernels: 0 us -> 10.8 us
  local copies, waits for them, and re-layouts: 1.08 us -> 6.99 us
    all_gather x6 -> x0, blocking collectives: 179 us -> none  [the longest x2 61.1 us: merged(): lax.all_gather(part.astype(kind), axis)]
    psum x1 -> x0, waiting for transfers between devices: 70 us -> none  [body(): summed = lax.psum(feed.astype(jnp.bfloat16), 'seq').astype(jnp.float32)]
    ppermute x0 -> x32, waiting for transfers between devices: none -> 50.5 us  [move(): return lax.ppermute(value, ('seq', 'req'), pairs)]
    all_gather x7 -> x0, waiting for transfers between devices: 39.1 us -> none  [the longest x1 23.8 us: body(): lax.all_gather(w_down, 'req', axis=1, tiled=True)]
    ppermute x0 -> x32, starting transfers between devices: none -> 37.1 us  [move(): return lax.ppermute(value, ('seq', 'req'), pairs)]
    dot_general x8 -> x0, matrix products: 15.7 us -> none  [the longest x1 3.76 us: body(): jnp.dot(normed2, full_up, preferred_element_type=jnp.float32) + b_up]
    pallas_call x0 -> x12, Pallas kernels: none -> 10.8 us  [call(): pl.pallas_call(kernel, name=name, out_shape=outs, in_specs=in_specs or [V...]
    add x17 -> x0, other arithmetic: 9.97 us -> none  [the longest x7 8.3 us: combine(): part = part_a * scale_a[..., None] + part_b * scale_b[..., None]]
  transfers between devices with their start and end apart: 8 -> 32, of which waited for: 3 -> 25; matrix products, arithmetic and copies ran while one was open for 7% -> 1% of each run, Pallas kernels for 0% -> 9%
where the time goes in v2:
time: 107 us
  waiting for transfers between devices  50.5 us (47%)
  starting transfers between devices  37.1 us (35%)
  Pallas kernels  10.8 us (10%)
  local copies, waits for them, and re-layouts  6.99 us (7%)
    ppermute x32, waiting for transfers between devices, move(): return lax.ppermute(value, ('seq', 'req'), pairs)  50.5 us
    ppermute x32, starting transfers between devices, move(): return lax.ppermute(value, ('seq', 'req'), pairs)  37.1 us
    pallas_call x12, Pallas kernels, call(): pl.pallas_call(kernel, name=name, out_shape=outs, in_specs=in_specs or [V...  10.8 us
    unnamed x32, local copies, waits for them, and re-layouts  6.02 us
  transfers between devices with their start and end apart: 32, of which 25 were waited for; matrix products, arithmetic and copies ran while one was open for 1% of the time, Pallas kernels for 9%

profile of v2, /device:TPU:0, one launch (start us, length us, event | category | flops | bytes accessed | tf_op | source)
XLA Modules:
  0.0 106.9 jit_solution(11793744546307375352)
XLA Ops:
  4.7 2.6 %collective-permute-start = (bf16[8,4,2048]{2,1,0:T(4,128)(2,1)}, bf16[8,4,2048]{2,1,0:T(4,128)(2,1)S(1)}, u32[]{:S(2)}, u32[]{:S(2)}) collective-permute-start(bf16[8,4,2048]{2,1,0:T(4,128)(2,1)} %refs_0_.3), channel_id=1, source_target_pairs={{0,2},{1,3},{2,0},{3,1},{4,6},{5,7},{6,4},{7,5},{8,10},{9,11},{10,... | collective-permute-start | bytes 393224 | tf_op jit(solution)/shard_map/ppermute | solution.py:62
  8.1 3.6 %collective-permute-done.refs_1_ = bf16[8,4,2048]{2,1,0:T(4,128)(2,1)S(1)} collective-permute-done((bf16[8,4,2048]{2,1,0:T(4,128)(2,1)}, bf16[8,4,2048]{2,1,0:T(4,128)(2,1)S(1)}, u32[]{:S(2)}, u32[]{:S(2)}) %collective-permute-start) | collective-permute-done | bytes 131104 | tf_op jit(solution)/shard_map/ppermute | solution.py:62
  14.6 1.8 %collective-permute-start.2 = (bf16[32,768]{1,0:T(8,128)(2,1)S(1)}, bf16[32,768]{1,0:T(8,128)(2,1)S(1)}, u32[]{:S(2)}, u32[]{:S(2)}) collective-permute-start(bf16[32,768]{1,0:T(8,128)(2,1)S(1)} %get-tuple-element.16), channel_id=1, source_target_pairs={{0,2},{1,3},{2,0},{3,1},{4,6},{5,7},{6,4},{7,5},{8,10},{9,11},{10,... | collective-permute-start | bytes 147464 | tf_op jit(solution)/shard_map/ppermute | solution.py:62
  16.5 1.5 %collective-permute-start.3 = (bf16[32,768]{1,0:T(8,128)(2,1)S(1)}, bf16[32,768]{1,0:T(8,128)(2,1)S(1)}, u32[]{:S(2)}, u32[]{:S(2)}) collective-permute-start(bf16[32,768]{1,0:T(8,128)(2,1)S(1)} %get-tuple-element.15.refs_0_), channel_id=1, source_target_pairs={{0,4},{1,5},{2,6},{3,7},{4,0},{5,1},{6,2},{7,3},{8,12},{9,13},{10,... | collective-permute-start | bytes 147464 | tf_op jit(solution)/shard_map/ppermute | solution.py:62
  18.8 1.9 %collective-permute-done.3.refs_2_ = bf16[32,768]{1,0:T(8,128)(2,1)S(1)} collective-permute-done((bf16[32,768]{1,0:T(8,128)(2,1)S(1)}, bf16[32,768]{1,0:T(8,128)(2,1)S(1)}, u32[]{:S(2)}, u32[]{:S(2)}) %collective-permute-start.3) | collective-permute-done | bytes 49184 | tf_op jit(solution)/shard_map/ppermute | solution.py:62
  20.6 2.3 %collective-permute-done.4.refs_3_ = bf16[32,768]{1,0:T(8,128)(2,1)S(1)} collective-permute-done((bf16[32,768]{1,0:T(8,128)(2,1)S(1)}, bf16[32,768]{1,0:T(8,128)(2,1)S(1)}, u32[]{:S(2)}, u32[]{:S(2)}) %collective-permute-start.4) | collective-permute-done | bytes 49184 | tf_op jit(solution)/shard_map/ppermute | solution.py:62
  23.0 1.6 %collective-permute-start.5 = (bf16[2,32,768]{2,1,0:T(8,128)(2,1)S(1)}, bf16[2,32,768]{2,1,0:T(8,128)(2,1)S(1)}, u32[]{:S(2)}, u32[]{:S(2)}) collective-permute-start(bf16[2,32,768]{2,1,0:T(8,128)(2,1)S(1)} %add_qkv.1.refs_0_), channel_id=1, source_target_pairs={{0,8},{1,9},{2,10},{3,11},{4,12},{5,13},{6,14},{7,15},{8,16},{9,17... | collective-permute-start | bytes 294920 | tf_op jit(solution)/shard_map/ppermute | solution.py:62
  24.6 2.6 %collective-permute-start.6 = (bf16[2,32,768]{2,1,0:T(8,128)(2,1)S(1)}, bf16[2,32,768]{2,1,0:T(8,128)(2,1)S(1)}, u32[]{:S(2)}, u32[]{:S(2)}) collective-permute-start(bf16[2,32,768]{2,1,0:T(8,128)(2,1)S(1)} %add_qkv.1.refs_0_), channel_id=1, source_target_pairs={{0,16},{1,17},{2,18},{3,19},{4,20},{5,21},{6,22},{7,23},{8,24},{9,... | collective-permute-start | bytes 294920 | tf_op jit(solution)/shard_map/ppermute | solution.py:62
  27.2 1.3 %collective-permute-start.7 = (bf16[2,32,768]{2,1,0:T(8,128)(2,1)S(1)}, bf16[2,32,768]{2,1,0:T(8,128)(2,1)S(1)}, u32[]{:S(2)}, u32[]{:S(2)}) collective-permute-start(bf16[2,32,768]{2,1,0:T(8,128)(2,1)S(1)} %add_qkv.1.refs_0_), channel_id=1, source_target_pairs={{0,24},{1,25},{2,26},{3,27},{4,28},{5,29},{6,30},{7,31},{8,0},{9,1... | collective-permute-start | bytes 294920 | tf_op jit(solution)/shard_map/ppermute | solution.py:62
  28.6 1.6 %collective-permute-done.5.refs_1_ = bf16[2,32,768]{2,1,0:T(8,128)(2,1)S(1)} collective-permute-done((bf16[2,32,768]{2,1,0:T(8,128)(2,1)S(1)}, bf16[2,32,768]{2,1,0:T(8,128)(2,1)S(1)}, u32[]{:S(2)}, u32[]{:S(2)}) %collective-permute-start.5) | collective-permute-done | bytes 98336 | tf_op jit(solution)/shard_map/ppermute | solution.py:62
  30.1 2.7 %collective-permute-done.6.refs_2_ = bf16[2,32,768]{2,1,0:T(8,128)(2,1)S(1)} collective-permute-done((bf16[2,32,768]{2,1,0:T(8,128)(2,1)S(1)}, bf16[2,32,768]{2,1,0:T(8,128)(2,1)S(1)}, u32[]{:S(2)}, u32[]{:S(2)}) %collective-permute-start.6) | collective-permute-done | bytes 98336 | tf_op jit(solution)/shard_map/ppermute | solution.py:62
  32.9 1.6 %copy-done.1 = bf16[8,64,2048]{2,1,0:T(8,128)(2,1)S(1)} copy-done((bf16[8,64,2048]{2,1,0:T(8,128)(2,1)S(1)}, bf16[8,64,2048]{2,1,0:T(8,128)(2,1)}, u32[]{:S(2)}) %copy-start.1) | copy-done | bytes 2097176
  34.4 7.0 %attention.1 = (bf16[8,64,2048]{2,1,0:T(8,128)(2,1)}, bf16[8,64,2048]{2,1,0:T(8,128)(2,1)}, bf16[32,1152]{1,0:T(8,128)(2,1)S(1)}, bf16[32,1152]{1,0:T(8,128)(2,1)S(1)}) custom-call(bf16[2,32,768]{2,1,0:T(8,128)(2,1)S(1)} %add_qkv.1.refs_0_, bf16[2,32,768]{2,1,0:T(8,128)(2,1)S(1)} %collective-permute-done.5.refs_1_, ...), custom_call_target="tpu_custom_call" | custom-call | tf_op jit(solution)/shard_map/attention/pallas_call | solution.py:85
  41.7 4.2 %collective-permute-done.8.refs_1_ = bf16[32,1152]{1,0:T(8,128)(2,1)S(1)} collective-permute-done((bf16[32,1152]{1,0:T(8,128)(2,1)S(1)}, bf16[32,1152]{1,0:T(8,128)(2,1)S(1)}, u32[]{:S(2)}, u32[]{:S(2)}) %collective-permute-start.8) | collective-permute-done | bytes 73760 | tf_op jit(solution)/shard_map/ppermute | solution.py:62
  46.2 3.5 %collective-permute-start.11 = (bf16[32,1152]{1,0:T(8,128)(2,1)S(1)}, bf16[32,1152]{1,0:T(8,128)(2,1)S(1)}, u32[]{:S(2)}, u32[]{:S(2)}) collective-permute-start(bf16[32,1152]{1,0:T(8,128)(2,1)S(1)} %merge_x.1.refs_0_), channel_id=1, source_target_pairs={{0,24},{1,25},{2,26},{3,27},{4,28},{5,29},{6,30},{7,31},{8,0},{9,1... | collective-permute-start | bytes 221192 | tf_op jit(solution)/shard_map/ppermute | solution.py:62
  49.8 3.2 %collective-permute-done.10.refs_2_ = bf16[32,1152]{1,0:T(8,128)(2,1)S(1)} collective-permute-done((bf16[32,1152]{1,0:T(8,128)(2,1)S(1)}, bf16[32,1152]{1,0:T(8,128)(2,1)S(1)}, u32[]{:S(2)}, u32[]{:S(2)}) %collective-permute-start.10) | collective-permute-done | bytes 73760 | tf_op jit(solution)/shard_map/ppermute | solution.py:62
  53.4 5.8 %collective-permute-done.9.refs_1_ = bf16[32,1152]{1,0:T(8,128)(2,1)S(1)} collective-permute-done((bf16[32,1152]{1,0:T(8,128)(2,1)S(1)}, bf16[32,1152]{1,0:T(8,128)(2,1)S(1)}, u32[]{:S(2)}, u32[]{:S(2)}) %collective-permute-start.9) | collective-permute-done | bytes 73760 | tf_op jit(solution)/shard_map/ppermute | solution.py:62
  60.6 2.5 %collective-permute-start.14 = (bf16[32,1024]{1,0:T(8,128)(2,1)S(1)}, bf16[32,1024]{1,0:T(8,128)(2,1)S(1)}, u32[]{:S(2)}, u32[]{:S(2)}) collective-permute-start(bf16[32,1024]{1,0:T(8,128)(2,1)S(1)} %merge_z.1.refs_0_), channel_id=1, source_target_pairs={{0,6},{1,7},{2,4},{3,5},{4,2},{5,3},{6,0},{7,1},{8,14},{9,15},{10,... | collective-permute-start | bytes 196616 | tf_op jit(solution)/shard_map/ppermute | solution.py:62
  64.9 1.2 %collective-permute-done.14.refs_3_ = bf16[32,1024]{1,0:T(8,128)(2,1)S(1)} collective-permute-done((bf16[32,1024]{1,0:T(8,128)(2,1)S(1)}, bf16[32,1024]{1,0:T(8,128)(2,1)S(1)}, u32[]{:S(2)}, u32[]{:S(2)}) %collective-permute-start.14) | collective-permute-done | bytes 65568 | tf_op jit(solution)/shard_map/ppermute | solution.py:62
  67.3 1.8 %collective-permute-start.17 = (bf16[64,256]{1,0:T(8,128)(2,1)S(1)}, bf16[64,256]{1,0:T(8,128)(2,1)S(1)}, u32[]{:S(2)}, u32[]{:S(2)}) collective-permute-start(bf16[64,256]{1,0:T(8,128)(2,1)S(1)} %out.1.refs_0_), channel_id=1, source_target_pairs={{0,4},{1,5},{2,6},{3,7},{4,0},{5,1},{6,2},{7,3},{8,12},{9,13},{10,... | collective-permute-start | bytes 98312 | tf_op jit(solution)/shard_map/ppermute | solution.py:62
  71.2 2.7 %collective-permute-done.18.refs_3_ = bf16[64,256]{1,0:T(8,128)(2,1)S(1)} collective-permute-done((bf16[64,256]{1,0:T(8,128)(2,1)S(1)}, bf16[64,256]{1,0:T(8,128)(2,1)S(1)}, u32[]{:S(2)}, u32[]{:S(2)}) %collective-permute-start.18) | collective-permute-done | bytes 32800 | tf_op jit(solution)/shard_map/ppermute | solution.py:62
  74.5 3.3 %collective-permute-start.21 = (bf16[2,64,256]{2,1,0:T(8,128)(2,1)S(1)}, bf16[2,64,256]{2,1,0:T(8,128)(2,1)S(1)}, u32[]{:S(2)}, u32[]{:S(2)}) collective-permute-start(bf16[2,64,256]{2,1,0:T(8,128)(2,1)S(1)} %add_out.1.refs_2_), channel_id=1, source_target_pairs={{0,24},{1,25},{2,26},{3,27},{4,28},{5,29},{6,30},{7,31},{8,0},{9,1... | collective-permute-start | bytes 196616 | tf_op jit(solution)/shard_map/ppermute | solution.py:62
  77.8 2.2 %collective-permute-done.19.refs_3_ = bf16[2,64,256]{2,1,0:T(8,128)(2,1)S(1)} collective-permute-done((bf16[2,64,256]{2,1,0:T(8,128)(2,1)S(1)}, bf16[2,64,256]{2,1,0:T(8,128)(2,1)S(1)}, u32[]{:S(2)}, u32[]{:S(2)}) %collective-permute-start.19) | collective-permute-done | bytes 65568 | tf_op jit(solution)/shard_map/ppermute | solution.py:62
  81.7 1.2 %collective-permute-start.23 = (bf16[64,1024]{1,0:T(8,128)(2,1)S(1)}, bf16[64,1024]{1,0:T(8,128)(2,1)S(1)}, u32[]{:S(2)}, u32[]{:S(2)}) collective-permute-start(bf16[64,1024]{1,0:T(8,128)(2,1)S(1)} %get-tuple-element.19.refs_0_), channel_id=1, source_target_pairs={{0,2},{1,3},{2,0},{3,1},{4,6},{5,7},{6,4},{7,5},{8,10},{9,11},{10,... | collective-permute-start | bytes 393224 | tf_op jit(solution)/shard_map/ppermute | solution.py:62
  82.8 3.9 %collective-permute-done.23.refs_1_ = bf16[64,1024]{1,0:T(8,128)(2,1)S(1)} collective-permute-done((bf16[64,1024]{1,0:T(8,128)(2,1)S(1)}, bf16[64,1024]{1,0:T(8,128)(2,1)S(1)}, u32[]{:S(2)}, u32[]{:S(2)}) %collective-permute-start.23) | collective-permute-done | bytes 131104 | tf_op jit(solution)/shard_map/ppermute | solution.py:62
  87.5 4.2 %collective-permute-done.25.refs_1_ = bf16[64,512]{1,0:T(8,128)(2,1)S(1)} collective-permute-done((bf16[64,512]{1,0:T(8,128)(2,1)S(1)}, bf16[64,512]{1,0:T(8,128)(2,1)S(1)}, u32[]{:S(2)}, u32[]{:S(2)}) %collective-permute-start.25) | collective-permute-done | bytes 65568 | tf_op jit(solution)/shard_map/ppermute | solution.py:62
  91.7 1.8 %collective-permute-start.26 = (bf16[64,512]{1,0:T(8,128)(2,1)S(1)}, bf16[64,512]{1,0:T(8,128)(2,1)S(1)}, u32[]{:S(2)}, u32[]{:S(2)}) collective-permute-start(bf16[64,512]{1,0:T(8,128)(2,1)S(1)} %add_x.1.refs_0_), channel_id=1, source_target_pairs={{0,8},{1,9},{2,10},{3,11},{4,12},{5,13},{6,14},{7,15},{8,16},{9,17... | collective-permute-start | bytes 196616 | tf_op jit(solution)/shard_map/ppermute | solution.py:62
  93.5 1.8 %collective-permute-start.27 = (bf16[64,512]{1,0:T(8,128)(2,1)S(1)}, bf16[64,512]{1,0:T(8,128)(2,1)S(1)}, u32[]{:S(2)}, u32[]{:S(2)}) collective-permute-start(bf16[64,512]{1,0:T(8,128)(2,1)S(1)} %add_x.1.refs_0_), channel_id=1, source_target_pairs={{0,16},{1,17},{2,18},{3,19},{4,20},{5,21},{6,22},{7,23},{8,24},{9,... | collective-permute-start | bytes 196616 | tf_op jit(solution)/shard_map/ppermute | solution.py:62
  95.9 1.9 %collective-permute-done.26.refs_1_ = bf16[64,512]{1,0:T(8,128)(2,1)S(1)} collective-permute-done((bf16[64,512]{1,0:T(8,128)(2,1)S(1)}, bf16[64,512]{1,0:T(8,128)(2,1)S(1)}, u32[]{:S(2)}, u32[]{:S(2)}) %collective-permute-start.26) | collective-permute-done | bytes 65568 | tf_op jit(solution)/shard_map/ppermute | solution.py:62
  97.9 1.4 %collective-permute-done.27.refs_2_ = bf16[64,512]{1,0:T(8,128)(2,1)S(1)} collective-permute-done((bf16[64,512]{1,0:T(8,128)(2,1)S(1)}, bf16[64,512]{1,0:T(8,128)(2,1)S(1)}, u32[]{:S(2)}, u32[]{:S(2)}) %collective-permute-start.27) | collective-permute-done | bytes 65568 | tf_op jit(solution)/shard_map/ppermute | solution.py:62
  101.4 2.2 %collective-permute-start.31 = (bf16[32,512]{1,0:T(8,128)(2,1)S(1)}, bf16[32,512]{1,0:T(8,128)(2,1)S(1)}, u32[]{:S(2)}, u32[]{:S(2)}) collective-permute-start(bf16[32,512]{1,0:T(8,128)(2,1)S(1)} %get-tuple-element.23), channel_id=1, source_target_pairs={{0,6},{1,7},{2,4},{3,5},{4,2},{5,3},{6,0},{7,1},{8,14},{9,15},{10,... | collective-permute-start | bytes 98312 | tf_op jit(solution)/shard_map/ppermute | solution.py:62
  105.0 1.2 %collective-permute-done.31.refs_3_ = bf16[32,512]{1,0:T(8,128)(2,1)S(1)} collective-permute-done((bf16[32,512]{1,0:T(8,128)(2,1)S(1)}, bf16[32,512]{1,0:T(8,128)(2,1)S(1)}, u32[]{:S(2)}, u32[]{:S(2)}) %collective-permute-start.31) | collective-permute-done | bytes 32800 | tf_op jit(solution)/shard_map/ppermute | solution.py:62
  (79 shorter events, 24.1 us)
Async XLA Ops:
  3.7 7.9 %collective-permute-start.1 = (bf16[512,768]{1,0:T(8,128)(2,1)S(1)}, bf16[512,768]{1,0:T(8,128)(2,1)S(1)}, u32[]{:S(2)}, u32[]{:S(2)}) collective-permute-start(bf16[512,768]{1,0:T(8,128)(2,1)S(1)} %constant_dynamic-update-slice_fusion.refs_4_), channel_id=1, source_target_pairs={{0,1},{1,0},{2,3},{3,2},{4,5},{5,4},{6,7},{7,6},{8,9},{9,8},{10,11... | collective-permute-start | bytes 2359304 | tf_op jit(solution)/shard_map/ppermute | solution.py:62
  4.2 73.6 %collective-permute-start.22 = (bf16[512,1024]{1,0:T(8,128)(2,1)}, bf16[512,1024]{1,0:T(8,128)(2,1)S(1)}, u32[]{:S(2)}, u32[]{:S(2)}) collective-permute-start(bf16[512,1024]{1,0:T(8,128)(2,1)} %refs_8_.1), channel_id=1, source_target_pairs={{0,1},{1,0},{2,3},{3,2},{4,5},{5,4},{6,7},{7,6},{8,9},{9,8},{10,11... | collective-permute-start | bytes 3145736 | tf_op jit(solution)/shard_map/ppermute | solution.py:62
  4.3 78.5 %collective-permute-start.24 = (bf16[1024,512]{1,0:T(8,128)(2,1)}, bf16[1024,512]{1,0:T(8,128)(2,1)S(1)}, u32[]{:S(2)}, u32[]{:S(2)}) collective-permute-start(bf16[1024,512]{1,0:T(8,128)(2,1)} %refs_2_.1), channel_id=1, source_target_pairs={{0,1},{1,0},{2,3},{3,2},{4,5},{5,4},{6,7},{7,6},{8,9},{9,8},{10,11... | collective-permute-start | bytes 3145736 | tf_op jit(solution)/shard_map/ppermute | solution.py:62
  4.7 6.9 %collective-permute-start = (bf16[8,4,2048]{2,1,0:T(4,128)(2,1)}, bf16[8,4,2048]{2,1,0:T(4,128)(2,1)S(1)}, u32[]{:S(2)}, u32[]{:S(2)}) collective-permute-start(bf16[8,4,2048]{2,1,0:T(4,128)(2,1)} %refs_0_.3), channel_id=1, source_target_pairs={{0,2},{1,3},{2,0},{3,1},{4,6},{5,7},{6,4},{7,5},{8,10},{9,11},{10,... | collective-permute-start | bytes 393224 | tf_op jit(solution)/shard_map/ppermute | solution.py:62
  14.6 4.2 %collective-permute-start.2 = (bf16[32,768]{1,0:T(8,128)(2,1)S(1)}, bf16[32,768]{1,0:T(8,128)(2,1)S(1)}, u32[]{:S(2)}, u32[]{:S(2)}) collective-permute-start(bf16[32,768]{1,0:T(8,128)(2,1)S(1)} %get-tuple-element.16), channel_id=1, source_target_pairs={{0,2},{1,3},{2,0},{3,1},{4,6},{5,7},{6,4},{7,5},{8,10},{9,11},{10,... | collective-permute-start | bytes 147464 | tf_op jit(solution)/shard_map/ppermute | solution.py:62
  16.5 4.2 %collective-permute-start.3 = (bf16[32,768]{1,0:T(8,128)(2,1)S(1)}, bf16[32,768]{1,0:T(8,128)(2,1)S(1)}, u32[]{:S(2)}, u32[]{:S(2)}) collective-permute-start(bf16[32,768]{1,0:T(8,128)(2,1)S(1)} %get-tuple-element.15.refs_0_), channel_id=1, source_target_pairs={{0,4},{1,5},{2,6},{3,7},{4,0},{5,1},{6,2},{7,3},{8,12},{9,13},{10,... | collective-permute-start | bytes 147464 | tf_op jit(solution)/shard_map/ppermute | solution.py:62
  18.0 5.0 %collective-permute-start.4 = (bf16[32,768]{1,0:T(8,128)(2,1)S(1)}, bf16[32,768]{1,0:T(8,128)(2,1)S(1)}, u32[]{:S(2)}, u32[]{:S(2)}) collective-permute-start(bf16[32,768]{1,0:T(8,128)(2,1)S(1)} %get-tuple-element.16), channel_id=1, source_target_pairs={{0,6},{1,7},{2,4},{3,5},{4,2},{5,3},{6,0},{7,1},{8,14},{9,15},{10,... | collective-permute-start | bytes 147464 | tf_op jit(solution)/shard_map/ppermute | solution.py:62
  23.0 7.1 %collective-permute-start.5 = (bf16[2,32,768]{2,1,0:T(8,128)(2,1)S(1)}, bf16[2,32,768]{2,1,0:T(8,128)(2,1)S(1)}, u32[]{:S(2)}, u32[]{:S(2)}) collective-permute-start(bf16[2,32,768]{2,1,0:T(8,128)(2,1)S(1)} %add_qkv.1.refs_0_), channel_id=1, source_target_pairs={{0,8},{1,9},{2,10},{3,11},{4,12},{5,13},{6,14},{7,15},{8,16},{9,17... | collective-permute-start | bytes 294920 | tf_op jit(solution)/shard_map/ppermute | solution.py:62
  24.6 8.2 %collective-permute-start.6 = (bf16[2,32,768]{2,1,0:T(8,128)(2,1)S(1)}, bf16[2,32,768]{2,1,0:T(8,128)(2,1)S(1)}, u32[]{:S(2)}, u32[]{:S(2)}) collective-permute-start(bf16[2,32,768]{2,1,0:T(8,128)(2,1)S(1)} %add_qkv.1.refs_0_), channel_id=1, source_target_pairs={{0,16},{1,17},{2,18},{3,19},{4,20},{5,21},{6,22},{7,23},{8,24},{9,... | collective-permute-start | bytes 294920 | tf_op jit(solution)/shard_map/ppermute | solution.py:62
  27.2 5.6 %collective-permute-start.7 = (bf16[2,32,768]{2,1,0:T(8,128)(2,1)S(1)}, bf16[2,32,768]{2,1,0:T(8,128)(2,1)S(1)}, u32[]{:S(2)}, u32[]{:S(2)}) collective-permute-start(bf16[2,32,768]{2,1,0:T(8,128)(2,1)S(1)} %add_qkv.1.refs_0_), channel_id=1, source_target_pairs={{0,24},{1,25},{2,26},{3,27},{4,28},{5,29},{6,30},{7,31},{8,0},{9,1... | collective-permute-start | bytes 294920 | tf_op jit(solution)/shard_map/ppermute | solution.py:62
  30.1 30.5 %collective-permute-start.15 = (bf16[512,256]{1,0:T(8,128)(2,1)S(1)}, bf16[512,256]{1,0:T(8,128)(2,1)S(1)}, u32[]{:S(2)}, u32[]{:S(2)}) collective-permute-start(bf16[512,256]{1,0:T(8,128)(2,1)S(1)} %copy-done.6), channel_id=1, source_target_pairs={{0,1},{1,0},{2,3},{3,2},{4,5},{5,4},{6,7},{7,6},{8,9},{9,8},{10,11... | collective-permute-start | bytes 786440 | tf_op jit(solution)/shard_map/ppermute | solution.py:62
  41.5 4.4 %collective-permute-start.8 = (bf16[32,1152]{1,0:T(8,128)(2,1)S(1)}, bf16[32,1152]{1,0:T(8,128)(2,1)S(1)}, u32[]{:S(2)}, u32[]{:S(2)}) collective-permute-start(bf16[32,1152]{1,0:T(8,128)(2,1)S(1)} %get-tuple-element.18), channel_id=1, source_target_pairs={{0,4},{1,5},{2,6},{3,7},{4,0},{5,1},{6,2},{7,3},{8,12},{9,13},{10,... | collective-permute-start | bytes 221192 | tf_op jit(solution)/shard_map/ppermute | solution.py:62
  46.2 6.8 %collective-permute-start.10 = (bf16[32,1152]{1,0:T(8,128)(2,1)S(1)}, bf16[32,1152]{1,0:T(8,128)(2,1)S(1)}, u32[]{:S(2)}, u32[]{:S(2)}) collective-permute-start(bf16[32,1152]{1,0:T(8,128)(2,1)S(1)} %merge_x.1.refs_0_), channel_id=1, source_target_pairs={{0,16},{1,17},{2,18},{3,19},{4,20},{5,21},{6,22},{7,23},{8,24},{9,... | collective-permute-start | bytes 221192 | tf_op jit(solution)/shard_map/ppermute | solution.py:62
  46.2 7.1 %collective-permute-start.11 = (bf16[32,1152]{1,0:T(8,128)(2,1)S(1)}, bf16[32,1152]{1,0:T(8,128)(2,1)S(1)}, u32[]{:S(2)}, u32[]{:S(2)}) collective-permute-start(bf16[32,1152]{1,0:T(8,128)(2,1)S(1)} %merge_x.1.refs_0_), channel_id=1, source_target_pairs={{0,24},{1,25},{2,26},{3,27},{4,28},{5,29},{6,30},{7,31},{8,0},{9,1... | collective-permute-start | bytes 221192 | tf_op jit(solution)/shard_map/ppermute | solution.py:62
  53.0 6.2 %collective-permute-start.9 = (bf16[32,1152]{1,0:T(8,128)(2,1)S(1)}, bf16[32,1152]{1,0:T(8,128)(2,1)S(1)}, u32[]{:S(2)}, u32[]{:S(2)}) collective-permute-start(bf16[32,1152]{1,0:T(8,128)(2,1)S(1)} %merge_x.1.refs_0_), channel_id=1, source_target_pairs={{0,8},{1,9},{2,10},{3,11},{4,12},{5,13},{6,14},{7,15},{8,16},{9,17... | collective-permute-start | bytes 221192 | tf_op jit(solution)/shard_map/ppermute | solution.py:62
  59.5 4.3 %collective-permute-start.12 = (bf16[32,1024]{1,0:T(8,128)(2,1)S(1)}, bf16[32,1024]{1,0:T(8,128)(2,1)S(1)}, u32[]{:S(2)}, u32[]{:S(2)}) collective-permute-start(bf16[32,1024]{1,0:T(8,128)(2,1)S(1)} %merge_z.1.refs_0_), channel_id=1, source_target_pairs={{0,2},{1,3},{2,0},{3,1},{4,6},{5,7},{6,4},{7,5},{8,10},{9,11},{10,... | collective-permute-start | bytes 196616 | tf_op jit(solution)/shard_map/ppermute | solution.py:62
  60.6 4.3 %collective-permute-start.13 = (bf16[32,1024]{1,0:T(8,128)(2,1)S(1)}, bf16[32,1024]{1,0:T(8,128)(2,1)S(1)}, u32[]{:S(2)}, u32[]{:S(2)}) collective-permute-start(bf16[32,1024]{1,0:T(8,128)(2,1)S(1)} %merge_z.1.refs_0_), channel_id=1, source_target_pairs={{0,4},{1,5},{2,6},{3,7},{4,0},{5,1},{6,2},{7,3},{8,12},{9,13},{10,... | collective-permute-start | bytes 196616 | tf_op jit(solution)/shard_map/ppermute | solution.py:62
  60.6 5.4 %collective-permute-start.14 = (bf16[32,1024]{1,0:T(8,128)(2,1)S(1)}, bf16[32,1024]{1,0:T(8,128)(2,1)S(1)}, u32[]{:S(2)}, u32[]{:S(2)}) collective-permute-start(bf16[32,1024]{1,0:T(8,128)(2,1)S(1)} %merge_z.1.refs_0_), channel_id=1, source_target_pairs={{0,6},{1,7},{2,4},{3,5},{4,2},{5,3},{6,0},{7,1},{8,14},{9,15},{10,... | collective-permute-start | bytes 196616 | tf_op jit(solution)/shard_map/ppermute | solution.py:62
  66.3 4.0 %collective-permute-start.16 = (bf16[64,256]{1,0:T(8,128)(2,1)S(1)}, bf16[64,256]{1,0:T(8,128)(2,1)S(1)}, u32[]{:S(2)}, u32[]{:S(2)}) collective-permute-start(bf16[64,256]{1,0:T(8,128)(2,1)S(1)} %out.1.refs_0_), channel_id=1, source_target_pairs={{0,2},{1,3},{2,0},{3,1},{4,6},{5,7},{6,4},{7,5},{8,10},{9,11},{10,... | collective-permute-start | bytes 98312 | tf_op jit(solution)/shard_map/ppermute | solution.py:62
  67.3 3.9 %collective-permute-start.17 = (bf16[64,256]{1,0:T(8,128)(2,1)S(1)}, bf16[64,256]{1,0:T(8,128)(2,1)S(1)}, u32[]{:S(2)}, u32[]{:S(2)}) collective-permute-start(bf16[64,256]{1,0:T(8,128)(2,1)S(1)} %out.1.refs_0_), channel_id=1, source_target_pairs={{0,4},{1,5},{2,6},{3,7},{4,0},{5,1},{6,2},{7,3},{8,12},{9,13},{10,... | collective-permute-start | bytes 98312 | tf_op jit(solution)/shard_map/ppermute | solution.py:62
  69.1 4.8 %collective-permute-start.18 = (bf16[64,256]{1,0:T(8,128)(2,1)S(1)}, bf16[64,256]{1,0:T(8,128)(2,1)S(1)}, u32[]{:S(2)}, u32[]{:S(2)}) collective-permute-start(bf16[64,256]{1,0:T(8,128)(2,1)S(1)} %out.1.refs_0_), channel_id=1, source_target_pairs={{0,6},{1,7},{2,4},{3,5},{4,2},{5,3},{6,0},{7,1},{8,14},{9,15},{10,... | collective-permute-start | bytes 98312 | tf_op jit(solution)/shard_map/ppermute | solution.py:62
  74.0 6.1 %collective-permute-start.19 = (bf16[2,64,256]{2,1,0:T(8,128)(2,1)S(1)}, bf16[2,64,256]{2,1,0:T(8,128)(2,1)S(1)}, u32[]{:S(2)}, u32[]{:S(2)}) collective-permute-start(bf16[2,64,256]{2,1,0:T(8,128)(2,1)S(1)} %add_out.1.refs_2_), channel_id=1, source_target_pairs={{0,8},{1,9},{2,10},{3,11},{4,12},{5,13},{6,14},{7,15},{8,16},{9,17... | collective-permute-start | bytes 196616 | tf_op jit(solution)/shard_map/ppermute | solution.py:62
  74.0 6.1 %collective-permute-start.20 = (bf16[2,64,256]{2,1,0:T(8,128)(2,1)S(1)}, bf16[2,64,256]{2,1,0:T(8,128)(2,1)S(1)}, u32[]{:S(2)}, u32[]{:S(2)}) collective-permute-start(bf16[2,64,256]{2,1,0:T(8,128)(2,1)S(1)} %add_out.1.refs_2_), channel_id=1, source_target_pairs={{0,16},{1,17},{2,18},{3,19},{4,20},{5,21},{6,22},{7,23},{8,24},{9,... | collective-permute-start | bytes 196616 | tf_op jit(solution)/shard_map/ppermute | solution.py:62
  74.5 6.2 %collective-permute-start.21 = (bf16[2,64,256]{2,1,0:T(8,128)(2,1)S(1)}, bf16[2,64,256]{2,1,0:T(8,128)(2,1)S(1)}, u32[]{:S(2)}, u32[]{:S(2)}) collective-permute-start(bf16[2,64,256]{2,1,0:T(8,128)(2,1)S(1)} %add_out.1.refs_2_), channel_id=1, source_target_pairs={{0,24},{1,25},{2,26},{3,27},{4,28},{5,29},{6,30},{7,31},{8,0},{9,1... | collective-permute-start | bytes 196616 | tf_op jit(solution)/shard_map/ppermute | solution.py:62
  81.7 5.0 %collective-permute-start.23 = (bf16[64,1024]{1,0:T(8,128)(2,1)S(1)}, bf16[64,1024]{1,0:T(8,128)(2,1)S(1)}, u32[]{:S(2)}, u32[]{:S(2)}) collective-permute-start(bf16[64,1024]{1,0:T(8,128)(2,1)S(1)} %get-tuple-element.19.refs_0_), channel_id=1, source_target_pairs={{0,2},{1,3},{2,0},{3,1},{4,6},{5,7},{6,4},{7,5},{8,10},{9,11},{10,... | collective-permute-start | bytes 393224 | tf_op jit(solution)/shard_map/ppermute | solution.py:62
  87.2 4.5 %collective-permute-start.25 = (bf16[64,512]{1,0:T(8,128)(2,1)S(1)}, bf16[64,512]{1,0:T(8,128)(2,1)S(1)}, u32[]{:S(2)}, u32[]{:S(2)}) collective-permute-start(bf16[64,512]{1,0:T(8,128)(2,1)S(1)} %get-tuple-element.21), channel_id=1, source_target_pairs={{0,4},{1,5},{2,6},{3,7},{4,0},{5,1},{6,2},{7,3},{8,12},{9,13},{10,... | collective-permute-start | bytes 196616 | tf_op jit(solution)/shard_map/ppermute | solution.py:62
  91.7 6.1 %collective-permute-start.26 = (bf16[64,512]{1,0:T(8,128)(2,1)S(1)}, bf16[64,512]{1,0:T(8,128)(2,1)S(1)}, u32[]{:S(2)}, u32[]{:S(2)}) collective-permute-start(bf16[64,512]{1,0:T(8,128)(2,1)S(1)} %add_x.1.refs_0_), channel_id=1, source_target_pairs={{0,8},{1,9},{2,10},{3,11},{4,12},{5,13},{6,14},{7,15},{8,16},{9,17... | collective-permute-start | bytes 196616 | tf_op jit(solution)/shard_map/ppermute | solution.py:62
  93.5 5.8 %collective-permute-start.27 = (bf16[64,512]{1,0:T(8,128)(2,1)S(1)}, bf16[64,512]{1,0:T(8,128)(2,1)S(1)}, u32[]{:S(2)}, u32[]{:S(2)}) collective-permute-start(bf16[64,512]{1,0:T(8,128)(2,1)S(1)} %add_x.1.refs_0_), channel_id=1, source_target_pairs={{0,16},{1,17},{2,18},{3,19},{4,20},{5,21},{6,22},{7,23},{8,24},{9,... | collective-permute-start | bytes 196616 | tf_op jit(solution)/shard_map/ppermute | solution.py:62
  95.3 4.6 %collective-permute-start.28 = (bf16[64,512]{1,0:T(8,128)(2,1)S(1)}, bf16[64,512]{1,0:T(8,128)(2,1)S(1)}, u32[]{:S(2)}, u32[]{:S(2)}) collective-permute-start(bf16[64,512]{1,0:T(8,128)(2,1)S(1)} %add_x.1.refs_0_), channel_id=1, source_target_pairs={{0,24},{1,25},{2,26},{3,27},{4,28},{5,29},{6,30},{7,31},{8,0},{9,1... | collective-permute-start | bytes 196616 | tf_op jit(solution)/shard_map/ppermute | solution.py:62
  100.0 4.0 %collective-permute-start.29 = (bf16[32,512]{1,0:T(8,128)(2,1)S(1)}, bf16[32,512]{1,0:T(8,128)(2,1)S(1)}, u32[]{:S(2)}, u32[]{:S(2)}) collective-permute-start(bf16[32,512]{1,0:T(8,128)(2,1)S(1)} %get-tuple-element.23), channel_id=1, source_target_pairs={{0,2},{1,3},{2,0},{3,1},{4,6},{5,7},{6,4},{7,5},{8,10},{9,11},{10,... | collective-permute-start | bytes 98312 | tf_op jit(solution)/shard_map/ppermute | solution.py:62
  101.1 3.9 %collective-permute-start.30 = (bf16[32,512]{1,0:T(8,128)(2,1)S(1)}, bf16[32,512]{1,0:T(8,128)(2,1)S(1)}, u32[]{:S(2)}, u32[]{:S(2)}) collective-permute-start(bf16[32,512]{1,0:T(8,128)(2,1)S(1)} %get-tuple-element.22.refs_0_), channel_id=1, source_target_pairs={{0,4},{1,5},{2,6},{3,7},{4,0},{5,1},{6,2},{7,3},{8,12},{9,13},{10,... | collective-permute-start | bytes 98312 | tf_op jit(solution)/shard_map/ppermute | solution.py:62
  101.4 4.8 %collective-permute-start.31 = (bf16[32,512]{1,0:T(8,128)(2,1)S(1)}, bf16[32,512]{1,0:T(8,128)(2,1)S(1)}, u32[]{:S(2)}, u32[]{:S(2)}) collective-permute-start(bf16[32,512]{1,0:T(8,128)(2,1)S(1)} %get-tuple-element.23), channel_id=1, source_target_pairs={{0,6},{1,7},{2,4},{3,5},{4,2},{5,3},{6,0},{7,1},{8,14},{9,15},{10,... | collective-permute-start | bytes 98312 | tf_op jit(solution)/shard_map/ppermute | solution.py:62
  (15 other events, 458.2 us)

commit v3 on v2

--- a/solution.py
+++ b/solution.py
@@ -14,13 +14,13 @@
 F32 = jnp.float32
 VMEM = pl.BlockSpec(memory_space=pltpu.VMEM)
 SMEM = pl.BlockSpec(memory_space=pltpu.SMEM)
-ANY = pl.BlockSpec(memory_space=pl.ANY)
+HBM = pl.BlockSpec(memory_space=pltpu.HBM)
 
 
 class Place:
     def __init__(self, seqs, reqs):
         self.ny = reqs // CORES
-        self.nx = self.ny if seqs % self.ny == 0 else 1
+        self.nx = self.ny
         self.nz = seqs // self.nx
         self.seqs = seqs
 
@@ -61,6 +61,21 @@
                         )
         return lax.ppermute(value, ("seq", "req"), pairs)
 
+    def transpose(self, value, k):
+        n = self.nx
+        pairs = []
+        for z in range(self.nz):
+            for x in range(n):
+                for y in range(n):
+                    for c in range(CORES):
+                        pairs.append(
+                            (
+                                ((z * n + x) * n + y) * CORES + c,
+                                ((z * n + y) * n + (x - k) % n) * CORES + c,
+                            )
+                        )
+        return lax.ppermute(value, ("seq", "req"), pairs)
+
     def gather_z(self, value):
         return [value] + [self.move(value, dz=dz) for dz in range(1, self.nz)]
 
@@ -108,24 +123,39 @@
     )
 
 
+def flatten(block, flat, start):
+    group, steps, _ = block.shape
+    for i in range(group):
+        flat[start + i * steps : start + (i + 1) * steps, :] = block[i].astype(F32)
+
+
+def norm_kernel(tokens, gain, shift, out, flat):
+    flatten(tokens, flat, 0)
+    out[...] = layer_norm(flat[...], gain[...], shift[...]).astype(BF16)
+
+
 def qkv_kernel(place, *refs):
     ny = place.ny
-    toks = refs[:ny]
-    gain, shift, own, sibling, bias = refs[ny : ny + 5]
-    outs = refs[ny + 5 : 2 * ny + 5]
-    flat, normed = refs[2 * ny + 5 :]
-    group, steps, _ = toks[0].shape
-    rows = group * steps
-    for j in range(ny):
-        for i in range(group):
-            flat[j * rows + i * steps : j * rows + (i + 1) * steps, :] = toks[j][i].astype(F32)
-    normed[...] = layer_norm(flat[...], gain[...], shift[...]).astype(BF16)
-    acc = two_halves(normed, own, sibling)
-    for j in range(ny):
-        part = acc[j * rows : (j + 1) * rows]
-        if j == 0:
-            part = part + bias[...]
-        outs[(ny - j) % ny][...] = part.astype(BF16)
+    mine = refs[0]
+    toks = refs[1:ny]
+    gain, shift = refs[ny : ny + 2]
+    weights = refs[ny + 2 : ny + 8]
+    biases = refs[ny + 8 : ny + 11]
+    outs = refs[ny + 11 : 2 * ny + 11]
+    flat, normed = refs[2 * ny + 11 :]
+    rows = mine.shape[0]
+    normed[:rows, :] = mine[...]
+    for j, tok in enumerate(toks):
+        flatten(tok, flat, j * rows)
+    normed[rows:, :] = layer_norm(flat[...], gain[...], shift[...]).astype(BF16)
+    cols = weights[0].shape[1]
+    for k in range(3):
+        acc = two_halves(normed, weights[2 * k], weights[2 * k + 1])
+        for j in range(ny):
+            part = acc[j * rows : (j + 1) * rows]
+            if j == 0:
+                part = part + biases[k][...]
+            outs[(ny - j) % ny][:, k * cols : (k + 1) * cols] = part.astype(BF16)
 
 
 def add_columns_kernel(place, *refs):
@@ -148,98 +178,111 @@
     return pltpu.roll(value, by % LANES, 1)
 
 
-def attention_kernel(place, heads, *refs):
+def attention_kernel(place, heads, steps, *refs):
     nx, nz = place.nx, place.nz
     gathered = refs[:nz]
     lengths, keys_in, values_in, keys_out, values_out = refs[nz : nz + 5]
     messages = refs[nz + 5 : nz + 5 + nx]
-    qs, ks, vs, part, stats, flat, flat_stats, mask, keys, values, in_sems, out_sems = refs[
-        nz + 5 + nx :
-    ]
+    qs, ks, vs, scores, part, stats, keys, values, in_sems, out_sems = refs[nz + 5 + nx :]
     group, slots, width = keys.shape
-    steps = qs.shape[1]
     cols = width // place.seqs
     seq = lax.axis_index("seq")
 
-    def copy_in(i, source, target, which):
-        return pltpu.make_async_copy(source.at[i], target.at[i], in_sems.at[which, i])
-
-    def copy_out(i, source, target, which):
-        return pltpu.make_async_copy(source.at[i], target.at[i], out_sems.at[which, i])
+    def copies(sources, targets, sems, i):
+        return [
+            pltpu.make_async_copy(source.at[i], target.at[i], sems.at[k, i])
+            for k, (source, target) in enumerate(zip(sources, targets))
+        ]
+
+    def coming(i):
+        return copies((keys_in, values_in), (keys, values), in_sems, i)
+
+    def going(i):
+        return copies((keys, values), (keys_out, values_out), out_sems, i)
 
     for i in range(group):
-        copy_in(i, keys_in, keys, 0).start()
-        copy_in(i, values_in, values, 1).start()
+        for copy in coming(i):
+            copy.start()
     for dz in range(nz):
         span = at(place.z_before(dz), nx * cols)
         for k, target in enumerate((qs, ks, vs)):
-            block = side_by_side(gathered[dz], k * cols, cols)
-            for i in range(group):
-                target[i, :, span] = block[i * steps : (i + 1) * steps]
-    across = steps * heads
-    row_head = lax.rem(lax.broadcasted_iota(jnp.int32, (across, width), 0), heads)
-    column_head = lax.div(lax.broadcasted_iota(jnp.int32, (across, width), 1), HEAD)
-    mask[...] = (row_head == column_head).astype(F32)
-
-    def one(i, carry):
-        length = lengths[i]
-        base = length - seq * slots
-        copy_in(i, keys_in, keys, 0).wait()
-        copy_in(i, values_in, values, 1).wait()
+            target[:, span] = side_by_side(gathered[dz], k * cols, cols)
+    window = min(32, slots)
+    for i in range(group):
+        base = lengths[i] - seq * slots
+        for copy in coming(i):
+            copy.wait()
 
         @pl.when((base > -steps) & (base < slots))
         def _():
-            slot = lax.broadcasted_iota(jnp.int32, (slots, width), 0)
-            new_k = ks[i]
-            new_v = vs[i]
-            k = keys[i].astype(F32)
-            v = values[i].astype(F32)
-            for t in range(steps):
-                k = jnp.where(slot == base + t, new_k[t : t + 1], k)
-                v = jnp.where(slot == base + t, new_v[t : t + 1], v)
-            keys[i] = k.astype(BF16)
-            values[i] = v.astype(BF16)
-
-        copy_out(i, keys, keys_out, 0).start()
-        copy_out(i, values, values_out, 1).start()
-        query = qs[i]
-        query = jnp.broadcast_to(query[:, None, :], (steps, heads, width)).reshape(across, width)
-        query = (query * mask[...]).astype(BF16)
-        scores = lax.dot_general(
-            query, keys[i], (((1,), (1,)), ((), ())), preferred_element_type=F32
-        ) * HEAD ** (-0.5)
-        position = seq * slots + lax.broadcasted_iota(jnp.int32, (across, slots), 1)
-        step = lax.div(lax.broadcasted_iota(jnp.int32, (across, slots), 0), heads)
-        valid = position <= length + step
-        masked = jnp.where(valid, scores, -1e30)
+            start = jnp.clip(lax.div(jnp.maximum(base, 0), 16) * 16, 0, slots - window)
+            here = pl.ds(pl.multiple_of(start, 16), window)
+            slot = start + lax.broadcasted_iota(jnp.int32, (window, width), 0)
+            for target, fresh in ((keys, ks), (values, vs)):
+                block = target[i, here, :].astype(F32)
+                for t in range(steps):
+                    at_row = fresh[i * steps + t : i * steps + t + 1, :]
+                    block = jnp.where(slot == base + t, at_row, block)
+                target[i, here, :] = block.astype(BF16)
+
+        for copy in going(i):
+            copy.start()
+
+    pack = max(1, min(group, 256 // slots))
+    rows = pack * steps
+    tile = 2 * HEAD
+    side = lax.rem(lax.div(lax.broadcasted_iota(jnp.int32, (rows, width), 1), HEAD), 2)
+    left = lax.broadcasted_iota(jnp.int32, (rows, tile), 1) < HEAD
+    many = heads * rows
+    row = lax.broadcasted_iota(jnp.int32, (many, pack * slots), 0)
+    column = lax.broadcasted_iota(jnp.int32, (many, pack * slots), 1)
+    owner = lax.div(lax.rem(row, rows), steps)
+    step = lax.rem(row, steps)
+    position = seq * slots + lax.rem(column, slots)
+    same = owner == lax.div(column, slots)
+    lane = lax.broadcasted_iota(jnp.int32, (rows, LANES), 1)
+    for g in range(group // pack):
+        mine = slice(g * rows, (g + 1) * rows)
+        query = qs[mine, :]
+        pair = jnp.concatenate(
+            [jnp.where(side == 0, query, 0.0), jnp.where(side == 1, query, 0.0)], axis=0
+        ).astype(BF16)
+        these = slice(g * pack, (g + 1) * pack)
+        key = keys[these].reshape(pack * slots, width)
+        value = values[these].reshape(pack * slots, width)
+        for j in range(heads // 2):
+            span = slice(j * tile, (j + 1) * tile)
+            scores[j * 2 * rows : (j + 1) * 2 * rows, :] = lax.dot_general(
+                pair[:, span], key[:, span], (((1,), (1,)), ((), ())), preferred_element_type=F32
+            )
+        limit = step
+        for k in range(pack):
+            limit = jnp.where(owner == k, step + lengths[g * pack + k], limit)
+        valid = same & (position <= limit)
+        masked = jnp.where(valid, scores[...] * HEAD ** (-0.5), -1e30)
         peak = jnp.max(masked, axis=-1, keepdims=True)
         expo = jnp.where(valid, jnp.exp(masked - peak), 0.0)
         total = jnp.sum(expo, axis=-1, keepdims=True)
-        mixed = dot(expo.astype(BF16), values[i]) * mask[...]
-        part[i] = jnp.sum(mixed.reshape(steps, heads, width), axis=1)
-        lane = lax.broadcasted_iota(jnp.int32, (across, LANES), 1)
-        head = lax.rem(lax.broadcasted_iota(jnp.int32, (across, LANES), 0), heads)
-        pieces = split_three(peak) + split_three(total)[:2]
-        tile = jnp.zeros((across, LANES), F32)
-        for k, piece in enumerate(pieces):
-            tile = jnp.where(lane == head + k * heads, piece, tile)
-        stats[i] = jnp.sum(tile.reshape(steps, heads, LANES), axis=1)
-        return carry
-
-    lax.fori_loop(0, group, one, 0)
-    for i in range(group):
-        flat[i * steps : (i + 1) * steps, :] = part[i]
-        flat_stats[i * steps : (i + 1) * steps, :] = stats[i]
+        probs = expo.astype(BF16)
+        for j in range(heads // 2):
+            span = slice(j * tile, (j + 1) * tile)
+            mixed = dot(probs[j * 2 * rows : (j + 1) * 2 * rows], value[:, span])
+            part[mine, span] = jnp.where(left, mixed[:rows], mixed[rows:])
+        line = jnp.zeros((rows, LANES), F32)
+        for k, piece in enumerate(split_three(peak) + split_three(total)[:2]):
+            for h in range(heads):
+                line = jnp.where(lane == k * heads + h, piece[h * rows : (h + 1) * rows], line)
+        stats[mine, :] = line
     share = width // nx
     for dx in range(nx):
         to = place.x_after(dx)
-        messages[dx][:, :share] = flat[:, at(to, share)].astype(BF16)
+        messages[dx][:, :share] = part[:, at(to, share)].astype(BF16)
         messages[dx][:, share:] = pltpu.roll(
-            flat_stats[...], lax.rem(LANES - to * (heads // nx), LANES), 1
+            stats[...], lax.rem(LANES - to * (heads // nx), LANES), 1
         ).astype(BF16)
     for i in range(group):
-        copy_out(i, keys, keys_out, 0).wait()
-        copy_out(i, values, values_out, 1).wait()
+        for copy in going(i):
+            copy.wait()
 
 
 def expand(factor, count):
@@ -288,16 +331,28 @@
     ).astype(BF16)
 
 
-def out_kernel(place, *refs):
-    nx, ny = place.nx, place.ny
-    parts = refs[: nx * ny]
-    own, sibling, bias, out, full = refs[nx * ny :]
-    rows, share = parts[0].shape
-    for dx in range(nx):
-        for dy in range(ny):
-            full[at(place.y_before(dy), rows), at(place.x_before(dx), share)] = parts[dx * ny + dy][...]
-    first = (place.y() == 0).astype(F32)
-    out[...] = (two_halves(full, own, sibling) + bias[...] * first).astype(BF16)
+def out_kernel(place, attn, *refs):
+    nx = place.nx
+    weights = refs[: 2 * nx]
+    bias, out, total = refs[2 * nx :]
+    depth = weights[0].shape[0]
+    core = place.core()
+    for k in range(nx):
+        block = lax.rem(place.y() + k, nx)
+        total[block] = dot(attn[:, at(core, depth)], weights[2 * k][...]) + dot(
+            attn[:, at(1 - core, depth)], weights[2 * k + 1][...]
+        )
+    total[place.x()] = total[place.x()] + bias[...]
+    out[...] = total[...].astype(BF16)
+
+
+def add_out_kernel(place, *refs):
+    out = refs[-1]
+    for dy in range(place.ny):
+        total = refs[dy][...].astype(F32)
+        for dx in range(1, place.nx):
+            total = total + refs[dx * place.ny + dy][...].astype(F32)
+        out[place.y_before(dy)] = total.astype(BF16)
 
 
 def up_kernel(place, *refs):
@@ -307,13 +362,14 @@
     gain, shift, own, sibling, bias, out, mid_out, proj, normed, flat = refs[ny + nz :]
     group, steps, _ = toks[0].shape
     rows = group * steps
-    cols = gathered[0].shape[2]
+    cols = gathered[0].shape[3]
     for dz in range(nz):
-        proj[:, at(place.z_before(dz), place.nx * cols)] = side_by_side(gathered[dz], 0, cols)
+        span = at(place.z_before(dz), place.nx * cols)
+        for y in range(ny):
+            proj[y * rows : (y + 1) * rows, span] = side_by_side(gathered[dz].at[y], 0, cols)
     for j in range(ny):
         here = at(place.y_before(j), rows)
-        for i in range(group):
-            flat[i * steps : (i + 1) * steps, :] = toks[j][i].astype(F32)
+        flatten(toks[j], flat, 0)
         mid = flat[...] + proj[here, :]
         if j == 0:
             mid_out[...] = mid
@@ -411,40 +467,52 @@
         ]
 
     toks = [tokens] + [place.move(tokens, dy=dy) for dy in range(1, ny)]
-    w_qkv = jnp.concatenate([w_query, w_key, w_value], axis=1)
-    w_qkv_sibling = place.move(w_qkv, dc=1)
-    b_qkv = jnp.concatenate([b_query, b_key, b_value])
+    cols = w_query.shape[1]
+    weights = []
+    for weight in (w_query, w_key, w_value):
+        weights += [weight, place.move(weight, dc=1)]
+    gain, shift = row(norm1_gain), row(norm1_bias)
+    normed = call(
+        norm_kernel,
+        "norm",
+        [tokens, gain, shift],
+        shape((rows, width)),
+        scratch=[pltpu.VMEM((rows, width), F32)],
+    )
     parts = call(
         bind(qkv_kernel, place),
         "norm_qkv",
-        [*toks, row(norm1_gain), row(norm1_bias), w_qkv, w_qkv_sibling, row(b_qkv)],
-        [shape((rows, w_qkv.shape[1]))] * ny,
-        scratch=[pltpu.VMEM((ny * rows, width), F32), pltpu.VMEM((ny * rows, width), BF16)],
-    )
-    w_out_sibling = place.move(w_out, dc=1)
+        [normed, *toks[1:], gain, shift, *weights, row(b_query), row(b_key), row(b_value)],
+        [shape((rows, 3 * cols))] * ny,
+        scratch=[pltpu.VMEM(((ny - 1) * rows, width), F32), pltpu.VMEM((ny * rows, width), BF16)],
+    )
+    w_outs = []
+    for k in range(nx):
+        block = place.transpose(w_out, k)
+        w_outs += [block, place.move(block, dc=1)]
     w_up_sibling = place.move(w_up, dc=1)
     w_down_sibling = place.move(w_down, dc=1)
     qkv = call(
-        bind(add_columns_kernel, place), "add_qkv", spread(parts), shape((nx, rows, w_qkv.shape[1]))
-    )
+        bind(add_columns_kernel, place), "add_qkv", spread(parts), shape((nx, rows, 3 * cols))
+    )
+
+    pack = max(1, min(group, 256 // slots))
     new_keys, new_values, *messages = call(
-        bind(attention_kernel, place, heads),
+        bind(attention_kernel, place, heads, steps),
         "attention",
         [*place.gather_z(qkv), lengths, cache_keys, cache_values],
         [shape(cache_keys.shape), shape(cache_values.shape)] + [shape((rows, share + LANES))] * nx,
-        in_specs=[VMEM] * place.nz + [SMEM, ANY, ANY],
-        out_specs=[ANY, ANY] + [VMEM] * nx,
+        in_specs=[VMEM] * place.nz + [SMEM, HBM, HBM],
+        out_specs=[HBM, HBM] + [VMEM] * nx,
         scratch=[
-            pltpu.VMEM((group, steps, width), F32),
-            pltpu.VMEM((group, steps, width), F32),
-            pltpu.VMEM((group, steps, width), F32),
-            pltpu.VMEM((group, steps, width), F32),
-            pltpu.VMEM((group, steps, LANES), F32),
+            pltpu.VMEM((rows, width), F32),
+            pltpu.VMEM((rows, width), F32),
+            pltpu.VMEM((rows, width), F32),
+            pltpu.VMEM((heads * pack * steps, pack * slots), F32),
             pltpu.VMEM((rows, width), F32),
             pltpu.VMEM((rows, LANES), F32),
-            pltpu.VMEM((steps * heads, width), F32),
-            pltpu.VMEM((group, slots, width), BF16),
-            pltpu.VMEM((group, slots, width), BF16),
+            pltpu.VMEM(cache_keys.shape, BF16),
+            pltpu.VMEM(cache_keys.shape, BF16),
             pltpu.SemaphoreType.DMA((2, group)),
             pltpu.SemaphoreType.DMA((2, group)),
         ],
@@ -459,15 +527,15 @@
     out_part = call(
         bind(out_kernel, place),
         "out",
-        [*spread([attn] * ny), w_out, w_out_sibling, row(b_out)],
-        shape((ny * rows, w_out.shape[1])),
-        scratch=[pltpu.VMEM((ny * rows, width), BF16)],
+        [attn, *w_outs, row(b_out)],
+        shape((nx, rows, cols)),
+        scratch=[pltpu.VMEM((nx, rows, cols), F32)],
     )
     projected = call(
-        bind(add_columns_kernel, place),
+        bind(add_out_kernel, place),
         "add_out",
         spread([out_part] * ny),
-        shape((nx, ny * rows, w_out.shape[1])),
+        shape((ny, nx, rows, cols)),
     )
     up_part, mid = call(
         bind(up_kernel, place),

time: 107 us -> 113 us (1.056)
  waiting for transfers between devices: 50.5 us -> 55.7 us
  Pallas kernels: 10.8 us -> 7.35 us
  starting transfers between devices: 37.1 us -> 39.4 us
  local copies, waits for them, and re-layouts: 6.99 us -> 8.82 us
    ppermute x32, waiting for transfers between devices: 50.5 us -> 55.6 us  [move(): return lax.ppermute(value, ('seq', 'req'), pairs)]
    ppermute x0 -> x2, starting transfers between devices: none -> 3.95 us  [transpose(): return lax.ppermute(value, ('seq', 'req'), pairs)]
    pallas_call x12 -> x13, Pallas kernels: 10.8 us -> 7.35 us  [call(): pl.pallas_call(kernel, name=name, out_shape=outs, in_specs=in_specs or [V...]
    unnamed x32 -> x40, local copies, waits for them, and re-layouts: 6.02 us -> 8.82 us
    ppermute x32, starting transfers between devices: 37.1 us -> 35.4 us  [move(): return lax.ppermute(value, ('seq', 'req'), pairs)]
  transfers between devices with their start and end apart: 32 -> 34, of which waited for: 25 -> 25; matrix products, arithmetic and copies ran while one was open for 1% -> 0% of each run, Pallas kernels for 9% -> 5%
where the time goes in v3:
time: 113 us; the launch traced here: 112 us
  waiting for transfers between devices  55.7 us (49%)
  starting transfers between devices  39.4 us (35%)
  local copies, waits for them, and re-layouts  8.82 us (8%)
  Pallas kernels  7.35 us (7%)
    ppermute x32, waiting for transfers between devices, move(): return lax.ppermute(value, ('seq', 'req'), pairs)  55.6 us
    ppermute x32, starting transfers between devices, move(): return lax.ppermute(value, ('seq', 'req'), pairs)  35.4 us
    unnamed x40, local copies, waits for them, and re-layouts  8.82 us
    pallas_call x13, Pallas kernels, call(): pl.pallas_call(kernel, name=name, out_shape=outs, in_specs=in_specs or [V...  7.35 us
    ppermute x2, starting transfers between devices, transpose(): return lax.ppermute(value, ('seq', 'req'), pairs)  3.95 us
  transfers between devices with their start and end apart: 34, of which 25 were waited for; matrix products, arithmetic and copies ran while one was open for 0% of the time, Pallas kernels for 5%

profile of v3, /device:TPU:0, one launch (start us, length us, event | category | flops | bytes accessed | tf_op | source)
XLA Modules:
  0.0 112.1 jit_solution(1057329980286340196)
XLA Ops:
  1.2 2.6 %collective-permute-start = (bf16[8,4,2048]{2,1,0:T(4,128)(2,1)}, bf16[8,4,2048]{2,1,0:T(4,128)(2,1)S(1)}, u32[]{:S(2)}, u32[]{:S(2)}) collective-permute-start(bf16[8,4,2048]{2,1,0:T(4,128)(2,1)} %refs_0_.1), channel_id=1, source_target_pairs={{0,2},{1,3},{2,0},{3,1},{4,6},{5,7},{6,4},{7,5},{8,10},{9,11},{10,... | collective-permute-start | bytes 393224 | tf_op jit(solution)/shard_map/ppermute | solution.py:62
  4.4 3.6 %collective-permute-done.refs_1_ = bf16[8,4,2048]{2,1,0:T(4,128)(2,1)S(1)} collective-permute-done((bf16[8,4,2048]{2,1,0:T(4,128)(2,1)}, bf16[8,4,2048]{2,1,0:T(4,128)(2,1)S(1)}, u32[]{:S(2)}, u32[]{:S(2)}) %collective-permute-start) | collective-permute-done | bytes 131104 | tf_op jit(solution)/shard_map/ppermute | solution.py:62
  16.2 1.8 %collective-permute-start.4 = (bf16[32,768]{1,0:T(8,128)(2,1)S(1)}, bf16[32,768]{1,0:T(8,128)(2,1)S(1)}, u32[]{:S(2)}, u32[]{:S(2)}) collective-permute-start(bf16[32,768]{1,0:T(8,128)(2,1)S(1)} %get-tuple-element.16), channel_id=1, source_target_pairs={{0,2},{1,3},{2,0},{3,1},{4,6},{5,7},{6,4},{7,5},{8,10},{9,11},{10,... | collective-permute-start | bytes 147464 | tf_op jit(solution)/shard_map/ppermute | solution.py:62
  18.0 1.5 %collective-permute-start.5 = (bf16[32,768]{1,0:T(8,128)(2,1)S(1)}, bf16[32,768]{1,0:T(8,128)(2,1)S(1)}, u32[]{:S(2)}, u32[]{:S(2)}) collective-permute-start(bf16[32,768]{1,0:T(8,128)(2,1)S(1)} %get-tuple-element.15.refs_0_), channel_id=1, source_target_pairs={{0,4},{1,5},{2,6},{3,7},{4,0},{5,1},{6,2},{7,3},{8,12},{9,13},{10,... | collective-permute-start | bytes 147464 | tf_op jit(solution)/shard_map/ppermute | solution.py:62
  20.4 1.9 %collective-permute-done.5.refs_2_ = bf16[32,768]{1,0:T(8,128)(2,1)S(1)} collective-permute-done((bf16[32,768]{1,0:T(8,128)(2,1)S(1)}, bf16[32,768]{1,0:T(8,128)(2,1)S(1)}, u32[]{:S(2)}, u32[]{:S(2)}) %collective-permute-start.5) | collective-permute-done | bytes 49184 | tf_op jit(solution)/shard_map/ppermute | solution.py:62
  22.3 2.2 %collective-permute-done.6.refs_3_ = bf16[32,768]{1,0:T(8,128)(2,1)S(1)} collective-permute-done((bf16[32,768]{1,0:T(8,128)(2,1)S(1)}, bf16[32,768]{1,0:T(8,128)(2,1)S(1)}, u32[]{:S(2)}, u32[]{:S(2)}) %collective-permute-start.6) | collective-permute-done | bytes 49184 | tf_op jit(solution)/shard_map/ppermute | solution.py:62
  24.6 1.6 %collective-permute-start.7 = (bf16[2,32,768]{2,1,0:T(8,128)(2,1)S(1)}, bf16[2,32,768]{2,1,0:T(8,128)(2,1)S(1)}, u32[]{:S(2)}, u32[]{:S(2)}) collective-permute-start(bf16[2,32,768]{2,1,0:T(8,128)(2,1)S(1)} %add_qkv.1.refs_0_), channel_id=1, source_target_pairs={{0,8},{1,9},{2,10},{3,11},{4,12},{5,13},{6,14},{7,15},{8,16},{9,17... | collective-permute-start | bytes 294920 | tf_op jit(solution)/shard_map/ppermute | solution.py:62
  26.2 1.6 %collective-permute-start.14 = (bf16[512,256]{1,0:T(8,128)(2,1)}, bf16[512,256]{1,0:T(8,128)(2,1)S(1)}, u32[]{:S(2)}, u32[]{:S(2)}) collective-permute-start(bf16[512,256]{1,0:T(8,128)(2,1)} %param.32), channel_id=1, source_target_pairs={{0,0},{1,1},{2,4},{3,5},{4,2},{5,3},{6,6},{7,7},{8,8},{9,9},{10,12... | collective-permute-start | bytes 786440 | tf_op jit(solution)/shard_map/ppermute | solution.py:77
  27.8 2.4 %collective-permute-start.16 = (bf16[512,256]{1,0:T(8,128)(2,1)}, bf16[512,256]{1,0:T(8,128)(2,1)S(1)}, u32[]{:S(2)}, u32[]{:S(2)}) collective-permute-start(bf16[512,256]{1,0:T(8,128)(2,1)} %param.32), channel_id=1, source_target_pairs={{0,2},{1,3},{2,6},{3,7},{4,0},{5,1},{6,4},{7,5},{8,10},{9,11},{10,... | collective-permute-start | bytes 786440 | tf_op jit(solution)/shard_map/ppermute | solution.py:77
  31.0 1.7 %collective-permute-start.8 = (bf16[2,32,768]{2,1,0:T(8,128)(2,1)S(1)}, bf16[2,32,768]{2,1,0:T(8,128)(2,1)S(1)}, u32[]{:S(2)}, u32[]{:S(2)}) collective-permute-start(bf16[2,32,768]{2,1,0:T(8,128)(2,1)S(1)} %add_qkv.1.refs_0_), channel_id=1, source_target_pairs={{0,16},{1,17},{2,18},{3,19},{4,20},{5,21},{6,22},{7,23},{8,24},{9,... | collective-permute-start | bytes 294920 | tf_op jit(solution)/shard_map/ppermute | solution.py:62
  32.7 5.7 %collective-permute-done.8.refs_2_ = bf16[2,32,768]{2,1,0:T(8,128)(2,1)S(1)} collective-permute-done((bf16[2,32,768]{2,1,0:T(8,128)(2,1)S(1)}, bf16[2,32,768]{2,1,0:T(8,128)(2,1)S(1)}, u32[]{:S(2)}, u32[]{:S(2)}) %collective-permute-start.8) | collective-permute-done | bytes 98336 | tf_op jit(solution)/shard_map/ppermute | solution.py:62
  38.4 2.0 %collective-permute-start.9 = (bf16[2,32,768]{2,1,0:T(8,128)(2,1)S(1)}, bf16[2,32,768]{2,1,0:T(8,128)(2,1)S(1)}, u32[]{:S(2)}, u32[]{:S(2)}) collective-permute-start(bf16[2,32,768]{2,1,0:T(8,128)(2,1)S(1)} %add_qkv.1.refs_0_), channel_id=1, source_target_pairs={{0,24},{1,25},{2,26},{3,27},{4,28},{5,29},{6,30},{7,31},{8,0},{9,1... | collective-permute-start | bytes 294920 | tf_op jit(solution)/shard_map/ppermute | solution.py:62
  40.4 2.6 %collective-permute-done.9.refs_3_ = bf16[2,32,768]{2,1,0:T(8,128)(2,1)S(1)} collective-permute-done((bf16[2,32,768]{2,1,0:T(8,128)(2,1)S(1)}, bf16[2,32,768]{2,1,0:T(8,128)(2,1)S(1)}, u32[]{:S(2)}, u32[]{:S(2)}) %collective-permute-start.9) | collective-permute-done | bytes 98336 | tf_op jit(solution)/shard_map/ppermute | solution.py:62
  43.0 1.6 %copy-done.1 = bf16[8,64,2048]{2,1,0:T(8,128)(2,1)S(1)} copy-done((bf16[8,64,2048]{2,1,0:T(8,128)(2,1)S(1)}, bf16[8,64,2048]{2,1,0:T(8,128)(2,1)}, u32[]{:S(2)}) %copy-start.1) | copy-done | bytes 2097176
  44.6 3.3 %attention.1 = (bf16[8,64,2048]{2,1,0:T(8,128)(2,1)}, bf16[8,64,2048]{2,1,0:T(8,128)(2,1)}, bf16[32,1152]{1,0:T(8,128)(2,1)S(1)}, bf16[32,1152]{1,0:T(8,128)(2,1)S(1)}) custom-call(bf16[2,32,768]{2,1,0:T(8,128)(2,1)S(1)} %add_qkv.1.refs_0_, bf16[2,32,768]{2,1,0:T(8,128)(2,1)S(1)} %collective-permute-done.7.refs_1_, ...), custom_call_target="tpu_custom_call" | custom-call | tf_op jit(solution)/shard_map/attention/pallas_call | solution.py:100
  48.8 3.6 %collective-permute-done.10.refs_1_ = bf16[32,1152]{1,0:T(8,128)(2,1)S(1)} collective-permute-done((bf16[32,1152]{1,0:T(8,128)(2,1)S(1)}, bf16[32,1152]{1,0:T(8,128)(2,1)S(1)}, u32[]{:S(2)}, u32[]{:S(2)}) %collective-permute-start.10) | collective-permute-done | bytes 73760 | tf_op jit(solution)/shard_map/ppermute | solution.py:62
  52.7 6.1 %collective-permute-done.11.refs_1_ = bf16[32,1152]{1,0:T(8,128)(2,1)S(1)} collective-permute-done((bf16[32,1152]{1,0:T(8,128)(2,1)S(1)}, bf16[32,1152]{1,0:T(8,128)(2,1)S(1)}, u32[]{:S(2)}, u32[]{:S(2)}) %collective-permute-start.11) | collective-permute-done | bytes 73760 | tf_op jit(solution)/shard_map/ppermute | solution.py:62
  59.4 5.0 %collective-permute-done.12.refs_2_ = bf16[32,1152]{1,0:T(8,128)(2,1)S(1)} collective-permute-done((bf16[32,1152]{1,0:T(8,128)(2,1)S(1)}, bf16[32,1152]{1,0:T(8,128)(2,1)S(1)}, u32[]{:S(2)}, u32[]{:S(2)}) %collective-permute-start.12) | collective-permute-done | bytes 73760 | tf_op jit(solution)/shard_map/ppermute | solution.py:62
  64.4 2.7 %collective-permute-start.13 = (bf16[32,1152]{1,0:T(8,128)(2,1)S(1)}, bf16[32,1152]{1,0:T(8,128)(2,1)S(1)}, u32[]{:S(2)}, u32[]{:S(2)}) collective-permute-start(bf16[32,1152]{1,0:T(8,128)(2,1)S(1)} %merge_x.1.refs_0_), channel_id=1, source_target_pairs={{0,24},{1,25},{2,26},{3,27},{4,28},{5,29},{6,30},{7,31},{8,0},{9,1... | collective-permute-start | bytes 221192 | tf_op jit(solution)/shard_map/ppermute | solution.py:62
  67.1 2.2 %collective-permute-done.13.refs_3_ = bf16[32,1152]{1,0:T(8,128)(2,1)S(1)} collective-permute-done((bf16[32,1152]{1,0:T(8,128)(2,1)S(1)}, bf16[32,1152]{1,0:T(8,128)(2,1)S(1)}, u32[]{:S(2)}, u32[]{:S(2)}) %collective-permute-start.13) | collective-permute-done | bytes 73760 | tf_op jit(solution)/shard_map/ppermute | solution.py:62
  70.2 3.4 %collective-permute-start.20 = (bf16[2,32,256]{2,1,0:T(8,128)(2,1)S(1)}, bf16[2,32,256]{2,1,0:T(8,128)(2,1)S(1)}, u32[]{:S(2)}, u32[]{:S(2)}) collective-permute-start(bf16[2,32,256]{2,1,0:T(8,128)(2,1)S(1)} %out.1.refs_0_), channel_id=1, source_target_pairs={{0,6},{1,7},{2,4},{3,5},{4,2},{5,3},{6,0},{7,1},{8,14},{9,15},{10,... | collective-permute-start | bytes 98312 | tf_op jit(solution)/shard_map/ppermute | solution.py:62
  74.0 1.7 %collective-permute-done.20.refs_3_ = bf16[2,32,256]{2,1,0:T(8,128)(2,1)S(1)} collective-permute-done((bf16[2,32,256]{2,1,0:T(8,128)(2,1)S(1)}, bf16[2,32,256]{2,1,0:T(8,128)(2,1)S(1)}, u32[]{:S(2)}, u32[]{:S(2)}) %collective-permute-start.20) | collective-permute-done | bytes 32800 | tf_op jit(solution)/shard_map/ppermute | solution.py:62
  75.9 4.8 %collective-permute-start.22 = (bf16[2,2,32,256]{3,2,1,0:T(8,128)(2,1)S(1)}, bf16[2,2,32,256]{3,2,1,0:T(8,128)(2,1)S(1)}, u32[]{:S(2)}, u32[]{:S(2)}) collective-permute-start(bf16[2,2,32,256]{3,2,1,0:T(8,128)(2,1)S(1)} %add_out.1.refs_2_), channel_id=1, source_target_pairs={{0,16},{1,17},{2,18},{3,19},{4,20},{5,21},{6,22},{7,23},{8,24},{9,... | collective-permute-start | bytes 196616 | tf_op jit(solution)/shard_map/ppermute | solution.py:62
  80.7 1.7 %collective-permute-done.21.refs_3_ = bf16[2,2,32,256]{3,2,1,0:T(8,128)(2,1)S(1)} collective-permute-done((bf16[2,2,32,256]{3,2,1,0:T(8,128)(2,1)S(1)}, bf16[2,2,32,256]{3,2,1,0:T(8,128)(2,1)S(1)}, u32[]{:S(2)}, u32[]{:S(2)}) %collective-permute-start.21) | collective-permute-done | bytes 65568 | tf_op jit(solution)/shard_map/ppermute | solution.py:62
  82.4 1.4 %collective-permute-done.22.refs_4_ = bf16[2,2,32,256]{3,2,1,0:T(8,128)(2,1)S(1)} collective-permute-done((bf16[2,2,32,256]{3,2,1,0:T(8,128)(2,1)S(1)}, bf16[2,2,32,256]{3,2,1,0:T(8,128)(2,1)S(1)}, u32[]{:S(2)}, u32[]{:S(2)}) %collective-permute-start.22) | collective-permute-done | bytes 65568 | tf_op jit(solution)/shard_map/ppermute | solution.py:62
  87.1 3.8 %collective-permute-done.25.refs_1_ = bf16[64,1024]{1,0:T(8,128)(2,1)S(1)} collective-permute-done((bf16[64,1024]{1,0:T(8,128)(2,1)S(1)}, bf16[64,1024]{1,0:T(8,128)(2,1)S(1)}, u32[]{:S(2)}, u32[]{:S(2)}) %collective-permute-start.25) | collective-permute-done | bytes 131104 | tf_op jit(solution)/shard_map/ppermute | solution.py:62
  91.4 1.3 %collective-permute-start.27 = (bf16[64,512]{1,0:T(8,128)(2,1)S(1)}, bf16[64,512]{1,0:T(8,128)(2,1)S(1)}, u32[]{:S(2)}, u32[]{:S(2)}) collective-permute-start(bf16[64,512]{1,0:T(8,128)(2,1)S(1)} %get-tuple-element.21), channel_id=1, source_target_pairs={{0,4},{1,5},{2,6},{3,7},{4,0},{5,1},{6,2},{7,3},{8,12},{9,13},{10,... | collective-permute-start | bytes 196616 | tf_op jit(solution)/shard_map/ppermute | solution.py:62
  92.7 3.1 %collective-permute-done.27.refs_1_ = bf16[64,512]{1,0:T(8,128)(2,1)S(1)} collective-permute-done((bf16[64,512]{1,0:T(8,128)(2,1)S(1)}, bf16[64,512]{1,0:T(8,128)(2,1)S(1)}, u32[]{:S(2)}, u32[]{:S(2)}) %collective-permute-start.27) | collective-permute-done | bytes 65568 | tf_op jit(solution)/shard_map/ppermute | solution.py:62
  96.5 2.7 %collective-permute-start.29 = (bf16[64,512]{1,0:T(8,128)(2,1)S(1)}, bf16[64,512]{1,0:T(8,128)(2,1)S(1)}, u32[]{:S(2)}, u32[]{:S(2)}) collective-permute-start(bf16[64,512]{1,0:T(8,128)(2,1)S(1)} %add_x.1.refs_0_), channel_id=1, source_target_pairs={{0,16},{1,17},{2,18},{3,19},{4,20},{5,21},{6,22},{7,23},{8,24},{9,... | collective-permute-start | bytes 196616 | tf_op jit(solution)/shard_map/ppermute | solution.py:62
  100.0 2.0 %collective-permute-done.28.refs_1_ = bf16[64,512]{1,0:T(8,128)(2,1)S(1)} collective-permute-done((bf16[64,512]{1,0:T(8,128)(2,1)S(1)}, bf16[64,512]{1,0:T(8,128)(2,1)S(1)}, u32[]{:S(2)}, u32[]{:S(2)}) %collective-permute-start.28) | collective-permute-done | bytes 65568 | tf_op jit(solution)/shard_map/ppermute | solution.py:62
  104.8 1.7 %collective-permute-start.32 = (bf16[32,512]{1,0:T(8,128)(2,1)S(1)}, bf16[32,512]{1,0:T(8,128)(2,1)S(1)}, u32[]{:S(2)}, u32[]{:S(2)}) collective-permute-start(bf16[32,512]{1,0:T(8,128)(2,1)S(1)} %get-tuple-element.22.refs_0_), channel_id=1, source_target_pairs={{0,4},{1,5},{2,6},{3,7},{4,0},{5,1},{6,2},{7,3},{8,12},{9,13},{10,... | collective-permute-start | bytes 98312 | tf_op jit(solution)/shard_map/ppermute | solution.py:62
  108.7 2.6 %collective-permute-done.33.refs_3_ = bf16[32,512]{1,0:T(8,128)(2,1)S(1)} collective-permute-done((bf16[32,512]{1,0:T(8,128)(2,1)S(1)}, bf16[32,512]{1,0:T(8,128)(2,1)S(1)}, u32[]{:S(2)}, u32[]{:S(2)}) %collective-permute-start.33) | collective-permute-done | bytes 32800 | tf_op jit(solution)/shard_map/ppermute | solution.py:62
  (89 shorter events, 25.3 us)
Async XLA Ops:
  0.6 84.3 %collective-permute-start.24 = (bf16[512,1024]{1,0:T(8,128)(2,1)}, bf16[512,1024]{1,0:T(8,128)(2,1)S(1)}, u32[]{:S(2)}, u32[]{:S(2)}) collective-permute-start(bf16[512,1024]{1,0:T(8,128)(2,1)} %refs_8_.3), channel_id=1, source_target_pairs={{0,1},{1,0},{2,3},{3,2},{4,5},{5,4},{6,7},{7,6},{8,9},{9,8},{10,11... | collective-permute-start | bytes 3145736 | tf_op jit(solution)/shard_map/ppermute | solution.py:62
  1.2 6.9 %collective-permute-start = (bf16[8,4,2048]{2,1,0:T(4,128)(2,1)}, bf16[8,4,2048]{2,1,0:T(4,128)(2,1)S(1)}, u32[]{:S(2)}, u32[]{:S(2)}) collective-permute-start(bf16[8,4,2048]{2,1,0:T(4,128)(2,1)} %refs_0_.1), channel_id=1, source_target_pairs={{0,2},{1,3},{2,0},{3,1},{4,6},{5,7},{6,4},{7,5},{8,10},{9,11},{10,... | collective-permute-start | bytes 393224 | tf_op jit(solution)/shard_map/ppermute | solution.py:62
  3.8 6.9 %collective-permute-start.1 = (bf16[512,256]{1,0:T(8,128)(2,1)}, bf16[512,256]{1,0:T(8,128)(2,1)S(1)}, u32[]{:S(2)}, u32[]{:S(2)}) collective-permute-start(bf16[512,256]{1,0:T(8,128)(2,1)} %refs_4_.2), channel_id=1, source_target_pairs={{0,1},{1,0},{2,3},{3,2},{4,5},{5,4},{6,7},{7,6},{8,9},{9,8},{10,11... | collective-permute-start | bytes 786440 | tf_op jit(solution)/shard_map/ppermute | solution.py:62
  3.9 6.7 %collective-permute-start.2 = (bf16[512,256]{1,0:T(8,128)(2,1)}, bf16[512,256]{1,0:T(8,128)(2,1)S(1)}, u32[]{:S(2)}, u32[]{:S(2)}) collective-permute-start(bf16[512,256]{1,0:T(8,128)(2,1)} %refs_6_.2), channel_id=1, source_target_pairs={{0,1},{1,0},{2,3},{3,2},{4,5},{5,4},{6,7},{7,6},{8,9},{9,8},{10,11... | collective-permute-start | bytes 786440 | tf_op jit(solution)/shard_map/ppermute | solution.py:62
  4.3 6.4 %collective-permute-start.3 = (bf16[512,256]{1,0:T(8,128)(2,1)}, bf16[512,256]{1,0:T(8,128)(2,1)S(1)}, u32[]{:S(2)}, u32[]{:S(2)}) collective-permute-start(bf16[512,256]{1,0:T(8,128)(2,1)} %refs_8_.2), channel_id=1, source_target_pairs={{0,1},{1,0},{2,3},{3,2},{4,5},{5,4},{6,7},{7,6},{8,9},{9,8},{10,11... | collective-permute-start | bytes 786440 | tf_op jit(solution)/shard_map/ppermute | solution.py:62
  8.1 79.0 %collective-permute-start.26 = (bf16[1024,512]{1,0:T(8,128)(2,1)}, bf16[1024,512]{1,0:T(8,128)(2,1)S(1)}, u32[]{:S(2)}, u32[]{:S(2)}) collective-permute-start(bf16[1024,512]{1,0:T(8,128)(2,1)} %refs_2_.1), channel_id=1, source_target_pairs={{0,1},{1,0},{2,3},{3,2},{4,5},{5,4},{6,7},{7,6},{8,9},{9,8},{10,11... | collective-permute-start | bytes 3145736 | tf_op jit(solution)/shard_map/ppermute | solution.py:62
  16.2 4.2 %collective-permute-start.4 = (bf16[32,768]{1,0:T(8,128)(2,1)S(1)}, bf16[32,768]{1,0:T(8,128)(2,1)S(1)}, u32[]{:S(2)}, u32[]{:S(2)}) collective-permute-start(bf16[32,768]{1,0:T(8,128)(2,1)S(1)} %get-tuple-element.16), channel_id=1, source_target_pairs={{0,2},{1,3},{2,0},{3,1},{4,6},{5,7},{6,4},{7,5},{8,10},{9,11},{10,... | collective-permute-start | bytes 147464 | tf_op jit(solution)/shard_map/ppermute | solution.py:62
  18.0 4.3 %collective-permute-start.5 = (bf16[32,768]{1,0:T(8,128)(2,1)S(1)}, bf16[32,768]{1,0:T(8,128)(2,1)S(1)}, u32[]{:S(2)}, u32[]{:S(2)}) collective-permute-start(bf16[32,768]{1,0:T(8,128)(2,1)S(1)} %get-tuple-element.15.refs_0_), channel_id=1, source_target_pairs={{0,4},{1,5},{2,6},{3,7},{4,0},{5,1},{6,2},{7,3},{8,12},{9,13},{10,... | collective-permute-start | bytes 147464 | tf_op jit(solution)/shard_map/ppermute | solution.py:62
  19.5 5.0 %collective-permute-start.6 = (bf16[32,768]{1,0:T(8,128)(2,1)S(1)}, bf16[32,768]{1,0:T(8,128)(2,1)S(1)}, u32[]{:S(2)}, u32[]{:S(2)}) collective-permute-start(bf16[32,768]{1,0:T(8,128)(2,1)S(1)} %get-tuple-element.16), channel_id=1, source_target_pairs={{0,6},{1,7},{2,4},{3,5},{4,2},{5,3},{6,0},{7,1},{8,14},{9,15},{10,... | collective-permute-start | bytes 147464 | tf_op jit(solution)/shard_map/ppermute | solution.py:62
  24.6 6.5 %collective-permute-start.7 = (bf16[2,32,768]{2,1,0:T(8,128)(2,1)S(1)}, bf16[2,32,768]{2,1,0:T(8,128)(2,1)S(1)}, u32[]{:S(2)}, u32[]{:S(2)}) collective-permute-start(bf16[2,32,768]{2,1,0:T(8,128)(2,1)S(1)} %add_qkv.1.refs_0_), channel_id=1, source_target_pairs={{0,8},{1,9},{2,10},{3,11},{4,12},{5,13},{6,14},{7,15},{8,16},{9,17... | collective-permute-start | bytes 294920 | tf_op jit(solution)/shard_map/ppermute | solution.py:62
  26.2 22.1 %collective-permute-start.14 = (bf16[512,256]{1,0:T(8,128)(2,1)}, bf16[512,256]{1,0:T(8,128)(2,1)S(1)}, u32[]{:S(2)}, u32[]{:S(2)}) collective-permute-start(bf16[512,256]{1,0:T(8,128)(2,1)} %param.32), channel_id=1, source_target_pairs={{0,0},{1,1},{2,4},{3,5},{4,2},{5,3},{6,6},{7,7},{8,8},{9,9},{10,12... | collective-permute-start | bytes 786440 | tf_op jit(solution)/shard_map/ppermute | solution.py:77
  27.8 20.5 %collective-permute-start.16 = (bf16[512,256]{1,0:T(8,128)(2,1)}, bf16[512,256]{1,0:T(8,128)(2,1)S(1)}, u32[]{:S(2)}, u32[]{:S(2)}) collective-permute-start(bf16[512,256]{1,0:T(8,128)(2,1)} %param.32), channel_id=1, source_target_pairs={{0,2},{1,3},{2,6},{3,7},{4,0},{5,1},{6,4},{7,5},{8,10},{9,11},{10,... | collective-permute-start | bytes 786440 | tf_op jit(solution)/shard_map/ppermute | solution.py:77
  31.0 7.4 %collective-permute-start.8 = (bf16[2,32,768]{2,1,0:T(8,128)(2,1)S(1)}, bf16[2,32,768]{2,1,0:T(8,128)(2,1)S(1)}, u32[]{:S(2)}, u32[]{:S(2)}) collective-permute-start(bf16[2,32,768]{2,1,0:T(8,128)(2,1)S(1)} %add_qkv.1.refs_0_), channel_id=1, source_target_pairs={{0,16},{1,17},{2,18},{3,19},{4,20},{5,21},{6,22},{7,23},{8,24},{9,... | collective-permute-start | bytes 294920 | tf_op jit(solution)/shard_map/ppermute | solution.py:62
  38.4 4.6 %collective-permute-start.9 = (bf16[2,32,768]{2,1,0:T(8,128)(2,1)S(1)}, bf16[2,32,768]{2,1,0:T(8,128)(2,1)S(1)}, u32[]{:S(2)}, u32[]{:S(2)}) collective-permute-start(bf16[2,32,768]{2,1,0:T(8,128)(2,1)S(1)} %add_qkv.1.refs_0_), channel_id=1, source_target_pairs={{0,24},{1,25},{2,26},{3,27},{4,28},{5,29},{6,30},{7,31},{8,0},{9,1... | collective-permute-start | bytes 294920 | tf_op jit(solution)/shard_map/ppermute | solution.py:62
  48.0 4.4 %collective-permute-start.10 = (bf16[32,1152]{1,0:T(8,128)(2,1)S(1)}, bf16[32,1152]{1,0:T(8,128)(2,1)S(1)}, u32[]{:S(2)}, u32[]{:S(2)}) collective-permute-start(bf16[32,1152]{1,0:T(8,128)(2,1)S(1)} %get-tuple-element.18), channel_id=1, source_target_pairs={{0,4},{1,5},{2,6},{3,7},{4,0},{5,1},{6,2},{7,3},{8,12},{9,13},{10,... | collective-permute-start | bytes 221192 | tf_op jit(solution)/shard_map/ppermute | solution.py:62
  48.3 21.4 %collective-permute-start.15 = (bf16[512,256]{1,0:T(8,128)(2,1)S(1)}, bf16[512,256]{1,0:T(8,128)(2,1)S(1)}, u32[]{:S(2)}, u32[]{:S(2)}) collective-permute-start(bf16[512,256]{1,0:T(8,128)(2,1)S(1)} %collective-permute-done.14.refs_0_), channel_id=1, source_target_pairs={{0,1},{1,0},{2,3},{3,2},{4,5},{5,4},{6,7},{7,6},{8,9},{9,8},{10,11... | collective-permute-start | bytes 786440 | tf_op jit(solution)/shard_map/ppermute | solution.py:62
  48.3 21.4 %collective-permute-start.17 = (bf16[512,256]{1,0:T(8,128)(2,1)S(1)}, bf16[512,256]{1,0:T(8,128)(2,1)S(1)}, u32[]{:S(2)}, u32[]{:S(2)}) collective-permute-start(bf16[512,256]{1,0:T(8,128)(2,1)S(1)} %collective-permute-done.16.refs_2_), channel_id=1, source_target_pairs={{0,1},{1,0},{2,3},{3,2},{4,5},{5,4},{6,7},{7,6},{8,9},{9,8},{10,11... | collective-permute-start | bytes 786440 | tf_op jit(solution)/shard_map/ppermute | solution.py:62
  52.6 6.2 %collective-permute-start.11 = (bf16[32,1152]{1,0:T(8,128)(2,1)S(1)}, bf16[32,1152]{1,0:T(8,128)(2,1)S(1)}, u32[]{:S(2)}, u32[]{:S(2)}) collective-permute-start(bf16[32,1152]{1,0:T(8,128)(2,1)S(1)} %merge_x.1.refs_0_), channel_id=1, source_target_pairs={{0,8},{1,9},{2,10},{3,11},{4,12},{5,13},{6,14},{7,15},{8,16},{9,17... | collective-permute-start | bytes 221192 | tf_op jit(solution)/shard_map/ppermute | solution.py:62
  58.9 5.5 %collective-permute-start.12 = (bf16[32,1152]{1,0:T(8,128)(2,1)S(1)}, bf16[32,1152]{1,0:T(8,128)(2,1)S(1)}, u32[]{:S(2)}, u32[]{:S(2)}) collective-permute-start(bf16[32,1152]{1,0:T(8,128)(2,1)S(1)} %merge_x.1.refs_0_), channel_id=1, source_target_pairs={{0,16},{1,17},{2,18},{3,19},{4,20},{5,21},{6,22},{7,23},{8,24},{9,... | collective-permute-start | bytes 221192 | tf_op jit(solution)/shard_map/ppermute | solution.py:62
  64.4 4.9 %collective-permute-start.13 = (bf16[32,1152]{1,0:T(8,128)(2,1)S(1)}, bf16[32,1152]{1,0:T(8,128)(2,1)S(1)}, u32[]{:S(2)}, u32[]{:S(2)}) collective-permute-start(bf16[32,1152]{1,0:T(8,128)(2,1)S(1)} %merge_x.1.refs_0_), channel_id=1, source_target_pairs={{0,24},{1,25},{2,26},{3,27},{4,28},{5,29},{6,30},{7,31},{8,0},{9,1... | collective-permute-start | bytes 221192 | tf_op jit(solution)/shard_map/ppermute | solution.py:62
  70.0 4.0 %collective-permute-start.18 = (bf16[2,32,256]{2,1,0:T(8,128)(2,1)S(1)}, bf16[2,32,256]{2,1,0:T(8,128)(2,1)S(1)}, u32[]{:S(2)}, u32[]{:S(2)}) collective-permute-start(bf16[2,32,256]{2,1,0:T(8,128)(2,1)S(1)} %out.1.refs_0_), channel_id=1, source_target_pairs={{0,2},{1,3},{2,0},{3,1},{4,6},{5,7},{6,4},{7,5},{8,10},{9,11},{10,... | collective-permute-start | bytes 98312 | tf_op jit(solution)/shard_map/ppermute | solution.py:62
  70.1 4.0 %collective-permute-start.19 = (bf16[2,32,256]{2,1,0:T(8,128)(2,1)S(1)}, bf16[2,32,256]{2,1,0:T(8,128)(2,1)S(1)}, u32[]{:S(2)}, u32[]{:S(2)}) collective-permute-start(bf16[2,32,256]{2,1,0:T(8,128)(2,1)S(1)} %out.1.refs_0_), channel_id=1, source_target_pairs={{0,4},{1,5},{2,6},{3,7},{4,0},{5,1},{6,2},{7,3},{8,12},{9,13},{10,... | collective-permute-start | bytes 98312 | tf_op jit(solution)/shard_map/ppermute | solution.py:62
  70.2 5.6 %collective-permute-start.20 = (bf16[2,32,256]{2,1,0:T(8,128)(2,1)S(1)}, bf16[2,32,256]{2,1,0:T(8,128)(2,1)S(1)}, u32[]{:S(2)}, u32[]{:S(2)}) collective-permute-start(bf16[2,32,256]{2,1,0:T(8,128)(2,1)S(1)} %out.1.refs_0_), channel_id=1, source_target_pairs={{0,6},{1,7},{2,4},{3,5},{4,2},{5,3},{6,0},{7,1},{8,14},{9,15},{10,... | collective-permute-start | bytes 98312 | tf_op jit(solution)/shard_map/ppermute | solution.py:62
  75.8 6.6 %collective-permute-start.21 = (bf16[2,2,32,256]{3,2,1,0:T(8,128)(2,1)S(1)}, bf16[2,2,32,256]{3,2,1,0:T(8,128)(2,1)S(1)}, u32[]{:S(2)}, u32[]{:S(2)}) collective-permute-start(bf16[2,2,32,256]{3,2,1,0:T(8,128)(2,1)S(1)} %add_out.1.refs_2_), channel_id=1, source_target_pairs={{0,8},{1,9},{2,10},{3,11},{4,12},{5,13},{6,14},{7,15},{8,16},{9,17... | collective-permute-start | bytes 196616 | tf_op jit(solution)/shard_map/ppermute | solution.py:62
  75.9 7.9 %collective-permute-start.22 = (bf16[2,2,32,256]{3,2,1,0:T(8,128)(2,1)S(1)}, bf16[2,2,32,256]{3,2,1,0:T(8,128)(2,1)S(1)}, u32[]{:S(2)}, u32[]{:S(2)}) collective-permute-start(bf16[2,2,32,256]{3,2,1,0:T(8,128)(2,1)S(1)} %add_out.1.refs_2_), channel_id=1, source_target_pairs={{0,16},{1,17},{2,18},{3,19},{4,20},{5,21},{6,22},{7,23},{8,24},{9,... | collective-permute-start | bytes 196616 | tf_op jit(solution)/shard_map/ppermute | solution.py:62
  80.7 4.3 %collective-permute-start.23 = (bf16[2,2,32,256]{3,2,1,0:T(8,128)(2,1)S(1)}, bf16[2,2,32,256]{3,2,1,0:T(8,128)(2,1)S(1)}, u32[]{:S(2)}, u32[]{:S(2)}) collective-permute-start(bf16[2,2,32,256]{3,2,1,0:T(8,128)(2,1)S(1)} %add_out.1.refs_2_), channel_id=1, source_target_pairs={{0,24},{1,25},{2,26},{3,27},{4,28},{5,29},{6,30},{7,31},{8,0},{9,1... | collective-permute-start | bytes 196616 | tf_op jit(solution)/shard_map/ppermute | solution.py:62
  85.9 5.0 %collective-permute-start.25 = (bf16[64,1024]{1,0:T(8,128)(2,1)S(1)}, bf16[64,1024]{1,0:T(8,128)(2,1)S(1)}, u32[]{:S(2)}, u32[]{:S(2)}) collective-permute-start(bf16[64,1024]{1,0:T(8,128)(2,1)S(1)} %get-tuple-element.19.refs_0_), channel_id=1, source_target_pairs={{0,2},{1,3},{2,0},{3,1},{4,6},{5,7},{6,4},{7,5},{8,10},{9,11},{10,... | collective-permute-start | bytes 393224 | tf_op jit(solution)/shard_map/ppermute | solution.py:62
  91.4 4.3 %collective-permute-start.27 = (bf16[64,512]{1,0:T(8,128)(2,1)S(1)}, bf16[64,512]{1,0:T(8,128)(2,1)S(1)}, u32[]{:S(2)}, u32[]{:S(2)}) collective-permute-start(bf16[64,512]{1,0:T(8,128)(2,1)S(1)} %get-tuple-element.21), channel_id=1, source_target_pairs={{0,4},{1,5},{2,6},{3,7},{4,0},{5,1},{6,2},{7,3},{8,12},{9,13},{10,... | collective-permute-start | bytes 196616 | tf_op jit(solution)/shard_map/ppermute | solution.py:62
  95.8 6.2 %collective-permute-start.28 = (bf16[64,512]{1,0:T(8,128)(2,1)S(1)}, bf16[64,512]{1,0:T(8,128)(2,1)S(1)}, u32[]{:S(2)}, u32[]{:S(2)}) collective-permute-start(bf16[64,512]{1,0:T(8,128)(2,1)S(1)} %add_x.1.refs_0_), channel_id=1, source_target_pairs={{0,8},{1,9},{2,10},{3,11},{4,12},{5,13},{6,14},{7,15},{8,16},{9,17... | collective-permute-start | bytes 196616 | tf_op jit(solution)/shard_map/ppermute | solution.py:62
  96.5 6.6 %collective-permute-start.29 = (bf16[64,512]{1,0:T(8,128)(2,1)S(1)}, bf16[64,512]{1,0:T(8,128)(2,1)S(1)}, u32[]{:S(2)}, u32[]{:S(2)}) collective-permute-start(bf16[64,512]{1,0:T(8,128)(2,1)S(1)} %add_x.1.refs_0_), channel_id=1, source_target_pairs={{0,16},{1,17},{2,18},{3,19},{4,20},{5,21},{6,22},{7,23},{8,24},{9,... | collective-permute-start | bytes 196616 | tf_op jit(solution)/shard_map/ppermute | solution.py:62
  99.2 4.6 %collective-permute-start.30 = (bf16[64,512]{1,0:T(8,128)(2,1)S(1)}, bf16[64,512]{1,0:T(8,128)(2,1)S(1)}, u32[]{:S(2)}, u32[]{:S(2)}) collective-permute-start(bf16[64,512]{1,0:T(8,128)(2,1)S(1)} %add_x.1.refs_0_), channel_id=1, source_target_pairs={{0,24},{1,25},{2,26},{3,27},{4,28},{5,29},{6,30},{7,31},{8,0},{9,1... | collective-permute-start | bytes 196616 | tf_op jit(solution)/shard_map/ppermute | solution.py:62
  106.6 4.8 %collective-permute-start.33 = (bf16[32,512]{1,0:T(8,128)(2,1)S(1)}, bf16[32,512]{1,0:T(8,128)(2,1)S(1)}, u32[]{:S(2)}, u32[]{:S(2)}) collective-permute-start(bf16[32,512]{1,0:T(8,128)(2,1)S(1)} %get-tuple-element.23), channel_id=1, source_target_pairs={{0,6},{1,7},{2,4},{3,5},{4,2},{5,3},{6,0},{7,1},{8,14},{9,15},{10,... | collective-permute-start | bytes 98312 | tf_op jit(solution)/shard_map/ppermute | solution.py:62
  (22 other events, 475.3 us)

commit v4 on v3

--- a/solution.py
+++ b/solution.py
@@ -42,8 +42,8 @@
     def y_before(self, dy):
         return lax.rem(self.y() + self.ny - dy, self.ny)
 
-    def z_before(self, dz):
-        return lax.rem(lax.div(lax.axis_index("seq"), self.nx) + self.nz - dz, self.nz)
+    def z_partner(self, dz):
+        return lax.bitwise_xor(lax.div(lax.axis_index("seq"), self.nx), dz)
 
     def move(self, value, dx=0, dy=0, dc=0, dz=0):
         pairs = []
@@ -52,7 +52,7 @@
                 for y in range(self.ny):
                     for c in range(CORES):
                         to_x, to_y, to_c = (x + dx) % self.nx, (y + dy) % self.ny, (c + dc) % CORES
-                        to_z = (z + dz) % self.nz
+                        to_z = z ^ dz
                         pairs.append(
                             (
                                 ((z * self.nx + x) * self.ny + y) * CORES + c,
@@ -94,7 +94,7 @@
     return pl.ds(pl.multiple_of(index * size, size), size)
 
 
-def call(kernel, name, ins, outs, in_specs=None, out_specs=None, scratch=()):
+def call(kernel, name, ins, outs, in_specs=None, out_specs=None, scratch=(), moved=2**20, limit=20):
     single = not isinstance(outs, (list, tuple))
     specs = out_specs or (VMEM if single else [VMEM] * len(outs))
     return pl.pallas_call(
@@ -104,7 +104,8 @@
         in_specs=in_specs or [VMEM] * len(ins),
         out_specs=specs,
         scratch_shapes=list(scratch),
-        compiler_params=pltpu.CompilerParams(vmem_limit_bytes=20 * 1024 * 1024),
+        cost_estimate=pl.CostEstimate(flops=0, bytes_accessed=moved, transcendentals=0),
+        compiler_params=pltpu.CompilerParams(vmem_limit_bytes=limit * 1024 * 1024),
     )(*ins)
 
 
@@ -129,32 +130,43 @@
         flat[start + i * steps : start + (i + 1) * steps, :] = block[i].astype(F32)
 
 
-def norm_kernel(tokens, gain, shift, out, flat):
+def norm_kernel(tokens, scales, *refs):
+    count = (len(refs) - 3) // 2
+    weights, out, kept = refs[:count], refs[count], refs[count + 1 : 2 * count + 1]
+    flat, sems = refs[-2:]
+    copies = [
+        pltpu.make_async_copy(source, target, sems.at[k])
+        for k, (source, target) in enumerate(zip(weights, kept))
+    ]
+    for copy in copies:
+        copy.start()
+    width = out.shape[1]
     flatten(tokens, flat, 0)
-    out[...] = layer_norm(flat[...], gain[...], shift[...]).astype(BF16)
+    out[...] = layer_norm(flat[...], scales[:, :width], scales[:, width:]).astype(BF16)
+    for copy in copies:
+        copy.wait()
 
 
 def qkv_kernel(place, *refs):
     ny = place.ny
     mine = refs[0]
     toks = refs[1:ny]
-    gain, shift = refs[ny : ny + 2]
+    scales, biases = refs[ny : ny + 2]
     weights = refs[ny + 2 : ny + 8]
-    biases = refs[ny + 8 : ny + 11]
-    outs = refs[ny + 11 : 2 * ny + 11]
-    flat, normed = refs[2 * ny + 11 :]
-    rows = mine.shape[0]
+    outs = refs[ny + 8 : 2 * ny + 8]
+    flat, normed = refs[2 * ny + 8 :]
+    rows, width = mine.shape
     normed[:rows, :] = mine[...]
     for j, tok in enumerate(toks):
         flatten(tok, flat, j * rows)
-    normed[rows:, :] = layer_norm(flat[...], gain[...], shift[...]).astype(BF16)
+    normed[rows:, :] = layer_norm(flat[...], scales[:, :width], scales[:, width:]).astype(BF16)
     cols = weights[0].shape[1]
     for k in range(3):
-        acc = two_halves(normed, weights[2 * k], weights[2 * k + 1])
+        acc = two_halves(normed, weights[k], weights[3 + k])
         for j in range(ny):
             part = acc[j * rows : (j + 1) * rows]
             if j == 0:
-                part = part + biases[k][...]
+                part = part + biases[:, k * cols : (k + 1) * cols]
             outs[(ny - j) % ny][:, k * cols : (k + 1) * cols] = part.astype(BF16)
 
 
@@ -204,7 +216,7 @@
         for copy in coming(i):
             copy.start()
     for dz in range(nz):
-        span = at(place.z_before(dz), nx * cols)
+        span = at(place.z_partner(dz), nx * cols)
         for k, target in enumerate((qs, ks, vs)):
             target[:, span] = side_by_side(gathered[dz], k * cols, cols)
     window = min(32, slots)
@@ -364,7 +376,7 @@
     rows = group * steps
     cols = gathered[0].shape[3]
     for dz in range(nz):
-        span = at(place.z_before(dz), place.nx * cols)
+        span = at(place.z_partner(dz), place.nx * cols)
         for y in range(ny):
             proj[y * rows : (y + 1) * rows, span] = side_by_side(gathered[dz].at[y], 0, cols)
     for j in range(ny):
@@ -468,34 +480,37 @@
 
     toks = [tokens] + [place.move(tokens, dy=dy) for dy in range(1, ny)]
     cols = w_query.shape[1]
-    weights = []
-    for weight in (w_query, w_key, w_value):
-        weights += [weight, place.move(weight, dc=1)]
-    gain, shift = row(norm1_gain), row(norm1_bias)
-    normed = call(
+    own = [w_query, w_key, w_value]
+    siblings = [place.move(weight, dc=1) for weight in own]
+    scales = row(jnp.concatenate([norm1_gain, norm1_bias]))
+    biases = row(jnp.concatenate([b_query, b_key, b_value]))
+    normed, *own = call(
         norm_kernel,
         "norm",
-        [tokens, gain, shift],
-        shape((rows, width)),
-        scratch=[pltpu.VMEM((rows, width), F32)],
+        [tokens, scales, *own],
+        [shape((rows, width))] + [shape(w.shape) for w in own],
+        in_specs=[VMEM] * 2 + [HBM] * 3,
+        scratch=[pltpu.VMEM((rows, width), F32), pltpu.SemaphoreType.DMA((3,))],
     )
     parts = call(
         bind(qkv_kernel, place),
         "norm_qkv",
-        [normed, *toks[1:], gain, shift, *weights, row(b_query), row(b_key), row(b_value)],
+        [normed, *toks[1:], scales, biases, *own, *siblings],
         [shape((rows, 3 * cols))] * ny,
         scratch=[pltpu.VMEM(((ny - 1) * rows, width), F32), pltpu.VMEM((ny * rows, width), BF16)],
     )
-    w_outs = []
-    for k in range(nx):
-        block = place.transpose(w_out, k)
-        w_outs += [block, place.move(block, dc=1)]
-    w_up_sibling = place.move(w_up, dc=1)
-    w_down_sibling = place.move(w_down, dc=1)
+    *parts, tied_up, tied_down = lax.optimization_barrier((*parts, w_up, w_down))
+    w_up_sibling = place.move(tied_up, dc=1)
+    w_down_sibling = place.move(tied_down, dc=1)
     qkv = call(
         bind(add_columns_kernel, place), "add_qkv", spread(parts), shape((nx, rows, 3 * cols))
     )
 
+    qkv, w_up_sibling, w_down_sibling = lax.optimization_barrier(
+        (qkv, w_up_sibling, w_down_sibling)
+    )
+    qkv, tied_w_out = lax.optimization_barrier((qkv, w_out))
+    blocks = [place.transpose(tied_w_out, k) for k in range(nx)]
     pack = max(1, min(group, 256 // slots))
     new_keys, new_values, *messages = call(
         bind(attention_kernel, place, heads, steps),
@@ -516,11 +531,17 @@
             pltpu.SemaphoreType.DMA((2, group)),
             pltpu.SemaphoreType.DMA((2, group)),
         ],
-    )
+        limit=52,
+    )
+    *messages, blocks = lax.optimization_barrier((*messages, blocks))
+    w_outs = []
+    for block in blocks:
+        w_outs += [block, place.move(block, dc=1)]
     messages = [messages[0]] + [place.move(messages[dx], dx=dx) for dx in range(1, nx)]
     merged = call(
         bind(merge_x_kernel, place, heads), "merge_x", messages, shape((rows, share + LANES))
     )
+    merged, *w_outs = lax.optimization_barrier((merged, *w_outs))
     attn = call(
         bind(merge_z_kernel, place, heads), "merge_z", place.gather_z(merged), shape((rows, share))
     )

time: 113 us -> 92.6 us (0.82)
  waiting for transfers between devices: 55.7 us -> 36.7 us
  local copies, waits for them, and re-layouts: 8.82 us -> 3.81 us
  Pallas kernels: 7.35 us -> 9.05 us
  other arithmetic: 0 us -> 1.44 us
    ppermute x32, waiting for transfers between devices: 55.6 us -> 36.7 us  [move(): return lax.ppermute(value, ('seq', 'req'), pairs)]
    unnamed x40 -> x28, local copies, waits for them, and re-layouts: 8.82 us -> 3.81 us
    ppermute x32, starting transfers between devices: 35.4 us -> 38.7 us  [move(): return lax.ppermute(value, ('seq', 'req'), pairs)]
    ppermute x2, starting transfers between devices: 3.95 us -> 1.76 us  [transpose(): return lax.ppermute(value, ('seq', 'req'), pairs)]
    pallas_call x13, Pallas kernels: 7.35 us -> 9.05 us  [call(): pl.pallas_call(kernel, name=name, out_shape=outs, in_specs=in_specs or [V...]
    concatenate x0 -> x2, other arithmetic: none -> 1.44 us  [the longest x1 0.72 us: body(): biases = row(jnp.concatenate([b_query, b_key, b_value]))]
  transfers between devices with their start and end apart: 34 -> 34, of which waited for: 25 -> 18; matrix products, arithmetic and copies ran while one was open for 0% -> 2% of each run, Pallas kernels for 5% -> 6%
where the time goes in v4:
time: 92.6 us; the launch traced here: 92.3 us
  starting transfers between devices  40.5 us (44%)
  waiting for transfers between devices  36.7 us (40%)
  Pallas kernels  9.05 us (10%)
  local copies, waits for them, and re-layouts  3.81 us (4%)
  other arithmetic  1.44 us (2%)
  between operations  0.94 us (1%)
    ppermute x32, starting transfers between devices, move(): return lax.ppermute(value, ('seq', 'req'), pairs)  38.7 us
    ppermute x32, waiting for transfers between devices, move(): return lax.ppermute(value, ('seq', 'req'), pairs)  36.7 us
    pallas_call x13, Pallas kernels, call(): pl.pallas_call(kernel, name=name, out_shape=outs, in_specs=in_specs or [V...  9.05 us
    unnamed x28, local copies, waits for them, and re-layouts  3.81 us
  transfers between devices with their start and end apart: 34, of which 18 were waited for; matrix products, arithmetic and copies ran while one was open for 2% of the time, Pallas kernels for 6%

profile of v4, /device:TPU:0, one launch (start us, length us, event | category | flops | bytes accessed | tf_op | source)
XLA Modules:
  0.0 92.3 jit_solution(17014971006840779690)
XLA Ops:
  1.7 2.6 %collective-permute-start = (bf16[8,4,2048]{2,1,0:T(4,128)(2,1)}, bf16[8,4,2048]{2,1,0:T(4,128)(2,1)S(1)}, u32[]{:S(2)}, u32[]{:S(2)}) collective-permute-start(bf16[8,4,2048]{2,1,0:T(4,128)(2,1)} %refs_0_.3), channel_id=1, source_target_pairs={{0,2},{1,3},{2,0},{3,1},{4,6},{5,7},{6,4},{7,5},{8,10},{9,11},{10,... | collective-permute-start | bytes 393224 | tf_op jit(solution)/shard_map/ppermute | solution.py:62
  11.1 1.5 %collective-permute-start.5 = (bf16[32,768]{1,0:T(8,128)(2,1)S(1)}, bf16[32,768]{1,0:T(8,128)(2,1)S(1)}, u32[]{:S(2)}, u32[]{:S(2)}) collective-permute-start(bf16[32,768]{1,0:T(8,128)(2,1)S(1)} %get-tuple-element.43.refs_0_), channel_id=1, source_target_pairs={{0,4},{1,5},{2,6},{3,7},{4,0},{5,1},{6,2},{7,3},{8,12},{9,13},{10,... | collective-permute-start | bytes 147464 | tf_op jit(solution)/shard_map/ppermute | solution.py:62
  13.0 1.6 %collective-permute-start.4 = (bf16[32,768]{1,0:T(8,128)(2,1)S(1)}, bf16[32,768]{1,0:T(8,128)(2,1)S(1)}, u32[]{:S(2)}, u32[]{:S(2)}) collective-permute-start(bf16[32,768]{1,0:T(8,128)(2,1)S(1)} %get-tuple-element.44), channel_id=1, source_target_pairs={{0,2},{1,3},{2,0},{3,1},{4,6},{5,7},{6,4},{7,5},{8,10},{9,11},{10,... | collective-permute-start | bytes 147464 | tf_op jit(solution)/shard_map/ppermute | solution.py:62
  15.5 2.2 %collective-permute-done.6.refs_3_ = bf16[32,768]{1,0:T(8,128)(2,1)S(1)} collective-permute-done((bf16[32,768]{1,0:T(8,128)(2,1)S(1)}, bf16[32,768]{1,0:T(8,128)(2,1)S(1)}, u32[]{:S(2)}, u32[]{:S(2)}) %collective-permute-start.6) | collective-permute-done | bytes 49184 | tf_op jit(solution)/shard_map/ppermute | solution.py:62
  17.8 1.1 %collective-permute-start.13 = (bf16[512,256]{1,0:T(8,128)(2,1)S(1)}, bf16[512,256]{1,0:T(8,128)(2,1)S(1)}, u32[]{:S(2)}, u32[]{:S(2)}) collective-permute-start(bf16[512,256]{1,0:T(8,128)(2,1)S(1)} %copy-done.13), channel_id=1, source_target_pairs={{0,2},{1,3},{2,6},{3,7},{4,0},{5,1},{6,4},{7,5},{8,10},{9,11},{10,... | collective-permute-start | bytes 786440 | tf_op jit(solution)/shard_map/ppermute | solution.py:77
  19.5 3.7 %collective-permute-start.11 = (bf16[2,32,768]{2,1,0:T(8,128)(2,1)S(1)}, bf16[2,32,768]{2,1,0:T(8,128)(2,1)S(1)}, u32[]{:S(2)}, u32[]{:S(2)}) collective-permute-start(bf16[2,32,768]{2,1,0:T(8,128)(2,1)S(1)} %add_qkv.1.refs_0_), channel_id=1, source_target_pairs={{0,24},{1,25},{2,26},{3,27},{4,28},{5,29},{6,30},{7,31},{8,16},{9,... | collective-permute-start | bytes 294920 | tf_op jit(solution)/shard_map/ppermute | solution.py:62
  24.0 2.9 %collective-permute-done.11.refs_3_ = bf16[2,32,768]{2,1,0:T(8,128)(2,1)S(1)} collective-permute-done((bf16[2,32,768]{2,1,0:T(8,128)(2,1)S(1)}, bf16[2,32,768]{2,1,0:T(8,128)(2,1)S(1)}, u32[]{:S(2)}, u32[]{:S(2)}) %collective-permute-start.11) | collective-permute-done | bytes 98336 | tf_op jit(solution)/shard_map/ppermute | solution.py:62
  26.9 4.0 %collective-permute-done.10.refs_2_ = bf16[2,32,768]{2,1,0:T(8,128)(2,1)S(1)} collective-permute-done((bf16[2,32,768]{2,1,0:T(8,128)(2,1)S(1)}, bf16[2,32,768]{2,1,0:T(8,128)(2,1)S(1)}, u32[]{:S(2)}, u32[]{:S(2)}) %collective-permute-start.10) | collective-permute-done | bytes 98336 | tf_op jit(solution)/shard_map/ppermute | solution.py:62
  30.9 4.9 %attention.1 = (bf16[8,64,2048]{2,1,0:T(8,128)(2,1)}, bf16[8,64,2048]{2,1,0:T(8,128)(2,1)}, bf16[32,1152]{1,0:T(8,128)(2,1)S(1)}, bf16[32,1152]{1,0:T(8,128)(2,1)S(1)}) custom-call(bf16[2,32,768]{2,1,0:T(8,128)(2,1)S(1)} %add_qkv.1.refs_0_, bf16[2,32,768]{2,1,0:T(8,128)(2,1)S(1)} %collective-permute-done.9.refs_1_, ...), custom_call_target="tpu_custom_call" | custom-call | bytes 1048576 | tf_op jit(solution)/shard_map/attention/pallas_call | solution.py:100
  36.4 3.3 %collective-permute-start.14 = (bf16[32,1152]{1,0:T(8,128)(2,1)S(1)}, bf16[32,1152]{1,0:T(8,128)(2,1)S(1)}, u32[]{:S(2)}, u32[]{:S(2)}) collective-permute-start(bf16[32,1152]{1,0:T(8,128)(2,1)S(1)} %get-tuple-element.53), channel_id=1, source_target_pairs={{0,4},{1,5},{2,6},{3,7},{4,0},{5,1},{6,2},{7,3},{8,12},{9,13},{10,... | collective-permute-start | bytes 221192 | tf_op jit(solution)/shard_map/ppermute | solution.py:62
  39.7 2.5 %collective-permute-done.14.refs_1_ = bf16[32,1152]{1,0:T(8,128)(2,1)S(1)} collective-permute-done((bf16[32,1152]{1,0:T(8,128)(2,1)S(1)}, bf16[32,1152]{1,0:T(8,128)(2,1)S(1)}, u32[]{:S(2)}, u32[]{:S(2)}) %collective-permute-start.14) | collective-permute-done | bytes 73760 | tf_op jit(solution)/shard_map/ppermute | solution.py:62
  42.5 2.5 %collective-permute-start.19 = (bf16[32,1152]{1,0:T(8,128)(2,1)S(1)}, bf16[32,1152]{1,0:T(8,128)(2,1)S(1)}, u32[]{:S(2)}, u32[]{:S(2)}) collective-permute-start(bf16[32,1152]{1,0:T(8,128)(2,1)S(1)} %merge_x.1.refs_0_), channel_id=1, source_target_pairs={{0,24},{1,25},{2,26},{3,27},{4,28},{5,29},{6,30},{7,31},{8,16},{9,... | collective-permute-start | bytes 221192 | tf_op jit(solution)/shard_map/ppermute | solution.py:62
  45.0 2.0 %collective-permute-start.17 = (bf16[32,1152]{1,0:T(8,128)(2,1)S(1)}, bf16[32,1152]{1,0:T(8,128)(2,1)S(1)}, u32[]{:S(2)}, u32[]{:S(2)}) collective-permute-start(bf16[32,1152]{1,0:T(8,128)(2,1)S(1)} %merge_x.1.refs_0_), channel_id=1, source_target_pairs={{0,8},{1,9},{2,10},{3,11},{4,12},{5,13},{6,14},{7,15},{8,0},{9,1},... | collective-permute-start | bytes 221192 | tf_op jit(solution)/shard_map/ppermute | solution.py:62
  47.0 2.1 %collective-permute-done.19.refs_3_ = bf16[32,1152]{1,0:T(8,128)(2,1)S(1)} collective-permute-done((bf16[32,1152]{1,0:T(8,128)(2,1)S(1)}, bf16[32,1152]{1,0:T(8,128)(2,1)S(1)}, u32[]{:S(2)}, u32[]{:S(2)}) %collective-permute-start.19) | collective-permute-done | bytes 73760 | tf_op jit(solution)/shard_map/ppermute | solution.py:62
  49.0 2.5 %collective-permute-done.18.refs_2_ = bf16[32,1152]{1,0:T(8,128)(2,1)S(1)} collective-permute-done((bf16[32,1152]{1,0:T(8,128)(2,1)S(1)}, bf16[32,1152]{1,0:T(8,128)(2,1)S(1)}, u32[]{:S(2)}, u32[]{:S(2)}) %collective-permute-start.18) | collective-permute-done | bytes 73760 | tf_op jit(solution)/shard_map/ppermute | solution.py:62
  53.3 1.6 %collective-permute-start.21 = (bf16[2,32,256]{2,1,0:T(8,128)(2,1)S(1)}, bf16[2,32,256]{2,1,0:T(8,128)(2,1)S(1)}, u32[]{:S(2)}, u32[]{:S(2)}) collective-permute-start(bf16[2,32,256]{2,1,0:T(8,128)(2,1)S(1)} %out.1.refs_0_), channel_id=1, source_target_pairs={{0,4},{1,5},{2,6},{3,7},{4,0},{5,1},{6,2},{7,3},{8,12},{9,13},{10,... | collective-permute-start | bytes 98312 | tf_op jit(solution)/shard_map/ppermute | solution.py:62
  55.8 1.6 %collective-permute-done.22.refs_3_ = bf16[2,32,256]{2,1,0:T(8,128)(2,1)S(1)} collective-permute-done((bf16[2,32,256]{2,1,0:T(8,128)(2,1)S(1)}, bf16[2,32,256]{2,1,0:T(8,128)(2,1)S(1)}, u32[]{:S(2)}, u32[]{:S(2)}) %collective-permute-start.22) | collective-permute-done | bytes 32800 | tf_op jit(solution)/shard_map/ppermute | solution.py:62
  57.4 1.4 %collective-permute-done.20.refs_1_ = bf16[2,32,256]{2,1,0:T(8,128)(2,1)S(1)} collective-permute-done((bf16[2,32,256]{2,1,0:T(8,128)(2,1)S(1)}, bf16[2,32,256]{2,1,0:T(8,128)(2,1)S(1)}, u32[]{:S(2)}, u32[]{:S(2)}) %collective-permute-start.20) | collective-permute-done | bytes 32800 | tf_op jit(solution)/shard_map/ppermute | solution.py:62
  58.8 2.0 %collective-permute-start.25 = (bf16[2,2,32,256]{3,2,1,0:T(8,128)(2,1)S(1)}, bf16[2,2,32,256]{3,2,1,0:T(8,128)(2,1)S(1)}, u32[]{:S(2)}, u32[]{:S(2)}) collective-permute-start(bf16[2,2,32,256]{3,2,1,0:T(8,128)(2,1)S(1)} %add_out.1.refs_2_), channel_id=1, source_target_pairs={{0,24},{1,25},{2,26},{3,27},{4,28},{5,29},{6,30},{7,31},{8,16},{9,... | collective-permute-start | bytes 196616 | tf_op jit(solution)/shard_map/ppermute | solution.py:62
  60.8 2.5 %collective-permute-start.23 = (bf16[2,2,32,256]{3,2,1,0:T(8,128)(2,1)S(1)}, bf16[2,2,32,256]{3,2,1,0:T(8,128)(2,1)S(1)}, u32[]{:S(2)}, u32[]{:S(2)}) collective-permute-start(bf16[2,2,32,256]{3,2,1,0:T(8,128)(2,1)S(1)} %add_out.1.refs_2_), channel_id=1, source_target_pairs={{0,8},{1,9},{2,10},{3,11},{4,12},{5,13},{6,14},{7,15},{8,0},{9,1},... | collective-permute-start | bytes 196616 | tf_op jit(solution)/shard_map/ppermute | solution.py:62
  63.3 1.7 %collective-permute-done.25.refs_5_ = bf16[2,2,32,256]{3,2,1,0:T(8,128)(2,1)S(1)} collective-permute-done((bf16[2,2,32,256]{3,2,1,0:T(8,128)(2,1)S(1)}, bf16[2,2,32,256]{3,2,1,0:T(8,128)(2,1)S(1)}, u32[]{:S(2)}, u32[]{:S(2)}) %collective-permute-start.25) | collective-permute-done | bytes 65568 | tf_op jit(solution)/shard_map/ppermute | solution.py:62
  64.9 1.4 %collective-permute-done.24.refs_4_ = bf16[2,2,32,256]{3,2,1,0:T(8,128)(2,1)S(1)} collective-permute-done((bf16[2,2,32,256]{3,2,1,0:T(8,128)(2,1)S(1)}, bf16[2,2,32,256]{3,2,1,0:T(8,128)(2,1)S(1)}, u32[]{:S(2)}, u32[]{:S(2)}) %collective-permute-start.24) | collective-permute-done | bytes 65568 | tf_op jit(solution)/shard_map/ppermute | solution.py:62
  67.3 1.5 %collective-permute-start.26 = (bf16[64,1024]{1,0:T(8,128)(2,1)S(1)}, bf16[64,1024]{1,0:T(8,128)(2,1)S(1)}, u32[]{:S(2)}, u32[]{:S(2)}) collective-permute-start(bf16[64,1024]{1,0:T(8,128)(2,1)S(1)} %get-tuple-element.62.refs_0_), channel_id=1, source_target_pairs={{0,2},{1,3},{2,0},{3,1},{4,6},{5,7},{6,4},{7,5},{8,10},{9,11},{10,... | collective-permute-start | bytes 393224 | tf_op jit(solution)/shard_map/ppermute | solution.py:62
  68.7 3.5 %collective-permute-done.26.refs_1_ = bf16[64,1024]{1,0:T(8,128)(2,1)S(1)} collective-permute-done((bf16[64,1024]{1,0:T(8,128)(2,1)S(1)}, bf16[64,1024]{1,0:T(8,128)(2,1)S(1)}, u32[]{:S(2)}, u32[]{:S(2)}) %collective-permute-start.26) | collective-permute-done | bytes 131104 | tf_op jit(solution)/shard_map/ppermute | solution.py:62
  73.5 3.6 %collective-permute-done.27.refs_1_ = bf16[64,512]{1,0:T(8,128)(2,1)S(1)} collective-permute-done((bf16[64,512]{1,0:T(8,128)(2,1)S(1)}, bf16[64,512]{1,0:T(8,128)(2,1)S(1)}, u32[]{:S(2)}, u32[]{:S(2)}) %collective-permute-start.27) | collective-permute-done | bytes 65568 | tf_op jit(solution)/shard_map/ppermute | solution.py:62
  77.1 2.0 %collective-permute-start.30 = (bf16[64,512]{1,0:T(8,128)(2,1)S(1)}, bf16[64,512]{1,0:T(8,128)(2,1)S(1)}, u32[]{:S(2)}, u32[]{:S(2)}) collective-permute-start(bf16[64,512]{1,0:T(8,128)(2,1)S(1)} %add_x.1.refs_0_), channel_id=1, source_target_pairs={{0,24},{1,25},{2,26},{3,27},{4,28},{5,29},{6,30},{7,31},{8,16},{9,... | collective-permute-start | bytes 196616 | tf_op jit(solution)/shard_map/ppermute | solution.py:62
  79.9 1.7 %collective-permute-start.28 = (bf16[64,512]{1,0:T(8,128)(2,1)S(1)}, bf16[64,512]{1,0:T(8,128)(2,1)S(1)}, u32[]{:S(2)}, u32[]{:S(2)}) collective-permute-start(bf16[64,512]{1,0:T(8,128)(2,1)S(1)} %add_x.1.refs_0_), channel_id=1, source_target_pairs={{0,8},{1,9},{2,10},{3,11},{4,12},{5,13},{6,14},{7,15},{8,0},{9,1},... | collective-permute-start | bytes 196616 | tf_op jit(solution)/shard_map/ppermute | solution.py:62
  81.6 1.7 %collective-permute-done.30.refs_3_ = bf16[64,512]{1,0:T(8,128)(2,1)S(1)} collective-permute-done((bf16[64,512]{1,0:T(8,128)(2,1)S(1)}, bf16[64,512]{1,0:T(8,128)(2,1)S(1)}, u32[]{:S(2)}, u32[]{:S(2)}) %collective-permute-start.30) | collective-permute-done | bytes 65568 | tf_op jit(solution)/shard_map/ppermute | solution.py:62
  83.3 1.5 %collective-permute-done.29.refs_2_ = bf16[64,512]{1,0:T(8,128)(2,1)S(1)} collective-permute-done((bf16[64,512]{1,0:T(8,128)(2,1)S(1)}, bf16[64,512]{1,0:T(8,128)(2,1)S(1)}, u32[]{:S(2)}, u32[]{:S(2)}) %collective-permute-start.29) | collective-permute-done | bytes 65568 | tf_op jit(solution)/shard_map/ppermute | solution.py:62
  85.6 2.1 %collective-permute-start.33 = (bf16[32,512]{1,0:T(8,128)(2,1)S(1)}, bf16[32,512]{1,0:T(8,128)(2,1)S(1)}, u32[]{:S(2)}, u32[]{:S(2)}) collective-permute-start(bf16[32,512]{1,0:T(8,128)(2,1)S(1)} %get-tuple-element.67), channel_id=1, source_target_pairs={{0,6},{1,7},{2,4},{3,5},{4,2},{5,3},{6,0},{7,1},{8,14},{9,15},{10,... | collective-permute-start | bytes 98312 | tf_op jit(solution)/shard_map/ppermute | solution.py:62
  88.9 1.5 %collective-permute-done.33.refs_3_ = bf16[32,512]{1,0:T(8,128)(2,1)S(1)} collective-permute-done((bf16[32,512]{1,0:T(8,128)(2,1)S(1)}, bf16[32,512]{1,0:T(8,128)(2,1)S(1)}, u32[]{:S(2)}, u32[]{:S(2)}) %collective-permute-start.33) | collective-permute-done | bytes 32800 | tf_op jit(solution)/shard_map/ppermute | solution.py:62
  90.4 1.2 %collective-permute-done.31.refs_1_ = bf16[32,512]{1,0:T(8,128)(2,1)S(1)} collective-permute-done((bf16[32,512]{1,0:T(8,128)(2,1)S(1)}, bf16[32,512]{1,0:T(8,128)(2,1)S(1)}, u32[]{:S(2)}, u32[]{:S(2)}) %collective-permute-start.31) | collective-permute-done | bytes 32800 | tf_op jit(solution)/shard_map/ppermute | solution.py:62
  (80 shorter events, 19.7 us)
Async XLA Ops:
  0.7 9.2 %collective-permute-start.1 = (bf16[512,256]{1,0:T(8,128)(2,1)}, bf16[512,256]{1,0:T(8,128)(2,1)S(1)}, u32[]{:S(2)}, u32[]{:S(2)}) collective-permute-start(bf16[512,256]{1,0:T(8,128)(2,1)} %refs_0_.2), channel_id=1, source_target_pairs={{0,1},{1,0},{2,3},{3,2},{4,5},{5,4},{6,7},{7,6},{8,9},{9,8},{10,11... | collective-permute-start | bytes 786440 | tf_op jit(solution)/shard_map/ppermute | solution.py:62
  1.2 8.7 %collective-permute-start.2 = (bf16[512,256]{1,0:T(8,128)(2,1)}, bf16[512,256]{1,0:T(8,128)(2,1)S(1)}, u32[]{:S(2)}, u32[]{:S(2)}) collective-permute-start(bf16[512,256]{1,0:T(8,128)(2,1)} %refs_1_.1), channel_id=1, source_target_pairs={{0,1},{1,0},{2,3},{3,2},{4,5},{5,4},{6,7},{7,6},{8,9},{9,8},{10,11... | collective-permute-start | bytes 786440 | tf_op jit(solution)/shard_map/ppermute | solution.py:62
  1.3 8.6 %collective-permute-start.3 = (bf16[512,256]{1,0:T(8,128)(2,1)}, bf16[512,256]{1,0:T(8,128)(2,1)S(1)}, u32[]{:S(2)}, u32[]{:S(2)}) collective-permute-start(bf16[512,256]{1,0:T(8,128)(2,1)} %refs_2_.2), channel_id=1, source_target_pairs={{0,1},{1,0},{2,3},{3,2},{4,5},{5,4},{6,7},{7,6},{8,9},{9,8},{10,11... | collective-permute-start | bytes 786440 | tf_op jit(solution)/shard_map/ppermute | solution.py:62
  1.7 8.2 %collective-permute-start = (bf16[8,4,2048]{2,1,0:T(4,128)(2,1)}, bf16[8,4,2048]{2,1,0:T(4,128)(2,1)S(1)}, u32[]{:S(2)}, u32[]{:S(2)}) collective-permute-start(bf16[8,4,2048]{2,1,0:T(4,128)(2,1)} %refs_0_.3), channel_id=1, source_target_pairs={{0,2},{1,3},{2,0},{3,1},{4,6},{5,7},{6,4},{7,5},{8,10},{9,11},{10,... | collective-permute-start | bytes 393224 | tf_op jit(solution)/shard_map/ppermute | solution.py:62
  10.5 7.2 %collective-permute-start.7 = (bf16[512,1024]{1,0:T(8,128)(2,1)S(1)}, bf16[512,1024]{1,0:T(8,128)(2,1)S(1)}, u32[]{:S(2)}, u32[]{:S(2)}) collective-permute-start(bf16[512,1024]{1,0:T(8,128)(2,1)S(1)} %copy-done), channel_id=1, source_target_pairs={{0,1},{1,0},{2,3},{3,2},{4,5},{5,4},{6,7},{7,6},{8,9},{9,8},{10,11... | collective-permute-start | bytes 3145736 | tf_op jit(solution)/shard_map/ppermute | solution.py:62
  10.8 7.0 %collective-permute-start.8 = (bf16[1024,512]{1,0:T(8,128)(2,1)S(1)}, bf16[1024,512]{1,0:T(8,128)(2,1)S(1)}, u32[]{:S(2)}, u32[]{:S(2)}) collective-permute-start(bf16[1024,512]{1,0:T(8,128)(2,1)S(1)} %copy-done.1), channel_id=1, source_target_pairs={{0,1},{1,0},{2,3},{3,2},{4,5},{5,4},{6,7},{7,6},{8,9},{9,8},{10,11... | collective-permute-start | bytes 3145736 | tf_op jit(solution)/shard_map/ppermute | solution.py:62
  11.1 4.4 %collective-permute-start.5 = (bf16[32,768]{1,0:T(8,128)(2,1)S(1)}, bf16[32,768]{1,0:T(8,128)(2,1)S(1)}, u32[]{:S(2)}, u32[]{:S(2)}) collective-permute-start(bf16[32,768]{1,0:T(8,128)(2,1)S(1)} %get-tuple-element.43.refs_0_), channel_id=1, source_target_pairs={{0,4},{1,5},{2,6},{3,7},{4,0},{5,1},{6,2},{7,3},{8,12},{9,13},{10,... | collective-permute-start | bytes 147464 | tf_op jit(solution)/shard_map/ppermute | solution.py:62
  12.6 5.1 %collective-permute-start.6 = (bf16[32,768]{1,0:T(8,128)(2,1)S(1)}, bf16[32,768]{1,0:T(8,128)(2,1)S(1)}, u32[]{:S(2)}, u32[]{:S(2)}) collective-permute-start(bf16[32,768]{1,0:T(8,128)(2,1)S(1)} %get-tuple-element.44), channel_id=1, source_target_pairs={{0,6},{1,7},{2,4},{3,5},{4,2},{5,3},{6,0},{7,1},{8,14},{9,15},{10,... | collective-permute-start | bytes 147464 | tf_op jit(solution)/shard_map/ppermute | solution.py:62
  13.0 4.6 %collective-permute-start.4 = (bf16[32,768]{1,0:T(8,128)(2,1)S(1)}, bf16[32,768]{1,0:T(8,128)(2,1)S(1)}, u32[]{:S(2)}, u32[]{:S(2)}) collective-permute-start(bf16[32,768]{1,0:T(8,128)(2,1)S(1)} %get-tuple-element.44), channel_id=1, source_target_pairs={{0,2},{1,3},{2,0},{3,1},{4,6},{5,7},{6,4},{7,5},{8,10},{9,11},{10,... | collective-permute-start | bytes 147464 | tf_op jit(solution)/shard_map/ppermute | solution.py:62
  17.8 18.0 %collective-permute-start.13 = (bf16[512,256]{1,0:T(8,128)(2,1)S(1)}, bf16[512,256]{1,0:T(8,128)(2,1)S(1)}, u32[]{:S(2)}, u32[]{:S(2)}) collective-permute-start(bf16[512,256]{1,0:T(8,128)(2,1)S(1)} %copy-done.13), channel_id=1, source_target_pairs={{0,2},{1,3},{2,6},{3,7},{4,0},{5,1},{6,4},{7,5},{8,10},{9,11},{10,... | collective-permute-start | bytes 786440 | tf_op jit(solution)/shard_map/ppermute | solution.py:77
  18.9 16.9 %collective-permute-start.12 = (bf16[512,256]{1,0:T(8,128)(2,1)S(1)}, bf16[512,256]{1,0:T(8,128)(2,1)S(1)}, u32[]{:S(2)}, u32[]{:S(2)}) collective-permute-start(bf16[512,256]{1,0:T(8,128)(2,1)S(1)} %copy-done.13), channel_id=1, source_target_pairs={{0,0},{1,1},{2,4},{3,5},{4,2},{5,3},{6,6},{7,7},{8,8},{9,9},{10,12... | collective-permute-start | bytes 786440 | tf_op jit(solution)/shard_map/ppermute | solution.py:77
  19.5 7.3 %collective-permute-start.11 = (bf16[2,32,768]{2,1,0:T(8,128)(2,1)S(1)}, bf16[2,32,768]{2,1,0:T(8,128)(2,1)S(1)}, u32[]{:S(2)}, u32[]{:S(2)}) collective-permute-start(bf16[2,32,768]{2,1,0:T(8,128)(2,1)S(1)} %add_qkv.1.refs_0_), channel_id=1, source_target_pairs={{0,24},{1,25},{2,26},{3,27},{4,28},{5,29},{6,30},{7,31},{8,16},{9,... | collective-permute-start | bytes 294920 | tf_op jit(solution)/shard_map/ppermute | solution.py:62
  23.2 7.7 %collective-permute-start.10 = (bf16[2,32,768]{2,1,0:T(8,128)(2,1)S(1)}, bf16[2,32,768]{2,1,0:T(8,128)(2,1)S(1)}, u32[]{:S(2)}, u32[]{:S(2)}) collective-permute-start(bf16[2,32,768]{2,1,0:T(8,128)(2,1)S(1)} %add_qkv.1.refs_0_), channel_id=1, source_target_pairs={{0,16},{1,17},{2,18},{3,19},{4,20},{5,21},{6,22},{7,23},{8,24},{9,... | collective-permute-start | bytes 294920 | tf_op jit(solution)/shard_map/ppermute | solution.py:62
  23.2 7.7 %collective-permute-start.9 = (bf16[2,32,768]{2,1,0:T(8,128)(2,1)S(1)}, bf16[2,32,768]{2,1,0:T(8,128)(2,1)S(1)}, u32[]{:S(2)}, u32[]{:S(2)}) collective-permute-start(bf16[2,32,768]{2,1,0:T(8,128)(2,1)S(1)} %add_qkv.1.refs_0_), channel_id=1, source_target_pairs={{0,8},{1,9},{2,10},{3,11},{4,12},{5,13},{6,14},{7,15},{8,0},{9,1},... | collective-permute-start | bytes 294920 | tf_op jit(solution)/shard_map/ppermute | solution.py:62
  35.8 6.7 %collective-permute-start.15 = (bf16[512,256]{1,0:T(8,128)(2,1)S(1)}, bf16[512,256]{1,0:T(8,128)(2,1)S(1)}, u32[]{:S(2)}, u32[]{:S(2)}) collective-permute-start(bf16[512,256]{1,0:T(8,128)(2,1)S(1)} %collective-permute-done.12.refs_0_), channel_id=1, source_target_pairs={{0,1},{1,0},{2,3},{3,2},{4,5},{5,4},{6,7},{7,6},{8,9},{9,8},{10,11... | collective-permute-start | bytes 786440 | tf_op jit(solution)/shard_map/ppermute | solution.py:62
  35.9 6.6 %collective-permute-start.16 = (bf16[512,256]{1,0:T(8,128)(2,1)S(1)}, bf16[512,256]{1,0:T(8,128)(2,1)S(1)}, u32[]{:S(2)}, u32[]{:S(2)}) collective-permute-start(bf16[512,256]{1,0:T(8,128)(2,1)S(1)} %collective-permute-done.13.refs_2_), channel_id=1, source_target_pairs={{0,1},{1,0},{2,3},{3,2},{4,5},{5,4},{6,7},{7,6},{8,9},{9,8},{10,11... | collective-permute-start | bytes 786440 | tf_op jit(solution)/shard_map/ppermute | solution.py:62
  36.4 5.8 %collective-permute-start.14 = (bf16[32,1152]{1,0:T(8,128)(2,1)S(1)}, bf16[32,1152]{1,0:T(8,128)(2,1)S(1)}, u32[]{:S(2)}, u32[]{:S(2)}) collective-permute-start(bf16[32,1152]{1,0:T(8,128)(2,1)S(1)} %get-tuple-element.53), channel_id=1, source_target_pairs={{0,4},{1,5},{2,6},{3,7},{4,0},{5,1},{6,2},{7,3},{8,12},{9,13},{10,... | collective-permute-start | bytes 221192 | tf_op jit(solution)/shard_map/ppermute | solution.py:62
  42.5 6.5 %collective-permute-start.19 = (bf16[32,1152]{1,0:T(8,128)(2,1)S(1)}, bf16[32,1152]{1,0:T(8,128)(2,1)S(1)}, u32[]{:S(2)}, u32[]{:S(2)}) collective-permute-start(bf16[32,1152]{1,0:T(8,128)(2,1)S(1)} %merge_x.1.refs_0_), channel_id=1, source_target_pairs={{0,24},{1,25},{2,26},{3,27},{4,28},{5,29},{6,30},{7,31},{8,16},{9,... | collective-permute-start | bytes 221192 | tf_op jit(solution)/shard_map/ppermute | solution.py:62
  45.0 6.5 %collective-permute-start.18 = (bf16[32,1152]{1,0:T(8,128)(2,1)S(1)}, bf16[32,1152]{1,0:T(8,128)(2,1)S(1)}, u32[]{:S(2)}, u32[]{:S(2)}) collective-permute-start(bf16[32,1152]{1,0:T(8,128)(2,1)S(1)} %merge_x.1.refs_0_), channel_id=1, source_target_pairs={{0,16},{1,17},{2,18},{3,19},{4,20},{5,21},{6,22},{7,23},{8,24},{9,... | collective-permute-start | bytes 221192 | tf_op jit(solution)/shard_map/ppermute | solution.py:62
  45.0 6.5 %collective-permute-start.17 = (bf16[32,1152]{1,0:T(8,128)(2,1)S(1)}, bf16[32,1152]{1,0:T(8,128)(2,1)S(1)}, u32[]{:S(2)}, u32[]{:S(2)}) collective-permute-start(bf16[32,1152]{1,0:T(8,128)(2,1)S(1)} %merge_x.1.refs_0_), channel_id=1, source_target_pairs={{0,8},{1,9},{2,10},{3,11},{4,12},{5,13},{6,14},{7,15},{8,0},{9,1},... | collective-permute-start | bytes 221192 | tf_op jit(solution)/shard_map/ppermute | solution.py:62
  52.2 5.2 %collective-permute-start.22 = (bf16[2,32,256]{2,1,0:T(8,128)(2,1)S(1)}, bf16[2,32,256]{2,1,0:T(8,128)(2,1)S(1)}, u32[]{:S(2)}, u32[]{:S(2)}) collective-permute-start(bf16[2,32,256]{2,1,0:T(8,128)(2,1)S(1)} %out.1.refs_0_), channel_id=1, source_target_pairs={{0,6},{1,7},{2,4},{3,5},{4,2},{5,3},{6,0},{7,1},{8,14},{9,15},{10,... | collective-permute-start | bytes 98312 | tf_op jit(solution)/shard_map/ppermute | solution.py:62
  53.3 4.1 %collective-permute-start.21 = (bf16[2,32,256]{2,1,0:T(8,128)(2,1)S(1)}, bf16[2,32,256]{2,1,0:T(8,128)(2,1)S(1)}, u32[]{:S(2)}, u32[]{:S(2)}) collective-permute-start(bf16[2,32,256]{2,1,0:T(8,128)(2,1)S(1)} %out.1.refs_0_), channel_id=1, source_target_pairs={{0,4},{1,5},{2,6},{3,7},{4,0},{5,1},{6,2},{7,3},{8,12},{9,13},{10,... | collective-permute-start | bytes 98312 | tf_op jit(solution)/shard_map/ppermute | solution.py:62
  58.8 6.1 %collective-permute-start.25 = (bf16[2,2,32,256]{3,2,1,0:T(8,128)(2,1)S(1)}, bf16[2,2,32,256]{3,2,1,0:T(8,128)(2,1)S(1)}, u32[]{:S(2)}, u32[]{:S(2)}) collective-permute-start(bf16[2,2,32,256]{3,2,1,0:T(8,128)(2,1)S(1)} %add_out.1.refs_2_), channel_id=1, source_target_pairs={{0,24},{1,25},{2,26},{3,27},{4,28},{5,29},{6,30},{7,31},{8,16},{9,... | collective-permute-start | bytes 196616 | tf_op jit(solution)/shard_map/ppermute | solution.py:62
  60.8 5.5 %collective-permute-start.24 = (bf16[2,2,32,256]{3,2,1,0:T(8,128)(2,1)S(1)}, bf16[2,2,32,256]{3,2,1,0:T(8,128)(2,1)S(1)}, u32[]{:S(2)}, u32[]{:S(2)}) collective-permute-start(bf16[2,2,32,256]{3,2,1,0:T(8,128)(2,1)S(1)} %add_out.1.refs_2_), channel_id=1, source_target_pairs={{0,16},{1,17},{2,18},{3,19},{4,20},{5,21},{6,22},{7,23},{8,24},{9,... | collective-permute-start | bytes 196616 | tf_op jit(solution)/shard_map/ppermute | solution.py:62
  60.8 5.5 %collective-permute-start.23 = (bf16[2,2,32,256]{3,2,1,0:T(8,128)(2,1)S(1)}, bf16[2,2,32,256]{3,2,1,0:T(8,128)(2,1)S(1)}, u32[]{:S(2)}, u32[]{:S(2)}) collective-permute-start(bf16[2,2,32,256]{3,2,1,0:T(8,128)(2,1)S(1)} %add_out.1.refs_2_), channel_id=1, source_target_pairs={{0,8},{1,9},{2,10},{3,11},{4,12},{5,13},{6,14},{7,15},{8,0},{9,1},... | collective-permute-start | bytes 196616 | tf_op jit(solution)/shard_map/ppermute | solution.py:62
  67.3 5.0 %collective-permute-start.26 = (bf16[64,1024]{1,0:T(8,128)(2,1)S(1)}, bf16[64,1024]{1,0:T(8,128)(2,1)S(1)}, u32[]{:S(2)}, u32[]{:S(2)}) collective-permute-start(bf16[64,1024]{1,0:T(8,128)(2,1)S(1)} %get-tuple-element.62.refs_0_), channel_id=1, source_target_pairs={{0,2},{1,3},{2,0},{3,1},{4,6},{5,7},{6,4},{7,5},{8,10},{9,11},{10,... | collective-permute-start | bytes 393224 | tf_op jit(solution)/shard_map/ppermute | solution.py:62
  72.8 4.3 %collective-permute-start.27 = (bf16[64,512]{1,0:T(8,128)(2,1)S(1)}, bf16[64,512]{1,0:T(8,128)(2,1)S(1)}, u32[]{:S(2)}, u32[]{:S(2)}) collective-permute-start(bf16[64,512]{1,0:T(8,128)(2,1)S(1)} %get-tuple-element.65), channel_id=1, source_target_pairs={{0,4},{1,5},{2,6},{3,7},{4,0},{5,1},{6,2},{7,3},{8,12},{9,13},{10,... | collective-permute-start | bytes 196616 | tf_op jit(solution)/shard_map/ppermute | solution.py:62
  77.1 6.1 %collective-permute-start.30 = (bf16[64,512]{1,0:T(8,128)(2,1)S(1)}, bf16[64,512]{1,0:T(8,128)(2,1)S(1)}, u32[]{:S(2)}, u32[]{:S(2)}) collective-permute-start(bf16[64,512]{1,0:T(8,128)(2,1)S(1)} %add_x.1.refs_0_), channel_id=1, source_target_pairs={{0,24},{1,25},{2,26},{3,27},{4,28},{5,29},{6,30},{7,31},{8,16},{9,... | collective-permute-start | bytes 196616 | tf_op jit(solution)/shard_map/ppermute | solution.py:62
  79.2 5.7 %collective-permute-start.29 = (bf16[64,512]{1,0:T(8,128)(2,1)S(1)}, bf16[64,512]{1,0:T(8,128)(2,1)S(1)}, u32[]{:S(2)}, u32[]{:S(2)}) collective-permute-start(bf16[64,512]{1,0:T(8,128)(2,1)S(1)} %add_x.1.refs_0_), channel_id=1, source_target_pairs={{0,16},{1,17},{2,18},{3,19},{4,20},{5,21},{6,22},{7,23},{8,24},{9,... | collective-permute-start | bytes 196616 | tf_op jit(solution)/shard_map/ppermute | solution.py:62
  79.9 5.0 %collective-permute-start.28 = (bf16[64,512]{1,0:T(8,128)(2,1)S(1)}, bf16[64,512]{1,0:T(8,128)(2,1)S(1)}, u32[]{:S(2)}, u32[]{:S(2)}) collective-permute-start(bf16[64,512]{1,0:T(8,128)(2,1)S(1)} %add_x.1.refs_0_), channel_id=1, source_target_pairs={{0,8},{1,9},{2,10},{3,11},{4,12},{5,13},{6,14},{7,15},{8,0},{9,1},... | collective-permute-start | bytes 196616 | tf_op jit(solution)/shard_map/ppermute | solution.py:62
  84.9 4.0 %collective-permute-start.32 = (bf16[32,512]{1,0:T(8,128)(2,1)S(1)}, bf16[32,512]{1,0:T(8,128)(2,1)S(1)}, u32[]{:S(2)}, u32[]{:S(2)}) collective-permute-start(bf16[32,512]{1,0:T(8,128)(2,1)S(1)} %get-tuple-element.66.refs_0_), channel_id=1, source_target_pairs={{0,4},{1,5},{2,6},{3,7},{4,0},{5,1},{6,2},{7,3},{8,12},{9,13},{10,... | collective-permute-start | bytes 98312 | tf_op jit(solution)/shard_map/ppermute | solution.py:62
  85.6 4.8 %collective-permute-start.33 = (bf16[32,512]{1,0:T(8,128)(2,1)S(1)}, bf16[32,512]{1,0:T(8,128)(2,1)S(1)}, u32[]{:S(2)}, u32[]{:S(2)}) collective-permute-start(bf16[32,512]{1,0:T(8,128)(2,1)S(1)} %get-tuple-element.67), channel_id=1, source_target_pairs={{0,6},{1,7},{2,4},{3,5},{4,2},{5,3},{6,0},{7,1},{8,14},{9,15},{10,... | collective-permute-start | bytes 98312 | tf_op jit(solution)/shard_map/ppermute | solution.py:62
  (16 other events, 315.3 us)

commit v5 on v4

--- a/solution.py
+++ b/solution.py
@@ -358,79 +358,60 @@
     out[...] = total[...].astype(BF16)
 
 
-def add_out_kernel(place, *refs):
-    out = refs[-1]
-    for dy in range(place.ny):
-        total = refs[dy][...].astype(F32)
-        for dx in range(1, place.nx):
-            total = total + refs[dx * place.ny + dy][...].astype(F32)
-        out[place.y_before(dy)] = total.astype(BF16)
-
-
-def up_kernel(place, *refs):
-    ny, nz = place.ny, place.nz
-    toks = refs[:ny]
-    gathered = refs[ny : ny + nz]
-    gain, shift, own, sibling, bias, out, mid_out, proj, normed, flat = refs[ny + nz :]
-    group, steps, _ = toks[0].shape
-    rows = group * steps
-    cols = gathered[0].shape[3]
+def feed_kernel(place, *refs):
+    nx, nz = place.nx, place.nz
+    blocks = CORES * place.ny
+    tokens = refs[0]
+    gathered = refs[1 : 1 + nz]
+    gain, shift, bias = refs[1 + nz : 4 + nz]
+    ups = refs[4 + nz : 4 + nz + blocks]
+    downs = refs[4 + nz + blocks : 4 + nz + 2 * blocks]
+    outs = refs[4 + nz + 2 * blocks : 4 + nz + 2 * blocks + nx]
+    mid_out, proj, normed, flat, feed = refs[4 + nz + 2 * blocks + nx :]
+    cols = gathered[0].shape[2]
     for dz in range(nz):
-        span = at(place.z_partner(dz), place.nx * cols)
-        for y in range(ny):
-            proj[y * rows : (y + 1) * rows, span] = side_by_side(gathered[dz].at[y], 0, cols)
-    for j in range(ny):
-        here = at(place.y_before(j), rows)
-        flatten(toks[j], flat, 0)
-        mid = flat[...] + proj[here, :]
-        if j == 0:
-            mid_out[...] = mid
-        normed[here, :] = layer_norm(mid, gain[...], shift[...]).astype(BF16)
-    first = (place.y() == 0).astype(F32)
-    out[...] = (two_halves(normed, own, sibling) + bias[...] * first).astype(BF16)
-
-
-def down_kernel(place, *refs):
-    nx, ny = place.nx, place.ny
-    parts = refs[:ny]
-    own, sibling = refs[ny : ny + 2]
-    outs = refs[ny + 2 : ny + 2 + nx]
-    feed = refs[-1]
-    total = sum(p[...].astype(F32) for p in parts)
+        proj[:, at(place.z_partner(dz), nx * cols)] = side_by_side(gathered[dz], 0, cols)
+    flatten(tokens, flat, 0)
+    mid = flat[...] + proj[...]
+    mid_out[...] = mid
+    normed[...] = layer_norm(mid, gain[...], shift[...]).astype(BF16)
+    depth = ups[0].shape[0]
+    owners = [
+        place.y_before(dy) * CORES + lax.rem(place.core() + dc, CORES)
+        for dy in range(place.ny)
+        for dc in range(CORES)
+    ]
+    total = bias[...]
+    for owner, up in zip(owners, ups):
+        total = total + dot(normed[:, at(owner, depth)], up[...])
     hidden = (0.5 * total * (1.0 + lax.erf(total * 0.5**0.5))).astype(BF16)
-    ncols = own.shape[1]
-    feed[:, at(place.core(), ncols)] = dot(hidden, own[...])
-    feed[:, at(1 - place.core(), ncols)] = dot(hidden, sibling[...])
-    width = outs[0].shape[1]
+    ncols = downs[0].shape[1]
+    for owner, down in zip(owners, downs):
+        feed[:, at(owner, ncols)] = dot(hidden, down[...])
+    share = outs[0].shape[1]
     for dx in range(nx):
-        outs[dx][...] = feed[:, at(place.x_after(dx), width)].astype(BF16)
-
-
-def add_x_kernel(place, *refs):
+        outs[dx][...] = feed[:, at(place.x_after(dx), share)].astype(BF16)
+
+
+def add_kernel(*refs):
     refs[-1][...] = sum(r[...].astype(F32) for r in refs[:-1]).astype(BF16)
 
 
-def add_z_kernel(place, *refs):
-    outs, total = refs[place.nz : -1], refs[-1]
-    total[...] = sum(r[...].astype(F32) for r in refs[: place.nz])
-    rows = outs[0].shape[0]
-    for dy in range(place.ny):
-        outs[dy][...] = total[at(lax.rem(place.y() + dy, place.ny), rows), :].astype(BF16)
-
-
 def last_kernel(place, *refs):
-    nx, ny = place.nx, place.ny
-    parts = refs[: nx * ny]
-    mid, bias, out, full = refs[nx * ny :]
+    nx = place.nx
+    parts = refs[:nx]
+    mid, bias, out, full = refs[nx:]
     group, steps, _ = out.shape
-    width = parts[0].shape[1]
+    share = parts[0].shape[1]
     for dx in range(nx):
-        for dy in range(ny):
-            block = place.y_before(dy) * nx + place.x_before(dx)
-            full[:, at(block, width)] = parts[dx * ny + dy][...].astype(F32)
+        full[:, at(place.x_before(dx), share)] = parts[dx][...].astype(F32)
     result = mid[...] + full[...] + bias[...]
     for i in range(group):
         out[i] = result[i * steps : (i + 1) * steps].astype(BF16)
+
+
+def tie(values):
+    return lax.optimization_barrier(values)
 
 
 def shape(sizes, kind=BF16):
@@ -478,10 +459,20 @@
             for dy in range(ny)
         ]
 
+    def over_y(weight):
+        return [place.move(weight, dy=dy) for dy in range(1, ny)]
+
+    def over_core(blocks):
+        return [place.move(block, dc=1) for block in blocks]
+
+    def over_x(value):
+        return [value] + [place.move(value, dx=dx) for dx in range(1, nx)]
+
     toks = [tokens] + [place.move(tokens, dy=dy) for dy in range(1, ny)]
     cols = w_query.shape[1]
     own = [w_query, w_key, w_value]
-    siblings = [place.move(weight, dc=1) for weight in own]
+    siblings = over_core(own)
+    up_ys = over_y(w_up)
     scales = row(jnp.concatenate([norm1_gain, norm1_bias]))
     biases = row(jnp.concatenate([b_query, b_key, b_value]))
     normed, *own = call(
@@ -499,18 +490,13 @@
         [shape((rows, 3 * cols))] * ny,
         scratch=[pltpu.VMEM(((ny - 1) * rows, width), F32), pltpu.VMEM((ny * rows, width), BF16)],
     )
-    *parts, tied_up, tied_down = lax.optimization_barrier((*parts, w_up, w_down))
-    w_up_sibling = place.move(tied_up, dc=1)
-    w_down_sibling = place.move(tied_down, dc=1)
+    parts, tied = tie((parts, w_up))
+    up_cores = over_core([tied])
     qkv = call(
         bind(add_columns_kernel, place), "add_qkv", spread(parts), shape((nx, rows, 3 * cols))
     )
-
-    qkv, w_up_sibling, w_down_sibling = lax.optimization_barrier(
-        (qkv, w_up_sibling, w_down_sibling)
-    )
-    qkv, tied_w_out = lax.optimization_barrier((qkv, w_out))
-    blocks = [place.transpose(tied_w_out, k) for k in range(nx)]
+    qkv, tied, up_cores = tie((qkv, w_out, up_cores))
+    blocks = [place.transpose(tied, 0)]
     pack = max(1, min(group, 256 // slots))
     new_keys, new_values, *messages = call(
         bind(attention_kernel, place, heads, steps),
@@ -533,72 +519,59 @@
         ],
         limit=52,
     )
-    *messages, blocks = lax.optimization_barrier((*messages, blocks))
-    w_outs = []
-    for block in blocks:
-        w_outs += [block, place.move(block, dc=1)]
+    messages, blocks, up_ys, tied = tie((messages, blocks, up_ys, (w_out, w_down)))
+    blocks += [place.transpose(tied[0], k) for k in range(1, nx)]
+    down_ys = over_y(tied[1])
+    block_cores = over_core(blocks[:1])
+    up_cores += over_core(up_ys)
     messages = [messages[0]] + [place.move(messages[dx], dx=dx) for dx in range(1, nx)]
     merged = call(
         bind(merge_x_kernel, place, heads), "merge_x", messages, shape((rows, share + LANES))
     )
-    merged, *w_outs = lax.optimization_barrier((merged, *w_outs))
+    merged, blocks, block_cores, up_cores = tie((merged, blocks, block_cores, up_cores))
+    block_cores += over_core(blocks[1:])
     attn = call(
         bind(merge_z_kernel, place, heads), "merge_z", place.gather_z(merged), shape((rows, share))
     )
+    attn, block_cores, tied = tie((attn, block_cores, w_down))
+    down_cores = over_core([tied])
     out_part = call(
         bind(out_kernel, place),
         "out",
-        [attn, *w_outs, row(b_out)],
+        [attn, *[b for pair in zip(blocks, block_cores) for b in pair], row(b_out)],
         shape((nx, rows, cols)),
         scratch=[pltpu.VMEM((nx, rows, cols), F32)],
     )
-    projected = call(
-        bind(add_out_kernel, place),
-        "add_out",
-        spread([out_part] * ny),
-        shape((ny, nx, rows, cols)),
-    )
-    up_part, mid = call(
-        bind(up_kernel, place),
-        "norm_up",
+    projected = call(add_kernel, "add_out", over_x(out_part), shape((nx, rows, cols)))
+    projected, down_ys, down_cores = tie((projected, down_ys, down_cores))
+    down_cores += over_core(down_ys)
+    *feeds, mid = call(
+        bind(feed_kernel, place),
+        "feed",
         [
-            *toks,
+            tokens,
             *place.gather_z(projected),
             row(norm2_gain),
             row(norm2_bias),
-            w_up,
-            w_up_sibling,
             row(b_up),
+            *[b for pair in zip([w_up] + up_ys, up_cores) for b in pair],
+            *[b for pair in zip([w_down] + down_ys, down_cores) for b in pair],
         ],
-        [shape((ny * rows, w_up.shape[1])), shape((rows, width), F32)],
+        [shape((rows, share))] * nx + [shape((rows, width), F32)],
         scratch=[
-            pltpu.VMEM((ny * rows, width), F32),
-            pltpu.VMEM((ny * rows, width), BF16),
+            pltpu.VMEM((rows, width), F32),
+            pltpu.VMEM((rows, width), BF16),
+            pltpu.VMEM((rows, width), F32),
             pltpu.VMEM((rows, width), F32),
         ],
     )
-    up_parts = [up_part] + [place.move(up_part, dy=dy) for dy in range(1, ny)]
-    piece = CORES * w_down.shape[1] // nx
-    feeds = call(
-        bind(down_kernel, place),
-        "gelu_down",
-        [*up_parts, w_down, w_down_sibling],
-        [shape((ny * rows, piece))] * nx,
-        scratch=[pltpu.VMEM((ny * rows, CORES * w_down.shape[1]), F32)],
-    )
     feeds = [feeds[0]] + [place.move(feeds[dx], dx=dx) for dx in range(1, nx)]
-    feed = call(bind(add_x_kernel, place), "add_x", feeds, shape((ny * rows, piece)))
-    summed = call(
-        bind(add_z_kernel, place),
-        "add_z",
-        place.gather_z(feed),
-        [shape((rows, piece))] * ny,
-        scratch=[pltpu.VMEM((ny * rows, piece), F32)],
-    )
+    feed = call(add_kernel, "add_x", feeds, shape((rows, share)))
+    summed = call(add_kernel, "add_z", place.gather_z(feed), shape((rows, share)))
     hidden_out = call(
         bind(last_kernel, place),
         "last",
-        [*spread(summed), mid, row(b_down)],
+        [*over_x(summed), mid, row(b_down)],
         shape(tokens.shape),
         scratch=[pltpu.VMEM((rows, width), F32)],
     )

time: 92.6 us -> 124 us (1.34)
  waiting for transfers between devices: 36.7 us -> 73.5 us
  starting transfers between devices: 40.5 us -> 34.7 us
    ppermute x32 -> x31, waiting for transfers between devices: 36.7 us -> 73.5 us  [move(): return lax.ppermute(value, ('seq', 'req'), pairs)]
    ppermute x32 -> x31, starting transfers between devices: 38.7 us -> 29.7 us  [move(): return lax.ppermute(value, ('seq', 'req'), pairs)]
    ppermute x2, starting transfers between devices: 1.76 us -> 5.07 us  [transpose(): return lax.ppermute(value, ('seq', 'req'), pairs)]
    pallas_call x13 -> x12, Pallas kernels: 9.05 us -> 9.08 us  [call(): pl.pallas_call(kernel, name=name, out_shape=outs, in_specs=in_specs or [V...]
  transfers between devices with their start and end apart: 34 -> 33, of which waited for: 18 -> 16; matrix products, arithmetic and copies ran while one was open for 2% -> 1% of each run, Pallas kernels for 6% -> 5%
where the time goes in v5:
time: 124 us
  waiting for transfers between devices  73.5 us (59%)
  starting transfers between devices  34.7 us (28%)
  Pallas kernels  9.08 us (7%)
  local copies, waits for them, and re-layouts  3.81 us (3%)
  other arithmetic  1.44 us (1%)
    ppermute x31, waiting for transfers between devices, move(): return lax.ppermute(value, ('seq', 'req'), pairs)  73.5 us
    ppermute x31, starting transfers between devices, move(): return lax.ppermute(value, ('seq', 'req'), pairs)  29.7 us
    pallas_call x12, Pallas kernels, call(): pl.pallas_call(kernel, name=name, out_shape=outs, in_specs=in_specs or [V...  9.08 us
    ppermute x2, starting transfers between devices, transpose(): return lax.ppermute(value, ('seq', 'req'), pairs)  5.07 us
    unnamed x28, local copies, waits for them, and re-layouts  3.81 us
  transfers between devices with their start and end apart: 33, of which 16 were waited for; matrix products, arithmetic and copies ran while one was open for 1% of the time, Pallas kernels for 5%

profile of v5, /device:TPU:0, one launch (start us, length us, event | category | flops | bytes accessed | tf_op | source)
XLA Modules:
  0.0 123.5 jit_solution(15169804836096367214)
XLA Ops:
  1.7 2.6 %collective-permute-start = (bf16[8,4,2048]{2,1,0:T(4,128)(2,1)}, bf16[8,4,2048]{2,1,0:T(4,128)(2,1)S(1)}, u32[]{:S(2)}, u32[]{:S(2)}) collective-permute-start(bf16[8,4,2048]{2,1,0:T(4,128)(2,1)} %refs_0_.3), channel_id=1, source_target_pairs={{0,2},{1,3},{2,0},{3,1},{4,6},{5,7},{6,4},{7,5},{8,10},{9,11},{10,... | collective-permute-start | bytes 393224 | tf_op jit(solution)/shard_map/ppermute | solution.py:62
  6.6 0.9 copy-done.4
  7.6 0.9 copy-done.5
  11.1 1.6 %collective-permute-start.5 = (bf16[32,768]{1,0:T(8,128)(2,1)S(1)}, bf16[32,768]{1,0:T(8,128)(2,1)S(1)}, u32[]{:S(2)}, u32[]{:S(2)}) collective-permute-start(bf16[32,768]{1,0:T(8,128)(2,1)S(1)} %get-tuple-element.47.refs_0_), channel_id=1, source_target_pairs={{0,4},{1,5},{2,6},{3,7},{4,0},{5,1},{6,2},{7,3},{8,12},{9,13},{10,... | collective-permute-start | bytes 147464 | tf_op jit(solution)/shard_map/ppermute | solution.py:62
  12.7 1.5 %collective-permute-start.6 = (bf16[32,768]{1,0:T(8,128)(2,1)S(1)}, bf16[32,768]{1,0:T(8,128)(2,1)S(1)}, u32[]{:S(2)}, u32[]{:S(2)}) collective-permute-start(bf16[32,768]{1,0:T(8,128)(2,1)S(1)} %get-tuple-element.48), channel_id=1, source_target_pairs={{0,6},{1,7},{2,4},{3,5},{4,2},{5,3},{6,0},{7,1},{8,14},{9,15},{10,... | collective-permute-start | bytes 147464 | tf_op jit(solution)/shard_map/ppermute | solution.py:62
  15.2 2.6 %collective-permute-done.6.refs_3_ = bf16[32,768]{1,0:T(8,128)(2,1)S(1)} collective-permute-done((bf16[32,768]{1,0:T(8,128)(2,1)S(1)}, bf16[32,768]{1,0:T(8,128)(2,1)S(1)}, u32[]{:S(2)}, u32[]{:S(2)}) %collective-permute-start.6) | collective-permute-done | bytes 49184 | tf_op jit(solution)/shard_map/ppermute | solution.py:62
  17.8 20.5 %collective-permute-done.4.refs_1_ = bf16[32,768]{1,0:T(8,128)(2,1)S(1)} collective-permute-done((bf16[32,768]{1,0:T(8,128)(2,1)S(1)}, bf16[32,768]{1,0:T(8,128)(2,1)S(1)}, u32[]{:S(2)}, u32[]{:S(2)}) %collective-permute-start.4) | collective-permute-done | bytes 49184 | tf_op jit(solution)/shard_map/ppermute | solution.py:62
  39.2 3.7 %collective-permute-start.10 = (bf16[2,32,768]{2,1,0:T(8,128)(2,1)S(1)}, bf16[2,32,768]{2,1,0:T(8,128)(2,1)S(1)}, u32[]{:S(2)}, u32[]{:S(2)}) collective-permute-start(bf16[2,32,768]{2,1,0:T(8,128)(2,1)S(1)} %add_qkv.1.refs_0_), channel_id=1, source_target_pairs={{0,24},{1,25},{2,26},{3,27},{4,28},{5,29},{6,30},{7,31},{8,16},{9,... | collective-permute-start | bytes 294920 | tf_op jit(solution)/shard_map/ppermute | solution.py:62
  43.7 3.2 %collective-permute-done.10.refs_3_ = bf16[2,32,768]{2,1,0:T(8,128)(2,1)S(1)} collective-permute-done((bf16[2,32,768]{2,1,0:T(8,128)(2,1)S(1)}, bf16[2,32,768]{2,1,0:T(8,128)(2,1)S(1)}, u32[]{:S(2)}, u32[]{:S(2)}) %collective-permute-start.10) | collective-permute-done | bytes 98336 | tf_op jit(solution)/shard_map/ppermute | solution.py:62
  46.9 4.0 %collective-permute-done.9.refs_2_ = bf16[2,32,768]{2,1,0:T(8,128)(2,1)S(1)} collective-permute-done((bf16[2,32,768]{2,1,0:T(8,128)(2,1)S(1)}, bf16[2,32,768]{2,1,0:T(8,128)(2,1)S(1)}, u32[]{:S(2)}, u32[]{:S(2)}) %collective-permute-start.9) | collective-permute-done | bytes 98336 | tf_op jit(solution)/shard_map/ppermute | solution.py:62
  50.8 4.5 %attention.1 = (bf16[8,64,2048]{2,1,0:T(8,128)(2,1)}, bf16[8,64,2048]{2,1,0:T(8,128)(2,1)}, bf16[32,1152]{1,0:T(8,128)(2,1)S(1)}, bf16[32,1152]{1,0:T(8,128)(2,1)S(1)}) custom-call(bf16[2,32,768]{2,1,0:T(8,128)(2,1)S(1)} %add_qkv.1.refs_0_, bf16[2,32,768]{2,1,0:T(8,128)(2,1)S(1)} %collective-permute-done.8.refs_1_, ...), custom_call_target="tpu_custom_call" | custom-call | bytes 1048576 | tf_op jit(solution)/shard_map/attention/pallas_call | solution.py:100
  55.4 4.3 %collective-permute-start.14 = (bf16[512,256]{1,0:T(8,128)(2,1)S(1)}, bf16[512,256]{1,0:T(8,128)(2,1)S(1)}, u32[]{:S(2)}, u32[]{:S(2)}) collective-permute-start(bf16[512,256]{1,0:T(8,128)(2,1)S(1)} %copy-done.13), channel_id=1, source_target_pairs={{0,2},{1,3},{2,6},{3,7},{4,0},{5,1},{6,4},{7,5},{8,10},{9,11},{10,... | collective-permute-start | bytes 786440 | tf_op jit(solution)/shard_map/ppermute | solution.py:77
  59.9 7.3 %collective-permute-done.13.refs_1_ = bf16[32,1152]{1,0:T(8,128)(2,1)S(1)} collective-permute-done((bf16[32,1152]{1,0:T(8,128)(2,1)S(1)}, bf16[32,1152]{1,0:T(8,128)(2,1)S(1)}, u32[]{:S(2)}, u32[]{:S(2)}) %collective-permute-start.13) | collective-permute-done | bytes 73760 | tf_op jit(solution)/shard_map/ppermute | solution.py:62
  67.6 2.6 %collective-permute-start.19 = (bf16[32,1152]{1,0:T(8,128)(2,1)S(1)}, bf16[32,1152]{1,0:T(8,128)(2,1)S(1)}, u32[]{:S(2)}, u32[]{:S(2)}) collective-permute-start(bf16[32,1152]{1,0:T(8,128)(2,1)S(1)} %merge_x.1.refs_0_), channel_id=1, source_target_pairs={{0,24},{1,25},{2,26},{3,27},{4,28},{5,29},{6,30},{7,31},{8,16},{9,... | collective-permute-start | bytes 221192 | tf_op jit(solution)/shard_map/ppermute | solution.py:62
  70.1 1.9 %collective-permute-start.17 = (bf16[32,1152]{1,0:T(8,128)(2,1)S(1)}, bf16[32,1152]{1,0:T(8,128)(2,1)S(1)}, u32[]{:S(2)}, u32[]{:S(2)}) collective-permute-start(bf16[32,1152]{1,0:T(8,128)(2,1)S(1)} %merge_x.1.refs_0_), channel_id=1, source_target_pairs={{0,8},{1,9},{2,10},{3,11},{4,12},{5,13},{6,14},{7,15},{8,0},{9,1},... | collective-permute-start | bytes 221192 | tf_op jit(solution)/shard_map/ppermute | solution.py:62
  72.8 1.8 %collective-permute-done.19.refs_3_ = bf16[32,1152]{1,0:T(8,128)(2,1)S(1)} collective-permute-done((bf16[32,1152]{1,0:T(8,128)(2,1)S(1)}, bf16[32,1152]{1,0:T(8,128)(2,1)S(1)}, u32[]{:S(2)}, u32[]{:S(2)}) %collective-permute-start.19) | collective-permute-done | bytes 73760 | tf_op jit(solution)/shard_map/ppermute | solution.py:62
  74.6 2.6 %collective-permute-done.18.refs_2_ = bf16[32,1152]{1,0:T(8,128)(2,1)S(1)} collective-permute-done((bf16[32,1152]{1,0:T(8,128)(2,1)S(1)}, bf16[32,1152]{1,0:T(8,128)(2,1)S(1)}, u32[]{:S(2)}, u32[]{:S(2)}) %collective-permute-start.18) | collective-permute-done | bytes 73760 | tf_op jit(solution)/shard_map/ppermute | solution.py:62
  78.1 3.9 %collective-permute-done.21.refs_1_ = bf16[2,32,256]{2,1,0:T(8,128)(2,1)S(1)} collective-permute-done((bf16[2,32,256]{2,1,0:T(8,128)(2,1)S(1)}, bf16[2,32,256]{2,1,0:T(8,128)(2,1)S(1)}, u32[]{:S(2)}, u32[]{:S(2)}) %collective-permute-start.21) | collective-permute-done | bytes 32800 | tf_op jit(solution)/shard_map/ppermute | solution.py:62
  82.0 14.7 %collective-permute-done.22.refs_14_ = bf16[1024,512]{1,0:T(8,128)(2,1)S(1)} collective-permute-done((bf16[1024,512]{1,0:T(8,128)(2,1)S(1)}, bf16[1024,512]{1,0:T(8,128)(2,1)S(1)}, u32[]{:S(2)}, u32[]{:S(2)}) %collective-permute-start.22) | collective-permute-done | bytes 1048608 | tf_op jit(solution)/shard_map/ppermute | solution.py:62
  96.7 2.5 %collective-permute-start.26 = (bf16[2,32,256]{2,1,0:T(8,128)(2,1)S(1)}, bf16[2,32,256]{2,1,0:T(8,128)(2,1)S(1)}, u32[]{:S(2)}, u32[]{:S(2)}) collective-permute-start(bf16[2,32,256]{2,1,0:T(8,128)(2,1)S(1)} %add_out.1.refs_1_), channel_id=1, source_target_pairs={{0,24},{1,25},{2,26},{3,27},{4,28},{5,29},{6,30},{7,31},{8,16},{9,... | collective-permute-start | bytes 98312 | tf_op jit(solution)/shard_map/ppermute | solution.py:62
  99.2 1.9 %collective-permute-start.24 = (bf16[2,32,256]{2,1,0:T(8,128)(2,1)S(1)}, bf16[2,32,256]{2,1,0:T(8,128)(2,1)S(1)}, u32[]{:S(2)}, u32[]{:S(2)}) collective-permute-start(bf16[2,32,256]{2,1,0:T(8,128)(2,1)S(1)} %add_out.1.refs_1_), channel_id=1, source_target_pairs={{0,8},{1,9},{2,10},{3,11},{4,12},{5,13},{6,14},{7,15},{8,0},{9,1},... | collective-permute-start | bytes 98312 | tf_op jit(solution)/shard_map/ppermute | solution.py:62
  101.1 1.6 %collective-permute-done.26.refs_4_ = bf16[2,32,256]{2,1,0:T(8,128)(2,1)S(1)} collective-permute-done((bf16[2,32,256]{2,1,0:T(8,128)(2,1)S(1)}, bf16[2,32,256]{2,1,0:T(8,128)(2,1)S(1)}, u32[]{:S(2)}, u32[]{:S(2)}) %collective-permute-start.26) | collective-permute-done | bytes 32800 | tf_op jit(solution)/shard_map/ppermute | solution.py:62
  102.7 1.4 %collective-permute-done.25.refs_3_ = bf16[2,32,256]{2,1,0:T(8,128)(2,1)S(1)} collective-permute-done((bf16[2,32,256]{2,1,0:T(8,128)(2,1)S(1)}, bf16[2,32,256]{2,1,0:T(8,128)(2,1)S(1)}, u32[]{:S(2)}, u32[]{:S(2)}) %collective-permute-start.25) | collective-permute-done | bytes 32800 | tf_op jit(solution)/shard_map/ppermute | solution.py:62
  104.1 1.8 %feed.1 = (bf16[32,1024]{1,0:T(8,128)(2,1)S(1)}, bf16[32,1024]{1,0:T(8,128)(2,1)S(1)}, f32[32,2048]{1,0:T(8,128)S(1)}) custom-call(bf16[8,4,2048]{2,1,0:T(4,128)(2,1)S(1)} %copy-done.3, bf16[2,32,256]{2,1,0:T(8,128)(2,1)S(1)} %add_out.1.refs_1_, bf16[2,32,256]{2,1,0:T(8,128)(2,1)S(1)} %collective-permute-done.24.refs_2_, ...), custom_call_target="tpu_custom_call" | custom-call | bytes 1048576 | tf_op jit(solution)/shard_map/feed/pallas_call | solution.py:100
  105.9 1.5 %collective-permute-start.28 = (bf16[32,1024]{1,0:T(8,128)(2,1)S(1)}, bf16[32,1024]{1,0:T(8,128)(2,1)S(1)}, u32[]{:S(2)}, u32[]{:S(2)}) collective-permute-start(bf16[32,1024]{1,0:T(8,128)(2,1)S(1)} %get-tuple-element.75), channel_id=1, source_target_pairs={{0,4},{1,5},{2,6},{3,7},{4,0},{5,1},{6,2},{7,3},{8,12},{9,13},{10,... | collective-permute-start | bytes 196616 | tf_op jit(solution)/shard_map/ppermute | solution.py:62
  107.4 2.9 %collective-permute-done.28.refs_1_ = bf16[32,1024]{1,0:T(8,128)(2,1)S(1)} collective-permute-done((bf16[32,1024]{1,0:T(8,128)(2,1)S(1)}, bf16[32,1024]{1,0:T(8,128)(2,1)S(1)}, u32[]{:S(2)}, u32[]{:S(2)}) %collective-permute-start.28) | collective-permute-done | bytes 65568 | tf_op jit(solution)/shard_map/ppermute | solution.py:62
  110.3 2.3 %collective-permute-start.31 = (bf16[32,1024]{1,0:T(8,128)(2,1)S(1)}, bf16[32,1024]{1,0:T(8,128)(2,1)S(1)}, u32[]{:S(2)}, u32[]{:S(2)}) collective-permute-start(bf16[32,1024]{1,0:T(8,128)(2,1)S(1)} %add_x.1.refs_0_), channel_id=1, source_target_pairs={{0,24},{1,25},{2,26},{3,27},{4,28},{5,29},{6,30},{7,31},{8,16},{9,... | collective-permute-start | bytes 196616 | tf_op jit(solution)/shard_map/ppermute | solution.py:62
  112.8 2.0 %collective-permute-start.29 = (bf16[32,1024]{1,0:T(8,128)(2,1)S(1)}, bf16[32,1024]{1,0:T(8,128)(2,1)S(1)}, u32[]{:S(2)}, u32[]{:S(2)}) collective-permute-start(bf16[32,1024]{1,0:T(8,128)(2,1)S(1)} %add_x.1.refs_0_), channel_id=1, source_target_pairs={{0,8},{1,9},{2,10},{3,11},{4,12},{5,13},{6,14},{7,15},{8,0},{9,1},... | collective-permute-start | bytes 196616 | tf_op jit(solution)/shard_map/ppermute | solution.py:62
  114.7 2.3 %collective-permute-done.31.refs_3_ = bf16[32,1024]{1,0:T(8,128)(2,1)S(1)} collective-permute-done((bf16[32,1024]{1,0:T(8,128)(2,1)S(1)}, bf16[32,1024]{1,0:T(8,128)(2,1)S(1)}, u32[]{:S(2)}, u32[]{:S(2)}) %collective-permute-start.31) | collective-permute-done | bytes 65568 | tf_op jit(solution)/shard_map/ppermute | solution.py:62
  117.0 1.4 %collective-permute-done.30.refs_2_ = bf16[32,1024]{1,0:T(8,128)(2,1)S(1)} collective-permute-done((bf16[32,1024]{1,0:T(8,128)(2,1)S(1)}, bf16[32,1024]{1,0:T(8,128)(2,1)S(1)}, u32[]{:S(2)}, u32[]{:S(2)}) %collective-permute-start.30) | collective-permute-done | bytes 65568 | tf_op jit(solution)/shard_map/ppermute | solution.py:62
  118.5 1.5 %collective-permute-start.32 = (bf16[32,1024]{1,0:T(8,128)(2,1)S(1)}, bf16[32,1024]{1,0:T(8,128)(2,1)S(1)}, u32[]{:S(2)}, u32[]{:S(2)}) collective-permute-start(bf16[32,1024]{1,0:T(8,128)(2,1)S(1)} %add_z.1.refs_0_), channel_id=1, source_target_pairs={{0,4},{1,5},{2,6},{3,7},{4,0},{5,1},{6,2},{7,3},{8,12},{9,13},{10,... | collective-permute-start | bytes 196616 | tf_op jit(solution)/shard_map/ppermute | solution.py:62
  119.9 2.9 %collective-permute-done.32.refs_1_ = bf16[32,1024]{1,0:T(8,128)(2,1)S(1)} collective-permute-done((bf16[32,1024]{1,0:T(8,128)(2,1)S(1)}, bf16[32,1024]{1,0:T(8,128)(2,1)S(1)}, u32[]{:S(2)}, u32[]{:S(2)}) %collective-permute-start.32) | collective-permute-done | bytes 65568 | tf_op jit(solution)/shard_map/ppermute | solution.py:62
  (77 shorter events, 11.9 us)
Async XLA Ops:
  0.6 9.2 %collective-permute-start.1 = (bf16[512,256]{1,0:T(8,128)(2,1)}, bf16[512,256]{1,0:T(8,128)(2,1)S(1)}, u32[]{:S(2)}, u32[]{:S(2)}) collective-permute-start(bf16[512,256]{1,0:T(8,128)(2,1)} %refs_0_.2), channel_id=1, source_target_pairs={{0,1},{1,0},{2,3},{3,2},{4,5},{5,4},{6,7},{7,6},{8,9},{9,8},{10,11... | collective-permute-start | bytes 786440 | tf_op jit(solution)/shard_map/ppermute | solution.py:62
  1.2 8.7 %collective-permute-start.2 = (bf16[512,256]{1,0:T(8,128)(2,1)}, bf16[512,256]{1,0:T(8,128)(2,1)S(1)}, u32[]{:S(2)}, u32[]{:S(2)}) collective-permute-start(bf16[512,256]{1,0:T(8,128)(2,1)} %refs_1_.1), channel_id=1, source_target_pairs={{0,1},{1,0},{2,3},{3,2},{4,5},{5,4},{6,7},{7,6},{8,9},{9,8},{10,11... | collective-permute-start | bytes 786440 | tf_op jit(solution)/shard_map/ppermute | solution.py:62
  1.2 8.6 %collective-permute-start.3 = (bf16[512,256]{1,0:T(8,128)(2,1)}, bf16[512,256]{1,0:T(8,128)(2,1)S(1)}, u32[]{:S(2)}, u32[]{:S(2)}) collective-permute-start(bf16[512,256]{1,0:T(8,128)(2,1)} %refs_2_.1), channel_id=1, source_target_pairs={{0,1},{1,0},{2,3},{3,2},{4,5},{5,4},{6,7},{7,6},{8,9},{9,8},{10,11... | collective-permute-start | bytes 786440 | tf_op jit(solution)/shard_map/ppermute | solution.py:62
  1.7 8.2 %collective-permute-start = (bf16[8,4,2048]{2,1,0:T(4,128)(2,1)}, bf16[8,4,2048]{2,1,0:T(4,128)(2,1)S(1)}, u32[]{:S(2)}, u32[]{:S(2)}) collective-permute-start(bf16[8,4,2048]{2,1,0:T(4,128)(2,1)} %refs_0_.3), channel_id=1, source_target_pairs={{0,2},{1,3},{2,0},{3,1},{4,6},{5,7},{6,4},{7,5},{8,10},{9,11},{10,... | collective-permute-start | bytes 393224 | tf_op jit(solution)/shard_map/ppermute | solution.py:62
  10.5 27.9 %collective-permute-start.7 = (bf16[512,1024]{1,0:T(8,128)(2,1)S(1)}, bf16[512,1024]{1,0:T(8,128)(2,1)S(1)}, u32[]{:S(2)}, u32[]{:S(2)}) collective-permute-start(bf16[512,1024]{1,0:T(8,128)(2,1)S(1)} %copy-done), channel_id=1, source_target_pairs={{0,1},{1,0},{2,3},{3,2},{4,5},{5,4},{6,7},{7,6},{8,9},{9,8},{10,11... | collective-permute-start | bytes 3145736 | tf_op jit(solution)/shard_map/ppermute | solution.py:62
  10.7 44.6 %collective-permute-start.12 = (bf16[512,1024]{1,0:T(8,128)(2,1)S(1)}, bf16[512,1024]{1,0:T(8,128)(2,1)S(1)}, u32[]{:S(2)}, u32[]{:S(2)}) collective-permute-start(bf16[512,1024]{1,0:T(8,128)(2,1)S(1)} %copy-done), channel_id=1, source_target_pairs={{0,2},{1,3},{2,0},{3,1},{4,6},{5,7},{6,4},{7,5},{8,10},{9,11},{10,... | collective-permute-start | bytes 3145736 | tf_op jit(solution)/shard_map/ppermute | solution.py:62
  11.1 4.1 %collective-permute-start.5 = (bf16[32,768]{1,0:T(8,128)(2,1)S(1)}, bf16[32,768]{1,0:T(8,128)(2,1)S(1)}, u32[]{:S(2)}, u32[]{:S(2)}) collective-permute-start(bf16[32,768]{1,0:T(8,128)(2,1)S(1)} %get-tuple-element.47.refs_0_), channel_id=1, source_target_pairs={{0,4},{1,5},{2,6},{3,7},{4,0},{5,1},{6,2},{7,3},{8,12},{9,13},{10,... | collective-permute-start | bytes 147464 | tf_op jit(solution)/shard_map/ppermute | solution.py:62
  12.7 5.0 %collective-permute-start.6 = (bf16[32,768]{1,0:T(8,128)(2,1)S(1)}, bf16[32,768]{1,0:T(8,128)(2,1)S(1)}, u32[]{:S(2)}, u32[]{:S(2)}) collective-permute-start(bf16[32,768]{1,0:T(8,128)(2,1)S(1)} %get-tuple-element.48), channel_id=1, source_target_pairs={{0,6},{1,7},{2,4},{3,5},{4,2},{5,3},{6,0},{7,1},{8,14},{9,15},{10,... | collective-permute-start | bytes 147464 | tf_op jit(solution)/shard_map/ppermute | solution.py:62
  14.2 24.0 %collective-permute-start.4 = (bf16[32,768]{1,0:T(8,128)(2,1)S(1)}, bf16[32,768]{1,0:T(8,128)(2,1)S(1)}, u32[]{:S(2)}, u32[]{:S(2)}) collective-permute-start(bf16[32,768]{1,0:T(8,128)(2,1)S(1)} %get-tuple-element.48), channel_id=1, source_target_pairs={{0,2},{1,3},{2,0},{3,1},{4,6},{5,7},{6,4},{7,5},{8,10},{9,11},{10,... | collective-permute-start | bytes 147464 | tf_op jit(solution)/shard_map/ppermute | solution.py:62
  38.4 17.0 %collective-permute-start.11 = (bf16[512,256]{1,0:T(8,128)(2,1)S(1)}, bf16[512,256]{1,0:T(8,128)(2,1)S(1)}, u32[]{:S(2)}, u32[]{:S(2)}) collective-permute-start(bf16[512,256]{1,0:T(8,128)(2,1)S(1)} %copy-done.13), channel_id=1, source_target_pairs={{0,0},{1,1},{2,4},{3,5},{4,2},{5,3},{6,6},{7,7},{8,8},{9,9},{10,12... | collective-permute-start | bytes 786440 | tf_op jit(solution)/shard_map/ppermute | solution.py:77
  39.2 7.7 %collective-permute-start.10 = (bf16[2,32,768]{2,1,0:T(8,128)(2,1)S(1)}, bf16[2,32,768]{2,1,0:T(8,128)(2,1)S(1)}, u32[]{:S(2)}, u32[]{:S(2)}) collective-permute-start(bf16[2,32,768]{2,1,0:T(8,128)(2,1)S(1)} %add_qkv.1.refs_0_), channel_id=1, source_target_pairs={{0,24},{1,25},{2,26},{3,27},{4,28},{5,29},{6,30},{7,31},{8,16},{9,... | collective-permute-start | bytes 294920 | tf_op jit(solution)/shard_map/ppermute | solution.py:62
  42.9 8.0 %collective-permute-start.9 = (bf16[2,32,768]{2,1,0:T(8,128)(2,1)S(1)}, bf16[2,32,768]{2,1,0:T(8,128)(2,1)S(1)}, u32[]{:S(2)}, u32[]{:S(2)}) collective-permute-start(bf16[2,32,768]{2,1,0:T(8,128)(2,1)S(1)} %add_qkv.1.refs_0_), channel_id=1, source_target_pairs={{0,16},{1,17},{2,18},{3,19},{4,20},{5,21},{6,22},{7,23},{8,24},{9,... | collective-permute-start | bytes 294920 | tf_op jit(solution)/shard_map/ppermute | solution.py:62
  42.9 8.0 %collective-permute-start.8 = (bf16[2,32,768]{2,1,0:T(8,128)(2,1)S(1)}, bf16[2,32,768]{2,1,0:T(8,128)(2,1)S(1)}, u32[]{:S(2)}, u32[]{:S(2)}) collective-permute-start(bf16[2,32,768]{2,1,0:T(8,128)(2,1)S(1)} %add_qkv.1.refs_0_), channel_id=1, source_target_pairs={{0,8},{1,9},{2,10},{3,11},{4,12},{5,13},{6,14},{7,15},{8,0},{9,1},... | collective-permute-start | bytes 294920 | tf_op jit(solution)/shard_map/ppermute | solution.py:62
  55.3 12.1 %collective-permute-start.16 = (bf16[512,1024]{1,0:T(8,128)(2,1)S(1)}, bf16[512,1024]{1,0:T(8,128)(2,1)S(1)}, u32[]{:S(2)}, u32[]{:S(2)}) collective-permute-start(bf16[512,1024]{1,0:T(8,128)(2,1)S(1)} %collective-permute-done.12.refs_10_), channel_id=1, source_target_pairs={{0,1},{1,0},{2,3},{3,2},{4,5},{5,4},{6,7},{7,6},{8,9},{9,8},{10,11... | collective-permute-start | bytes 3145736 | tf_op jit(solution)/shard_map/ppermute | solution.py:62
  55.4 12.0 %collective-permute-start.14 = (bf16[512,256]{1,0:T(8,128)(2,1)S(1)}, bf16[512,256]{1,0:T(8,128)(2,1)S(1)}, u32[]{:S(2)}, u32[]{:S(2)}) collective-permute-start(bf16[512,256]{1,0:T(8,128)(2,1)S(1)} %copy-done.13), channel_id=1, source_target_pairs={{0,2},{1,3},{2,6},{3,7},{4,0},{5,1},{6,4},{7,5},{8,10},{9,11},{10,... | collective-permute-start | bytes 786440 | tf_op jit(solution)/shard_map/ppermute | solution.py:77
  59.7 7.8 %collective-permute-start.15 = (bf16[512,256]{1,0:T(8,128)(2,1)S(1)}, bf16[512,256]{1,0:T(8,128)(2,1)S(1)}, u32[]{:S(2)}, u32[]{:S(2)}) collective-permute-start(bf16[512,256]{1,0:T(8,128)(2,1)S(1)} %collective-permute-done.11.refs_0_), channel_id=1, source_target_pairs={{0,1},{1,0},{2,3},{3,2},{4,5},{5,4},{6,7},{7,6},{8,9},{9,8},{10,11... | collective-permute-start | bytes 786440 | tf_op jit(solution)/shard_map/ppermute | solution.py:62
  59.8 7.3 %collective-permute-start.13 = (bf16[32,1152]{1,0:T(8,128)(2,1)S(1)}, bf16[32,1152]{1,0:T(8,128)(2,1)S(1)}, u32[]{:S(2)}, u32[]{:S(2)}) collective-permute-start(bf16[32,1152]{1,0:T(8,128)(2,1)S(1)} %get-tuple-element.55), channel_id=1, source_target_pairs={{0,4},{1,5},{2,6},{3,7},{4,0},{5,1},{6,2},{7,3},{8,12},{9,13},{10,... | collective-permute-start | bytes 221192 | tf_op jit(solution)/shard_map/ppermute | solution.py:62
  67.5 10.1 %collective-permute-start.20 = (bf16[512,256]{1,0:T(8,128)(2,1)S(1)}, bf16[512,256]{1,0:T(8,128)(2,1)S(1)}, u32[]{:S(2)}, u32[]{:S(2)}) collective-permute-start(bf16[512,256]{1,0:T(8,128)(2,1)S(1)} %collective-permute-done.14.refs_2_), channel_id=1, source_target_pairs={{0,1},{1,0},{2,3},{3,2},{4,5},{5,4},{6,7},{7,6},{8,9},{9,8},{10,11... | collective-permute-start | bytes 786440 | tf_op jit(solution)/shard_map/ppermute | solution.py:62
  67.6 7.0 %collective-permute-start.19 = (bf16[32,1152]{1,0:T(8,128)(2,1)S(1)}, bf16[32,1152]{1,0:T(8,128)(2,1)S(1)}, u32[]{:S(2)}, u32[]{:S(2)}) collective-permute-start(bf16[32,1152]{1,0:T(8,128)(2,1)S(1)} %merge_x.1.refs_0_), channel_id=1, source_target_pairs={{0,24},{1,25},{2,26},{3,27},{4,28},{5,29},{6,30},{7,31},{8,16},{9,... | collective-permute-start | bytes 221192 | tf_op jit(solution)/shard_map/ppermute | solution.py:62
  70.1 7.1 %collective-permute-start.18 = (bf16[32,1152]{1,0:T(8,128)(2,1)S(1)}, bf16[32,1152]{1,0:T(8,128)(2,1)S(1)}, u32[]{:S(2)}, u32[]{:S(2)}) collective-permute-start(bf16[32,1152]{1,0:T(8,128)(2,1)S(1)} %merge_x.1.refs_0_), channel_id=1, source_target_pairs={{0,16},{1,17},{2,18},{3,19},{4,20},{5,21},{6,22},{7,23},{8,24},{9,... | collective-permute-start | bytes 221192 | tf_op jit(solution)/shard_map/ppermute | solution.py:62
  70.1 7.1 %collective-permute-start.17 = (bf16[32,1152]{1,0:T(8,128)(2,1)S(1)}, bf16[32,1152]{1,0:T(8,128)(2,1)S(1)}, u32[]{:S(2)}, u32[]{:S(2)}) collective-permute-start(bf16[32,1152]{1,0:T(8,128)(2,1)S(1)} %merge_x.1.refs_0_), channel_id=1, source_target_pairs={{0,8},{1,9},{2,10},{3,11},{4,12},{5,13},{6,14},{7,15},{8,0},{9,1},... | collective-permute-start | bytes 221192 | tf_op jit(solution)/shard_map/ppermute | solution.py:62
  72.0 24.7 %collective-permute-start.22 = (bf16[1024,512]{1,0:T(8,128)(2,1)S(1)}, bf16[1024,512]{1,0:T(8,128)(2,1)S(1)}, u32[]{:S(2)}, u32[]{:S(2)}) collective-permute-start(bf16[1024,512]{1,0:T(8,128)(2,1)S(1)} %copy-done.1), channel_id=1, source_target_pairs={{0,2},{1,3},{2,0},{3,1},{4,6},{5,7},{6,4},{7,5},{8,10},{9,11},{10,... | collective-permute-start | bytes 3145736 | tf_op jit(solution)/shard_map/ppermute | solution.py:62
  77.6 19.1 %collective-permute-start.23 = (bf16[1024,512]{1,0:T(8,128)(2,1)S(1)}, bf16[1024,512]{1,0:T(8,128)(2,1)S(1)}, u32[]{:S(2)}, u32[]{:S(2)}) collective-permute-start(bf16[1024,512]{1,0:T(8,128)(2,1)S(1)} %copy-done.1), channel_id=1, source_target_pairs={{0,1},{1,0},{2,3},{3,2},{4,5},{5,4},{6,7},{7,6},{8,9},{9,8},{10,11... | collective-permute-start | bytes 3145736 | tf_op jit(solution)/shard_map/ppermute | solution.py:62
  96.7 7.3 %collective-permute-start.27 = (bf16[1024,512]{1,0:T(8,128)(2,1)S(1)}, bf16[1024,512]{1,0:T(8,128)(2,1)S(1)}, u32[]{:S(2)}, u32[]{:S(2)}) collective-permute-start(bf16[1024,512]{1,0:T(8,128)(2,1)S(1)} %collective-permute-done.22.refs_14_), channel_id=1, source_target_pairs={{0,1},{1,0},{2,3},{3,2},{4,5},{5,4},{6,7},{7,6},{8,9},{9,8},{10,11... | collective-permute-start | bytes 3145736 | tf_op jit(solution)/shard_map/ppermute | solution.py:62
  96.7 6.0 %collective-permute-start.26 = (bf16[2,32,256]{2,1,0:T(8,128)(2,1)S(1)}, bf16[2,32,256]{2,1,0:T(8,128)(2,1)S(1)}, u32[]{:S(2)}, u32[]{:S(2)}) collective-permute-start(bf16[2,32,256]{2,1,0:T(8,128)(2,1)S(1)} %add_out.1.refs_1_), channel_id=1, source_target_pairs={{0,24},{1,25},{2,26},{3,27},{4,28},{5,29},{6,30},{7,31},{8,16},{9,... | collective-permute-start | bytes 98312 | tf_op jit(solution)/shard_map/ppermute | solution.py:62
  99.2 4.8 %collective-permute-start.25 = (bf16[2,32,256]{2,1,0:T(8,128)(2,1)S(1)}, bf16[2,32,256]{2,1,0:T(8,128)(2,1)S(1)}, u32[]{:S(2)}, u32[]{:S(2)}) collective-permute-start(bf16[2,32,256]{2,1,0:T(8,128)(2,1)S(1)} %add_out.1.refs_1_), channel_id=1, source_target_pairs={{0,16},{1,17},{2,18},{3,19},{4,20},{5,21},{6,22},{7,23},{8,24},{9,... | collective-permute-start | bytes 98312 | tf_op jit(solution)/shard_map/ppermute | solution.py:62
  99.2 4.8 %collective-permute-start.24 = (bf16[2,32,256]{2,1,0:T(8,128)(2,1)S(1)}, bf16[2,32,256]{2,1,0:T(8,128)(2,1)S(1)}, u32[]{:S(2)}, u32[]{:S(2)}) collective-permute-start(bf16[2,32,256]{2,1,0:T(8,128)(2,1)S(1)} %add_out.1.refs_1_), channel_id=1, source_target_pairs={{0,8},{1,9},{2,10},{3,11},{4,12},{5,13},{6,14},{7,15},{8,0},{9,1},... | collective-permute-start | bytes 98312 | tf_op jit(solution)/shard_map/ppermute | solution.py:62
  105.9 4.3 %collective-permute-start.28 = (bf16[32,1024]{1,0:T(8,128)(2,1)S(1)}, bf16[32,1024]{1,0:T(8,128)(2,1)S(1)}, u32[]{:S(2)}, u32[]{:S(2)}) collective-permute-start(bf16[32,1024]{1,0:T(8,128)(2,1)S(1)} %get-tuple-element.75), channel_id=1, source_target_pairs={{0,4},{1,5},{2,6},{3,7},{4,0},{5,1},{6,2},{7,3},{8,12},{9,13},{10,... | collective-permute-start | bytes 196616 | tf_op jit(solution)/shard_map/ppermute | solution.py:62
  110.3 6.7 %collective-permute-start.31 = (bf16[32,1024]{1,0:T(8,128)(2,1)S(1)}, bf16[32,1024]{1,0:T(8,128)(2,1)S(1)}, u32[]{:S(2)}, u32[]{:S(2)}) collective-permute-start(bf16[32,1024]{1,0:T(8,128)(2,1)S(1)} %add_x.1.refs_0_), channel_id=1, source_target_pairs={{0,24},{1,25},{2,26},{3,27},{4,28},{5,29},{6,30},{7,31},{8,16},{9,... | collective-permute-start | bytes 196616 | tf_op jit(solution)/shard_map/ppermute | solution.py:62
  112.5 5.9 %collective-permute-start.30 = (bf16[32,1024]{1,0:T(8,128)(2,1)S(1)}, bf16[32,1024]{1,0:T(8,128)(2,1)S(1)}, u32[]{:S(2)}, u32[]{:S(2)}) collective-permute-start(bf16[32,1024]{1,0:T(8,128)(2,1)S(1)} %add_x.1.refs_0_), channel_id=1, source_target_pairs={{0,16},{1,17},{2,18},{3,19},{4,20},{5,21},{6,22},{7,23},{8,24},{9,... | collective-permute-start | bytes 196616 | tf_op jit(solution)/shard_map/ppermute | solution.py:62
  112.8 5.6 %collective-permute-start.29 = (bf16[32,1024]{1,0:T(8,128)(2,1)S(1)}, bf16[32,1024]{1,0:T(8,128)(2,1)S(1)}, u32[]{:S(2)}, u32[]{:S(2)}) collective-permute-start(bf16[32,1024]{1,0:T(8,128)(2,1)S(1)} %add_x.1.refs_0_), channel_id=1, source_target_pairs={{0,8},{1,9},{2,10},{3,11},{4,12},{5,13},{6,14},{7,15},{8,0},{9,1},... | collective-permute-start | bytes 196616 | tf_op jit(solution)/shard_map/ppermute | solution.py:62
  118.5 4.3 %collective-permute-start.32 = (bf16[32,1024]{1,0:T(8,128)(2,1)S(1)}, bf16[32,1024]{1,0:T(8,128)(2,1)S(1)}, u32[]{:S(2)}, u32[]{:S(2)}) collective-permute-start(bf16[32,1024]{1,0:T(8,128)(2,1)S(1)} %add_z.1.refs_0_), channel_id=1, source_target_pairs={{0,4},{1,5},{2,6},{3,7},{4,0},{5,1},{6,2},{7,3},{8,12},{9,13},{10,... | collective-permute-start | bytes 196616 | tf_op jit(solution)/shard_map/ppermute | solution.py:62
  (15 other events, 442.6 us)

commit v6 on v4

--- a/solution.py
+++ b/solution.py
@@ -90,11 +90,15 @@
     return jnp.dot(a, b, preferred_element_type=F32)
 
 
+def across(a, b):
+    return lax.dot_general(a, b, (((1,), (1,)), ((), ())), preferred_element_type=F32)
+
+
 def at(index, size):
     return pl.ds(pl.multiple_of(index * size, size), size)
 
 
-def call(kernel, name, ins, outs, in_specs=None, out_specs=None, scratch=(), moved=2**20, limit=20):
+def call(kernel, name, ins, outs, in_specs=None, out_specs=None, scratch=(), moved=2**20, limit=20, aliases=None):
     single = not isinstance(outs, (list, tuple))
     specs = out_specs or (VMEM if single else [VMEM] * len(outs))
     return pl.pallas_call(
@@ -104,6 +108,7 @@
         in_specs=in_specs or [VMEM] * len(ins),
         out_specs=specs,
         scratch_shapes=list(scratch),
+        input_output_aliases=aliases or {},
         cost_estimate=pl.CostEstimate(flops=0, bytes_accessed=moved, transcendentals=0),
         compiler_params=pltpu.CompilerParams(vmem_limit_bytes=limit * 1024 * 1024),
     )(*ins)
@@ -130,7 +135,7 @@
         flat[start + i * steps : start + (i + 1) * steps, :] = block[i].astype(F32)
 
 
-def norm_kernel(tokens, scales, *refs):
+def norm_kernel(mark, tokens, scales, *refs):
     count = (len(refs) - 3) // 2
     weights, out, kept = refs[:count], refs[count], refs[count + 1 : 2 * count + 1]
     flat, sems = refs[-2:]
@@ -170,13 +175,90 @@
             outs[(ny - j) % ny][:, k * cols : (k + 1) * cols] = part.astype(BF16)
 
 
-def add_columns_kernel(place, *refs):
-    out = refs[-1]
+def add_qkv_kernel(place, *refs):
+    query, fresh = refs[-2:]
+    cols = query.shape[2]
     for dx in range(place.nx):
         total = refs[dx * place.ny][...].astype(F32)
         for dy in range(1, place.ny):
             total = total + refs[dx * place.ny + dy][...].astype(F32)
-        out[place.x_before(dx)] = total.astype(BF16)
+        total = total.astype(BF16)
+        query[place.x_before(dx)] = total[:, :cols]
+        fresh[place.x_before(dx)] = total[:, cols:]
+
+
+def cache_kernel(keys_in, values_in, keys_out, values_out, keys, values, mark, in_sems, out_sems):
+    group = keys.shape[0]
+    arrays = ((keys_in, keys, keys_out), (values_in, values, values_out))
+    coming = [
+        pltpu.make_async_copy(source.at[i], here.at[i], in_sems.at[k, i])
+        for i in range(group)
+        for k, (source, here, _) in enumerate(arrays)
+    ]
+    going = [
+        pltpu.make_async_copy(here.at[i], target.at[i], out_sems.at[k, i])
+        for i in range(group)
+        for k, (_, here, target) in enumerate(arrays)
+    ]
+    for copy in coming:
+        copy.start()
+    mark[...] = jnp.zeros_like(mark)
+    for arrived, copy in zip(coming, going):
+        arrived.wait()
+        copy.start()
+    for copy in going:
+        copy.wait()
+
+
+def insert_kernel(place, steps, *refs):
+    nx, nz = place.nx, place.nz
+    gathered = refs[:nz]
+    lengths, keys, values, _, _, keys_out, values_out, ks, vs, k_rows, v_rows, sems = refs[nz:]
+    group, slots, width = keys.shape
+    cols = width // place.seqs
+    base_of = lax.axis_index("seq") * slots
+    for dz in range(nz):
+        span = at(place.z_partner(dz), nx * cols)
+        for k, target in enumerate((ks, vs)):
+            target[:, span] = side_by_side(gathered[dz], k * cols, cols)
+    window = k_rows.shape[1]
+
+    def place_of(i):
+        base = lengths[i] - base_of
+        start = jnp.clip(lax.div(jnp.maximum(base, 0), 16) * 16, 0, slots - window)
+        return base, pl.multiple_of(start, 16)
+
+    def copies(i):
+        _, start = place_of(i)
+        return [
+            pltpu.make_async_copy(
+                rows.at[i], target.at[i, pl.ds(start, window), :], sems.at[k, i]
+            )
+            for k, (rows, target) in enumerate(((k_rows, keys_out), (v_rows, values_out)))
+        ]
+
+    for i in range(group):
+        base, start = place_of(i)
+
+        @pl.when((base > -steps) & (base < slots))
+        def _():
+            slot = start + lax.broadcasted_iota(jnp.int32, (window, width), 0)
+            for source, fresh, rows in ((keys, ks, k_rows), (values, vs, v_rows)):
+                block = source[i, pl.ds(start, window), :].astype(F32)
+                for t in range(steps):
+                    at_row = fresh[i * steps + t : i * steps + t + 1, :]
+                    block = jnp.where(slot == base + t, at_row, block)
+                rows[i] = block.astype(BF16)
+            for copy in copies(i):
+                copy.start()
+
+    for i in range(group):
+        base, _ = place_of(i)
+
+        @pl.when((base > -steps) & (base < slots))
+        def _():
+            for copy in copies(i):
+                copy.wait()
 
 
 def split_three(value):
@@ -190,96 +272,88 @@
     return pltpu.roll(value, by % LANES, 1)
 
 
+def pairs_of(query):
+    side = lax.rem(lax.div(lax.broadcasted_iota(jnp.int32, query.shape, 1), HEAD), 2)
+    return jnp.concatenate(
+        [jnp.where(side == 0, query, 0.0), jnp.where(side == 1, query, 0.0)], axis=0
+    ).astype(BF16)
+
+
 def attention_kernel(place, heads, steps, *refs):
     nx, nz = place.nx, place.nz
     gathered = refs[:nz]
-    lengths, keys_in, values_in, keys_out, values_out = refs[nz : nz + 5]
-    messages = refs[nz + 5 : nz + 5 + nx]
-    qs, ks, vs, scores, part, stats, keys, values, in_sems, out_sems = refs[nz + 5 + nx :]
+    fresh, lengths, keys, values = refs[nz : nz + 4]
+    messages = refs[nz + 4 : nz + 4 + nx]
+    qs, scores, part, stats = refs[nz + 4 + nx :]
     group, slots, width = keys.shape
     cols = width // place.seqs
     seq = lax.axis_index("seq")
-
-    def copies(sources, targets, sems, i):
-        return [
-            pltpu.make_async_copy(source.at[i], target.at[i], sems.at[k, i])
-            for k, (source, target) in enumerate(zip(sources, targets))
-        ]
-
-    def coming(i):
-        return copies((keys_in, values_in), (keys, values), in_sems, i)
-
-    def going(i):
-        return copies((keys, values), (keys_out, values_out), out_sems, i)
-
-    for i in range(group):
-        for copy in coming(i):
-            copy.start()
     for dz in range(nz):
-        span = at(place.z_partner(dz), nx * cols)
-        for k, target in enumerate((qs, ks, vs)):
-            target[:, span] = side_by_side(gathered[dz], k * cols, cols)
-    window = min(32, slots)
-    for i in range(group):
-        base = lengths[i] - seq * slots
-        for copy in coming(i):
-            copy.wait()
-
-        @pl.when((base > -steps) & (base < slots))
-        def _():
-            start = jnp.clip(lax.div(jnp.maximum(base, 0), 16) * 16, 0, slots - window)
-            here = pl.ds(pl.multiple_of(start, 16), window)
-            slot = start + lax.broadcasted_iota(jnp.int32, (window, width), 0)
-            for target, fresh in ((keys, ks), (values, vs)):
-                block = target[i, here, :].astype(F32)
-                for t in range(steps):
-                    at_row = fresh[i * steps + t : i * steps + t + 1, :]
-                    block = jnp.where(slot == base + t, at_row, block)
-                target[i, here, :] = block.astype(BF16)
-
-        for copy in going(i):
-            copy.start()
-
+        qs[:, at(place.z_partner(dz), nx * cols)] = side_by_side(gathered[dz], 0, cols)
     pack = max(1, min(group, 256 // slots))
     rows = pack * steps
     tile = 2 * HEAD
-    side = lax.rem(lax.div(lax.broadcasted_iota(jnp.int32, (rows, width), 1), HEAD), 2)
+    tiles = nx * cols // tile
+    first = place.z_partner(0) * tiles
+    own_query = side_by_side(gathered[0], 0, cols)
+    own_key = side_by_side(fresh, 0, cols)
+    own_value = side_by_side(fresh, cols, cols)
     left = lax.broadcasted_iota(jnp.int32, (rows, tile), 1) < HEAD
-    many = heads * rows
-    row = lax.broadcasted_iota(jnp.int32, (many, pack * slots), 0)
-    column = lax.broadcasted_iota(jnp.int32, (many, pack * slots), 1)
+    many, cached = heads * rows, pack * slots
+    row = lax.broadcasted_iota(jnp.int32, (many, cached + LANES), 0)
+    column = lax.broadcasted_iota(jnp.int32, (many, cached + LANES), 1)
     owner = lax.div(lax.rem(row, rows), steps)
-    step = lax.rem(row, steps)
     position = seq * slots + lax.rem(column, slots)
-    same = owner == lax.div(column, slots)
+    same = (column < cached) & (owner == lax.div(column, slots))
+    mine_tile = lax.div(row, 2 * rows) - first
+    new = column - cached
+    own = (
+        (new >= 0)
+        & (new < rows)
+        & (lax.div(new, steps) == owner)
+        & (lax.rem(new, steps) <= lax.rem(row, steps))
+        & (mine_tile >= 0)
+        & (mine_tile < tiles)
+        & (place.x() == 0)
+    )
     lane = lax.broadcasted_iota(jnp.int32, (rows, LANES), 1)
+    blank = jnp.zeros((LANES - rows, nx * cols), BF16)
     for g in range(group // pack):
         mine = slice(g * rows, (g + 1) * rows)
-        query = qs[mine, :]
-        pair = jnp.concatenate(
-            [jnp.where(side == 0, query, 0.0), jnp.where(side == 1, query, 0.0)], axis=0
-        ).astype(BF16)
         these = slice(g * pack, (g + 1) * pack)
-        key = keys[these].reshape(pack * slots, width)
-        value = values[these].reshape(pack * slots, width)
+        pair = pairs_of(qs[mine, :])
+        key = keys[these].reshape(cached, width)
+        value = values[these].reshape(cached, width)
+        new_key = jnp.concatenate([own_key[mine].astype(BF16), blank], axis=0)
+        new_value = jnp.concatenate([own_value[mine].astype(BF16), blank], axis=0)
+        own_pair = pairs_of(own_query[mine])
         for j in range(heads // 2):
             span = slice(j * tile, (j + 1) * tile)
-            scores[j * 2 * rows : (j + 1) * 2 * rows, :] = lax.dot_general(
-                pair[:, span], key[:, span], (((1,), (1,)), ((), ())), preferred_element_type=F32
-            )
-        limit = step
+            scores[j * 2 * rows : (j + 1) * 2 * rows, :cached] = across(pair[:, span], key[:, span])
+        scores[:, cached:] = jnp.zeros((many, LANES), F32)
+        for j in range(tiles):
+            span = slice(j * tile, (j + 1) * tile)
+            scores[at(first + j, 2 * rows), cached:] = across(own_pair[:, span], new_key[:, span])
+        limit = jnp.zeros_like(owner)
         for k in range(pack):
-            limit = jnp.where(owner == k, step + lengths[g * pack + k], limit)
-        valid = same & (position <= limit)
+            limit = jnp.where(owner == k, lengths[g * pack + k], limit)
+        valid = (same & (position < limit)) | own
         masked = jnp.where(valid, scores[...] * HEAD ** (-0.5), -1e30)
         peak = jnp.max(masked, axis=-1, keepdims=True)
         expo = jnp.where(valid, jnp.exp(masked - peak), 0.0)
         total = jnp.sum(expo, axis=-1, keepdims=True)
-        probs = expo.astype(BF16)
+        scores[...] = expo
         for j in range(heads // 2):
             span = slice(j * tile, (j + 1) * tile)
-            mixed = dot(probs[j * 2 * rows : (j + 1) * 2 * rows], value[:, span])
+            probs = scores[j * 2 * rows : (j + 1) * 2 * rows, :cached].astype(BF16)
+            mixed = dot(probs, value[:, span])
             part[mine, span] = jnp.where(left, mixed[:rows], mixed[rows:])
+        for j in range(tiles):
+            span = slice(j * tile, (j + 1) * tile)
+            probs = scores[at(first + j, 2 * rows), cached:].astype(BF16)
+            mixed = dot(probs, new_value[:, span])
+            here = at(first + j, tile)
+            part[mine, here] = part[mine, here] + jnp.where(left, mixed[:rows], mixed[rows:])
         line = jnp.zeros((rows, LANES), F32)
         for k, piece in enumerate(split_three(peak) + split_three(total)[:2]):
             for h in range(heads):
@@ -292,9 +366,6 @@
         messages[dx][:, share:] = pltpu.roll(
             stats[...], lax.rem(LANES - to * (heads // nx), LANES), 1
         ).astype(BF16)
-    for i in range(group):
-        for copy in going(i):
-            copy.wait()
 
 
 def expand(factor, count):
@@ -482,14 +553,25 @@
     cols = w_query.shape[1]
     own = [w_query, w_key, w_value]
     siblings = [place.move(weight, dc=1) for weight in own]
+    new_keys, new_values, keys, values, mark = call(
+        cache_kernel,
+        "caches",
+        [cache_keys, cache_values],
+        [shape(cache_keys.shape)] * 4 + [shape((8, LANES), F32)],
+        in_specs=[HBM, HBM],
+        out_specs=[HBM, HBM, VMEM, VMEM, VMEM],
+        scratch=[pltpu.SemaphoreType.DMA((2, group)), pltpu.SemaphoreType.DMA((2, group))],
+        moved=16 * 1024 * 1024,
+        limit=46,
+    )
     scales = row(jnp.concatenate([norm1_gain, norm1_bias]))
     biases = row(jnp.concatenate([b_query, b_key, b_value]))
     normed, *own = call(
         norm_kernel,
         "norm",
-        [tokens, scales, *own],
+        [mark, tokens, scales, *own],
         [shape((rows, width))] + [shape(w.shape) for w in own],
-        in_specs=[VMEM] * 2 + [HBM] * 3,
+        in_specs=[VMEM] * 3 + [HBM] * 3,
         scratch=[pltpu.VMEM((rows, width), F32), pltpu.SemaphoreType.DMA((3,))],
     )
     parts = call(
@@ -502,46 +584,63 @@
     *parts, tied_up, tied_down = lax.optimization_barrier((*parts, w_up, w_down))
     w_up_sibling = place.move(tied_up, dc=1)
     w_down_sibling = place.move(tied_down, dc=1)
-    qkv = call(
-        bind(add_columns_kernel, place), "add_qkv", spread(parts), shape((nx, rows, 3 * cols))
-    )
-
-    qkv, w_up_sibling, w_down_sibling = lax.optimization_barrier(
-        (qkv, w_up_sibling, w_down_sibling)
-    )
-    qkv, tied_w_out = lax.optimization_barrier((qkv, w_out))
-    blocks = [place.transpose(tied_w_out, k) for k in range(nx)]
-    pack = max(1, min(group, 256 // slots))
-    new_keys, new_values, *messages = call(
+    query, fresh = call(
+        bind(add_qkv_kernel, place),
+        "add_qkv",
+        spread(parts),
+        [shape((nx, rows, cols)), shape((nx, rows, 2 * cols))],
+    )
+    query, fresh, w_up_sibling, w_down_sibling, tied = lax.optimization_barrier(
+        (query, fresh, w_up_sibling, w_down_sibling, w_out)
+    )
+    blocks = [place.transpose(tied, k) for k in range(nx)]
+    queries, fresh = lax.optimization_barrier((place.gather_z(query), fresh))
+    messages = call(
         bind(attention_kernel, place, heads, steps),
         "attention",
-        [*place.gather_z(qkv), lengths, cache_keys, cache_values],
-        [shape(cache_keys.shape), shape(cache_values.shape)] + [shape((rows, share + LANES))] * nx,
-        in_specs=[VMEM] * place.nz + [SMEM, HBM, HBM],
-        out_specs=[HBM, HBM] + [VMEM] * nx,
+        [*queries, fresh, lengths, keys, values],
+        [shape((rows, share + LANES))] * nx,
+        in_specs=[VMEM] * (place.nz + 1) + [SMEM, VMEM, VMEM],
+        scratch=[
+            pltpu.VMEM((rows, width), F32),
+            pltpu.VMEM(
+                (
+                    heads * max(1, min(group, 256 // slots)) * steps,
+                    max(1, min(group, 256 // slots)) * slots + LANES,
+                ),
+                F32,
+            ),
+            pltpu.VMEM((rows, width), F32),
+            pltpu.VMEM((rows, LANES), F32),
+        ],
+    )
+    fresh = place.gather_z(fresh)
+    messages, blocks = lax.optimization_barrier((messages, blocks))
+    messages = [messages[0]] + [place.move(messages[dx], dx=dx) for dx in range(1, nx)]
+    merged = call(
+        bind(merge_x_kernel, place, heads), "merge_x", messages, shape((rows, share + LANES))
+    )
+    merged, blocks, fresh = lax.optimization_barrier((merged, blocks, fresh))
+    w_outs = []
+    for block in blocks:
+        w_outs += [block, place.move(block, dc=1)]
+    window = min(32, slots)
+    new_keys, new_values = call(
+        bind(insert_kernel, place, steps),
+        "insert",
+        [*fresh, lengths, keys, values, new_keys, new_values],
+        [shape(cache_keys.shape)] * 2,
+        in_specs=[VMEM] * place.nz + [SMEM, VMEM, VMEM, HBM, HBM],
+        out_specs=[HBM, HBM],
         scratch=[
             pltpu.VMEM((rows, width), F32),
             pltpu.VMEM((rows, width), F32),
-            pltpu.VMEM((rows, width), F32),
-            pltpu.VMEM((heads * pack * steps, pack * slots), F32),
-            pltpu.VMEM((rows, width), F32),
-            pltpu.VMEM((rows, LANES), F32),
-            pltpu.VMEM(cache_keys.shape, BF16),
-            pltpu.VMEM(cache_keys.shape, BF16),
-            pltpu.SemaphoreType.DMA((2, group)),
+            pltpu.VMEM((group, window, width), BF16),
+            pltpu.VMEM((group, window, width), BF16),
             pltpu.SemaphoreType.DMA((2, group)),
         ],
-        limit=52,
-    )
-    *messages, blocks = lax.optimization_barrier((*messages, blocks))
-    w_outs = []
-    for block in blocks:
-        w_outs += [block, place.move(block, dc=1)]
-    messages = [messages[0]] + [place.move(messages[dx], dx=dx) for dx in range(1, nx)]
-    merged = call(
-        bind(merge_x_kernel, place, heads), "merge_x", messages, shape((rows, share + LANES))
-    )
-    merged, *w_outs = lax.optimization_barrier((merged, *w_outs))
+        aliases={place.nz + 3: 0, place.nz + 4: 1},
+    )
     attn = call(
         bind(merge_z_kernel, place, heads), "merge_z", place.gather_z(merged), shape((rows, share))
     )

time: 92.6 us -> 98.2 us (1.060)
  starting transfers between devices: 40.5 us -> 43.6 us
  waiting for transfers between devices: 36.7 us -> 39.4 us
  Pallas kernels: 9.05 us -> 11.4 us
  local copies, waits for them, and re-layouts: 3.81 us -> 1.9 us
    ppermute x32 -> x35, waiting for transfers between devices: 36.7 us -> 39.4 us  [move(): return lax.ppermute(value, ('seq', 'req'), pairs)]
    ppermute x2, starting transfers between devices: 1.76 us -> 4.12 us  [transpose(): return lax.ppermute(value, ('seq', 'req'), pairs)]
    pallas_call x13 -> x15, Pallas kernels: 9.05 us -> 11.4 us  [call(): pl.pallas_call(kernel, name=name, out_shape=outs, in_specs=in_specs or [V...]
    unnamed x28 -> x32, local copies, waits for them, and re-layouts: 3.81 us -> 1.9 us
    ppermute x32 -> x35, starting transfers between devices: 38.7 us -> 39.4 us  [move(): return lax.ppermute(value, ('seq', 'req'), pairs)]
  transfers between devices with their start and end apart: 34 -> 37, of which waited for: 18 -> 21; matrix products, arithmetic and copies ran while one was open for 2% -> 1% of each run, Pallas kernels for 6% -> 8%
where the time goes in v6:
time: 98.2 us; the launch traced here: 98 us
  starting transfers between devices  43.6 us (44%)
  waiting for transfers between devices  39.4 us (40%)
  Pallas kernels  11.4 us (12%)
  local copies, waits for them, and re-layouts  1.9 us (2%)
  between operations  1.01 us (1%)
    ppermute x35, starting transfers between devices, move(): return lax.ppermute(value, ('seq', 'req'), pairs)  39.4 us
    ppermute x35, waiting for transfers between devices, move(): return lax.ppermute(value, ('seq', 'req'), pairs)  39.4 us
    pallas_call x15, Pallas kernels, call(): pl.pallas_call(kernel, name=name, out_shape=outs, in_specs=in_specs or [V...  11.4 us
    ppermute x2, starting transfers between devices, transpose(): return lax.ppermute(value, ('seq', 'req'), pairs)  4.12 us
  transfers between devices with their start and end apart: 37, of which 21 were waited for; matrix products, arithmetic and copies ran while one was open for 1% of the time, Pallas kernels for 8%

profile of v6, /device:TPU:0, one launch (start us, length us, event | category | flops | bytes accessed | tf_op | source)
XLA Modules:
  0.0 98.0 jit_solution(16296709844098279147)
XLA Ops:
  1.7 2.6 %collective-permute-start = (bf16[8,4,2048]{2,1,0:T(4,128)(2,1)}, bf16[8,4,2048]{2,1,0:T(4,128)(2,1)S(1)}, u32[]{:S(2)}, u32[]{:S(2)}) collective-permute-start(bf16[8,4,2048]{2,1,0:T(4,128)(2,1)} %refs_0_.3), channel_id=1, source_target_pairs={{0,2},{1,3},{2,0},{3,1},{4,6},{5,7},{6,4},{7,5},{8,10},{9,11},{10,... | collective-permute-start | bytes 393224 | tf_op jit(solution)/shard_map/ppermute | solution.py:62
  5.0 1.6 %copy-done = bf16[8,64,2048]{2,1,0:T(8,128)(2,1)S(1)} copy-done((bf16[8,64,2048]{2,1,0:T(8,128)(2,1)S(1)}, bf16[8,64,2048]{2,1,0:T(8,128)(2,1)}, u32[]{:S(2)}) %copy-start) | copy-done | bytes 2097176
  6.6 3.2 %caches.1 = (bf16[8,64,2048]{2,1,0:T(8,128)(2,1)}, bf16[8,64,2048]{2,1,0:T(8,128)(2,1)}, bf16[8,64,2048]{2,1,0:T(8,128)(2,1)S(1)}, bf16[8,64,2048]{2,1,0:T(8,128)(2,1)S(1)}, f32[8,128]{1,0:T(8,128)S(1)}) custom-call(bf16[8,64,2048]{2,1,0:T(8,128)(2,1)S(1)} %copy-done, bf16[8,64,2048]{2,1,0:T(8,128)(2,1)} %values_in.1), custom_call_target="tpu_custom_call" | custom-call | bytes 16777216 | tf_op jit(solution)/shard_map/caches/pallas_call | solution.py:104
  11.9 1.8 %collective-permute-start.5 = (bf16[32,768]{1,0:T(8,128)(2,1)S(1)}, bf16[32,768]{1,0:T(8,128)(2,1)S(1)}, u32[]{:S(2)}, u32[]{:S(2)}) collective-permute-start(bf16[32,768]{1,0:T(8,128)(2,1)S(1)} %get-tuple-element.58.refs_0_), channel_id=1, source_target_pairs={{0,4},{1,5},{2,6},{3,7},{4,0},{5,1},{6,2},{7,3},{8,12},{9,13},{10,... | collective-permute-start | bytes 147464 | tf_op jit(solution)/shard_map/ppermute | solution.py:62
  13.6 1.5 %collective-permute-start.6 = (bf16[32,768]{1,0:T(8,128)(2,1)S(1)}, bf16[32,768]{1,0:T(8,128)(2,1)S(1)}, u32[]{:S(2)}, u32[]{:S(2)}) collective-permute-start(bf16[32,768]{1,0:T(8,128)(2,1)S(1)} %get-tuple-element.59), channel_id=1, source_target_pairs={{0,6},{1,7},{2,4},{3,5},{4,2},{5,3},{6,0},{7,1},{8,14},{9,15},{10,... | collective-permute-start | bytes 147464 | tf_op jit(solution)/shard_map/ppermute | solution.py:62
  15.9 2.7 %collective-permute-done.6.refs_3_ = bf16[32,768]{1,0:T(8,128)(2,1)S(1)} collective-permute-done((bf16[32,768]{1,0:T(8,128)(2,1)S(1)}, bf16[32,768]{1,0:T(8,128)(2,1)S(1)}, u32[]{:S(2)}, u32[]{:S(2)}) %collective-permute-start.6) | collective-permute-done | bytes 49184 | tf_op jit(solution)/shard_map/ppermute | solution.py:62
  19.4 3.4 %collective-permute-start.13 = (bf16[512,256]{1,0:T(8,128)(2,1)S(1)}, bf16[512,256]{1,0:T(8,128)(2,1)S(1)}, u32[]{:S(2)}, u32[]{:S(2)}) collective-permute-start(bf16[512,256]{1,0:T(8,128)(2,1)S(1)} %copy-done.15), channel_id=1, source_target_pairs={{0,2},{1,3},{2,6},{3,7},{4,0},{5,1},{6,4},{7,5},{8,10},{9,11},{10,... | collective-permute-start | bytes 786440 | tf_op jit(solution)/shard_map/ppermute | solution.py:77
  22.8 1.6 %collective-permute-start.9 = (bf16[2,32,256]{2,1,0:T(8,128)(2,1)S(1)}, bf16[2,32,256]{2,1,0:T(8,128)(2,1)S(1)}, u32[]{:S(2)}, u32[]{:S(2)}) collective-permute-start(bf16[2,32,256]{2,1,0:T(8,128)(2,1)S(1)} %get-tuple-element.66.refs_0_), channel_id=1, source_target_pairs={{0,8},{1,9},{2,10},{3,11},{4,12},{5,13},{6,14},{7,15},{8,0},{9,1},... | collective-permute-start | bytes 98312 | tf_op jit(solution)/shard_map/ppermute | solution.py:62
  24.4 2.6 %collective-permute-start.10 = (bf16[2,32,256]{2,1,0:T(8,128)(2,1)S(1)}, bf16[2,32,256]{2,1,0:T(8,128)(2,1)S(1)}, u32[]{:S(2)}, u32[]{:S(2)}) collective-permute-start(bf16[2,32,256]{2,1,0:T(8,128)(2,1)S(1)} %get-tuple-element.66.refs_0_), channel_id=1, source_target_pairs={{0,16},{1,17},{2,18},{3,19},{4,20},{5,21},{6,22},{7,23},{8,24},{9,... | collective-permute-start | bytes 98312 | tf_op jit(solution)/shard_map/ppermute | solution.py:62
  27.2 2.6 %collective-permute-done.10.refs_2_ = bf16[2,32,256]{2,1,0:T(8,128)(2,1)S(1)} collective-permute-done((bf16[2,32,256]{2,1,0:T(8,128)(2,1)S(1)}, bf16[2,32,256]{2,1,0:T(8,128)(2,1)S(1)}, u32[]{:S(2)}, u32[]{:S(2)}) %collective-permute-start.10) | collective-permute-done | bytes 32800 | tf_op jit(solution)/shard_map/ppermute | solution.py:62
  29.8 2.9 %collective-permute-done.11.refs_3_ = bf16[2,32,256]{2,1,0:T(8,128)(2,1)S(1)} collective-permute-done((bf16[2,32,256]{2,1,0:T(8,128)(2,1)S(1)}, bf16[2,32,256]{2,1,0:T(8,128)(2,1)S(1)}, u32[]{:S(2)}, u32[]{:S(2)}) %collective-permute-start.11) | collective-permute-done | bytes 32800 | tf_op jit(solution)/shard_map/ppermute | solution.py:62
  32.7 2.2 %attention.1 = (bf16[32,1152]{1,0:T(8,128)(2,1)S(1)}, bf16[32,1152]{1,0:T(8,128)(2,1)S(1)}) custom-call(bf16[2,32,256]{2,1,0:T(8,128)(2,1)S(1)} %get-tuple-element.66.refs_0_, bf16[2,32,256]{2,1,0:T(8,128)(2,1)S(1)} %collective-permute-done.9.refs_1_, bf16[2,32,256]{2,1,0:T(8,128)(2,1)S(1)} %collective-permute-done.10.refs_2_, ...), custom_call_target="tpu_custom_call" | custom-call | bytes 1048576 | tf_op jit(solution)/shard_map/attention/pallas_call | solution.py:104
  36.5 2.6 %collective-permute-start.16 = (bf16[2,32,512]{2,1,0:T(8,128)(2,1)S(1)}, bf16[2,32,512]{2,1,0:T(8,128)(2,1)S(1)}, u32[]{:S(2)}, u32[]{:S(2)}) collective-permute-start(bf16[2,32,512]{2,1,0:T(8,128)(2,1)S(1)} %get-tuple-element.91.refs_4_.refs_0_), channel_id=1, source_target_pairs={{0,16},{1,17},{2,18},{3,19},{4,20},{5,21},{6,22},{7,23},{8,24},{9,... | collective-permute-start | bytes 196616 | tf_op jit(solution)/shard_map/ppermute | solution.py:62
  40.8 2.8 %collective-permute-done.16.refs_2_ = bf16[2,32,512]{2,1,0:T(8,128)(2,1)S(1)} collective-permute-done((bf16[2,32,512]{2,1,0:T(8,128)(2,1)S(1)}, bf16[2,32,512]{2,1,0:T(8,128)(2,1)S(1)}, u32[]{:S(2)}, u32[]{:S(2)}) %collective-permute-start.16) | collective-permute-done | bytes 65568 | tf_op jit(solution)/shard_map/ppermute | solution.py:62
  43.6 1.5 %collective-permute-done.17.refs_3_ = bf16[2,32,512]{2,1,0:T(8,128)(2,1)S(1)} collective-permute-done((bf16[2,32,512]{2,1,0:T(8,128)(2,1)S(1)}, bf16[2,32,512]{2,1,0:T(8,128)(2,1)S(1)}, u32[]{:S(2)}, u32[]{:S(2)}) %collective-permute-start.17) | collective-permute-done | bytes 65568 | tf_op jit(solution)/shard_map/ppermute | solution.py:62
  45.6 2.3 %collective-permute-start.19 = (bf16[32,1152]{1,0:T(8,128)(2,1)S(1)}, bf16[32,1152]{1,0:T(8,128)(2,1)S(1)}, u32[]{:S(2)}, u32[]{:S(2)}) collective-permute-start(bf16[32,1152]{1,0:T(8,128)(2,1)S(1)} %merge_x.1.refs_0_), channel_id=1, source_target_pairs={{0,16},{1,17},{2,18},{3,19},{4,20},{5,21},{6,22},{7,23},{8,24},{9,... | collective-permute-start | bytes 221192 | tf_op jit(solution)/shard_map/ppermute | solution.py:62
  47.9 2.1 %collective-permute-start.20 = (bf16[32,1152]{1,0:T(8,128)(2,1)S(1)}, bf16[32,1152]{1,0:T(8,128)(2,1)S(1)}, u32[]{:S(2)}, u32[]{:S(2)}) collective-permute-start(bf16[32,1152]{1,0:T(8,128)(2,1)S(1)} %merge_x.1.refs_0_), channel_id=1, source_target_pairs={{0,24},{1,25},{2,26},{3,27},{4,28},{5,29},{6,30},{7,31},{8,16},{9,... | collective-permute-start | bytes 221192 | tf_op jit(solution)/shard_map/ppermute | solution.py:62
  51.2 3.4 %collective-permute-done.19.refs_2_ = bf16[32,1152]{1,0:T(8,128)(2,1)S(1)} collective-permute-done((bf16[32,1152]{1,0:T(8,128)(2,1)S(1)}, bf16[32,1152]{1,0:T(8,128)(2,1)S(1)}, u32[]{:S(2)}, u32[]{:S(2)}) %collective-permute-start.19) | collective-permute-done | bytes 73760 | tf_op jit(solution)/shard_map/ppermute | solution.py:62
  55.3 1.3 %collective-permute-start.23 = (bf16[2,32,256]{2,1,0:T(8,128)(2,1)S(1)}, bf16[2,32,256]{2,1,0:T(8,128)(2,1)S(1)}, u32[]{:S(2)}, u32[]{:S(2)}) collective-permute-start(bf16[2,32,256]{2,1,0:T(8,128)(2,1)S(1)} %out.1.refs_0_), channel_id=1, source_target_pairs={{0,2},{1,3},{2,0},{3,1},{4,6},{5,7},{6,4},{7,5},{8,10},{9,11},{10,... | collective-permute-start | bytes 98312 | tf_op jit(solution)/shard_map/ppermute | solution.py:62
  60.5 2.0 %collective-permute-done.25.refs_3_ = bf16[2,32,256]{2,1,0:T(8,128)(2,1)S(1)} collective-permute-done((bf16[2,32,256]{2,1,0:T(8,128)(2,1)S(1)}, bf16[2,32,256]{2,1,0:T(8,128)(2,1)S(1)}, u32[]{:S(2)}, u32[]{:S(2)}) %collective-permute-start.25) | collective-permute-done | bytes 32800 | tf_op jit(solution)/shard_map/ppermute | solution.py:62
  62.5 1.7 %collective-permute-start.26 = (bf16[2,2,32,256]{3,2,1,0:T(8,128)(2,1)S(1)}, bf16[2,2,32,256]{3,2,1,0:T(8,128)(2,1)S(1)}, u32[]{:S(2)}, u32[]{:S(2)}) collective-permute-start(bf16[2,2,32,256]{3,2,1,0:T(8,128)(2,1)S(1)} %add_out.1.refs_2_), channel_id=1, source_target_pairs={{0,8},{1,9},{2,10},{3,11},{4,12},{5,13},{6,14},{7,15},{8,0},{9,1},... | collective-permute-start | bytes 196616 | tf_op jit(solution)/shard_map/ppermute | solution.py:62
  64.3 1.2 %collective-permute-start.27 = (bf16[2,2,32,256]{3,2,1,0:T(8,128)(2,1)S(1)}, bf16[2,2,32,256]{3,2,1,0:T(8,128)(2,1)S(1)}, u32[]{:S(2)}, u32[]{:S(2)}) collective-permute-start(bf16[2,2,32,256]{3,2,1,0:T(8,128)(2,1)S(1)} %add_out.1.refs_2_), channel_id=1, source_target_pairs={{0,16},{1,17},{2,18},{3,19},{4,20},{5,21},{6,22},{7,23},{8,24},{9,... | collective-permute-start | bytes 196616 | tf_op jit(solution)/shard_map/ppermute | solution.py:62
  65.5 1.5 %collective-permute-start.28 = (bf16[2,2,32,256]{3,2,1,0:T(8,128)(2,1)S(1)}, bf16[2,2,32,256]{3,2,1,0:T(8,128)(2,1)S(1)}, u32[]{:S(2)}, u32[]{:S(2)}) collective-permute-start(bf16[2,2,32,256]{3,2,1,0:T(8,128)(2,1)S(1)} %add_out.1.refs_2_), channel_id=1, source_target_pairs={{0,24},{1,25},{2,26},{3,27},{4,28},{5,29},{6,30},{7,31},{8,16},{9,... | collective-permute-start | bytes 196616 | tf_op jit(solution)/shard_map/ppermute | solution.py:62
  67.3 2.8 %collective-permute-done.27.refs_4_ = bf16[2,2,32,256]{3,2,1,0:T(8,128)(2,1)S(1)} collective-permute-done((bf16[2,2,32,256]{3,2,1,0:T(8,128)(2,1)S(1)}, bf16[2,2,32,256]{3,2,1,0:T(8,128)(2,1)S(1)}, u32[]{:S(2)}, u32[]{:S(2)}) %collective-permute-start.27) | collective-permute-done | bytes 65568 | tf_op jit(solution)/shard_map/ppermute | solution.py:62
  70.1 1.4 %collective-permute-done.28.refs_5_ = bf16[2,2,32,256]{3,2,1,0:T(8,128)(2,1)S(1)} collective-permute-done((bf16[2,2,32,256]{3,2,1,0:T(8,128)(2,1)S(1)}, bf16[2,2,32,256]{3,2,1,0:T(8,128)(2,1)S(1)}, u32[]{:S(2)}, u32[]{:S(2)}) %collective-permute-start.28) | collective-permute-done | bytes 65568 | tf_op jit(solution)/shard_map/ppermute | solution.py:62
  73.1 4.4 %collective-permute-done.29.refs_1_ = bf16[64,1024]{1,0:T(8,128)(2,1)S(1)} collective-permute-done((bf16[64,1024]{1,0:T(8,128)(2,1)S(1)}, bf16[64,1024]{1,0:T(8,128)(2,1)S(1)}, u32[]{:S(2)}, u32[]{:S(2)}) %collective-permute-start.29) | collective-permute-done | bytes 131104 | tf_op jit(solution)/shard_map/ppermute | solution.py:62
  78.7 3.7 %collective-permute-done.30.refs_1_ = bf16[64,512]{1,0:T(8,128)(2,1)S(1)} collective-permute-done((bf16[64,512]{1,0:T(8,128)(2,1)S(1)}, bf16[64,512]{1,0:T(8,128)(2,1)S(1)}, u32[]{:S(2)}, u32[]{:S(2)}) %collective-permute-start.30) | collective-permute-done | bytes 65568 | tf_op jit(solution)/shard_map/ppermute | solution.py:62
  82.4 2.2 %collective-permute-start.32 = (bf16[64,512]{1,0:T(8,128)(2,1)S(1)}, bf16[64,512]{1,0:T(8,128)(2,1)S(1)}, u32[]{:S(2)}, u32[]{:S(2)}) collective-permute-start(bf16[64,512]{1,0:T(8,128)(2,1)S(1)} %add_x.1.refs_0_), channel_id=1, source_target_pairs={{0,16},{1,17},{2,18},{3,19},{4,20},{5,21},{6,22},{7,23},{8,24},{9,... | collective-permute-start | bytes 196616 | tf_op jit(solution)/shard_map/ppermute | solution.py:62
  84.6 2.2 %collective-permute-start.33 = (bf16[64,512]{1,0:T(8,128)(2,1)S(1)}, bf16[64,512]{1,0:T(8,128)(2,1)S(1)}, u32[]{:S(2)}, u32[]{:S(2)}) collective-permute-start(bf16[64,512]{1,0:T(8,128)(2,1)S(1)} %add_x.1.refs_0_), channel_id=1, source_target_pairs={{0,24},{1,25},{2,26},{3,27},{4,28},{5,29},{6,30},{7,31},{8,16},{9,... | collective-permute-start | bytes 196616 | tf_op jit(solution)/shard_map/ppermute | solution.py:62
  87.6 3.0 %collective-permute-done.33.refs_3_ = bf16[64,512]{1,0:T(8,128)(2,1)S(1)} collective-permute-done((bf16[64,512]{1,0:T(8,128)(2,1)S(1)}, bf16[64,512]{1,0:T(8,128)(2,1)S(1)}, u32[]{:S(2)}, u32[]{:S(2)}) %collective-permute-start.33) | collective-permute-done | bytes 65568 | tf_op jit(solution)/shard_map/ppermute | solution.py:62
  92.4 1.8 %collective-permute-start.36 = (bf16[32,512]{1,0:T(8,128)(2,1)S(1)}, bf16[32,512]{1,0:T(8,128)(2,1)S(1)}, u32[]{:S(2)}, u32[]{:S(2)}) collective-permute-start(bf16[32,512]{1,0:T(8,128)(2,1)S(1)} %get-tuple-element.89), channel_id=1, source_target_pairs={{0,6},{1,7},{2,4},{3,5},{4,2},{5,3},{6,0},{7,1},{8,14},{9,15},{10,... | collective-permute-start | bytes 98312 | tf_op jit(solution)/shard_map/ppermute | solution.py:62
  94.2 1.8 %insert.1 = (bf16[8,64,2048]{2,1,0:T(8,128)(2,1)}, bf16[8,64,2048]{2,1,0:T(8,128)(2,1)}) custom-call(bf16[2,32,512]{2,1,0:T(8,128)(2,1)S(1)} %get-tuple-element.91.refs_4_.refs_0_, bf16[2,32,512]{2,1,0:T(8,128)(2,1)S(1)} %collective-permute-done.15.refs_1_, ...), custom_call_target="tpu_custom_call", output_to_operand_aliasing={{0}: (7, {}), {1}: (8, {})} | custom-call | bytes 1048576 | tf_op jit(solution)/shard_map/insert/pallas_call | solution.py:104
  (92 shorter events, 22.7 us)
Async XLA Ops:
  0.6 9.7 %collective-permute-start.1 = (bf16[512,256]{1,0:T(8,128)(2,1)}, bf16[512,256]{1,0:T(8,128)(2,1)S(1)}, u32[]{:S(2)}, u32[]{:S(2)}) collective-permute-start(bf16[512,256]{1,0:T(8,128)(2,1)} %refs_0_.2), channel_id=1, source_target_pairs={{0,1},{1,0},{2,3},{3,2},{4,5},{5,4},{6,7},{7,6},{8,9},{9,8},{10,11... | collective-permute-start | bytes 786440 | tf_op jit(solution)/shard_map/ppermute | solution.py:62
  1.1 9.2 %collective-permute-start.2 = (bf16[512,256]{1,0:T(8,128)(2,1)}, bf16[512,256]{1,0:T(8,128)(2,1)S(1)}, u32[]{:S(2)}, u32[]{:S(2)}) collective-permute-start(bf16[512,256]{1,0:T(8,128)(2,1)} %refs_1_.1), channel_id=1, source_target_pairs={{0,1},{1,0},{2,3},{3,2},{4,5},{5,4},{6,7},{7,6},{8,9},{9,8},{10,11... | collective-permute-start | bytes 786440 | tf_op jit(solution)/shard_map/ppermute | solution.py:62
  1.2 9.1 %collective-permute-start.3 = (bf16[512,256]{1,0:T(8,128)(2,1)}, bf16[512,256]{1,0:T(8,128)(2,1)S(1)}, u32[]{:S(2)}, u32[]{:S(2)}) collective-permute-start(bf16[512,256]{1,0:T(8,128)(2,1)} %refs_2_.2), channel_id=1, source_target_pairs={{0,1},{1,0},{2,3},{3,2},{4,5},{5,4},{6,7},{7,6},{8,9},{9,8},{10,11... | collective-permute-start | bytes 786440 | tf_op jit(solution)/shard_map/ppermute | solution.py:62
  1.7 8.7 %collective-permute-start = (bf16[8,4,2048]{2,1,0:T(4,128)(2,1)}, bf16[8,4,2048]{2,1,0:T(4,128)(2,1)S(1)}, u32[]{:S(2)}, u32[]{:S(2)}) collective-permute-start(bf16[8,4,2048]{2,1,0:T(4,128)(2,1)} %refs_0_.3), channel_id=1, source_target_pairs={{0,2},{1,3},{2,0},{3,1},{4,6},{5,7},{6,4},{7,5},{8,10},{9,11},{10,... | collective-permute-start | bytes 393224 | tf_op jit(solution)/shard_map/ppermute | solution.py:62
  11.1 7.5 %collective-permute-start.7 = (bf16[512,1024]{1,0:T(8,128)(2,1)S(1)}, bf16[512,1024]{1,0:T(8,128)(2,1)S(1)}, u32[]{:S(2)}, u32[]{:S(2)}) collective-permute-start(bf16[512,1024]{1,0:T(8,128)(2,1)S(1)} %copy-done.1), channel_id=1, source_target_pairs={{0,1},{1,0},{2,3},{3,2},{4,5},{5,4},{6,7},{7,6},{8,9},{9,8},{10,11... | collective-permute-start | bytes 3145736 | tf_op jit(solution)/shard_map/ppermute | solution.py:62
  11.4 7.2 %collective-permute-start.8 = (bf16[1024,512]{1,0:T(8,128)(2,1)S(1)}, bf16[1024,512]{1,0:T(8,128)(2,1)S(1)}, u32[]{:S(2)}, u32[]{:S(2)}) collective-permute-start(bf16[1024,512]{1,0:T(8,128)(2,1)S(1)} %copy-done.2), channel_id=1, source_target_pairs={{0,1},{1,0},{2,3},{3,2},{4,5},{5,4},{6,7},{7,6},{8,9},{9,8},{10,11... | collective-permute-start | bytes 3145736 | tf_op jit(solution)/shard_map/ppermute | solution.py:62
  13.6 5.0 %collective-permute-start.6 = (bf16[32,768]{1,0:T(8,128)(2,1)S(1)}, bf16[32,768]{1,0:T(8,128)(2,1)S(1)}, u32[]{:S(2)}, u32[]{:S(2)}) collective-permute-start(bf16[32,768]{1,0:T(8,128)(2,1)S(1)} %get-tuple-element.59), channel_id=1, source_target_pairs={{0,6},{1,7},{2,4},{3,5},{4,2},{5,3},{6,0},{7,1},{8,14},{9,15},{10,... | collective-permute-start | bytes 147464 | tf_op jit(solution)/shard_map/ppermute | solution.py:62
  18.7 16.2 %collective-permute-start.12 = (bf16[512,256]{1,0:T(8,128)(2,1)S(1)}, bf16[512,256]{1,0:T(8,128)(2,1)S(1)}, u32[]{:S(2)}, u32[]{:S(2)}) collective-permute-start(bf16[512,256]{1,0:T(8,128)(2,1)S(1)} %copy-done.15), channel_id=1, source_target_pairs={{0,0},{1,1},{2,4},{3,5},{4,2},{5,3},{6,6},{7,7},{8,8},{9,9},{10,12... | collective-permute-start | bytes 786440 | tf_op jit(solution)/shard_map/ppermute | solution.py:77
  19.4 15.6 %collective-permute-start.13 = (bf16[512,256]{1,0:T(8,128)(2,1)S(1)}, bf16[512,256]{1,0:T(8,128)(2,1)S(1)}, u32[]{:S(2)}, u32[]{:S(2)}) collective-permute-start(bf16[512,256]{1,0:T(8,128)(2,1)S(1)} %copy-done.15), channel_id=1, source_target_pairs={{0,2},{1,3},{2,6},{3,7},{4,0},{5,1},{6,4},{7,5},{8,10},{9,11},{10,... | collective-permute-start | bytes 786440 | tf_op jit(solution)/shard_map/ppermute | solution.py:77
  22.8 4.4 %collective-permute-start.9 = (bf16[2,32,256]{2,1,0:T(8,128)(2,1)S(1)}, bf16[2,32,256]{2,1,0:T(8,128)(2,1)S(1)}, u32[]{:S(2)}, u32[]{:S(2)}) collective-permute-start(bf16[2,32,256]{2,1,0:T(8,128)(2,1)S(1)} %get-tuple-element.66.refs_0_), channel_id=1, source_target_pairs={{0,8},{1,9},{2,10},{3,11},{4,12},{5,13},{6,14},{7,15},{8,0},{9,1},... | collective-permute-start | bytes 98312 | tf_op jit(solution)/shard_map/ppermute | solution.py:62
  24.4 5.4 %collective-permute-start.10 = (bf16[2,32,256]{2,1,0:T(8,128)(2,1)S(1)}, bf16[2,32,256]{2,1,0:T(8,128)(2,1)S(1)}, u32[]{:S(2)}, u32[]{:S(2)}) collective-permute-start(bf16[2,32,256]{2,1,0:T(8,128)(2,1)S(1)} %get-tuple-element.66.refs_0_), channel_id=1, source_target_pairs={{0,16},{1,17},{2,18},{3,19},{4,20},{5,21},{6,22},{7,23},{8,24},{9,... | collective-permute-start | bytes 98312 | tf_op jit(solution)/shard_map/ppermute | solution.py:62
  27.0 5.7 %collective-permute-start.11 = (bf16[2,32,256]{2,1,0:T(8,128)(2,1)S(1)}, bf16[2,32,256]{2,1,0:T(8,128)(2,1)S(1)}, u32[]{:S(2)}, u32[]{:S(2)}) collective-permute-start(bf16[2,32,256]{2,1,0:T(8,128)(2,1)S(1)} %get-tuple-element.66.refs_0_), channel_id=1, source_target_pairs={{0,24},{1,25},{2,26},{3,27},{4,28},{5,29},{6,30},{7,31},{8,16},{9,... | collective-permute-start | bytes 98312 | tf_op jit(solution)/shard_map/ppermute | solution.py:62
  34.9 5.3 %collective-permute-start.14 = (bf16[32,1152]{1,0:T(8,128)(2,1)S(1)}, bf16[32,1152]{1,0:T(8,128)(2,1)S(1)}, u32[]{:S(2)}, u32[]{:S(2)}) collective-permute-start(bf16[32,1152]{1,0:T(8,128)(2,1)S(1)} %get-tuple-element.77), channel_id=1, source_target_pairs={{0,4},{1,5},{2,6},{3,7},{4,0},{5,1},{6,2},{7,3},{8,12},{9,13},{10,... | collective-permute-start | bytes 221192 | tf_op jit(solution)/shard_map/ppermute | solution.py:62
  35.9 4.9 %collective-permute-start.15 = (bf16[2,32,512]{2,1,0:T(8,128)(2,1)S(1)}, bf16[2,32,512]{2,1,0:T(8,128)(2,1)S(1)}, u32[]{:S(2)}, u32[]{:S(2)}) collective-permute-start(bf16[2,32,512]{2,1,0:T(8,128)(2,1)S(1)} %get-tuple-element.91.refs_4_.refs_0_), channel_id=1, source_target_pairs={{0,8},{1,9},{2,10},{3,11},{4,12},{5,13},{6,14},{7,15},{8,0},{9,1},... | collective-permute-start | bytes 196616 | tf_op jit(solution)/shard_map/ppermute | solution.py:62
  36.5 7.2 %collective-permute-start.16 = (bf16[2,32,512]{2,1,0:T(8,128)(2,1)S(1)}, bf16[2,32,512]{2,1,0:T(8,128)(2,1)S(1)}, u32[]{:S(2)}, u32[]{:S(2)}) collective-permute-start(bf16[2,32,512]{2,1,0:T(8,128)(2,1)S(1)} %get-tuple-element.91.refs_4_.refs_0_), channel_id=1, source_target_pairs={{0,16},{1,17},{2,18},{3,19},{4,20},{5,21},{6,22},{7,23},{8,24},{9,... | collective-permute-start | bytes 196616 | tf_op jit(solution)/shard_map/ppermute | solution.py:62
  39.0 6.1 %collective-permute-start.17 = (bf16[2,32,512]{2,1,0:T(8,128)(2,1)S(1)}, bf16[2,32,512]{2,1,0:T(8,128)(2,1)S(1)}, u32[]{:S(2)}, u32[]{:S(2)}) collective-permute-start(bf16[2,32,512]{2,1,0:T(8,128)(2,1)S(1)} %get-tuple-element.91.refs_4_.refs_0_), channel_id=1, source_target_pairs={{0,24},{1,25},{2,26},{3,27},{4,28},{5,29},{6,30},{7,31},{8,16},{9,... | collective-permute-start | bytes 196616 | tf_op jit(solution)/shard_map/ppermute | solution.py:62
  45.1 9.8 %collective-permute-start.21 = (bf16[512,256]{1,0:T(8,128)(2,1)S(1)}, bf16[512,256]{1,0:T(8,128)(2,1)S(1)}, u32[]{:S(2)}, u32[]{:S(2)}) collective-permute-start(bf16[512,256]{1,0:T(8,128)(2,1)S(1)} %collective-permute-done.12.refs_0_), channel_id=1, source_target_pairs={{0,1},{1,0},{2,3},{3,2},{4,5},{5,4},{6,7},{7,6},{8,9},{9,8},{10,11... | collective-permute-start | bytes 786440 | tf_op jit(solution)/shard_map/ppermute | solution.py:62
  45.1 9.8 %collective-permute-start.22 = (bf16[512,256]{1,0:T(8,128)(2,1)S(1)}, bf16[512,256]{1,0:T(8,128)(2,1)S(1)}, u32[]{:S(2)}, u32[]{:S(2)}) collective-permute-start(bf16[512,256]{1,0:T(8,128)(2,1)S(1)} %collective-permute-done.13.refs_2_), channel_id=1, source_target_pairs={{0,1},{1,0},{2,3},{3,2},{4,5},{5,4},{6,7},{7,6},{8,9},{9,8},{10,11... | collective-permute-start | bytes 786440 | tf_op jit(solution)/shard_map/ppermute | solution.py:62
  45.6 5.6 %collective-permute-start.18 = (bf16[32,1152]{1,0:T(8,128)(2,1)S(1)}, bf16[32,1152]{1,0:T(8,128)(2,1)S(1)}, u32[]{:S(2)}, u32[]{:S(2)}) collective-permute-start(bf16[32,1152]{1,0:T(8,128)(2,1)S(1)} %merge_x.1.refs_0_), channel_id=1, source_target_pairs={{0,8},{1,9},{2,10},{3,11},{4,12},{5,13},{6,14},{7,15},{8,0},{9,1},... | collective-permute-start | bytes 221192 | tf_op jit(solution)/shard_map/ppermute | solution.py:62
  45.6 8.9 %collective-permute-start.19 = (bf16[32,1152]{1,0:T(8,128)(2,1)S(1)}, bf16[32,1152]{1,0:T(8,128)(2,1)S(1)}, u32[]{:S(2)}, u32[]{:S(2)}) collective-permute-start(bf16[32,1152]{1,0:T(8,128)(2,1)S(1)} %merge_x.1.refs_0_), channel_id=1, source_target_pairs={{0,16},{1,17},{2,18},{3,19},{4,20},{5,21},{6,22},{7,23},{8,24},{9,... | collective-permute-start | bytes 221192 | tf_op jit(solution)/shard_map/ppermute | solution.py:62
  47.9 6.7 %collective-permute-start.20 = (bf16[32,1152]{1,0:T(8,128)(2,1)S(1)}, bf16[32,1152]{1,0:T(8,128)(2,1)S(1)}, u32[]{:S(2)}, u32[]{:S(2)}) collective-permute-start(bf16[32,1152]{1,0:T(8,128)(2,1)S(1)} %merge_x.1.refs_0_), channel_id=1, source_target_pairs={{0,24},{1,25},{2,26},{3,27},{4,28},{5,29},{6,30},{7,31},{8,16},{9,... | collective-permute-start | bytes 221192 | tf_op jit(solution)/shard_map/ppermute | solution.py:62
  57.7 4.8 %collective-permute-start.25 = (bf16[2,32,256]{2,1,0:T(8,128)(2,1)S(1)}, bf16[2,32,256]{2,1,0:T(8,128)(2,1)S(1)}, u32[]{:S(2)}, u32[]{:S(2)}) collective-permute-start(bf16[2,32,256]{2,1,0:T(8,128)(2,1)S(1)} %out.1.refs_0_), channel_id=1, source_target_pairs={{0,6},{1,7},{2,4},{3,5},{4,2},{5,3},{6,0},{7,1},{8,14},{9,15},{10,... | collective-permute-start | bytes 98312 | tf_op jit(solution)/shard_map/ppermute | solution.py:62
  62.5 4.8 %collective-permute-start.26 = (bf16[2,2,32,256]{3,2,1,0:T(8,128)(2,1)S(1)}, bf16[2,2,32,256]{3,2,1,0:T(8,128)(2,1)S(1)}, u32[]{:S(2)}, u32[]{:S(2)}) collective-permute-start(bf16[2,2,32,256]{3,2,1,0:T(8,128)(2,1)S(1)} %add_out.1.refs_2_), channel_id=1, source_target_pairs={{0,8},{1,9},{2,10},{3,11},{4,12},{5,13},{6,14},{7,15},{8,0},{9,1},... | collective-permute-start | bytes 196616 | tf_op jit(solution)/shard_map/ppermute | solution.py:62
  64.3 5.9 %collective-permute-start.27 = (bf16[2,2,32,256]{3,2,1,0:T(8,128)(2,1)S(1)}, bf16[2,2,32,256]{3,2,1,0:T(8,128)(2,1)S(1)}, u32[]{:S(2)}, u32[]{:S(2)}) collective-permute-start(bf16[2,2,32,256]{3,2,1,0:T(8,128)(2,1)S(1)} %add_out.1.refs_2_), channel_id=1, source_target_pairs={{0,16},{1,17},{2,18},{3,19},{4,20},{5,21},{6,22},{7,23},{8,24},{9,... | collective-permute-start | bytes 196616 | tf_op jit(solution)/shard_map/ppermute | solution.py:62
  65.5 6.1 %collective-permute-start.28 = (bf16[2,2,32,256]{3,2,1,0:T(8,128)(2,1)S(1)}, bf16[2,2,32,256]{3,2,1,0:T(8,128)(2,1)S(1)}, u32[]{:S(2)}, u32[]{:S(2)}) collective-permute-start(bf16[2,2,32,256]{3,2,1,0:T(8,128)(2,1)S(1)} %add_out.1.refs_2_), channel_id=1, source_target_pairs={{0,24},{1,25},{2,26},{3,27},{4,28},{5,29},{6,30},{7,31},{8,16},{9,... | collective-permute-start | bytes 196616 | tf_op jit(solution)/shard_map/ppermute | solution.py:62
  72.4 5.0 %collective-permute-start.29 = (bf16[64,1024]{1,0:T(8,128)(2,1)S(1)}, bf16[64,1024]{1,0:T(8,128)(2,1)S(1)}, u32[]{:S(2)}, u32[]{:S(2)}) collective-permute-start(bf16[64,1024]{1,0:T(8,128)(2,1)S(1)} %get-tuple-element.84.refs_0_), channel_id=1, source_target_pairs={{0,2},{1,3},{2,0},{3,1},{4,6},{5,7},{6,4},{7,5},{8,10},{9,11},{10,... | collective-permute-start | bytes 393224 | tf_op jit(solution)/shard_map/ppermute | solution.py:62
  82.3 4.5 %collective-permute-start.31 = (bf16[64,512]{1,0:T(8,128)(2,1)S(1)}, bf16[64,512]{1,0:T(8,128)(2,1)S(1)}, u32[]{:S(2)}, u32[]{:S(2)}) collective-permute-start(bf16[64,512]{1,0:T(8,128)(2,1)S(1)} %add_x.1.refs_0_), channel_id=1, source_target_pairs={{0,8},{1,9},{2,10},{3,11},{4,12},{5,13},{6,14},{7,15},{8,0},{9,1},... | collective-permute-start | bytes 196616 | tf_op jit(solution)/shard_map/ppermute | solution.py:62
  82.4 5.2 %collective-permute-start.32 = (bf16[64,512]{1,0:T(8,128)(2,1)S(1)}, bf16[64,512]{1,0:T(8,128)(2,1)S(1)}, u32[]{:S(2)}, u32[]{:S(2)}) collective-permute-start(bf16[64,512]{1,0:T(8,128)(2,1)S(1)} %add_x.1.refs_0_), channel_id=1, source_target_pairs={{0,16},{1,17},{2,18},{3,19},{4,20},{5,21},{6,22},{7,23},{8,24},{9,... | collective-permute-start | bytes 196616 | tf_op jit(solution)/shard_map/ppermute | solution.py:62
  84.6 6.1 %collective-permute-start.33 = (bf16[64,512]{1,0:T(8,128)(2,1)S(1)}, bf16[64,512]{1,0:T(8,128)(2,1)S(1)}, u32[]{:S(2)}, u32[]{:S(2)}) collective-permute-start(bf16[64,512]{1,0:T(8,128)(2,1)S(1)} %add_x.1.refs_0_), channel_id=1, source_target_pairs={{0,24},{1,25},{2,26},{3,27},{4,28},{5,29},{6,30},{7,31},{8,16},{9,... | collective-permute-start | bytes 196616 | tf_op jit(solution)/shard_map/ppermute | solution.py:62
  90.7 5.4 %collective-permute-start.34 = (bf16[32,512]{1,0:T(8,128)(2,1)S(1)}, bf16[32,512]{1,0:T(8,128)(2,1)S(1)}, u32[]{:S(2)}, u32[]{:S(2)}) collective-permute-start(bf16[32,512]{1,0:T(8,128)(2,1)S(1)} %get-tuple-element.89), channel_id=1, source_target_pairs={{0,2},{1,3},{2,0},{3,1},{4,6},{5,7},{6,4},{7,5},{8,10},{9,11},{10,... | collective-permute-start | bytes 98312 | tf_op jit(solution)/shard_map/ppermute | solution.py:62
  91.6 4.4 %collective-permute-start.35 = (bf16[32,512]{1,0:T(8,128)(2,1)S(1)}, bf16[32,512]{1,0:T(8,128)(2,1)S(1)}, u32[]{:S(2)}, u32[]{:S(2)}) collective-permute-start(bf16[32,512]{1,0:T(8,128)(2,1)S(1)} %get-tuple-element.88.refs_0_), channel_id=1, source_target_pairs={{0,4},{1,5},{2,6},{3,7},{4,0},{5,1},{6,2},{7,3},{8,12},{9,13},{10,... | collective-permute-start | bytes 98312 | tf_op jit(solution)/shard_map/ppermute | solution.py:62
  92.4 4.8 %collective-permute-start.36 = (bf16[32,512]{1,0:T(8,128)(2,1)S(1)}, bf16[32,512]{1,0:T(8,128)(2,1)S(1)}, u32[]{:S(2)}, u32[]{:S(2)}) collective-permute-start(bf16[32,512]{1,0:T(8,128)(2,1)S(1)} %get-tuple-element.89), channel_id=1, source_target_pairs={{0,6},{1,7},{2,4},{3,5},{4,2},{5,3},{6,0},{7,1},{8,14},{9,15},{10,... | collective-permute-start | bytes 98312 | tf_op jit(solution)/shard_map/ppermute | solution.py:62
  (21 other events, 218.6 us)

commit v7 on v4

--- a/solution.py
+++ b/solution.py
@@ -90,11 +90,15 @@
     return jnp.dot(a, b, preferred_element_type=F32)
 
 
+def across(a, b):
+    return lax.dot_general(a, b, (((1,), (1,)), ((), ())), preferred_element_type=F32)
+
+
 def at(index, size):
     return pl.ds(pl.multiple_of(index * size, size), size)
 
 
-def call(kernel, name, ins, outs, in_specs=None, out_specs=None, scratch=(), moved=2**20, limit=20):
+def call(kernel, name, ins, outs, in_specs=None, out_specs=None, scratch=(), moved=2**20, limit=20, aliases=None):
     single = not isinstance(outs, (list, tuple))
     specs = out_specs or (VMEM if single else [VMEM] * len(outs))
     return pl.pallas_call(
@@ -104,8 +108,9 @@
         in_specs=in_specs or [VMEM] * len(ins),
         out_specs=specs,
         scratch_shapes=list(scratch),
+        input_output_aliases=aliases or {},
         cost_estimate=pl.CostEstimate(flops=0, bytes_accessed=moved, transcendentals=0),
-        compiler_params=pltpu.CompilerParams(vmem_limit_bytes=limit * 1024 * 1024),
+        compiler_params=pltpu.CompilerParams(vmem_limit_bytes=int(limit * 1024 * 1024)),
     )(*ins)
 
 
@@ -179,6 +184,29 @@
         out[place.x_before(dx)] = total.astype(BF16)
 
 
+def cache_kernel(keys_in, values_in, keys_out, values_out, keys, values, mark, in_sems, out_sems):
+    group = keys.shape[0]
+    arrays = ((keys_in, keys, keys_out), (values_in, values, values_out))
+    coming = [
+        pltpu.make_async_copy(source.at[i], here.at[i], in_sems.at[k, i])
+        for i in range(group)
+        for k, (source, here, _) in enumerate(arrays)
+    ]
+    going = [
+        pltpu.make_async_copy(here.at[i], target.at[i], out_sems.at[k, i])
+        for i in range(group)
+        for k, (_, here, target) in enumerate(arrays)
+    ]
+    for copy in coming:
+        copy.start()
+    mark[...] = jnp.zeros_like(mark)
+    for arrived, copy in zip(coming, going):
+        arrived.wait()
+        copy.start()
+    for copy in going:
+        copy.wait()
+
+
 def split_three(value):
     first = value.astype(BF16).astype(F32)
     rest = value - first
@@ -190,87 +218,97 @@
     return pltpu.roll(value, by % LANES, 1)
 
 
+def pairs_of(query):
+    side = lax.rem(lax.div(lax.broadcasted_iota(jnp.int32, query.shape, 1), HEAD), 2)
+    return jnp.concatenate(
+        [jnp.where(side == 0, query, 0.0), jnp.where(side == 1, query, 0.0)], axis=0
+    ).astype(BF16)
+
+
 def attention_kernel(place, heads, steps, *refs):
     nx, nz = place.nx, place.nz
     gathered = refs[:nz]
-    lengths, keys_in, values_in, keys_out, values_out = refs[nz : nz + 5]
-    messages = refs[nz + 5 : nz + 5 + nx]
-    qs, ks, vs, scores, part, stats, keys, values, in_sems, out_sems = refs[nz + 5 + nx :]
+    lengths, keys, values = refs[nz : nz + 3]
+    keys_out, values_out = refs[nz + 5 : nz + 7]
+    messages = refs[nz + 7 : nz + 7 + nx]
+    qs, ks, vs, scores, part, stats, k_rows, v_rows, sems = refs[nz + 7 + nx :]
     group, slots, width = keys.shape
     cols = width // place.seqs
     seq = lax.axis_index("seq")
-
-    def copies(sources, targets, sems, i):
-        return [
-            pltpu.make_async_copy(source.at[i], target.at[i], sems.at[k, i])
-            for k, (source, target) in enumerate(zip(sources, targets))
-        ]
-
-    def coming(i):
-        return copies((keys_in, values_in), (keys, values), in_sems, i)
-
-    def going(i):
-        return copies((keys, values), (keys_out, values_out), out_sems, i)
-
-    for i in range(group):
-        for copy in coming(i):
-            copy.start()
     for dz in range(nz):
         span = at(place.z_partner(dz), nx * cols)
         for k, target in enumerate((qs, ks, vs)):
             target[:, span] = side_by_side(gathered[dz], k * cols, cols)
-    window = min(32, slots)
+
+    window = k_rows.shape[1]
+
+    def place_of(i):
+        base = lengths[i] - seq * slots
+        start = jnp.clip(lax.div(jnp.maximum(base, 0), 16) * 16, 0, slots - window)
+        return base, pl.multiple_of(start, 16)
+
+    def copies(i):
+        _, start = place_of(i)
+        return [
+            pltpu.make_async_copy(
+                rows.at[i], target.at[i, pl.ds(start, window), :], sems.at[k, i]
+            )
+            for k, (rows, target) in enumerate(((k_rows, keys_out), (v_rows, values_out)))
+        ]
+
     for i in range(group):
-        base = lengths[i] - seq * slots
-        for copy in coming(i):
-            copy.wait()
+        base, start = place_of(i)
 
         @pl.when((base > -steps) & (base < slots))
         def _():
-            start = jnp.clip(lax.div(jnp.maximum(base, 0), 16) * 16, 0, slots - window)
-            here = pl.ds(pl.multiple_of(start, 16), window)
             slot = start + lax.broadcasted_iota(jnp.int32, (window, width), 0)
-            for target, fresh in ((keys, ks), (values, vs)):
-                block = target[i, here, :].astype(F32)
+            for source, fresh, rows in ((keys, ks, k_rows), (values, vs, v_rows)):
+                block = source[i, pl.ds(start, window), :].astype(F32)
                 for t in range(steps):
                     at_row = fresh[i * steps + t : i * steps + t + 1, :]
                     block = jnp.where(slot == base + t, at_row, block)
-                target[i, here, :] = block.astype(BF16)
-
-        for copy in going(i):
-            copy.start()
+                rows[i] = block.astype(BF16)
+            for copy in copies(i):
+                copy.start()
 
     pack = max(1, min(group, 256 // slots))
     rows = pack * steps
     tile = 2 * HEAD
-    side = lax.rem(lax.div(lax.broadcasted_iota(jnp.int32, (rows, width), 1), HEAD), 2)
     left = lax.broadcasted_iota(jnp.int32, (rows, tile), 1) < HEAD
-    many = heads * rows
-    row = lax.broadcasted_iota(jnp.int32, (many, pack * slots), 0)
-    column = lax.broadcasted_iota(jnp.int32, (many, pack * slots), 1)
+    many, cached = heads * rows, pack * slots
+    row = lax.broadcasted_iota(jnp.int32, (many, cached + LANES), 0)
+    column = lax.broadcasted_iota(jnp.int32, (many, cached + LANES), 1)
     owner = lax.div(lax.rem(row, rows), steps)
-    step = lax.rem(row, steps)
-    position = seq * slots + lax.rem(column, slots)
-    same = owner == lax.div(column, slots)
+    position = lax.rem(column, slots)
+    old = (column < cached) & (owner == lax.div(column, slots))
+    new = column - cached
+    later = lax.rem(new, steps)
+    fresh = (
+        (new >= 0)
+        & (new < rows)
+        & (lax.div(new, steps) == owner)
+        & (later <= lax.rem(row, steps))
+    )
     lane = lax.broadcasted_iota(jnp.int32, (rows, LANES), 1)
+    blank = jnp.zeros((LANES - rows, width), BF16)
     for g in range(group // pack):
         mine = slice(g * rows, (g + 1) * rows)
-        query = qs[mine, :]
-        pair = jnp.concatenate(
-            [jnp.where(side == 0, query, 0.0), jnp.where(side == 1, query, 0.0)], axis=0
-        ).astype(BF16)
         these = slice(g * pack, (g + 1) * pack)
-        key = keys[these].reshape(pack * slots, width)
-        value = values[these].reshape(pack * slots, width)
+        pair = pairs_of(qs[mine, :])
+        key = keys[these].reshape(cached, width)
+        value = values[these].reshape(cached, width)
+        new_key = jnp.concatenate([ks[mine, :].astype(BF16), blank], axis=0)
+        new_value = jnp.concatenate([vs[mine, :].astype(BF16), blank], axis=0)
         for j in range(heads // 2):
             span = slice(j * tile, (j + 1) * tile)
-            scores[j * 2 * rows : (j + 1) * 2 * rows, :] = lax.dot_general(
-                pair[:, span], key[:, span], (((1,), (1,)), ((), ())), preferred_element_type=F32
-            )
-        limit = step
+            these_rows = slice(j * 2 * rows, (j + 1) * 2 * rows)
+            scores[these_rows, :cached] = across(pair[:, span], key[:, span])
+            scores[these_rows, cached:] = across(pair[:, span], new_key[:, span])
+        base = jnp.zeros_like(owner)
         for k in range(pack):
-            limit = jnp.where(owner == k, step + lengths[g * pack + k], limit)
-        valid = same & (position <= limit)
+            base = jnp.where(owner == k, lengths[g * pack + k] - seq * slots, base)
+        at_new = base + later
+        valid = (old & (position < base)) | (fresh & (at_new >= 0) & (at_new < slots))
         masked = jnp.where(valid, scores[...] * HEAD ** (-0.5), -1e30)
         peak = jnp.max(masked, axis=-1, keepdims=True)
         expo = jnp.where(valid, jnp.exp(masked - peak), 0.0)
@@ -278,7 +316,9 @@
         probs = expo.astype(BF16)
         for j in range(heads // 2):
             span = slice(j * tile, (j + 1) * tile)
-            mixed = dot(probs[j * 2 * rows : (j + 1) * 2 * rows], value[:, span])
+            these_rows = slice(j * 2 * rows, (j + 1) * 2 * rows)
+            mixed = dot(probs[these_rows, :cached], value[:, span])
+            mixed = mixed + dot(probs[these_rows, cached:], new_value[:, span])
             part[mine, span] = jnp.where(left, mixed[:rows], mixed[rows:])
         line = jnp.zeros((rows, LANES), F32)
         for k, piece in enumerate(split_three(peak) + split_three(total)[:2]):
@@ -293,8 +333,12 @@
             stats[...], lax.rem(LANES - to * (heads // nx), LANES), 1
         ).astype(BF16)
     for i in range(group):
-        for copy in going(i):
-            copy.wait()
+        base, _ = place_of(i)
+
+        @pl.when((base > -steps) & (base < slots))
+        def _():
+            for copy in copies(i):
+                copy.wait()
 
 
 def expand(factor, count):
@@ -491,6 +535,7 @@
         [shape((rows, width))] + [shape(w.shape) for w in own],
         in_specs=[VMEM] * 2 + [HBM] * 3,
         scratch=[pltpu.VMEM((rows, width), F32), pltpu.SemaphoreType.DMA((3,))],
+        limit=52.75,
     )
     parts = call(
         bind(qkv_kernel, place),
@@ -502,38 +547,52 @@
     *parts, tied_up, tied_down = lax.optimization_barrier((*parts, w_up, w_down))
     w_up_sibling = place.move(tied_up, dc=1)
     w_down_sibling = place.move(tied_down, dc=1)
+    parts, tied_keys, tied_values = lax.optimization_barrier((parts, cache_keys, cache_values))
+    new_keys, new_values, keys, values, mark = call(
+        cache_kernel,
+        "caches",
+        [tied_keys, tied_values],
+        [shape(cache_keys.shape)] * 4 + [shape((8, LANES), F32)],
+        in_specs=[HBM, HBM],
+        out_specs=[HBM, HBM, VMEM, VMEM, VMEM],
+        scratch=[pltpu.SemaphoreType.DMA((2, group)), pltpu.SemaphoreType.DMA((2, group))],
+        moved=16 * 1024 * 1024,
+        limit=46,
+    )
     qkv = call(
-        bind(add_columns_kernel, place), "add_qkv", spread(parts), shape((nx, rows, 3 * cols))
-    )
-
-    qkv, w_up_sibling, w_down_sibling = lax.optimization_barrier(
-        (qkv, w_up_sibling, w_down_sibling)
-    )
-    qkv, tied_w_out = lax.optimization_barrier((qkv, w_out))
-    blocks = [place.transpose(tied_w_out, k) for k in range(nx)]
+        bind(add_columns_kernel, place),
+        "add_qkv",
+        [*spread(parts), mark],
+        shape((nx, rows, 3 * cols)),
+    )
+    qkv, w_up_sibling, w_down_sibling, tied = lax.optimization_barrier(
+        (qkv, w_up_sibling, w_down_sibling, w_out)
+    )
+    pieces = place.gather_z(qkv)
+    blocks = [place.transpose(tied, k) for k in range(nx)]
     pack = max(1, min(group, 256 // slots))
+    window = min(32, slots)
     new_keys, new_values, *messages = call(
         bind(attention_kernel, place, heads, steps),
         "attention",
-        [*place.gather_z(qkv), lengths, cache_keys, cache_values],
-        [shape(cache_keys.shape), shape(cache_values.shape)] + [shape((rows, share + LANES))] * nx,
-        in_specs=[VMEM] * place.nz + [SMEM, HBM, HBM],
+        [*pieces, lengths, keys, values, new_keys, new_values],
+        [shape(cache_keys.shape)] * 2 + [shape((rows, share + LANES))] * nx,
+        in_specs=[VMEM] * place.nz + [SMEM, VMEM, VMEM, HBM, HBM],
         out_specs=[HBM, HBM] + [VMEM] * nx,
         scratch=[
             pltpu.VMEM((rows, width), F32),
             pltpu.VMEM((rows, width), F32),
             pltpu.VMEM((rows, width), F32),
-            pltpu.VMEM((heads * pack * steps, pack * slots), F32),
+            pltpu.VMEM((heads * pack * steps, pack * slots + LANES), F32),
             pltpu.VMEM((rows, width), F32),
             pltpu.VMEM((rows, LANES), F32),
-            pltpu.VMEM(cache_keys.shape, BF16),
-            pltpu.VMEM(cache_keys.shape, BF16),
-            pltpu.SemaphoreType.DMA((2, group)),
+            pltpu.VMEM((group, window, width), BF16),
+            pltpu.VMEM((group, window, width), BF16),
             pltpu.SemaphoreType.DMA((2, group)),
         ],
-        limit=52,
-    )
-    *messages, blocks = lax.optimization_barrier((*messages, blocks))
+        aliases={place.nz + 3: 0, place.nz + 4: 1},
+    )
+    messages, blocks = lax.optimization_barrier((messages, blocks))
     w_outs = []
     for block in blocks:
         w_outs += [block, place.move(block, dc=1)]
@@ -542,9 +601,8 @@
         bind(merge_x_kernel, place, heads), "merge_x", messages, shape((rows, share + LANES))
     )
     merged, *w_outs = lax.optimization_barrier((merged, *w_outs))
-    attn = call(
-        bind(merge_z_kernel, place, heads), "merge_z", place.gather_z(merged), shape((rows, share))
-    )
+    pieces = place.gather_z(merged)
+    attn = call(bind(merge_z_kernel, place, heads), "merge_z", pieces, shape((rows, share)))
     out_part = call(
         bind(out_kernel, place),
         "out",

time: 92.6 us -> 89.9 us (0.971)
  local copies, waits for them, and re-layouts: 3.81 us -> 0.97 us
  Pallas kernels: 9.05 us -> 10.7 us
  waiting for transfers between devices: 36.7 us -> 35.6 us
    unnamed x28 -> x24, local copies, waits for them, and re-layouts: 3.81 us -> 0.97 us
    pallas_call x13 -> x14, Pallas kernels: 9.05 us -> 10.7 us  [call(): pl.pallas_call(kernel, name=name, out_shape=outs, in_specs=in_specs or [V...]
    ppermute x32, waiting for transfers between devices: 36.7 us -> 35.6 us  [move(): return lax.ppermute(value, ('seq', 'req'), pairs)]
  transfers between devices with their start and end apart: 34 -> 34, of which waited for: 18 -> 20; matrix products, arithmetic and copies ran while one was open for 2% -> 2% of each run, Pallas kernels for 6% -> 8%
where the time goes in v7:
time: 89.9 us; the launch traced here: 89.6 us
  starting transfers between devices  39.8 us (44%)
  waiting for transfers between devices  35.6 us (40%)
  Pallas kernels  10.7 us (12%)
  other arithmetic  1.44 us (2%)
  local copies, waits for them, and re-layouts  0.97 us (1%)
  between operations  0.95 us (1%)
    ppermute x32, starting transfers between devices, move(): return lax.ppermute(value, ('seq', 'req'), pairs)  38 us
    ppermute x32, waiting for transfers between devices, move(): return lax.ppermute(value, ('seq', 'req'), pairs)  35.6 us
    pallas_call x14, Pallas kernels, call(): pl.pallas_call(kernel, name=name, out_shape=outs, in_specs=in_specs or [V...  10.7 us
    ppermute x2, starting transfers between devices, transpose(): return lax.ppermute(value, ('seq', 'req'), pairs)  1.85 us
  transfers between devices with their start and end apart: 34, of which 20 were waited for; matrix products, arithmetic and copies ran while one was open for 2% of the time, Pallas kernels for 8%

profile of v7, /device:TPU:0, one launch (start us, length us, event | category | flops | bytes accessed | tf_op | source)
XLA Modules:
  0.0 89.6 jit_solution(14228512207949075297)
XLA Ops:
  1.7 2.6 %collective-permute-start = (bf16[8,4,2048]{2,1,0:T(4,128)(2,1)}, bf16[8,4,2048]{2,1,0:T(4,128)(2,1)S(1)}, u32[]{:S(2)}, u32[]{:S(2)}) collective-permute-start(bf16[8,4,2048]{2,1,0:T(4,128)(2,1)} %refs_0_.3), channel_id=1, source_target_pairs={{0,2},{1,3},{2,0},{3,1},{4,6},{5,7},{6,4},{7,5},{8,10},{9,11},{10,... | collective-permute-start | bytes 393224 | tf_op jit(solution)/shard_map/ppermute | solution.py:62
  6.6 1.1 %norm.1 = (bf16[32,2048]{1,0:T(8,128)(2,1)S(1)}, bf16[512,256]{1,0:T(8,128)(2,1)S(1)}, bf16[512,256]{1,0:T(8,128)(2,1)S(1)}, bf16[512,256]{1,0:T(8,128)(2,1)S(1)}) custom-call(bf16[8,4,2048]{2,1,0:T(4,128)(2,1)S(1)} %copy-done.3, f32[1,4096]{1,0:T(1,128)S(1)} %bitcast.6, bf16[512,256]{1,0:T(8,128)(2,1)} %refs_0_.2, bf16[512,256]{1,0:T(8,128)(2,1)} %refs_1_.1, ...), custom_call_target="tpu_custom_call" | custom-call | bytes 1048576 | tf_op jit(solution)/shard_map/norm/pallas_call | solution.py:104
  9.8 1.7 %collective-permute-start.5 = (bf16[32,768]{1,0:T(8,128)(2,1)S(1)}, bf16[32,768]{1,0:T(8,128)(2,1)S(1)}, u32[]{:S(2)}, u32[]{:S(2)}) collective-permute-start(bf16[32,768]{1,0:T(8,128)(2,1)S(1)} %get-tuple-element.53.refs_0_), channel_id=1, source_target_pairs={{0,4},{1,5},{2,6},{3,7},{4,0},{5,1},{6,2},{7,3},{8,12},{9,13},{10,... | collective-permute-start | bytes 147464 | tf_op jit(solution)/shard_map/ppermute | solution.py:62
  11.5 1.5 %collective-permute-start.6 = (bf16[32,768]{1,0:T(8,128)(2,1)S(1)}, bf16[32,768]{1,0:T(8,128)(2,1)S(1)}, u32[]{:S(2)}, u32[]{:S(2)}) collective-permute-start(bf16[32,768]{1,0:T(8,128)(2,1)S(1)} %get-tuple-element.54), channel_id=1, source_target_pairs={{0,6},{1,7},{2,4},{3,5},{4,2},{5,3},{6,0},{7,1},{8,14},{9,15},{10,... | collective-permute-start | bytes 147464 | tf_op jit(solution)/shard_map/ppermute | solution.py:62
  13.3 3.2 %caches.1 = (bf16[8,64,2048]{2,1,0:T(8,128)(2,1)}, bf16[8,64,2048]{2,1,0:T(8,128)(2,1)}, bf16[8,64,2048]{2,1,0:T(8,128)(2,1)S(1)}, bf16[8,64,2048]{2,1,0:T(8,128)(2,1)S(1)}, f32[8,128]{1,0:T(8,128)S(1)}) custom-call(bf16[8,64,2048]{2,1,0:T(8,128)(2,1)S(1)} %copy-done, bf16[8,64,2048]{2,1,0:T(8,128)(2,1)} %values_in), custom_call_target="tpu_custom_call" | custom-call | bytes 16777216 | tf_op jit(solution)/shard_map/caches/pallas_call | solution.py:104
  17.2 1.2 %collective-permute-start.13 = (bf16[512,256]{1,0:T(8,128)(2,1)S(1)}, bf16[512,256]{1,0:T(8,128)(2,1)S(1)}, u32[]{:S(2)}, u32[]{:S(2)}) collective-permute-start(bf16[512,256]{1,0:T(8,128)(2,1)S(1)} %copy-done.11), channel_id=1, source_target_pairs={{0,2},{1,3},{2,6},{3,7},{4,0},{5,1},{6,4},{7,5},{8,10},{9,11},{10,... | collective-permute-start | bytes 786440 | tf_op jit(solution)/shard_map/ppermute | solution.py:77
  19.0 3.7 %collective-permute-start.11 = (bf16[2,32,768]{2,1,0:T(8,128)(2,1)S(1)}, bf16[2,32,768]{2,1,0:T(8,128)(2,1)S(1)}, u32[]{:S(2)}, u32[]{:S(2)}) collective-permute-start(bf16[2,32,768]{2,1,0:T(8,128)(2,1)S(1)} %add_qkv.1.refs_0_), channel_id=1, source_target_pairs={{0,24},{1,25},{2,26},{3,27},{4,28},{5,29},{6,30},{7,31},{8,16},{9,... | collective-permute-start | bytes 294920 | tf_op jit(solution)/shard_map/ppermute | solution.py:62
  23.5 2.6 %collective-permute-done.11.refs_3_ = bf16[2,32,768]{2,1,0:T(8,128)(2,1)S(1)} collective-permute-done((bf16[2,32,768]{2,1,0:T(8,128)(2,1)S(1)}, bf16[2,32,768]{2,1,0:T(8,128)(2,1)S(1)}, u32[]{:S(2)}, u32[]{:S(2)}) %collective-permute-start.11) | collective-permute-done | bytes 98336 | tf_op jit(solution)/shard_map/ppermute | solution.py:62
  26.1 4.0 %collective-permute-done.10.refs_2_ = bf16[2,32,768]{2,1,0:T(8,128)(2,1)S(1)} collective-permute-done((bf16[2,32,768]{2,1,0:T(8,128)(2,1)S(1)}, bf16[2,32,768]{2,1,0:T(8,128)(2,1)S(1)}, u32[]{:S(2)}, u32[]{:S(2)}) %collective-permute-start.10) | collective-permute-done | bytes 98336 | tf_op jit(solution)/shard_map/ppermute | solution.py:62
  30.2 2.7 %attention.1 = (bf16[8,64,2048]{2,1,0:T(8,128)(2,1)}, bf16[8,64,2048]{2,1,0:T(8,128)(2,1)}, bf16[32,1152]{1,0:T(8,128)(2,1)S(1)}, bf16[32,1152]{1,0:T(8,128)(2,1)S(1)}) custom-call(bf16[2,32,768]{2,1,0:T(8,128)(2,1)S(1)} %add_qkv.1.refs_0_, bf16[2,32,768]{2,1,0:T(8,128)(2,1)S(1)} %collective-permute-done.9.refs_1_, ...), custom_call_target="tpu_custom_call", output_to_operand_aliasing={{0}: (7, {}), {1}: (8, {})} | custom-call | bytes 1048576 | tf_op jit(solution)/shard_map/attention/pallas_call | solution.py:104
  33.5 3.6 %collective-permute-start.14 = (bf16[32,1152]{1,0:T(8,128)(2,1)S(1)}, bf16[32,1152]{1,0:T(8,128)(2,1)S(1)}, u32[]{:S(2)}, u32[]{:S(2)}) collective-permute-start(bf16[32,1152]{1,0:T(8,128)(2,1)S(1)} %get-tuple-element.69), channel_id=1, source_target_pairs={{0,4},{1,5},{2,6},{3,7},{4,0},{5,1},{6,2},{7,3},{8,12},{9,13},{10,... | collective-permute-start | bytes 221192 | tf_op jit(solution)/shard_map/ppermute | solution.py:62
  37.1 2.5 %collective-permute-done.14.refs_1_ = bf16[32,1152]{1,0:T(8,128)(2,1)S(1)} collective-permute-done((bf16[32,1152]{1,0:T(8,128)(2,1)S(1)}, bf16[32,1152]{1,0:T(8,128)(2,1)S(1)}, u32[]{:S(2)}, u32[]{:S(2)}) %collective-permute-start.14) | collective-permute-done | bytes 73760 | tf_op jit(solution)/shard_map/ppermute | solution.py:62
  39.9 2.5 %collective-permute-start.19 = (bf16[32,1152]{1,0:T(8,128)(2,1)S(1)}, bf16[32,1152]{1,0:T(8,128)(2,1)S(1)}, u32[]{:S(2)}, u32[]{:S(2)}) collective-permute-start(bf16[32,1152]{1,0:T(8,128)(2,1)S(1)} %merge_x.1.refs_0_), channel_id=1, source_target_pairs={{0,24},{1,25},{2,26},{3,27},{4,28},{5,29},{6,30},{7,31},{8,16},{9,... | collective-permute-start | bytes 221192 | tf_op jit(solution)/shard_map/ppermute | solution.py:62
  42.4 2.0 %collective-permute-start.17 = (bf16[32,1152]{1,0:T(8,128)(2,1)S(1)}, bf16[32,1152]{1,0:T(8,128)(2,1)S(1)}, u32[]{:S(2)}, u32[]{:S(2)}) collective-permute-start(bf16[32,1152]{1,0:T(8,128)(2,1)S(1)} %merge_x.1.refs_0_), channel_id=1, source_target_pairs={{0,8},{1,9},{2,10},{3,11},{4,12},{5,13},{6,14},{7,15},{8,0},{9,1},... | collective-permute-start | bytes 221192 | tf_op jit(solution)/shard_map/ppermute | solution.py:62
  44.3 2.1 %collective-permute-done.19.refs_3_ = bf16[32,1152]{1,0:T(8,128)(2,1)S(1)} collective-permute-done((bf16[32,1152]{1,0:T(8,128)(2,1)S(1)}, bf16[32,1152]{1,0:T(8,128)(2,1)S(1)}, u32[]{:S(2)}, u32[]{:S(2)}) %collective-permute-start.19) | collective-permute-done | bytes 73760 | tf_op jit(solution)/shard_map/ppermute | solution.py:62
  46.4 2.4 %collective-permute-done.18.refs_2_ = bf16[32,1152]{1,0:T(8,128)(2,1)S(1)} collective-permute-done((bf16[32,1152]{1,0:T(8,128)(2,1)S(1)}, bf16[32,1152]{1,0:T(8,128)(2,1)S(1)}, u32[]{:S(2)}, u32[]{:S(2)}) %collective-permute-start.18) | collective-permute-done | bytes 73760 | tf_op jit(solution)/shard_map/ppermute | solution.py:62
  49.5 1.4 %collective-permute-start.22 = (bf16[2,32,256]{2,1,0:T(8,128)(2,1)S(1)}, bf16[2,32,256]{2,1,0:T(8,128)(2,1)S(1)}, u32[]{:S(2)}, u32[]{:S(2)}) collective-permute-start(bf16[2,32,256]{2,1,0:T(8,128)(2,1)S(1)} %out.1.refs_0_), channel_id=1, source_target_pairs={{0,6},{1,7},{2,4},{3,5},{4,2},{5,3},{6,0},{7,1},{8,14},{9,15},{10,... | collective-permute-start | bytes 98312 | tf_op jit(solution)/shard_map/ppermute | solution.py:62
  50.9 1.8 %collective-permute-start.21 = (bf16[2,32,256]{2,1,0:T(8,128)(2,1)S(1)}, bf16[2,32,256]{2,1,0:T(8,128)(2,1)S(1)}, u32[]{:S(2)}, u32[]{:S(2)}) collective-permute-start(bf16[2,32,256]{2,1,0:T(8,128)(2,1)S(1)} %out.1.refs_0_), channel_id=1, source_target_pairs={{0,4},{1,5},{2,6},{3,7},{4,0},{5,1},{6,2},{7,3},{8,12},{9,13},{10,... | collective-permute-start | bytes 98312 | tf_op jit(solution)/shard_map/ppermute | solution.py:62
  53.1 1.6 %collective-permute-done.22.refs_3_ = bf16[2,32,256]{2,1,0:T(8,128)(2,1)S(1)} collective-permute-done((bf16[2,32,256]{2,1,0:T(8,128)(2,1)S(1)}, bf16[2,32,256]{2,1,0:T(8,128)(2,1)S(1)}, u32[]{:S(2)}, u32[]{:S(2)}) %collective-permute-start.22) | collective-permute-done | bytes 32800 | tf_op jit(solution)/shard_map/ppermute | solution.py:62
  55.0 1.7 %collective-permute-done.20.refs_1_ = bf16[2,32,256]{2,1,0:T(8,128)(2,1)S(1)} collective-permute-done((bf16[2,32,256]{2,1,0:T(8,128)(2,1)S(1)}, bf16[2,32,256]{2,1,0:T(8,128)(2,1)S(1)}, u32[]{:S(2)}, u32[]{:S(2)}) %collective-permute-start.20) | collective-permute-done | bytes 32800 | tf_op jit(solution)/shard_map/ppermute | solution.py:62
  56.7 1.5 %collective-permute-start.25 = (bf16[2,2,32,256]{3,2,1,0:T(8,128)(2,1)S(1)}, bf16[2,2,32,256]{3,2,1,0:T(8,128)(2,1)S(1)}, u32[]{:S(2)}, u32[]{:S(2)}) collective-permute-start(bf16[2,2,32,256]{3,2,1,0:T(8,128)(2,1)S(1)} %add_out.1.refs_2_), channel_id=1, source_target_pairs={{0,24},{1,25},{2,26},{3,27},{4,28},{5,29},{6,30},{7,31},{8,16},{9,... | collective-permute-start | bytes 196616 | tf_op jit(solution)/shard_map/ppermute | solution.py:62
  58.2 3.0 %collective-permute-start.23 = (bf16[2,2,32,256]{3,2,1,0:T(8,128)(2,1)S(1)}, bf16[2,2,32,256]{3,2,1,0:T(8,128)(2,1)S(1)}, u32[]{:S(2)}, u32[]{:S(2)}) collective-permute-start(bf16[2,2,32,256]{3,2,1,0:T(8,128)(2,1)S(1)} %add_out.1.refs_2_), channel_id=1, source_target_pairs={{0,8},{1,9},{2,10},{3,11},{4,12},{5,13},{6,14},{7,15},{8,0},{9,1},... | collective-permute-start | bytes 196616 | tf_op jit(solution)/shard_map/ppermute | solution.py:62
  61.1 1.7 %collective-permute-done.25.refs_5_ = bf16[2,2,32,256]{3,2,1,0:T(8,128)(2,1)S(1)} collective-permute-done((bf16[2,2,32,256]{3,2,1,0:T(8,128)(2,1)S(1)}, bf16[2,2,32,256]{3,2,1,0:T(8,128)(2,1)S(1)}, u32[]{:S(2)}, u32[]{:S(2)}) %collective-permute-start.25) | collective-permute-done | bytes 65568 | tf_op jit(solution)/shard_map/ppermute | solution.py:62
  62.8 1.4 %collective-permute-done.24.refs_4_ = bf16[2,2,32,256]{3,2,1,0:T(8,128)(2,1)S(1)} collective-permute-done((bf16[2,2,32,256]{3,2,1,0:T(8,128)(2,1)S(1)}, bf16[2,2,32,256]{3,2,1,0:T(8,128)(2,1)S(1)}, u32[]{:S(2)}, u32[]{:S(2)}) %collective-permute-start.24) | collective-permute-done | bytes 65568 | tf_op jit(solution)/shard_map/ppermute | solution.py:62
  66.0 4.2 %collective-permute-done.26.refs_1_ = bf16[64,1024]{1,0:T(8,128)(2,1)S(1)} collective-permute-done((bf16[64,1024]{1,0:T(8,128)(2,1)S(1)}, bf16[64,1024]{1,0:T(8,128)(2,1)S(1)}, u32[]{:S(2)}, u32[]{:S(2)}) %collective-permute-start.26) | collective-permute-done | bytes 131104 | tf_op jit(solution)/shard_map/ppermute | solution.py:62
  71.0 4.0 %collective-permute-done.27.refs_1_ = bf16[64,512]{1,0:T(8,128)(2,1)S(1)} collective-permute-done((bf16[64,512]{1,0:T(8,128)(2,1)S(1)}, bf16[64,512]{1,0:T(8,128)(2,1)S(1)}, u32[]{:S(2)}, u32[]{:S(2)}) %collective-permute-start.27) | collective-permute-done | bytes 65568 | tf_op jit(solution)/shard_map/ppermute | solution.py:62
  75.0 1.9 %collective-permute-start.30 = (bf16[64,512]{1,0:T(8,128)(2,1)S(1)}, bf16[64,512]{1,0:T(8,128)(2,1)S(1)}, u32[]{:S(2)}, u32[]{:S(2)}) collective-permute-start(bf16[64,512]{1,0:T(8,128)(2,1)S(1)} %add_x.1.refs_0_), channel_id=1, source_target_pairs={{0,24},{1,25},{2,26},{3,27},{4,28},{5,29},{6,30},{7,31},{8,16},{9,... | collective-permute-start | bytes 196616 | tf_op jit(solution)/shard_map/ppermute | solution.py:62
  77.7 1.8 %collective-permute-start.28 = (bf16[64,512]{1,0:T(8,128)(2,1)S(1)}, bf16[64,512]{1,0:T(8,128)(2,1)S(1)}, u32[]{:S(2)}, u32[]{:S(2)}) collective-permute-start(bf16[64,512]{1,0:T(8,128)(2,1)S(1)} %add_x.1.refs_0_), channel_id=1, source_target_pairs={{0,8},{1,9},{2,10},{3,11},{4,12},{5,13},{6,14},{7,15},{8,0},{9,1},... | collective-permute-start | bytes 196616 | tf_op jit(solution)/shard_map/ppermute | solution.py:62
  79.5 1.7 %collective-permute-done.30.refs_3_ = bf16[64,512]{1,0:T(8,128)(2,1)S(1)} collective-permute-done((bf16[64,512]{1,0:T(8,128)(2,1)S(1)}, bf16[64,512]{1,0:T(8,128)(2,1)S(1)}, u32[]{:S(2)}, u32[]{:S(2)}) %collective-permute-start.30) | collective-permute-done | bytes 65568 | tf_op jit(solution)/shard_map/ppermute | solution.py:62
  81.2 1.5 %collective-permute-done.29.refs_2_ = bf16[64,512]{1,0:T(8,128)(2,1)S(1)} collective-permute-done((bf16[64,512]{1,0:T(8,128)(2,1)S(1)}, bf16[64,512]{1,0:T(8,128)(2,1)S(1)}, u32[]{:S(2)}, u32[]{:S(2)}) %collective-permute-start.29) | collective-permute-done | bytes 65568 | tf_op jit(solution)/shard_map/ppermute | solution.py:62
  83.0 1.9 %collective-permute-start.33 = (bf16[32,512]{1,0:T(8,128)(2,1)S(1)}, bf16[32,512]{1,0:T(8,128)(2,1)S(1)}, u32[]{:S(2)}, u32[]{:S(2)}) collective-permute-start(bf16[32,512]{1,0:T(8,128)(2,1)S(1)} %get-tuple-element.83), channel_id=1, source_target_pairs={{0,6},{1,7},{2,4},{3,5},{4,2},{5,3},{6,0},{7,1},{8,14},{9,15},{10,... | collective-permute-start | bytes 98312 | tf_op jit(solution)/shard_map/ppermute | solution.py:62
  84.9 1.4 %collective-permute-start.31 = (bf16[32,512]{1,0:T(8,128)(2,1)S(1)}, bf16[32,512]{1,0:T(8,128)(2,1)S(1)}, u32[]{:S(2)}, u32[]{:S(2)}) collective-permute-start(bf16[32,512]{1,0:T(8,128)(2,1)S(1)} %get-tuple-element.83), channel_id=1, source_target_pairs={{0,2},{1,3},{2,0},{3,1},{4,6},{5,7},{6,4},{7,5},{8,10},{9,11},{10,... | collective-permute-start | bytes 98312 | tf_op jit(solution)/shard_map/ppermute | solution.py:62
  (77 shorter events, 17.0 us)
Async XLA Ops:
  0.6 7.9 %collective-permute-start.1 = (bf16[512,256]{1,0:T(8,128)(2,1)}, bf16[512,256]{1,0:T(8,128)(2,1)S(1)}, u32[]{:S(2)}, u32[]{:S(2)}) collective-permute-start(bf16[512,256]{1,0:T(8,128)(2,1)} %refs_0_.2), channel_id=1, source_target_pairs={{0,1},{1,0},{2,3},{3,2},{4,5},{5,4},{6,7},{7,6},{8,9},{9,8},{10,11... | collective-permute-start | bytes 786440 | tf_op jit(solution)/shard_map/ppermute | solution.py:62
  1.2 7.4 %collective-permute-start.2 = (bf16[512,256]{1,0:T(8,128)(2,1)}, bf16[512,256]{1,0:T(8,128)(2,1)S(1)}, u32[]{:S(2)}, u32[]{:S(2)}) collective-permute-start(bf16[512,256]{1,0:T(8,128)(2,1)} %refs_1_.1), channel_id=1, source_target_pairs={{0,1},{1,0},{2,3},{3,2},{4,5},{5,4},{6,7},{7,6},{8,9},{9,8},{10,11... | collective-permute-start | bytes 786440 | tf_op jit(solution)/shard_map/ppermute | solution.py:62
  1.2 7.3 %collective-permute-start.3 = (bf16[512,256]{1,0:T(8,128)(2,1)}, bf16[512,256]{1,0:T(8,128)(2,1)S(1)}, u32[]{:S(2)}, u32[]{:S(2)}) collective-permute-start(bf16[512,256]{1,0:T(8,128)(2,1)} %refs_2_.2), channel_id=1, source_target_pairs={{0,1},{1,0},{2,3},{3,2},{4,5},{5,4},{6,7},{7,6},{8,9},{9,8},{10,11... | collective-permute-start | bytes 786440 | tf_op jit(solution)/shard_map/ppermute | solution.py:62
  1.7 6.9 %collective-permute-start = (bf16[8,4,2048]{2,1,0:T(4,128)(2,1)}, bf16[8,4,2048]{2,1,0:T(4,128)(2,1)S(1)}, u32[]{:S(2)}, u32[]{:S(2)}) collective-permute-start(bf16[8,4,2048]{2,1,0:T(4,128)(2,1)} %refs_0_.3), channel_id=1, source_target_pairs={{0,2},{1,3},{2,0},{3,1},{4,6},{5,7},{6,4},{7,5},{8,10},{9,11},{10,... | collective-permute-start | bytes 393224 | tf_op jit(solution)/shard_map/ppermute | solution.py:62
  9.2 7.9 %collective-permute-start.7 = (bf16[512,1024]{1,0:T(8,128)(2,1)}, bf16[512,1024]{1,0:T(8,128)(2,1)S(1)}, u32[]{:S(2)}, u32[]{:S(2)}) collective-permute-start(bf16[512,1024]{1,0:T(8,128)(2,1)} %refs_8_.1), channel_id=1, source_target_pairs={{0,1},{1,0},{2,3},{3,2},{4,5},{5,4},{6,7},{7,6},{8,9},{9,8},{10,11... | collective-permute-start | bytes 3145736 | tf_op jit(solution)/shard_map/ppermute | solution.py:62
  9.3 7.9 %collective-permute-start.8 = (bf16[1024,512]{1,0:T(8,128)(2,1)}, bf16[1024,512]{1,0:T(8,128)(2,1)S(1)}, u32[]{:S(2)}, u32[]{:S(2)}) collective-permute-start(bf16[1024,512]{1,0:T(8,128)(2,1)} %refs_2_.3), channel_id=1, source_target_pairs={{0,1},{1,0},{2,3},{3,2},{4,5},{5,4},{6,7},{7,6},{8,9},{9,8},{10,11... | collective-permute-start | bytes 3145736 | tf_op jit(solution)/shard_map/ppermute | solution.py:62
  9.8 6.7 %collective-permute-start.5 = (bf16[32,768]{1,0:T(8,128)(2,1)S(1)}, bf16[32,768]{1,0:T(8,128)(2,1)S(1)}, u32[]{:S(2)}, u32[]{:S(2)}) collective-permute-start(bf16[32,768]{1,0:T(8,128)(2,1)S(1)} %get-tuple-element.53.refs_0_), channel_id=1, source_target_pairs={{0,4},{1,5},{2,6},{3,7},{4,0},{5,1},{6,2},{7,3},{8,12},{9,13},{10,... | collective-permute-start | bytes 147464 | tf_op jit(solution)/shard_map/ppermute | solution.py:62
  11.5 5.0 %collective-permute-start.6 = (bf16[32,768]{1,0:T(8,128)(2,1)S(1)}, bf16[32,768]{1,0:T(8,128)(2,1)S(1)}, u32[]{:S(2)}, u32[]{:S(2)}) collective-permute-start(bf16[32,768]{1,0:T(8,128)(2,1)S(1)} %get-tuple-element.54), channel_id=1, source_target_pairs={{0,6},{1,7},{2,4},{3,5},{4,2},{5,3},{6,0},{7,1},{8,14},{9,15},{10,... | collective-permute-start | bytes 147464 | tf_op jit(solution)/shard_map/ppermute | solution.py:62
  13.0 4.1 %collective-permute-start.4 = (bf16[32,768]{1,0:T(8,128)(2,1)S(1)}, bf16[32,768]{1,0:T(8,128)(2,1)S(1)}, u32[]{:S(2)}, u32[]{:S(2)}) collective-permute-start(bf16[32,768]{1,0:T(8,128)(2,1)S(1)} %get-tuple-element.54), channel_id=1, source_target_pairs={{0,2},{1,3},{2,0},{3,1},{4,6},{5,7},{6,4},{7,5},{8,10},{9,11},{10,... | collective-permute-start | bytes 147464 | tf_op jit(solution)/shard_map/ppermute | solution.py:62
  17.2 15.7 %collective-permute-start.13 = (bf16[512,256]{1,0:T(8,128)(2,1)S(1)}, bf16[512,256]{1,0:T(8,128)(2,1)S(1)}, u32[]{:S(2)}, u32[]{:S(2)}) collective-permute-start(bf16[512,256]{1,0:T(8,128)(2,1)S(1)} %copy-done.11), channel_id=1, source_target_pairs={{0,2},{1,3},{2,6},{3,7},{4,0},{5,1},{6,4},{7,5},{8,10},{9,11},{10,... | collective-permute-start | bytes 786440 | tf_op jit(solution)/shard_map/ppermute | solution.py:77
  18.4 14.5 %collective-permute-start.12 = (bf16[512,256]{1,0:T(8,128)(2,1)S(1)}, bf16[512,256]{1,0:T(8,128)(2,1)S(1)}, u32[]{:S(2)}, u32[]{:S(2)}) collective-permute-start(bf16[512,256]{1,0:T(8,128)(2,1)S(1)} %copy-done.11), channel_id=1, source_target_pairs={{0,0},{1,1},{2,4},{3,5},{4,2},{5,3},{6,6},{7,7},{8,8},{9,9},{10,12... | collective-permute-start | bytes 786440 | tf_op jit(solution)/shard_map/ppermute | solution.py:77
  19.0 7.0 %collective-permute-start.11 = (bf16[2,32,768]{2,1,0:T(8,128)(2,1)S(1)}, bf16[2,32,768]{2,1,0:T(8,128)(2,1)S(1)}, u32[]{:S(2)}, u32[]{:S(2)}) collective-permute-start(bf16[2,32,768]{2,1,0:T(8,128)(2,1)S(1)} %add_qkv.1.refs_0_), channel_id=1, source_target_pairs={{0,24},{1,25},{2,26},{3,27},{4,28},{5,29},{6,30},{7,31},{8,16},{9,... | collective-permute-start | bytes 294920 | tf_op jit(solution)/shard_map/ppermute | solution.py:62
  22.7 7.4 %collective-permute-start.10 = (bf16[2,32,768]{2,1,0:T(8,128)(2,1)S(1)}, bf16[2,32,768]{2,1,0:T(8,128)(2,1)S(1)}, u32[]{:S(2)}, u32[]{:S(2)}) collective-permute-start(bf16[2,32,768]{2,1,0:T(8,128)(2,1)S(1)} %add_qkv.1.refs_0_), channel_id=1, source_target_pairs={{0,16},{1,17},{2,18},{3,19},{4,20},{5,21},{6,22},{7,23},{8,24},{9,... | collective-permute-start | bytes 294920 | tf_op jit(solution)/shard_map/ppermute | solution.py:62
  22.7 7.4 %collective-permute-start.9 = (bf16[2,32,768]{2,1,0:T(8,128)(2,1)S(1)}, bf16[2,32,768]{2,1,0:T(8,128)(2,1)S(1)}, u32[]{:S(2)}, u32[]{:S(2)}) collective-permute-start(bf16[2,32,768]{2,1,0:T(8,128)(2,1)S(1)} %add_qkv.1.refs_0_), channel_id=1, source_target_pairs={{0,8},{1,9},{2,10},{3,11},{4,12},{5,13},{6,14},{7,15},{8,0},{9,1},... | collective-permute-start | bytes 294920 | tf_op jit(solution)/shard_map/ppermute | solution.py:62
  32.9 7.0 %collective-permute-start.15 = (bf16[512,256]{1,0:T(8,128)(2,1)S(1)}, bf16[512,256]{1,0:T(8,128)(2,1)S(1)}, u32[]{:S(2)}, u32[]{:S(2)}) collective-permute-start(bf16[512,256]{1,0:T(8,128)(2,1)S(1)} %collective-permute-done.12.refs_0_), channel_id=1, source_target_pairs={{0,1},{1,0},{2,3},{3,2},{4,5},{5,4},{6,7},{7,6},{8,9},{9,8},{10,11... | collective-permute-start | bytes 786440 | tf_op jit(solution)/shard_map/ppermute | solution.py:62
  33.0 6.9 %collective-permute-start.16 = (bf16[512,256]{1,0:T(8,128)(2,1)S(1)}, bf16[512,256]{1,0:T(8,128)(2,1)S(1)}, u32[]{:S(2)}, u32[]{:S(2)}) collective-permute-start(bf16[512,256]{1,0:T(8,128)(2,1)S(1)} %collective-permute-done.13.refs_2_), channel_id=1, source_target_pairs={{0,1},{1,0},{2,3},{3,2},{4,5},{5,4},{6,7},{7,6},{8,9},{9,8},{10,11... | collective-permute-start | bytes 786440 | tf_op jit(solution)/shard_map/ppermute | solution.py:62
  33.5 6.1 %collective-permute-start.14 = (bf16[32,1152]{1,0:T(8,128)(2,1)S(1)}, bf16[32,1152]{1,0:T(8,128)(2,1)S(1)}, u32[]{:S(2)}, u32[]{:S(2)}) collective-permute-start(bf16[32,1152]{1,0:T(8,128)(2,1)S(1)} %get-tuple-element.69), channel_id=1, source_target_pairs={{0,4},{1,5},{2,6},{3,7},{4,0},{5,1},{6,2},{7,3},{8,12},{9,13},{10,... | collective-permute-start | bytes 221192 | tf_op jit(solution)/shard_map/ppermute | solution.py:62
  39.9 6.5 %collective-permute-start.19 = (bf16[32,1152]{1,0:T(8,128)(2,1)S(1)}, bf16[32,1152]{1,0:T(8,128)(2,1)S(1)}, u32[]{:S(2)}, u32[]{:S(2)}) collective-permute-start(bf16[32,1152]{1,0:T(8,128)(2,1)S(1)} %merge_x.1.refs_0_), channel_id=1, source_target_pairs={{0,24},{1,25},{2,26},{3,27},{4,28},{5,29},{6,30},{7,31},{8,16},{9,... | collective-permute-start | bytes 221192 | tf_op jit(solution)/shard_map/ppermute | solution.py:62
  42.4 6.4 %collective-permute-start.18 = (bf16[32,1152]{1,0:T(8,128)(2,1)S(1)}, bf16[32,1152]{1,0:T(8,128)(2,1)S(1)}, u32[]{:S(2)}, u32[]{:S(2)}) collective-permute-start(bf16[32,1152]{1,0:T(8,128)(2,1)S(1)} %merge_x.1.refs_0_), channel_id=1, source_target_pairs={{0,16},{1,17},{2,18},{3,19},{4,20},{5,21},{6,22},{7,23},{8,24},{9,... | collective-permute-start | bytes 221192 | tf_op jit(solution)/shard_map/ppermute | solution.py:62
  42.4 6.4 %collective-permute-start.17 = (bf16[32,1152]{1,0:T(8,128)(2,1)S(1)}, bf16[32,1152]{1,0:T(8,128)(2,1)S(1)}, u32[]{:S(2)}, u32[]{:S(2)}) collective-permute-start(bf16[32,1152]{1,0:T(8,128)(2,1)S(1)} %merge_x.1.refs_0_), channel_id=1, source_target_pairs={{0,8},{1,9},{2,10},{3,11},{4,12},{5,13},{6,14},{7,15},{8,0},{9,1},... | collective-permute-start | bytes 221192 | tf_op jit(solution)/shard_map/ppermute | solution.py:62
  49.5 5.2 %collective-permute-start.22 = (bf16[2,32,256]{2,1,0:T(8,128)(2,1)S(1)}, bf16[2,32,256]{2,1,0:T(8,128)(2,1)S(1)}, u32[]{:S(2)}, u32[]{:S(2)}) collective-permute-start(bf16[2,32,256]{2,1,0:T(8,128)(2,1)S(1)} %out.1.refs_0_), channel_id=1, source_target_pairs={{0,6},{1,7},{2,4},{3,5},{4,2},{5,3},{6,0},{7,1},{8,14},{9,15},{10,... | collective-permute-start | bytes 98312 | tf_op jit(solution)/shard_map/ppermute | solution.py:62
  50.9 4.1 %collective-permute-start.21 = (bf16[2,32,256]{2,1,0:T(8,128)(2,1)S(1)}, bf16[2,32,256]{2,1,0:T(8,128)(2,1)S(1)}, u32[]{:S(2)}, u32[]{:S(2)}) collective-permute-start(bf16[2,32,256]{2,1,0:T(8,128)(2,1)S(1)} %out.1.refs_0_), channel_id=1, source_target_pairs={{0,4},{1,5},{2,6},{3,7},{4,0},{5,1},{6,2},{7,3},{8,12},{9,13},{10,... | collective-permute-start | bytes 98312 | tf_op jit(solution)/shard_map/ppermute | solution.py:62
  56.7 6.2 %collective-permute-start.25 = (bf16[2,2,32,256]{3,2,1,0:T(8,128)(2,1)S(1)}, bf16[2,2,32,256]{3,2,1,0:T(8,128)(2,1)S(1)}, u32[]{:S(2)}, u32[]{:S(2)}) collective-permute-start(bf16[2,2,32,256]{3,2,1,0:T(8,128)(2,1)S(1)} %add_out.1.refs_2_), channel_id=1, source_target_pairs={{0,24},{1,25},{2,26},{3,27},{4,28},{5,29},{6,30},{7,31},{8,16},{9,... | collective-permute-start | bytes 196616 | tf_op jit(solution)/shard_map/ppermute | solution.py:62
  58.1 6.1 %collective-permute-start.24 = (bf16[2,2,32,256]{3,2,1,0:T(8,128)(2,1)S(1)}, bf16[2,2,32,256]{3,2,1,0:T(8,128)(2,1)S(1)}, u32[]{:S(2)}, u32[]{:S(2)}) collective-permute-start(bf16[2,2,32,256]{3,2,1,0:T(8,128)(2,1)S(1)} %add_out.1.refs_2_), channel_id=1, source_target_pairs={{0,16},{1,17},{2,18},{3,19},{4,20},{5,21},{6,22},{7,23},{8,24},{9,... | collective-permute-start | bytes 196616 | tf_op jit(solution)/shard_map/ppermute | solution.py:62
  58.2 6.1 %collective-permute-start.23 = (bf16[2,2,32,256]{3,2,1,0:T(8,128)(2,1)S(1)}, bf16[2,2,32,256]{3,2,1,0:T(8,128)(2,1)S(1)}, u32[]{:S(2)}, u32[]{:S(2)}) collective-permute-start(bf16[2,2,32,256]{3,2,1,0:T(8,128)(2,1)S(1)} %add_out.1.refs_2_), channel_id=1, source_target_pairs={{0,8},{1,9},{2,10},{3,11},{4,12},{5,13},{6,14},{7,15},{8,0},{9,1},... | collective-permute-start | bytes 196616 | tf_op jit(solution)/shard_map/ppermute | solution.py:62
  65.1 5.0 %collective-permute-start.26 = (bf16[64,1024]{1,0:T(8,128)(2,1)S(1)}, bf16[64,1024]{1,0:T(8,128)(2,1)S(1)}, u32[]{:S(2)}, u32[]{:S(2)}) collective-permute-start(bf16[64,1024]{1,0:T(8,128)(2,1)S(1)} %get-tuple-element.78.refs_0_), channel_id=1, source_target_pairs={{0,2},{1,3},{2,0},{3,1},{4,6},{5,7},{6,4},{7,5},{8,10},{9,11},{10,... | collective-permute-start | bytes 393224 | tf_op jit(solution)/shard_map/ppermute | solution.py:62
  70.7 4.3 %collective-permute-start.27 = (bf16[64,512]{1,0:T(8,128)(2,1)S(1)}, bf16[64,512]{1,0:T(8,128)(2,1)S(1)}, u32[]{:S(2)}, u32[]{:S(2)}) collective-permute-start(bf16[64,512]{1,0:T(8,128)(2,1)S(1)} %get-tuple-element.81), channel_id=1, source_target_pairs={{0,4},{1,5},{2,6},{3,7},{4,0},{5,1},{6,2},{7,3},{8,12},{9,13},{10,... | collective-permute-start | bytes 196616 | tf_op jit(solution)/shard_map/ppermute | solution.py:62
  75.0 6.1 %collective-permute-start.30 = (bf16[64,512]{1,0:T(8,128)(2,1)S(1)}, bf16[64,512]{1,0:T(8,128)(2,1)S(1)}, u32[]{:S(2)}, u32[]{:S(2)}) collective-permute-start(bf16[64,512]{1,0:T(8,128)(2,1)S(1)} %add_x.1.refs_0_), channel_id=1, source_target_pairs={{0,24},{1,25},{2,26},{3,27},{4,28},{5,29},{6,30},{7,31},{8,16},{9,... | collective-permute-start | bytes 196616 | tf_op jit(solution)/shard_map/ppermute | solution.py:62
  76.9 5.8 %collective-permute-start.29 = (bf16[64,512]{1,0:T(8,128)(2,1)S(1)}, bf16[64,512]{1,0:T(8,128)(2,1)S(1)}, u32[]{:S(2)}, u32[]{:S(2)}) collective-permute-start(bf16[64,512]{1,0:T(8,128)(2,1)S(1)} %add_x.1.refs_0_), channel_id=1, source_target_pairs={{0,16},{1,17},{2,18},{3,19},{4,20},{5,21},{6,22},{7,23},{8,24},{9,... | collective-permute-start | bytes 196616 | tf_op jit(solution)/shard_map/ppermute | solution.py:62
  77.7 5.0 %collective-permute-start.28 = (bf16[64,512]{1,0:T(8,128)(2,1)S(1)}, bf16[64,512]{1,0:T(8,128)(2,1)S(1)}, u32[]{:S(2)}, u32[]{:S(2)}) collective-permute-start(bf16[64,512]{1,0:T(8,128)(2,1)S(1)} %add_x.1.refs_0_), channel_id=1, source_target_pairs={{0,8},{1,9},{2,10},{3,11},{4,12},{5,13},{6,14},{7,15},{8,0},{9,1},... | collective-permute-start | bytes 196616 | tf_op jit(solution)/shard_map/ppermute | solution.py:62
  82.8 4.0 %collective-permute-start.32 = (bf16[32,512]{1,0:T(8,128)(2,1)S(1)}, bf16[32,512]{1,0:T(8,128)(2,1)S(1)}, u32[]{:S(2)}, u32[]{:S(2)}) collective-permute-start(bf16[32,512]{1,0:T(8,128)(2,1)S(1)} %get-tuple-element.82.refs_0_), channel_id=1, source_target_pairs={{0,4},{1,5},{2,6},{3,7},{4,0},{5,1},{6,2},{7,3},{8,12},{9,13},{10,... | collective-permute-start | bytes 98312 | tf_op jit(solution)/shard_map/ppermute | solution.py:62
  83.0 4.8 %collective-permute-start.33 = (bf16[32,512]{1,0:T(8,128)(2,1)S(1)}, bf16[32,512]{1,0:T(8,128)(2,1)S(1)}, u32[]{:S(2)}, u32[]{:S(2)}) collective-permute-start(bf16[32,512]{1,0:T(8,128)(2,1)S(1)} %get-tuple-element.83), channel_id=1, source_target_pairs={{0,6},{1,7},{2,4},{3,5},{4,2},{5,3},{6,0},{7,1},{8,14},{9,15},{10,... | collective-permute-start | bytes 98312 | tf_op jit(solution)/shard_map/ppermute | solution.py:62
  (14 other events, 292.0 us)

commit v8 on v7

--- a/solution.py
+++ b/solution.py
@@ -435,23 +435,15 @@
 
 
 def down_kernel(place, *refs):
-    nx, ny = place.nx, place.ny
+    ny = place.ny
     parts = refs[:ny]
-    own, sibling = refs[ny : ny + 2]
-    outs = refs[ny + 2 : ny + 2 + nx]
-    feed = refs[-1]
+    own, sibling, out, feed = refs[ny:]
     total = sum(p[...].astype(F32) for p in parts)
     hidden = (0.5 * total * (1.0 + lax.erf(total * 0.5**0.5))).astype(BF16)
     ncols = own.shape[1]
     feed[:, at(place.core(), ncols)] = dot(hidden, own[...])
     feed[:, at(1 - place.core(), ncols)] = dot(hidden, sibling[...])
-    width = outs[0].shape[1]
-    for dx in range(nx):
-        outs[dx][...] = feed[:, at(place.x_after(dx), width)].astype(BF16)
-
-
-def add_x_kernel(place, *refs):
-    refs[-1][...] = sum(r[...].astype(F32) for r in refs[:-1]).astype(BF16)
+    out[...] = feed[...].astype(BF16)
 
 
 def add_z_kernel(place, *refs):
@@ -468,10 +460,11 @@
     mid, bias, out, full = refs[nx * ny :]
     group, steps, _ = out.shape
     width = parts[0].shape[1]
-    for dx in range(nx):
-        for dy in range(ny):
-            block = place.y_before(dy) * nx + place.x_before(dx)
-            full[:, at(block, width)] = parts[dx * ny + dy][...].astype(F32)
+    for dy in range(ny):
+        total = parts[dy][...].astype(F32)
+        for dx in range(1, nx):
+            total = total + parts[dx * ny + dy][...].astype(F32)
+        full[:, at(place.y_before(dy), width)] = total
     result = mid[...] + full[...] + bias[...]
     for i in range(group):
         out[i] = result[i * steps : (i + 1) * steps].astype(BF16)
@@ -636,16 +629,14 @@
         ],
     )
     up_parts = [up_part] + [place.move(up_part, dy=dy) for dy in range(1, ny)]
-    piece = CORES * w_down.shape[1] // nx
-    feeds = call(
+    piece = CORES * w_down.shape[1]
+    feed = call(
         bind(down_kernel, place),
         "gelu_down",
         [*up_parts, w_down, w_down_sibling],
-        [shape((ny * rows, piece))] * nx,
-        scratch=[pltpu.VMEM((ny * rows, CORES * w_down.shape[1]), F32)],
-    )
-    feeds = [feeds[0]] + [place.move(feeds[dx], dx=dx) for dx in range(1, nx)]
-    feed = call(bind(add_x_kernel, place), "add_x", feeds, shape((ny * rows, piece)))
+        shape((ny * rows, piece)),
+        scratch=[pltpu.VMEM((ny * rows, piece), F32)],
+    )
     summed = call(
         bind(add_z_kernel, place),
         "add_z",

time: 89.9 us -> 89.1 us (level)
    ppermute x32 -> x31, waiting for transfers between devices: 35.6 us -> 34.9 us  [move(): return lax.ppermute(value, ('seq', 'req'), pairs)]
    pallas_call x14 -> x13, Pallas kernels: 10.7 us -> 10.4 us  [call(): pl.pallas_call(kernel, name=name, out_shape=outs, in_specs=in_specs or [V...]
    ppermute x32 -> x31, starting transfers between devices: 38 us -> 38.2 us  [move(): return lax.ppermute(value, ('seq', 'req'), pairs)]
  transfers between devices with their start and end apart: 34 -> 33, of which waited for: 20 -> 18; matrix products, arithmetic and copies ran while one was open for 2% -> 2% of each run, Pallas kernels for 8% -> 8%
where the time goes in v8:
time: 89.1 us; the launch traced here: 88.8 us
  starting transfers between devices  40.1 us (45%)
  waiting for transfers between devices  34.9 us (39%)
  Pallas kernels  10.4 us (12%)
  other arithmetic  1.44 us (2%)
  local copies, waits for them, and re-layouts  0.97 us (1%)
  between operations  0.94 us (1%)
    ppermute x31, starting transfers between devices, move(): return lax.ppermute(value, ('seq', 'req'), pairs)  38.2 us
    ppermute x31, waiting for transfers between devices, move(): return lax.ppermute(value, ('seq', 'req'), pairs)  34.9 us
    pallas_call x13, Pallas kernels, call(): pl.pallas_call(kernel, name=name, out_shape=outs, in_specs=in_specs or [V...  10.4 us
    ppermute x2, starting transfers between devices, transpose(): return lax.ppermute(value, ('seq', 'req'), pairs)  1.85 us
  transfers between devices with their start and end apart: 33, of which 18 were waited for; matrix products, arithmetic and copies ran while one was open for 2% of the time, Pallas kernels for 8%

profile of v8, /device:TPU:0, one launch (start us, length us, event | category | flops | bytes accessed | tf_op | source)
XLA Modules:
  0.0 88.8 jit_solution(3501685704716746073)
XLA Ops:
  1.7 2.6 %collective-permute-start = (bf16[8,4,2048]{2,1,0:T(4,128)(2,1)}, bf16[8,4,2048]{2,1,0:T(4,128)(2,1)S(1)}, u32[]{:S(2)}, u32[]{:S(2)}) collective-permute-start(bf16[8,4,2048]{2,1,0:T(4,128)(2,1)} %refs_0_.3), channel_id=1, source_target_pairs={{0,2},{1,3},{2,0},{3,1},{4,6},{5,7},{6,4},{7,5},{8,10},{9,11},{10,... | collective-permute-start | bytes 393224 | tf_op jit(solution)/shard_map/ppermute | solution.py:62
  6.6 1.1 %norm.1 = (bf16[32,2048]{1,0:T(8,128)(2,1)S(1)}, bf16[512,256]{1,0:T(8,128)(2,1)S(1)}, bf16[512,256]{1,0:T(8,128)(2,1)S(1)}, bf16[512,256]{1,0:T(8,128)(2,1)S(1)}) custom-call(bf16[8,4,2048]{2,1,0:T(4,128)(2,1)S(1)} %copy-done.3, f32[1,4096]{1,0:T(1,128)S(1)} %bitcast.6, bf16[512,256]{1,0:T(8,128)(2,1)} %refs_0_.2, bf16[512,256]{1,0:T(8,128)(2,1)} %refs_1_.1, ...), custom_call_target="tpu_custom_call" | custom-call | bytes 1048576 | tf_op jit(solution)/shard_map/norm/pallas_call | solution.py:104
  9.8 1.7 %collective-permute-start.5 = (bf16[32,768]{1,0:T(8,128)(2,1)S(1)}, bf16[32,768]{1,0:T(8,128)(2,1)S(1)}, u32[]{:S(2)}, u32[]{:S(2)}) collective-permute-start(bf16[32,768]{1,0:T(8,128)(2,1)S(1)} %get-tuple-element.51.refs_0_), channel_id=1, source_target_pairs={{0,4},{1,5},{2,6},{3,7},{4,0},{5,1},{6,2},{7,3},{8,12},{9,13},{10,... | collective-permute-start | bytes 147464 | tf_op jit(solution)/shard_map/ppermute | solution.py:62
  11.5 1.5 %collective-permute-start.6 = (bf16[32,768]{1,0:T(8,128)(2,1)S(1)}, bf16[32,768]{1,0:T(8,128)(2,1)S(1)}, u32[]{:S(2)}, u32[]{:S(2)}) collective-permute-start(bf16[32,768]{1,0:T(8,128)(2,1)S(1)} %get-tuple-element.52), channel_id=1, source_target_pairs={{0,6},{1,7},{2,4},{3,5},{4,2},{5,3},{6,0},{7,1},{8,14},{9,15},{10,... | collective-permute-start | bytes 147464 | tf_op jit(solution)/shard_map/ppermute | solution.py:62
  13.3 3.2 %caches.1 = (bf16[8,64,2048]{2,1,0:T(8,128)(2,1)}, bf16[8,64,2048]{2,1,0:T(8,128)(2,1)}, bf16[8,64,2048]{2,1,0:T(8,128)(2,1)S(1)}, bf16[8,64,2048]{2,1,0:T(8,128)(2,1)S(1)}, f32[8,128]{1,0:T(8,128)S(1)}) custom-call(bf16[8,64,2048]{2,1,0:T(8,128)(2,1)S(1)} %copy-done, bf16[8,64,2048]{2,1,0:T(8,128)(2,1)} %values_in), custom_call_target="tpu_custom_call" | custom-call | bytes 16777216 | tf_op jit(solution)/shard_map/caches/pallas_call | solution.py:104
  17.2 1.2 %collective-permute-start.13 = (bf16[512,256]{1,0:T(8,128)(2,1)S(1)}, bf16[512,256]{1,0:T(8,128)(2,1)S(1)}, u32[]{:S(2)}, u32[]{:S(2)}) collective-permute-start(bf16[512,256]{1,0:T(8,128)(2,1)S(1)} %copy-done.11), channel_id=1, source_target_pairs={{0,2},{1,3},{2,6},{3,7},{4,0},{5,1},{6,4},{7,5},{8,10},{9,11},{10,... | collective-permute-start | bytes 786440 | tf_op jit(solution)/shard_map/ppermute | solution.py:77
  19.0 3.7 %collective-permute-start.11 = (bf16[2,32,768]{2,1,0:T(8,128)(2,1)S(1)}, bf16[2,32,768]{2,1,0:T(8,128)(2,1)S(1)}, u32[]{:S(2)}, u32[]{:S(2)}) collective-permute-start(bf16[2,32,768]{2,1,0:T(8,128)(2,1)S(1)} %add_qkv.1.refs_0_), channel_id=1, source_target_pairs={{0,24},{1,25},{2,26},{3,27},{4,28},{5,29},{6,30},{7,31},{8,16},{9,... | collective-permute-start | bytes 294920 | tf_op jit(solution)/shard_map/ppermute | solution.py:62
  23.5 2.6 %collective-permute-done.11.refs_3_ = bf16[2,32,768]{2,1,0:T(8,128)(2,1)S(1)} collective-permute-done((bf16[2,32,768]{2,1,0:T(8,128)(2,1)S(1)}, bf16[2,32,768]{2,1,0:T(8,128)(2,1)S(1)}, u32[]{:S(2)}, u32[]{:S(2)}) %collective-permute-start.11) | collective-permute-done | bytes 98336 | tf_op jit(solution)/shard_map/ppermute | solution.py:62
  26.1 4.0 %collective-permute-done.10.refs_2_ = bf16[2,32,768]{2,1,0:T(8,128)(2,1)S(1)} collective-permute-done((bf16[2,32,768]{2,1,0:T(8,128)(2,1)S(1)}, bf16[2,32,768]{2,1,0:T(8,128)(2,1)S(1)}, u32[]{:S(2)}, u32[]{:S(2)}) %collective-permute-start.10) | collective-permute-done | bytes 98336 | tf_op jit(solution)/shard_map/ppermute | solution.py:62
  30.2 2.3 %attention.1 = (bf16[8,64,2048]{2,1,0:T(8,128)(2,1)}, bf16[8,64,2048]{2,1,0:T(8,128)(2,1)}, bf16[32,1152]{1,0:T(8,128)(2,1)S(1)}, bf16[32,1152]{1,0:T(8,128)(2,1)S(1)}) custom-call(bf16[2,32,768]{2,1,0:T(8,128)(2,1)S(1)} %add_qkv.1.refs_0_, bf16[2,32,768]{2,1,0:T(8,128)(2,1)S(1)} %collective-permute-done.9.refs_1_, ...), custom_call_target="tpu_custom_call", output_to_operand_aliasing={{0}: (7, {}), {1}: (8, {})} | custom-call | bytes 1048576 | tf_op jit(solution)/shard_map/attention/pallas_call | solution.py:104
  33.1 4.2 %collective-permute-start.14 = (bf16[32,1152]{1,0:T(8,128)(2,1)S(1)}, bf16[32,1152]{1,0:T(8,128)(2,1)S(1)}, u32[]{:S(2)}, u32[]{:S(2)}) collective-permute-start(bf16[32,1152]{1,0:T(8,128)(2,1)S(1)} %get-tuple-element.67), channel_id=1, source_target_pairs={{0,4},{1,5},{2,6},{3,7},{4,0},{5,1},{6,2},{7,3},{8,12},{9,13},{10,... | collective-permute-start | bytes 221192 | tf_op jit(solution)/shard_map/ppermute | solution.py:62
  37.3 2.5 %collective-permute-done.14.refs_1_ = bf16[32,1152]{1,0:T(8,128)(2,1)S(1)} collective-permute-done((bf16[32,1152]{1,0:T(8,128)(2,1)S(1)}, bf16[32,1152]{1,0:T(8,128)(2,1)S(1)}, u32[]{:S(2)}, u32[]{:S(2)}) %collective-permute-start.14) | collective-permute-done | bytes 73760 | tf_op jit(solution)/shard_map/ppermute | solution.py:62
  40.1 2.4 %collective-permute-start.19 = (bf16[32,1152]{1,0:T(8,128)(2,1)S(1)}, bf16[32,1152]{1,0:T(8,128)(2,1)S(1)}, u32[]{:S(2)}, u32[]{:S(2)}) collective-permute-start(bf16[32,1152]{1,0:T(8,128)(2,1)S(1)} %merge_x.1.refs_0_), channel_id=1, source_target_pairs={{0,24},{1,25},{2,26},{3,27},{4,28},{5,29},{6,30},{7,31},{8,16},{9,... | collective-permute-start | bytes 221192 | tf_op jit(solution)/shard_map/ppermute | solution.py:62
  42.5 2.1 %collective-permute-start.17 = (bf16[32,1152]{1,0:T(8,128)(2,1)S(1)}, bf16[32,1152]{1,0:T(8,128)(2,1)S(1)}, u32[]{:S(2)}, u32[]{:S(2)}) collective-permute-start(bf16[32,1152]{1,0:T(8,128)(2,1)S(1)} %merge_x.1.refs_0_), channel_id=1, source_target_pairs={{0,8},{1,9},{2,10},{3,11},{4,12},{5,13},{6,14},{7,15},{8,0},{9,1},... | collective-permute-start | bytes 221192 | tf_op jit(solution)/shard_map/ppermute | solution.py:62
  44.6 2.1 %collective-permute-done.19.refs_3_ = bf16[32,1152]{1,0:T(8,128)(2,1)S(1)} collective-permute-done((bf16[32,1152]{1,0:T(8,128)(2,1)S(1)}, bf16[32,1152]{1,0:T(8,128)(2,1)S(1)}, u32[]{:S(2)}, u32[]{:S(2)}) %collective-permute-start.19) | collective-permute-done | bytes 73760 | tf_op jit(solution)/shard_map/ppermute | solution.py:62
  46.7 2.2 %collective-permute-done.18.refs_2_ = bf16[32,1152]{1,0:T(8,128)(2,1)S(1)} collective-permute-done((bf16[32,1152]{1,0:T(8,128)(2,1)S(1)}, bf16[32,1152]{1,0:T(8,128)(2,1)S(1)}, u32[]{:S(2)}, u32[]{:S(2)}) %collective-permute-start.18) | collective-permute-done | bytes 73760 | tf_op jit(solution)/shard_map/ppermute | solution.py:62
  49.6 1.1 %collective-permute-start.22 = (bf16[2,32,256]{2,1,0:T(8,128)(2,1)S(1)}, bf16[2,32,256]{2,1,0:T(8,128)(2,1)S(1)}, u32[]{:S(2)}, u32[]{:S(2)}) collective-permute-start(bf16[2,32,256]{2,1,0:T(8,128)(2,1)S(1)} %out.1.refs_0_), channel_id=1, source_target_pairs={{0,6},{1,7},{2,4},{3,5},{4,2},{5,3},{6,0},{7,1},{8,14},{9,15},{10,... | collective-permute-start | bytes 98312 | tf_op jit(solution)/shard_map/ppermute | solution.py:62
  50.7 1.8 %collective-permute-start.21 = (bf16[2,32,256]{2,1,0:T(8,128)(2,1)S(1)}, bf16[2,32,256]{2,1,0:T(8,128)(2,1)S(1)}, u32[]{:S(2)}, u32[]{:S(2)}) collective-permute-start(bf16[2,32,256]{2,1,0:T(8,128)(2,1)S(1)} %out.1.refs_0_), channel_id=1, source_target_pairs={{0,4},{1,5},{2,6},{3,7},{4,0},{5,1},{6,2},{7,3},{8,12},{9,13},{10,... | collective-permute-start | bytes 98312 | tf_op jit(solution)/shard_map/ppermute | solution.py:62
  53.2 1.6 %collective-permute-done.22.refs_3_ = bf16[2,32,256]{2,1,0:T(8,128)(2,1)S(1)} collective-permute-done((bf16[2,32,256]{2,1,0:T(8,128)(2,1)S(1)}, bf16[2,32,256]{2,1,0:T(8,128)(2,1)S(1)}, u32[]{:S(2)}, u32[]{:S(2)}) %collective-permute-start.22) | collective-permute-done | bytes 32800 | tf_op jit(solution)/shard_map/ppermute | solution.py:62
  54.8 1.7 %collective-permute-done.20.refs_1_ = bf16[2,32,256]{2,1,0:T(8,128)(2,1)S(1)} collective-permute-done((bf16[2,32,256]{2,1,0:T(8,128)(2,1)S(1)}, bf16[2,32,256]{2,1,0:T(8,128)(2,1)S(1)}, u32[]{:S(2)}, u32[]{:S(2)}) %collective-permute-start.20) | collective-permute-done | bytes 32800 | tf_op jit(solution)/shard_map/ppermute | solution.py:62
  56.5 1.6 %collective-permute-start.25 = (bf16[2,2,32,256]{3,2,1,0:T(8,128)(2,1)S(1)}, bf16[2,2,32,256]{3,2,1,0:T(8,128)(2,1)S(1)}, u32[]{:S(2)}, u32[]{:S(2)}) collective-permute-start(bf16[2,2,32,256]{3,2,1,0:T(8,128)(2,1)S(1)} %add_out.1.refs_2_), channel_id=1, source_target_pairs={{0,24},{1,25},{2,26},{3,27},{4,28},{5,29},{6,30},{7,31},{8,16},{9,... | collective-permute-start | bytes 196616 | tf_op jit(solution)/shard_map/ppermute | solution.py:62
  58.1 2.9 %collective-permute-start.23 = (bf16[2,2,32,256]{3,2,1,0:T(8,128)(2,1)S(1)}, bf16[2,2,32,256]{3,2,1,0:T(8,128)(2,1)S(1)}, u32[]{:S(2)}, u32[]{:S(2)}) collective-permute-start(bf16[2,2,32,256]{3,2,1,0:T(8,128)(2,1)S(1)} %add_out.1.refs_2_), channel_id=1, source_target_pairs={{0,8},{1,9},{2,10},{3,11},{4,12},{5,13},{6,14},{7,15},{8,0},{9,1},... | collective-permute-start | bytes 196616 | tf_op jit(solution)/shard_map/ppermute | solution.py:62
  60.9 1.8 %collective-permute-done.25.refs_5_ = bf16[2,2,32,256]{3,2,1,0:T(8,128)(2,1)S(1)} collective-permute-done((bf16[2,2,32,256]{3,2,1,0:T(8,128)(2,1)S(1)}, bf16[2,2,32,256]{3,2,1,0:T(8,128)(2,1)S(1)}, u32[]{:S(2)}, u32[]{:S(2)}) %collective-permute-start.25) | collective-permute-done | bytes 65568 | tf_op jit(solution)/shard_map/ppermute | solution.py:62
  62.7 1.4 %collective-permute-done.24.refs_4_ = bf16[2,2,32,256]{3,2,1,0:T(8,128)(2,1)S(1)} collective-permute-done((bf16[2,2,32,256]{3,2,1,0:T(8,128)(2,1)S(1)}, bf16[2,2,32,256]{3,2,1,0:T(8,128)(2,1)S(1)}, u32[]{:S(2)}, u32[]{:S(2)}) %collective-permute-start.24) | collective-permute-done | bytes 65568 | tf_op jit(solution)/shard_map/ppermute | solution.py:62
  65.9 4.2 %collective-permute-done.26.refs_1_ = bf16[64,1024]{1,0:T(8,128)(2,1)S(1)} collective-permute-done((bf16[64,1024]{1,0:T(8,128)(2,1)S(1)}, bf16[64,1024]{1,0:T(8,128)(2,1)S(1)}, u32[]{:S(2)}, u32[]{:S(2)}) %collective-permute-start.26) | collective-permute-done | bytes 131104 | tf_op jit(solution)/shard_map/ppermute | solution.py:62
  70.6 1.9 %collective-permute-start.29 = (bf16[64,1024]{1,0:T(8,128)(2,1)S(1)}, bf16[64,1024]{1,0:T(8,128)(2,1)S(1)}, u32[]{:S(2)}, u32[]{:S(2)}) collective-permute-start(bf16[64,1024]{1,0:T(8,128)(2,1)S(1)} %gelu_down.1.refs_0_), channel_id=1, source_target_pairs={{0,24},{1,25},{2,26},{3,27},{4,28},{5,29},{6,30},{7,31},{8,16},{9,... | collective-permute-start | bytes 393224 | tf_op jit(solution)/shard_map/ppermute | solution.py:62
  73.2 1.9 %collective-permute-start.27 = (bf16[64,1024]{1,0:T(8,128)(2,1)S(1)}, bf16[64,1024]{1,0:T(8,128)(2,1)S(1)}, u32[]{:S(2)}, u32[]{:S(2)}) collective-permute-start(bf16[64,1024]{1,0:T(8,128)(2,1)S(1)} %gelu_down.1.refs_0_), channel_id=1, source_target_pairs={{0,8},{1,9},{2,10},{3,11},{4,12},{5,13},{6,14},{7,15},{8,0},{9,1},... | collective-permute-start | bytes 393224 | tf_op jit(solution)/shard_map/ppermute | solution.py:62
  75.1 2.6 %collective-permute-done.29.refs_3_ = bf16[64,1024]{1,0:T(8,128)(2,1)S(1)} collective-permute-done((bf16[64,1024]{1,0:T(8,128)(2,1)S(1)}, bf16[64,1024]{1,0:T(8,128)(2,1)S(1)}, u32[]{:S(2)}, u32[]{:S(2)}) %collective-permute-start.29) | collective-permute-done | bytes 131104 | tf_op jit(solution)/shard_map/ppermute | solution.py:62
  77.6 3.7 %collective-permute-done.28.refs_2_ = bf16[64,1024]{1,0:T(8,128)(2,1)S(1)} collective-permute-done((bf16[64,1024]{1,0:T(8,128)(2,1)S(1)}, bf16[64,1024]{1,0:T(8,128)(2,1)S(1)}, u32[]{:S(2)}, u32[]{:S(2)}) %collective-permute-start.28) | collective-permute-done | bytes 131104 | tf_op jit(solution)/shard_map/ppermute | solution.py:62
  82.1 1.4 %collective-permute-start.32 = (bf16[32,1024]{1,0:T(8,128)(2,1)S(1)}, bf16[32,1024]{1,0:T(8,128)(2,1)S(1)}, u32[]{:S(2)}, u32[]{:S(2)}) collective-permute-start(bf16[32,1024]{1,0:T(8,128)(2,1)S(1)} %get-tuple-element.79), channel_id=1, source_target_pairs={{0,6},{1,7},{2,4},{3,5},{4,2},{5,3},{6,0},{7,1},{8,14},{9,15},{10,... | collective-permute-start | bytes 196616 | tf_op jit(solution)/shard_map/ppermute | solution.py:62
  83.6 1.4 %collective-permute-start.30 = (bf16[32,1024]{1,0:T(8,128)(2,1)S(1)}, bf16[32,1024]{1,0:T(8,128)(2,1)S(1)}, u32[]{:S(2)}, u32[]{:S(2)}) collective-permute-start(bf16[32,1024]{1,0:T(8,128)(2,1)S(1)} %get-tuple-element.79), channel_id=1, source_target_pairs={{0,2},{1,3},{2,0},{3,1},{4,6},{5,7},{6,4},{7,5},{8,10},{9,11},{10,... | collective-permute-start | bytes 196616 | tf_op jit(solution)/shard_map/ppermute | solution.py:62
  85.7 1.6 %collective-permute-done.32.refs_3_ = bf16[32,1024]{1,0:T(8,128)(2,1)S(1)} collective-permute-done((bf16[32,1024]{1,0:T(8,128)(2,1)S(1)}, bf16[32,1024]{1,0:T(8,128)(2,1)S(1)}, u32[]{:S(2)}, u32[]{:S(2)}) %collective-permute-start.32) | collective-permute-done | bytes 65568 | tf_op jit(solution)/shard_map/ppermute | solution.py:62
  (74 shorter events, 15.9 us)
Async XLA Ops:
  0.6 7.9 %collective-permute-start.1 = (bf16[512,256]{1,0:T(8,128)(2,1)}, bf16[512,256]{1,0:T(8,128)(2,1)S(1)}, u32[]{:S(2)}, u32[]{:S(2)}) collective-permute-start(bf16[512,256]{1,0:T(8,128)(2,1)} %refs_0_.2), channel_id=1, source_target_pairs={{0,1},{1,0},{2,3},{3,2},{4,5},{5,4},{6,7},{7,6},{8,9},{9,8},{10,11... | collective-permute-start | bytes 786440 | tf_op jit(solution)/shard_map/ppermute | solution.py:62
  1.2 7.4 %collective-permute-start.2 = (bf16[512,256]{1,0:T(8,128)(2,1)}, bf16[512,256]{1,0:T(8,128)(2,1)S(1)}, u32[]{:S(2)}, u32[]{:S(2)}) collective-permute-start(bf16[512,256]{1,0:T(8,128)(2,1)} %refs_1_.1), channel_id=1, source_target_pairs={{0,1},{1,0},{2,3},{3,2},{4,5},{5,4},{6,7},{7,6},{8,9},{9,8},{10,11... | collective-permute-start | bytes 786440 | tf_op jit(solution)/shard_map/ppermute | solution.py:62
  1.2 7.3 %collective-permute-start.3 = (bf16[512,256]{1,0:T(8,128)(2,1)}, bf16[512,256]{1,0:T(8,128)(2,1)S(1)}, u32[]{:S(2)}, u32[]{:S(2)}) collective-permute-start(bf16[512,256]{1,0:T(8,128)(2,1)} %refs_2_.2), channel_id=1, source_target_pairs={{0,1},{1,0},{2,3},{3,2},{4,5},{5,4},{6,7},{7,6},{8,9},{9,8},{10,11... | collective-permute-start | bytes 786440 | tf_op jit(solution)/shard_map/ppermute | solution.py:62
  1.7 6.9 %collective-permute-start = (bf16[8,4,2048]{2,1,0:T(4,128)(2,1)}, bf16[8,4,2048]{2,1,0:T(4,128)(2,1)S(1)}, u32[]{:S(2)}, u32[]{:S(2)}) collective-permute-start(bf16[8,4,2048]{2,1,0:T(4,128)(2,1)} %refs_0_.3), channel_id=1, source_target_pairs={{0,2},{1,3},{2,0},{3,1},{4,6},{5,7},{6,4},{7,5},{8,10},{9,11},{10,... | collective-permute-start | bytes 393224 | tf_op jit(solution)/shard_map/ppermute | solution.py:62
  9.2 7.9 %collective-permute-start.7 = (bf16[512,1024]{1,0:T(8,128)(2,1)}, bf16[512,1024]{1,0:T(8,128)(2,1)S(1)}, u32[]{:S(2)}, u32[]{:S(2)}) collective-permute-start(bf16[512,1024]{1,0:T(8,128)(2,1)} %refs_8_.1), channel_id=1, source_target_pairs={{0,1},{1,0},{2,3},{3,2},{4,5},{5,4},{6,7},{7,6},{8,9},{9,8},{10,11... | collective-permute-start | bytes 3145736 | tf_op jit(solution)/shard_map/ppermute | solution.py:62
  9.3 7.9 %collective-permute-start.8 = (bf16[1024,512]{1,0:T(8,128)(2,1)}, bf16[1024,512]{1,0:T(8,128)(2,1)S(1)}, u32[]{:S(2)}, u32[]{:S(2)}) collective-permute-start(bf16[1024,512]{1,0:T(8,128)(2,1)} %refs_2_.3), channel_id=1, source_target_pairs={{0,1},{1,0},{2,3},{3,2},{4,5},{5,4},{6,7},{7,6},{8,9},{9,8},{10,11... | collective-permute-start | bytes 3145736 | tf_op jit(solution)/shard_map/ppermute | solution.py:62
  9.8 6.7 %collective-permute-start.5 = (bf16[32,768]{1,0:T(8,128)(2,1)S(1)}, bf16[32,768]{1,0:T(8,128)(2,1)S(1)}, u32[]{:S(2)}, u32[]{:S(2)}) collective-permute-start(bf16[32,768]{1,0:T(8,128)(2,1)S(1)} %get-tuple-element.51.refs_0_), channel_id=1, source_target_pairs={{0,4},{1,5},{2,6},{3,7},{4,0},{5,1},{6,2},{7,3},{8,12},{9,13},{10,... | collective-permute-start | bytes 147464 | tf_op jit(solution)/shard_map/ppermute | solution.py:62
  11.5 5.0 %collective-permute-start.6 = (bf16[32,768]{1,0:T(8,128)(2,1)S(1)}, bf16[32,768]{1,0:T(8,128)(2,1)S(1)}, u32[]{:S(2)}, u32[]{:S(2)}) collective-permute-start(bf16[32,768]{1,0:T(8,128)(2,1)S(1)} %get-tuple-element.52), channel_id=1, source_target_pairs={{0,6},{1,7},{2,4},{3,5},{4,2},{5,3},{6,0},{7,1},{8,14},{9,15},{10,... | collective-permute-start | bytes 147464 | tf_op jit(solution)/shard_map/ppermute | solution.py:62
  13.0 4.1 %collective-permute-start.4 = (bf16[32,768]{1,0:T(8,128)(2,1)S(1)}, bf16[32,768]{1,0:T(8,128)(2,1)S(1)}, u32[]{:S(2)}, u32[]{:S(2)}) collective-permute-start(bf16[32,768]{1,0:T(8,128)(2,1)S(1)} %get-tuple-element.52), channel_id=1, source_target_pairs={{0,2},{1,3},{2,0},{3,1},{4,6},{5,7},{6,4},{7,5},{8,10},{9,11},{10,... | collective-permute-start | bytes 147464 | tf_op jit(solution)/shard_map/ppermute | solution.py:62
  17.2 15.3 %collective-permute-start.13 = (bf16[512,256]{1,0:T(8,128)(2,1)S(1)}, bf16[512,256]{1,0:T(8,128)(2,1)S(1)}, u32[]{:S(2)}, u32[]{:S(2)}) collective-permute-start(bf16[512,256]{1,0:T(8,128)(2,1)S(1)} %copy-done.11), channel_id=1, source_target_pairs={{0,2},{1,3},{2,6},{3,7},{4,0},{5,1},{6,4},{7,5},{8,10},{9,11},{10,... | collective-permute-start | bytes 786440 | tf_op jit(solution)/shard_map/ppermute | solution.py:77
  18.4 14.1 %collective-permute-start.12 = (bf16[512,256]{1,0:T(8,128)(2,1)S(1)}, bf16[512,256]{1,0:T(8,128)(2,1)S(1)}, u32[]{:S(2)}, u32[]{:S(2)}) collective-permute-start(bf16[512,256]{1,0:T(8,128)(2,1)S(1)} %copy-done.11), channel_id=1, source_target_pairs={{0,0},{1,1},{2,4},{3,5},{4,2},{5,3},{6,6},{7,7},{8,8},{9,9},{10,12... | collective-permute-start | bytes 786440 | tf_op jit(solution)/shard_map/ppermute | solution.py:77
  19.0 7.0 %collective-permute-start.11 = (bf16[2,32,768]{2,1,0:T(8,128)(2,1)S(1)}, bf16[2,32,768]{2,1,0:T(8,128)(2,1)S(1)}, u32[]{:S(2)}, u32[]{:S(2)}) collective-permute-start(bf16[2,32,768]{2,1,0:T(8,128)(2,1)S(1)} %add_qkv.1.refs_0_), channel_id=1, source_target_pairs={{0,24},{1,25},{2,26},{3,27},{4,28},{5,29},{6,30},{7,31},{8,16},{9,... | collective-permute-start | bytes 294920 | tf_op jit(solution)/shard_map/ppermute | solution.py:62
  22.7 7.4 %collective-permute-start.10 = (bf16[2,32,768]{2,1,0:T(8,128)(2,1)S(1)}, bf16[2,32,768]{2,1,0:T(8,128)(2,1)S(1)}, u32[]{:S(2)}, u32[]{:S(2)}) collective-permute-start(bf16[2,32,768]{2,1,0:T(8,128)(2,1)S(1)} %add_qkv.1.refs_0_), channel_id=1, source_target_pairs={{0,16},{1,17},{2,18},{3,19},{4,20},{5,21},{6,22},{7,23},{8,24},{9,... | collective-permute-start | bytes 294920 | tf_op jit(solution)/shard_map/ppermute | solution.py:62
  22.7 7.4 %collective-permute-start.9 = (bf16[2,32,768]{2,1,0:T(8,128)(2,1)S(1)}, bf16[2,32,768]{2,1,0:T(8,128)(2,1)S(1)}, u32[]{:S(2)}, u32[]{:S(2)}) collective-permute-start(bf16[2,32,768]{2,1,0:T(8,128)(2,1)S(1)} %add_qkv.1.refs_0_), channel_id=1, source_target_pairs={{0,8},{1,9},{2,10},{3,11},{4,12},{5,13},{6,14},{7,15},{8,0},{9,1},... | collective-permute-start | bytes 294920 | tf_op jit(solution)/shard_map/ppermute | solution.py:62
  32.5 7.6 %collective-permute-start.15 = (bf16[512,256]{1,0:T(8,128)(2,1)S(1)}, bf16[512,256]{1,0:T(8,128)(2,1)S(1)}, u32[]{:S(2)}, u32[]{:S(2)}) collective-permute-start(bf16[512,256]{1,0:T(8,128)(2,1)S(1)} %collective-permute-done.12.refs_0_), channel_id=1, source_target_pairs={{0,1},{1,0},{2,3},{3,2},{4,5},{5,4},{6,7},{7,6},{8,9},{9,8},{10,11... | collective-permute-start | bytes 786440 | tf_op jit(solution)/shard_map/ppermute | solution.py:62
  32.6 7.5 %collective-permute-start.16 = (bf16[512,256]{1,0:T(8,128)(2,1)S(1)}, bf16[512,256]{1,0:T(8,128)(2,1)S(1)}, u32[]{:S(2)}, u32[]{:S(2)}) collective-permute-start(bf16[512,256]{1,0:T(8,128)(2,1)S(1)} %collective-permute-done.13.refs_2_), channel_id=1, source_target_pairs={{0,1},{1,0},{2,3},{3,2},{4,5},{5,4},{6,7},{7,6},{8,9},{9,8},{10,11... | collective-permute-start | bytes 786440 | tf_op jit(solution)/shard_map/ppermute | solution.py:62
  33.1 6.7 %collective-permute-start.14 = (bf16[32,1152]{1,0:T(8,128)(2,1)S(1)}, bf16[32,1152]{1,0:T(8,128)(2,1)S(1)}, u32[]{:S(2)}, u32[]{:S(2)}) collective-permute-start(bf16[32,1152]{1,0:T(8,128)(2,1)S(1)} %get-tuple-element.67), channel_id=1, source_target_pairs={{0,4},{1,5},{2,6},{3,7},{4,0},{5,1},{6,2},{7,3},{8,12},{9,13},{10,... | collective-permute-start | bytes 221192 | tf_op jit(solution)/shard_map/ppermute | solution.py:62
  40.1 6.5 %collective-permute-start.19 = (bf16[32,1152]{1,0:T(8,128)(2,1)S(1)}, bf16[32,1152]{1,0:T(8,128)(2,1)S(1)}, u32[]{:S(2)}, u32[]{:S(2)}) collective-permute-start(bf16[32,1152]{1,0:T(8,128)(2,1)S(1)} %merge_x.1.refs_0_), channel_id=1, source_target_pairs={{0,24},{1,25},{2,26},{3,27},{4,28},{5,29},{6,30},{7,31},{8,16},{9,... | collective-permute-start | bytes 221192 | tf_op jit(solution)/shard_map/ppermute | solution.py:62
  42.5 6.4 %collective-permute-start.18 = (bf16[32,1152]{1,0:T(8,128)(2,1)S(1)}, bf16[32,1152]{1,0:T(8,128)(2,1)S(1)}, u32[]{:S(2)}, u32[]{:S(2)}) collective-permute-start(bf16[32,1152]{1,0:T(8,128)(2,1)S(1)} %merge_x.1.refs_0_), channel_id=1, source_target_pairs={{0,16},{1,17},{2,18},{3,19},{4,20},{5,21},{6,22},{7,23},{8,24},{9,... | collective-permute-start | bytes 221192 | tf_op jit(solution)/shard_map/ppermute | solution.py:62
  42.5 6.4 %collective-permute-start.17 = (bf16[32,1152]{1,0:T(8,128)(2,1)S(1)}, bf16[32,1152]{1,0:T(8,128)(2,1)S(1)}, u32[]{:S(2)}, u32[]{:S(2)}) collective-permute-start(bf16[32,1152]{1,0:T(8,128)(2,1)S(1)} %merge_x.1.refs_0_), channel_id=1, source_target_pairs={{0,8},{1,9},{2,10},{3,11},{4,12},{5,13},{6,14},{7,15},{8,0},{9,1},... | collective-permute-start | bytes 221192 | tf_op jit(solution)/shard_map/ppermute | solution.py:62
  49.6 5.2 %collective-permute-start.22 = (bf16[2,32,256]{2,1,0:T(8,128)(2,1)S(1)}, bf16[2,32,256]{2,1,0:T(8,128)(2,1)S(1)}, u32[]{:S(2)}, u32[]{:S(2)}) collective-permute-start(bf16[2,32,256]{2,1,0:T(8,128)(2,1)S(1)} %out.1.refs_0_), channel_id=1, source_target_pairs={{0,6},{1,7},{2,4},{3,5},{4,2},{5,3},{6,0},{7,1},{8,14},{9,15},{10,... | collective-permute-start | bytes 98312 | tf_op jit(solution)/shard_map/ppermute | solution.py:62
  50.7 4.1 %collective-permute-start.21 = (bf16[2,32,256]{2,1,0:T(8,128)(2,1)S(1)}, bf16[2,32,256]{2,1,0:T(8,128)(2,1)S(1)}, u32[]{:S(2)}, u32[]{:S(2)}) collective-permute-start(bf16[2,32,256]{2,1,0:T(8,128)(2,1)S(1)} %out.1.refs_0_), channel_id=1, source_target_pairs={{0,4},{1,5},{2,6},{3,7},{4,0},{5,1},{6,2},{7,3},{8,12},{9,13},{10,... | collective-permute-start | bytes 98312 | tf_op jit(solution)/shard_map/ppermute | solution.py:62
  56.5 6.3 %collective-permute-start.25 = (bf16[2,2,32,256]{3,2,1,0:T(8,128)(2,1)S(1)}, bf16[2,2,32,256]{3,2,1,0:T(8,128)(2,1)S(1)}, u32[]{:S(2)}, u32[]{:S(2)}) collective-permute-start(bf16[2,2,32,256]{3,2,1,0:T(8,128)(2,1)S(1)} %add_out.1.refs_2_), channel_id=1, source_target_pairs={{0,24},{1,25},{2,26},{3,27},{4,28},{5,29},{6,30},{7,31},{8,16},{9,... | collective-permute-start | bytes 196616 | tf_op jit(solution)/shard_map/ppermute | solution.py:62
  58.1 6.1 %collective-permute-start.24 = (bf16[2,2,32,256]{3,2,1,0:T(8,128)(2,1)S(1)}, bf16[2,2,32,256]{3,2,1,0:T(8,128)(2,1)S(1)}, u32[]{:S(2)}, u32[]{:S(2)}) collective-permute-start(bf16[2,2,32,256]{3,2,1,0:T(8,128)(2,1)S(1)} %add_out.1.refs_2_), channel_id=1, source_target_pairs={{0,16},{1,17},{2,18},{3,19},{4,20},{5,21},{6,22},{7,23},{8,24},{9,... | collective-permute-start | bytes 196616 | tf_op jit(solution)/shard_map/ppermute | solution.py:62
  58.1 6.1 %collective-permute-start.23 = (bf16[2,2,32,256]{3,2,1,0:T(8,128)(2,1)S(1)}, bf16[2,2,32,256]{3,2,1,0:T(8,128)(2,1)S(1)}, u32[]{:S(2)}, u32[]{:S(2)}) collective-permute-start(bf16[2,2,32,256]{3,2,1,0:T(8,128)(2,1)S(1)} %add_out.1.refs_2_), channel_id=1, source_target_pairs={{0,8},{1,9},{2,10},{3,11},{4,12},{5,13},{6,14},{7,15},{8,0},{9,1},... | collective-permute-start | bytes 196616 | tf_op jit(solution)/shard_map/ppermute | solution.py:62
  65.1 5.0 %collective-permute-start.26 = (bf16[64,1024]{1,0:T(8,128)(2,1)S(1)}, bf16[64,1024]{1,0:T(8,128)(2,1)S(1)}, u32[]{:S(2)}, u32[]{:S(2)}) collective-permute-start(bf16[64,1024]{1,0:T(8,128)(2,1)S(1)} %get-tuple-element.76.refs_0_), channel_id=1, source_target_pairs={{0,2},{1,3},{2,0},{3,1},{4,6},{5,7},{6,4},{7,5},{8,10},{9,11},{10,... | collective-permute-start | bytes 393224 | tf_op jit(solution)/shard_map/ppermute | solution.py:62
  70.6 7.0 %collective-permute-start.29 = (bf16[64,1024]{1,0:T(8,128)(2,1)S(1)}, bf16[64,1024]{1,0:T(8,128)(2,1)S(1)}, u32[]{:S(2)}, u32[]{:S(2)}) collective-permute-start(bf16[64,1024]{1,0:T(8,128)(2,1)S(1)} %gelu_down.1.refs_0_), channel_id=1, source_target_pairs={{0,24},{1,25},{2,26},{3,27},{4,28},{5,29},{6,30},{7,31},{8,16},{9,... | collective-permute-start | bytes 393224 | tf_op jit(solution)/shard_map/ppermute | solution.py:62
  72.5 8.8 %collective-permute-start.28 = (bf16[64,1024]{1,0:T(8,128)(2,1)S(1)}, bf16[64,1024]{1,0:T(8,128)(2,1)S(1)}, u32[]{:S(2)}, u32[]{:S(2)}) collective-permute-start(bf16[64,1024]{1,0:T(8,128)(2,1)S(1)} %gelu_down.1.refs_0_), channel_id=1, source_target_pairs={{0,16},{1,17},{2,18},{3,19},{4,20},{5,21},{6,22},{7,23},{8,24},{9,... | collective-permute-start | bytes 393224 | tf_op jit(solution)/shard_map/ppermute | solution.py:62
  73.2 8.2 %collective-permute-start.27 = (bf16[64,1024]{1,0:T(8,128)(2,1)S(1)}, bf16[64,1024]{1,0:T(8,128)(2,1)S(1)}, u32[]{:S(2)}, u32[]{:S(2)}) collective-permute-start(bf16[64,1024]{1,0:T(8,128)(2,1)S(1)} %gelu_down.1.refs_0_), channel_id=1, source_target_pairs={{0,8},{1,9},{2,10},{3,11},{4,12},{5,13},{6,14},{7,15},{8,0},{9,1},... | collective-permute-start | bytes 393224 | tf_op jit(solution)/shard_map/ppermute | solution.py:62
  81.4 4.3 %collective-permute-start.31 = (bf16[32,1024]{1,0:T(8,128)(2,1)S(1)}, bf16[32,1024]{1,0:T(8,128)(2,1)S(1)}, u32[]{:S(2)}, u32[]{:S(2)}) collective-permute-start(bf16[32,1024]{1,0:T(8,128)(2,1)S(1)} %get-tuple-element.78.refs_0_), channel_id=1, source_target_pairs={{0,4},{1,5},{2,6},{3,7},{4,0},{5,1},{6,2},{7,3},{8,12},{9,13},{10,... | collective-permute-start | bytes 196616 | tf_op jit(solution)/shard_map/ppermute | solution.py:62
  82.1 5.2 %collective-permute-start.32 = (bf16[32,1024]{1,0:T(8,128)(2,1)S(1)}, bf16[32,1024]{1,0:T(8,128)(2,1)S(1)}, u32[]{:S(2)}, u32[]{:S(2)}) collective-permute-start(bf16[32,1024]{1,0:T(8,128)(2,1)S(1)} %get-tuple-element.79), channel_id=1, source_target_pairs={{0,6},{1,7},{2,4},{3,5},{4,2},{5,3},{6,0},{7,1},{8,14},{9,15},{10,... | collective-permute-start | bytes 196616 | tf_op jit(solution)/shard_map/ppermute | solution.py:62
  83.6 4.5 %collective-permute-start.30 = (bf16[32,1024]{1,0:T(8,128)(2,1)S(1)}, bf16[32,1024]{1,0:T(8,128)(2,1)S(1)}, u32[]{:S(2)}, u32[]{:S(2)}) collective-permute-start(bf16[32,1024]{1,0:T(8,128)(2,1)S(1)} %get-tuple-element.79), channel_id=1, source_target_pairs={{0,2},{1,3},{2,0},{3,1},{4,6},{5,7},{6,4},{7,5},{8,10},{9,11},{10,... | collective-permute-start | bytes 196616 | tf_op jit(solution)/shard_map/ppermute | solution.py:62
  (13 other events, 286.3 us)

commit v9 on v7

--- a/solution.py
+++ b/solution.py
@@ -67,13 +67,17 @@
         for z in range(self.nz):
             for x in range(n):
                 for y in range(n):
-                    for c in range(CORES):
-                        pairs.append(
-                            (
-                                ((z * n + x) * n + y) * CORES + c,
-                                ((z * n + y) * n + (x - k) % n) * CORES + c,
-                            )
+                    pairs.append(
+                        (
+                            ((z * n + x) * n + y) * CORES + 1,
+                            ((z * n + y) * n + (x - k) % n) * CORES + 1,
                         )
+                    )
+        return lax.ppermute(value, ("seq", "req"), pairs)
+
+    def hand(self, value, source):
+        chips = self.nz * self.nx * self.ny
+        pairs = [(i * CORES + source, i * CORES + 1 - source) for i in range(chips)]
         return lax.ppermute(value, ("seq", "req"), pairs)
 
     def gather_z(self, value):
@@ -184,7 +188,7 @@
         out[place.x_before(dx)] = total.astype(BF16)
 
 
-def cache_kernel(keys_in, values_in, keys_out, values_out, keys, values, mark, in_sems, out_sems):
+def cache_kernel(keys_in, values_in, keys_out, values_out, keys, values, in_sems, out_sems):
     group = keys.shape[0]
     arrays = ((keys_in, keys, keys_out), (values_in, values, values_out))
     coming = [
@@ -199,7 +203,6 @@
     ]
     for copy in coming:
         copy.start()
-    mark[...] = jnp.zeros_like(mark)
     for arrived, copy in zip(coming, going):
         arrived.wait()
         copy.start()
@@ -387,17 +390,37 @@
     ).astype(BF16)
 
 
+def pack_kernel(own, sibling, out, sems):
+    copies = [
+        pltpu.make_async_copy(sibling, out.at[0], sems.at[0]),
+        pltpu.make_async_copy(own, out.at[1], sems.at[1]),
+    ]
+    for copy in copies:
+        copy.start()
+    for copy in copies:
+        copy.wait()
+
+
 def out_kernel(place, attn, *refs):
     nx = place.nx
     weights = refs[: 2 * nx]
     bias, out, total = refs[2 * nx :]
-    depth = weights[0].shape[0]
-    core = place.core()
-    for k in range(nx):
-        block = lax.rem(place.y() + k, nx)
-        total[block] = dot(attn[:, at(core, depth)], weights[2 * k][...]) + dot(
-            attn[:, at(1 - core, depth)], weights[2 * k + 1][...]
-        )
+    depth = weights[0].shape[1]
+
+    def multiply(mine):
+        for k in range(nx):
+            block = lax.rem(place.y() + k, nx)
+            weight = weights[2 * k + mine]
+            total[block] = dot(attn[:, :depth], weight[0]) + dot(attn[:, depth:], weight[1])
+
+    @pl.when(place.core() == 1)
+    def _():
+        multiply(0)
+
+    @pl.when(place.core() == 0)
+    def _():
+        multiply(1)
+
     total[place.x()] = total[place.x()] + bias[...]
     out[...] = total[...].astype(BF16)
 
@@ -544,32 +567,44 @@
         [shape((rows, 3 * cols))] * ny,
         scratch=[pltpu.VMEM(((ny - 1) * rows, width), F32), pltpu.VMEM((ny * rows, width), BF16)],
     )
-    *parts, tied_up, tied_down = lax.optimization_barrier((*parts, w_up, w_down))
+    out_sibling = place.hand(w_out, 0)
+    *parts, tied_up, tied_down, out_sibling = lax.optimization_barrier(
+        (*parts, w_up, w_down, out_sibling)
+    )
+    packed = call(
+        pack_kernel,
+        "pack",
+        [w_out, out_sibling],
+        shape((CORES, *w_out.shape)),
+        in_specs=[HBM, VMEM],
+        scratch=[pltpu.SemaphoreType.DMA((2,))],
+        moved=4 * 1024 * 1024,
+    )
     w_up_sibling = place.move(tied_up, dc=1)
     w_down_sibling = place.move(tied_down, dc=1)
-    parts, tied_keys, tied_values = lax.optimization_barrier((parts, cache_keys, cache_values))
-    new_keys, new_values, keys, values, mark = call(
+    qkv = call(
+        bind(add_columns_kernel, place),
+        "add_qkv",
+        spread(parts),
+        shape((nx, rows, 3 * cols)),
+    )
+    qkv, w_up_sibling, w_down_sibling, packed = lax.optimization_barrier(
+        (qkv, w_up_sibling, w_down_sibling, packed)
+    )
+    qkv, tied_keys, tied_values = lax.optimization_barrier((qkv, cache_keys, cache_values))
+    new_keys, new_values, keys, values = call(
         cache_kernel,
         "caches",
         [tied_keys, tied_values],
-        [shape(cache_keys.shape)] * 4 + [shape((8, LANES), F32)],
+        [shape(cache_keys.shape)] * 4,
         in_specs=[HBM, HBM],
-        out_specs=[HBM, HBM, VMEM, VMEM, VMEM],
+        out_specs=[HBM, HBM, VMEM, VMEM],
         scratch=[pltpu.SemaphoreType.DMA((2, group)), pltpu.SemaphoreType.DMA((2, group))],
         moved=16 * 1024 * 1024,
         limit=46,
     )
-    qkv = call(
-        bind(add_columns_kernel, place),
-        "add_qkv",
-        [*spread(parts), mark],
-        shape((nx, rows, 3 * cols)),
-    )
-    qkv, w_up_sibling, w_down_sibling, tied = lax.optimization_barrier(
-        (qkv, w_up_sibling, w_down_sibling, w_out)
-    )
     pieces = place.gather_z(qkv)
-    blocks = [place.transpose(tied, k) for k in range(nx)]
+    blocks = [place.transpose(packed, k) for k in range(nx)]
     pack = max(1, min(group, 256 // slots))
     window = min(32, slots)
     new_keys, new_values, *messages = call(
@@ -595,12 +630,11 @@
     messages, blocks = lax.optimization_barrier((messages, blocks))
     w_outs = []
     for block in blocks:
-        w_outs += [block, place.move(block, dc=1)]
+        w_outs += [block, place.hand(block, 1)]
     messages = [messages[0]] + [place.move(messages[dx], dx=dx) for dx in range(1, nx)]
     merged = call(
         bind(merge_x_kernel, place, heads), "merge_x", messages, shape((rows, share + LANES))
     )
-    merged, *w_outs = lax.optimization_barrier((merged, *w_outs))
     pieces = place.gather_z(merged)
     attn = call(bind(merge_z_kernel, place, heads), "merge_z", pieces, shape((rows, share)))
     out_part = call(

time: 89.9 us -> 98.3 us (1.093)
  starting transfers between devices: 39.8 us -> 45.2 us
  waiting for transfers between devices: 35.6 us -> 38 us
    ppermute x0 -> x3, starting transfers between devices: none -> 4.84 us  [hand(): return lax.ppermute(value, ('seq', 'req'), pairs)]
    ppermute x32 -> x30, waiting for transfers between devices: 35.6 us -> 38 us  [move(): return lax.ppermute(value, ('seq', 'req'), pairs)]
    ppermute x32 -> x30, starting transfers between devices: 38 us -> 38.9 us  [move(): return lax.ppermute(value, ('seq', 'req'), pairs)]
    pallas_call x14 -> x15, Pallas kernels: 10.7 us -> 10.6 us  [call(): pl.pallas_call(kernel, name=name, out_shape=outs, in_specs=in_specs or [V...]
  transfers between devices with their start and end apart: 34 -> 35, of which waited for: 20 -> 20; matrix products, arithmetic and copies ran while one was open for 2% -> 1% of each run, Pallas kernels for 8% -> 8%
where the time goes in v9:
time: 98.3 us; the launch traced here: 98 us
  starting transfers between devices  45.2 us (46%)
  waiting for transfers between devices  38 us (39%)
  Pallas kernels  10.6 us (11%)
  local copies, waits for them, and re-layouts  1.92 us (2%)
  other arithmetic  1.44 us (1%)
  between operations  0.99 us (1%)
    ppermute x30, starting transfers between devices, move(): return lax.ppermute(value, ('seq', 'req'), pairs)  38.9 us
    ppermute x30, waiting for transfers between devices, move(): return lax.ppermute(value, ('seq', 'req'), pairs)  38 us
    pallas_call x15, Pallas kernels, call(): pl.pallas_call(kernel, name=name, out_shape=outs, in_specs=in_specs or [V...  10.6 us
    ppermute x3, starting transfers between devices, hand(): return lax.ppermute(value, ('seq', 'req'), pairs)  4.84 us
  transfers between devices with their start and end apart: 35, of which 20 were waited for; matrix products, arithmetic and copies ran while one was open for 1% of the time, Pallas kernels for 8%

profile of v9, /device:TPU:0, one launch (start us, length us, event | category | flops | bytes accessed | tf_op | source)
XLA Modules:
  0.0 98.0 jit_solution(6397864706497941606)
XLA Ops:
  1.7 2.1 %collective-permute-start.4 = (bf16[512,256]{1,0:T(8,128)(2,1)}, bf16[512,256]{1,0:T(8,128)(2,1)S(1)}, u32[]{:S(2)}, u32[]{:S(2)}) collective-permute-start(bf16[512,256]{1,0:T(8,128)(2,1)} %own.1), channel_id=1, source_target_pairs={{0,1},{2,3},{4,5},{6,7},{8,9},{10,11},{12,13},{14,15},{16,17},{18,... | collective-permute-start | bytes 786440 | tf_op jit(solution)/shard_map/ppermute | solution.py:81
  3.8 2.9 %collective-permute-start = (bf16[8,4,2048]{2,1,0:T(4,128)(2,1)}, bf16[8,4,2048]{2,1,0:T(4,128)(2,1)S(1)}, u32[]{:S(2)}, u32[]{:S(2)}) collective-permute-start(bf16[8,4,2048]{2,1,0:T(4,128)(2,1)} %refs_0_.3), channel_id=1, source_target_pairs={{0,2},{1,3},{2,0},{3,1},{4,6},{5,7},{6,4},{7,5},{8,10},{9,11},{10,... | collective-permute-start | bytes 393224 | tf_op jit(solution)/shard_map/ppermute | solution.py:62
  11.4 1.7 %collective-permute-start.5 = (bf16[32,768]{1,0:T(8,128)(2,1)S(1)}, bf16[32,768]{1,0:T(8,128)(2,1)S(1)}, u32[]{:S(2)}, u32[]{:S(2)}) collective-permute-start(bf16[32,768]{1,0:T(8,128)(2,1)S(1)} %get-tuple-element.46), channel_id=1, source_target_pairs={{0,2},{1,3},{2,0},{3,1},{4,6},{5,7},{6,4},{7,5},{8,10},{9,11},{10,... | collective-permute-start | bytes 147464 | tf_op jit(solution)/shard_map/ppermute | solution.py:62
  13.1 1.5 %collective-permute-start.6 = (bf16[32,768]{1,0:T(8,128)(2,1)S(1)}, bf16[32,768]{1,0:T(8,128)(2,1)S(1)}, u32[]{:S(2)}, u32[]{:S(2)}) collective-permute-start(bf16[32,768]{1,0:T(8,128)(2,1)S(1)} %get-tuple-element.45.refs_0_), channel_id=1, source_target_pairs={{0,4},{1,5},{2,6},{3,7},{4,0},{5,1},{6,2},{7,3},{8,12},{9,13},{10,... | collective-permute-start | bytes 147464 | tf_op jit(solution)/shard_map/ppermute | solution.py:62
  16.0 1.7 %collective-permute-done.6.refs_2_ = bf16[32,768]{1,0:T(8,128)(2,1)S(1)} collective-permute-done((bf16[32,768]{1,0:T(8,128)(2,1)S(1)}, bf16[32,768]{1,0:T(8,128)(2,1)S(1)}, u32[]{:S(2)}, u32[]{:S(2)}) %collective-permute-start.6) | collective-permute-done | bytes 49184 | tf_op jit(solution)/shard_map/ppermute | solution.py:62
  17.7 1.9 %collective-permute-done.7.refs_3_ = bf16[32,768]{1,0:T(8,128)(2,1)S(1)} collective-permute-done((bf16[32,768]{1,0:T(8,128)(2,1)S(1)}, bf16[32,768]{1,0:T(8,128)(2,1)S(1)}, u32[]{:S(2)}, u32[]{:S(2)}) %collective-permute-start.7) | collective-permute-done | bytes 49184 | tf_op jit(solution)/shard_map/ppermute | solution.py:62
  21.1 1.6 %collective-permute-start.10 = (bf16[2,32,768]{2,1,0:T(8,128)(2,1)S(1)}, bf16[2,32,768]{2,1,0:T(8,128)(2,1)S(1)}, u32[]{:S(2)}, u32[]{:S(2)}) collective-permute-start(bf16[2,32,768]{2,1,0:T(8,128)(2,1)S(1)} %add_qkv.1.refs_0_), channel_id=1, source_target_pairs={{0,8},{1,9},{2,10},{3,11},{4,12},{5,13},{6,14},{7,15},{8,0},{9,1},... | collective-permute-start | bytes 294920 | tf_op jit(solution)/shard_map/ppermute | solution.py:62
  22.7 2.6 %collective-permute-start.11 = (bf16[2,32,768]{2,1,0:T(8,128)(2,1)S(1)}, bf16[2,32,768]{2,1,0:T(8,128)(2,1)S(1)}, u32[]{:S(2)}, u32[]{:S(2)}) collective-permute-start(bf16[2,32,768]{2,1,0:T(8,128)(2,1)S(1)} %add_qkv.1.refs_0_), channel_id=1, source_target_pairs={{0,16},{1,17},{2,18},{3,19},{4,20},{5,21},{6,22},{7,23},{8,24},{9,... | collective-permute-start | bytes 294920 | tf_op jit(solution)/shard_map/ppermute | solution.py:62
  25.5 3.2 %caches.1 = (bf16[8,64,2048]{2,1,0:T(8,128)(2,1)}, bf16[8,64,2048]{2,1,0:T(8,128)(2,1)}, bf16[8,64,2048]{2,1,0:T(8,128)(2,1)S(1)}, bf16[8,64,2048]{2,1,0:T(8,128)(2,1)S(1)}) custom-call(bf16[8,64,2048]{2,1,0:T(8,128)(2,1)S(1)} %copy-done, bf16[8,64,2048]{2,1,0:T(8,128)(2,1)} %values_in), custom_call_target="tpu_custom_call" | custom-call | bytes 16777216 | tf_op jit(solution)/shard_map/caches/pallas_call | solution.py:108
  29.6 2.7 %collective-permute-done.12.refs_3_ = bf16[2,32,768]{2,1,0:T(8,128)(2,1)S(1)} collective-permute-done((bf16[2,32,768]{2,1,0:T(8,128)(2,1)S(1)}, bf16[2,32,768]{2,1,0:T(8,128)(2,1)S(1)}, u32[]{:S(2)}, u32[]{:S(2)}) %collective-permute-start.12) | collective-permute-done | bytes 98336 | tf_op jit(solution)/shard_map/ppermute | solution.py:62
  32.2 2.4 %attention.1 = (bf16[8,64,2048]{2,1,0:T(8,128)(2,1)}, bf16[8,64,2048]{2,1,0:T(8,128)(2,1)}, bf16[32,1152]{1,0:T(8,128)(2,1)S(1)}, bf16[32,1152]{1,0:T(8,128)(2,1)S(1)}) custom-call(bf16[2,32,768]{2,1,0:T(8,128)(2,1)S(1)} %add_qkv.1.refs_0_, bf16[2,32,768]{2,1,0:T(8,128)(2,1)S(1)} %collective-permute-done.10.refs_1_, ...), custom_call_target="tpu_custom_call", output_to_operand_aliasing={{0}: (7, {}), {1}: (8, {})} | custom-call | bytes 1048576 | tf_op jit(solution)/shard_map/attention/pallas_call | solution.py:108
  34.7 1.4 %collective-permute-start.19 = (bf16[2,512,256]{2,1,0:T(8,128)(2,1)S(1)}, bf16[2,512,256]{2,1,0:T(8,128)(2,1)S(1)}, u32[]{:S(2)}, u32[]{:S(2)}) collective-permute-start(bf16[2,512,256]{2,1,0:T(8,128)(2,1)S(1)} %collective-permute-done.13.refs_0_), channel_id=1, source_target_pairs={{1,0},{3,2},{5,4},{7,6},{9,8},{11,10},{13,12},{15,14},{17,16},{19,... | collective-permute-start | bytes 1572872 | tf_op jit(solution)/shard_map/ppermute | solution.py:81
  38.2 3.7 %collective-permute-done.15.refs_1_ = bf16[32,1152]{1,0:T(8,128)(2,1)S(1)} collective-permute-done((bf16[32,1152]{1,0:T(8,128)(2,1)S(1)}, bf16[32,1152]{1,0:T(8,128)(2,1)S(1)}, u32[]{:S(2)}, u32[]{:S(2)}) %collective-permute-start.15) | collective-permute-done | bytes 73760 | tf_op jit(solution)/shard_map/ppermute | solution.py:62
  42.2 3.9 %collective-permute-start.16 = (bf16[32,1152]{1,0:T(8,128)(2,1)S(1)}, bf16[32,1152]{1,0:T(8,128)(2,1)S(1)}, u32[]{:S(2)}, u32[]{:S(2)}) collective-permute-start(bf16[32,1152]{1,0:T(8,128)(2,1)S(1)} %merge_x.1.refs_0_), channel_id=1, source_target_pairs={{0,8},{1,9},{2,10},{3,11},{4,12},{5,13},{6,14},{7,15},{8,0},{9,1},... | collective-permute-start | bytes 221192 | tf_op jit(solution)/shard_map/ppermute | solution.py:62
  46.3 2.2 %collective-permute-start.18 = (bf16[32,1152]{1,0:T(8,128)(2,1)S(1)}, bf16[32,1152]{1,0:T(8,128)(2,1)S(1)}, u32[]{:S(2)}, u32[]{:S(2)}) collective-permute-start(bf16[32,1152]{1,0:T(8,128)(2,1)S(1)} %merge_x.1.refs_0_), channel_id=1, source_target_pairs={{0,24},{1,25},{2,26},{3,27},{4,28},{5,29},{6,30},{7,31},{8,16},{9,... | collective-permute-start | bytes 221192 | tf_op jit(solution)/shard_map/ppermute | solution.py:62
  48.7 5.9 %collective-permute-done.17.refs_2_ = bf16[32,1152]{1,0:T(8,128)(2,1)S(1)} collective-permute-done((bf16[32,1152]{1,0:T(8,128)(2,1)S(1)}, bf16[32,1152]{1,0:T(8,128)(2,1)S(1)}, u32[]{:S(2)}, u32[]{:S(2)}) %collective-permute-start.17) | collective-permute-done | bytes 73760 | tf_op jit(solution)/shard_map/ppermute | solution.py:62
  56.0 2.9 %collective-permute-start.23 = (bf16[2,32,256]{2,1,0:T(8,128)(2,1)S(1)}, bf16[2,32,256]{2,1,0:T(8,128)(2,1)S(1)}, u32[]{:S(2)}, u32[]{:S(2)}) collective-permute-start(bf16[2,32,256]{2,1,0:T(8,128)(2,1)S(1)} %out.1.refs_0_), channel_id=1, source_target_pairs={{0,6},{1,7},{2,4},{3,5},{4,2},{5,3},{6,0},{7,1},{8,14},{9,15},{10,... | collective-permute-start | bytes 98312 | tf_op jit(solution)/shard_map/ppermute | solution.py:62
  61.2 1.6 %collective-permute-start.24 = (bf16[2,2,32,256]{3,2,1,0:T(8,128)(2,1)S(1)}, bf16[2,2,32,256]{3,2,1,0:T(8,128)(2,1)S(1)}, u32[]{:S(2)}, u32[]{:S(2)}) collective-permute-start(bf16[2,2,32,256]{3,2,1,0:T(8,128)(2,1)S(1)} %add_out.1.refs_2_), channel_id=1, source_target_pairs={{0,8},{1,9},{2,10},{3,11},{4,12},{5,13},{6,14},{7,15},{8,0},{9,1},... | collective-permute-start | bytes 196616 | tf_op jit(solution)/shard_map/ppermute | solution.py:62
  63.7 2.0 %collective-permute-start.26 = (bf16[2,2,32,256]{3,2,1,0:T(8,128)(2,1)S(1)}, bf16[2,2,32,256]{3,2,1,0:T(8,128)(2,1)S(1)}, u32[]{:S(2)}, u32[]{:S(2)}) collective-permute-start(bf16[2,2,32,256]{3,2,1,0:T(8,128)(2,1)S(1)} %add_out.1.refs_2_), channel_id=1, source_target_pairs={{0,24},{1,25},{2,26},{3,27},{4,28},{5,29},{6,30},{7,31},{8,16},{9,... | collective-permute-start | bytes 196616 | tf_op jit(solution)/shard_map/ppermute | solution.py:62
  66.8 1.8 %collective-permute-done.25.refs_4_ = bf16[2,2,32,256]{3,2,1,0:T(8,128)(2,1)S(1)} collective-permute-done((bf16[2,2,32,256]{3,2,1,0:T(8,128)(2,1)S(1)}, bf16[2,2,32,256]{3,2,1,0:T(8,128)(2,1)S(1)}, u32[]{:S(2)}, u32[]{:S(2)}) %collective-permute-start.25) | collective-permute-done | bytes 65568 | tf_op jit(solution)/shard_map/ppermute | solution.py:62
  70.7 1.8 %collective-permute-start.27 = (bf16[64,1024]{1,0:T(8,128)(2,1)S(1)}, bf16[64,1024]{1,0:T(8,128)(2,1)S(1)}, u32[]{:S(2)}, u32[]{:S(2)}) collective-permute-start(bf16[64,1024]{1,0:T(8,128)(2,1)S(1)} %get-tuple-element.66.refs_0_), channel_id=1, source_target_pairs={{0,2},{1,3},{2,0},{3,1},{4,6},{5,7},{6,4},{7,5},{8,10},{9,11},{10,... | collective-permute-start | bytes 393224 | tf_op jit(solution)/shard_map/ppermute | solution.py:62
  72.5 3.3 %collective-permute-done.27.refs_1_ = bf16[64,1024]{1,0:T(8,128)(2,1)S(1)} collective-permute-done((bf16[64,1024]{1,0:T(8,128)(2,1)S(1)}, bf16[64,1024]{1,0:T(8,128)(2,1)S(1)}, u32[]{:S(2)}, u32[]{:S(2)}) %collective-permute-start.27) | collective-permute-done | bytes 131104 | tf_op jit(solution)/shard_map/ppermute | solution.py:62
  76.3 1.6 %collective-permute-start.28 = (bf16[64,512]{1,0:T(8,128)(2,1)S(1)}, bf16[64,512]{1,0:T(8,128)(2,1)S(1)}, u32[]{:S(2)}, u32[]{:S(2)}) collective-permute-start(bf16[64,512]{1,0:T(8,128)(2,1)S(1)} %get-tuple-element.69), channel_id=1, source_target_pairs={{0,4},{1,5},{2,6},{3,7},{4,0},{5,1},{6,2},{7,3},{8,12},{9,13},{10,... | collective-permute-start | bytes 196616 | tf_op jit(solution)/shard_map/ppermute | solution.py:62
  77.9 2.7 %collective-permute-done.28.refs_1_ = bf16[64,512]{1,0:T(8,128)(2,1)S(1)} collective-permute-done((bf16[64,512]{1,0:T(8,128)(2,1)S(1)}, bf16[64,512]{1,0:T(8,128)(2,1)S(1)}, u32[]{:S(2)}, u32[]{:S(2)}) %collective-permute-start.28) | collective-permute-done | bytes 65568 | tf_op jit(solution)/shard_map/ppermute | solution.py:62
  81.4 1.8 %collective-permute-start.30 = (bf16[64,512]{1,0:T(8,128)(2,1)S(1)}, bf16[64,512]{1,0:T(8,128)(2,1)S(1)}, u32[]{:S(2)}, u32[]{:S(2)}) collective-permute-start(bf16[64,512]{1,0:T(8,128)(2,1)S(1)} %add_x.1.refs_0_), channel_id=1, source_target_pairs={{0,16},{1,17},{2,18},{3,19},{4,20},{5,21},{6,22},{7,23},{8,24},{9,... | collective-permute-start | bytes 196616 | tf_op jit(solution)/shard_map/ppermute | solution.py:62
  83.2 1.9 %collective-permute-start.31 = (bf16[64,512]{1,0:T(8,128)(2,1)S(1)}, bf16[64,512]{1,0:T(8,128)(2,1)S(1)}, u32[]{:S(2)}, u32[]{:S(2)}) collective-permute-start(bf16[64,512]{1,0:T(8,128)(2,1)S(1)} %add_x.1.refs_0_), channel_id=1, source_target_pairs={{0,24},{1,25},{2,26},{3,27},{4,28},{5,29},{6,30},{7,31},{8,16},{9,... | collective-permute-start | bytes 196616 | tf_op jit(solution)/shard_map/ppermute | solution.py:62
  85.1 1.5 %collective-permute-done.30.refs_2_ = bf16[64,512]{1,0:T(8,128)(2,1)S(1)} collective-permute-done((bf16[64,512]{1,0:T(8,128)(2,1)S(1)}, bf16[64,512]{1,0:T(8,128)(2,1)S(1)}, u32[]{:S(2)}, u32[]{:S(2)}) %collective-permute-start.30) | collective-permute-done | bytes 65568 | tf_op jit(solution)/shard_map/ppermute | solution.py:62
  86.6 2.7 %collective-permute-done.31.refs_3_ = bf16[64,512]{1,0:T(8,128)(2,1)S(1)} collective-permute-done((bf16[64,512]{1,0:T(8,128)(2,1)S(1)}, bf16[64,512]{1,0:T(8,128)(2,1)S(1)}, u32[]{:S(2)}, u32[]{:S(2)}) %collective-permute-start.31) | collective-permute-done | bytes 65568 | tf_op jit(solution)/shard_map/ppermute | solution.py:62
  89.3 1.7 %collective-permute-start.32 = (bf16[32,512]{1,0:T(8,128)(2,1)S(1)}, bf16[32,512]{1,0:T(8,128)(2,1)S(1)}, u32[]{:S(2)}, u32[]{:S(2)}) collective-permute-start(bf16[32,512]{1,0:T(8,128)(2,1)S(1)} %get-tuple-element.71), channel_id=1, source_target_pairs={{0,2},{1,3},{2,0},{3,1},{4,6},{5,7},{6,4},{7,5},{8,10},{9,11},{10,... | collective-permute-start | bytes 98312 | tf_op jit(solution)/shard_map/ppermute | solution.py:62
  91.0 1.5 %collective-permute-start.33 = (bf16[32,512]{1,0:T(8,128)(2,1)S(1)}, bf16[32,512]{1,0:T(8,128)(2,1)S(1)}, u32[]{:S(2)}, u32[]{:S(2)}) collective-permute-start(bf16[32,512]{1,0:T(8,128)(2,1)S(1)} %get-tuple-element.70.refs_0_), channel_id=1, source_target_pairs={{0,4},{1,5},{2,6},{3,7},{4,0},{5,1},{6,2},{7,3},{8,12},{9,13},{10,... | collective-permute-start | bytes 98312 | tf_op jit(solution)/shard_map/ppermute | solution.py:62
  93.3 1.7 %collective-permute-done.33.refs_2_ = bf16[32,512]{1,0:T(8,128)(2,1)S(1)} collective-permute-done((bf16[32,512]{1,0:T(8,128)(2,1)S(1)}, bf16[32,512]{1,0:T(8,128)(2,1)S(1)}, u32[]{:S(2)}, u32[]{:S(2)}) %collective-permute-start.33) | collective-permute-done | bytes 32800 | tf_op jit(solution)/shard_map/ppermute | solution.py:62
  94.9 2.4 %collective-permute-done.34.refs_3_ = bf16[32,512]{1,0:T(8,128)(2,1)S(1)} collective-permute-done((bf16[32,512]{1,0:T(8,128)(2,1)S(1)}, bf16[32,512]{1,0:T(8,128)(2,1)S(1)}, u32[]{:S(2)}, u32[]{:S(2)}) %collective-permute-start.34) | collective-permute-done | bytes 32800 | tf_op jit(solution)/shard_map/ppermute | solution.py:62
  (80 shorter events, 23.0 us)
Async XLA Ops:
  0.7 9.5 %collective-permute-start.1 = (bf16[512,256]{1,0:T(8,128)(2,1)}, bf16[512,256]{1,0:T(8,128)(2,1)S(1)}, u32[]{:S(2)}, u32[]{:S(2)}) collective-permute-start(bf16[512,256]{1,0:T(8,128)(2,1)} %refs_0_.2), channel_id=1, source_target_pairs={{0,1},{1,0},{2,3},{3,2},{4,5},{5,4},{6,7},{7,6},{8,9},{9,8},{10,11... | collective-permute-start | bytes 786440 | tf_op jit(solution)/shard_map/ppermute | solution.py:62
  1.2 9.0 %collective-permute-start.2 = (bf16[512,256]{1,0:T(8,128)(2,1)}, bf16[512,256]{1,0:T(8,128)(2,1)S(1)}, u32[]{:S(2)}, u32[]{:S(2)}) collective-permute-start(bf16[512,256]{1,0:T(8,128)(2,1)} %refs_1_.1), channel_id=1, source_target_pairs={{0,1},{1,0},{2,3},{3,2},{4,5},{5,4},{6,7},{7,6},{8,9},{9,8},{10,11... | collective-permute-start | bytes 786440 | tf_op jit(solution)/shard_map/ppermute | solution.py:62
  1.3 9.0 %collective-permute-start.3 = (bf16[512,256]{1,0:T(8,128)(2,1)}, bf16[512,256]{1,0:T(8,128)(2,1)S(1)}, u32[]{:S(2)}, u32[]{:S(2)}) collective-permute-start(bf16[512,256]{1,0:T(8,128)(2,1)} %refs_2_.2), channel_id=1, source_target_pairs={{0,1},{1,0},{2,3},{3,2},{4,5},{5,4},{6,7},{7,6},{8,9},{9,8},{10,11... | collective-permute-start | bytes 786440 | tf_op jit(solution)/shard_map/ppermute | solution.py:62
  1.7 9.2 %collective-permute-start.4 = (bf16[512,256]{1,0:T(8,128)(2,1)}, bf16[512,256]{1,0:T(8,128)(2,1)S(1)}, u32[]{:S(2)}, u32[]{:S(2)}) collective-permute-start(bf16[512,256]{1,0:T(8,128)(2,1)} %own.1), channel_id=1, source_target_pairs={{0,1},{2,3},{4,5},{6,7},{8,9},{10,11},{12,13},{14,15},{16,17},{18,... | collective-permute-start | bytes 786440 | tf_op jit(solution)/shard_map/ppermute | solution.py:81
  3.8 6.4 %collective-permute-start = (bf16[8,4,2048]{2,1,0:T(4,128)(2,1)}, bf16[8,4,2048]{2,1,0:T(4,128)(2,1)S(1)}, u32[]{:S(2)}, u32[]{:S(2)}) collective-permute-start(bf16[8,4,2048]{2,1,0:T(4,128)(2,1)} %refs_0_.3), channel_id=1, source_target_pairs={{0,2},{1,3},{2,0},{3,1},{4,6},{5,7},{6,4},{7,5},{8,10},{9,11},{10,... | collective-permute-start | bytes 393224 | tf_op jit(solution)/shard_map/ppermute | solution.py:62
  10.9 8.8 %collective-permute-start.8 = (bf16[512,1024]{1,0:T(8,128)(2,1)S(1)}, bf16[512,1024]{1,0:T(8,128)(2,1)S(1)}, u32[]{:S(2)}, u32[]{:S(2)}) collective-permute-start(bf16[512,1024]{1,0:T(8,128)(2,1)S(1)} %copy-done.1), channel_id=1, source_target_pairs={{0,1},{1,0},{2,3},{3,2},{4,5},{5,4},{6,7},{7,6},{8,9},{9,8},{10,11... | collective-permute-start | bytes 3145736 | tf_op jit(solution)/shard_map/ppermute | solution.py:62
  11.0 8.7 %collective-permute-start.9 = (bf16[1024,512]{1,0:T(8,128)(2,1)}, bf16[1024,512]{1,0:T(8,128)(2,1)S(1)}, u32[]{:S(2)}, u32[]{:S(2)}) collective-permute-start(bf16[1024,512]{1,0:T(8,128)(2,1)} %refs_2_.3), channel_id=1, source_target_pairs={{0,1},{1,0},{2,3},{3,2},{4,5},{5,4},{6,7},{7,6},{8,9},{9,8},{10,11... | collective-permute-start | bytes 3145736 | tf_op jit(solution)/shard_map/ppermute | solution.py:62
  11.4 4.5 %collective-permute-start.5 = (bf16[32,768]{1,0:T(8,128)(2,1)S(1)}, bf16[32,768]{1,0:T(8,128)(2,1)S(1)}, u32[]{:S(2)}, u32[]{:S(2)}) collective-permute-start(bf16[32,768]{1,0:T(8,128)(2,1)S(1)} %get-tuple-element.46), channel_id=1, source_target_pairs={{0,2},{1,3},{2,0},{3,1},{4,6},{5,7},{6,4},{7,5},{8,10},{9,11},{10,... | collective-permute-start | bytes 147464 | tf_op jit(solution)/shard_map/ppermute | solution.py:62
  13.1 4.6 %collective-permute-start.6 = (bf16[32,768]{1,0:T(8,128)(2,1)S(1)}, bf16[32,768]{1,0:T(8,128)(2,1)S(1)}, u32[]{:S(2)}, u32[]{:S(2)}) collective-permute-start(bf16[32,768]{1,0:T(8,128)(2,1)S(1)} %get-tuple-element.45.refs_0_), channel_id=1, source_target_pairs={{0,4},{1,5},{2,6},{3,7},{4,0},{5,1},{6,2},{7,3},{8,12},{9,13},{10,... | collective-permute-start | bytes 147464 | tf_op jit(solution)/shard_map/ppermute | solution.py:62
  14.6 5.0 %collective-permute-start.7 = (bf16[32,768]{1,0:T(8,128)(2,1)S(1)}, bf16[32,768]{1,0:T(8,128)(2,1)S(1)}, u32[]{:S(2)}, u32[]{:S(2)}) collective-permute-start(bf16[32,768]{1,0:T(8,128)(2,1)S(1)} %get-tuple-element.46), channel_id=1, source_target_pairs={{0,6},{1,7},{2,4},{3,5},{4,2},{5,3},{6,0},{7,1},{8,14},{9,15},{10,... | collective-permute-start | bytes 147464 | tf_op jit(solution)/shard_map/ppermute | solution.py:62
  19.7 15.1 %collective-permute-start.13 = (bf16[2,512,256]{2,1,0:T(8,128)(2,1)S(1)}, bf16[2,512,256]{2,1,0:T(8,128)(2,1)S(1)}, u32[]{:S(2)}, u32[]{:S(2)}) collective-permute-start(bf16[2,512,256]{2,1,0:T(8,128)(2,1)S(1)} %pack.1), channel_id=1, source_target_pairs={{1,1},{3,5},{5,3},{7,7},{9,9},{11,13},{13,11},{15,15},{17,17},{19,... | collective-permute-start | bytes 1572872 | tf_op jit(solution)/shard_map/ppermute | solution.py:76
  20.4 14.4 %collective-permute-start.14 = (bf16[2,512,256]{2,1,0:T(8,128)(2,1)S(1)}, bf16[2,512,256]{2,1,0:T(8,128)(2,1)S(1)}, u32[]{:S(2)}, u32[]{:S(2)}) collective-permute-start(bf16[2,512,256]{2,1,0:T(8,128)(2,1)S(1)} %pack.1), channel_id=1, source_target_pairs={{1,3},{3,7},{5,1},{7,5},{9,11},{11,15},{13,9},{15,13},{17,19},{19,... | collective-permute-start | bytes 1572872 | tf_op jit(solution)/shard_map/ppermute | solution.py:76
  21.1 7.6 %collective-permute-start.10 = (bf16[2,32,768]{2,1,0:T(8,128)(2,1)S(1)}, bf16[2,32,768]{2,1,0:T(8,128)(2,1)S(1)}, u32[]{:S(2)}, u32[]{:S(2)}) collective-permute-start(bf16[2,32,768]{2,1,0:T(8,128)(2,1)S(1)} %add_qkv.1.refs_0_), channel_id=1, source_target_pairs={{0,8},{1,9},{2,10},{3,11},{4,12},{5,13},{6,14},{7,15},{8,0},{9,1},... | collective-permute-start | bytes 294920 | tf_op jit(solution)/shard_map/ppermute | solution.py:62
  22.7 6.9 %collective-permute-start.11 = (bf16[2,32,768]{2,1,0:T(8,128)(2,1)S(1)}, bf16[2,32,768]{2,1,0:T(8,128)(2,1)S(1)}, u32[]{:S(2)}, u32[]{:S(2)}) collective-permute-start(bf16[2,32,768]{2,1,0:T(8,128)(2,1)S(1)} %add_qkv.1.refs_0_), channel_id=1, source_target_pairs={{0,16},{1,17},{2,18},{3,19},{4,20},{5,21},{6,22},{7,23},{8,24},{9,... | collective-permute-start | bytes 294920 | tf_op jit(solution)/shard_map/ppermute | solution.py:62
  25.3 6.9 %collective-permute-start.12 = (bf16[2,32,768]{2,1,0:T(8,128)(2,1)S(1)}, bf16[2,32,768]{2,1,0:T(8,128)(2,1)S(1)}, u32[]{:S(2)}, u32[]{:S(2)}) collective-permute-start(bf16[2,32,768]{2,1,0:T(8,128)(2,1)S(1)} %add_qkv.1.refs_0_), channel_id=1, source_target_pairs={{0,24},{1,25},{2,26},{3,27},{4,28},{5,29},{6,30},{7,31},{8,16},{9,... | collective-permute-start | bytes 294920 | tf_op jit(solution)/shard_map/ppermute | solution.py:62
  34.7 20.2 %collective-permute-start.19 = (bf16[2,512,256]{2,1,0:T(8,128)(2,1)S(1)}, bf16[2,512,256]{2,1,0:T(8,128)(2,1)S(1)}, u32[]{:S(2)}, u32[]{:S(2)}) collective-permute-start(bf16[2,512,256]{2,1,0:T(8,128)(2,1)S(1)} %collective-permute-done.13.refs_0_), channel_id=1, source_target_pairs={{1,0},{3,2},{5,4},{7,6},{9,8},{11,10},{13,12},{15,14},{17,16},{19,... | collective-permute-start | bytes 1572872 | tf_op jit(solution)/shard_map/ppermute | solution.py:81
  36.2 18.8 %collective-permute-start.20 = (bf16[2,512,256]{2,1,0:T(8,128)(2,1)S(1)}, bf16[2,512,256]{2,1,0:T(8,128)(2,1)S(1)}, u32[]{:S(2)}, u32[]{:S(2)}) collective-permute-start(bf16[2,512,256]{2,1,0:T(8,128)(2,1)S(1)} %collective-permute-done.14.refs_2_), channel_id=1, source_target_pairs={{1,0},{3,2},{5,4},{7,6},{9,8},{11,10},{13,12},{15,14},{17,16},{19,... | collective-permute-start | bytes 1572872 | tf_op jit(solution)/shard_map/ppermute | solution.py:81
  37.5 4.4 %collective-permute-start.15 = (bf16[32,1152]{1,0:T(8,128)(2,1)S(1)}, bf16[32,1152]{1,0:T(8,128)(2,1)S(1)}, u32[]{:S(2)}, u32[]{:S(2)}) collective-permute-start(bf16[32,1152]{1,0:T(8,128)(2,1)S(1)} %get-tuple-element.62), channel_id=1, source_target_pairs={{0,4},{1,5},{2,6},{3,7},{4,0},{5,1},{6,2},{7,3},{8,12},{9,13},{10,... | collective-permute-start | bytes 221192 | tf_op jit(solution)/shard_map/ppermute | solution.py:62
  42.2 6.5 %collective-permute-start.16 = (bf16[32,1152]{1,0:T(8,128)(2,1)S(1)}, bf16[32,1152]{1,0:T(8,128)(2,1)S(1)}, u32[]{:S(2)}, u32[]{:S(2)}) collective-permute-start(bf16[32,1152]{1,0:T(8,128)(2,1)S(1)} %merge_x.1.refs_0_), channel_id=1, source_target_pairs={{0,8},{1,9},{2,10},{3,11},{4,12},{5,13},{6,14},{7,15},{8,0},{9,1},... | collective-permute-start | bytes 221192 | tf_op jit(solution)/shard_map/ppermute | solution.py:62
  46.1 8.5 %collective-permute-start.17 = (bf16[32,1152]{1,0:T(8,128)(2,1)S(1)}, bf16[32,1152]{1,0:T(8,128)(2,1)S(1)}, u32[]{:S(2)}, u32[]{:S(2)}) collective-permute-start(bf16[32,1152]{1,0:T(8,128)(2,1)S(1)} %merge_x.1.refs_0_), channel_id=1, source_target_pairs={{0,16},{1,17},{2,18},{3,19},{4,20},{5,21},{6,22},{7,23},{8,24},{9,... | collective-permute-start | bytes 221192 | tf_op jit(solution)/shard_map/ppermute | solution.py:62
  46.3 8.3 %collective-permute-start.18 = (bf16[32,1152]{1,0:T(8,128)(2,1)S(1)}, bf16[32,1152]{1,0:T(8,128)(2,1)S(1)}, u32[]{:S(2)}, u32[]{:S(2)}) collective-permute-start(bf16[32,1152]{1,0:T(8,128)(2,1)S(1)} %merge_x.1.refs_0_), channel_id=1, source_target_pairs={{0,24},{1,25},{2,26},{3,27},{4,28},{5,29},{6,30},{7,31},{8,16},{9,... | collective-permute-start | bytes 221192 | tf_op jit(solution)/shard_map/ppermute | solution.py:62
  55.4 4.0 %collective-permute-start.21 = (bf16[2,32,256]{2,1,0:T(8,128)(2,1)S(1)}, bf16[2,32,256]{2,1,0:T(8,128)(2,1)S(1)}, u32[]{:S(2)}, u32[]{:S(2)}) collective-permute-start(bf16[2,32,256]{2,1,0:T(8,128)(2,1)S(1)} %out.1.refs_0_), channel_id=1, source_target_pairs={{0,2},{1,3},{2,0},{3,1},{4,6},{5,7},{6,4},{7,5},{8,10},{9,11},{10,... | collective-permute-start | bytes 98312 | tf_op jit(solution)/shard_map/ppermute | solution.py:62
  56.0 5.1 %collective-permute-start.23 = (bf16[2,32,256]{2,1,0:T(8,128)(2,1)S(1)}, bf16[2,32,256]{2,1,0:T(8,128)(2,1)S(1)}, u32[]{:S(2)}, u32[]{:S(2)}) collective-permute-start(bf16[2,32,256]{2,1,0:T(8,128)(2,1)S(1)} %out.1.refs_0_), channel_id=1, source_target_pairs={{0,6},{1,7},{2,4},{3,5},{4,2},{5,3},{6,0},{7,1},{8,14},{9,15},{10,... | collective-permute-start | bytes 98312 | tf_op jit(solution)/shard_map/ppermute | solution.py:62
  61.2 5.6 %collective-permute-start.24 = (bf16[2,2,32,256]{3,2,1,0:T(8,128)(2,1)S(1)}, bf16[2,2,32,256]{3,2,1,0:T(8,128)(2,1)S(1)}, u32[]{:S(2)}, u32[]{:S(2)}) collective-permute-start(bf16[2,2,32,256]{3,2,1,0:T(8,128)(2,1)S(1)} %add_out.1.refs_2_), channel_id=1, source_target_pairs={{0,8},{1,9},{2,10},{3,11},{4,12},{5,13},{6,14},{7,15},{8,0},{9,1},... | collective-permute-start | bytes 196616 | tf_op jit(solution)/shard_map/ppermute | solution.py:62
  62.8 5.8 %collective-permute-start.25 = (bf16[2,2,32,256]{3,2,1,0:T(8,128)(2,1)S(1)}, bf16[2,2,32,256]{3,2,1,0:T(8,128)(2,1)S(1)}, u32[]{:S(2)}, u32[]{:S(2)}) collective-permute-start(bf16[2,2,32,256]{3,2,1,0:T(8,128)(2,1)S(1)} %add_out.1.refs_2_), channel_id=1, source_target_pairs={{0,16},{1,17},{2,18},{3,19},{4,20},{5,21},{6,22},{7,23},{8,24},{9,... | collective-permute-start | bytes 196616 | tf_op jit(solution)/shard_map/ppermute | solution.py:62
  63.7 6.2 %collective-permute-start.26 = (bf16[2,2,32,256]{3,2,1,0:T(8,128)(2,1)S(1)}, bf16[2,2,32,256]{3,2,1,0:T(8,128)(2,1)S(1)}, u32[]{:S(2)}, u32[]{:S(2)}) collective-permute-start(bf16[2,2,32,256]{3,2,1,0:T(8,128)(2,1)S(1)} %add_out.1.refs_2_), channel_id=1, source_target_pairs={{0,24},{1,25},{2,26},{3,27},{4,28},{5,29},{6,30},{7,31},{8,16},{9,... | collective-permute-start | bytes 196616 | tf_op jit(solution)/shard_map/ppermute | solution.py:62
  70.7 5.0 %collective-permute-start.27 = (bf16[64,1024]{1,0:T(8,128)(2,1)S(1)}, bf16[64,1024]{1,0:T(8,128)(2,1)S(1)}, u32[]{:S(2)}, u32[]{:S(2)}) collective-permute-start(bf16[64,1024]{1,0:T(8,128)(2,1)S(1)} %get-tuple-element.66.refs_0_), channel_id=1, source_target_pairs={{0,2},{1,3},{2,0},{3,1},{4,6},{5,7},{6,4},{7,5},{8,10},{9,11},{10,... | collective-permute-start | bytes 393224 | tf_op jit(solution)/shard_map/ppermute | solution.py:62
  76.3 4.3 %collective-permute-start.28 = (bf16[64,512]{1,0:T(8,128)(2,1)S(1)}, bf16[64,512]{1,0:T(8,128)(2,1)S(1)}, u32[]{:S(2)}, u32[]{:S(2)}) collective-permute-start(bf16[64,512]{1,0:T(8,128)(2,1)S(1)} %get-tuple-element.69), channel_id=1, source_target_pairs={{0,4},{1,5},{2,6},{3,7},{4,0},{5,1},{6,2},{7,3},{8,12},{9,13},{10,... | collective-permute-start | bytes 196616 | tf_op jit(solution)/shard_map/ppermute | solution.py:62
  80.6 4.5 %collective-permute-start.29 = (bf16[64,512]{1,0:T(8,128)(2,1)S(1)}, bf16[64,512]{1,0:T(8,128)(2,1)S(1)}, u32[]{:S(2)}, u32[]{:S(2)}) collective-permute-start(bf16[64,512]{1,0:T(8,128)(2,1)S(1)} %add_x.1.refs_0_), channel_id=1, source_target_pairs={{0,8},{1,9},{2,10},{3,11},{4,12},{5,13},{6,14},{7,15},{8,0},{9,1},... | collective-permute-start | bytes 196616 | tf_op jit(solution)/shard_map/ppermute | solution.py:62
  81.4 5.2 %collective-permute-start.30 = (bf16[64,512]{1,0:T(8,128)(2,1)S(1)}, bf16[64,512]{1,0:T(8,128)(2,1)S(1)}, u32[]{:S(2)}, u32[]{:S(2)}) collective-permute-start(bf16[64,512]{1,0:T(8,128)(2,1)S(1)} %add_x.1.refs_0_), channel_id=1, source_target_pairs={{0,16},{1,17},{2,18},{3,19},{4,20},{5,21},{6,22},{7,23},{8,24},{9,... | collective-permute-start | bytes 196616 | tf_op jit(solution)/shard_map/ppermute | solution.py:62
  83.2 6.1 %collective-permute-start.31 = (bf16[64,512]{1,0:T(8,128)(2,1)S(1)}, bf16[64,512]{1,0:T(8,128)(2,1)S(1)}, u32[]{:S(2)}, u32[]{:S(2)}) collective-permute-start(bf16[64,512]{1,0:T(8,128)(2,1)S(1)} %add_x.1.refs_0_), channel_id=1, source_target_pairs={{0,24},{1,25},{2,26},{3,27},{4,28},{5,29},{6,30},{7,31},{8,16},{9,... | collective-permute-start | bytes 196616 | tf_op jit(solution)/shard_map/ppermute | solution.py:62
  92.5 4.8 %collective-permute-start.34 = (bf16[32,512]{1,0:T(8,128)(2,1)S(1)}, bf16[32,512]{1,0:T(8,128)(2,1)S(1)}, u32[]{:S(2)}, u32[]{:S(2)}) collective-permute-start(bf16[32,512]{1,0:T(8,128)(2,1)S(1)} %get-tuple-element.71), channel_id=1, source_target_pairs={{0,6},{1,7},{2,4},{3,5},{4,2},{5,3},{6,0},{7,1},{8,14},{9,15},{10,... | collective-permute-start | bytes 98312 | tf_op jit(solution)/shard_map/ppermute | solution.py:62
  (15 other events, 273.0 us)

commit v10 on v7

--- a/solution.py
+++ b/solution.py
@@ -570,6 +570,10 @@
     )
     pieces = place.gather_z(qkv)
     blocks = [place.transpose(tied, k) for k in range(nx)]
+    pieces, blocks = lax.optimization_barrier((pieces, blocks))
+    w_outs = []
+    for block in blocks:
+        w_outs += [block, place.move(block, dc=1)]
     pack = max(1, min(group, 256 // slots))
     window = min(32, slots)
     new_keys, new_values, *messages = call(
@@ -591,16 +595,13 @@
             pltpu.SemaphoreType.DMA((2, group)),
         ],
         aliases={place.nz + 3: 0, place.nz + 4: 1},
-    )
-    messages, blocks = lax.optimization_barrier((messages, blocks))
-    w_outs = []
-    for block in blocks:
-        w_outs += [block, place.move(block, dc=1)]
+        moved=16 * 1024 * 1024,
+    )
+    messages, w_outs = lax.optimization_barrier((messages, w_outs))
     messages = [messages[0]] + [place.move(messages[dx], dx=dx) for dx in range(1, nx)]
     merged = call(
         bind(merge_x_kernel, place, heads), "merge_x", messages, shape((rows, share + LANES))
     )
-    merged, *w_outs = lax.optimization_barrier((merged, *w_outs))
     pieces = place.gather_z(merged)
     attn = call(bind(merge_z_kernel, place, heads), "merge_z", pieces, shape((rows, share)))
     out_part = call(

time: 89.9 us -> 89.8 us (level)
  starting transfers between devices: 39.8 us -> 40.7 us
  transfers between devices with their start and end apart: 34 -> 34, of which waited for: 20 -> 19; matrix products, arithmetic and copies ran while one was open for 2% -> 2% of each run, Pallas kernels for 8% -> 7%
where the time goes in v10:
time: 89.8 us
  starting transfers between devices  40.7 us (45%)
  waiting for transfers between devices  35.4 us (39%)
  Pallas kernels  10.4 us (12%)
  other arithmetic  1.44 us (2%)
  local copies, waits for them, and re-layouts  0.97 us (1%)
  between operations  0.92 us (1%)
    ppermute x32, starting transfers between devices, move(): return lax.ppermute(value, ('seq', 'req'), pairs)  38.8 us
    ppermute x32, waiting for transfers between devices, move(): return lax.ppermute(value, ('seq', 'req'), pairs)  35.4 us
    pallas_call x14, Pallas kernels, call(): pl.pallas_call(kernel, name=name, out_shape=outs, in_specs=in_specs or [V...  10.4 us
    ppermute x2, starting transfers between devices, transpose(): return lax.ppermute(value, ('seq', 'req'), pairs)  1.85 us
  transfers between devices with their start and end apart: 34, of which 19 were waited for; matrix products, arithmetic and copies ran while one was open for 2% of the time, Pallas kernels for 7%

profile of v10, /device:TPU:0, one launch (start us, length us, event | category | flops | bytes accessed | tf_op | source)
XLA Modules:
  0.0 89.8 jit_solution(7208315537610574567)
XLA Ops:
  1.7 2.6 %collective-permute-start = (bf16[8,4,2048]{2,1,0:T(4,128)(2,1)}, bf16[8,4,2048]{2,1,0:T(4,128)(2,1)S(1)}, u32[]{:S(2)}, u32[]{:S(2)}) collective-permute-start(bf16[8,4,2048]{2,1,0:T(4,128)(2,1)} %refs_0_.3), channel_id=1, source_target_pairs={{0,2},{1,3},{2,0},{3,1},{4,6},{5,7},{6,4},{7,5},{8,10},{9,11},{10,... | collective-permute-start | bytes 393224 | tf_op jit(solution)/shard_map/ppermute | solution.py:62
  9.8 1.7 %collective-permute-start.5 = (bf16[32,768]{1,0:T(8,128)(2,1)S(1)}, bf16[32,768]{1,0:T(8,128)(2,1)S(1)}, u32[]{:S(2)}, u32[]{:S(2)}) collective-permute-start(bf16[32,768]{1,0:T(8,128)(2,1)S(1)} %get-tuple-element.56.refs_0_), channel_id=1, source_target_pairs={{0,4},{1,5},{2,6},{3,7},{4,0},{5,1},{6,2},{7,3},{8,12},{9,13},{10,... | collective-permute-start | bytes 147464 | tf_op jit(solution)/shard_map/ppermute | solution.py:62
  11.5 1.5 %collective-permute-start.6 = (bf16[32,768]{1,0:T(8,128)(2,1)S(1)}, bf16[32,768]{1,0:T(8,128)(2,1)S(1)}, u32[]{:S(2)}, u32[]{:S(2)}) collective-permute-start(bf16[32,768]{1,0:T(8,128)(2,1)S(1)} %get-tuple-element.57), channel_id=1, source_target_pairs={{0,6},{1,7},{2,4},{3,5},{4,2},{5,3},{6,0},{7,1},{8,14},{9,15},{10,... | collective-permute-start | bytes 147464 | tf_op jit(solution)/shard_map/ppermute | solution.py:62
  13.3 3.2 %caches.1 = (bf16[8,64,2048]{2,1,0:T(8,128)(2,1)}, bf16[8,64,2048]{2,1,0:T(8,128)(2,1)}, bf16[8,64,2048]{2,1,0:T(8,128)(2,1)S(1)}, bf16[8,64,2048]{2,1,0:T(8,128)(2,1)S(1)}, f32[8,128]{1,0:T(8,128)S(1)}) custom-call(bf16[8,64,2048]{2,1,0:T(8,128)(2,1)S(1)} %copy-done, bf16[8,64,2048]{2,1,0:T(8,128)(2,1)} %values_in), custom_call_target="tpu_custom_call" | custom-call | bytes 16777216 | tf_op jit(solution)/shard_map/caches/pallas_call | solution.py:104
  17.2 1.2 %collective-permute-start.13 = (bf16[512,256]{1,0:T(8,128)(2,1)S(1)}, bf16[512,256]{1,0:T(8,128)(2,1)S(1)}, u32[]{:S(2)}, u32[]{:S(2)}) collective-permute-start(bf16[512,256]{1,0:T(8,128)(2,1)S(1)} %copy-done.11), channel_id=1, source_target_pairs={{0,2},{1,3},{2,6},{3,7},{4,0},{5,1},{6,4},{7,5},{8,10},{9,11},{10,... | collective-permute-start | bytes 786440 | tf_op jit(solution)/shard_map/ppermute | solution.py:77
  19.0 3.7 %collective-permute-start.11 = (bf16[2,32,768]{2,1,0:T(8,128)(2,1)S(1)}, bf16[2,32,768]{2,1,0:T(8,128)(2,1)S(1)}, u32[]{:S(2)}, u32[]{:S(2)}) collective-permute-start(bf16[2,32,768]{2,1,0:T(8,128)(2,1)S(1)} %add_qkv.1.refs_0_), channel_id=1, source_target_pairs={{0,24},{1,25},{2,26},{3,27},{4,28},{5,29},{6,30},{7,31},{8,16},{9,... | collective-permute-start | bytes 294920 | tf_op jit(solution)/shard_map/ppermute | solution.py:62
  23.5 2.6 %collective-permute-done.11.refs_3_ = bf16[2,32,768]{2,1,0:T(8,128)(2,1)S(1)} collective-permute-done((bf16[2,32,768]{2,1,0:T(8,128)(2,1)S(1)}, bf16[2,32,768]{2,1,0:T(8,128)(2,1)S(1)}, u32[]{:S(2)}, u32[]{:S(2)}) %collective-permute-start.11) | collective-permute-done | bytes 98336 | tf_op jit(solution)/shard_map/ppermute | solution.py:62
  26.1 4.0 %collective-permute-done.10.refs_2_ = bf16[2,32,768]{2,1,0:T(8,128)(2,1)S(1)} collective-permute-done((bf16[2,32,768]{2,1,0:T(8,128)(2,1)S(1)}, bf16[2,32,768]{2,1,0:T(8,128)(2,1)S(1)}, u32[]{:S(2)}, u32[]{:S(2)}) %collective-permute-start.10) | collective-permute-done | bytes 98336 | tf_op jit(solution)/shard_map/ppermute | solution.py:62
  30.7 2.3 %attention.1 = (bf16[8,64,2048]{2,1,0:T(8,128)(2,1)}, bf16[8,64,2048]{2,1,0:T(8,128)(2,1)}, bf16[32,1152]{1,0:T(8,128)(2,1)S(1)}, bf16[32,1152]{1,0:T(8,128)(2,1)S(1)}) custom-call(bf16[2,32,768]{2,1,0:T(8,128)(2,1)S(1)} %add_qkv.1.refs_0_, bf16[2,32,768]{2,1,0:T(8,128)(2,1)S(1)} %collective-permute-done.9.refs_1_, ...), custom_call_target="tpu_custom_call", output_to_operand_aliasing={{0}: (7, {}), {1}: (8, {})} | custom-call | bytes 16777216 | tf_op jit(solution)/shard_map/attention/pallas_call | solution.py:104
  33.1 4.2 %collective-permute-start.16 = (bf16[32,1152]{1,0:T(8,128)(2,1)S(1)}, bf16[32,1152]{1,0:T(8,128)(2,1)S(1)}, u32[]{:S(2)}, u32[]{:S(2)}) collective-permute-start(bf16[32,1152]{1,0:T(8,128)(2,1)S(1)} %get-tuple-element.78), channel_id=1, source_target_pairs={{0,4},{1,5},{2,6},{3,7},{4,0},{5,1},{6,2},{7,3},{8,12},{9,13},{10,... | collective-permute-start | bytes 221192 | tf_op jit(solution)/shard_map/ppermute | solution.py:62
  37.3 2.5 %collective-permute-done.16.refs_1_ = bf16[32,1152]{1,0:T(8,128)(2,1)S(1)} collective-permute-done((bf16[32,1152]{1,0:T(8,128)(2,1)S(1)}, bf16[32,1152]{1,0:T(8,128)(2,1)S(1)}, u32[]{:S(2)}, u32[]{:S(2)}) %collective-permute-start.16) | collective-permute-done | bytes 73760 | tf_op jit(solution)/shard_map/ppermute | solution.py:62
  40.1 2.4 %collective-permute-start.19 = (bf16[32,1152]{1,0:T(8,128)(2,1)S(1)}, bf16[32,1152]{1,0:T(8,128)(2,1)S(1)}, u32[]{:S(2)}, u32[]{:S(2)}) collective-permute-start(bf16[32,1152]{1,0:T(8,128)(2,1)S(1)} %merge_x.1.refs_0_), channel_id=1, source_target_pairs={{0,24},{1,25},{2,26},{3,27},{4,28},{5,29},{6,30},{7,31},{8,16},{9,... | collective-permute-start | bytes 221192 | tf_op jit(solution)/shard_map/ppermute | solution.py:62
  42.4 2.1 %collective-permute-start.17 = (bf16[32,1152]{1,0:T(8,128)(2,1)S(1)}, bf16[32,1152]{1,0:T(8,128)(2,1)S(1)}, u32[]{:S(2)}, u32[]{:S(2)}) collective-permute-start(bf16[32,1152]{1,0:T(8,128)(2,1)S(1)} %merge_x.1.refs_0_), channel_id=1, source_target_pairs={{0,8},{1,9},{2,10},{3,11},{4,12},{5,13},{6,14},{7,15},{8,0},{9,1},... | collective-permute-start | bytes 221192 | tf_op jit(solution)/shard_map/ppermute | solution.py:62
  44.5 2.1 %collective-permute-done.19.refs_3_ = bf16[32,1152]{1,0:T(8,128)(2,1)S(1)} collective-permute-done((bf16[32,1152]{1,0:T(8,128)(2,1)S(1)}, bf16[32,1152]{1,0:T(8,128)(2,1)S(1)}, u32[]{:S(2)}, u32[]{:S(2)}) %collective-permute-start.19) | collective-permute-done | bytes 73760 | tf_op jit(solution)/shard_map/ppermute | solution.py:62
  46.6 2.3 %collective-permute-done.18.refs_2_ = bf16[32,1152]{1,0:T(8,128)(2,1)S(1)} collective-permute-done((bf16[32,1152]{1,0:T(8,128)(2,1)S(1)}, bf16[32,1152]{1,0:T(8,128)(2,1)S(1)}, u32[]{:S(2)}, u32[]{:S(2)}) %collective-permute-start.18) | collective-permute-done | bytes 73760 | tf_op jit(solution)/shard_map/ppermute | solution.py:62
  49.6 1.2 %collective-permute-start.22 = (bf16[2,32,256]{2,1,0:T(8,128)(2,1)S(1)}, bf16[2,32,256]{2,1,0:T(8,128)(2,1)S(1)}, u32[]{:S(2)}, u32[]{:S(2)}) collective-permute-start(bf16[2,32,256]{2,1,0:T(8,128)(2,1)S(1)} %out.1.refs_0_), channel_id=1, source_target_pairs={{0,6},{1,7},{2,4},{3,5},{4,2},{5,3},{6,0},{7,1},{8,14},{9,15},{10,... | collective-permute-start | bytes 98312 | tf_op jit(solution)/shard_map/ppermute | solution.py:62
  50.8 1.7 %collective-permute-start.21 = (bf16[2,32,256]{2,1,0:T(8,128)(2,1)S(1)}, bf16[2,32,256]{2,1,0:T(8,128)(2,1)S(1)}, u32[]{:S(2)}, u32[]{:S(2)}) collective-permute-start(bf16[2,32,256]{2,1,0:T(8,128)(2,1)S(1)} %out.1.refs_0_), channel_id=1, source_target_pairs={{0,4},{1,5},{2,6},{3,7},{4,0},{5,1},{6,2},{7,3},{8,12},{9,13},{10,... | collective-permute-start | bytes 98312 | tf_op jit(solution)/shard_map/ppermute | solution.py:62
  53.2 1.6 %collective-permute-done.22.refs_3_ = bf16[2,32,256]{2,1,0:T(8,128)(2,1)S(1)} collective-permute-done((bf16[2,32,256]{2,1,0:T(8,128)(2,1)S(1)}, bf16[2,32,256]{2,1,0:T(8,128)(2,1)S(1)}, u32[]{:S(2)}, u32[]{:S(2)}) %collective-permute-start.22) | collective-permute-done | bytes 32800 | tf_op jit(solution)/shard_map/ppermute | solution.py:62
  54.8 1.7 %collective-permute-done.20.refs_1_ = bf16[2,32,256]{2,1,0:T(8,128)(2,1)S(1)} collective-permute-done((bf16[2,32,256]{2,1,0:T(8,128)(2,1)S(1)}, bf16[2,32,256]{2,1,0:T(8,128)(2,1)S(1)}, u32[]{:S(2)}, u32[]{:S(2)}) %collective-permute-start.20) | collective-permute-done | bytes 32800 | tf_op jit(solution)/shard_map/ppermute | solution.py:62
  56.5 1.9 %collective-permute-start.25 = (bf16[2,2,32,256]{3,2,1,0:T(8,128)(2,1)S(1)}, bf16[2,2,32,256]{3,2,1,0:T(8,128)(2,1)S(1)}, u32[]{:S(2)}, u32[]{:S(2)}) collective-permute-start(bf16[2,2,32,256]{3,2,1,0:T(8,128)(2,1)S(1)} %add_out.1.refs_2_), channel_id=1, source_target_pairs={{0,24},{1,25},{2,26},{3,27},{4,28},{5,29},{6,30},{7,31},{8,16},{9,... | collective-permute-start | bytes 196616 | tf_op jit(solution)/shard_map/ppermute | solution.py:62
  58.4 2.5 %collective-permute-start.23 = (bf16[2,2,32,256]{3,2,1,0:T(8,128)(2,1)S(1)}, bf16[2,2,32,256]{3,2,1,0:T(8,128)(2,1)S(1)}, u32[]{:S(2)}, u32[]{:S(2)}) collective-permute-start(bf16[2,2,32,256]{3,2,1,0:T(8,128)(2,1)S(1)} %add_out.1.refs_2_), channel_id=1, source_target_pairs={{0,8},{1,9},{2,10},{3,11},{4,12},{5,13},{6,14},{7,15},{8,0},{9,1},... | collective-permute-start | bytes 196616 | tf_op jit(solution)/shard_map/ppermute | solution.py:62
  60.9 1.8 %collective-permute-done.25.refs_5_ = bf16[2,2,32,256]{3,2,1,0:T(8,128)(2,1)S(1)} collective-permute-done((bf16[2,2,32,256]{3,2,1,0:T(8,128)(2,1)S(1)}, bf16[2,2,32,256]{3,2,1,0:T(8,128)(2,1)S(1)}, u32[]{:S(2)}, u32[]{:S(2)}) %collective-permute-start.25) | collective-permute-done | bytes 65568 | tf_op jit(solution)/shard_map/ppermute | solution.py:62
  62.7 1.4 %collective-permute-done.24.refs_4_ = bf16[2,2,32,256]{3,2,1,0:T(8,128)(2,1)S(1)} collective-permute-done((bf16[2,2,32,256]{3,2,1,0:T(8,128)(2,1)S(1)}, bf16[2,2,32,256]{3,2,1,0:T(8,128)(2,1)S(1)}, u32[]{:S(2)}, u32[]{:S(2)}) %collective-permute-start.24) | collective-permute-done | bytes 65568 | tf_op jit(solution)/shard_map/ppermute | solution.py:62
  66.2 3.9 %collective-permute-done.26.refs_1_ = bf16[64,1024]{1,0:T(8,128)(2,1)S(1)} collective-permute-done((bf16[64,1024]{1,0:T(8,128)(2,1)S(1)}, bf16[64,1024]{1,0:T(8,128)(2,1)S(1)}, u32[]{:S(2)}, u32[]{:S(2)}) %collective-permute-start.26) | collective-permute-done | bytes 131104 | tf_op jit(solution)/shard_map/ppermute | solution.py:62
  71.0 4.0 %collective-permute-done.27.refs_1_ = bf16[64,512]{1,0:T(8,128)(2,1)S(1)} collective-permute-done((bf16[64,512]{1,0:T(8,128)(2,1)S(1)}, bf16[64,512]{1,0:T(8,128)(2,1)S(1)}, u32[]{:S(2)}, u32[]{:S(2)}) %collective-permute-start.27) | collective-permute-done | bytes 65568 | tf_op jit(solution)/shard_map/ppermute | solution.py:62
  75.0 1.8 %collective-permute-start.30 = (bf16[64,512]{1,0:T(8,128)(2,1)S(1)}, bf16[64,512]{1,0:T(8,128)(2,1)S(1)}, u32[]{:S(2)}, u32[]{:S(2)}) collective-permute-start(bf16[64,512]{1,0:T(8,128)(2,1)S(1)} %add_x.1.refs_0_), channel_id=1, source_target_pairs={{0,24},{1,25},{2,26},{3,27},{4,28},{5,29},{6,30},{7,31},{8,16},{9,... | collective-permute-start | bytes 196616 | tf_op jit(solution)/shard_map/ppermute | solution.py:62
  77.5 1.9 %collective-permute-start.28 = (bf16[64,512]{1,0:T(8,128)(2,1)S(1)}, bf16[64,512]{1,0:T(8,128)(2,1)S(1)}, u32[]{:S(2)}, u32[]{:S(2)}) collective-permute-start(bf16[64,512]{1,0:T(8,128)(2,1)S(1)} %add_x.1.refs_0_), channel_id=1, source_target_pairs={{0,8},{1,9},{2,10},{3,11},{4,12},{5,13},{6,14},{7,15},{8,0},{9,1},... | collective-permute-start | bytes 196616 | tf_op jit(solution)/shard_map/ppermute | solution.py:62
  79.4 1.7 %collective-permute-done.30.refs_3_ = bf16[64,512]{1,0:T(8,128)(2,1)S(1)} collective-permute-done((bf16[64,512]{1,0:T(8,128)(2,1)S(1)}, bf16[64,512]{1,0:T(8,128)(2,1)S(1)}, u32[]{:S(2)}, u32[]{:S(2)}) %collective-permute-start.30) | collective-permute-done | bytes 65568 | tf_op jit(solution)/shard_map/ppermute | solution.py:62
  81.1 1.4 %collective-permute-done.29.refs_2_ = bf16[64,512]{1,0:T(8,128)(2,1)S(1)} collective-permute-done((bf16[64,512]{1,0:T(8,128)(2,1)S(1)}, bf16[64,512]{1,0:T(8,128)(2,1)S(1)}, u32[]{:S(2)}, u32[]{:S(2)}) %collective-permute-start.29) | collective-permute-done | bytes 65568 | tf_op jit(solution)/shard_map/ppermute | solution.py:62
  83.1 2.1 %collective-permute-start.33 = (bf16[32,512]{1,0:T(8,128)(2,1)S(1)}, bf16[32,512]{1,0:T(8,128)(2,1)S(1)}, u32[]{:S(2)}, u32[]{:S(2)}) collective-permute-start(bf16[32,512]{1,0:T(8,128)(2,1)S(1)} %get-tuple-element.89), channel_id=1, source_target_pairs={{0,6},{1,7},{2,4},{3,5},{4,2},{5,3},{6,0},{7,1},{8,14},{9,15},{10,... | collective-permute-start | bytes 98312 | tf_op jit(solution)/shard_map/ppermute | solution.py:62
  86.5 1.3 %collective-permute-done.33.refs_3_ = bf16[32,512]{1,0:T(8,128)(2,1)S(1)} collective-permute-done((bf16[32,512]{1,0:T(8,128)(2,1)S(1)}, bf16[32,512]{1,0:T(8,128)(2,1)S(1)}, u32[]{:S(2)}, u32[]{:S(2)}) %collective-permute-start.33) | collective-permute-done | bytes 32800 | tf_op jit(solution)/shard_map/ppermute | solution.py:62
  87.9 1.2 %collective-permute-done.31.refs_1_ = bf16[32,512]{1,0:T(8,128)(2,1)S(1)} collective-permute-done((bf16[32,512]{1,0:T(8,128)(2,1)S(1)}, bf16[32,512]{1,0:T(8,128)(2,1)S(1)}, u32[]{:S(2)}, u32[]{:S(2)}) %collective-permute-start.31) | collective-permute-done | bytes 32800 | tf_op jit(solution)/shard_map/ppermute | solution.py:62
  (77 shorter events, 17.5 us)
Async XLA Ops:
  0.6 7.9 %collective-permute-start.1 = (bf16[512,256]{1,0:T(8,128)(2,1)}, bf16[512,256]{1,0:T(8,128)(2,1)S(1)}, u32[]{:S(2)}, u32[]{:S(2)}) collective-permute-start(bf16[512,256]{1,0:T(8,128)(2,1)} %refs_0_.2), channel_id=1, source_target_pairs={{0,1},{1,0},{2,3},{3,2},{4,5},{5,4},{6,7},{7,6},{8,9},{9,8},{10,11... | collective-permute-start | bytes 786440 | tf_op jit(solution)/shard_map/ppermute | solution.py:62
  1.2 7.4 %collective-permute-start.2 = (bf16[512,256]{1,0:T(8,128)(2,1)}, bf16[512,256]{1,0:T(8,128)(2,1)S(1)}, u32[]{:S(2)}, u32[]{:S(2)}) collective-permute-start(bf16[512,256]{1,0:T(8,128)(2,1)} %refs_1_.1), channel_id=1, source_target_pairs={{0,1},{1,0},{2,3},{3,2},{4,5},{5,4},{6,7},{7,6},{8,9},{9,8},{10,11... | collective-permute-start | bytes 786440 | tf_op jit(solution)/shard_map/ppermute | solution.py:62
  1.2 7.3 %collective-permute-start.3 = (bf16[512,256]{1,0:T(8,128)(2,1)}, bf16[512,256]{1,0:T(8,128)(2,1)S(1)}, u32[]{:S(2)}, u32[]{:S(2)}) collective-permute-start(bf16[512,256]{1,0:T(8,128)(2,1)} %refs_2_.2), channel_id=1, source_target_pairs={{0,1},{1,0},{2,3},{3,2},{4,5},{5,4},{6,7},{7,6},{8,9},{9,8},{10,11... | collective-permute-start | bytes 786440 | tf_op jit(solution)/shard_map/ppermute | solution.py:62
  1.7 6.9 %collective-permute-start = (bf16[8,4,2048]{2,1,0:T(4,128)(2,1)}, bf16[8,4,2048]{2,1,0:T(4,128)(2,1)S(1)}, u32[]{:S(2)}, u32[]{:S(2)}) collective-permute-start(bf16[8,4,2048]{2,1,0:T(4,128)(2,1)} %refs_0_.3), channel_id=1, source_target_pairs={{0,2},{1,3},{2,0},{3,1},{4,6},{5,7},{6,4},{7,5},{8,10},{9,11},{10,... | collective-permute-start | bytes 393224 | tf_op jit(solution)/shard_map/ppermute | solution.py:62
  9.2 7.9 %collective-permute-start.7 = (bf16[512,1024]{1,0:T(8,128)(2,1)}, bf16[512,1024]{1,0:T(8,128)(2,1)S(1)}, u32[]{:S(2)}, u32[]{:S(2)}) collective-permute-start(bf16[512,1024]{1,0:T(8,128)(2,1)} %refs_8_.1), channel_id=1, source_target_pairs={{0,1},{1,0},{2,3},{3,2},{4,5},{5,4},{6,7},{7,6},{8,9},{9,8},{10,11... | collective-permute-start | bytes 3145736 | tf_op jit(solution)/shard_map/ppermute | solution.py:62
  9.3 7.9 %collective-permute-start.8 = (bf16[1024,512]{1,0:T(8,128)(2,1)}, bf16[1024,512]{1,0:T(8,128)(2,1)S(1)}, u32[]{:S(2)}, u32[]{:S(2)}) collective-permute-start(bf16[1024,512]{1,0:T(8,128)(2,1)} %refs_2_.3), channel_id=1, source_target_pairs={{0,1},{1,0},{2,3},{3,2},{4,5},{5,4},{6,7},{7,6},{8,9},{9,8},{10,11... | collective-permute-start | bytes 3145736 | tf_op jit(solution)/shard_map/ppermute | solution.py:62
  9.8 6.7 %collective-permute-start.5 = (bf16[32,768]{1,0:T(8,128)(2,1)S(1)}, bf16[32,768]{1,0:T(8,128)(2,1)S(1)}, u32[]{:S(2)}, u32[]{:S(2)}) collective-permute-start(bf16[32,768]{1,0:T(8,128)(2,1)S(1)} %get-tuple-element.56.refs_0_), channel_id=1, source_target_pairs={{0,4},{1,5},{2,6},{3,7},{4,0},{5,1},{6,2},{7,3},{8,12},{9,13},{10,... | collective-permute-start | bytes 147464 | tf_op jit(solution)/shard_map/ppermute | solution.py:62
  11.5 5.0 %collective-permute-start.6 = (bf16[32,768]{1,0:T(8,128)(2,1)S(1)}, bf16[32,768]{1,0:T(8,128)(2,1)S(1)}, u32[]{:S(2)}, u32[]{:S(2)}) collective-permute-start(bf16[32,768]{1,0:T(8,128)(2,1)S(1)} %get-tuple-element.57), channel_id=1, source_target_pairs={{0,6},{1,7},{2,4},{3,5},{4,2},{5,3},{6,0},{7,1},{8,14},{9,15},{10,... | collective-permute-start | bytes 147464 | tf_op jit(solution)/shard_map/ppermute | solution.py:62
  13.0 4.1 %collective-permute-start.4 = (bf16[32,768]{1,0:T(8,128)(2,1)S(1)}, bf16[32,768]{1,0:T(8,128)(2,1)S(1)}, u32[]{:S(2)}, u32[]{:S(2)}) collective-permute-start(bf16[32,768]{1,0:T(8,128)(2,1)S(1)} %get-tuple-element.57), channel_id=1, source_target_pairs={{0,2},{1,3},{2,0},{3,1},{4,6},{5,7},{6,4},{7,5},{8,10},{9,11},{10,... | collective-permute-start | bytes 147464 | tf_op jit(solution)/shard_map/ppermute | solution.py:62
  17.2 12.9 %collective-permute-start.13 = (bf16[512,256]{1,0:T(8,128)(2,1)S(1)}, bf16[512,256]{1,0:T(8,128)(2,1)S(1)}, u32[]{:S(2)}, u32[]{:S(2)}) collective-permute-start(bf16[512,256]{1,0:T(8,128)(2,1)S(1)} %copy-done.11), channel_id=1, source_target_pairs={{0,2},{1,3},{2,6},{3,7},{4,0},{5,1},{6,4},{7,5},{8,10},{9,11},{10,... | collective-permute-start | bytes 786440 | tf_op jit(solution)/shard_map/ppermute | solution.py:77
  18.4 11.7 %collective-permute-start.12 = (bf16[512,256]{1,0:T(8,128)(2,1)S(1)}, bf16[512,256]{1,0:T(8,128)(2,1)S(1)}, u32[]{:S(2)}, u32[]{:S(2)}) collective-permute-start(bf16[512,256]{1,0:T(8,128)(2,1)S(1)} %copy-done.11), channel_id=1, source_target_pairs={{0,0},{1,1},{2,4},{3,5},{4,2},{5,3},{6,6},{7,7},{8,8},{9,9},{10,12... | collective-permute-start | bytes 786440 | tf_op jit(solution)/shard_map/ppermute | solution.py:77
  19.0 7.0 %collective-permute-start.11 = (bf16[2,32,768]{2,1,0:T(8,128)(2,1)S(1)}, bf16[2,32,768]{2,1,0:T(8,128)(2,1)S(1)}, u32[]{:S(2)}, u32[]{:S(2)}) collective-permute-start(bf16[2,32,768]{2,1,0:T(8,128)(2,1)S(1)} %add_qkv.1.refs_0_), channel_id=1, source_target_pairs={{0,24},{1,25},{2,26},{3,27},{4,28},{5,29},{6,30},{7,31},{8,16},{9,... | collective-permute-start | bytes 294920 | tf_op jit(solution)/shard_map/ppermute | solution.py:62
  22.7 7.4 %collective-permute-start.10 = (bf16[2,32,768]{2,1,0:T(8,128)(2,1)S(1)}, bf16[2,32,768]{2,1,0:T(8,128)(2,1)S(1)}, u32[]{:S(2)}, u32[]{:S(2)}) collective-permute-start(bf16[2,32,768]{2,1,0:T(8,128)(2,1)S(1)} %add_qkv.1.refs_0_), channel_id=1, source_target_pairs={{0,16},{1,17},{2,18},{3,19},{4,20},{5,21},{6,22},{7,23},{8,24},{9,... | collective-permute-start | bytes 294920 | tf_op jit(solution)/shard_map/ppermute | solution.py:62
  22.7 7.4 %collective-permute-start.9 = (bf16[2,32,768]{2,1,0:T(8,128)(2,1)S(1)}, bf16[2,32,768]{2,1,0:T(8,128)(2,1)S(1)}, u32[]{:S(2)}, u32[]{:S(2)}) collective-permute-start(bf16[2,32,768]{2,1,0:T(8,128)(2,1)S(1)} %add_qkv.1.refs_0_), channel_id=1, source_target_pairs={{0,8},{1,9},{2,10},{3,11},{4,12},{5,13},{6,14},{7,15},{8,0},{9,1},... | collective-permute-start | bytes 294920 | tf_op jit(solution)/shard_map/ppermute | solution.py:62
  33.1 6.7 %collective-permute-start.16 = (bf16[32,1152]{1,0:T(8,128)(2,1)S(1)}, bf16[32,1152]{1,0:T(8,128)(2,1)S(1)}, u32[]{:S(2)}, u32[]{:S(2)}) collective-permute-start(bf16[32,1152]{1,0:T(8,128)(2,1)S(1)} %get-tuple-element.78), channel_id=1, source_target_pairs={{0,4},{1,5},{2,6},{3,7},{4,0},{5,1},{6,2},{7,3},{8,12},{9,13},{10,... | collective-permute-start | bytes 221192 | tf_op jit(solution)/shard_map/ppermute | solution.py:62
  40.1 6.5 %collective-permute-start.19 = (bf16[32,1152]{1,0:T(8,128)(2,1)S(1)}, bf16[32,1152]{1,0:T(8,128)(2,1)S(1)}, u32[]{:S(2)}, u32[]{:S(2)}) collective-permute-start(bf16[32,1152]{1,0:T(8,128)(2,1)S(1)} %merge_x.1.refs_0_), channel_id=1, source_target_pairs={{0,24},{1,25},{2,26},{3,27},{4,28},{5,29},{6,30},{7,31},{8,16},{9,... | collective-permute-start | bytes 221192 | tf_op jit(solution)/shard_map/ppermute | solution.py:62
  42.4 6.5 %collective-permute-start.18 = (bf16[32,1152]{1,0:T(8,128)(2,1)S(1)}, bf16[32,1152]{1,0:T(8,128)(2,1)S(1)}, u32[]{:S(2)}, u32[]{:S(2)}) collective-permute-start(bf16[32,1152]{1,0:T(8,128)(2,1)S(1)} %merge_x.1.refs_0_), channel_id=1, source_target_pairs={{0,16},{1,17},{2,18},{3,19},{4,20},{5,21},{6,22},{7,23},{8,24},{9,... | collective-permute-start | bytes 221192 | tf_op jit(solution)/shard_map/ppermute | solution.py:62
  42.4 6.5 %collective-permute-start.17 = (bf16[32,1152]{1,0:T(8,128)(2,1)S(1)}, bf16[32,1152]{1,0:T(8,128)(2,1)S(1)}, u32[]{:S(2)}, u32[]{:S(2)}) collective-permute-start(bf16[32,1152]{1,0:T(8,128)(2,1)S(1)} %merge_x.1.refs_0_), channel_id=1, source_target_pairs={{0,8},{1,9},{2,10},{3,11},{4,12},{5,13},{6,14},{7,15},{8,0},{9,1},... | collective-permute-start | bytes 221192 | tf_op jit(solution)/shard_map/ppermute | solution.py:62
  49.6 5.1 %collective-permute-start.22 = (bf16[2,32,256]{2,1,0:T(8,128)(2,1)S(1)}, bf16[2,32,256]{2,1,0:T(8,128)(2,1)S(1)}, u32[]{:S(2)}, u32[]{:S(2)}) collective-permute-start(bf16[2,32,256]{2,1,0:T(8,128)(2,1)S(1)} %out.1.refs_0_), channel_id=1, source_target_pairs={{0,6},{1,7},{2,4},{3,5},{4,2},{5,3},{6,0},{7,1},{8,14},{9,15},{10,... | collective-permute-start | bytes 98312 | tf_op jit(solution)/shard_map/ppermute | solution.py:62
  50.8 4.0 %collective-permute-start.21 = (bf16[2,32,256]{2,1,0:T(8,128)(2,1)S(1)}, bf16[2,32,256]{2,1,0:T(8,128)(2,1)S(1)}, u32[]{:S(2)}, u32[]{:S(2)}) collective-permute-start(bf16[2,32,256]{2,1,0:T(8,128)(2,1)S(1)} %out.1.refs_0_), channel_id=1, source_target_pairs={{0,4},{1,5},{2,6},{3,7},{4,0},{5,1},{6,2},{7,3},{8,12},{9,13},{10,... | collective-permute-start | bytes 98312 | tf_op jit(solution)/shard_map/ppermute | solution.py:62
  52.5 3.9 %collective-permute-start.20 = (bf16[2,32,256]{2,1,0:T(8,128)(2,1)S(1)}, bf16[2,32,256]{2,1,0:T(8,128)(2,1)S(1)}, u32[]{:S(2)}, u32[]{:S(2)}) collective-permute-start(bf16[2,32,256]{2,1,0:T(8,128)(2,1)S(1)} %out.1.refs_0_), channel_id=1, source_target_pairs={{0,2},{1,3},{2,0},{3,1},{4,6},{5,7},{6,4},{7,5},{8,10},{9,11},{10,... | collective-permute-start | bytes 98312 | tf_op jit(solution)/shard_map/ppermute | solution.py:62
  56.5 6.3 %collective-permute-start.25 = (bf16[2,2,32,256]{3,2,1,0:T(8,128)(2,1)S(1)}, bf16[2,2,32,256]{3,2,1,0:T(8,128)(2,1)S(1)}, u32[]{:S(2)}, u32[]{:S(2)}) collective-permute-start(bf16[2,2,32,256]{3,2,1,0:T(8,128)(2,1)S(1)} %add_out.1.refs_2_), channel_id=1, source_target_pairs={{0,24},{1,25},{2,26},{3,27},{4,28},{5,29},{6,30},{7,31},{8,16},{9,... | collective-permute-start | bytes 196616 | tf_op jit(solution)/shard_map/ppermute | solution.py:62
  58.4 5.8 %collective-permute-start.24 = (bf16[2,2,32,256]{3,2,1,0:T(8,128)(2,1)S(1)}, bf16[2,2,32,256]{3,2,1,0:T(8,128)(2,1)S(1)}, u32[]{:S(2)}, u32[]{:S(2)}) collective-permute-start(bf16[2,2,32,256]{3,2,1,0:T(8,128)(2,1)S(1)} %add_out.1.refs_2_), channel_id=1, source_target_pairs={{0,16},{1,17},{2,18},{3,19},{4,20},{5,21},{6,22},{7,23},{8,24},{9,... | collective-permute-start | bytes 196616 | tf_op jit(solution)/shard_map/ppermute | solution.py:62
  58.4 5.8 %collective-permute-start.23 = (bf16[2,2,32,256]{3,2,1,0:T(8,128)(2,1)S(1)}, bf16[2,2,32,256]{3,2,1,0:T(8,128)(2,1)S(1)}, u32[]{:S(2)}, u32[]{:S(2)}) collective-permute-start(bf16[2,2,32,256]{3,2,1,0:T(8,128)(2,1)S(1)} %add_out.1.refs_2_), channel_id=1, source_target_pairs={{0,8},{1,9},{2,10},{3,11},{4,12},{5,13},{6,14},{7,15},{8,0},{9,1},... | collective-permute-start | bytes 196616 | tf_op jit(solution)/shard_map/ppermute | solution.py:62
  65.1 5.0 %collective-permute-start.26 = (bf16[64,1024]{1,0:T(8,128)(2,1)S(1)}, bf16[64,1024]{1,0:T(8,128)(2,1)S(1)}, u32[]{:S(2)}, u32[]{:S(2)}) collective-permute-start(bf16[64,1024]{1,0:T(8,128)(2,1)S(1)} %get-tuple-element.84.refs_0_), channel_id=1, source_target_pairs={{0,2},{1,3},{2,0},{3,1},{4,6},{5,7},{6,4},{7,5},{8,10},{9,11},{10,... | collective-permute-start | bytes 393224 | tf_op jit(solution)/shard_map/ppermute | solution.py:62
  70.6 4.3 %collective-permute-start.27 = (bf16[64,512]{1,0:T(8,128)(2,1)S(1)}, bf16[64,512]{1,0:T(8,128)(2,1)S(1)}, u32[]{:S(2)}, u32[]{:S(2)}) collective-permute-start(bf16[64,512]{1,0:T(8,128)(2,1)S(1)} %get-tuple-element.87), channel_id=1, source_target_pairs={{0,4},{1,5},{2,6},{3,7},{4,0},{5,1},{6,2},{7,3},{8,12},{9,13},{10,... | collective-permute-start | bytes 196616 | tf_op jit(solution)/shard_map/ppermute | solution.py:62
  75.0 6.1 %collective-permute-start.30 = (bf16[64,512]{1,0:T(8,128)(2,1)S(1)}, bf16[64,512]{1,0:T(8,128)(2,1)S(1)}, u32[]{:S(2)}, u32[]{:S(2)}) collective-permute-start(bf16[64,512]{1,0:T(8,128)(2,1)S(1)} %add_x.1.refs_0_), channel_id=1, source_target_pairs={{0,24},{1,25},{2,26},{3,27},{4,28},{5,29},{6,30},{7,31},{8,16},{9,... | collective-permute-start | bytes 196616 | tf_op jit(solution)/shard_map/ppermute | solution.py:62
  76.8 5.7 %collective-permute-start.29 = (bf16[64,512]{1,0:T(8,128)(2,1)S(1)}, bf16[64,512]{1,0:T(8,128)(2,1)S(1)}, u32[]{:S(2)}, u32[]{:S(2)}) collective-permute-start(bf16[64,512]{1,0:T(8,128)(2,1)S(1)} %add_x.1.refs_0_), channel_id=1, source_target_pairs={{0,16},{1,17},{2,18},{3,19},{4,20},{5,21},{6,22},{7,23},{8,24},{9,... | collective-permute-start | bytes 196616 | tf_op jit(solution)/shard_map/ppermute | solution.py:62
  77.5 5.0 %collective-permute-start.28 = (bf16[64,512]{1,0:T(8,128)(2,1)S(1)}, bf16[64,512]{1,0:T(8,128)(2,1)S(1)}, u32[]{:S(2)}, u32[]{:S(2)}) collective-permute-start(bf16[64,512]{1,0:T(8,128)(2,1)S(1)} %add_x.1.refs_0_), channel_id=1, source_target_pairs={{0,8},{1,9},{2,10},{3,11},{4,12},{5,13},{6,14},{7,15},{8,0},{9,1},... | collective-permute-start | bytes 196616 | tf_op jit(solution)/shard_map/ppermute | solution.py:62
  82.6 4.0 %collective-permute-start.32 = (bf16[32,512]{1,0:T(8,128)(2,1)S(1)}, bf16[32,512]{1,0:T(8,128)(2,1)S(1)}, u32[]{:S(2)}, u32[]{:S(2)}) collective-permute-start(bf16[32,512]{1,0:T(8,128)(2,1)S(1)} %get-tuple-element.88.refs_0_), channel_id=1, source_target_pairs={{0,4},{1,5},{2,6},{3,7},{4,0},{5,1},{6,2},{7,3},{8,12},{9,13},{10,... | collective-permute-start | bytes 98312 | tf_op jit(solution)/shard_map/ppermute | solution.py:62
  83.1 4.8 %collective-permute-start.33 = (bf16[32,512]{1,0:T(8,128)(2,1)S(1)}, bf16[32,512]{1,0:T(8,128)(2,1)S(1)}, u32[]{:S(2)}, u32[]{:S(2)}) collective-permute-start(bf16[32,512]{1,0:T(8,128)(2,1)S(1)} %get-tuple-element.89), channel_id=1, source_target_pairs={{0,6},{1,7},{2,4},{3,5},{4,2},{5,3},{6,0},{7,1},{8,14},{9,15},{10,... | collective-permute-start | bytes 98312 | tf_op jit(solution)/shard_map/ppermute | solution.py:62
  85.1 3.9 %collective-permute-start.31 = (bf16[32,512]{1,0:T(8,128)(2,1)S(1)}, bf16[32,512]{1,0:T(8,128)(2,1)S(1)}, u32[]{:S(2)}, u32[]{:S(2)}) collective-permute-start(bf16[32,512]{1,0:T(8,128)(2,1)S(1)} %get-tuple-element.89), channel_id=1, source_target_pairs={{0,2},{1,3},{2,0},{3,1},{4,6},{5,7},{6,4},{7,5},{8,10},{9,11},{10,... | collective-permute-start | bytes 98312 | tf_op jit(solution)/shard_map/ppermute | solution.py:62
  (14 other events, 287.3 us)

commit v11 on v10

--- a/solution.py
+++ b/solution.py
@@ -394,7 +394,7 @@
     depth = weights[0].shape[0]
     core = place.core()
     for k in range(nx):
-        block = lax.rem(place.y() + k, nx)
+        block = lax.rem(place.y() + nx - 1 - k, nx)
         total[block] = dot(attn[:, at(core, depth)], weights[2 * k][...]) + dot(
             attn[:, at(1 - core, depth)], weights[2 * k + 1][...]
         )
@@ -569,7 +569,7 @@
         (qkv, w_up_sibling, w_down_sibling, w_out)
     )
     pieces = place.gather_z(qkv)
-    blocks = [place.transpose(tied, k) for k in range(nx)]
+    blocks = [place.transpose(tied, nx - 1 - k) for k in range(nx)]
     pieces, blocks = lax.optimization_barrier((pieces, blocks))
     w_outs = []
     for block in blocks:

time: 89.8 us -> 90.9 us (1.012)
  waiting for transfers between devices: 35.4 us -> 36.9 us
  starting transfers between devices: 40.7 us -> 39.3 us
    ppermute x32, starting transfers between devices: 38.8 us -> 34.4 us  [move(): return lax.ppermute(value, ('seq', 'req'), pairs)]
    ppermute x2, starting transfers between devices: 1.85 us -> 4.91 us  [transpose(): return lax.ppermute(value, ('seq', 'req'), pairs)]
    ppermute x32, waiting for transfers between devices: 35.4 us -> 36.7 us  [move(): return lax.ppermute(value, ('seq', 'req'), pairs)]
  transfers between devices with their start and end apart: 34 -> 34, of which waited for: 19 -> 21; matrix products, arithmetic and copies ran while one was open for 2% -> 2% of each run, Pallas kernels for 7% -> 8%
where the time goes in v11:
time: 90.9 us; the launch traced here: 90.5 us
  starting transfers between devices  39.3 us (43%)
  waiting for transfers between devices  36.9 us (41%)
  Pallas kernels  11 us (12%)
  other arithmetic  1.44 us (2%)
  local copies, waits for them, and re-layouts  0.97 us (1%)
  between operations  0.91 us (1%)
    ppermute x32, waiting for transfers between devices, move(): return lax.ppermute(value, ('seq', 'req'), pairs)  36.7 us
    ppermute x32, starting transfers between devices, move(): return lax.ppermute(value, ('seq', 'req'), pairs)  34.4 us
    pallas_call x14, Pallas kernels, call(): pl.pallas_call(kernel, name=name, out_shape=outs, in_specs=in_specs or [V...  11 us
    ppermute x2, starting transfers between devices, transpose(): return lax.ppermute(value, ('seq', 'req'), pairs)  4.91 us
  transfers between devices with their start and end apart: 34, of which 21 were waited for; matrix products, arithmetic and copies ran while one was open for 2% of the time, Pallas kernels for 8%

profile of v11, /device:TPU:0, one launch (start us, length us, event | category | flops | bytes accessed | tf_op | source)
XLA Modules:
  0.0 90.5 jit_solution(11425461148927682740)
XLA Ops:
  1.7 2.6 %collective-permute-start = (bf16[8,4,2048]{2,1,0:T(4,128)(2,1)}, bf16[8,4,2048]{2,1,0:T(4,128)(2,1)S(1)}, u32[]{:S(2)}, u32[]{:S(2)}) collective-permute-start(bf16[8,4,2048]{2,1,0:T(4,128)(2,1)} %refs_0_.3), channel_id=1, source_target_pairs={{0,2},{1,3},{2,0},{3,1},{4,6},{5,7},{6,4},{7,5},{8,10},{9,11},{10,... | collective-permute-start | bytes 393224 | tf_op jit(solution)/shard_map/ppermute | solution.py:62
  6.6 1.1 %norm.1 = (bf16[32,2048]{1,0:T(8,128)(2,1)S(1)}, bf16[512,256]{1,0:T(8,128)(2,1)S(1)}, bf16[512,256]{1,0:T(8,128)(2,1)S(1)}, bf16[512,256]{1,0:T(8,128)(2,1)S(1)}) custom-call(bf16[8,4,2048]{2,1,0:T(4,128)(2,1)S(1)} %copy-done.3, f32[1,4096]{1,0:T(1,128)S(1)} %bitcast.6, bf16[512,256]{1,0:T(8,128)(2,1)} %refs_0_.2, bf16[512,256]{1,0:T(8,128)(2,1)} %refs_1_.1, ...), custom_call_target="tpu_custom_call" | custom-call | bytes 1048576 | tf_op jit(solution)/shard_map/norm/pallas_call | solution.py:104
  9.8 1.7 %collective-permute-start.5 = (bf16[32,768]{1,0:T(8,128)(2,1)S(1)}, bf16[32,768]{1,0:T(8,128)(2,1)S(1)}, u32[]{:S(2)}, u32[]{:S(2)}) collective-permute-start(bf16[32,768]{1,0:T(8,128)(2,1)S(1)} %get-tuple-element.56.refs_0_), channel_id=1, source_target_pairs={{0,4},{1,5},{2,6},{3,7},{4,0},{5,1},{6,2},{7,3},{8,12},{9,13},{10,... | collective-permute-start | bytes 147464 | tf_op jit(solution)/shard_map/ppermute | solution.py:62
  11.5 1.5 %collective-permute-start.6 = (bf16[32,768]{1,0:T(8,128)(2,1)S(1)}, bf16[32,768]{1,0:T(8,128)(2,1)S(1)}, u32[]{:S(2)}, u32[]{:S(2)}) collective-permute-start(bf16[32,768]{1,0:T(8,128)(2,1)S(1)} %get-tuple-element.57), channel_id=1, source_target_pairs={{0,6},{1,7},{2,4},{3,5},{4,2},{5,3},{6,0},{7,1},{8,14},{9,15},{10,... | collective-permute-start | bytes 147464 | tf_op jit(solution)/shard_map/ppermute | solution.py:62
  13.3 3.2 %caches.1 = (bf16[8,64,2048]{2,1,0:T(8,128)(2,1)}, bf16[8,64,2048]{2,1,0:T(8,128)(2,1)}, bf16[8,64,2048]{2,1,0:T(8,128)(2,1)S(1)}, bf16[8,64,2048]{2,1,0:T(8,128)(2,1)S(1)}, f32[8,128]{1,0:T(8,128)S(1)}) custom-call(bf16[8,64,2048]{2,1,0:T(8,128)(2,1)S(1)} %copy-done, bf16[8,64,2048]{2,1,0:T(8,128)(2,1)} %values_in), custom_call_target="tpu_custom_call" | custom-call | bytes 16777216 | tf_op jit(solution)/shard_map/caches/pallas_call | solution.py:104
  17.9 4.2 %collective-permute-start.12 = (bf16[512,256]{1,0:T(8,128)(2,1)S(1)}, bf16[512,256]{1,0:T(8,128)(2,1)S(1)}, u32[]{:S(2)}, u32[]{:S(2)}) collective-permute-start(bf16[512,256]{1,0:T(8,128)(2,1)S(1)} %copy-done.11), channel_id=1, source_target_pairs={{0,2},{1,3},{2,6},{3,7},{4,0},{5,1},{6,4},{7,5},{8,10},{9,11},{10,... | collective-permute-start | bytes 786440 | tf_op jit(solution)/shard_map/ppermute | solution.py:77
  22.1 3.6 %collective-permute-start.11 = (bf16[2,32,768]{2,1,0:T(8,128)(2,1)S(1)}, bf16[2,32,768]{2,1,0:T(8,128)(2,1)S(1)}, u32[]{:S(2)}, u32[]{:S(2)}) collective-permute-start(bf16[2,32,768]{2,1,0:T(8,128)(2,1)S(1)} %add_qkv.1.refs_0_), channel_id=1, source_target_pairs={{0,24},{1,25},{2,26},{3,27},{4,28},{5,29},{6,30},{7,31},{8,16},{9,... | collective-permute-start | bytes 294920 | tf_op jit(solution)/shard_map/ppermute | solution.py:62
  26.5 2.1 %collective-permute-done.11.refs_3_ = bf16[2,32,768]{2,1,0:T(8,128)(2,1)S(1)} collective-permute-done((bf16[2,32,768]{2,1,0:T(8,128)(2,1)S(1)}, bf16[2,32,768]{2,1,0:T(8,128)(2,1)S(1)}, u32[]{:S(2)}, u32[]{:S(2)}) %collective-permute-start.11) | collective-permute-done | bytes 98336 | tf_op jit(solution)/shard_map/ppermute | solution.py:62
  28.6 4.0 %collective-permute-done.10.refs_2_ = bf16[2,32,768]{2,1,0:T(8,128)(2,1)S(1)} collective-permute-done((bf16[2,32,768]{2,1,0:T(8,128)(2,1)S(1)}, bf16[2,32,768]{2,1,0:T(8,128)(2,1)S(1)}, u32[]{:S(2)}, u32[]{:S(2)}) %collective-permute-start.10) | collective-permute-done | bytes 98336 | tf_op jit(solution)/shard_map/ppermute | solution.py:62
  33.3 2.9 %attention.1 = (bf16[8,64,2048]{2,1,0:T(8,128)(2,1)}, bf16[8,64,2048]{2,1,0:T(8,128)(2,1)}, bf16[32,1152]{1,0:T(8,128)(2,1)S(1)}, bf16[32,1152]{1,0:T(8,128)(2,1)S(1)}) custom-call(bf16[2,32,768]{2,1,0:T(8,128)(2,1)S(1)} %add_qkv.1.refs_0_, bf16[2,32,768]{2,1,0:T(8,128)(2,1)S(1)} %collective-permute-done.9.refs_1_, ...), custom_call_target="tpu_custom_call", output_to_operand_aliasing={{0}: (7, {}), {1}: (8, {})} | custom-call | bytes 16777216 | tf_op jit(solution)/shard_map/attention/pallas_call | solution.py:104
  37.2 3.5 %collective-permute-done.16.refs_1_ = bf16[32,1152]{1,0:T(8,128)(2,1)S(1)} collective-permute-done((bf16[32,1152]{1,0:T(8,128)(2,1)S(1)}, bf16[32,1152]{1,0:T(8,128)(2,1)S(1)}, u32[]{:S(2)}, u32[]{:S(2)}) %collective-permute-start.16) | collective-permute-done | bytes 73760 | tf_op jit(solution)/shard_map/ppermute | solution.py:62
  41.0 2.9 %collective-permute-start.19 = (bf16[32,1152]{1,0:T(8,128)(2,1)S(1)}, bf16[32,1152]{1,0:T(8,128)(2,1)S(1)}, u32[]{:S(2)}, u32[]{:S(2)}) collective-permute-start(bf16[32,1152]{1,0:T(8,128)(2,1)S(1)} %merge_x.1.refs_0_), channel_id=1, source_target_pairs={{0,24},{1,25},{2,26},{3,27},{4,28},{5,29},{6,30},{7,31},{8,16},{9,... | collective-permute-start | bytes 221192 | tf_op jit(solution)/shard_map/ppermute | solution.py:62
  43.9 1.5 %collective-permute-start.17 = (bf16[32,1152]{1,0:T(8,128)(2,1)S(1)}, bf16[32,1152]{1,0:T(8,128)(2,1)S(1)}, u32[]{:S(2)}, u32[]{:S(2)}) collective-permute-start(bf16[32,1152]{1,0:T(8,128)(2,1)S(1)} %merge_x.1.refs_0_), channel_id=1, source_target_pairs={{0,8},{1,9},{2,10},{3,11},{4,12},{5,13},{6,14},{7,15},{8,0},{9,1},... | collective-permute-start | bytes 221192 | tf_op jit(solution)/shard_map/ppermute | solution.py:62
  45.4 1.9 %collective-permute-done.19.refs_3_ = bf16[32,1152]{1,0:T(8,128)(2,1)S(1)} collective-permute-done((bf16[32,1152]{1,0:T(8,128)(2,1)S(1)}, bf16[32,1152]{1,0:T(8,128)(2,1)S(1)}, u32[]{:S(2)}, u32[]{:S(2)}) %collective-permute-start.19) | collective-permute-done | bytes 73760 | tf_op jit(solution)/shard_map/ppermute | solution.py:62
  47.3 2.3 %collective-permute-done.18.refs_2_ = bf16[32,1152]{1,0:T(8,128)(2,1)S(1)} collective-permute-done((bf16[32,1152]{1,0:T(8,128)(2,1)S(1)}, bf16[32,1152]{1,0:T(8,128)(2,1)S(1)}, u32[]{:S(2)}, u32[]{:S(2)}) %collective-permute-start.18) | collective-permute-done | bytes 73760 | tf_op jit(solution)/shard_map/ppermute | solution.py:62
  50.3 1.6 %collective-permute-start.22 = (bf16[2,32,256]{2,1,0:T(8,128)(2,1)S(1)}, bf16[2,32,256]{2,1,0:T(8,128)(2,1)S(1)}, u32[]{:S(2)}, u32[]{:S(2)}) collective-permute-start(bf16[2,32,256]{2,1,0:T(8,128)(2,1)S(1)} %out.1.refs_0_), channel_id=1, source_target_pairs={{0,6},{1,7},{2,4},{3,5},{4,2},{5,3},{6,0},{7,1},{8,14},{9,15},{10,... | collective-permute-start | bytes 98312 | tf_op jit(solution)/shard_map/ppermute | solution.py:62
  52.0 2.1 %collective-permute-start.21 = (bf16[2,32,256]{2,1,0:T(8,128)(2,1)S(1)}, bf16[2,32,256]{2,1,0:T(8,128)(2,1)S(1)}, u32[]{:S(2)}, u32[]{:S(2)}) collective-permute-start(bf16[2,32,256]{2,1,0:T(8,128)(2,1)S(1)} %out.1.refs_0_), channel_id=1, source_target_pairs={{0,4},{1,5},{2,6},{3,7},{4,0},{5,1},{6,2},{7,3},{8,12},{9,13},{10,... | collective-permute-start | bytes 98312 | tf_op jit(solution)/shard_map/ppermute | solution.py:62
  54.1 1.4 %collective-permute-done.22.refs_3_ = bf16[2,32,256]{2,1,0:T(8,128)(2,1)S(1)} collective-permute-done((bf16[2,32,256]{2,1,0:T(8,128)(2,1)S(1)}, bf16[2,32,256]{2,1,0:T(8,128)(2,1)S(1)}, u32[]{:S(2)}, u32[]{:S(2)}) %collective-permute-start.22) | collective-permute-done | bytes 32800 | tf_op jit(solution)/shard_map/ppermute | solution.py:62
  56.3 1.7 %collective-permute-done.20.refs_1_ = bf16[2,32,256]{2,1,0:T(8,128)(2,1)S(1)} collective-permute-done((bf16[2,32,256]{2,1,0:T(8,128)(2,1)S(1)}, bf16[2,32,256]{2,1,0:T(8,128)(2,1)S(1)}, u32[]{:S(2)}, u32[]{:S(2)}) %collective-permute-start.20) | collective-permute-done | bytes 32800 | tf_op jit(solution)/shard_map/ppermute | solution.py:62
  58.0 2.4 %collective-permute-start.25 = (bf16[2,2,32,256]{3,2,1,0:T(8,128)(2,1)S(1)}, bf16[2,2,32,256]{3,2,1,0:T(8,128)(2,1)S(1)}, u32[]{:S(2)}, u32[]{:S(2)}) collective-permute-start(bf16[2,2,32,256]{3,2,1,0:T(8,128)(2,1)S(1)} %add_out.1.refs_2_), channel_id=1, source_target_pairs={{0,24},{1,25},{2,26},{3,27},{4,28},{5,29},{6,30},{7,31},{8,16},{9,... | collective-permute-start | bytes 196616 | tf_op jit(solution)/shard_map/ppermute | solution.py:62
  60.4 2.1 %collective-permute-start.23 = (bf16[2,2,32,256]{3,2,1,0:T(8,128)(2,1)S(1)}, bf16[2,2,32,256]{3,2,1,0:T(8,128)(2,1)S(1)}, u32[]{:S(2)}, u32[]{:S(2)}) collective-permute-start(bf16[2,2,32,256]{3,2,1,0:T(8,128)(2,1)S(1)} %add_out.1.refs_2_), channel_id=1, source_target_pairs={{0,8},{1,9},{2,10},{3,11},{4,12},{5,13},{6,14},{7,15},{8,0},{9,1},... | collective-permute-start | bytes 196616 | tf_op jit(solution)/shard_map/ppermute | solution.py:62
  62.5 1.8 %collective-permute-done.25.refs_5_ = bf16[2,2,32,256]{3,2,1,0:T(8,128)(2,1)S(1)} collective-permute-done((bf16[2,2,32,256]{3,2,1,0:T(8,128)(2,1)S(1)}, bf16[2,2,32,256]{3,2,1,0:T(8,128)(2,1)S(1)}, u32[]{:S(2)}, u32[]{:S(2)}) %collective-permute-start.25) | collective-permute-done | bytes 65568 | tf_op jit(solution)/shard_map/ppermute | solution.py:62
  64.3 1.4 %collective-permute-done.24.refs_4_ = bf16[2,2,32,256]{3,2,1,0:T(8,128)(2,1)S(1)} collective-permute-done((bf16[2,2,32,256]{3,2,1,0:T(8,128)(2,1)S(1)}, bf16[2,2,32,256]{3,2,1,0:T(8,128)(2,1)S(1)}, u32[]{:S(2)}, u32[]{:S(2)}) %collective-permute-start.24) | collective-permute-done | bytes 65568 | tf_op jit(solution)/shard_map/ppermute | solution.py:62
  66.7 4.9 %collective-permute-done.26.refs_1_ = bf16[64,1024]{1,0:T(8,128)(2,1)S(1)} collective-permute-done((bf16[64,1024]{1,0:T(8,128)(2,1)S(1)}, bf16[64,1024]{1,0:T(8,128)(2,1)S(1)}, u32[]{:S(2)}, u32[]{:S(2)}) %collective-permute-start.26) | collective-permute-done | bytes 131104 | tf_op jit(solution)/shard_map/ppermute | solution.py:62
  72.3 4.2 %collective-permute-done.27.refs_1_ = bf16[64,512]{1,0:T(8,128)(2,1)S(1)} collective-permute-done((bf16[64,512]{1,0:T(8,128)(2,1)S(1)}, bf16[64,512]{1,0:T(8,128)(2,1)S(1)}, u32[]{:S(2)}, u32[]{:S(2)}) %collective-permute-start.27) | collective-permute-done | bytes 65568 | tf_op jit(solution)/shard_map/ppermute | solution.py:62
  76.5 2.2 %collective-permute-start.30 = (bf16[64,512]{1,0:T(8,128)(2,1)S(1)}, bf16[64,512]{1,0:T(8,128)(2,1)S(1)}, u32[]{:S(2)}, u32[]{:S(2)}) collective-permute-start(bf16[64,512]{1,0:T(8,128)(2,1)S(1)} %add_x.1.refs_0_), channel_id=1, source_target_pairs={{0,24},{1,25},{2,26},{3,27},{4,28},{5,29},{6,30},{7,31},{8,16},{9,... | collective-permute-start | bytes 196616 | tf_op jit(solution)/shard_map/ppermute | solution.py:62
  79.1 1.9 %collective-permute-start.28 = (bf16[64,512]{1,0:T(8,128)(2,1)S(1)}, bf16[64,512]{1,0:T(8,128)(2,1)S(1)}, u32[]{:S(2)}, u32[]{:S(2)}) collective-permute-start(bf16[64,512]{1,0:T(8,128)(2,1)S(1)} %add_x.1.refs_0_), channel_id=1, source_target_pairs={{0,8},{1,9},{2,10},{3,11},{4,12},{5,13},{6,14},{7,15},{8,0},{9,1},... | collective-permute-start | bytes 196616 | tf_op jit(solution)/shard_map/ppermute | solution.py:62
  80.9 1.7 %collective-permute-done.30.refs_3_ = bf16[64,512]{1,0:T(8,128)(2,1)S(1)} collective-permute-done((bf16[64,512]{1,0:T(8,128)(2,1)S(1)}, bf16[64,512]{1,0:T(8,128)(2,1)S(1)}, u32[]{:S(2)}, u32[]{:S(2)}) %collective-permute-start.30) | collective-permute-done | bytes 65568 | tf_op jit(solution)/shard_map/ppermute | solution.py:62
  82.6 1.7 %collective-permute-done.29.refs_2_ = bf16[64,512]{1,0:T(8,128)(2,1)S(1)} collective-permute-done((bf16[64,512]{1,0:T(8,128)(2,1)S(1)}, bf16[64,512]{1,0:T(8,128)(2,1)S(1)}, u32[]{:S(2)}, u32[]{:S(2)}) %collective-permute-start.29) | collective-permute-done | bytes 65568 | tf_op jit(solution)/shard_map/ppermute | solution.py:62
  84.6 1.3 %collective-permute-start.33 = (bf16[32,512]{1,0:T(8,128)(2,1)S(1)}, bf16[32,512]{1,0:T(8,128)(2,1)S(1)}, u32[]{:S(2)}, u32[]{:S(2)}) collective-permute-start(bf16[32,512]{1,0:T(8,128)(2,1)S(1)} %get-tuple-element.89), channel_id=1, source_target_pairs={{0,6},{1,7},{2,4},{3,5},{4,2},{5,3},{6,0},{7,1},{8,14},{9,15},{10,... | collective-permute-start | bytes 98312 | tf_op jit(solution)/shard_map/ppermute | solution.py:62
  85.9 2.0 %collective-permute-start.31 = (bf16[32,512]{1,0:T(8,128)(2,1)S(1)}, bf16[32,512]{1,0:T(8,128)(2,1)S(1)}, u32[]{:S(2)}, u32[]{:S(2)}) collective-permute-start(bf16[32,512]{1,0:T(8,128)(2,1)S(1)} %get-tuple-element.89), channel_id=1, source_target_pairs={{0,2},{1,3},{2,0},{3,1},{4,6},{5,7},{6,4},{7,5},{8,10},{9,11},{10,... | collective-permute-start | bytes 98312 | tf_op jit(solution)/shard_map/ppermute | solution.py:62
  88.3 1.1 %collective-permute-done.33.refs_3_ = bf16[32,512]{1,0:T(8,128)(2,1)S(1)} collective-permute-done((bf16[32,512]{1,0:T(8,128)(2,1)S(1)}, bf16[32,512]{1,0:T(8,128)(2,1)S(1)}, u32[]{:S(2)}, u32[]{:S(2)}) %collective-permute-start.33) | collective-permute-done | bytes 32800 | tf_op jit(solution)/shard_map/ppermute | solution.py:62
  (77 shorter events, 15.2 us)
Async XLA Ops:
  0.6 7.9 %collective-permute-start.1 = (bf16[512,256]{1,0:T(8,128)(2,1)}, bf16[512,256]{1,0:T(8,128)(2,1)S(1)}, u32[]{:S(2)}, u32[]{:S(2)}) collective-permute-start(bf16[512,256]{1,0:T(8,128)(2,1)} %refs_0_.2), channel_id=1, source_target_pairs={{0,1},{1,0},{2,3},{3,2},{4,5},{5,4},{6,7},{7,6},{8,9},{9,8},{10,11... | collective-permute-start | bytes 786440 | tf_op jit(solution)/shard_map/ppermute | solution.py:62
  1.2 7.4 %collective-permute-start.2 = (bf16[512,256]{1,0:T(8,128)(2,1)}, bf16[512,256]{1,0:T(8,128)(2,1)S(1)}, u32[]{:S(2)}, u32[]{:S(2)}) collective-permute-start(bf16[512,256]{1,0:T(8,128)(2,1)} %refs_1_.1), channel_id=1, source_target_pairs={{0,1},{1,0},{2,3},{3,2},{4,5},{5,4},{6,7},{7,6},{8,9},{9,8},{10,11... | collective-permute-start | bytes 786440 | tf_op jit(solution)/shard_map/ppermute | solution.py:62
  1.2 7.3 %collective-permute-start.3 = (bf16[512,256]{1,0:T(8,128)(2,1)}, bf16[512,256]{1,0:T(8,128)(2,1)S(1)}, u32[]{:S(2)}, u32[]{:S(2)}) collective-permute-start(bf16[512,256]{1,0:T(8,128)(2,1)} %refs_2_.2), channel_id=1, source_target_pairs={{0,1},{1,0},{2,3},{3,2},{4,5},{5,4},{6,7},{7,6},{8,9},{9,8},{10,11... | collective-permute-start | bytes 786440 | tf_op jit(solution)/shard_map/ppermute | solution.py:62
  1.7 6.9 %collective-permute-start = (bf16[8,4,2048]{2,1,0:T(4,128)(2,1)}, bf16[8,4,2048]{2,1,0:T(4,128)(2,1)S(1)}, u32[]{:S(2)}, u32[]{:S(2)}) collective-permute-start(bf16[8,4,2048]{2,1,0:T(4,128)(2,1)} %refs_0_.3), channel_id=1, source_target_pairs={{0,2},{1,3},{2,0},{3,1},{4,6},{5,7},{6,4},{7,5},{8,10},{9,11},{10,... | collective-permute-start | bytes 393224 | tf_op jit(solution)/shard_map/ppermute | solution.py:62
  9.2 7.9 %collective-permute-start.7 = (bf16[512,1024]{1,0:T(8,128)(2,1)}, bf16[512,1024]{1,0:T(8,128)(2,1)S(1)}, u32[]{:S(2)}, u32[]{:S(2)}) collective-permute-start(bf16[512,1024]{1,0:T(8,128)(2,1)} %refs_8_.1), channel_id=1, source_target_pairs={{0,1},{1,0},{2,3},{3,2},{4,5},{5,4},{6,7},{7,6},{8,9},{9,8},{10,11... | collective-permute-start | bytes 3145736 | tf_op jit(solution)/shard_map/ppermute | solution.py:62
  9.3 7.9 %collective-permute-start.8 = (bf16[1024,512]{1,0:T(8,128)(2,1)}, bf16[1024,512]{1,0:T(8,128)(2,1)S(1)}, u32[]{:S(2)}, u32[]{:S(2)}) collective-permute-start(bf16[1024,512]{1,0:T(8,128)(2,1)} %refs_2_.3), channel_id=1, source_target_pairs={{0,1},{1,0},{2,3},{3,2},{4,5},{5,4},{6,7},{7,6},{8,9},{9,8},{10,11... | collective-permute-start | bytes 3145736 | tf_op jit(solution)/shard_map/ppermute | solution.py:62
  9.8 6.7 %collective-permute-start.5 = (bf16[32,768]{1,0:T(8,128)(2,1)S(1)}, bf16[32,768]{1,0:T(8,128)(2,1)S(1)}, u32[]{:S(2)}, u32[]{:S(2)}) collective-permute-start(bf16[32,768]{1,0:T(8,128)(2,1)S(1)} %get-tuple-element.56.refs_0_), channel_id=1, source_target_pairs={{0,4},{1,5},{2,6},{3,7},{4,0},{5,1},{6,2},{7,3},{8,12},{9,13},{10,... | collective-permute-start | bytes 147464 | tf_op jit(solution)/shard_map/ppermute | solution.py:62
  11.5 5.0 %collective-permute-start.6 = (bf16[32,768]{1,0:T(8,128)(2,1)S(1)}, bf16[32,768]{1,0:T(8,128)(2,1)S(1)}, u32[]{:S(2)}, u32[]{:S(2)}) collective-permute-start(bf16[32,768]{1,0:T(8,128)(2,1)S(1)} %get-tuple-element.57), channel_id=1, source_target_pairs={{0,6},{1,7},{2,4},{3,5},{4,2},{5,3},{6,0},{7,1},{8,14},{9,15},{10,... | collective-permute-start | bytes 147464 | tf_op jit(solution)/shard_map/ppermute | solution.py:62
  13.0 4.1 %collective-permute-start.4 = (bf16[32,768]{1,0:T(8,128)(2,1)S(1)}, bf16[32,768]{1,0:T(8,128)(2,1)S(1)}, u32[]{:S(2)}, u32[]{:S(2)}) collective-permute-start(bf16[32,768]{1,0:T(8,128)(2,1)S(1)} %get-tuple-element.57), channel_id=1, source_target_pairs={{0,2},{1,3},{2,0},{3,1},{4,6},{5,7},{6,4},{7,5},{8,10},{9,11},{10,... | collective-permute-start | bytes 147464 | tf_op jit(solution)/shard_map/ppermute | solution.py:62
  17.2 15.4 %collective-permute-start.13 = (bf16[512,256]{1,0:T(8,128)(2,1)S(1)}, bf16[512,256]{1,0:T(8,128)(2,1)S(1)}, u32[]{:S(2)}, u32[]{:S(2)}) collective-permute-start(bf16[512,256]{1,0:T(8,128)(2,1)S(1)} %copy-done.11), channel_id=1, source_target_pairs={{0,0},{1,1},{2,4},{3,5},{4,2},{5,3},{6,6},{7,7},{8,8},{9,9},{10,12... | collective-permute-start | bytes 786440 | tf_op jit(solution)/shard_map/ppermute | solution.py:77
  17.9 14.9 %collective-permute-start.12 = (bf16[512,256]{1,0:T(8,128)(2,1)S(1)}, bf16[512,256]{1,0:T(8,128)(2,1)S(1)}, u32[]{:S(2)}, u32[]{:S(2)}) collective-permute-start(bf16[512,256]{1,0:T(8,128)(2,1)S(1)} %copy-done.11), channel_id=1, source_target_pairs={{0,2},{1,3},{2,6},{3,7},{4,0},{5,1},{6,4},{7,5},{8,10},{9,11},{10,... | collective-permute-start | bytes 786440 | tf_op jit(solution)/shard_map/ppermute | solution.py:77
  22.1 6.5 %collective-permute-start.11 = (bf16[2,32,768]{2,1,0:T(8,128)(2,1)S(1)}, bf16[2,32,768]{2,1,0:T(8,128)(2,1)S(1)}, u32[]{:S(2)}, u32[]{:S(2)}) collective-permute-start(bf16[2,32,768]{2,1,0:T(8,128)(2,1)S(1)} %add_qkv.1.refs_0_), channel_id=1, source_target_pairs={{0,24},{1,25},{2,26},{3,27},{4,28},{5,29},{6,30},{7,31},{8,16},{9,... | collective-permute-start | bytes 294920 | tf_op jit(solution)/shard_map/ppermute | solution.py:62
  25.7 6.9 %collective-permute-start.10 = (bf16[2,32,768]{2,1,0:T(8,128)(2,1)S(1)}, bf16[2,32,768]{2,1,0:T(8,128)(2,1)S(1)}, u32[]{:S(2)}, u32[]{:S(2)}) collective-permute-start(bf16[2,32,768]{2,1,0:T(8,128)(2,1)S(1)} %add_qkv.1.refs_0_), channel_id=1, source_target_pairs={{0,16},{1,17},{2,18},{3,19},{4,20},{5,21},{6,22},{7,23},{8,24},{9,... | collective-permute-start | bytes 294920 | tf_op jit(solution)/shard_map/ppermute | solution.py:62
  25.7 6.9 %collective-permute-start.9 = (bf16[2,32,768]{2,1,0:T(8,128)(2,1)S(1)}, bf16[2,32,768]{2,1,0:T(8,128)(2,1)S(1)}, u32[]{:S(2)}, u32[]{:S(2)}) collective-permute-start(bf16[2,32,768]{2,1,0:T(8,128)(2,1)S(1)} %add_qkv.1.refs_0_), channel_id=1, source_target_pairs={{0,8},{1,9},{2,10},{3,11},{4,12},{5,13},{6,14},{7,15},{8,0},{9,1},... | collective-permute-start | bytes 294920 | tf_op jit(solution)/shard_map/ppermute | solution.py:62
  36.3 4.4 %collective-permute-start.16 = (bf16[32,1152]{1,0:T(8,128)(2,1)S(1)}, bf16[32,1152]{1,0:T(8,128)(2,1)S(1)}, u32[]{:S(2)}, u32[]{:S(2)}) collective-permute-start(bf16[32,1152]{1,0:T(8,128)(2,1)S(1)} %get-tuple-element.78), channel_id=1, source_target_pairs={{0,4},{1,5},{2,6},{3,7},{4,0},{5,1},{6,2},{7,3},{8,12},{9,13},{10,... | collective-permute-start | bytes 221192 | tf_op jit(solution)/shard_map/ppermute | solution.py:62
  41.0 6.3 %collective-permute-start.19 = (bf16[32,1152]{1,0:T(8,128)(2,1)S(1)}, bf16[32,1152]{1,0:T(8,128)(2,1)S(1)}, u32[]{:S(2)}, u32[]{:S(2)}) collective-permute-start(bf16[32,1152]{1,0:T(8,128)(2,1)S(1)} %merge_x.1.refs_0_), channel_id=1, source_target_pairs={{0,24},{1,25},{2,26},{3,27},{4,28},{5,29},{6,30},{7,31},{8,16},{9,... | collective-permute-start | bytes 221192 | tf_op jit(solution)/shard_map/ppermute | solution.py:62
  43.9 5.7 %collective-permute-start.18 = (bf16[32,1152]{1,0:T(8,128)(2,1)S(1)}, bf16[32,1152]{1,0:T(8,128)(2,1)S(1)}, u32[]{:S(2)}, u32[]{:S(2)}) collective-permute-start(bf16[32,1152]{1,0:T(8,128)(2,1)S(1)} %merge_x.1.refs_0_), channel_id=1, source_target_pairs={{0,16},{1,17},{2,18},{3,19},{4,20},{5,21},{6,22},{7,23},{8,24},{9,... | collective-permute-start | bytes 221192 | tf_op jit(solution)/shard_map/ppermute | solution.py:62
  43.9 5.7 %collective-permute-start.17 = (bf16[32,1152]{1,0:T(8,128)(2,1)S(1)}, bf16[32,1152]{1,0:T(8,128)(2,1)S(1)}, u32[]{:S(2)}, u32[]{:S(2)}) collective-permute-start(bf16[32,1152]{1,0:T(8,128)(2,1)S(1)} %merge_x.1.refs_0_), channel_id=1, source_target_pairs={{0,8},{1,9},{2,10},{3,11},{4,12},{5,13},{6,14},{7,15},{8,0},{9,1},... | collective-permute-start | bytes 221192 | tf_op jit(solution)/shard_map/ppermute | solution.py:62
  50.3 5.1 %collective-permute-start.22 = (bf16[2,32,256]{2,1,0:T(8,128)(2,1)S(1)}, bf16[2,32,256]{2,1,0:T(8,128)(2,1)S(1)}, u32[]{:S(2)}, u32[]{:S(2)}) collective-permute-start(bf16[2,32,256]{2,1,0:T(8,128)(2,1)S(1)} %out.1.refs_0_), channel_id=1, source_target_pairs={{0,6},{1,7},{2,4},{3,5},{4,2},{5,3},{6,0},{7,1},{8,14},{9,15},{10,... | collective-permute-start | bytes 98312 | tf_op jit(solution)/shard_map/ppermute | solution.py:62
  52.0 4.3 %collective-permute-start.21 = (bf16[2,32,256]{2,1,0:T(8,128)(2,1)S(1)}, bf16[2,32,256]{2,1,0:T(8,128)(2,1)S(1)}, u32[]{:S(2)}, u32[]{:S(2)}) collective-permute-start(bf16[2,32,256]{2,1,0:T(8,128)(2,1)S(1)} %out.1.refs_0_), channel_id=1, source_target_pairs={{0,4},{1,5},{2,6},{3,7},{4,0},{5,1},{6,2},{7,3},{8,12},{9,13},{10,... | collective-permute-start | bytes 98312 | tf_op jit(solution)/shard_map/ppermute | solution.py:62
  54.1 3.9 %collective-permute-start.20 = (bf16[2,32,256]{2,1,0:T(8,128)(2,1)S(1)}, bf16[2,32,256]{2,1,0:T(8,128)(2,1)S(1)}, u32[]{:S(2)}, u32[]{:S(2)}) collective-permute-start(bf16[2,32,256]{2,1,0:T(8,128)(2,1)S(1)} %out.1.refs_0_), channel_id=1, source_target_pairs={{0,2},{1,3},{2,0},{3,1},{4,6},{5,7},{6,4},{7,5},{8,10},{9,11},{10,... | collective-permute-start | bytes 98312 | tf_op jit(solution)/shard_map/ppermute | solution.py:62
  58.0 6.3 %collective-permute-start.25 = (bf16[2,2,32,256]{3,2,1,0:T(8,128)(2,1)S(1)}, bf16[2,2,32,256]{3,2,1,0:T(8,128)(2,1)S(1)}, u32[]{:S(2)}, u32[]{:S(2)}) collective-permute-start(bf16[2,2,32,256]{3,2,1,0:T(8,128)(2,1)S(1)} %add_out.1.refs_2_), channel_id=1, source_target_pairs={{0,24},{1,25},{2,26},{3,27},{4,28},{5,29},{6,30},{7,31},{8,16},{9,... | collective-permute-start | bytes 196616 | tf_op jit(solution)/shard_map/ppermute | solution.py:62
  60.4 5.3 %collective-permute-start.24 = (bf16[2,2,32,256]{3,2,1,0:T(8,128)(2,1)S(1)}, bf16[2,2,32,256]{3,2,1,0:T(8,128)(2,1)S(1)}, u32[]{:S(2)}, u32[]{:S(2)}) collective-permute-start(bf16[2,2,32,256]{3,2,1,0:T(8,128)(2,1)S(1)} %add_out.1.refs_2_), channel_id=1, source_target_pairs={{0,16},{1,17},{2,18},{3,19},{4,20},{5,21},{6,22},{7,23},{8,24},{9,... | collective-permute-start | bytes 196616 | tf_op jit(solution)/shard_map/ppermute | solution.py:62
  60.4 5.3 %collective-permute-start.23 = (bf16[2,2,32,256]{3,2,1,0:T(8,128)(2,1)S(1)}, bf16[2,2,32,256]{3,2,1,0:T(8,128)(2,1)S(1)}, u32[]{:S(2)}, u32[]{:S(2)}) collective-permute-start(bf16[2,2,32,256]{3,2,1,0:T(8,128)(2,1)S(1)} %add_out.1.refs_2_), channel_id=1, source_target_pairs={{0,8},{1,9},{2,10},{3,11},{4,12},{5,13},{6,14},{7,15},{8,0},{9,1},... | collective-permute-start | bytes 196616 | tf_op jit(solution)/shard_map/ppermute | solution.py:62
  66.6 5.0 %collective-permute-start.26 = (bf16[64,1024]{1,0:T(8,128)(2,1)S(1)}, bf16[64,1024]{1,0:T(8,128)(2,1)S(1)}, u32[]{:S(2)}, u32[]{:S(2)}) collective-permute-start(bf16[64,1024]{1,0:T(8,128)(2,1)S(1)} %get-tuple-element.84.refs_0_), channel_id=1, source_target_pairs={{0,2},{1,3},{2,0},{3,1},{4,6},{5,7},{6,4},{7,5},{8,10},{9,11},{10,... | collective-permute-start | bytes 393224 | tf_op jit(solution)/shard_map/ppermute | solution.py:62
  72.1 4.3 %collective-permute-start.27 = (bf16[64,512]{1,0:T(8,128)(2,1)S(1)}, bf16[64,512]{1,0:T(8,128)(2,1)S(1)}, u32[]{:S(2)}, u32[]{:S(2)}) collective-permute-start(bf16[64,512]{1,0:T(8,128)(2,1)S(1)} %get-tuple-element.87), channel_id=1, source_target_pairs={{0,4},{1,5},{2,6},{3,7},{4,0},{5,1},{6,2},{7,3},{8,12},{9,13},{10,... | collective-permute-start | bytes 196616 | tf_op jit(solution)/shard_map/ppermute | solution.py:62
  76.5 6.1 %collective-permute-start.30 = (bf16[64,512]{1,0:T(8,128)(2,1)S(1)}, bf16[64,512]{1,0:T(8,128)(2,1)S(1)}, u32[]{:S(2)}, u32[]{:S(2)}) collective-permute-start(bf16[64,512]{1,0:T(8,128)(2,1)S(1)} %add_x.1.refs_0_), channel_id=1, source_target_pairs={{0,24},{1,25},{2,26},{3,27},{4,28},{5,29},{6,30},{7,31},{8,16},{9,... | collective-permute-start | bytes 196616 | tf_op jit(solution)/shard_map/ppermute | solution.py:62
  78.7 5.6 %collective-permute-start.29 = (bf16[64,512]{1,0:T(8,128)(2,1)S(1)}, bf16[64,512]{1,0:T(8,128)(2,1)S(1)}, u32[]{:S(2)}, u32[]{:S(2)}) collective-permute-start(bf16[64,512]{1,0:T(8,128)(2,1)S(1)} %add_x.1.refs_0_), channel_id=1, source_target_pairs={{0,16},{1,17},{2,18},{3,19},{4,20},{5,21},{6,22},{7,23},{8,24},{9,... | collective-permute-start | bytes 196616 | tf_op jit(solution)/shard_map/ppermute | solution.py:62
  79.1 5.2 %collective-permute-start.28 = (bf16[64,512]{1,0:T(8,128)(2,1)S(1)}, bf16[64,512]{1,0:T(8,128)(2,1)S(1)}, u32[]{:S(2)}, u32[]{:S(2)}) collective-permute-start(bf16[64,512]{1,0:T(8,128)(2,1)S(1)} %add_x.1.refs_0_), channel_id=1, source_target_pairs={{0,8},{1,9},{2,10},{3,11},{4,12},{5,13},{6,14},{7,15},{8,0},{9,1},... | collective-permute-start | bytes 196616 | tf_op jit(solution)/shard_map/ppermute | solution.py:62
  84.3 4.0 %collective-permute-start.32 = (bf16[32,512]{1,0:T(8,128)(2,1)S(1)}, bf16[32,512]{1,0:T(8,128)(2,1)S(1)}, u32[]{:S(2)}, u32[]{:S(2)}) collective-permute-start(bf16[32,512]{1,0:T(8,128)(2,1)S(1)} %get-tuple-element.88.refs_0_), channel_id=1, source_target_pairs={{0,4},{1,5},{2,6},{3,7},{4,0},{5,1},{6,2},{7,3},{8,12},{9,13},{10,... | collective-permute-start | bytes 98312 | tf_op jit(solution)/shard_map/ppermute | solution.py:62
  84.6 4.8 %collective-permute-start.33 = (bf16[32,512]{1,0:T(8,128)(2,1)S(1)}, bf16[32,512]{1,0:T(8,128)(2,1)S(1)}, u32[]{:S(2)}, u32[]{:S(2)}) collective-permute-start(bf16[32,512]{1,0:T(8,128)(2,1)S(1)} %get-tuple-element.89), channel_id=1, source_target_pairs={{0,6},{1,7},{2,4},{3,5},{4,2},{5,3},{6,0},{7,1},{8,14},{9,15},{10,... | collective-permute-start | bytes 98312 | tf_op jit(solution)/shard_map/ppermute | solution.py:62
  85.9 3.9 %collective-permute-start.31 = (bf16[32,512]{1,0:T(8,128)(2,1)S(1)}, bf16[32,512]{1,0:T(8,128)(2,1)S(1)}, u32[]{:S(2)}, u32[]{:S(2)}) collective-permute-start(bf16[32,512]{1,0:T(8,128)(2,1)S(1)} %get-tuple-element.89), channel_id=1, source_target_pairs={{0,2},{1,3},{2,0},{3,1},{4,6},{5,7},{6,4},{7,5},{8,10},{9,11},{10,... | collective-permute-start | bytes 98312 | tf_op jit(solution)/shard_map/ppermute | solution.py:62
  (14 other events, 283.0 us)

commit v12 on v7

--- a/solution.py
+++ b/solution.py
@@ -394,7 +394,7 @@
     depth = weights[0].shape[0]
     core = place.core()
     for k in range(nx):
-        block = lax.rem(place.y() + k, nx)
+        block = lax.rem(place.y() + nx - 1 - k, nx)
         total[block] = dot(attn[:, at(core, depth)], weights[2 * k][...]) + dot(
             attn[:, at(1 - core, depth)], weights[2 * k + 1][...]
         )
@@ -569,7 +569,7 @@
         (qkv, w_up_sibling, w_down_sibling, w_out)
     )
     pieces = place.gather_z(qkv)
-    blocks = [place.transpose(tied, k) for k in range(nx)]
+    blocks = [place.transpose(tied, nx - 1 - k) for k in range(nx)]
     pack = max(1, min(group, 256 // slots))
     window = min(32, slots)
     new_keys, new_values, *messages = call(

time: 89.9 us -> 89.9 us (level)
  starting transfers between devices: 39.8 us -> 41.4 us
  waiting for transfers between devices: 35.6 us -> 34.2 us
    ppermute x2, starting transfers between devices: 1.85 us -> 4.91 us  [transpose(): return lax.ppermute(value, ('seq', 'req'), pairs)]
    ppermute x32, starting transfers between devices: 38 us -> 36.5 us  [move(): return lax.ppermute(value, ('seq', 'req'), pairs)]
    ppermute x32, waiting for transfers between devices: 35.6 us -> 34.2 us  [move(): return lax.ppermute(value, ('seq', 'req'), pairs)]
where the time goes in v12:
time: 89.9 us; the launch traced here: 89.6 us
  starting transfers between devices  41.4 us (46%)
  waiting for transfers between devices  34.2 us (38%)
  Pallas kernels  10.6 us (12%)
  other arithmetic  1.44 us (2%)
  local copies, waits for them, and re-layouts  0.97 us (1%)
  between operations  0.95 us (1%)
    ppermute x32, starting transfers between devices, move(): return lax.ppermute(value, ('seq', 'req'), pairs)  36.5 us
    ppermute x32, waiting for transfers between devices, move(): return lax.ppermute(value, ('seq', 'req'), pairs)  34.2 us
    pallas_call x14, Pallas kernels, call(): pl.pallas_call(kernel, name=name, out_shape=outs, in_specs=in_specs or [V...  10.6 us
    ppermute x2, starting transfers between devices, transpose(): return lax.ppermute(value, ('seq', 'req'), pairs)  4.91 us
  transfers between devices with their start and end apart: 34, of which 20 were waited for; matrix products, arithmetic and copies ran while one was open for 2% of the time, Pallas kernels for 8%

profile of v12, /device:TPU:0, one launch (start us, length us, event | category | flops | bytes accessed | tf_op | source)
XLA Modules:
  0.0 89.6 jit_solution(5388985514792115720)
XLA Ops:
  1.7 2.6 %collective-permute-start = (bf16[8,4,2048]{2,1,0:T(4,128)(2,1)}, bf16[8,4,2048]{2,1,0:T(4,128)(2,1)S(1)}, u32[]{:S(2)}, u32[]{:S(2)}) collective-permute-start(bf16[8,4,2048]{2,1,0:T(4,128)(2,1)} %refs_0_.3), channel_id=1, source_target_pairs={{0,2},{1,3},{2,0},{3,1},{4,6},{5,7},{6,4},{7,5},{8,10},{9,11},{10,... | collective-permute-start | bytes 393224 | tf_op jit(solution)/shard_map/ppermute | solution.py:62
  9.8 1.7 %collective-permute-start.5 = (bf16[32,768]{1,0:T(8,128)(2,1)S(1)}, bf16[32,768]{1,0:T(8,128)(2,1)S(1)}, u32[]{:S(2)}, u32[]{:S(2)}) collective-permute-start(bf16[32,768]{1,0:T(8,128)(2,1)S(1)} %get-tuple-element.53.refs_0_), channel_id=1, source_target_pairs={{0,4},{1,5},{2,6},{3,7},{4,0},{5,1},{6,2},{7,3},{8,12},{9,13},{10,... | collective-permute-start | bytes 147464 | tf_op jit(solution)/shard_map/ppermute | solution.py:62
  11.5 1.5 %collective-permute-start.6 = (bf16[32,768]{1,0:T(8,128)(2,1)S(1)}, bf16[32,768]{1,0:T(8,128)(2,1)S(1)}, u32[]{:S(2)}, u32[]{:S(2)}) collective-permute-start(bf16[32,768]{1,0:T(8,128)(2,1)S(1)} %get-tuple-element.54), channel_id=1, source_target_pairs={{0,6},{1,7},{2,4},{3,5},{4,2},{5,3},{6,0},{7,1},{8,14},{9,15},{10,... | collective-permute-start | bytes 147464 | tf_op jit(solution)/shard_map/ppermute | solution.py:62
  13.3 3.2 %caches.1 = (bf16[8,64,2048]{2,1,0:T(8,128)(2,1)}, bf16[8,64,2048]{2,1,0:T(8,128)(2,1)}, bf16[8,64,2048]{2,1,0:T(8,128)(2,1)S(1)}, bf16[8,64,2048]{2,1,0:T(8,128)(2,1)S(1)}, f32[8,128]{1,0:T(8,128)S(1)}) custom-call(bf16[8,64,2048]{2,1,0:T(8,128)(2,1)S(1)} %copy-done, bf16[8,64,2048]{2,1,0:T(8,128)(2,1)} %values_in), custom_call_target="tpu_custom_call" | custom-call | bytes 16777216 | tf_op jit(solution)/shard_map/caches/pallas_call | solution.py:104
  17.9 4.2 %collective-permute-start.12 = (bf16[512,256]{1,0:T(8,128)(2,1)S(1)}, bf16[512,256]{1,0:T(8,128)(2,1)S(1)}, u32[]{:S(2)}, u32[]{:S(2)}) collective-permute-start(bf16[512,256]{1,0:T(8,128)(2,1)S(1)} %copy-done.11), channel_id=1, source_target_pairs={{0,2},{1,3},{2,6},{3,7},{4,0},{5,1},{6,4},{7,5},{8,10},{9,11},{10,... | collective-permute-start | bytes 786440 | tf_op jit(solution)/shard_map/ppermute | solution.py:77
  22.1 3.6 %collective-permute-start.11 = (bf16[2,32,768]{2,1,0:T(8,128)(2,1)S(1)}, bf16[2,32,768]{2,1,0:T(8,128)(2,1)S(1)}, u32[]{:S(2)}, u32[]{:S(2)}) collective-permute-start(bf16[2,32,768]{2,1,0:T(8,128)(2,1)S(1)} %add_qkv.1.refs_0_), channel_id=1, source_target_pairs={{0,24},{1,25},{2,26},{3,27},{4,28},{5,29},{6,30},{7,31},{8,16},{9,... | collective-permute-start | bytes 294920 | tf_op jit(solution)/shard_map/ppermute | solution.py:62
  26.5 2.1 %collective-permute-done.11.refs_3_ = bf16[2,32,768]{2,1,0:T(8,128)(2,1)S(1)} collective-permute-done((bf16[2,32,768]{2,1,0:T(8,128)(2,1)S(1)}, bf16[2,32,768]{2,1,0:T(8,128)(2,1)S(1)}, u32[]{:S(2)}, u32[]{:S(2)}) %collective-permute-start.11) | collective-permute-done | bytes 98336 | tf_op jit(solution)/shard_map/ppermute | solution.py:62
  28.6 4.0 %collective-permute-done.10.refs_2_ = bf16[2,32,768]{2,1,0:T(8,128)(2,1)S(1)} collective-permute-done((bf16[2,32,768]{2,1,0:T(8,128)(2,1)S(1)}, bf16[2,32,768]{2,1,0:T(8,128)(2,1)S(1)}, u32[]{:S(2)}, u32[]{:S(2)}) %collective-permute-start.10) | collective-permute-done | bytes 98336 | tf_op jit(solution)/shard_map/ppermute | solution.py:62
  32.6 2.6 %attention.1 = (bf16[8,64,2048]{2,1,0:T(8,128)(2,1)}, bf16[8,64,2048]{2,1,0:T(8,128)(2,1)}, bf16[32,1152]{1,0:T(8,128)(2,1)S(1)}, bf16[32,1152]{1,0:T(8,128)(2,1)S(1)}) custom-call(bf16[2,32,768]{2,1,0:T(8,128)(2,1)S(1)} %add_qkv.1.refs_0_, bf16[2,32,768]{2,1,0:T(8,128)(2,1)S(1)} %collective-permute-done.9.refs_1_, ...), custom_call_target="tpu_custom_call", output_to_operand_aliasing={{0}: (7, {}), {1}: (8, {})} | custom-call | bytes 1048576 | tf_op jit(solution)/shard_map/attention/pallas_call | solution.py:104
  35.8 4.3 %collective-permute-done.14.refs_1_ = bf16[32,1152]{1,0:T(8,128)(2,1)S(1)} collective-permute-done((bf16[32,1152]{1,0:T(8,128)(2,1)S(1)}, bf16[32,1152]{1,0:T(8,128)(2,1)S(1)}, u32[]{:S(2)}, u32[]{:S(2)}) %collective-permute-start.14) | collective-permute-done | bytes 73760 | tf_op jit(solution)/shard_map/ppermute | solution.py:62
  40.4 2.1 %collective-permute-start.19 = (bf16[32,1152]{1,0:T(8,128)(2,1)S(1)}, bf16[32,1152]{1,0:T(8,128)(2,1)S(1)}, u32[]{:S(2)}, u32[]{:S(2)}) collective-permute-start(bf16[32,1152]{1,0:T(8,128)(2,1)S(1)} %merge_x.1.refs_0_), channel_id=1, source_target_pairs={{0,24},{1,25},{2,26},{3,27},{4,28},{5,29},{6,30},{7,31},{8,16},{9,... | collective-permute-start | bytes 221192 | tf_op jit(solution)/shard_map/ppermute | solution.py:62
  42.5 2.4 %collective-permute-start.17 = (bf16[32,1152]{1,0:T(8,128)(2,1)S(1)}, bf16[32,1152]{1,0:T(8,128)(2,1)S(1)}, u32[]{:S(2)}, u32[]{:S(2)}) collective-permute-start(bf16[32,1152]{1,0:T(8,128)(2,1)S(1)} %merge_x.1.refs_0_), channel_id=1, source_target_pairs={{0,8},{1,9},{2,10},{3,11},{4,12},{5,13},{6,14},{7,15},{8,0},{9,1},... | collective-permute-start | bytes 221192 | tf_op jit(solution)/shard_map/ppermute | solution.py:62
  44.9 2.6 %collective-permute-done.19.refs_3_ = bf16[32,1152]{1,0:T(8,128)(2,1)S(1)} collective-permute-done((bf16[32,1152]{1,0:T(8,128)(2,1)S(1)}, bf16[32,1152]{1,0:T(8,128)(2,1)S(1)}, u32[]{:S(2)}, u32[]{:S(2)}) %collective-permute-start.19) | collective-permute-done | bytes 73760 | tf_op jit(solution)/shard_map/ppermute | solution.py:62
  47.5 1.7 %collective-permute-done.18.refs_2_ = bf16[32,1152]{1,0:T(8,128)(2,1)S(1)} collective-permute-done((bf16[32,1152]{1,0:T(8,128)(2,1)S(1)}, bf16[32,1152]{1,0:T(8,128)(2,1)S(1)}, u32[]{:S(2)}, u32[]{:S(2)}) %collective-permute-start.18) | collective-permute-done | bytes 73760 | tf_op jit(solution)/shard_map/ppermute | solution.py:62
  49.9 1.5 %collective-permute-start.22 = (bf16[2,32,256]{2,1,0:T(8,128)(2,1)S(1)}, bf16[2,32,256]{2,1,0:T(8,128)(2,1)S(1)}, u32[]{:S(2)}, u32[]{:S(2)}) collective-permute-start(bf16[2,32,256]{2,1,0:T(8,128)(2,1)S(1)} %out.1.refs_0_), channel_id=1, source_target_pairs={{0,6},{1,7},{2,4},{3,5},{4,2},{5,3},{6,0},{7,1},{8,14},{9,15},{10,... | collective-permute-start | bytes 98312 | tf_op jit(solution)/shard_map/ppermute | solution.py:62
  51.8 1.7 %collective-permute-start.20 = (bf16[2,32,256]{2,1,0:T(8,128)(2,1)S(1)}, bf16[2,32,256]{2,1,0:T(8,128)(2,1)S(1)}, u32[]{:S(2)}, u32[]{:S(2)}) collective-permute-start(bf16[2,32,256]{2,1,0:T(8,128)(2,1)S(1)} %out.1.refs_0_), channel_id=1, source_target_pairs={{0,2},{1,3},{2,0},{3,1},{4,6},{5,7},{6,4},{7,5},{8,10},{9,11},{10,... | collective-permute-start | bytes 98312 | tf_op jit(solution)/shard_map/ppermute | solution.py:62
  53.4 1.3 %collective-permute-done.22.refs_3_ = bf16[2,32,256]{2,1,0:T(8,128)(2,1)S(1)} collective-permute-done((bf16[2,32,256]{2,1,0:T(8,128)(2,1)S(1)}, bf16[2,32,256]{2,1,0:T(8,128)(2,1)S(1)}, u32[]{:S(2)}, u32[]{:S(2)}) %collective-permute-start.22) | collective-permute-done | bytes 32800 | tf_op jit(solution)/shard_map/ppermute | solution.py:62
  55.7 2.4 %collective-permute-start.25 = (bf16[2,2,32,256]{3,2,1,0:T(8,128)(2,1)S(1)}, bf16[2,2,32,256]{3,2,1,0:T(8,128)(2,1)S(1)}, u32[]{:S(2)}, u32[]{:S(2)}) collective-permute-start(bf16[2,2,32,256]{3,2,1,0:T(8,128)(2,1)S(1)} %add_out.1.refs_2_), channel_id=1, source_target_pairs={{0,24},{1,25},{2,26},{3,27},{4,28},{5,29},{6,30},{7,31},{8,16},{9,... | collective-permute-start | bytes 196616 | tf_op jit(solution)/shard_map/ppermute | solution.py:62
  58.0 2.1 %collective-permute-start.23 = (bf16[2,2,32,256]{3,2,1,0:T(8,128)(2,1)S(1)}, bf16[2,2,32,256]{3,2,1,0:T(8,128)(2,1)S(1)}, u32[]{:S(2)}, u32[]{:S(2)}) collective-permute-start(bf16[2,2,32,256]{3,2,1,0:T(8,128)(2,1)S(1)} %add_out.1.refs_2_), channel_id=1, source_target_pairs={{0,8},{1,9},{2,10},{3,11},{4,12},{5,13},{6,14},{7,15},{8,0},{9,1},... | collective-permute-start | bytes 196616 | tf_op jit(solution)/shard_map/ppermute | solution.py:62
  60.1 1.7 %collective-permute-done.25.refs_5_ = bf16[2,2,32,256]{3,2,1,0:T(8,128)(2,1)S(1)} collective-permute-done((bf16[2,2,32,256]{3,2,1,0:T(8,128)(2,1)S(1)}, bf16[2,2,32,256]{3,2,1,0:T(8,128)(2,1)S(1)}, u32[]{:S(2)}, u32[]{:S(2)}) %collective-permute-start.25) | collective-permute-done | bytes 65568 | tf_op jit(solution)/shard_map/ppermute | solution.py:62
  61.8 1.4 %collective-permute-done.24.refs_4_ = bf16[2,2,32,256]{3,2,1,0:T(8,128)(2,1)S(1)} collective-permute-done((bf16[2,2,32,256]{3,2,1,0:T(8,128)(2,1)S(1)}, bf16[2,2,32,256]{3,2,1,0:T(8,128)(2,1)S(1)}, u32[]{:S(2)}, u32[]{:S(2)}) %collective-permute-start.24) | collective-permute-done | bytes 65568 | tf_op jit(solution)/shard_map/ppermute | solution.py:62
  64.1 1.7 %collective-permute-start.26 = (bf16[64,1024]{1,0:T(8,128)(2,1)S(1)}, bf16[64,1024]{1,0:T(8,128)(2,1)S(1)}, u32[]{:S(2)}, u32[]{:S(2)}) collective-permute-start(bf16[64,1024]{1,0:T(8,128)(2,1)S(1)} %get-tuple-element.78.refs_0_), channel_id=1, source_target_pairs={{0,2},{1,3},{2,0},{3,1},{4,6},{5,7},{6,4},{7,5},{8,10},{9,11},{10,... | collective-permute-start | bytes 393224 | tf_op jit(solution)/shard_map/ppermute | solution.py:62
  65.9 3.3 %collective-permute-done.26.refs_1_ = bf16[64,1024]{1,0:T(8,128)(2,1)S(1)} collective-permute-done((bf16[64,1024]{1,0:T(8,128)(2,1)S(1)}, bf16[64,1024]{1,0:T(8,128)(2,1)S(1)}, u32[]{:S(2)}, u32[]{:S(2)}) %collective-permute-start.26) | collective-permute-done | bytes 131104 | tf_op jit(solution)/shard_map/ppermute | solution.py:62
  69.7 1.7 %collective-permute-start.27 = (bf16[64,512]{1,0:T(8,128)(2,1)S(1)}, bf16[64,512]{1,0:T(8,128)(2,1)S(1)}, u32[]{:S(2)}, u32[]{:S(2)}) collective-permute-start(bf16[64,512]{1,0:T(8,128)(2,1)S(1)} %get-tuple-element.81), channel_id=1, source_target_pairs={{0,4},{1,5},{2,6},{3,7},{4,0},{5,1},{6,2},{7,3},{8,12},{9,13},{10,... | collective-permute-start | bytes 196616 | tf_op jit(solution)/shard_map/ppermute | solution.py:62
  71.4 2.7 %collective-permute-done.27.refs_1_ = bf16[64,512]{1,0:T(8,128)(2,1)S(1)} collective-permute-done((bf16[64,512]{1,0:T(8,128)(2,1)S(1)}, bf16[64,512]{1,0:T(8,128)(2,1)S(1)}, u32[]{:S(2)}, u32[]{:S(2)}) %collective-permute-start.27) | collective-permute-done | bytes 65568 | tf_op jit(solution)/shard_map/ppermute | solution.py:62
  74.0 2.3 %collective-permute-start.30 = (bf16[64,512]{1,0:T(8,128)(2,1)S(1)}, bf16[64,512]{1,0:T(8,128)(2,1)S(1)}, u32[]{:S(2)}, u32[]{:S(2)}) collective-permute-start(bf16[64,512]{1,0:T(8,128)(2,1)S(1)} %add_x.1.refs_0_), channel_id=1, source_target_pairs={{0,24},{1,25},{2,26},{3,27},{4,28},{5,29},{6,30},{7,31},{8,16},{9,... | collective-permute-start | bytes 196616 | tf_op jit(solution)/shard_map/ppermute | solution.py:62
  76.7 1.8 %collective-permute-start.28 = (bf16[64,512]{1,0:T(8,128)(2,1)S(1)}, bf16[64,512]{1,0:T(8,128)(2,1)S(1)}, u32[]{:S(2)}, u32[]{:S(2)}) collective-permute-start(bf16[64,512]{1,0:T(8,128)(2,1)S(1)} %add_x.1.refs_0_), channel_id=1, source_target_pairs={{0,8},{1,9},{2,10},{3,11},{4,12},{5,13},{6,14},{7,15},{8,0},{9,1},... | collective-permute-start | bytes 196616 | tf_op jit(solution)/shard_map/ppermute | solution.py:62
  78.5 1.7 %collective-permute-done.30.refs_3_ = bf16[64,512]{1,0:T(8,128)(2,1)S(1)} collective-permute-done((bf16[64,512]{1,0:T(8,128)(2,1)S(1)}, bf16[64,512]{1,0:T(8,128)(2,1)S(1)}, u32[]{:S(2)}, u32[]{:S(2)}) %collective-permute-start.30) | collective-permute-done | bytes 65568 | tf_op jit(solution)/shard_map/ppermute | solution.py:62
  80.2 1.8 %collective-permute-done.29.refs_2_ = bf16[64,512]{1,0:T(8,128)(2,1)S(1)} collective-permute-done((bf16[64,512]{1,0:T(8,128)(2,1)S(1)}, bf16[64,512]{1,0:T(8,128)(2,1)S(1)}, u32[]{:S(2)}, u32[]{:S(2)}) %collective-permute-start.29) | collective-permute-done | bytes 65568 | tf_op jit(solution)/shard_map/ppermute | solution.py:62
  82.0 1.4 %collective-permute-start.32 = (bf16[32,512]{1,0:T(8,128)(2,1)S(1)}, bf16[32,512]{1,0:T(8,128)(2,1)S(1)}, u32[]{:S(2)}, u32[]{:S(2)}) collective-permute-start(bf16[32,512]{1,0:T(8,128)(2,1)S(1)} %get-tuple-element.82.refs_0_), channel_id=1, source_target_pairs={{0,4},{1,5},{2,6},{3,7},{4,0},{5,1},{6,2},{7,3},{8,12},{9,13},{10,... | collective-permute-start | bytes 98312 | tf_op jit(solution)/shard_map/ppermute | solution.py:62
  83.4 1.5 %collective-permute-start.33 = (bf16[32,512]{1,0:T(8,128)(2,1)S(1)}, bf16[32,512]{1,0:T(8,128)(2,1)S(1)}, u32[]{:S(2)}, u32[]{:S(2)}) collective-permute-start(bf16[32,512]{1,0:T(8,128)(2,1)S(1)} %get-tuple-element.83), channel_id=1, source_target_pairs={{0,6},{1,7},{2,4},{3,5},{4,2},{5,3},{6,0},{7,1},{8,14},{9,15},{10,... | collective-permute-start | bytes 98312 | tf_op jit(solution)/shard_map/ppermute | solution.py:62
  86.0 2.2 %collective-permute-done.33.refs_3_ = bf16[32,512]{1,0:T(8,128)(2,1)S(1)} collective-permute-done((bf16[32,512]{1,0:T(8,128)(2,1)S(1)}, bf16[32,512]{1,0:T(8,128)(2,1)S(1)}, u32[]{:S(2)}, u32[]{:S(2)}) %collective-permute-start.33) | collective-permute-done | bytes 32800 | tf_op jit(solution)/shard_map/ppermute | solution.py:62
  (77 shorter events, 16.1 us)
Async XLA Ops:
  0.6 7.9 %collective-permute-start.1 = (bf16[512,256]{1,0:T(8,128)(2,1)}, bf16[512,256]{1,0:T(8,128)(2,1)S(1)}, u32[]{:S(2)}, u32[]{:S(2)}) collective-permute-start(bf16[512,256]{1,0:T(8,128)(2,1)} %refs_0_.2), channel_id=1, source_target_pairs={{0,1},{1,0},{2,3},{3,2},{4,5},{5,4},{6,7},{7,6},{8,9},{9,8},{10,11... | collective-permute-start | bytes 786440 | tf_op jit(solution)/shard_map/ppermute | solution.py:62
  1.2 7.4 %collective-permute-start.2 = (bf16[512,256]{1,0:T(8,128)(2,1)}, bf16[512,256]{1,0:T(8,128)(2,1)S(1)}, u32[]{:S(2)}, u32[]{:S(2)}) collective-permute-start(bf16[512,256]{1,0:T(8,128)(2,1)} %refs_1_.1), channel_id=1, source_target_pairs={{0,1},{1,0},{2,3},{3,2},{4,5},{5,4},{6,7},{7,6},{8,9},{9,8},{10,11... | collective-permute-start | bytes 786440 | tf_op jit(solution)/shard_map/ppermute | solution.py:62
  1.2 7.3 %collective-permute-start.3 = (bf16[512,256]{1,0:T(8,128)(2,1)}, bf16[512,256]{1,0:T(8,128)(2,1)S(1)}, u32[]{:S(2)}, u32[]{:S(2)}) collective-permute-start(bf16[512,256]{1,0:T(8,128)(2,1)} %refs_2_.2), channel_id=1, source_target_pairs={{0,1},{1,0},{2,3},{3,2},{4,5},{5,4},{6,7},{7,6},{8,9},{9,8},{10,11... | collective-permute-start | bytes 786440 | tf_op jit(solution)/shard_map/ppermute | solution.py:62
  1.7 6.9 %collective-permute-start = (bf16[8,4,2048]{2,1,0:T(4,128)(2,1)}, bf16[8,4,2048]{2,1,0:T(4,128)(2,1)S(1)}, u32[]{:S(2)}, u32[]{:S(2)}) collective-permute-start(bf16[8,4,2048]{2,1,0:T(4,128)(2,1)} %refs_0_.3), channel_id=1, source_target_pairs={{0,2},{1,3},{2,0},{3,1},{4,6},{5,7},{6,4},{7,5},{8,10},{9,11},{10,... | collective-permute-start | bytes 393224 | tf_op jit(solution)/shard_map/ppermute | solution.py:62
  9.2 7.9 %collective-permute-start.7 = (bf16[512,1024]{1,0:T(8,128)(2,1)}, bf16[512,1024]{1,0:T(8,128)(2,1)S(1)}, u32[]{:S(2)}, u32[]{:S(2)}) collective-permute-start(bf16[512,1024]{1,0:T(8,128)(2,1)} %refs_8_.1), channel_id=1, source_target_pairs={{0,1},{1,0},{2,3},{3,2},{4,5},{5,4},{6,7},{7,6},{8,9},{9,8},{10,11... | collective-permute-start | bytes 3145736 | tf_op jit(solution)/shard_map/ppermute | solution.py:62
  9.3 7.9 %collective-permute-start.8 = (bf16[1024,512]{1,0:T(8,128)(2,1)}, bf16[1024,512]{1,0:T(8,128)(2,1)S(1)}, u32[]{:S(2)}, u32[]{:S(2)}) collective-permute-start(bf16[1024,512]{1,0:T(8,128)(2,1)} %refs_2_.3), channel_id=1, source_target_pairs={{0,1},{1,0},{2,3},{3,2},{4,5},{5,4},{6,7},{7,6},{8,9},{9,8},{10,11... | collective-permute-start | bytes 3145736 | tf_op jit(solution)/shard_map/ppermute | solution.py:62
  9.8 6.7 %collective-permute-start.5 = (bf16[32,768]{1,0:T(8,128)(2,1)S(1)}, bf16[32,768]{1,0:T(8,128)(2,1)S(1)}, u32[]{:S(2)}, u32[]{:S(2)}) collective-permute-start(bf16[32,768]{1,0:T(8,128)(2,1)S(1)} %get-tuple-element.53.refs_0_), channel_id=1, source_target_pairs={{0,4},{1,5},{2,6},{3,7},{4,0},{5,1},{6,2},{7,3},{8,12},{9,13},{10,... | collective-permute-start | bytes 147464 | tf_op jit(solution)/shard_map/ppermute | solution.py:62
  11.5 5.0 %collective-permute-start.6 = (bf16[32,768]{1,0:T(8,128)(2,1)S(1)}, bf16[32,768]{1,0:T(8,128)(2,1)S(1)}, u32[]{:S(2)}, u32[]{:S(2)}) collective-permute-start(bf16[32,768]{1,0:T(8,128)(2,1)S(1)} %get-tuple-element.54), channel_id=1, source_target_pairs={{0,6},{1,7},{2,4},{3,5},{4,2},{5,3},{6,0},{7,1},{8,14},{9,15},{10,... | collective-permute-start | bytes 147464 | tf_op jit(solution)/shard_map/ppermute | solution.py:62
  13.0 4.1 %collective-permute-start.4 = (bf16[32,768]{1,0:T(8,128)(2,1)S(1)}, bf16[32,768]{1,0:T(8,128)(2,1)S(1)}, u32[]{:S(2)}, u32[]{:S(2)}) collective-permute-start(bf16[32,768]{1,0:T(8,128)(2,1)S(1)} %get-tuple-element.54), channel_id=1, source_target_pairs={{0,2},{1,3},{2,0},{3,1},{4,6},{5,7},{6,4},{7,5},{8,10},{9,11},{10,... | collective-permute-start | bytes 147464 | tf_op jit(solution)/shard_map/ppermute | solution.py:62
  17.2 18.0 %collective-permute-start.13 = (bf16[512,256]{1,0:T(8,128)(2,1)S(1)}, bf16[512,256]{1,0:T(8,128)(2,1)S(1)}, u32[]{:S(2)}, u32[]{:S(2)}) collective-permute-start(bf16[512,256]{1,0:T(8,128)(2,1)S(1)} %copy-done.11), channel_id=1, source_target_pairs={{0,0},{1,1},{2,4},{3,5},{4,2},{5,3},{6,6},{7,7},{8,8},{9,9},{10,12... | collective-permute-start | bytes 786440 | tf_op jit(solution)/shard_map/ppermute | solution.py:77
  17.9 17.3 %collective-permute-start.12 = (bf16[512,256]{1,0:T(8,128)(2,1)S(1)}, bf16[512,256]{1,0:T(8,128)(2,1)S(1)}, u32[]{:S(2)}, u32[]{:S(2)}) collective-permute-start(bf16[512,256]{1,0:T(8,128)(2,1)S(1)} %copy-done.11), channel_id=1, source_target_pairs={{0,2},{1,3},{2,6},{3,7},{4,0},{5,1},{6,4},{7,5},{8,10},{9,11},{10,... | collective-permute-start | bytes 786440 | tf_op jit(solution)/shard_map/ppermute | solution.py:77
  22.1 6.5 %collective-permute-start.11 = (bf16[2,32,768]{2,1,0:T(8,128)(2,1)S(1)}, bf16[2,32,768]{2,1,0:T(8,128)(2,1)S(1)}, u32[]{:S(2)}, u32[]{:S(2)}) collective-permute-start(bf16[2,32,768]{2,1,0:T(8,128)(2,1)S(1)} %add_qkv.1.refs_0_), channel_id=1, source_target_pairs={{0,24},{1,25},{2,26},{3,27},{4,28},{5,29},{6,30},{7,31},{8,16},{9,... | collective-permute-start | bytes 294920 | tf_op jit(solution)/shard_map/ppermute | solution.py:62
  25.7 6.9 %collective-permute-start.10 = (bf16[2,32,768]{2,1,0:T(8,128)(2,1)S(1)}, bf16[2,32,768]{2,1,0:T(8,128)(2,1)S(1)}, u32[]{:S(2)}, u32[]{:S(2)}) collective-permute-start(bf16[2,32,768]{2,1,0:T(8,128)(2,1)S(1)} %add_qkv.1.refs_0_), channel_id=1, source_target_pairs={{0,16},{1,17},{2,18},{3,19},{4,20},{5,21},{6,22},{7,23},{8,24},{9,... | collective-permute-start | bytes 294920 | tf_op jit(solution)/shard_map/ppermute | solution.py:62
  25.7 6.9 %collective-permute-start.9 = (bf16[2,32,768]{2,1,0:T(8,128)(2,1)S(1)}, bf16[2,32,768]{2,1,0:T(8,128)(2,1)S(1)}, u32[]{:S(2)}, u32[]{:S(2)}) collective-permute-start(bf16[2,32,768]{2,1,0:T(8,128)(2,1)S(1)} %add_qkv.1.refs_0_), channel_id=1, source_target_pairs={{0,8},{1,9},{2,10},{3,11},{4,12},{5,13},{6,14},{7,15},{8,0},{9,1},... | collective-permute-start | bytes 294920 | tf_op jit(solution)/shard_map/ppermute | solution.py:62
  35.2 5.2 %collective-permute-start.15 = (bf16[512,256]{1,0:T(8,128)(2,1)S(1)}, bf16[512,256]{1,0:T(8,128)(2,1)S(1)}, u32[]{:S(2)}, u32[]{:S(2)}) collective-permute-start(bf16[512,256]{1,0:T(8,128)(2,1)S(1)} %collective-permute-done.12.refs_0_), channel_id=1, source_target_pairs={{0,1},{1,0},{2,3},{3,2},{4,5},{5,4},{6,7},{7,6},{8,9},{9,8},{10,11... | collective-permute-start | bytes 786440 | tf_op jit(solution)/shard_map/ppermute | solution.py:62
  35.3 5.1 %collective-permute-start.16 = (bf16[512,256]{1,0:T(8,128)(2,1)S(1)}, bf16[512,256]{1,0:T(8,128)(2,1)S(1)}, u32[]{:S(2)}, u32[]{:S(2)}) collective-permute-start(bf16[512,256]{1,0:T(8,128)(2,1)S(1)} %collective-permute-done.13.refs_2_), channel_id=1, source_target_pairs={{0,1},{1,0},{2,3},{3,2},{4,5},{5,4},{6,7},{7,6},{8,9},{9,8},{10,11... | collective-permute-start | bytes 786440 | tf_op jit(solution)/shard_map/ppermute | solution.py:62
  35.8 4.4 %collective-permute-start.14 = (bf16[32,1152]{1,0:T(8,128)(2,1)S(1)}, bf16[32,1152]{1,0:T(8,128)(2,1)S(1)}, u32[]{:S(2)}, u32[]{:S(2)}) collective-permute-start(bf16[32,1152]{1,0:T(8,128)(2,1)S(1)} %get-tuple-element.69), channel_id=1, source_target_pairs={{0,4},{1,5},{2,6},{3,7},{4,0},{5,1},{6,2},{7,3},{8,12},{9,13},{10,... | collective-permute-start | bytes 221192 | tf_op jit(solution)/shard_map/ppermute | solution.py:62
  40.4 7.0 %collective-permute-start.19 = (bf16[32,1152]{1,0:T(8,128)(2,1)S(1)}, bf16[32,1152]{1,0:T(8,128)(2,1)S(1)}, u32[]{:S(2)}, u32[]{:S(2)}) collective-permute-start(bf16[32,1152]{1,0:T(8,128)(2,1)S(1)} %merge_x.1.refs_0_), channel_id=1, source_target_pairs={{0,24},{1,25},{2,26},{3,27},{4,28},{5,29},{6,30},{7,31},{8,16},{9,... | collective-permute-start | bytes 221192 | tf_op jit(solution)/shard_map/ppermute | solution.py:62
  42.5 6.6 %collective-permute-start.18 = (bf16[32,1152]{1,0:T(8,128)(2,1)S(1)}, bf16[32,1152]{1,0:T(8,128)(2,1)S(1)}, u32[]{:S(2)}, u32[]{:S(2)}) collective-permute-start(bf16[32,1152]{1,0:T(8,128)(2,1)S(1)} %merge_x.1.refs_0_), channel_id=1, source_target_pairs={{0,16},{1,17},{2,18},{3,19},{4,20},{5,21},{6,22},{7,23},{8,24},{9,... | collective-permute-start | bytes 221192 | tf_op jit(solution)/shard_map/ppermute | solution.py:62
  42.5 6.6 %collective-permute-start.17 = (bf16[32,1152]{1,0:T(8,128)(2,1)S(1)}, bf16[32,1152]{1,0:T(8,128)(2,1)S(1)}, u32[]{:S(2)}, u32[]{:S(2)}) collective-permute-start(bf16[32,1152]{1,0:T(8,128)(2,1)S(1)} %merge_x.1.refs_0_), channel_id=1, source_target_pairs={{0,8},{1,9},{2,10},{3,11},{4,12},{5,13},{6,14},{7,15},{8,0},{9,1},... | collective-permute-start | bytes 221192 | tf_op jit(solution)/shard_map/ppermute | solution.py:62
  49.9 4.9 %collective-permute-start.22 = (bf16[2,32,256]{2,1,0:T(8,128)(2,1)S(1)}, bf16[2,32,256]{2,1,0:T(8,128)(2,1)S(1)}, u32[]{:S(2)}, u32[]{:S(2)}) collective-permute-start(bf16[2,32,256]{2,1,0:T(8,128)(2,1)S(1)} %out.1.refs_0_), channel_id=1, source_target_pairs={{0,6},{1,7},{2,4},{3,5},{4,2},{5,3},{6,0},{7,1},{8,14},{9,15},{10,... | collective-permute-start | bytes 98312 | tf_op jit(solution)/shard_map/ppermute | solution.py:62
  51.3 3.9 %collective-permute-start.21 = (bf16[2,32,256]{2,1,0:T(8,128)(2,1)S(1)}, bf16[2,32,256]{2,1,0:T(8,128)(2,1)S(1)}, u32[]{:S(2)}, u32[]{:S(2)}) collective-permute-start(bf16[2,32,256]{2,1,0:T(8,128)(2,1)S(1)} %out.1.refs_0_), channel_id=1, source_target_pairs={{0,4},{1,5},{2,6},{3,7},{4,0},{5,1},{6,2},{7,3},{8,12},{9,13},{10,... | collective-permute-start | bytes 98312 | tf_op jit(solution)/shard_map/ppermute | solution.py:62
  55.7 6.1 %collective-permute-start.25 = (bf16[2,2,32,256]{3,2,1,0:T(8,128)(2,1)S(1)}, bf16[2,2,32,256]{3,2,1,0:T(8,128)(2,1)S(1)}, u32[]{:S(2)}, u32[]{:S(2)}) collective-permute-start(bf16[2,2,32,256]{3,2,1,0:T(8,128)(2,1)S(1)} %add_out.1.refs_2_), channel_id=1, source_target_pairs={{0,24},{1,25},{2,26},{3,27},{4,28},{5,29},{6,30},{7,31},{8,16},{9,... | collective-permute-start | bytes 196616 | tf_op jit(solution)/shard_map/ppermute | solution.py:62
  58.0 5.2 %collective-permute-start.24 = (bf16[2,2,32,256]{3,2,1,0:T(8,128)(2,1)S(1)}, bf16[2,2,32,256]{3,2,1,0:T(8,128)(2,1)S(1)}, u32[]{:S(2)}, u32[]{:S(2)}) collective-permute-start(bf16[2,2,32,256]{3,2,1,0:T(8,128)(2,1)S(1)} %add_out.1.refs_2_), channel_id=1, source_target_pairs={{0,16},{1,17},{2,18},{3,19},{4,20},{5,21},{6,22},{7,23},{8,24},{9,... | collective-permute-start | bytes 196616 | tf_op jit(solution)/shard_map/ppermute | solution.py:62
  58.0 5.2 %collective-permute-start.23 = (bf16[2,2,32,256]{3,2,1,0:T(8,128)(2,1)S(1)}, bf16[2,2,32,256]{3,2,1,0:T(8,128)(2,1)S(1)}, u32[]{:S(2)}, u32[]{:S(2)}) collective-permute-start(bf16[2,2,32,256]{3,2,1,0:T(8,128)(2,1)S(1)} %add_out.1.refs_2_), channel_id=1, source_target_pairs={{0,8},{1,9},{2,10},{3,11},{4,12},{5,13},{6,14},{7,15},{8,0},{9,1},... | collective-permute-start | bytes 196616 | tf_op jit(solution)/shard_map/ppermute | solution.py:62
  64.1 5.0 %collective-permute-start.26 = (bf16[64,1024]{1,0:T(8,128)(2,1)S(1)}, bf16[64,1024]{1,0:T(8,128)(2,1)S(1)}, u32[]{:S(2)}, u32[]{:S(2)}) collective-permute-start(bf16[64,1024]{1,0:T(8,128)(2,1)S(1)} %get-tuple-element.78.refs_0_), channel_id=1, source_target_pairs={{0,2},{1,3},{2,0},{3,1},{4,6},{5,7},{6,4},{7,5},{8,10},{9,11},{10,... | collective-permute-start | bytes 393224 | tf_op jit(solution)/shard_map/ppermute | solution.py:62
  69.7 4.3 %collective-permute-start.27 = (bf16[64,512]{1,0:T(8,128)(2,1)S(1)}, bf16[64,512]{1,0:T(8,128)(2,1)S(1)}, u32[]{:S(2)}, u32[]{:S(2)}) collective-permute-start(bf16[64,512]{1,0:T(8,128)(2,1)S(1)} %get-tuple-element.81), channel_id=1, source_target_pairs={{0,4},{1,5},{2,6},{3,7},{4,0},{5,1},{6,2},{7,3},{8,12},{9,13},{10,... | collective-permute-start | bytes 196616 | tf_op jit(solution)/shard_map/ppermute | solution.py:62
  74.0 6.1 %collective-permute-start.30 = (bf16[64,512]{1,0:T(8,128)(2,1)S(1)}, bf16[64,512]{1,0:T(8,128)(2,1)S(1)}, u32[]{:S(2)}, u32[]{:S(2)}) collective-permute-start(bf16[64,512]{1,0:T(8,128)(2,1)S(1)} %add_x.1.refs_0_), channel_id=1, source_target_pairs={{0,24},{1,25},{2,26},{3,27},{4,28},{5,29},{6,30},{7,31},{8,16},{9,... | collective-permute-start | bytes 196616 | tf_op jit(solution)/shard_map/ppermute | solution.py:62
  76.4 5.6 %collective-permute-start.29 = (bf16[64,512]{1,0:T(8,128)(2,1)S(1)}, bf16[64,512]{1,0:T(8,128)(2,1)S(1)}, u32[]{:S(2)}, u32[]{:S(2)}) collective-permute-start(bf16[64,512]{1,0:T(8,128)(2,1)S(1)} %add_x.1.refs_0_), channel_id=1, source_target_pairs={{0,16},{1,17},{2,18},{3,19},{4,20},{5,21},{6,22},{7,23},{8,24},{9,... | collective-permute-start | bytes 196616 | tf_op jit(solution)/shard_map/ppermute | solution.py:62
  76.7 5.2 %collective-permute-start.28 = (bf16[64,512]{1,0:T(8,128)(2,1)S(1)}, bf16[64,512]{1,0:T(8,128)(2,1)S(1)}, u32[]{:S(2)}, u32[]{:S(2)}) collective-permute-start(bf16[64,512]{1,0:T(8,128)(2,1)S(1)} %add_x.1.refs_0_), channel_id=1, source_target_pairs={{0,8},{1,9},{2,10},{3,11},{4,12},{5,13},{6,14},{7,15},{8,0},{9,1},... | collective-permute-start | bytes 196616 | tf_op jit(solution)/shard_map/ppermute | solution.py:62
  82.0 4.0 %collective-permute-start.32 = (bf16[32,512]{1,0:T(8,128)(2,1)S(1)}, bf16[32,512]{1,0:T(8,128)(2,1)S(1)}, u32[]{:S(2)}, u32[]{:S(2)}) collective-permute-start(bf16[32,512]{1,0:T(8,128)(2,1)S(1)} %get-tuple-element.82.refs_0_), channel_id=1, source_target_pairs={{0,4},{1,5},{2,6},{3,7},{4,0},{5,1},{6,2},{7,3},{8,12},{9,13},{10,... | collective-permute-start | bytes 98312 | tf_op jit(solution)/shard_map/ppermute | solution.py:62
  83.4 4.8 %collective-permute-start.33 = (bf16[32,512]{1,0:T(8,128)(2,1)S(1)}, bf16[32,512]{1,0:T(8,128)(2,1)S(1)}, u32[]{:S(2)}, u32[]{:S(2)}) collective-permute-start(bf16[32,512]{1,0:T(8,128)(2,1)S(1)} %get-tuple-element.83), channel_id=1, source_target_pairs={{0,6},{1,7},{2,4},{3,5},{4,2},{5,3},{6,0},{7,1},{8,14},{9,15},{10,... | collective-permute-start | bytes 98312 | tf_op jit(solution)/shard_map/ppermute | solution.py:62
  (14 other events, 274.7 us)

commit v13 on v7

--- a/solution.py
+++ b/solution.py
@@ -184,7 +184,7 @@
         out[place.x_before(dx)] = total.astype(BF16)
 
 
-def cache_kernel(keys_in, values_in, keys_out, values_out, keys, values, mark, in_sems, out_sems):
+def cache_kernel(keys_in, values_in, keys_out, values_out, keys, values, in_sems, out_sems):
     group = keys.shape[0]
     arrays = ((keys_in, keys, keys_out), (values_in, values, values_out))
     coming = [
@@ -199,7 +199,6 @@
     ]
     for copy in coming:
         copy.start()
-    mark[...] = jnp.zeros_like(mark)
     for arrived, copy in zip(coming, going):
         arrived.wait()
         copy.start()
@@ -376,21 +375,17 @@
     out[:, share:] = tile.astype(BF16)
 
 
-def merge_z_kernel(place, heads, *refs):
-    share = refs[0].shape[1] - LANES
-    count = share // HEAD
-    out = refs[-1]
-    messages = [r[...] for r in refs[:-1]]
-    _, total, scales = merge(messages, heads, share)
-    out[...] = sum(
-        m[:, :share].astype(F32) * expand(s / total, count) for m, s in zip(messages, scales)
+def out_kernel(place, heads, *refs):
+    nx, nz = place.nx, place.nz
+    messages = [r[...] for r in refs[:nz]]
+    weights = refs[nz : nz + 2 * nx]
+    bias, out, total, attn = refs[nz + 2 * nx :]
+    share = attn.shape[1]
+    _, whole, scales = merge(messages, heads, share)
+    attn[...] = sum(
+        m[:, :share].astype(F32) * expand(s / whole, share // HEAD)
+        for m, s in zip(messages, scales)
     ).astype(BF16)
-
-
-def out_kernel(place, attn, *refs):
-    nx = place.nx
-    weights = refs[: 2 * nx]
-    bias, out, total = refs[2 * nx :]
     depth = weights[0].shape[0]
     core = place.core()
     for k in range(nx):
@@ -547,26 +542,26 @@
     *parts, tied_up, tied_down = lax.optimization_barrier((*parts, w_up, w_down))
     w_up_sibling = place.move(tied_up, dc=1)
     w_down_sibling = place.move(tied_down, dc=1)
-    parts, tied_keys, tied_values = lax.optimization_barrier((parts, cache_keys, cache_values))
-    new_keys, new_values, keys, values, mark = call(
+    qkv = call(
+        bind(add_columns_kernel, place),
+        "add_qkv",
+        spread(parts),
+        shape((nx, rows, 3 * cols)),
+    )
+    qkv, w_up_sibling, w_down_sibling, tied = lax.optimization_barrier(
+        (qkv, w_up_sibling, w_down_sibling, w_out)
+    )
+    qkv, tied_keys, tied_values = lax.optimization_barrier((qkv, cache_keys, cache_values))
+    new_keys, new_values, keys, values = call(
         cache_kernel,
         "caches",
         [tied_keys, tied_values],
-        [shape(cache_keys.shape)] * 4 + [shape((8, LANES), F32)],
+        [shape(cache_keys.shape)] * 4,
         in_specs=[HBM, HBM],
-        out_specs=[HBM, HBM, VMEM, VMEM, VMEM],
+        out_specs=[HBM, HBM, VMEM, VMEM],
         scratch=[pltpu.SemaphoreType.DMA((2, group)), pltpu.SemaphoreType.DMA((2, group))],
         moved=16 * 1024 * 1024,
         limit=46,
-    )
-    qkv = call(
-        bind(add_columns_kernel, place),
-        "add_qkv",
-        [*spread(parts), mark],
-        shape((nx, rows, 3 * cols)),
-    )
-    qkv, w_up_sibling, w_down_sibling, tied = lax.optimization_barrier(
-        (qkv, w_up_sibling, w_down_sibling, w_out)
     )
     pieces = place.gather_z(qkv)
     blocks = [place.transpose(tied, k) for k in range(nx)]
@@ -602,13 +597,12 @@
     )
     merged, *w_outs = lax.optimization_barrier((merged, *w_outs))
     pieces = place.gather_z(merged)
-    attn = call(bind(merge_z_kernel, place, heads), "merge_z", pieces, shape((rows, share)))
     out_part = call(
-        bind(out_kernel, place),
+        bind(out_kernel, place, heads),
         "out",
-        [attn, *w_outs, row(b_out)],
+        [*pieces, *w_outs, row(b_out)],
         shape((nx, rows, cols)),
-        scratch=[pltpu.VMEM((nx, rows, cols), F32)],
+        scratch=[pltpu.VMEM((nx, rows, cols), F32), pltpu.VMEM((rows, share), BF16)],
     )
     projected = call(
         bind(add_out_kernel, place),

time: 89.9 us -> 92.7 us (1.031)
  waiting for transfers between devices: 35.6 us -> 40.1 us
  starting transfers between devices: 39.8 us -> 38.1 us
    ppermute x32, waiting for transfers between devices: 35.6 us -> 40.1 us  [move(): return lax.ppermute(value, ('seq', 'req'), pairs)]
    ppermute x32, starting transfers between devices: 38 us -> 34.2 us  [move(): return lax.ppermute(value, ('seq', 'req'), pairs)]
    ppermute x2, starting transfers between devices: 1.85 us -> 3.96 us  [transpose(): return lax.ppermute(value, ('seq', 'req'), pairs)]
    pallas_call x14 -> x13, Pallas kernels: 10.7 us -> 10.8 us  [call(): pl.pallas_call(kernel, name=name, out_shape=outs, in_specs=in_specs or [V...]
  transfers between devices with their start and end apart: 34 -> 34, of which waited for: 20 -> 22; matrix products, arithmetic and copies ran while one was open for 2% -> 2% of each run, Pallas kernels for 8% -> 8%
where the time goes in v13:
time: 92.7 us; the launch traced here: 92.4 us
  waiting for transfers between devices  40.1 us (43%)
  starting transfers between devices  38.1 us (41%)
  Pallas kernels  10.8 us (12%)
  other arithmetic  1.44 us (2%)
  local copies, waits for them, and re-layouts  0.96 us (1%)
    ppermute x32, waiting for transfers between devices, move(): return lax.ppermute(value, ('seq', 'req'), pairs)  40.1 us
    ppermute x32, starting transfers between devices, move(): return lax.ppermute(value, ('seq', 'req'), pairs)  34.2 us
    pallas_call x13, Pallas kernels, call(): pl.pallas_call(kernel, name=name, out_shape=outs, in_specs=in_specs or [V...  10.8 us
    ppermute x2, starting transfers between devices, transpose(): return lax.ppermute(value, ('seq', 'req'), pairs)  3.96 us
  transfers between devices with their start and end apart: 34, of which 22 were waited for; matrix products, arithmetic and copies ran while one was open for 2% of the time, Pallas kernels for 8%

profile of v13, /device:TPU:0, one launch (start us, length us, event | category | flops | bytes accessed | tf_op | source)
XLA Modules:
  0.0 92.4 jit_solution(7829392685270243135)
XLA Ops:
  1.7 2.6 %collective-permute-start = (bf16[8,4,2048]{2,1,0:T(4,128)(2,1)}, bf16[8,4,2048]{2,1,0:T(4,128)(2,1)S(1)}, u32[]{:S(2)}, u32[]{:S(2)}) collective-permute-start(bf16[8,4,2048]{2,1,0:T(4,128)(2,1)} %refs_0_.3), channel_id=1, source_target_pairs={{0,2},{1,3},{2,0},{3,1},{4,6},{5,7},{6,4},{7,5},{8,10},{9,11},{10,... | collective-permute-start | bytes 393224 | tf_op jit(solution)/shard_map/ppermute | solution.py:62
  5.9 1.2 %norm.1 = (bf16[32,2048]{1,0:T(8,128)(2,1)S(1)}, bf16[512,256]{1,0:T(8,128)(2,1)S(1)}, bf16[512,256]{1,0:T(8,128)(2,1)S(1)}, bf16[512,256]{1,0:T(8,128)(2,1)S(1)}) custom-call(bf16[8,4,2048]{2,1,0:T(4,128)(2,1)S(1)} %copy-done.3, f32[1,4096]{1,0:T(1,128)S(1)} %bitcast.6, bf16[512,256]{1,0:T(8,128)(2,1)} %refs_0_.2, bf16[512,256]{1,0:T(8,128)(2,1)} %refs_1_.1, ...), custom_call_target="tpu_custom_call" | custom-call | bytes 1048576 | tf_op jit(solution)/shard_map/norm/pallas_call | solution.py:104
  9.8 1.8 %collective-permute-start.4 = (bf16[32,768]{1,0:T(8,128)(2,1)S(1)}, bf16[32,768]{1,0:T(8,128)(2,1)S(1)}, u32[]{:S(2)}, u32[]{:S(2)}) collective-permute-start(bf16[32,768]{1,0:T(8,128)(2,1)S(1)} %get-tuple-element.50), channel_id=1, source_target_pairs={{0,2},{1,3},{2,0},{3,1},{4,6},{5,7},{6,4},{7,5},{8,10},{9,11},{10,... | collective-permute-start | bytes 147464 | tf_op jit(solution)/shard_map/ppermute | solution.py:62
  11.5 1.5 %collective-permute-start.5 = (bf16[32,768]{1,0:T(8,128)(2,1)S(1)}, bf16[32,768]{1,0:T(8,128)(2,1)S(1)}, u32[]{:S(2)}, u32[]{:S(2)}) collective-permute-start(bf16[32,768]{1,0:T(8,128)(2,1)S(1)} %get-tuple-element.49.refs_0_), channel_id=1, source_target_pairs={{0,4},{1,5},{2,6},{3,7},{4,0},{5,1},{6,2},{7,3},{8,12},{9,13},{10,... | collective-permute-start | bytes 147464 | tf_op jit(solution)/shard_map/ppermute | solution.py:62
  13.9 2.3 %collective-permute-done.5.refs_2_ = bf16[32,768]{1,0:T(8,128)(2,1)S(1)} collective-permute-done((bf16[32,768]{1,0:T(8,128)(2,1)S(1)}, bf16[32,768]{1,0:T(8,128)(2,1)S(1)}, u32[]{:S(2)}, u32[]{:S(2)}) %collective-permute-start.5) | collective-permute-done | bytes 49184 | tf_op jit(solution)/shard_map/ppermute | solution.py:62
  16.1 1.9 %collective-permute-done.6.refs_3_ = bf16[32,768]{1,0:T(8,128)(2,1)S(1)} collective-permute-done((bf16[32,768]{1,0:T(8,128)(2,1)S(1)}, bf16[32,768]{1,0:T(8,128)(2,1)S(1)}, u32[]{:S(2)}, u32[]{:S(2)}) %collective-permute-start.6) | collective-permute-done | bytes 49184 | tf_op jit(solution)/shard_map/ppermute | solution.py:62
  18.8 3.3 %collective-permute-start.13 = (bf16[512,256]{1,0:T(8,128)(2,1)S(1)}, bf16[512,256]{1,0:T(8,128)(2,1)S(1)}, u32[]{:S(2)}, u32[]{:S(2)}) collective-permute-start(bf16[512,256]{1,0:T(8,128)(2,1)S(1)} %copy-done.11), channel_id=1, source_target_pairs={{0,2},{1,3},{2,6},{3,7},{4,0},{5,1},{6,4},{7,5},{8,10},{9,11},{10,... | collective-permute-start | bytes 786440 | tf_op jit(solution)/shard_map/ppermute | solution.py:77
  22.1 2.6 %collective-permute-start.10 = (bf16[2,32,768]{2,1,0:T(8,128)(2,1)S(1)}, bf16[2,32,768]{2,1,0:T(8,128)(2,1)S(1)}, u32[]{:S(2)}, u32[]{:S(2)}) collective-permute-start(bf16[2,32,768]{2,1,0:T(8,128)(2,1)S(1)} %add_qkv.1.refs_0_), channel_id=1, source_target_pairs={{0,16},{1,17},{2,18},{3,19},{4,20},{5,21},{6,22},{7,23},{8,24},{9,... | collective-permute-start | bytes 294920 | tf_op jit(solution)/shard_map/ppermute | solution.py:62
  24.7 1.3 %collective-permute-start.11 = (bf16[2,32,768]{2,1,0:T(8,128)(2,1)S(1)}, bf16[2,32,768]{2,1,0:T(8,128)(2,1)S(1)}, u32[]{:S(2)}, u32[]{:S(2)}) collective-permute-start(bf16[2,32,768]{2,1,0:T(8,128)(2,1)S(1)} %add_qkv.1.refs_0_), channel_id=1, source_target_pairs={{0,24},{1,25},{2,26},{3,27},{4,28},{5,29},{6,30},{7,31},{8,16},{9,... | collective-permute-start | bytes 294920 | tf_op jit(solution)/shard_map/ppermute | solution.py:62
  26.2 3.2 %caches.1 = (bf16[8,64,2048]{2,1,0:T(8,128)(2,1)}, bf16[8,64,2048]{2,1,0:T(8,128)(2,1)}, bf16[8,64,2048]{2,1,0:T(8,128)(2,1)S(1)}, bf16[8,64,2048]{2,1,0:T(8,128)(2,1)S(1)}) custom-call(bf16[8,64,2048]{2,1,0:T(8,128)(2,1)S(1)} %copy-done, bf16[8,64,2048]{2,1,0:T(8,128)(2,1)} %values_in), custom_call_target="tpu_custom_call" | custom-call | bytes 16777216 | tf_op jit(solution)/shard_map/caches/pallas_call | solution.py:104
  29.4 2.2 %collective-permute-done.10.refs_2_ = bf16[2,32,768]{2,1,0:T(8,128)(2,1)S(1)} collective-permute-done((bf16[2,32,768]{2,1,0:T(8,128)(2,1)S(1)}, bf16[2,32,768]{2,1,0:T(8,128)(2,1)S(1)}, u32[]{:S(2)}, u32[]{:S(2)}) %collective-permute-start.10) | collective-permute-done | bytes 98336 | tf_op jit(solution)/shard_map/ppermute | solution.py:62
  32.3 2.8 %attention.1 = (bf16[8,64,2048]{2,1,0:T(8,128)(2,1)}, bf16[8,64,2048]{2,1,0:T(8,128)(2,1)}, bf16[32,1152]{1,0:T(8,128)(2,1)S(1)}, bf16[32,1152]{1,0:T(8,128)(2,1)S(1)}) custom-call(bf16[2,32,768]{2,1,0:T(8,128)(2,1)S(1)} %add_qkv.1.refs_0_, bf16[2,32,768]{2,1,0:T(8,128)(2,1)S(1)} %collective-permute-done.9.refs_1_, ...), custom_call_target="tpu_custom_call", output_to_operand_aliasing={{0}: (7, {}), {1}: (8, {})} | custom-call | bytes 1048576 | tf_op jit(solution)/shard_map/attention/pallas_call | solution.py:104
  35.7 4.3 %collective-permute-done.14.refs_1_ = bf16[32,1152]{1,0:T(8,128)(2,1)S(1)} collective-permute-done((bf16[32,1152]{1,0:T(8,128)(2,1)S(1)}, bf16[32,1152]{1,0:T(8,128)(2,1)S(1)}, u32[]{:S(2)}, u32[]{:S(2)}) %collective-permute-start.14) | collective-permute-done | bytes 73760 | tf_op jit(solution)/shard_map/ppermute | solution.py:62
  40.7 2.1 %collective-permute-start.18 = (bf16[32,1152]{1,0:T(8,128)(2,1)S(1)}, bf16[32,1152]{1,0:T(8,128)(2,1)S(1)}, u32[]{:S(2)}, u32[]{:S(2)}) collective-permute-start(bf16[32,1152]{1,0:T(8,128)(2,1)S(1)} %merge_x.1.refs_0_), channel_id=1, source_target_pairs={{0,16},{1,17},{2,18},{3,19},{4,20},{5,21},{6,22},{7,23},{8,24},{9,... | collective-permute-start | bytes 221192 | tf_op jit(solution)/shard_map/ppermute | solution.py:62
  42.8 2.0 %collective-permute-start.19 = (bf16[32,1152]{1,0:T(8,128)(2,1)S(1)}, bf16[32,1152]{1,0:T(8,128)(2,1)S(1)}, u32[]{:S(2)}, u32[]{:S(2)}) collective-permute-start(bf16[32,1152]{1,0:T(8,128)(2,1)S(1)} %merge_x.1.refs_0_), channel_id=1, source_target_pairs={{0,24},{1,25},{2,26},{3,27},{4,28},{5,29},{6,30},{7,31},{8,16},{9,... | collective-permute-start | bytes 221192 | tf_op jit(solution)/shard_map/ppermute | solution.py:62
  44.8 3.3 %collective-permute-done.18.refs_2_ = bf16[32,1152]{1,0:T(8,128)(2,1)S(1)} collective-permute-done((bf16[32,1152]{1,0:T(8,128)(2,1)S(1)}, bf16[32,1152]{1,0:T(8,128)(2,1)S(1)}, u32[]{:S(2)}, u32[]{:S(2)}) %collective-permute-start.18) | collective-permute-done | bytes 73760 | tf_op jit(solution)/shard_map/ppermute | solution.py:62
  50.4 1.4 %collective-permute-start.21 = (bf16[2,32,256]{2,1,0:T(8,128)(2,1)S(1)}, bf16[2,32,256]{2,1,0:T(8,128)(2,1)S(1)}, u32[]{:S(2)}, u32[]{:S(2)}) collective-permute-start(bf16[2,32,256]{2,1,0:T(8,128)(2,1)S(1)} %out.1.refs_0_), channel_id=1, source_target_pairs={{0,4},{1,5},{2,6},{3,7},{4,0},{5,1},{6,2},{7,3},{8,12},{9,13},{10,... | collective-permute-start | bytes 98312 | tf_op jit(solution)/shard_map/ppermute | solution.py:62
  51.7 1.5 %collective-permute-start.22 = (bf16[2,32,256]{2,1,0:T(8,128)(2,1)S(1)}, bf16[2,32,256]{2,1,0:T(8,128)(2,1)S(1)}, u32[]{:S(2)}, u32[]{:S(2)}) collective-permute-start(bf16[2,32,256]{2,1,0:T(8,128)(2,1)S(1)} %out.1.refs_0_), channel_id=1, source_target_pairs={{0,6},{1,7},{2,4},{3,5},{4,2},{5,3},{6,0},{7,1},{8,14},{9,15},{10,... | collective-permute-start | bytes 98312 | tf_op jit(solution)/shard_map/ppermute | solution.py:62
  54.3 2.3 %collective-permute-done.22.refs_3_ = bf16[2,32,256]{2,1,0:T(8,128)(2,1)S(1)} collective-permute-done((bf16[2,32,256]{2,1,0:T(8,128)(2,1)S(1)}, bf16[2,32,256]{2,1,0:T(8,128)(2,1)S(1)}, u32[]{:S(2)}, u32[]{:S(2)}) %collective-permute-start.22) | collective-permute-done | bytes 32800 | tf_op jit(solution)/shard_map/ppermute | solution.py:62
  56.6 1.3 %collective-permute-start.23 = (bf16[2,2,32,256]{3,2,1,0:T(8,128)(2,1)S(1)}, bf16[2,2,32,256]{3,2,1,0:T(8,128)(2,1)S(1)}, u32[]{:S(2)}, u32[]{:S(2)}) collective-permute-start(bf16[2,2,32,256]{3,2,1,0:T(8,128)(2,1)S(1)} %add_out.1.refs_2_), channel_id=1, source_target_pairs={{0,8},{1,9},{2,10},{3,11},{4,12},{5,13},{6,14},{7,15},{8,0},{9,1},... | collective-permute-start | bytes 196616 | tf_op jit(solution)/shard_map/ppermute | solution.py:62
  57.9 1.7 %collective-permute-start.24 = (bf16[2,2,32,256]{3,2,1,0:T(8,128)(2,1)S(1)}, bf16[2,2,32,256]{3,2,1,0:T(8,128)(2,1)S(1)}, u32[]{:S(2)}, u32[]{:S(2)}) collective-permute-start(bf16[2,2,32,256]{3,2,1,0:T(8,128)(2,1)S(1)} %add_out.1.refs_2_), channel_id=1, source_target_pairs={{0,16},{1,17},{2,18},{3,19},{4,20},{5,21},{6,22},{7,23},{8,24},{9,... | collective-permute-start | bytes 196616 | tf_op jit(solution)/shard_map/ppermute | solution.py:62
  59.6 1.5 %collective-permute-start.25 = (bf16[2,2,32,256]{3,2,1,0:T(8,128)(2,1)S(1)}, bf16[2,2,32,256]{3,2,1,0:T(8,128)(2,1)S(1)}, u32[]{:S(2)}, u32[]{:S(2)}) collective-permute-start(bf16[2,2,32,256]{3,2,1,0:T(8,128)(2,1)S(1)} %add_out.1.refs_2_), channel_id=1, source_target_pairs={{0,24},{1,25},{2,26},{3,27},{4,28},{5,29},{6,30},{7,31},{8,16},{9,... | collective-permute-start | bytes 196616 | tf_op jit(solution)/shard_map/ppermute | solution.py:62
  61.6 2.1 %collective-permute-done.24.refs_4_ = bf16[2,2,32,256]{3,2,1,0:T(8,128)(2,1)S(1)} collective-permute-done((bf16[2,2,32,256]{3,2,1,0:T(8,128)(2,1)S(1)}, bf16[2,2,32,256]{3,2,1,0:T(8,128)(2,1)S(1)}, u32[]{:S(2)}, u32[]{:S(2)}) %collective-permute-start.24) | collective-permute-done | bytes 65568 | tf_op jit(solution)/shard_map/ppermute | solution.py:62
  63.7 1.9 %collective-permute-done.25.refs_5_ = bf16[2,2,32,256]{3,2,1,0:T(8,128)(2,1)S(1)} collective-permute-done((bf16[2,2,32,256]{3,2,1,0:T(8,128)(2,1)S(1)}, bf16[2,2,32,256]{3,2,1,0:T(8,128)(2,1)S(1)}, u32[]{:S(2)}, u32[]{:S(2)}) %collective-permute-start.25) | collective-permute-done | bytes 65568 | tf_op jit(solution)/shard_map/ppermute | solution.py:62
  67.1 4.4 %collective-permute-done.26.refs_1_ = bf16[64,1024]{1,0:T(8,128)(2,1)S(1)} collective-permute-done((bf16[64,1024]{1,0:T(8,128)(2,1)S(1)}, bf16[64,1024]{1,0:T(8,128)(2,1)S(1)}, u32[]{:S(2)}, u32[]{:S(2)}) %collective-permute-start.26) | collective-permute-done | bytes 131104 | tf_op jit(solution)/shard_map/ppermute | solution.py:62
  72.8 3.6 %collective-permute-done.27.refs_1_ = bf16[64,512]{1,0:T(8,128)(2,1)S(1)} collective-permute-done((bf16[64,512]{1,0:T(8,128)(2,1)S(1)}, bf16[64,512]{1,0:T(8,128)(2,1)S(1)}, u32[]{:S(2)}, u32[]{:S(2)}) %collective-permute-start.27) | collective-permute-done | bytes 65568 | tf_op jit(solution)/shard_map/ppermute | solution.py:62
  76.5 2.1 %collective-permute-start.29 = (bf16[64,512]{1,0:T(8,128)(2,1)S(1)}, bf16[64,512]{1,0:T(8,128)(2,1)S(1)}, u32[]{:S(2)}, u32[]{:S(2)}) collective-permute-start(bf16[64,512]{1,0:T(8,128)(2,1)S(1)} %add_x.1.refs_0_), channel_id=1, source_target_pairs={{0,16},{1,17},{2,18},{3,19},{4,20},{5,21},{6,22},{7,23},{8,24},{9,... | collective-permute-start | bytes 196616 | tf_op jit(solution)/shard_map/ppermute | solution.py:62
  78.6 2.3 %collective-permute-start.30 = (bf16[64,512]{1,0:T(8,128)(2,1)S(1)}, bf16[64,512]{1,0:T(8,128)(2,1)S(1)}, u32[]{:S(2)}, u32[]{:S(2)}) collective-permute-start(bf16[64,512]{1,0:T(8,128)(2,1)S(1)} %add_x.1.refs_0_), channel_id=1, source_target_pairs={{0,24},{1,25},{2,26},{3,27},{4,28},{5,29},{6,30},{7,31},{8,16},{9,... | collective-permute-start | bytes 196616 | tf_op jit(solution)/shard_map/ppermute | solution.py:62
  81.7 2.9 %collective-permute-done.30.refs_3_ = bf16[64,512]{1,0:T(8,128)(2,1)S(1)} collective-permute-done((bf16[64,512]{1,0:T(8,128)(2,1)S(1)}, bf16[64,512]{1,0:T(8,128)(2,1)S(1)}, u32[]{:S(2)}, u32[]{:S(2)}) %collective-permute-start.30) | collective-permute-done | bytes 65568 | tf_op jit(solution)/shard_map/ppermute | solution.py:62
  85.5 1.3 %collective-permute-start.32 = (bf16[32,512]{1,0:T(8,128)(2,1)S(1)}, bf16[32,512]{1,0:T(8,128)(2,1)S(1)}, u32[]{:S(2)}, u32[]{:S(2)}) collective-permute-start(bf16[32,512]{1,0:T(8,128)(2,1)S(1)} %get-tuple-element.78.refs_0_), channel_id=1, source_target_pairs={{0,4},{1,5},{2,6},{3,7},{4,0},{5,1},{6,2},{7,3},{8,12},{9,13},{10,... | collective-permute-start | bytes 98312 | tf_op jit(solution)/shard_map/ppermute | solution.py:62
  86.8 1.5 %collective-permute-start.33 = (bf16[32,512]{1,0:T(8,128)(2,1)S(1)}, bf16[32,512]{1,0:T(8,128)(2,1)S(1)}, u32[]{:S(2)}, u32[]{:S(2)}) collective-permute-start(bf16[32,512]{1,0:T(8,128)(2,1)S(1)} %get-tuple-element.79), channel_id=1, source_target_pairs={{0,6},{1,7},{2,4},{3,5},{4,2},{5,3},{6,0},{7,1},{8,14},{9,15},{10,... | collective-permute-start | bytes 98312 | tf_op jit(solution)/shard_map/ppermute | solution.py:62
  89.4 2.2 %collective-permute-done.33.refs_3_ = bf16[32,512]{1,0:T(8,128)(2,1)S(1)} collective-permute-done((bf16[32,512]{1,0:T(8,128)(2,1)S(1)}, bf16[32,512]{1,0:T(8,128)(2,1)S(1)}, u32[]{:S(2)}, u32[]{:S(2)}) %collective-permute-start.33) | collective-permute-done | bytes 32800 | tf_op jit(solution)/shard_map/ppermute | solution.py:62
  (76 shorter events, 19.3 us)
Async XLA Ops:
  0.6 7.9 %collective-permute-start.1 = (bf16[512,256]{1,0:T(8,128)(2,1)}, bf16[512,256]{1,0:T(8,128)(2,1)S(1)}, u32[]{:S(2)}, u32[]{:S(2)}) collective-permute-start(bf16[512,256]{1,0:T(8,128)(2,1)} %refs_0_.2), channel_id=1, source_target_pairs={{0,1},{1,0},{2,3},{3,2},{4,5},{5,4},{6,7},{7,6},{8,9},{9,8},{10,11... | collective-permute-start | bytes 786440 | tf_op jit(solution)/shard_map/ppermute | solution.py:62
  1.2 7.4 %collective-permute-start.2 = (bf16[512,256]{1,0:T(8,128)(2,1)}, bf16[512,256]{1,0:T(8,128)(2,1)S(1)}, u32[]{:S(2)}, u32[]{:S(2)}) collective-permute-start(bf16[512,256]{1,0:T(8,128)(2,1)} %refs_1_.1), channel_id=1, source_target_pairs={{0,1},{1,0},{2,3},{3,2},{4,5},{5,4},{6,7},{7,6},{8,9},{9,8},{10,11... | collective-permute-start | bytes 786440 | tf_op jit(solution)/shard_map/ppermute | solution.py:62
  1.2 7.3 %collective-permute-start.3 = (bf16[512,256]{1,0:T(8,128)(2,1)}, bf16[512,256]{1,0:T(8,128)(2,1)S(1)}, u32[]{:S(2)}, u32[]{:S(2)}) collective-permute-start(bf16[512,256]{1,0:T(8,128)(2,1)} %refs_2_.2), channel_id=1, source_target_pairs={{0,1},{1,0},{2,3},{3,2},{4,5},{5,4},{6,7},{7,6},{8,9},{9,8},{10,11... | collective-permute-start | bytes 786440 | tf_op jit(solution)/shard_map/ppermute | solution.py:62
  1.7 6.9 %collective-permute-start = (bf16[8,4,2048]{2,1,0:T(4,128)(2,1)}, bf16[8,4,2048]{2,1,0:T(4,128)(2,1)S(1)}, u32[]{:S(2)}, u32[]{:S(2)}) collective-permute-start(bf16[8,4,2048]{2,1,0:T(4,128)(2,1)} %refs_0_.3), channel_id=1, source_target_pairs={{0,2},{1,3},{2,0},{3,1},{4,6},{5,7},{6,4},{7,5},{8,10},{9,11},{10,... | collective-permute-start | bytes 393224 | tf_op jit(solution)/shard_map/ppermute | solution.py:62
  9.2 8.9 %collective-permute-start.7 = (bf16[512,1024]{1,0:T(8,128)(2,1)}, bf16[512,1024]{1,0:T(8,128)(2,1)S(1)}, u32[]{:S(2)}, u32[]{:S(2)}) collective-permute-start(bf16[512,1024]{1,0:T(8,128)(2,1)} %refs_8_.1), channel_id=1, source_target_pairs={{0,1},{1,0},{2,3},{3,2},{4,5},{5,4},{6,7},{7,6},{8,9},{9,8},{10,11... | collective-permute-start | bytes 3145736 | tf_op jit(solution)/shard_map/ppermute | solution.py:62
  9.3 8.8 %collective-permute-start.8 = (bf16[1024,512]{1,0:T(8,128)(2,1)}, bf16[1024,512]{1,0:T(8,128)(2,1)S(1)}, u32[]{:S(2)}, u32[]{:S(2)}) collective-permute-start(bf16[1024,512]{1,0:T(8,128)(2,1)} %refs_2_.3), channel_id=1, source_target_pairs={{0,1},{1,0},{2,3},{3,2},{4,5},{5,4},{6,7},{7,6},{8,9},{9,8},{10,11... | collective-permute-start | bytes 3145736 | tf_op jit(solution)/shard_map/ppermute | solution.py:62
  9.8 4.1 %collective-permute-start.4 = (bf16[32,768]{1,0:T(8,128)(2,1)S(1)}, bf16[32,768]{1,0:T(8,128)(2,1)S(1)}, u32[]{:S(2)}, u32[]{:S(2)}) collective-permute-start(bf16[32,768]{1,0:T(8,128)(2,1)S(1)} %get-tuple-element.50), channel_id=1, source_target_pairs={{0,2},{1,3},{2,0},{3,1},{4,6},{5,7},{6,4},{7,5},{8,10},{9,11},{10,... | collective-permute-start | bytes 147464 | tf_op jit(solution)/shard_map/ppermute | solution.py:62
  11.5 4.6 %collective-permute-start.5 = (bf16[32,768]{1,0:T(8,128)(2,1)S(1)}, bf16[32,768]{1,0:T(8,128)(2,1)S(1)}, u32[]{:S(2)}, u32[]{:S(2)}) collective-permute-start(bf16[32,768]{1,0:T(8,128)(2,1)S(1)} %get-tuple-element.49.refs_0_), channel_id=1, source_target_pairs={{0,4},{1,5},{2,6},{3,7},{4,0},{5,1},{6,2},{7,3},{8,12},{9,13},{10,... | collective-permute-start | bytes 147464 | tf_op jit(solution)/shard_map/ppermute | solution.py:62
  13.0 5.0 %collective-permute-start.6 = (bf16[32,768]{1,0:T(8,128)(2,1)S(1)}, bf16[32,768]{1,0:T(8,128)(2,1)S(1)}, u32[]{:S(2)}, u32[]{:S(2)}) collective-permute-start(bf16[32,768]{1,0:T(8,128)(2,1)S(1)} %get-tuple-element.50), channel_id=1, source_target_pairs={{0,6},{1,7},{2,4},{3,5},{4,2},{5,3},{6,0},{7,1},{8,14},{9,15},{10,... | collective-permute-start | bytes 147464 | tf_op jit(solution)/shard_map/ppermute | solution.py:62
  18.1 17.0 %collective-permute-start.12 = (bf16[512,256]{1,0:T(8,128)(2,1)S(1)}, bf16[512,256]{1,0:T(8,128)(2,1)S(1)}, u32[]{:S(2)}, u32[]{:S(2)}) collective-permute-start(bf16[512,256]{1,0:T(8,128)(2,1)S(1)} %copy-done.11), channel_id=1, source_target_pairs={{0,0},{1,1},{2,4},{3,5},{4,2},{5,3},{6,6},{7,7},{8,8},{9,9},{10,12... | collective-permute-start | bytes 786440 | tf_op jit(solution)/shard_map/ppermute | solution.py:77
  18.8 16.3 %collective-permute-start.13 = (bf16[512,256]{1,0:T(8,128)(2,1)S(1)}, bf16[512,256]{1,0:T(8,128)(2,1)S(1)}, u32[]{:S(2)}, u32[]{:S(2)}) collective-permute-start(bf16[512,256]{1,0:T(8,128)(2,1)S(1)} %copy-done.11), channel_id=1, source_target_pairs={{0,2},{1,3},{2,6},{3,7},{4,0},{5,1},{6,4},{7,5},{8,10},{9,11},{10,... | collective-permute-start | bytes 786440 | tf_op jit(solution)/shard_map/ppermute | solution.py:77
  22.1 9.5 %collective-permute-start.10 = (bf16[2,32,768]{2,1,0:T(8,128)(2,1)S(1)}, bf16[2,32,768]{2,1,0:T(8,128)(2,1)S(1)}, u32[]{:S(2)}, u32[]{:S(2)}) collective-permute-start(bf16[2,32,768]{2,1,0:T(8,128)(2,1)S(1)} %add_qkv.1.refs_0_), channel_id=1, source_target_pairs={{0,16},{1,17},{2,18},{3,19},{4,20},{5,21},{6,22},{7,23},{8,24},{9,... | collective-permute-start | bytes 294920 | tf_op jit(solution)/shard_map/ppermute | solution.py:62
  24.7 7.0 %collective-permute-start.11 = (bf16[2,32,768]{2,1,0:T(8,128)(2,1)S(1)}, bf16[2,32,768]{2,1,0:T(8,128)(2,1)S(1)}, u32[]{:S(2)}, u32[]{:S(2)}) collective-permute-start(bf16[2,32,768]{2,1,0:T(8,128)(2,1)S(1)} %add_qkv.1.refs_0_), channel_id=1, source_target_pairs={{0,24},{1,25},{2,26},{3,27},{4,28},{5,29},{6,30},{7,31},{8,16},{9,... | collective-permute-start | bytes 294920 | tf_op jit(solution)/shard_map/ppermute | solution.py:62
  26.0 6.2 %collective-permute-start.9 = (bf16[2,32,768]{2,1,0:T(8,128)(2,1)S(1)}, bf16[2,32,768]{2,1,0:T(8,128)(2,1)S(1)}, u32[]{:S(2)}, u32[]{:S(2)}) collective-permute-start(bf16[2,32,768]{2,1,0:T(8,128)(2,1)S(1)} %add_qkv.1.refs_0_), channel_id=1, source_target_pairs={{0,8},{1,9},{2,10},{3,11},{4,12},{5,13},{6,14},{7,15},{8,0},{9,1},... | collective-permute-start | bytes 294920 | tf_op jit(solution)/shard_map/ppermute | solution.py:62
  35.1 5.2 %collective-permute-start.15 = (bf16[512,256]{1,0:T(8,128)(2,1)S(1)}, bf16[512,256]{1,0:T(8,128)(2,1)S(1)}, u32[]{:S(2)}, u32[]{:S(2)}) collective-permute-start(bf16[512,256]{1,0:T(8,128)(2,1)S(1)} %collective-permute-done.12.refs_4_), channel_id=1, source_target_pairs={{0,1},{1,0},{2,3},{3,2},{4,5},{5,4},{6,7},{7,6},{8,9},{9,8},{10,11... | collective-permute-start | bytes 786440 | tf_op jit(solution)/shard_map/ppermute | solution.py:62
  35.2 5.1 %collective-permute-start.16 = (bf16[512,256]{1,0:T(8,128)(2,1)S(1)}, bf16[512,256]{1,0:T(8,128)(2,1)S(1)}, u32[]{:S(2)}, u32[]{:S(2)}) collective-permute-start(bf16[512,256]{1,0:T(8,128)(2,1)S(1)} %collective-permute-done.13.refs_6_), channel_id=1, source_target_pairs={{0,1},{1,0},{2,3},{3,2},{4,5},{5,4},{6,7},{7,6},{8,9},{9,8},{10,11... | collective-permute-start | bytes 786440 | tf_op jit(solution)/shard_map/ppermute | solution.py:62
  35.7 4.4 %collective-permute-start.14 = (bf16[32,1152]{1,0:T(8,128)(2,1)S(1)}, bf16[32,1152]{1,0:T(8,128)(2,1)S(1)}, u32[]{:S(2)}, u32[]{:S(2)}) collective-permute-start(bf16[32,1152]{1,0:T(8,128)(2,1)S(1)} %get-tuple-element.65), channel_id=1, source_target_pairs={{0,4},{1,5},{2,6},{3,7},{4,0},{5,1},{6,2},{7,3},{8,12},{9,13},{10,... | collective-permute-start | bytes 221192 | tf_op jit(solution)/shard_map/ppermute | solution.py:62
  40.3 4.5 %collective-permute-start.17 = (bf16[32,1152]{1,0:T(8,128)(2,1)S(1)}, bf16[32,1152]{1,0:T(8,128)(2,1)S(1)}, u32[]{:S(2)}, u32[]{:S(2)}) collective-permute-start(bf16[32,1152]{1,0:T(8,128)(2,1)S(1)} %merge_x.1.refs_0_), channel_id=1, source_target_pairs={{0,8},{1,9},{2,10},{3,11},{4,12},{5,13},{6,14},{7,15},{8,0},{9,1},... | collective-permute-start | bytes 221192 | tf_op jit(solution)/shard_map/ppermute | solution.py:62
  40.7 7.4 %collective-permute-start.18 = (bf16[32,1152]{1,0:T(8,128)(2,1)S(1)}, bf16[32,1152]{1,0:T(8,128)(2,1)S(1)}, u32[]{:S(2)}, u32[]{:S(2)}) collective-permute-start(bf16[32,1152]{1,0:T(8,128)(2,1)S(1)} %merge_x.1.refs_0_), channel_id=1, source_target_pairs={{0,16},{1,17},{2,18},{3,19},{4,20},{5,21},{6,22},{7,23},{8,24},{9,... | collective-permute-start | bytes 221192 | tf_op jit(solution)/shard_map/ppermute | solution.py:62
  42.8 6.2 %collective-permute-start.19 = (bf16[32,1152]{1,0:T(8,128)(2,1)S(1)}, bf16[32,1152]{1,0:T(8,128)(2,1)S(1)}, u32[]{:S(2)}, u32[]{:S(2)}) collective-permute-start(bf16[32,1152]{1,0:T(8,128)(2,1)S(1)} %merge_x.1.refs_0_), channel_id=1, source_target_pairs={{0,24},{1,25},{2,26},{3,27},{4,28},{5,29},{6,30},{7,31},{8,16},{9,... | collective-permute-start | bytes 221192 | tf_op jit(solution)/shard_map/ppermute | solution.py:62
  49.6 4.0 %collective-permute-start.20 = (bf16[2,32,256]{2,1,0:T(8,128)(2,1)S(1)}, bf16[2,32,256]{2,1,0:T(8,128)(2,1)S(1)}, u32[]{:S(2)}, u32[]{:S(2)}) collective-permute-start(bf16[2,32,256]{2,1,0:T(8,128)(2,1)S(1)} %out.1.refs_0_), channel_id=1, source_target_pairs={{0,2},{1,3},{2,0},{3,1},{4,6},{5,7},{6,4},{7,5},{8,10},{9,11},{10,... | collective-permute-start | bytes 98312 | tf_op jit(solution)/shard_map/ppermute | solution.py:62
  51.7 4.8 %collective-permute-start.22 = (bf16[2,32,256]{2,1,0:T(8,128)(2,1)S(1)}, bf16[2,32,256]{2,1,0:T(8,128)(2,1)S(1)}, u32[]{:S(2)}, u32[]{:S(2)}) collective-permute-start(bf16[2,32,256]{2,1,0:T(8,128)(2,1)S(1)} %out.1.refs_0_), channel_id=1, source_target_pairs={{0,6},{1,7},{2,4},{3,5},{4,2},{5,3},{6,0},{7,1},{8,14},{9,15},{10,... | collective-permute-start | bytes 98312 | tf_op jit(solution)/shard_map/ppermute | solution.py:62
  56.6 5.0 %collective-permute-start.23 = (bf16[2,2,32,256]{3,2,1,0:T(8,128)(2,1)S(1)}, bf16[2,2,32,256]{3,2,1,0:T(8,128)(2,1)S(1)}, u32[]{:S(2)}, u32[]{:S(2)}) collective-permute-start(bf16[2,2,32,256]{3,2,1,0:T(8,128)(2,1)S(1)} %add_out.1.refs_2_), channel_id=1, source_target_pairs={{0,8},{1,9},{2,10},{3,11},{4,12},{5,13},{6,14},{7,15},{8,0},{9,1},... | collective-permute-start | bytes 196616 | tf_op jit(solution)/shard_map/ppermute | solution.py:62
  57.9 5.9 %collective-permute-start.24 = (bf16[2,2,32,256]{3,2,1,0:T(8,128)(2,1)S(1)}, bf16[2,2,32,256]{3,2,1,0:T(8,128)(2,1)S(1)}, u32[]{:S(2)}, u32[]{:S(2)}) collective-permute-start(bf16[2,2,32,256]{3,2,1,0:T(8,128)(2,1)S(1)} %add_out.1.refs_2_), channel_id=1, source_target_pairs={{0,16},{1,17},{2,18},{3,19},{4,20},{5,21},{6,22},{7,23},{8,24},{9,... | collective-permute-start | bytes 196616 | tf_op jit(solution)/shard_map/ppermute | solution.py:62
  59.6 6.1 %collective-permute-start.25 = (bf16[2,2,32,256]{3,2,1,0:T(8,128)(2,1)S(1)}, bf16[2,2,32,256]{3,2,1,0:T(8,128)(2,1)S(1)}, u32[]{:S(2)}, u32[]{:S(2)}) collective-permute-start(bf16[2,2,32,256]{3,2,1,0:T(8,128)(2,1)S(1)} %add_out.1.refs_2_), channel_id=1, source_target_pairs={{0,24},{1,25},{2,26},{3,27},{4,28},{5,29},{6,30},{7,31},{8,16},{9,... | collective-permute-start | bytes 196616 | tf_op jit(solution)/shard_map/ppermute | solution.py:62
  66.5 5.0 %collective-permute-start.26 = (bf16[64,1024]{1,0:T(8,128)(2,1)S(1)}, bf16[64,1024]{1,0:T(8,128)(2,1)S(1)}, u32[]{:S(2)}, u32[]{:S(2)}) collective-permute-start(bf16[64,1024]{1,0:T(8,128)(2,1)S(1)} %get-tuple-element.74.refs_0_), channel_id=1, source_target_pairs={{0,2},{1,3},{2,0},{3,1},{4,6},{5,7},{6,4},{7,5},{8,10},{9,11},{10,... | collective-permute-start | bytes 393224 | tf_op jit(solution)/shard_map/ppermute | solution.py:62
  72.1 4.3 %collective-permute-start.27 = (bf16[64,512]{1,0:T(8,128)(2,1)S(1)}, bf16[64,512]{1,0:T(8,128)(2,1)S(1)}, u32[]{:S(2)}, u32[]{:S(2)}) collective-permute-start(bf16[64,512]{1,0:T(8,128)(2,1)S(1)} %get-tuple-element.77), channel_id=1, source_target_pairs={{0,4},{1,5},{2,6},{3,7},{4,0},{5,1},{6,2},{7,3},{8,12},{9,13},{10,... | collective-permute-start | bytes 196616 | tf_op jit(solution)/shard_map/ppermute | solution.py:62
  76.4 4.5 %collective-permute-start.28 = (bf16[64,512]{1,0:T(8,128)(2,1)S(1)}, bf16[64,512]{1,0:T(8,128)(2,1)S(1)}, u32[]{:S(2)}, u32[]{:S(2)}) collective-permute-start(bf16[64,512]{1,0:T(8,128)(2,1)S(1)} %add_x.1.refs_0_), channel_id=1, source_target_pairs={{0,8},{1,9},{2,10},{3,11},{4,12},{5,13},{6,14},{7,15},{8,0},{9,1},... | collective-permute-start | bytes 196616 | tf_op jit(solution)/shard_map/ppermute | solution.py:62
  76.5 5.2 %collective-permute-start.29 = (bf16[64,512]{1,0:T(8,128)(2,1)S(1)}, bf16[64,512]{1,0:T(8,128)(2,1)S(1)}, u32[]{:S(2)}, u32[]{:S(2)}) collective-permute-start(bf16[64,512]{1,0:T(8,128)(2,1)S(1)} %add_x.1.refs_0_), channel_id=1, source_target_pairs={{0,16},{1,17},{2,18},{3,19},{4,20},{5,21},{6,22},{7,23},{8,24},{9,... | collective-permute-start | bytes 196616 | tf_op jit(solution)/shard_map/ppermute | solution.py:62
  78.6 6.1 %collective-permute-start.30 = (bf16[64,512]{1,0:T(8,128)(2,1)S(1)}, bf16[64,512]{1,0:T(8,128)(2,1)S(1)}, u32[]{:S(2)}, u32[]{:S(2)}) collective-permute-start(bf16[64,512]{1,0:T(8,128)(2,1)S(1)} %add_x.1.refs_0_), channel_id=1, source_target_pairs={{0,24},{1,25},{2,26},{3,27},{4,28},{5,29},{6,30},{7,31},{8,16},{9,... | collective-permute-start | bytes 196616 | tf_op jit(solution)/shard_map/ppermute | solution.py:62
  84.7 4.0 %collective-permute-start.31 = (bf16[32,512]{1,0:T(8,128)(2,1)S(1)}, bf16[32,512]{1,0:T(8,128)(2,1)S(1)}, u32[]{:S(2)}, u32[]{:S(2)}) collective-permute-start(bf16[32,512]{1,0:T(8,128)(2,1)S(1)} %get-tuple-element.79), channel_id=1, source_target_pairs={{0,2},{1,3},{2,0},{3,1},{4,6},{5,7},{6,4},{7,5},{8,10},{9,11},{10,... | collective-permute-start | bytes 98312 | tf_op jit(solution)/shard_map/ppermute | solution.py:62
  86.8 4.8 %collective-permute-start.33 = (bf16[32,512]{1,0:T(8,128)(2,1)S(1)}, bf16[32,512]{1,0:T(8,128)(2,1)S(1)}, u32[]{:S(2)}, u32[]{:S(2)}) collective-permute-start(bf16[32,512]{1,0:T(8,128)(2,1)S(1)} %get-tuple-element.79), channel_id=1, source_target_pairs={{0,6},{1,7},{2,4},{3,5},{4,2},{5,3},{6,0},{7,1},{8,14},{9,15},{10,... | collective-permute-start | bytes 98312 | tf_op jit(solution)/shard_map/ppermute | solution.py:62
  (14 other events, 290.1 us)

commit v14 on v13

--- a/solution.py
+++ b/solution.py
@@ -184,7 +184,7 @@
         out[place.x_before(dx)] = total.astype(BF16)
 
 
-def cache_kernel(keys_in, values_in, keys_out, values_out, keys, values, in_sems, out_sems):
+def cache_kernel(keys_in, values_in, keys_out, values_out, keys, values, mark, in_sems, out_sems):
     group = keys.shape[0]
     arrays = ((keys_in, keys, keys_out), (values_in, values, values_out))
     coming = [
@@ -199,6 +199,7 @@
     ]
     for copy in coming:
         copy.start()
+    mark[...] = jnp.zeros_like(mark)
     for arrived, copy in zip(coming, going):
         arrived.wait()
         copy.start()
@@ -542,26 +543,26 @@
     *parts, tied_up, tied_down = lax.optimization_barrier((*parts, w_up, w_down))
     w_up_sibling = place.move(tied_up, dc=1)
     w_down_sibling = place.move(tied_down, dc=1)
+    parts, tied_keys, tied_values = lax.optimization_barrier((parts, cache_keys, cache_values))
+    new_keys, new_values, keys, values, mark = call(
+        cache_kernel,
+        "caches",
+        [tied_keys, tied_values],
+        [shape(cache_keys.shape)] * 4 + [shape((8, LANES), F32)],
+        in_specs=[HBM, HBM],
+        out_specs=[HBM, HBM, VMEM, VMEM, VMEM],
+        scratch=[pltpu.SemaphoreType.DMA((2, group)), pltpu.SemaphoreType.DMA((2, group))],
+        moved=16 * 1024 * 1024,
+        limit=46,
+    )
     qkv = call(
         bind(add_columns_kernel, place),
         "add_qkv",
-        spread(parts),
+        [*spread(parts), mark],
         shape((nx, rows, 3 * cols)),
     )
     qkv, w_up_sibling, w_down_sibling, tied = lax.optimization_barrier(
         (qkv, w_up_sibling, w_down_sibling, w_out)
-    )
-    qkv, tied_keys, tied_values = lax.optimization_barrier((qkv, cache_keys, cache_values))
-    new_keys, new_values, keys, values = call(
-        cache_kernel,
-        "caches",
-        [tied_keys, tied_values],
-        [shape(cache_keys.shape)] * 4,
-        in_specs=[HBM, HBM],
-        out_specs=[HBM, HBM, VMEM, VMEM],
-        scratch=[pltpu.SemaphoreType.DMA((2, group)), pltpu.SemaphoreType.DMA((2, group))],
-        moved=16 * 1024 * 1024,
-        limit=46,
     )
     pieces = place.gather_z(qkv)
     blocks = [place.transpose(tied, k) for k in range(nx)]

time: 92.7 us -> 89.6 us (0.967)
  waiting for transfers between devices: 40.1 us -> 35.2 us
  starting transfers between devices: 38.1 us -> 40.3 us
    ppermute x32, waiting for transfers between devices: 40.1 us -> 35.2 us  [move(): return lax.ppermute(value, ('seq', 'req'), pairs)]
    ppermute x32, starting transfers between devices: 34.2 us -> 38.4 us  [move(): return lax.ppermute(value, ('seq', 'req'), pairs)]
    ppermute x2, starting transfers between devices: 3.96 us -> 1.85 us  [transpose(): return lax.ppermute(value, ('seq', 'req'), pairs)]
  transfers between devices with their start and end apart: 34 -> 34, of which waited for: 22 -> 20; matrix products, arithmetic and copies ran while one was open for 2% -> 2% of each run, Pallas kernels for 8% -> 8%
where the time goes in v14:
time: 89.6 us; the launch traced here: 89.3 us
  starting transfers between devices  40.3 us (45%)
  waiting for transfers between devices  35.2 us (39%)
  Pallas kernels  10.5 us (12%)
  other arithmetic  1.44 us (2%)
  local copies, waits for them, and re-layouts  0.97 us (1%)
  between operations  0.93 us (1%)
    ppermute x32, starting transfers between devices, move(): return lax.ppermute(value, ('seq', 'req'), pairs)  38.4 us
    ppermute x32, waiting for transfers between devices, move(): return lax.ppermute(value, ('seq', 'req'), pairs)  35.2 us
    pallas_call x13, Pallas kernels, call(): pl.pallas_call(kernel, name=name, out_shape=outs, in_specs=in_specs or [V...  10.5 us
    ppermute x2, starting transfers between devices, transpose(): return lax.ppermute(value, ('seq', 'req'), pairs)  1.85 us
  transfers between devices with their start and end apart: 34, of which 20 were waited for; matrix products, arithmetic and copies ran while one was open for 2% of the time, Pallas kernels for 8%

profile of v14, /device:TPU:0, one launch (start us, length us, event | category | flops | bytes accessed | tf_op | source)
XLA Modules:
  0.0 89.3 jit_solution(18379353150001339164)
XLA Ops:
  1.7 2.6 %collective-permute-start = (bf16[8,4,2048]{2,1,0:T(4,128)(2,1)}, bf16[8,4,2048]{2,1,0:T(4,128)(2,1)S(1)}, u32[]{:S(2)}, u32[]{:S(2)}) collective-permute-start(bf16[8,4,2048]{2,1,0:T(4,128)(2,1)} %refs_0_.3), channel_id=1, source_target_pairs={{0,2},{1,3},{2,0},{3,1},{4,6},{5,7},{6,4},{7,5},{8,10},{9,11},{10,... | collective-permute-start | bytes 393224 | tf_op jit(solution)/shard_map/ppermute | solution.py:62
  9.8 1.7 %collective-permute-start.5 = (bf16[32,768]{1,0:T(8,128)(2,1)S(1)}, bf16[32,768]{1,0:T(8,128)(2,1)S(1)}, u32[]{:S(2)}, u32[]{:S(2)}) collective-permute-start(bf16[32,768]{1,0:T(8,128)(2,1)S(1)} %get-tuple-element.53.refs_0_), channel_id=1, source_target_pairs={{0,4},{1,5},{2,6},{3,7},{4,0},{5,1},{6,2},{7,3},{8,12},{9,13},{10,... | collective-permute-start | bytes 147464 | tf_op jit(solution)/shard_map/ppermute | solution.py:62
  11.5 1.5 %collective-permute-start.6 = (bf16[32,768]{1,0:T(8,128)(2,1)S(1)}, bf16[32,768]{1,0:T(8,128)(2,1)S(1)}, u32[]{:S(2)}, u32[]{:S(2)}) collective-permute-start(bf16[32,768]{1,0:T(8,128)(2,1)S(1)} %get-tuple-element.54), channel_id=1, source_target_pairs={{0,6},{1,7},{2,4},{3,5},{4,2},{5,3},{6,0},{7,1},{8,14},{9,15},{10,... | collective-permute-start | bytes 147464 | tf_op jit(solution)/shard_map/ppermute | solution.py:62
  13.3 3.2 %caches.1 = (bf16[8,64,2048]{2,1,0:T(8,128)(2,1)}, bf16[8,64,2048]{2,1,0:T(8,128)(2,1)}, bf16[8,64,2048]{2,1,0:T(8,128)(2,1)S(1)}, bf16[8,64,2048]{2,1,0:T(8,128)(2,1)S(1)}, f32[8,128]{1,0:T(8,128)S(1)}) custom-call(bf16[8,64,2048]{2,1,0:T(8,128)(2,1)S(1)} %copy-done, bf16[8,64,2048]{2,1,0:T(8,128)(2,1)} %values_in), custom_call_target="tpu_custom_call" | custom-call | bytes 16777216 | tf_op jit(solution)/shard_map/caches/pallas_call | solution.py:104
  17.2 1.2 %collective-permute-start.13 = (bf16[512,256]{1,0:T(8,128)(2,1)S(1)}, bf16[512,256]{1,0:T(8,128)(2,1)S(1)}, u32[]{:S(2)}, u32[]{:S(2)}) collective-permute-start(bf16[512,256]{1,0:T(8,128)(2,1)S(1)} %copy-done.11), channel_id=1, source_target_pairs={{0,2},{1,3},{2,6},{3,7},{4,0},{5,1},{6,4},{7,5},{8,10},{9,11},{10,... | collective-permute-start | bytes 786440 | tf_op jit(solution)/shard_map/ppermute | solution.py:77
  19.0 3.7 %collective-permute-start.11 = (bf16[2,32,768]{2,1,0:T(8,128)(2,1)S(1)}, bf16[2,32,768]{2,1,0:T(8,128)(2,1)S(1)}, u32[]{:S(2)}, u32[]{:S(2)}) collective-permute-start(bf16[2,32,768]{2,1,0:T(8,128)(2,1)S(1)} %add_qkv.1.refs_0_), channel_id=1, source_target_pairs={{0,24},{1,25},{2,26},{3,27},{4,28},{5,29},{6,30},{7,31},{8,16},{9,... | collective-permute-start | bytes 294920 | tf_op jit(solution)/shard_map/ppermute | solution.py:62
  23.5 2.6 %collective-permute-done.11.refs_3_ = bf16[2,32,768]{2,1,0:T(8,128)(2,1)S(1)} collective-permute-done((bf16[2,32,768]{2,1,0:T(8,128)(2,1)S(1)}, bf16[2,32,768]{2,1,0:T(8,128)(2,1)S(1)}, u32[]{:S(2)}, u32[]{:S(2)}) %collective-permute-start.11) | collective-permute-done | bytes 98336 | tf_op jit(solution)/shard_map/ppermute | solution.py:62
  26.1 4.0 %collective-permute-done.10.refs_2_ = bf16[2,32,768]{2,1,0:T(8,128)(2,1)S(1)} collective-permute-done((bf16[2,32,768]{2,1,0:T(8,128)(2,1)S(1)}, bf16[2,32,768]{2,1,0:T(8,128)(2,1)S(1)}, u32[]{:S(2)}, u32[]{:S(2)}) %collective-permute-start.10) | collective-permute-done | bytes 98336 | tf_op jit(solution)/shard_map/ppermute | solution.py:62
  30.2 2.6 %attention.1 = (bf16[8,64,2048]{2,1,0:T(8,128)(2,1)}, bf16[8,64,2048]{2,1,0:T(8,128)(2,1)}, bf16[32,1152]{1,0:T(8,128)(2,1)S(1)}, bf16[32,1152]{1,0:T(8,128)(2,1)S(1)}) custom-call(bf16[2,32,768]{2,1,0:T(8,128)(2,1)S(1)} %add_qkv.1.refs_0_, bf16[2,32,768]{2,1,0:T(8,128)(2,1)S(1)} %collective-permute-done.9.refs_1_, ...), custom_call_target="tpu_custom_call", output_to_operand_aliasing={{0}: (7, {}), {1}: (8, {})} | custom-call | bytes 1048576 | tf_op jit(solution)/shard_map/attention/pallas_call | solution.py:104
  33.3 3.9 %collective-permute-start.14 = (bf16[32,1152]{1,0:T(8,128)(2,1)S(1)}, bf16[32,1152]{1,0:T(8,128)(2,1)S(1)}, u32[]{:S(2)}, u32[]{:S(2)}) collective-permute-start(bf16[32,1152]{1,0:T(8,128)(2,1)S(1)} %get-tuple-element.69), channel_id=1, source_target_pairs={{0,4},{1,5},{2,6},{3,7},{4,0},{5,1},{6,2},{7,3},{8,12},{9,13},{10,... | collective-permute-start | bytes 221192 | tf_op jit(solution)/shard_map/ppermute | solution.py:62
  37.2 2.5 %collective-permute-done.14.refs_1_ = bf16[32,1152]{1,0:T(8,128)(2,1)S(1)} collective-permute-done((bf16[32,1152]{1,0:T(8,128)(2,1)S(1)}, bf16[32,1152]{1,0:T(8,128)(2,1)S(1)}, u32[]{:S(2)}, u32[]{:S(2)}) %collective-permute-start.14) | collective-permute-done | bytes 73760 | tf_op jit(solution)/shard_map/ppermute | solution.py:62
  40.0 2.2 %collective-permute-start.19 = (bf16[32,1152]{1,0:T(8,128)(2,1)S(1)}, bf16[32,1152]{1,0:T(8,128)(2,1)S(1)}, u32[]{:S(2)}, u32[]{:S(2)}) collective-permute-start(bf16[32,1152]{1,0:T(8,128)(2,1)S(1)} %merge_x.1.refs_0_), channel_id=1, source_target_pairs={{0,24},{1,25},{2,26},{3,27},{4,28},{5,29},{6,30},{7,31},{8,16},{9,... | collective-permute-start | bytes 221192 | tf_op jit(solution)/shard_map/ppermute | solution.py:62
  42.3 2.2 %collective-permute-start.17 = (bf16[32,1152]{1,0:T(8,128)(2,1)S(1)}, bf16[32,1152]{1,0:T(8,128)(2,1)S(1)}, u32[]{:S(2)}, u32[]{:S(2)}) collective-permute-start(bf16[32,1152]{1,0:T(8,128)(2,1)S(1)} %merge_x.1.refs_0_), channel_id=1, source_target_pairs={{0,8},{1,9},{2,10},{3,11},{4,12},{5,13},{6,14},{7,15},{8,0},{9,1},... | collective-permute-start | bytes 221192 | tf_op jit(solution)/shard_map/ppermute | solution.py:62
  44.5 2.2 %collective-permute-done.19.refs_3_ = bf16[32,1152]{1,0:T(8,128)(2,1)S(1)} collective-permute-done((bf16[32,1152]{1,0:T(8,128)(2,1)S(1)}, bf16[32,1152]{1,0:T(8,128)(2,1)S(1)}, u32[]{:S(2)}, u32[]{:S(2)}) %collective-permute-start.19) | collective-permute-done | bytes 73760 | tf_op jit(solution)/shard_map/ppermute | solution.py:62
  46.7 2.1 %collective-permute-done.18.refs_2_ = bf16[32,1152]{1,0:T(8,128)(2,1)S(1)} collective-permute-done((bf16[32,1152]{1,0:T(8,128)(2,1)S(1)}, bf16[32,1152]{1,0:T(8,128)(2,1)S(1)}, u32[]{:S(2)}, u32[]{:S(2)}) %collective-permute-start.18) | collective-permute-done | bytes 73760 | tf_op jit(solution)/shard_map/ppermute | solution.py:62
  49.4 1.2 %collective-permute-start.22 = (bf16[2,32,256]{2,1,0:T(8,128)(2,1)S(1)}, bf16[2,32,256]{2,1,0:T(8,128)(2,1)S(1)}, u32[]{:S(2)}, u32[]{:S(2)}) collective-permute-start(bf16[2,32,256]{2,1,0:T(8,128)(2,1)S(1)} %out.1.refs_0_), channel_id=1, source_target_pairs={{0,6},{1,7},{2,4},{3,5},{4,2},{5,3},{6,0},{7,1},{8,14},{9,15},{10,... | collective-permute-start | bytes 98312 | tf_op jit(solution)/shard_map/ppermute | solution.py:62
  50.6 1.8 %collective-permute-start.21 = (bf16[2,32,256]{2,1,0:T(8,128)(2,1)S(1)}, bf16[2,32,256]{2,1,0:T(8,128)(2,1)S(1)}, u32[]{:S(2)}, u32[]{:S(2)}) collective-permute-start(bf16[2,32,256]{2,1,0:T(8,128)(2,1)S(1)} %out.1.refs_0_), channel_id=1, source_target_pairs={{0,4},{1,5},{2,6},{3,7},{4,0},{5,1},{6,2},{7,3},{8,12},{9,13},{10,... | collective-permute-start | bytes 98312 | tf_op jit(solution)/shard_map/ppermute | solution.py:62
  52.9 1.5 %collective-permute-done.22.refs_3_ = bf16[2,32,256]{2,1,0:T(8,128)(2,1)S(1)} collective-permute-done((bf16[2,32,256]{2,1,0:T(8,128)(2,1)S(1)}, bf16[2,32,256]{2,1,0:T(8,128)(2,1)S(1)}, u32[]{:S(2)}, u32[]{:S(2)}) %collective-permute-start.22) | collective-permute-done | bytes 32800 | tf_op jit(solution)/shard_map/ppermute | solution.py:62
  54.7 1.7 %collective-permute-done.20.refs_1_ = bf16[2,32,256]{2,1,0:T(8,128)(2,1)S(1)} collective-permute-done((bf16[2,32,256]{2,1,0:T(8,128)(2,1)S(1)}, bf16[2,32,256]{2,1,0:T(8,128)(2,1)S(1)}, u32[]{:S(2)}, u32[]{:S(2)}) %collective-permute-start.20) | collective-permute-done | bytes 32800 | tf_op jit(solution)/shard_map/ppermute | solution.py:62
  56.3 1.6 %collective-permute-start.25 = (bf16[2,2,32,256]{3,2,1,0:T(8,128)(2,1)S(1)}, bf16[2,2,32,256]{3,2,1,0:T(8,128)(2,1)S(1)}, u32[]{:S(2)}, u32[]{:S(2)}) collective-permute-start(bf16[2,2,32,256]{3,2,1,0:T(8,128)(2,1)S(1)} %add_out.1.refs_2_), channel_id=1, source_target_pairs={{0,24},{1,25},{2,26},{3,27},{4,28},{5,29},{6,30},{7,31},{8,16},{9,... | collective-permute-start | bytes 196616 | tf_op jit(solution)/shard_map/ppermute | solution.py:62
  57.9 2.9 %collective-permute-start.23 = (bf16[2,2,32,256]{3,2,1,0:T(8,128)(2,1)S(1)}, bf16[2,2,32,256]{3,2,1,0:T(8,128)(2,1)S(1)}, u32[]{:S(2)}, u32[]{:S(2)}) collective-permute-start(bf16[2,2,32,256]{3,2,1,0:T(8,128)(2,1)S(1)} %add_out.1.refs_2_), channel_id=1, source_target_pairs={{0,8},{1,9},{2,10},{3,11},{4,12},{5,13},{6,14},{7,15},{8,0},{9,1},... | collective-permute-start | bytes 196616 | tf_op jit(solution)/shard_map/ppermute | solution.py:62
  60.8 1.7 %collective-permute-done.25.refs_5_ = bf16[2,2,32,256]{3,2,1,0:T(8,128)(2,1)S(1)} collective-permute-done((bf16[2,2,32,256]{3,2,1,0:T(8,128)(2,1)S(1)}, bf16[2,2,32,256]{3,2,1,0:T(8,128)(2,1)S(1)}, u32[]{:S(2)}, u32[]{:S(2)}) %collective-permute-start.25) | collective-permute-done | bytes 65568 | tf_op jit(solution)/shard_map/ppermute | solution.py:62
  62.5 1.4 %collective-permute-done.24.refs_4_ = bf16[2,2,32,256]{3,2,1,0:T(8,128)(2,1)S(1)} collective-permute-done((bf16[2,2,32,256]{3,2,1,0:T(8,128)(2,1)S(1)}, bf16[2,2,32,256]{3,2,1,0:T(8,128)(2,1)S(1)}, u32[]{:S(2)}, u32[]{:S(2)}) %collective-permute-start.24) | collective-permute-done | bytes 65568 | tf_op jit(solution)/shard_map/ppermute | solution.py:62
  65.7 4.1 %collective-permute-done.26.refs_1_ = bf16[64,1024]{1,0:T(8,128)(2,1)S(1)} collective-permute-done((bf16[64,1024]{1,0:T(8,128)(2,1)S(1)}, bf16[64,1024]{1,0:T(8,128)(2,1)S(1)}, u32[]{:S(2)}, u32[]{:S(2)}) %collective-permute-start.26) | collective-permute-done | bytes 131104 | tf_op jit(solution)/shard_map/ppermute | solution.py:62
  70.8 3.9 %collective-permute-done.27.refs_1_ = bf16[64,512]{1,0:T(8,128)(2,1)S(1)} collective-permute-done((bf16[64,512]{1,0:T(8,128)(2,1)S(1)}, bf16[64,512]{1,0:T(8,128)(2,1)S(1)}, u32[]{:S(2)}, u32[]{:S(2)}) %collective-permute-start.27) | collective-permute-done | bytes 65568 | tf_op jit(solution)/shard_map/ppermute | solution.py:62
  74.7 2.0 %collective-permute-start.30 = (bf16[64,512]{1,0:T(8,128)(2,1)S(1)}, bf16[64,512]{1,0:T(8,128)(2,1)S(1)}, u32[]{:S(2)}, u32[]{:S(2)}) collective-permute-start(bf16[64,512]{1,0:T(8,128)(2,1)S(1)} %add_x.1.refs_0_), channel_id=1, source_target_pairs={{0,24},{1,25},{2,26},{3,27},{4,28},{5,29},{6,30},{7,31},{8,16},{9,... | collective-permute-start | bytes 196616 | tf_op jit(solution)/shard_map/ppermute | solution.py:62
  77.4 1.8 %collective-permute-start.28 = (bf16[64,512]{1,0:T(8,128)(2,1)S(1)}, bf16[64,512]{1,0:T(8,128)(2,1)S(1)}, u32[]{:S(2)}, u32[]{:S(2)}) collective-permute-start(bf16[64,512]{1,0:T(8,128)(2,1)S(1)} %add_x.1.refs_0_), channel_id=1, source_target_pairs={{0,8},{1,9},{2,10},{3,11},{4,12},{5,13},{6,14},{7,15},{8,0},{9,1},... | collective-permute-start | bytes 196616 | tf_op jit(solution)/shard_map/ppermute | solution.py:62
  79.2 1.7 %collective-permute-done.30.refs_3_ = bf16[64,512]{1,0:T(8,128)(2,1)S(1)} collective-permute-done((bf16[64,512]{1,0:T(8,128)(2,1)S(1)}, bf16[64,512]{1,0:T(8,128)(2,1)S(1)}, u32[]{:S(2)}, u32[]{:S(2)}) %collective-permute-start.30) | collective-permute-done | bytes 65568 | tf_op jit(solution)/shard_map/ppermute | solution.py:62
  80.8 1.5 %collective-permute-done.29.refs_2_ = bf16[64,512]{1,0:T(8,128)(2,1)S(1)} collective-permute-done((bf16[64,512]{1,0:T(8,128)(2,1)S(1)}, bf16[64,512]{1,0:T(8,128)(2,1)S(1)}, u32[]{:S(2)}, u32[]{:S(2)}) %collective-permute-start.29) | collective-permute-done | bytes 65568 | tf_op jit(solution)/shard_map/ppermute | solution.py:62
  82.8 1.8 %collective-permute-start.33 = (bf16[32,512]{1,0:T(8,128)(2,1)S(1)}, bf16[32,512]{1,0:T(8,128)(2,1)S(1)}, u32[]{:S(2)}, u32[]{:S(2)}) collective-permute-start(bf16[32,512]{1,0:T(8,128)(2,1)S(1)} %get-tuple-element.83), channel_id=1, source_target_pairs={{0,6},{1,7},{2,4},{3,5},{4,2},{5,3},{6,0},{7,1},{8,14},{9,15},{10,... | collective-permute-start | bytes 98312 | tf_op jit(solution)/shard_map/ppermute | solution.py:62
  84.7 1.3 %collective-permute-start.31 = (bf16[32,512]{1,0:T(8,128)(2,1)S(1)}, bf16[32,512]{1,0:T(8,128)(2,1)S(1)}, u32[]{:S(2)}, u32[]{:S(2)}) collective-permute-start(bf16[32,512]{1,0:T(8,128)(2,1)S(1)} %get-tuple-element.83), channel_id=1, source_target_pairs={{0,2},{1,3},{2,0},{3,1},{4,6},{5,7},{6,4},{7,5},{8,10},{9,11},{10,... | collective-permute-start | bytes 98312 | tf_op jit(solution)/shard_map/ppermute | solution.py:62
  86.4 1.3 %collective-permute-done.33.refs_3_ = bf16[32,512]{1,0:T(8,128)(2,1)S(1)} collective-permute-done((bf16[32,512]{1,0:T(8,128)(2,1)S(1)}, bf16[32,512]{1,0:T(8,128)(2,1)S(1)}, u32[]{:S(2)}, u32[]{:S(2)}) %collective-permute-start.33) | collective-permute-done | bytes 32800 | tf_op jit(solution)/shard_map/ppermute | solution.py:62
  (76 shorter events, 17.2 us)
Async XLA Ops:
  0.6 7.9 %collective-permute-start.1 = (bf16[512,256]{1,0:T(8,128)(2,1)}, bf16[512,256]{1,0:T(8,128)(2,1)S(1)}, u32[]{:S(2)}, u32[]{:S(2)}) collective-permute-start(bf16[512,256]{1,0:T(8,128)(2,1)} %refs_0_.2), channel_id=1, source_target_pairs={{0,1},{1,0},{2,3},{3,2},{4,5},{5,4},{6,7},{7,6},{8,9},{9,8},{10,11... | collective-permute-start | bytes 786440 | tf_op jit(solution)/shard_map/ppermute | solution.py:62
  1.2 7.4 %collective-permute-start.2 = (bf16[512,256]{1,0:T(8,128)(2,1)}, bf16[512,256]{1,0:T(8,128)(2,1)S(1)}, u32[]{:S(2)}, u32[]{:S(2)}) collective-permute-start(bf16[512,256]{1,0:T(8,128)(2,1)} %refs_1_.1), channel_id=1, source_target_pairs={{0,1},{1,0},{2,3},{3,2},{4,5},{5,4},{6,7},{7,6},{8,9},{9,8},{10,11... | collective-permute-start | bytes 786440 | tf_op jit(solution)/shard_map/ppermute | solution.py:62
  1.2 7.3 %collective-permute-start.3 = (bf16[512,256]{1,0:T(8,128)(2,1)}, bf16[512,256]{1,0:T(8,128)(2,1)S(1)}, u32[]{:S(2)}, u32[]{:S(2)}) collective-permute-start(bf16[512,256]{1,0:T(8,128)(2,1)} %refs_2_.2), channel_id=1, source_target_pairs={{0,1},{1,0},{2,3},{3,2},{4,5},{5,4},{6,7},{7,6},{8,9},{9,8},{10,11... | collective-permute-start | bytes 786440 | tf_op jit(solution)/shard_map/ppermute | solution.py:62
  1.7 6.9 %collective-permute-start = (bf16[8,4,2048]{2,1,0:T(4,128)(2,1)}, bf16[8,4,2048]{2,1,0:T(4,128)(2,1)S(1)}, u32[]{:S(2)}, u32[]{:S(2)}) collective-permute-start(bf16[8,4,2048]{2,1,0:T(4,128)(2,1)} %refs_0_.3), channel_id=1, source_target_pairs={{0,2},{1,3},{2,0},{3,1},{4,6},{5,7},{6,4},{7,5},{8,10},{9,11},{10,... | collective-permute-start | bytes 393224 | tf_op jit(solution)/shard_map/ppermute | solution.py:62
  9.2 7.9 %collective-permute-start.7 = (bf16[512,1024]{1,0:T(8,128)(2,1)}, bf16[512,1024]{1,0:T(8,128)(2,1)S(1)}, u32[]{:S(2)}, u32[]{:S(2)}) collective-permute-start(bf16[512,1024]{1,0:T(8,128)(2,1)} %refs_8_.1), channel_id=1, source_target_pairs={{0,1},{1,0},{2,3},{3,2},{4,5},{5,4},{6,7},{7,6},{8,9},{9,8},{10,11... | collective-permute-start | bytes 3145736 | tf_op jit(solution)/shard_map/ppermute | solution.py:62
  9.3 7.9 %collective-permute-start.8 = (bf16[1024,512]{1,0:T(8,128)(2,1)}, bf16[1024,512]{1,0:T(8,128)(2,1)S(1)}, u32[]{:S(2)}, u32[]{:S(2)}) collective-permute-start(bf16[1024,512]{1,0:T(8,128)(2,1)} %refs_2_.3), channel_id=1, source_target_pairs={{0,1},{1,0},{2,3},{3,2},{4,5},{5,4},{6,7},{7,6},{8,9},{9,8},{10,11... | collective-permute-start | bytes 3145736 | tf_op jit(solution)/shard_map/ppermute | solution.py:62
  9.8 6.7 %collective-permute-start.5 = (bf16[32,768]{1,0:T(8,128)(2,1)S(1)}, bf16[32,768]{1,0:T(8,128)(2,1)S(1)}, u32[]{:S(2)}, u32[]{:S(2)}) collective-permute-start(bf16[32,768]{1,0:T(8,128)(2,1)S(1)} %get-tuple-element.53.refs_0_), channel_id=1, source_target_pairs={{0,4},{1,5},{2,6},{3,7},{4,0},{5,1},{6,2},{7,3},{8,12},{9,13},{10,... | collective-permute-start | bytes 147464 | tf_op jit(solution)/shard_map/ppermute | solution.py:62
  11.5 5.0 %collective-permute-start.6 = (bf16[32,768]{1,0:T(8,128)(2,1)S(1)}, bf16[32,768]{1,0:T(8,128)(2,1)S(1)}, u32[]{:S(2)}, u32[]{:S(2)}) collective-permute-start(bf16[32,768]{1,0:T(8,128)(2,1)S(1)} %get-tuple-element.54), channel_id=1, source_target_pairs={{0,6},{1,7},{2,4},{3,5},{4,2},{5,3},{6,0},{7,1},{8,14},{9,15},{10,... | collective-permute-start | bytes 147464 | tf_op jit(solution)/shard_map/ppermute | solution.py:62
  13.0 4.1 %collective-permute-start.4 = (bf16[32,768]{1,0:T(8,128)(2,1)S(1)}, bf16[32,768]{1,0:T(8,128)(2,1)S(1)}, u32[]{:S(2)}, u32[]{:S(2)}) collective-permute-start(bf16[32,768]{1,0:T(8,128)(2,1)S(1)} %get-tuple-element.54), channel_id=1, source_target_pairs={{0,2},{1,3},{2,0},{3,1},{4,6},{5,7},{6,4},{7,5},{8,10},{9,11},{10,... | collective-permute-start | bytes 147464 | tf_op jit(solution)/shard_map/ppermute | solution.py:62
  17.2 15.6 %collective-permute-start.13 = (bf16[512,256]{1,0:T(8,128)(2,1)S(1)}, bf16[512,256]{1,0:T(8,128)(2,1)S(1)}, u32[]{:S(2)}, u32[]{:S(2)}) collective-permute-start(bf16[512,256]{1,0:T(8,128)(2,1)S(1)} %copy-done.11), channel_id=1, source_target_pairs={{0,2},{1,3},{2,6},{3,7},{4,0},{5,1},{6,4},{7,5},{8,10},{9,11},{10,... | collective-permute-start | bytes 786440 | tf_op jit(solution)/shard_map/ppermute | solution.py:77
  18.4 14.4 %collective-permute-start.12 = (bf16[512,256]{1,0:T(8,128)(2,1)S(1)}, bf16[512,256]{1,0:T(8,128)(2,1)S(1)}, u32[]{:S(2)}, u32[]{:S(2)}) collective-permute-start(bf16[512,256]{1,0:T(8,128)(2,1)S(1)} %copy-done.11), channel_id=1, source_target_pairs={{0,0},{1,1},{2,4},{3,5},{4,2},{5,3},{6,6},{7,7},{8,8},{9,9},{10,12... | collective-permute-start | bytes 786440 | tf_op jit(solution)/shard_map/ppermute | solution.py:77
  19.0 7.0 %collective-permute-start.11 = (bf16[2,32,768]{2,1,0:T(8,128)(2,1)S(1)}, bf16[2,32,768]{2,1,0:T(8,128)(2,1)S(1)}, u32[]{:S(2)}, u32[]{:S(2)}) collective-permute-start(bf16[2,32,768]{2,1,0:T(8,128)(2,1)S(1)} %add_qkv.1.refs_0_), channel_id=1, source_target_pairs={{0,24},{1,25},{2,26},{3,27},{4,28},{5,29},{6,30},{7,31},{8,16},{9,... | collective-permute-start | bytes 294920 | tf_op jit(solution)/shard_map/ppermute | solution.py:62
  22.7 7.4 %collective-permute-start.10 = (bf16[2,32,768]{2,1,0:T(8,128)(2,1)S(1)}, bf16[2,32,768]{2,1,0:T(8,128)(2,1)S(1)}, u32[]{:S(2)}, u32[]{:S(2)}) collective-permute-start(bf16[2,32,768]{2,1,0:T(8,128)(2,1)S(1)} %add_qkv.1.refs_0_), channel_id=1, source_target_pairs={{0,16},{1,17},{2,18},{3,19},{4,20},{5,21},{6,22},{7,23},{8,24},{9,... | collective-permute-start | bytes 294920 | tf_op jit(solution)/shard_map/ppermute | solution.py:62
  22.7 7.4 %collective-permute-start.9 = (bf16[2,32,768]{2,1,0:T(8,128)(2,1)S(1)}, bf16[2,32,768]{2,1,0:T(8,128)(2,1)S(1)}, u32[]{:S(2)}, u32[]{:S(2)}) collective-permute-start(bf16[2,32,768]{2,1,0:T(8,128)(2,1)S(1)} %add_qkv.1.refs_0_), channel_id=1, source_target_pairs={{0,8},{1,9},{2,10},{3,11},{4,12},{5,13},{6,14},{7,15},{8,0},{9,1},... | collective-permute-start | bytes 294920 | tf_op jit(solution)/shard_map/ppermute | solution.py:62
  32.8 7.2 %collective-permute-start.15 = (bf16[512,256]{1,0:T(8,128)(2,1)S(1)}, bf16[512,256]{1,0:T(8,128)(2,1)S(1)}, u32[]{:S(2)}, u32[]{:S(2)}) collective-permute-start(bf16[512,256]{1,0:T(8,128)(2,1)S(1)} %collective-permute-done.12.refs_4_), channel_id=1, source_target_pairs={{0,1},{1,0},{2,3},{3,2},{4,5},{5,4},{6,7},{7,6},{8,9},{9,8},{10,11... | collective-permute-start | bytes 786440 | tf_op jit(solution)/shard_map/ppermute | solution.py:62
  32.8 7.2 %collective-permute-start.16 = (bf16[512,256]{1,0:T(8,128)(2,1)S(1)}, bf16[512,256]{1,0:T(8,128)(2,1)S(1)}, u32[]{:S(2)}, u32[]{:S(2)}) collective-permute-start(bf16[512,256]{1,0:T(8,128)(2,1)S(1)} %collective-permute-done.13.refs_6_), channel_id=1, source_target_pairs={{0,1},{1,0},{2,3},{3,2},{4,5},{5,4},{6,7},{7,6},{8,9},{9,8},{10,11... | collective-permute-start | bytes 786440 | tf_op jit(solution)/shard_map/ppermute | solution.py:62
  33.3 6.4 %collective-permute-start.14 = (bf16[32,1152]{1,0:T(8,128)(2,1)S(1)}, bf16[32,1152]{1,0:T(8,128)(2,1)S(1)}, u32[]{:S(2)}, u32[]{:S(2)}) collective-permute-start(bf16[32,1152]{1,0:T(8,128)(2,1)S(1)} %get-tuple-element.69), channel_id=1, source_target_pairs={{0,4},{1,5},{2,6},{3,7},{4,0},{5,1},{6,2},{7,3},{8,12},{9,13},{10,... | collective-permute-start | bytes 221192 | tf_op jit(solution)/shard_map/ppermute | solution.py:62
  40.0 6.7 %collective-permute-start.19 = (bf16[32,1152]{1,0:T(8,128)(2,1)S(1)}, bf16[32,1152]{1,0:T(8,128)(2,1)S(1)}, u32[]{:S(2)}, u32[]{:S(2)}) collective-permute-start(bf16[32,1152]{1,0:T(8,128)(2,1)S(1)} %merge_x.1.refs_0_), channel_id=1, source_target_pairs={{0,24},{1,25},{2,26},{3,27},{4,28},{5,29},{6,30},{7,31},{8,16},{9,... | collective-permute-start | bytes 221192 | tf_op jit(solution)/shard_map/ppermute | solution.py:62
  42.3 6.5 %collective-permute-start.18 = (bf16[32,1152]{1,0:T(8,128)(2,1)S(1)}, bf16[32,1152]{1,0:T(8,128)(2,1)S(1)}, u32[]{:S(2)}, u32[]{:S(2)}) collective-permute-start(bf16[32,1152]{1,0:T(8,128)(2,1)S(1)} %merge_x.1.refs_0_), channel_id=1, source_target_pairs={{0,16},{1,17},{2,18},{3,19},{4,20},{5,21},{6,22},{7,23},{8,24},{9,... | collective-permute-start | bytes 221192 | tf_op jit(solution)/shard_map/ppermute | solution.py:62
  42.3 6.5 %collective-permute-start.17 = (bf16[32,1152]{1,0:T(8,128)(2,1)S(1)}, bf16[32,1152]{1,0:T(8,128)(2,1)S(1)}, u32[]{:S(2)}, u32[]{:S(2)}) collective-permute-start(bf16[32,1152]{1,0:T(8,128)(2,1)S(1)} %merge_x.1.refs_0_), channel_id=1, source_target_pairs={{0,8},{1,9},{2,10},{3,11},{4,12},{5,13},{6,14},{7,15},{8,0},{9,1},... | collective-permute-start | bytes 221192 | tf_op jit(solution)/shard_map/ppermute | solution.py:62
  49.4 5.1 %collective-permute-start.22 = (bf16[2,32,256]{2,1,0:T(8,128)(2,1)S(1)}, bf16[2,32,256]{2,1,0:T(8,128)(2,1)S(1)}, u32[]{:S(2)}, u32[]{:S(2)}) collective-permute-start(bf16[2,32,256]{2,1,0:T(8,128)(2,1)S(1)} %out.1.refs_0_), channel_id=1, source_target_pairs={{0,6},{1,7},{2,4},{3,5},{4,2},{5,3},{6,0},{7,1},{8,14},{9,15},{10,... | collective-permute-start | bytes 98312 | tf_op jit(solution)/shard_map/ppermute | solution.py:62
  50.6 4.1 %collective-permute-start.21 = (bf16[2,32,256]{2,1,0:T(8,128)(2,1)S(1)}, bf16[2,32,256]{2,1,0:T(8,128)(2,1)S(1)}, u32[]{:S(2)}, u32[]{:S(2)}) collective-permute-start(bf16[2,32,256]{2,1,0:T(8,128)(2,1)S(1)} %out.1.refs_0_), channel_id=1, source_target_pairs={{0,4},{1,5},{2,6},{3,7},{4,0},{5,1},{6,2},{7,3},{8,12},{9,13},{10,... | collective-permute-start | bytes 98312 | tf_op jit(solution)/shard_map/ppermute | solution.py:62
  56.3 6.1 %collective-permute-start.25 = (bf16[2,2,32,256]{3,2,1,0:T(8,128)(2,1)S(1)}, bf16[2,2,32,256]{3,2,1,0:T(8,128)(2,1)S(1)}, u32[]{:S(2)}, u32[]{:S(2)}) collective-permute-start(bf16[2,2,32,256]{3,2,1,0:T(8,128)(2,1)S(1)} %add_out.1.refs_2_), channel_id=1, source_target_pairs={{0,24},{1,25},{2,26},{3,27},{4,28},{5,29},{6,30},{7,31},{8,16},{9,... | collective-permute-start | bytes 196616 | tf_op jit(solution)/shard_map/ppermute | solution.py:62
  57.9 5.9 %collective-permute-start.24 = (bf16[2,2,32,256]{3,2,1,0:T(8,128)(2,1)S(1)}, bf16[2,2,32,256]{3,2,1,0:T(8,128)(2,1)S(1)}, u32[]{:S(2)}, u32[]{:S(2)}) collective-permute-start(bf16[2,2,32,256]{3,2,1,0:T(8,128)(2,1)S(1)} %add_out.1.refs_2_), channel_id=1, source_target_pairs={{0,16},{1,17},{2,18},{3,19},{4,20},{5,21},{6,22},{7,23},{8,24},{9,... | collective-permute-start | bytes 196616 | tf_op jit(solution)/shard_map/ppermute | solution.py:62
  57.9 5.9 %collective-permute-start.23 = (bf16[2,2,32,256]{3,2,1,0:T(8,128)(2,1)S(1)}, bf16[2,2,32,256]{3,2,1,0:T(8,128)(2,1)S(1)}, u32[]{:S(2)}, u32[]{:S(2)}) collective-permute-start(bf16[2,2,32,256]{3,2,1,0:T(8,128)(2,1)S(1)} %add_out.1.refs_2_), channel_id=1, source_target_pairs={{0,8},{1,9},{2,10},{3,11},{4,12},{5,13},{6,14},{7,15},{8,0},{9,1},... | collective-permute-start | bytes 196616 | tf_op jit(solution)/shard_map/ppermute | solution.py:62
  64.8 5.0 %collective-permute-start.26 = (bf16[64,1024]{1,0:T(8,128)(2,1)S(1)}, bf16[64,1024]{1,0:T(8,128)(2,1)S(1)}, u32[]{:S(2)}, u32[]{:S(2)}) collective-permute-start(bf16[64,1024]{1,0:T(8,128)(2,1)S(1)} %get-tuple-element.78.refs_0_), channel_id=1, source_target_pairs={{0,2},{1,3},{2,0},{3,1},{4,6},{5,7},{6,4},{7,5},{8,10},{9,11},{10,... | collective-permute-start | bytes 393224 | tf_op jit(solution)/shard_map/ppermute | solution.py:62
  70.3 4.3 %collective-permute-start.27 = (bf16[64,512]{1,0:T(8,128)(2,1)S(1)}, bf16[64,512]{1,0:T(8,128)(2,1)S(1)}, u32[]{:S(2)}, u32[]{:S(2)}) collective-permute-start(bf16[64,512]{1,0:T(8,128)(2,1)S(1)} %get-tuple-element.81), channel_id=1, source_target_pairs={{0,4},{1,5},{2,6},{3,7},{4,0},{5,1},{6,2},{7,3},{8,12},{9,13},{10,... | collective-permute-start | bytes 196616 | tf_op jit(solution)/shard_map/ppermute | solution.py:62
  74.7 6.1 %collective-permute-start.30 = (bf16[64,512]{1,0:T(8,128)(2,1)S(1)}, bf16[64,512]{1,0:T(8,128)(2,1)S(1)}, u32[]{:S(2)}, u32[]{:S(2)}) collective-permute-start(bf16[64,512]{1,0:T(8,128)(2,1)S(1)} %add_x.1.refs_0_), channel_id=1, source_target_pairs={{0,24},{1,25},{2,26},{3,27},{4,28},{5,29},{6,30},{7,31},{8,16},{9,... | collective-permute-start | bytes 196616 | tf_op jit(solution)/shard_map/ppermute | solution.py:62
  76.7 5.6 %collective-permute-start.29 = (bf16[64,512]{1,0:T(8,128)(2,1)S(1)}, bf16[64,512]{1,0:T(8,128)(2,1)S(1)}, u32[]{:S(2)}, u32[]{:S(2)}) collective-permute-start(bf16[64,512]{1,0:T(8,128)(2,1)S(1)} %add_x.1.refs_0_), channel_id=1, source_target_pairs={{0,16},{1,17},{2,18},{3,19},{4,20},{5,21},{6,22},{7,23},{8,24},{9,... | collective-permute-start | bytes 196616 | tf_op jit(solution)/shard_map/ppermute | solution.py:62
  77.4 5.0 %collective-permute-start.28 = (bf16[64,512]{1,0:T(8,128)(2,1)S(1)}, bf16[64,512]{1,0:T(8,128)(2,1)S(1)}, u32[]{:S(2)}, u32[]{:S(2)}) collective-permute-start(bf16[64,512]{1,0:T(8,128)(2,1)S(1)} %add_x.1.refs_0_), channel_id=1, source_target_pairs={{0,8},{1,9},{2,10},{3,11},{4,12},{5,13},{6,14},{7,15},{8,0},{9,1},... | collective-permute-start | bytes 196616 | tf_op jit(solution)/shard_map/ppermute | solution.py:62
  82.4 4.0 %collective-permute-start.32 = (bf16[32,512]{1,0:T(8,128)(2,1)S(1)}, bf16[32,512]{1,0:T(8,128)(2,1)S(1)}, u32[]{:S(2)}, u32[]{:S(2)}) collective-permute-start(bf16[32,512]{1,0:T(8,128)(2,1)S(1)} %get-tuple-element.82.refs_0_), channel_id=1, source_target_pairs={{0,4},{1,5},{2,6},{3,7},{4,0},{5,1},{6,2},{7,3},{8,12},{9,13},{10,... | collective-permute-start | bytes 98312 | tf_op jit(solution)/shard_map/ppermute | solution.py:62
  82.8 4.8 %collective-permute-start.33 = (bf16[32,512]{1,0:T(8,128)(2,1)S(1)}, bf16[32,512]{1,0:T(8,128)(2,1)S(1)}, u32[]{:S(2)}, u32[]{:S(2)}) collective-permute-start(bf16[32,512]{1,0:T(8,128)(2,1)S(1)} %get-tuple-element.83), channel_id=1, source_target_pairs={{0,6},{1,7},{2,4},{3,5},{4,2},{5,3},{6,0},{7,1},{8,14},{9,15},{10,... | collective-permute-start | bytes 98312 | tf_op jit(solution)/shard_map/ppermute | solution.py:62
  (14 other events, 280.9 us)

commit v15 on v14

--- a/solution.py
+++ b/solution.py
@@ -114,9 +114,9 @@
     )(*ins)
 
 
-def side_by_side(blocks, start, size):
+def side_by_side(blocks, start, size, kind=F32):
     return jnp.concatenate(
-        [blocks[x, :, start : start + size].astype(F32) for x in range(blocks.shape[0])], axis=1
+        [blocks[x, :, start : start + size].astype(kind) for x in range(blocks.shape[0])], axis=1
     )
 
 
@@ -238,7 +238,7 @@
     for dz in range(nz):
         span = at(place.z_partner(dz), nx * cols)
         for k, target in enumerate((qs, ks, vs)):
-            target[:, span] = side_by_side(gathered[dz], k * cols, cols)
+            target[:, span] = side_by_side(gathered[dz], k * cols, cols, target.dtype)
 
     window = k_rows.shape[1]
 
@@ -264,8 +264,11 @@
             slot = start + lax.broadcasted_iota(jnp.int32, (window, width), 0)
             for source, fresh, rows in ((keys, ks, k_rows), (values, vs, v_rows)):
                 block = source[i, pl.ds(start, window), :].astype(F32)
+                first = i * steps // 16 * 16
+                some = fresh[first : first + 16, :].astype(F32)
                 for t in range(steps):
-                    at_row = fresh[i * steps + t : i * steps + t + 1, :]
+                    row_at = i * steps + t - first
+                    at_row = some[row_at : row_at + 1, :]
                     block = jnp.where(slot == base + t, at_row, block)
                 rows[i] = block.astype(BF16)
             for copy in copies(i):
@@ -297,8 +300,8 @@
         pair = pairs_of(qs[mine, :])
         key = keys[these].reshape(cached, width)
         value = values[these].reshape(cached, width)
-        new_key = jnp.concatenate([ks[mine, :].astype(BF16), blank], axis=0)
-        new_value = jnp.concatenate([vs[mine, :].astype(BF16), blank], axis=0)
+        new_key = jnp.concatenate([ks[mine, :], blank], axis=0)
+        new_value = jnp.concatenate([vs[mine, :], blank], axis=0)
         for j in range(heads // 2):
             span = slice(j * tile, (j + 1) * tile)
             these_rows = slice(j * 2 * rows, (j + 1) * 2 * rows)
@@ -409,10 +412,10 @@
 
 def up_kernel(place, *refs):
     ny, nz = place.ny, place.nz
-    toks = refs[:ny]
-    gathered = refs[ny : ny + nz]
-    gain, shift, own, sibling, bias, out, mid_out, proj, normed, flat = refs[ny + nz :]
-    group, steps, _ = toks[0].shape
+    tokens, flats = refs[:2]
+    gathered = refs[2 : 2 + nz]
+    gain, shift, own, sibling, bias, out, mid_out, proj, normed, flat = refs[2 + nz :]
+    group, steps, _ = tokens.shape
     rows = group * steps
     cols = gathered[0].shape[3]
     for dz in range(nz):
@@ -421,8 +424,10 @@
             proj[y * rows : (y + 1) * rows, span] = side_by_side(gathered[dz].at[y], 0, cols)
     for j in range(ny):
         here = at(place.y_before(j), rows)
-        flatten(toks[j], flat, 0)
-        mid = flat[...] + proj[here, :]
+        if j == 0:
+            flatten(tokens, flat, 0)
+        mine = flat[...] if j == 0 else flats[(j - 1) * rows : j * rows, :]
+        mid = mine + proj[here, :]
         if j == 0:
             mid_out[...] = mid
         normed[here, :] = layer_norm(mid, gain[...], shift[...]).astype(BF16)
@@ -533,12 +538,12 @@
         scratch=[pltpu.VMEM((rows, width), F32), pltpu.SemaphoreType.DMA((3,))],
         limit=52.75,
     )
-    parts = call(
+    *parts, flats = call(
         bind(qkv_kernel, place),
         "norm_qkv",
         [normed, *toks[1:], scales, biases, *own, *siblings],
-        [shape((rows, 3 * cols))] * ny,
-        scratch=[pltpu.VMEM(((ny - 1) * rows, width), F32), pltpu.VMEM((ny * rows, width), BF16)],
+        [shape((rows, 3 * cols))] * ny + [shape(((ny - 1) * rows, width), F32)],
+        scratch=[pltpu.VMEM((ny * rows, width), BF16)],
     )
     *parts, tied_up, tied_down = lax.optimization_barrier((*parts, w_up, w_down))
     w_up_sibling = place.move(tied_up, dc=1)
@@ -577,8 +582,8 @@
         out_specs=[HBM, HBM] + [VMEM] * nx,
         scratch=[
             pltpu.VMEM((rows, width), F32),
-            pltpu.VMEM((rows, width), F32),
-            pltpu.VMEM((rows, width), F32),
+            pltpu.VMEM((rows, width), BF16),
+            pltpu.VMEM((rows, width), BF16),
             pltpu.VMEM((heads * pack * steps, pack * slots + LANES), F32),
             pltpu.VMEM((rows, width), F32),
             pltpu.VMEM((rows, LANES), F32),
@@ -615,7 +620,8 @@
         bind(up_kernel, place),
         "norm_up",
         [
-            *toks,
+            tokens,
+            flats,
             *place.gather_z(projected),
             row(norm2_gain),
             row(norm2_bias),

time: 89.6 us -> 89.8 us (level)
  no operation moved by 1% of the time
where the time goes in v15:
time: 89.8 us; the launch traced here: 89.6 us
  starting transfers between devices  41 us (46%)
  waiting for transfers between devices  34.8 us (39%)
  Pallas kernels  10.5 us (12%)
  other arithmetic  1.44 us (2%)
  local copies, waits for them, and re-layouts  0.97 us (1%)
  between operations  0.93 us (1%)
    ppermute x32, starting transfers between devices, move(): return lax.ppermute(value, ('seq', 'req'), pairs)  39.1 us
    ppermute x32, waiting for transfers between devices, move(): return lax.ppermute(value, ('seq', 'req'), pairs)  34.8 us
    pallas_call x13, Pallas kernels, call(): pl.pallas_call(kernel, name=name, out_shape=outs, in_specs=in_specs or [V...  10.5 us
    ppermute x2, starting transfers between devices, transpose(): return lax.ppermute(value, ('seq', 'req'), pairs)  1.86 us
  transfers between devices with their start and end apart: 34, of which 20 were waited for; matrix products, arithmetic and copies ran while one was open for 2% of the time, Pallas kernels for 8%

profile of v15, /device:TPU:0, one launch (start us, length us, event | category | flops | bytes accessed | tf_op | source)
XLA Modules:
  0.0 89.6 jit_solution(18443966904560305074)
XLA Ops:
  1.7 2.6 %collective-permute-start = (bf16[8,4,2048]{2,1,0:T(4,128)(2,1)}, bf16[8,4,2048]{2,1,0:T(4,128)(2,1)S(1)}, u32[]{:S(2)}, u32[]{:S(2)}) collective-permute-start(bf16[8,4,2048]{2,1,0:T(4,128)(2,1)} %refs_0_.3), channel_id=1, source_target_pairs={{0,2},{1,3},{2,0},{3,1},{4,6},{5,7},{6,4},{7,5},{8,10},{9,11},{10,... | collective-permute-start | bytes 393224 | tf_op jit(solution)/shard_map/ppermute | solution.py:62
  9.8 1.7 %collective-permute-start.5 = (bf16[32,768]{1,0:T(8,128)(2,1)S(1)}, bf16[32,768]{1,0:T(8,128)(2,1)S(1)}, u32[]{:S(2)}, u32[]{:S(2)}) collective-permute-start(bf16[32,768]{1,0:T(8,128)(2,1)S(1)} %get-tuple-element.55.refs_0_), channel_id=1, source_target_pairs={{0,4},{1,5},{2,6},{3,7},{4,0},{5,1},{6,2},{7,3},{8,12},{9,13},{10,... | collective-permute-start | bytes 147464 | tf_op jit(solution)/shard_map/ppermute | solution.py:62
  11.5 1.5 %collective-permute-start.6 = (bf16[32,768]{1,0:T(8,128)(2,1)S(1)}, bf16[32,768]{1,0:T(8,128)(2,1)S(1)}, u32[]{:S(2)}, u32[]{:S(2)}) collective-permute-start(bf16[32,768]{1,0:T(8,128)(2,1)S(1)} %get-tuple-element.56), channel_id=1, source_target_pairs={{0,6},{1,7},{2,4},{3,5},{4,2},{5,3},{6,0},{7,1},{8,14},{9,15},{10,... | collective-permute-start | bytes 147464 | tf_op jit(solution)/shard_map/ppermute | solution.py:62
  13.3 3.2 %caches.1 = (bf16[8,64,2048]{2,1,0:T(8,128)(2,1)}, bf16[8,64,2048]{2,1,0:T(8,128)(2,1)}, bf16[8,64,2048]{2,1,0:T(8,128)(2,1)S(1)}, bf16[8,64,2048]{2,1,0:T(8,128)(2,1)S(1)}, f32[8,128]{1,0:T(8,128)S(1)}) custom-call(bf16[8,64,2048]{2,1,0:T(8,128)(2,1)S(1)} %copy-done, bf16[8,64,2048]{2,1,0:T(8,128)(2,1)} %values_in), custom_call_target="tpu_custom_call" | custom-call | bytes 16777216 | tf_op jit(solution)/shard_map/caches/pallas_call | solution.py:104
  17.2 1.2 %collective-permute-start.13 = (bf16[512,256]{1,0:T(8,128)(2,1)S(1)}, bf16[512,256]{1,0:T(8,128)(2,1)S(1)}, u32[]{:S(2)}, u32[]{:S(2)}) collective-permute-start(bf16[512,256]{1,0:T(8,128)(2,1)S(1)} %copy-done.11), channel_id=1, source_target_pairs={{0,2},{1,3},{2,6},{3,7},{4,0},{5,1},{6,4},{7,5},{8,10},{9,11},{10,... | collective-permute-start | bytes 786440 | tf_op jit(solution)/shard_map/ppermute | solution.py:77
  19.1 3.7 %collective-permute-start.11 = (bf16[2,32,768]{2,1,0:T(8,128)(2,1)S(1)}, bf16[2,32,768]{2,1,0:T(8,128)(2,1)S(1)}, u32[]{:S(2)}, u32[]{:S(2)}) collective-permute-start(bf16[2,32,768]{2,1,0:T(8,128)(2,1)S(1)} %add_qkv.1.refs_0_), channel_id=1, source_target_pairs={{0,24},{1,25},{2,26},{3,27},{4,28},{5,29},{6,30},{7,31},{8,16},{9,... | collective-permute-start | bytes 294920 | tf_op jit(solution)/shard_map/ppermute | solution.py:62
  23.5 2.6 %collective-permute-done.11.refs_3_ = bf16[2,32,768]{2,1,0:T(8,128)(2,1)S(1)} collective-permute-done((bf16[2,32,768]{2,1,0:T(8,128)(2,1)S(1)}, bf16[2,32,768]{2,1,0:T(8,128)(2,1)S(1)}, u32[]{:S(2)}, u32[]{:S(2)}) %collective-permute-start.11) | collective-permute-done | bytes 98336 | tf_op jit(solution)/shard_map/ppermute | solution.py:62
  26.1 4.0 %collective-permute-done.10.refs_2_ = bf16[2,32,768]{2,1,0:T(8,128)(2,1)S(1)} collective-permute-done((bf16[2,32,768]{2,1,0:T(8,128)(2,1)S(1)}, bf16[2,32,768]{2,1,0:T(8,128)(2,1)S(1)}, u32[]{:S(2)}, u32[]{:S(2)}) %collective-permute-start.10) | collective-permute-done | bytes 98336 | tf_op jit(solution)/shard_map/ppermute | solution.py:62
  30.2 2.5 %attention.1 = (bf16[8,64,2048]{2,1,0:T(8,128)(2,1)}, bf16[8,64,2048]{2,1,0:T(8,128)(2,1)}, bf16[32,1152]{1,0:T(8,128)(2,1)S(1)}, bf16[32,1152]{1,0:T(8,128)(2,1)S(1)}) custom-call(bf16[2,32,768]{2,1,0:T(8,128)(2,1)S(1)} %add_qkv.1.refs_0_, bf16[2,32,768]{2,1,0:T(8,128)(2,1)S(1)} %collective-permute-done.9.refs_1_, ...), custom_call_target="tpu_custom_call", output_to_operand_aliasing={{0}: (7, {}), {1}: (8, {})} | custom-call | bytes 1048576 | tf_op jit(solution)/shard_map/attention/pallas_call | solution.py:104
  33.3 3.8 %collective-permute-start.14 = (bf16[32,1152]{1,0:T(8,128)(2,1)S(1)}, bf16[32,1152]{1,0:T(8,128)(2,1)S(1)}, u32[]{:S(2)}, u32[]{:S(2)}) collective-permute-start(bf16[32,1152]{1,0:T(8,128)(2,1)S(1)} %get-tuple-element.71), channel_id=1, source_target_pairs={{0,4},{1,5},{2,6},{3,7},{4,0},{5,1},{6,2},{7,3},{8,12},{9,13},{10,... | collective-permute-start | bytes 221192 | tf_op jit(solution)/shard_map/ppermute | solution.py:62
  37.1 2.5 %collective-permute-done.14.refs_1_ = bf16[32,1152]{1,0:T(8,128)(2,1)S(1)} collective-permute-done((bf16[32,1152]{1,0:T(8,128)(2,1)S(1)}, bf16[32,1152]{1,0:T(8,128)(2,1)S(1)}, u32[]{:S(2)}, u32[]{:S(2)}) %collective-permute-start.14) | collective-permute-done | bytes 73760 | tf_op jit(solution)/shard_map/ppermute | solution.py:62
  39.9 2.4 %collective-permute-start.19 = (bf16[32,1152]{1,0:T(8,128)(2,1)S(1)}, bf16[32,1152]{1,0:T(8,128)(2,1)S(1)}, u32[]{:S(2)}, u32[]{:S(2)}) collective-permute-start(bf16[32,1152]{1,0:T(8,128)(2,1)S(1)} %merge_x.1.refs_0_), channel_id=1, source_target_pairs={{0,24},{1,25},{2,26},{3,27},{4,28},{5,29},{6,30},{7,31},{8,16},{9,... | collective-permute-start | bytes 221192 | tf_op jit(solution)/shard_map/ppermute | solution.py:62
  42.2 2.1 %collective-permute-start.17 = (bf16[32,1152]{1,0:T(8,128)(2,1)S(1)}, bf16[32,1152]{1,0:T(8,128)(2,1)S(1)}, u32[]{:S(2)}, u32[]{:S(2)}) collective-permute-start(bf16[32,1152]{1,0:T(8,128)(2,1)S(1)} %merge_x.1.refs_0_), channel_id=1, source_target_pairs={{0,8},{1,9},{2,10},{3,11},{4,12},{5,13},{6,14},{7,15},{8,0},{9,1},... | collective-permute-start | bytes 221192 | tf_op jit(solution)/shard_map/ppermute | solution.py:62
  44.3 2.1 %collective-permute-done.19.refs_3_ = bf16[32,1152]{1,0:T(8,128)(2,1)S(1)} collective-permute-done((bf16[32,1152]{1,0:T(8,128)(2,1)S(1)}, bf16[32,1152]{1,0:T(8,128)(2,1)S(1)}, u32[]{:S(2)}, u32[]{:S(2)}) %collective-permute-start.19) | collective-permute-done | bytes 73760 | tf_op jit(solution)/shard_map/ppermute | solution.py:62
  46.4 2.6 %collective-permute-done.18.refs_2_ = bf16[32,1152]{1,0:T(8,128)(2,1)S(1)} collective-permute-done((bf16[32,1152]{1,0:T(8,128)(2,1)S(1)}, bf16[32,1152]{1,0:T(8,128)(2,1)S(1)}, u32[]{:S(2)}, u32[]{:S(2)}) %collective-permute-start.18) | collective-permute-done | bytes 73760 | tf_op jit(solution)/shard_map/ppermute | solution.py:62
  49.6 1.2 %collective-permute-start.22 = (bf16[2,32,256]{2,1,0:T(8,128)(2,1)S(1)}, bf16[2,32,256]{2,1,0:T(8,128)(2,1)S(1)}, u32[]{:S(2)}, u32[]{:S(2)}) collective-permute-start(bf16[2,32,256]{2,1,0:T(8,128)(2,1)S(1)} %out.1.refs_0_), channel_id=1, source_target_pairs={{0,6},{1,7},{2,4},{3,5},{4,2},{5,3},{6,0},{7,1},{8,14},{9,15},{10,... | collective-permute-start | bytes 98312 | tf_op jit(solution)/shard_map/ppermute | solution.py:62
  50.8 1.3 %collective-permute-start.21 = (bf16[2,32,256]{2,1,0:T(8,128)(2,1)S(1)}, bf16[2,32,256]{2,1,0:T(8,128)(2,1)S(1)}, u32[]{:S(2)}, u32[]{:S(2)}) collective-permute-start(bf16[2,32,256]{2,1,0:T(8,128)(2,1)S(1)} %out.1.refs_0_), channel_id=1, source_target_pairs={{0,4},{1,5},{2,6},{3,7},{4,0},{5,1},{6,2},{7,3},{8,12},{9,13},{10,... | collective-permute-start | bytes 98312 | tf_op jit(solution)/shard_map/ppermute | solution.py:62
  53.2 1.5 %collective-permute-done.22.refs_3_ = bf16[2,32,256]{2,1,0:T(8,128)(2,1)S(1)} collective-permute-done((bf16[2,32,256]{2,1,0:T(8,128)(2,1)S(1)}, bf16[2,32,256]{2,1,0:T(8,128)(2,1)S(1)}, u32[]{:S(2)}, u32[]{:S(2)}) %collective-permute-start.22) | collective-permute-done | bytes 32800 | tf_op jit(solution)/shard_map/ppermute | solution.py:62
  54.7 1.3 %collective-permute-done.20.refs_1_ = bf16[2,32,256]{2,1,0:T(8,128)(2,1)S(1)} collective-permute-done((bf16[2,32,256]{2,1,0:T(8,128)(2,1)S(1)}, bf16[2,32,256]{2,1,0:T(8,128)(2,1)S(1)}, u32[]{:S(2)}, u32[]{:S(2)}) %collective-permute-start.20) | collective-permute-done | bytes 32800 | tf_op jit(solution)/shard_map/ppermute | solution.py:62
  56.1 1.9 %collective-permute-start.25 = (bf16[2,2,32,256]{3,2,1,0:T(8,128)(2,1)S(1)}, bf16[2,2,32,256]{3,2,1,0:T(8,128)(2,1)S(1)}, u32[]{:S(2)}, u32[]{:S(2)}) collective-permute-start(bf16[2,2,32,256]{3,2,1,0:T(8,128)(2,1)S(1)} %add_out.1.refs_2_), channel_id=1, source_target_pairs={{0,24},{1,25},{2,26},{3,27},{4,28},{5,29},{6,30},{7,31},{8,16},{9,... | collective-permute-start | bytes 196616 | tf_op jit(solution)/shard_map/ppermute | solution.py:62
  57.9 2.6 %collective-permute-start.23 = (bf16[2,2,32,256]{3,2,1,0:T(8,128)(2,1)S(1)}, bf16[2,2,32,256]{3,2,1,0:T(8,128)(2,1)S(1)}, u32[]{:S(2)}, u32[]{:S(2)}) collective-permute-start(bf16[2,2,32,256]{3,2,1,0:T(8,128)(2,1)S(1)} %add_out.1.refs_2_), channel_id=1, source_target_pairs={{0,8},{1,9},{2,10},{3,11},{4,12},{5,13},{6,14},{7,15},{8,0},{9,1},... | collective-permute-start | bytes 196616 | tf_op jit(solution)/shard_map/ppermute | solution.py:62
  60.5 1.7 %collective-permute-done.25.refs_5_ = bf16[2,2,32,256]{3,2,1,0:T(8,128)(2,1)S(1)} collective-permute-done((bf16[2,2,32,256]{3,2,1,0:T(8,128)(2,1)S(1)}, bf16[2,2,32,256]{3,2,1,0:T(8,128)(2,1)S(1)}, u32[]{:S(2)}, u32[]{:S(2)}) %collective-permute-start.25) | collective-permute-done | bytes 65568 | tf_op jit(solution)/shard_map/ppermute | solution.py:62
  62.2 1.4 %collective-permute-done.24.refs_4_ = bf16[2,2,32,256]{3,2,1,0:T(8,128)(2,1)S(1)} collective-permute-done((bf16[2,2,32,256]{3,2,1,0:T(8,128)(2,1)S(1)}, bf16[2,2,32,256]{3,2,1,0:T(8,128)(2,1)S(1)}, u32[]{:S(2)}, u32[]{:S(2)}) %collective-permute-start.24) | collective-permute-done | bytes 65568 | tf_op jit(solution)/shard_map/ppermute | solution.py:62
  64.5 1.5 %collective-permute-start.26 = (bf16[64,1024]{1,0:T(8,128)(2,1)S(1)}, bf16[64,1024]{1,0:T(8,128)(2,1)S(1)}, u32[]{:S(2)}, u32[]{:S(2)}) collective-permute-start(bf16[64,1024]{1,0:T(8,128)(2,1)S(1)} %get-tuple-element.80.refs_0_), channel_id=1, source_target_pairs={{0,2},{1,3},{2,0},{3,1},{4,6},{5,7},{6,4},{7,5},{8,10},{9,11},{10,... | collective-permute-start | bytes 393224 | tf_op jit(solution)/shard_map/ppermute | solution.py:62
  66.0 3.6 %collective-permute-done.26.refs_1_ = bf16[64,1024]{1,0:T(8,128)(2,1)S(1)} collective-permute-done((bf16[64,1024]{1,0:T(8,128)(2,1)S(1)}, bf16[64,1024]{1,0:T(8,128)(2,1)S(1)}, u32[]{:S(2)}, u32[]{:S(2)}) %collective-permute-start.26) | collective-permute-done | bytes 131104 | tf_op jit(solution)/shard_map/ppermute | solution.py:62
  70.8 3.6 %collective-permute-done.27.refs_1_ = bf16[64,512]{1,0:T(8,128)(2,1)S(1)} collective-permute-done((bf16[64,512]{1,0:T(8,128)(2,1)S(1)}, bf16[64,512]{1,0:T(8,128)(2,1)S(1)}, u32[]{:S(2)}, u32[]{:S(2)}) %collective-permute-start.27) | collective-permute-done | bytes 65568 | tf_op jit(solution)/shard_map/ppermute | solution.py:62
  74.4 1.9 %collective-permute-start.30 = (bf16[64,512]{1,0:T(8,128)(2,1)S(1)}, bf16[64,512]{1,0:T(8,128)(2,1)S(1)}, u32[]{:S(2)}, u32[]{:S(2)}) collective-permute-start(bf16[64,512]{1,0:T(8,128)(2,1)S(1)} %add_x.1.refs_0_), channel_id=1, source_target_pairs={{0,24},{1,25},{2,26},{3,27},{4,28},{5,29},{6,30},{7,31},{8,16},{9,... | collective-permute-start | bytes 196616 | tf_op jit(solution)/shard_map/ppermute | solution.py:62
  77.1 1.8 %collective-permute-start.28 = (bf16[64,512]{1,0:T(8,128)(2,1)S(1)}, bf16[64,512]{1,0:T(8,128)(2,1)S(1)}, u32[]{:S(2)}, u32[]{:S(2)}) collective-permute-start(bf16[64,512]{1,0:T(8,128)(2,1)S(1)} %add_x.1.refs_0_), channel_id=1, source_target_pairs={{0,8},{1,9},{2,10},{3,11},{4,12},{5,13},{6,14},{7,15},{8,0},{9,1},... | collective-permute-start | bytes 196616 | tf_op jit(solution)/shard_map/ppermute | solution.py:62
  78.8 1.7 %collective-permute-done.30.refs_3_ = bf16[64,512]{1,0:T(8,128)(2,1)S(1)} collective-permute-done((bf16[64,512]{1,0:T(8,128)(2,1)S(1)}, bf16[64,512]{1,0:T(8,128)(2,1)S(1)}, u32[]{:S(2)}, u32[]{:S(2)}) %collective-permute-start.30) | collective-permute-done | bytes 65568 | tf_op jit(solution)/shard_map/ppermute | solution.py:62
  80.5 1.5 %collective-permute-done.29.refs_2_ = bf16[64,512]{1,0:T(8,128)(2,1)S(1)} collective-permute-done((bf16[64,512]{1,0:T(8,128)(2,1)S(1)}, bf16[64,512]{1,0:T(8,128)(2,1)S(1)}, u32[]{:S(2)}, u32[]{:S(2)}) %collective-permute-start.29) | collective-permute-done | bytes 65568 | tf_op jit(solution)/shard_map/ppermute | solution.py:62
  82.9 2.0 %collective-permute-start.33 = (bf16[32,512]{1,0:T(8,128)(2,1)S(1)}, bf16[32,512]{1,0:T(8,128)(2,1)S(1)}, u32[]{:S(2)}, u32[]{:S(2)}) collective-permute-start(bf16[32,512]{1,0:T(8,128)(2,1)S(1)} %get-tuple-element.85), channel_id=1, source_target_pairs={{0,6},{1,7},{2,4},{3,5},{4,2},{5,3},{6,0},{7,1},{8,14},{9,15},{10,... | collective-permute-start | bytes 98312 | tf_op jit(solution)/shard_map/ppermute | solution.py:62
  86.1 1.6 %collective-permute-done.33.refs_3_ = bf16[32,512]{1,0:T(8,128)(2,1)S(1)} collective-permute-done((bf16[32,512]{1,0:T(8,128)(2,1)S(1)}, bf16[32,512]{1,0:T(8,128)(2,1)S(1)}, u32[]{:S(2)}, u32[]{:S(2)}) %collective-permute-start.33) | collective-permute-done | bytes 32800 | tf_op jit(solution)/shard_map/ppermute | solution.py:62
  (76 shorter events, 18.4 us)
Async XLA Ops:
  0.6 7.9 %collective-permute-start.1 = (bf16[512,256]{1,0:T(8,128)(2,1)}, bf16[512,256]{1,0:T(8,128)(2,1)S(1)}, u32[]{:S(2)}, u32[]{:S(2)}) collective-permute-start(bf16[512,256]{1,0:T(8,128)(2,1)} %refs_0_.2), channel_id=1, source_target_pairs={{0,1},{1,0},{2,3},{3,2},{4,5},{5,4},{6,7},{7,6},{8,9},{9,8},{10,11... | collective-permute-start | bytes 786440 | tf_op jit(solution)/shard_map/ppermute | solution.py:62
  1.2 7.4 %collective-permute-start.2 = (bf16[512,256]{1,0:T(8,128)(2,1)}, bf16[512,256]{1,0:T(8,128)(2,1)S(1)}, u32[]{:S(2)}, u32[]{:S(2)}) collective-permute-start(bf16[512,256]{1,0:T(8,128)(2,1)} %refs_1_.1), channel_id=1, source_target_pairs={{0,1},{1,0},{2,3},{3,2},{4,5},{5,4},{6,7},{7,6},{8,9},{9,8},{10,11... | collective-permute-start | bytes 786440 | tf_op jit(solution)/shard_map/ppermute | solution.py:62
  1.2 7.3 %collective-permute-start.3 = (bf16[512,256]{1,0:T(8,128)(2,1)}, bf16[512,256]{1,0:T(8,128)(2,1)S(1)}, u32[]{:S(2)}, u32[]{:S(2)}) collective-permute-start(bf16[512,256]{1,0:T(8,128)(2,1)} %refs_2_.2), channel_id=1, source_target_pairs={{0,1},{1,0},{2,3},{3,2},{4,5},{5,4},{6,7},{7,6},{8,9},{9,8},{10,11... | collective-permute-start | bytes 786440 | tf_op jit(solution)/shard_map/ppermute | solution.py:62
  1.7 6.9 %collective-permute-start = (bf16[8,4,2048]{2,1,0:T(4,128)(2,1)}, bf16[8,4,2048]{2,1,0:T(4,128)(2,1)S(1)}, u32[]{:S(2)}, u32[]{:S(2)}) collective-permute-start(bf16[8,4,2048]{2,1,0:T(4,128)(2,1)} %refs_0_.3), channel_id=1, source_target_pairs={{0,2},{1,3},{2,0},{3,1},{4,6},{5,7},{6,4},{7,5},{8,10},{9,11},{10,... | collective-permute-start | bytes 393224 | tf_op jit(solution)/shard_map/ppermute | solution.py:62
  9.2 7.9 %collective-permute-start.7 = (bf16[512,1024]{1,0:T(8,128)(2,1)}, bf16[512,1024]{1,0:T(8,128)(2,1)S(1)}, u32[]{:S(2)}, u32[]{:S(2)}) collective-permute-start(bf16[512,1024]{1,0:T(8,128)(2,1)} %refs_8_.1), channel_id=1, source_target_pairs={{0,1},{1,0},{2,3},{3,2},{4,5},{5,4},{6,7},{7,6},{8,9},{9,8},{10,11... | collective-permute-start | bytes 3145736 | tf_op jit(solution)/shard_map/ppermute | solution.py:62
  9.3 7.8 %collective-permute-start.8 = (bf16[1024,512]{1,0:T(8,128)(2,1)}, bf16[1024,512]{1,0:T(8,128)(2,1)S(1)}, u32[]{:S(2)}, u32[]{:S(2)}) collective-permute-start(bf16[1024,512]{1,0:T(8,128)(2,1)} %refs_2_.3), channel_id=1, source_target_pairs={{0,1},{1,0},{2,3},{3,2},{4,5},{5,4},{6,7},{7,6},{8,9},{9,8},{10,11... | collective-permute-start | bytes 3145736 | tf_op jit(solution)/shard_map/ppermute | solution.py:62
  9.8 6.7 %collective-permute-start.5 = (bf16[32,768]{1,0:T(8,128)(2,1)S(1)}, bf16[32,768]{1,0:T(8,128)(2,1)S(1)}, u32[]{:S(2)}, u32[]{:S(2)}) collective-permute-start(bf16[32,768]{1,0:T(8,128)(2,1)S(1)} %get-tuple-element.55.refs_0_), channel_id=1, source_target_pairs={{0,4},{1,5},{2,6},{3,7},{4,0},{5,1},{6,2},{7,3},{8,12},{9,13},{10,... | collective-permute-start | bytes 147464 | tf_op jit(solution)/shard_map/ppermute | solution.py:62
  11.5 5.0 %collective-permute-start.6 = (bf16[32,768]{1,0:T(8,128)(2,1)S(1)}, bf16[32,768]{1,0:T(8,128)(2,1)S(1)}, u32[]{:S(2)}, u32[]{:S(2)}) collective-permute-start(bf16[32,768]{1,0:T(8,128)(2,1)S(1)} %get-tuple-element.56), channel_id=1, source_target_pairs={{0,6},{1,7},{2,4},{3,5},{4,2},{5,3},{6,0},{7,1},{8,14},{9,15},{10,... | collective-permute-start | bytes 147464 | tf_op jit(solution)/shard_map/ppermute | solution.py:62
  13.0 4.1 %collective-permute-start.4 = (bf16[32,768]{1,0:T(8,128)(2,1)S(1)}, bf16[32,768]{1,0:T(8,128)(2,1)S(1)}, u32[]{:S(2)}, u32[]{:S(2)}) collective-permute-start(bf16[32,768]{1,0:T(8,128)(2,1)S(1)} %get-tuple-element.56), channel_id=1, source_target_pairs={{0,2},{1,3},{2,0},{3,1},{4,6},{5,7},{6,4},{7,5},{8,10},{9,11},{10,... | collective-permute-start | bytes 147464 | tf_op jit(solution)/shard_map/ppermute | solution.py:62
  17.2 15.5 %collective-permute-start.13 = (bf16[512,256]{1,0:T(8,128)(2,1)S(1)}, bf16[512,256]{1,0:T(8,128)(2,1)S(1)}, u32[]{:S(2)}, u32[]{:S(2)}) collective-permute-start(bf16[512,256]{1,0:T(8,128)(2,1)S(1)} %copy-done.11), channel_id=1, source_target_pairs={{0,2},{1,3},{2,6},{3,7},{4,0},{5,1},{6,4},{7,5},{8,10},{9,11},{10,... | collective-permute-start | bytes 786440 | tf_op jit(solution)/shard_map/ppermute | solution.py:77
  18.4 14.4 %collective-permute-start.12 = (bf16[512,256]{1,0:T(8,128)(2,1)S(1)}, bf16[512,256]{1,0:T(8,128)(2,1)S(1)}, u32[]{:S(2)}, u32[]{:S(2)}) collective-permute-start(bf16[512,256]{1,0:T(8,128)(2,1)S(1)} %copy-done.11), channel_id=1, source_target_pairs={{0,0},{1,1},{2,4},{3,5},{4,2},{5,3},{6,6},{7,7},{8,8},{9,9},{10,12... | collective-permute-start | bytes 786440 | tf_op jit(solution)/shard_map/ppermute | solution.py:77
  19.1 7.0 %collective-permute-start.11 = (bf16[2,32,768]{2,1,0:T(8,128)(2,1)S(1)}, bf16[2,32,768]{2,1,0:T(8,128)(2,1)S(1)}, u32[]{:S(2)}, u32[]{:S(2)}) collective-permute-start(bf16[2,32,768]{2,1,0:T(8,128)(2,1)S(1)} %add_qkv.1.refs_0_), channel_id=1, source_target_pairs={{0,24},{1,25},{2,26},{3,27},{4,28},{5,29},{6,30},{7,31},{8,16},{9,... | collective-permute-start | bytes 294920 | tf_op jit(solution)/shard_map/ppermute | solution.py:62
  22.7 7.4 %collective-permute-start.10 = (bf16[2,32,768]{2,1,0:T(8,128)(2,1)S(1)}, bf16[2,32,768]{2,1,0:T(8,128)(2,1)S(1)}, u32[]{:S(2)}, u32[]{:S(2)}) collective-permute-start(bf16[2,32,768]{2,1,0:T(8,128)(2,1)S(1)} %add_qkv.1.refs_0_), channel_id=1, source_target_pairs={{0,16},{1,17},{2,18},{3,19},{4,20},{5,21},{6,22},{7,23},{8,24},{9,... | collective-permute-start | bytes 294920 | tf_op jit(solution)/shard_map/ppermute | solution.py:62
  22.7 7.4 %collective-permute-start.9 = (bf16[2,32,768]{2,1,0:T(8,128)(2,1)S(1)}, bf16[2,32,768]{2,1,0:T(8,128)(2,1)S(1)}, u32[]{:S(2)}, u32[]{:S(2)}) collective-permute-start(bf16[2,32,768]{2,1,0:T(8,128)(2,1)S(1)} %add_qkv.1.refs_0_), channel_id=1, source_target_pairs={{0,8},{1,9},{2,10},{3,11},{4,12},{5,13},{6,14},{7,15},{8,0},{9,1},... | collective-permute-start | bytes 294920 | tf_op jit(solution)/shard_map/ppermute | solution.py:62
  32.7 7.1 %collective-permute-start.15 = (bf16[512,256]{1,0:T(8,128)(2,1)S(1)}, bf16[512,256]{1,0:T(8,128)(2,1)S(1)}, u32[]{:S(2)}, u32[]{:S(2)}) collective-permute-start(bf16[512,256]{1,0:T(8,128)(2,1)S(1)} %collective-permute-done.12.refs_4_), channel_id=1, source_target_pairs={{0,1},{1,0},{2,3},{3,2},{4,5},{5,4},{6,7},{7,6},{8,9},{9,8},{10,11... | collective-permute-start | bytes 786440 | tf_op jit(solution)/shard_map/ppermute | solution.py:62
  32.8 7.0 %collective-permute-start.16 = (bf16[512,256]{1,0:T(8,128)(2,1)S(1)}, bf16[512,256]{1,0:T(8,128)(2,1)S(1)}, u32[]{:S(2)}, u32[]{:S(2)}) collective-permute-start(bf16[512,256]{1,0:T(8,128)(2,1)S(1)} %collective-permute-done.13.refs_6_), channel_id=1, source_target_pairs={{0,1},{1,0},{2,3},{3,2},{4,5},{5,4},{6,7},{7,6},{8,9},{9,8},{10,11... | collective-permute-start | bytes 786440 | tf_op jit(solution)/shard_map/ppermute | solution.py:62
  33.3 6.3 %collective-permute-start.14 = (bf16[32,1152]{1,0:T(8,128)(2,1)S(1)}, bf16[32,1152]{1,0:T(8,128)(2,1)S(1)}, u32[]{:S(2)}, u32[]{:S(2)}) collective-permute-start(bf16[32,1152]{1,0:T(8,128)(2,1)S(1)} %get-tuple-element.71), channel_id=1, source_target_pairs={{0,4},{1,5},{2,6},{3,7},{4,0},{5,1},{6,2},{7,3},{8,12},{9,13},{10,... | collective-permute-start | bytes 221192 | tf_op jit(solution)/shard_map/ppermute | solution.py:62
  39.9 6.5 %collective-permute-start.19 = (bf16[32,1152]{1,0:T(8,128)(2,1)S(1)}, bf16[32,1152]{1,0:T(8,128)(2,1)S(1)}, u32[]{:S(2)}, u32[]{:S(2)}) collective-permute-start(bf16[32,1152]{1,0:T(8,128)(2,1)S(1)} %merge_x.1.refs_0_), channel_id=1, source_target_pairs={{0,24},{1,25},{2,26},{3,27},{4,28},{5,29},{6,30},{7,31},{8,16},{9,... | collective-permute-start | bytes 221192 | tf_op jit(solution)/shard_map/ppermute | solution.py:62
  42.2 6.8 %collective-permute-start.18 = (bf16[32,1152]{1,0:T(8,128)(2,1)S(1)}, bf16[32,1152]{1,0:T(8,128)(2,1)S(1)}, u32[]{:S(2)}, u32[]{:S(2)}) collective-permute-start(bf16[32,1152]{1,0:T(8,128)(2,1)S(1)} %merge_x.1.refs_0_), channel_id=1, source_target_pairs={{0,16},{1,17},{2,18},{3,19},{4,20},{5,21},{6,22},{7,23},{8,24},{9,... | collective-permute-start | bytes 221192 | tf_op jit(solution)/shard_map/ppermute | solution.py:62
  42.2 6.8 %collective-permute-start.17 = (bf16[32,1152]{1,0:T(8,128)(2,1)S(1)}, bf16[32,1152]{1,0:T(8,128)(2,1)S(1)}, u32[]{:S(2)}, u32[]{:S(2)}) collective-permute-start(bf16[32,1152]{1,0:T(8,128)(2,1)S(1)} %merge_x.1.refs_0_), channel_id=1, source_target_pairs={{0,8},{1,9},{2,10},{3,11},{4,12},{5,13},{6,14},{7,15},{8,0},{9,1},... | collective-permute-start | bytes 221192 | tf_op jit(solution)/shard_map/ppermute | solution.py:62
  49.6 5.0 %collective-permute-start.22 = (bf16[2,32,256]{2,1,0:T(8,128)(2,1)S(1)}, bf16[2,32,256]{2,1,0:T(8,128)(2,1)S(1)}, u32[]{:S(2)}, u32[]{:S(2)}) collective-permute-start(bf16[2,32,256]{2,1,0:T(8,128)(2,1)S(1)} %out.1.refs_0_), channel_id=1, source_target_pairs={{0,6},{1,7},{2,4},{3,5},{4,2},{5,3},{6,0},{7,1},{8,14},{9,15},{10,... | collective-permute-start | bytes 98312 | tf_op jit(solution)/shard_map/ppermute | solution.py:62
  50.8 3.9 %collective-permute-start.21 = (bf16[2,32,256]{2,1,0:T(8,128)(2,1)S(1)}, bf16[2,32,256]{2,1,0:T(8,128)(2,1)S(1)}, u32[]{:S(2)}, u32[]{:S(2)}) collective-permute-start(bf16[2,32,256]{2,1,0:T(8,128)(2,1)S(1)} %out.1.refs_0_), channel_id=1, source_target_pairs={{0,4},{1,5},{2,6},{3,7},{4,0},{5,1},{6,2},{7,3},{8,12},{9,13},{10,... | collective-permute-start | bytes 98312 | tf_op jit(solution)/shard_map/ppermute | solution.py:62
  56.1 6.1 %collective-permute-start.25 = (bf16[2,2,32,256]{3,2,1,0:T(8,128)(2,1)S(1)}, bf16[2,2,32,256]{3,2,1,0:T(8,128)(2,1)S(1)}, u32[]{:S(2)}, u32[]{:S(2)}) collective-permute-start(bf16[2,2,32,256]{3,2,1,0:T(8,128)(2,1)S(1)} %add_out.1.refs_2_), channel_id=1, source_target_pairs={{0,24},{1,25},{2,26},{3,27},{4,28},{5,29},{6,30},{7,31},{8,16},{9,... | collective-permute-start | bytes 196616 | tf_op jit(solution)/shard_map/ppermute | solution.py:62
  57.9 5.7 %collective-permute-start.24 = (bf16[2,2,32,256]{3,2,1,0:T(8,128)(2,1)S(1)}, bf16[2,2,32,256]{3,2,1,0:T(8,128)(2,1)S(1)}, u32[]{:S(2)}, u32[]{:S(2)}) collective-permute-start(bf16[2,2,32,256]{3,2,1,0:T(8,128)(2,1)S(1)} %add_out.1.refs_2_), channel_id=1, source_target_pairs={{0,16},{1,17},{2,18},{3,19},{4,20},{5,21},{6,22},{7,23},{8,24},{9,... | collective-permute-start | bytes 196616 | tf_op jit(solution)/shard_map/ppermute | solution.py:62
  57.9 5.7 %collective-permute-start.23 = (bf16[2,2,32,256]{3,2,1,0:T(8,128)(2,1)S(1)}, bf16[2,2,32,256]{3,2,1,0:T(8,128)(2,1)S(1)}, u32[]{:S(2)}, u32[]{:S(2)}) collective-permute-start(bf16[2,2,32,256]{3,2,1,0:T(8,128)(2,1)S(1)} %add_out.1.refs_2_), channel_id=1, source_target_pairs={{0,8},{1,9},{2,10},{3,11},{4,12},{5,13},{6,14},{7,15},{8,0},{9,1},... | collective-permute-start | bytes 196616 | tf_op jit(solution)/shard_map/ppermute | solution.py:62
  64.5 5.0 %collective-permute-start.26 = (bf16[64,1024]{1,0:T(8,128)(2,1)S(1)}, bf16[64,1024]{1,0:T(8,128)(2,1)S(1)}, u32[]{:S(2)}, u32[]{:S(2)}) collective-permute-start(bf16[64,1024]{1,0:T(8,128)(2,1)S(1)} %get-tuple-element.80.refs_0_), channel_id=1, source_target_pairs={{0,2},{1,3},{2,0},{3,1},{4,6},{5,7},{6,4},{7,5},{8,10},{9,11},{10,... | collective-permute-start | bytes 393224 | tf_op jit(solution)/shard_map/ppermute | solution.py:62
  70.0 4.3 %collective-permute-start.27 = (bf16[64,512]{1,0:T(8,128)(2,1)S(1)}, bf16[64,512]{1,0:T(8,128)(2,1)S(1)}, u32[]{:S(2)}, u32[]{:S(2)}) collective-permute-start(bf16[64,512]{1,0:T(8,128)(2,1)S(1)} %get-tuple-element.83), channel_id=1, source_target_pairs={{0,4},{1,5},{2,6},{3,7},{4,0},{5,1},{6,2},{7,3},{8,12},{9,13},{10,... | collective-permute-start | bytes 196616 | tf_op jit(solution)/shard_map/ppermute | solution.py:62
  74.4 6.1 %collective-permute-start.30 = (bf16[64,512]{1,0:T(8,128)(2,1)S(1)}, bf16[64,512]{1,0:T(8,128)(2,1)S(1)}, u32[]{:S(2)}, u32[]{:S(2)}) collective-permute-start(bf16[64,512]{1,0:T(8,128)(2,1)S(1)} %add_x.1.refs_0_), channel_id=1, source_target_pairs={{0,24},{1,25},{2,26},{3,27},{4,28},{5,29},{6,30},{7,31},{8,16},{9,... | collective-permute-start | bytes 196616 | tf_op jit(solution)/shard_map/ppermute | solution.py:62
  76.2 5.8 %collective-permute-start.29 = (bf16[64,512]{1,0:T(8,128)(2,1)S(1)}, bf16[64,512]{1,0:T(8,128)(2,1)S(1)}, u32[]{:S(2)}, u32[]{:S(2)}) collective-permute-start(bf16[64,512]{1,0:T(8,128)(2,1)S(1)} %add_x.1.refs_0_), channel_id=1, source_target_pairs={{0,16},{1,17},{2,18},{3,19},{4,20},{5,21},{6,22},{7,23},{8,24},{9,... | collective-permute-start | bytes 196616 | tf_op jit(solution)/shard_map/ppermute | solution.py:62
  77.1 5.0 %collective-permute-start.28 = (bf16[64,512]{1,0:T(8,128)(2,1)S(1)}, bf16[64,512]{1,0:T(8,128)(2,1)S(1)}, u32[]{:S(2)}, u32[]{:S(2)}) collective-permute-start(bf16[64,512]{1,0:T(8,128)(2,1)S(1)} %add_x.1.refs_0_), channel_id=1, source_target_pairs={{0,8},{1,9},{2,10},{3,11},{4,12},{5,13},{6,14},{7,15},{8,0},{9,1},... | collective-permute-start | bytes 196616 | tf_op jit(solution)/shard_map/ppermute | solution.py:62
  82.1 4.0 %collective-permute-start.32 = (bf16[32,512]{1,0:T(8,128)(2,1)S(1)}, bf16[32,512]{1,0:T(8,128)(2,1)S(1)}, u32[]{:S(2)}, u32[]{:S(2)}) collective-permute-start(bf16[32,512]{1,0:T(8,128)(2,1)S(1)} %get-tuple-element.84.refs_0_), channel_id=1, source_target_pairs={{0,4},{1,5},{2,6},{3,7},{4,0},{5,1},{6,2},{7,3},{8,12},{9,13},{10,... | collective-permute-start | bytes 98312 | tf_op jit(solution)/shard_map/ppermute | solution.py:62
  82.9 4.8 %collective-permute-start.33 = (bf16[32,512]{1,0:T(8,128)(2,1)S(1)}, bf16[32,512]{1,0:T(8,128)(2,1)S(1)}, u32[]{:S(2)}, u32[]{:S(2)}) collective-permute-start(bf16[32,512]{1,0:T(8,128)(2,1)S(1)} %get-tuple-element.85), channel_id=1, source_target_pairs={{0,6},{1,7},{2,4},{3,5},{4,2},{5,3},{6,0},{7,1},{8,14},{9,15},{10,... | collective-permute-start | bytes 98312 | tf_op jit(solution)/shard_map/ppermute | solution.py:62
  (14 other events, 278.8 us)

commit v16 on v14

--- a/solution.py
+++ b/solution.py
@@ -390,7 +390,7 @@
     depth = weights[0].shape[0]
     core = place.core()
     for k in range(nx):
-        block = lax.rem(place.y() + k, nx)
+        block = lax.rem(place.y() + nx - 1 - k, nx)
         total[block] = dot(attn[:, at(core, depth)], weights[2 * k][...]) + dot(
             attn[:, at(1 - core, depth)], weights[2 * k + 1][...]
         )
@@ -565,7 +565,7 @@
         (qkv, w_up_sibling, w_down_sibling, w_out)
     )
     pieces = place.gather_z(qkv)
-    blocks = [place.transpose(tied, k) for k in range(nx)]
+    blocks = [place.transpose(tied, nx - 1 - k) for k in range(nx)]
     pack = max(1, min(group, 256 // slots))
     window = min(32, slots)
     new_keys, new_values, *messages = call(

time: 89.6 us -> 89.8 us (level)
  starting transfers between devices: 40.3 us -> 41.7 us
  waiting for transfers between devices: 35.2 us -> 34 us
    ppermute x2, starting transfers between devices: 1.85 us -> 4.91 us  [transpose(): return lax.ppermute(value, ('seq', 'req'), pairs)]
    ppermute x32, starting transfers between devices: 38.4 us -> 36.7 us  [move(): return lax.ppermute(value, ('seq', 'req'), pairs)]
    ppermute x32, waiting for transfers between devices: 35.2 us -> 34 us  [move(): return lax.ppermute(value, ('seq', 'req'), pairs)]
where the time goes in v16:
time: 89.8 us; the launch traced here: 89.6 us
  starting transfers between devices  41.7 us (46%)
  waiting for transfers between devices  34 us (38%)
  Pallas kernels  10.7 us (12%)
  other arithmetic  1.44 us (2%)
  local copies, waits for them, and re-layouts  0.97 us (1%)
  between operations  0.93 us (1%)
    ppermute x32, starting transfers between devices, move(): return lax.ppermute(value, ('seq', 'req'), pairs)  36.7 us
    ppermute x32, waiting for transfers between devices, move(): return lax.ppermute(value, ('seq', 'req'), pairs)  34 us
    pallas_call x13, Pallas kernels, call(): pl.pallas_call(kernel, name=name, out_shape=outs, in_specs=in_specs or [V...  10.7 us
    ppermute x2, starting transfers between devices, transpose(): return lax.ppermute(value, ('seq', 'req'), pairs)  4.91 us
  transfers between devices with their start and end apart: 34, of which 20 were waited for; matrix products, arithmetic and copies ran while one was open for 2% of the time, Pallas kernels for 8%

profile of v16, /device:TPU:0, one launch (start us, length us, event | category | flops | bytes accessed | tf_op | source)
XLA Modules:
  0.0 89.6 jit_solution(5705513296553782616)
XLA Ops:
  1.7 2.6 %collective-permute-start = (bf16[8,4,2048]{2,1,0:T(4,128)(2,1)}, bf16[8,4,2048]{2,1,0:T(4,128)(2,1)S(1)}, u32[]{:S(2)}, u32[]{:S(2)}) collective-permute-start(bf16[8,4,2048]{2,1,0:T(4,128)(2,1)} %refs_0_.3), channel_id=1, source_target_pairs={{0,2},{1,3},{2,0},{3,1},{4,6},{5,7},{6,4},{7,5},{8,10},{9,11},{10,... | collective-permute-start | bytes 393224 | tf_op jit(solution)/shard_map/ppermute | solution.py:62
  9.8 1.7 %collective-permute-start.5 = (bf16[32,768]{1,0:T(8,128)(2,1)S(1)}, bf16[32,768]{1,0:T(8,128)(2,1)S(1)}, u32[]{:S(2)}, u32[]{:S(2)}) collective-permute-start(bf16[32,768]{1,0:T(8,128)(2,1)S(1)} %get-tuple-element.53.refs_0_), channel_id=1, source_target_pairs={{0,4},{1,5},{2,6},{3,7},{4,0},{5,1},{6,2},{7,3},{8,12},{9,13},{10,... | collective-permute-start | bytes 147464 | tf_op jit(solution)/shard_map/ppermute | solution.py:62
  11.5 1.5 %collective-permute-start.6 = (bf16[32,768]{1,0:T(8,128)(2,1)S(1)}, bf16[32,768]{1,0:T(8,128)(2,1)S(1)}, u32[]{:S(2)}, u32[]{:S(2)}) collective-permute-start(bf16[32,768]{1,0:T(8,128)(2,1)S(1)} %get-tuple-element.54), channel_id=1, source_target_pairs={{0,6},{1,7},{2,4},{3,5},{4,2},{5,3},{6,0},{7,1},{8,14},{9,15},{10,... | collective-permute-start | bytes 147464 | tf_op jit(solution)/shard_map/ppermute | solution.py:62
  13.3 3.2 %caches.1 = (bf16[8,64,2048]{2,1,0:T(8,128)(2,1)}, bf16[8,64,2048]{2,1,0:T(8,128)(2,1)}, bf16[8,64,2048]{2,1,0:T(8,128)(2,1)S(1)}, bf16[8,64,2048]{2,1,0:T(8,128)(2,1)S(1)}, f32[8,128]{1,0:T(8,128)S(1)}) custom-call(bf16[8,64,2048]{2,1,0:T(8,128)(2,1)S(1)} %copy-done, bf16[8,64,2048]{2,1,0:T(8,128)(2,1)} %values_in), custom_call_target="tpu_custom_call" | custom-call | bytes 16777216 | tf_op jit(solution)/shard_map/caches/pallas_call | solution.py:104
  17.9 4.2 %collective-permute-start.12 = (bf16[512,256]{1,0:T(8,128)(2,1)S(1)}, bf16[512,256]{1,0:T(8,128)(2,1)S(1)}, u32[]{:S(2)}, u32[]{:S(2)}) collective-permute-start(bf16[512,256]{1,0:T(8,128)(2,1)S(1)} %copy-done.11), channel_id=1, source_target_pairs={{0,2},{1,3},{2,6},{3,7},{4,0},{5,1},{6,4},{7,5},{8,10},{9,11},{10,... | collective-permute-start | bytes 786440 | tf_op jit(solution)/shard_map/ppermute | solution.py:77
  22.1 3.6 %collective-permute-start.11 = (bf16[2,32,768]{2,1,0:T(8,128)(2,1)S(1)}, bf16[2,32,768]{2,1,0:T(8,128)(2,1)S(1)}, u32[]{:S(2)}, u32[]{:S(2)}) collective-permute-start(bf16[2,32,768]{2,1,0:T(8,128)(2,1)S(1)} %add_qkv.1.refs_0_), channel_id=1, source_target_pairs={{0,24},{1,25},{2,26},{3,27},{4,28},{5,29},{6,30},{7,31},{8,16},{9,... | collective-permute-start | bytes 294920 | tf_op jit(solution)/shard_map/ppermute | solution.py:62
  26.5 2.1 %collective-permute-done.11.refs_3_ = bf16[2,32,768]{2,1,0:T(8,128)(2,1)S(1)} collective-permute-done((bf16[2,32,768]{2,1,0:T(8,128)(2,1)S(1)}, bf16[2,32,768]{2,1,0:T(8,128)(2,1)S(1)}, u32[]{:S(2)}, u32[]{:S(2)}) %collective-permute-start.11) | collective-permute-done | bytes 98336 | tf_op jit(solution)/shard_map/ppermute | solution.py:62
  28.6 4.0 %collective-permute-done.10.refs_2_ = bf16[2,32,768]{2,1,0:T(8,128)(2,1)S(1)} collective-permute-done((bf16[2,32,768]{2,1,0:T(8,128)(2,1)S(1)}, bf16[2,32,768]{2,1,0:T(8,128)(2,1)S(1)}, u32[]{:S(2)}, u32[]{:S(2)}) %collective-permute-start.10) | collective-permute-done | bytes 98336 | tf_op jit(solution)/shard_map/ppermute | solution.py:62
  32.6 2.7 %attention.1 = (bf16[8,64,2048]{2,1,0:T(8,128)(2,1)}, bf16[8,64,2048]{2,1,0:T(8,128)(2,1)}, bf16[32,1152]{1,0:T(8,128)(2,1)S(1)}, bf16[32,1152]{1,0:T(8,128)(2,1)S(1)}) custom-call(bf16[2,32,768]{2,1,0:T(8,128)(2,1)S(1)} %add_qkv.1.refs_0_, bf16[2,32,768]{2,1,0:T(8,128)(2,1)S(1)} %collective-permute-done.9.refs_1_, ...), custom_call_target="tpu_custom_call", output_to_operand_aliasing={{0}: (7, {}), {1}: (8, {})} | custom-call | bytes 1048576 | tf_op jit(solution)/shard_map/attention/pallas_call | solution.py:104
  35.9 4.3 %collective-permute-done.14.refs_1_ = bf16[32,1152]{1,0:T(8,128)(2,1)S(1)} collective-permute-done((bf16[32,1152]{1,0:T(8,128)(2,1)S(1)}, bf16[32,1152]{1,0:T(8,128)(2,1)S(1)}, u32[]{:S(2)}, u32[]{:S(2)}) %collective-permute-start.14) | collective-permute-done | bytes 73760 | tf_op jit(solution)/shard_map/ppermute | solution.py:62
  40.6 2.0 %collective-permute-start.19 = (bf16[32,1152]{1,0:T(8,128)(2,1)S(1)}, bf16[32,1152]{1,0:T(8,128)(2,1)S(1)}, u32[]{:S(2)}, u32[]{:S(2)}) collective-permute-start(bf16[32,1152]{1,0:T(8,128)(2,1)S(1)} %merge_x.1.refs_0_), channel_id=1, source_target_pairs={{0,24},{1,25},{2,26},{3,27},{4,28},{5,29},{6,30},{7,31},{8,16},{9,... | collective-permute-start | bytes 221192 | tf_op jit(solution)/shard_map/ppermute | solution.py:62
  42.5 2.5 %collective-permute-start.17 = (bf16[32,1152]{1,0:T(8,128)(2,1)S(1)}, bf16[32,1152]{1,0:T(8,128)(2,1)S(1)}, u32[]{:S(2)}, u32[]{:S(2)}) collective-permute-start(bf16[32,1152]{1,0:T(8,128)(2,1)S(1)} %merge_x.1.refs_0_), channel_id=1, source_target_pairs={{0,8},{1,9},{2,10},{3,11},{4,12},{5,13},{6,14},{7,15},{8,0},{9,1},... | collective-permute-start | bytes 221192 | tf_op jit(solution)/shard_map/ppermute | solution.py:62
  45.0 2.5 %collective-permute-done.19.refs_3_ = bf16[32,1152]{1,0:T(8,128)(2,1)S(1)} collective-permute-done((bf16[32,1152]{1,0:T(8,128)(2,1)S(1)}, bf16[32,1152]{1,0:T(8,128)(2,1)S(1)}, u32[]{:S(2)}, u32[]{:S(2)}) %collective-permute-start.19) | collective-permute-done | bytes 73760 | tf_op jit(solution)/shard_map/ppermute | solution.py:62
  47.5 1.8 %collective-permute-done.18.refs_2_ = bf16[32,1152]{1,0:T(8,128)(2,1)S(1)} collective-permute-done((bf16[32,1152]{1,0:T(8,128)(2,1)S(1)}, bf16[32,1152]{1,0:T(8,128)(2,1)S(1)}, u32[]{:S(2)}, u32[]{:S(2)}) %collective-permute-start.18) | collective-permute-done | bytes 73760 | tf_op jit(solution)/shard_map/ppermute | solution.py:62
  49.9 1.5 %collective-permute-start.22 = (bf16[2,32,256]{2,1,0:T(8,128)(2,1)S(1)}, bf16[2,32,256]{2,1,0:T(8,128)(2,1)S(1)}, u32[]{:S(2)}, u32[]{:S(2)}) collective-permute-start(bf16[2,32,256]{2,1,0:T(8,128)(2,1)S(1)} %out.1.refs_0_), channel_id=1, source_target_pairs={{0,6},{1,7},{2,4},{3,5},{4,2},{5,3},{6,0},{7,1},{8,14},{9,15},{10,... | collective-permute-start | bytes 98312 | tf_op jit(solution)/shard_map/ppermute | solution.py:62
  51.6 1.8 %collective-permute-start.20 = (bf16[2,32,256]{2,1,0:T(8,128)(2,1)S(1)}, bf16[2,32,256]{2,1,0:T(8,128)(2,1)S(1)}, u32[]{:S(2)}, u32[]{:S(2)}) collective-permute-start(bf16[2,32,256]{2,1,0:T(8,128)(2,1)S(1)} %out.1.refs_0_), channel_id=1, source_target_pairs={{0,2},{1,3},{2,0},{3,1},{4,6},{5,7},{6,4},{7,5},{8,10},{9,11},{10,... | collective-permute-start | bytes 98312 | tf_op jit(solution)/shard_map/ppermute | solution.py:62
  53.4 1.3 %collective-permute-done.22.refs_3_ = bf16[2,32,256]{2,1,0:T(8,128)(2,1)S(1)} collective-permute-done((bf16[2,32,256]{2,1,0:T(8,128)(2,1)S(1)}, bf16[2,32,256]{2,1,0:T(8,128)(2,1)S(1)}, u32[]{:S(2)}, u32[]{:S(2)}) %collective-permute-start.22) | collective-permute-done | bytes 32800 | tf_op jit(solution)/shard_map/ppermute | solution.py:62
  55.6 2.3 %collective-permute-start.25 = (bf16[2,2,32,256]{3,2,1,0:T(8,128)(2,1)S(1)}, bf16[2,2,32,256]{3,2,1,0:T(8,128)(2,1)S(1)}, u32[]{:S(2)}, u32[]{:S(2)}) collective-permute-start(bf16[2,2,32,256]{3,2,1,0:T(8,128)(2,1)S(1)} %add_out.1.refs_2_), channel_id=1, source_target_pairs={{0,24},{1,25},{2,26},{3,27},{4,28},{5,29},{6,30},{7,31},{8,16},{9,... | collective-permute-start | bytes 196616 | tf_op jit(solution)/shard_map/ppermute | solution.py:62
  57.9 2.1 %collective-permute-start.23 = (bf16[2,2,32,256]{3,2,1,0:T(8,128)(2,1)S(1)}, bf16[2,2,32,256]{3,2,1,0:T(8,128)(2,1)S(1)}, u32[]{:S(2)}, u32[]{:S(2)}) collective-permute-start(bf16[2,2,32,256]{3,2,1,0:T(8,128)(2,1)S(1)} %add_out.1.refs_2_), channel_id=1, source_target_pairs={{0,8},{1,9},{2,10},{3,11},{4,12},{5,13},{6,14},{7,15},{8,0},{9,1},... | collective-permute-start | bytes 196616 | tf_op jit(solution)/shard_map/ppermute | solution.py:62
  60.0 1.7 %collective-permute-done.25.refs_5_ = bf16[2,2,32,256]{3,2,1,0:T(8,128)(2,1)S(1)} collective-permute-done((bf16[2,2,32,256]{3,2,1,0:T(8,128)(2,1)S(1)}, bf16[2,2,32,256]{3,2,1,0:T(8,128)(2,1)S(1)}, u32[]{:S(2)}, u32[]{:S(2)}) %collective-permute-start.25) | collective-permute-done | bytes 65568 | tf_op jit(solution)/shard_map/ppermute | solution.py:62
  61.7 1.4 %collective-permute-done.24.refs_4_ = bf16[2,2,32,256]{3,2,1,0:T(8,128)(2,1)S(1)} collective-permute-done((bf16[2,2,32,256]{3,2,1,0:T(8,128)(2,1)S(1)}, bf16[2,2,32,256]{3,2,1,0:T(8,128)(2,1)S(1)}, u32[]{:S(2)}, u32[]{:S(2)}) %collective-permute-start.24) | collective-permute-done | bytes 65568 | tf_op jit(solution)/shard_map/ppermute | solution.py:62
  64.0 1.8 %collective-permute-start.26 = (bf16[64,1024]{1,0:T(8,128)(2,1)S(1)}, bf16[64,1024]{1,0:T(8,128)(2,1)S(1)}, u32[]{:S(2)}, u32[]{:S(2)}) collective-permute-start(bf16[64,1024]{1,0:T(8,128)(2,1)S(1)} %get-tuple-element.78.refs_0_), channel_id=1, source_target_pairs={{0,2},{1,3},{2,0},{3,1},{4,6},{5,7},{6,4},{7,5},{8,10},{9,11},{10,... | collective-permute-start | bytes 393224 | tf_op jit(solution)/shard_map/ppermute | solution.py:62
  65.9 3.2 %collective-permute-done.26.refs_1_ = bf16[64,1024]{1,0:T(8,128)(2,1)S(1)} collective-permute-done((bf16[64,1024]{1,0:T(8,128)(2,1)S(1)}, bf16[64,1024]{1,0:T(8,128)(2,1)S(1)}, u32[]{:S(2)}, u32[]{:S(2)}) %collective-permute-start.26) | collective-permute-done | bytes 131104 | tf_op jit(solution)/shard_map/ppermute | solution.py:62
  69.6 1.8 %collective-permute-start.27 = (bf16[64,512]{1,0:T(8,128)(2,1)S(1)}, bf16[64,512]{1,0:T(8,128)(2,1)S(1)}, u32[]{:S(2)}, u32[]{:S(2)}) collective-permute-start(bf16[64,512]{1,0:T(8,128)(2,1)S(1)} %get-tuple-element.81), channel_id=1, source_target_pairs={{0,4},{1,5},{2,6},{3,7},{4,0},{5,1},{6,2},{7,3},{8,12},{9,13},{10,... | collective-permute-start | bytes 196616 | tf_op jit(solution)/shard_map/ppermute | solution.py:62
  71.4 2.5 %collective-permute-done.27.refs_1_ = bf16[64,512]{1,0:T(8,128)(2,1)S(1)} collective-permute-done((bf16[64,512]{1,0:T(8,128)(2,1)S(1)}, bf16[64,512]{1,0:T(8,128)(2,1)S(1)}, u32[]{:S(2)}, u32[]{:S(2)}) %collective-permute-start.27) | collective-permute-done | bytes 65568 | tf_op jit(solution)/shard_map/ppermute | solution.py:62
  73.9 2.3 %collective-permute-start.30 = (bf16[64,512]{1,0:T(8,128)(2,1)S(1)}, bf16[64,512]{1,0:T(8,128)(2,1)S(1)}, u32[]{:S(2)}, u32[]{:S(2)}) collective-permute-start(bf16[64,512]{1,0:T(8,128)(2,1)S(1)} %add_x.1.refs_0_), channel_id=1, source_target_pairs={{0,24},{1,25},{2,26},{3,27},{4,28},{5,29},{6,30},{7,31},{8,16},{9,... | collective-permute-start | bytes 196616 | tf_op jit(solution)/shard_map/ppermute | solution.py:62
  76.6 1.8 %collective-permute-start.28 = (bf16[64,512]{1,0:T(8,128)(2,1)S(1)}, bf16[64,512]{1,0:T(8,128)(2,1)S(1)}, u32[]{:S(2)}, u32[]{:S(2)}) collective-permute-start(bf16[64,512]{1,0:T(8,128)(2,1)S(1)} %add_x.1.refs_0_), channel_id=1, source_target_pairs={{0,8},{1,9},{2,10},{3,11},{4,12},{5,13},{6,14},{7,15},{8,0},{9,1},... | collective-permute-start | bytes 196616 | tf_op jit(solution)/shard_map/ppermute | solution.py:62
  78.4 1.7 %collective-permute-done.30.refs_3_ = bf16[64,512]{1,0:T(8,128)(2,1)S(1)} collective-permute-done((bf16[64,512]{1,0:T(8,128)(2,1)S(1)}, bf16[64,512]{1,0:T(8,128)(2,1)S(1)}, u32[]{:S(2)}, u32[]{:S(2)}) %collective-permute-start.30) | collective-permute-done | bytes 65568 | tf_op jit(solution)/shard_map/ppermute | solution.py:62
  80.1 1.8 %collective-permute-done.29.refs_2_ = bf16[64,512]{1,0:T(8,128)(2,1)S(1)} collective-permute-done((bf16[64,512]{1,0:T(8,128)(2,1)S(1)}, bf16[64,512]{1,0:T(8,128)(2,1)S(1)}, u32[]{:S(2)}, u32[]{:S(2)}) %collective-permute-start.29) | collective-permute-done | bytes 65568 | tf_op jit(solution)/shard_map/ppermute | solution.py:62
  81.9 1.5 %collective-permute-start.32 = (bf16[32,512]{1,0:T(8,128)(2,1)S(1)}, bf16[32,512]{1,0:T(8,128)(2,1)S(1)}, u32[]{:S(2)}, u32[]{:S(2)}) collective-permute-start(bf16[32,512]{1,0:T(8,128)(2,1)S(1)} %get-tuple-element.82.refs_0_), channel_id=1, source_target_pairs={{0,4},{1,5},{2,6},{3,7},{4,0},{5,1},{6,2},{7,3},{8,12},{9,13},{10,... | collective-permute-start | bytes 98312 | tf_op jit(solution)/shard_map/ppermute | solution.py:62
  83.5 1.5 %collective-permute-start.33 = (bf16[32,512]{1,0:T(8,128)(2,1)S(1)}, bf16[32,512]{1,0:T(8,128)(2,1)S(1)}, u32[]{:S(2)}, u32[]{:S(2)}) collective-permute-start(bf16[32,512]{1,0:T(8,128)(2,1)S(1)} %get-tuple-element.83), channel_id=1, source_target_pairs={{0,6},{1,7},{2,4},{3,5},{4,2},{5,3},{6,0},{7,1},{8,14},{9,15},{10,... | collective-permute-start | bytes 98312 | tf_op jit(solution)/shard_map/ppermute | solution.py:62
  85.9 2.4 %collective-permute-done.33.refs_3_ = bf16[32,512]{1,0:T(8,128)(2,1)S(1)} collective-permute-done((bf16[32,512]{1,0:T(8,128)(2,1)S(1)}, bf16[32,512]{1,0:T(8,128)(2,1)S(1)}, u32[]{:S(2)}, u32[]{:S(2)}) %collective-permute-start.33) | collective-permute-done | bytes 32800 | tf_op jit(solution)/shard_map/ppermute | solution.py:62
  (76 shorter events, 15.6 us)
Async XLA Ops:
  0.6 7.9 %collective-permute-start.1 = (bf16[512,256]{1,0:T(8,128)(2,1)}, bf16[512,256]{1,0:T(8,128)(2,1)S(1)}, u32[]{:S(2)}, u32[]{:S(2)}) collective-permute-start(bf16[512,256]{1,0:T(8,128)(2,1)} %refs_0_.2), channel_id=1, source_target_pairs={{0,1},{1,0},{2,3},{3,2},{4,5},{5,4},{6,7},{7,6},{8,9},{9,8},{10,11... | collective-permute-start | bytes 786440 | tf_op jit(solution)/shard_map/ppermute | solution.py:62
  1.2 7.4 %collective-permute-start.2 = (bf16[512,256]{1,0:T(8,128)(2,1)}, bf16[512,256]{1,0:T(8,128)(2,1)S(1)}, u32[]{:S(2)}, u32[]{:S(2)}) collective-permute-start(bf16[512,256]{1,0:T(8,128)(2,1)} %refs_1_.1), channel_id=1, source_target_pairs={{0,1},{1,0},{2,3},{3,2},{4,5},{5,4},{6,7},{7,6},{8,9},{9,8},{10,11... | collective-permute-start | bytes 786440 | tf_op jit(solution)/shard_map/ppermute | solution.py:62
  1.2 7.3 %collective-permute-start.3 = (bf16[512,256]{1,0:T(8,128)(2,1)}, bf16[512,256]{1,0:T(8,128)(2,1)S(1)}, u32[]{:S(2)}, u32[]{:S(2)}) collective-permute-start(bf16[512,256]{1,0:T(8,128)(2,1)} %refs_2_.2), channel_id=1, source_target_pairs={{0,1},{1,0},{2,3},{3,2},{4,5},{5,4},{6,7},{7,6},{8,9},{9,8},{10,11... | collective-permute-start | bytes 786440 | tf_op jit(solution)/shard_map/ppermute | solution.py:62
  1.7 6.9 %collective-permute-start = (bf16[8,4,2048]{2,1,0:T(4,128)(2,1)}, bf16[8,4,2048]{2,1,0:T(4,128)(2,1)S(1)}, u32[]{:S(2)}, u32[]{:S(2)}) collective-permute-start(bf16[8,4,2048]{2,1,0:T(4,128)(2,1)} %refs_0_.3), channel_id=1, source_target_pairs={{0,2},{1,3},{2,0},{3,1},{4,6},{5,7},{6,4},{7,5},{8,10},{9,11},{10,... | collective-permute-start | bytes 393224 | tf_op jit(solution)/shard_map/ppermute | solution.py:62
  9.2 7.9 %collective-permute-start.7 = (bf16[512,1024]{1,0:T(8,128)(2,1)}, bf16[512,1024]{1,0:T(8,128)(2,1)S(1)}, u32[]{:S(2)}, u32[]{:S(2)}) collective-permute-start(bf16[512,1024]{1,0:T(8,128)(2,1)} %refs_8_.1), channel_id=1, source_target_pairs={{0,1},{1,0},{2,3},{3,2},{4,5},{5,4},{6,7},{7,6},{8,9},{9,8},{10,11... | collective-permute-start | bytes 3145736 | tf_op jit(solution)/shard_map/ppermute | solution.py:62
  9.3 7.9 %collective-permute-start.8 = (bf16[1024,512]{1,0:T(8,128)(2,1)}, bf16[1024,512]{1,0:T(8,128)(2,1)S(1)}, u32[]{:S(2)}, u32[]{:S(2)}) collective-permute-start(bf16[1024,512]{1,0:T(8,128)(2,1)} %refs_2_.3), channel_id=1, source_target_pairs={{0,1},{1,0},{2,3},{3,2},{4,5},{5,4},{6,7},{7,6},{8,9},{9,8},{10,11... | collective-permute-start | bytes 3145736 | tf_op jit(solution)/shard_map/ppermute | solution.py:62
  9.8 6.7 %collective-permute-start.5 = (bf16[32,768]{1,0:T(8,128)(2,1)S(1)}, bf16[32,768]{1,0:T(8,128)(2,1)S(1)}, u32[]{:S(2)}, u32[]{:S(2)}) collective-permute-start(bf16[32,768]{1,0:T(8,128)(2,1)S(1)} %get-tuple-element.53.refs_0_), channel_id=1, source_target_pairs={{0,4},{1,5},{2,6},{3,7},{4,0},{5,1},{6,2},{7,3},{8,12},{9,13},{10,... | collective-permute-start | bytes 147464 | tf_op jit(solution)/shard_map/ppermute | solution.py:62
  11.5 5.0 %collective-permute-start.6 = (bf16[32,768]{1,0:T(8,128)(2,1)S(1)}, bf16[32,768]{1,0:T(8,128)(2,1)S(1)}, u32[]{:S(2)}, u32[]{:S(2)}) collective-permute-start(bf16[32,768]{1,0:T(8,128)(2,1)S(1)} %get-tuple-element.54), channel_id=1, source_target_pairs={{0,6},{1,7},{2,4},{3,5},{4,2},{5,3},{6,0},{7,1},{8,14},{9,15},{10,... | collective-permute-start | bytes 147464 | tf_op jit(solution)/shard_map/ppermute | solution.py:62
  13.0 4.1 %collective-permute-start.4 = (bf16[32,768]{1,0:T(8,128)(2,1)S(1)}, bf16[32,768]{1,0:T(8,128)(2,1)S(1)}, u32[]{:S(2)}, u32[]{:S(2)}) collective-permute-start(bf16[32,768]{1,0:T(8,128)(2,1)S(1)} %get-tuple-element.54), channel_id=1, source_target_pairs={{0,2},{1,3},{2,0},{3,1},{4,6},{5,7},{6,4},{7,5},{8,10},{9,11},{10,... | collective-permute-start | bytes 147464 | tf_op jit(solution)/shard_map/ppermute | solution.py:62
  17.2 18.1 %collective-permute-start.13 = (bf16[512,256]{1,0:T(8,128)(2,1)S(1)}, bf16[512,256]{1,0:T(8,128)(2,1)S(1)}, u32[]{:S(2)}, u32[]{:S(2)}) collective-permute-start(bf16[512,256]{1,0:T(8,128)(2,1)S(1)} %copy-done.11), channel_id=1, source_target_pairs={{0,0},{1,1},{2,4},{3,5},{4,2},{5,3},{6,6},{7,7},{8,8},{9,9},{10,12... | collective-permute-start | bytes 786440 | tf_op jit(solution)/shard_map/ppermute | solution.py:77
  17.9 17.5 %collective-permute-start.12 = (bf16[512,256]{1,0:T(8,128)(2,1)S(1)}, bf16[512,256]{1,0:T(8,128)(2,1)S(1)}, u32[]{:S(2)}, u32[]{:S(2)}) collective-permute-start(bf16[512,256]{1,0:T(8,128)(2,1)S(1)} %copy-done.11), channel_id=1, source_target_pairs={{0,2},{1,3},{2,6},{3,7},{4,0},{5,1},{6,4},{7,5},{8,10},{9,11},{10,... | collective-permute-start | bytes 786440 | tf_op jit(solution)/shard_map/ppermute | solution.py:77
  22.1 6.5 %collective-permute-start.11 = (bf16[2,32,768]{2,1,0:T(8,128)(2,1)S(1)}, bf16[2,32,768]{2,1,0:T(8,128)(2,1)S(1)}, u32[]{:S(2)}, u32[]{:S(2)}) collective-permute-start(bf16[2,32,768]{2,1,0:T(8,128)(2,1)S(1)} %add_qkv.1.refs_0_), channel_id=1, source_target_pairs={{0,24},{1,25},{2,26},{3,27},{4,28},{5,29},{6,30},{7,31},{8,16},{9,... | collective-permute-start | bytes 294920 | tf_op jit(solution)/shard_map/ppermute | solution.py:62
  25.7 6.9 %collective-permute-start.10 = (bf16[2,32,768]{2,1,0:T(8,128)(2,1)S(1)}, bf16[2,32,768]{2,1,0:T(8,128)(2,1)S(1)}, u32[]{:S(2)}, u32[]{:S(2)}) collective-permute-start(bf16[2,32,768]{2,1,0:T(8,128)(2,1)S(1)} %add_qkv.1.refs_0_), channel_id=1, source_target_pairs={{0,16},{1,17},{2,18},{3,19},{4,20},{5,21},{6,22},{7,23},{8,24},{9,... | collective-permute-start | bytes 294920 | tf_op jit(solution)/shard_map/ppermute | solution.py:62
  25.7 6.9 %collective-permute-start.9 = (bf16[2,32,768]{2,1,0:T(8,128)(2,1)S(1)}, bf16[2,32,768]{2,1,0:T(8,128)(2,1)S(1)}, u32[]{:S(2)}, u32[]{:S(2)}) collective-permute-start(bf16[2,32,768]{2,1,0:T(8,128)(2,1)S(1)} %add_qkv.1.refs_0_), channel_id=1, source_target_pairs={{0,8},{1,9},{2,10},{3,11},{4,12},{5,13},{6,14},{7,15},{8,0},{9,1},... | collective-permute-start | bytes 294920 | tf_op jit(solution)/shard_map/ppermute | solution.py:62
  35.3 5.2 %collective-permute-start.15 = (bf16[512,256]{1,0:T(8,128)(2,1)S(1)}, bf16[512,256]{1,0:T(8,128)(2,1)S(1)}, u32[]{:S(2)}, u32[]{:S(2)}) collective-permute-start(bf16[512,256]{1,0:T(8,128)(2,1)S(1)} %collective-permute-done.12.refs_4_), channel_id=1, source_target_pairs={{0,1},{1,0},{2,3},{3,2},{4,5},{5,4},{6,7},{7,6},{8,9},{9,8},{10,11... | collective-permute-start | bytes 786440 | tf_op jit(solution)/shard_map/ppermute | solution.py:62
  35.4 5.1 %collective-permute-start.16 = (bf16[512,256]{1,0:T(8,128)(2,1)S(1)}, bf16[512,256]{1,0:T(8,128)(2,1)S(1)}, u32[]{:S(2)}, u32[]{:S(2)}) collective-permute-start(bf16[512,256]{1,0:T(8,128)(2,1)S(1)} %collective-permute-done.13.refs_6_), channel_id=1, source_target_pairs={{0,1},{1,0},{2,3},{3,2},{4,5},{5,4},{6,7},{7,6},{8,9},{9,8},{10,11... | collective-permute-start | bytes 786440 | tf_op jit(solution)/shard_map/ppermute | solution.py:62
  35.9 4.4 %collective-permute-start.14 = (bf16[32,1152]{1,0:T(8,128)(2,1)S(1)}, bf16[32,1152]{1,0:T(8,128)(2,1)S(1)}, u32[]{:S(2)}, u32[]{:S(2)}) collective-permute-start(bf16[32,1152]{1,0:T(8,128)(2,1)S(1)} %get-tuple-element.69), channel_id=1, source_target_pairs={{0,4},{1,5},{2,6},{3,7},{4,0},{5,1},{6,2},{7,3},{8,12},{9,13},{10,... | collective-permute-start | bytes 221192 | tf_op jit(solution)/shard_map/ppermute | solution.py:62
  40.6 6.9 %collective-permute-start.19 = (bf16[32,1152]{1,0:T(8,128)(2,1)S(1)}, bf16[32,1152]{1,0:T(8,128)(2,1)S(1)}, u32[]{:S(2)}, u32[]{:S(2)}) collective-permute-start(bf16[32,1152]{1,0:T(8,128)(2,1)S(1)} %merge_x.1.refs_0_), channel_id=1, source_target_pairs={{0,24},{1,25},{2,26},{3,27},{4,28},{5,29},{6,30},{7,31},{8,16},{9,... | collective-permute-start | bytes 221192 | tf_op jit(solution)/shard_map/ppermute | solution.py:62
  42.5 6.7 %collective-permute-start.18 = (bf16[32,1152]{1,0:T(8,128)(2,1)S(1)}, bf16[32,1152]{1,0:T(8,128)(2,1)S(1)}, u32[]{:S(2)}, u32[]{:S(2)}) collective-permute-start(bf16[32,1152]{1,0:T(8,128)(2,1)S(1)} %merge_x.1.refs_0_), channel_id=1, source_target_pairs={{0,16},{1,17},{2,18},{3,19},{4,20},{5,21},{6,22},{7,23},{8,24},{9,... | collective-permute-start | bytes 221192 | tf_op jit(solution)/shard_map/ppermute | solution.py:62
  42.5 6.7 %collective-permute-start.17 = (bf16[32,1152]{1,0:T(8,128)(2,1)S(1)}, bf16[32,1152]{1,0:T(8,128)(2,1)S(1)}, u32[]{:S(2)}, u32[]{:S(2)}) collective-permute-start(bf16[32,1152]{1,0:T(8,128)(2,1)S(1)} %merge_x.1.refs_0_), channel_id=1, source_target_pairs={{0,8},{1,9},{2,10},{3,11},{4,12},{5,13},{6,14},{7,15},{8,0},{9,1},... | collective-permute-start | bytes 221192 | tf_op jit(solution)/shard_map/ppermute | solution.py:62
  49.9 4.9 %collective-permute-start.22 = (bf16[2,32,256]{2,1,0:T(8,128)(2,1)S(1)}, bf16[2,32,256]{2,1,0:T(8,128)(2,1)S(1)}, u32[]{:S(2)}, u32[]{:S(2)}) collective-permute-start(bf16[2,32,256]{2,1,0:T(8,128)(2,1)S(1)} %out.1.refs_0_), channel_id=1, source_target_pairs={{0,6},{1,7},{2,4},{3,5},{4,2},{5,3},{6,0},{7,1},{8,14},{9,15},{10,... | collective-permute-start | bytes 98312 | tf_op jit(solution)/shard_map/ppermute | solution.py:62
  51.4 3.9 %collective-permute-start.21 = (bf16[2,32,256]{2,1,0:T(8,128)(2,1)S(1)}, bf16[2,32,256]{2,1,0:T(8,128)(2,1)S(1)}, u32[]{:S(2)}, u32[]{:S(2)}) collective-permute-start(bf16[2,32,256]{2,1,0:T(8,128)(2,1)S(1)} %out.1.refs_0_), channel_id=1, source_target_pairs={{0,4},{1,5},{2,6},{3,7},{4,0},{5,1},{6,2},{7,3},{8,12},{9,13},{10,... | collective-permute-start | bytes 98312 | tf_op jit(solution)/shard_map/ppermute | solution.py:62
  55.6 6.1 %collective-permute-start.25 = (bf16[2,2,32,256]{3,2,1,0:T(8,128)(2,1)S(1)}, bf16[2,2,32,256]{3,2,1,0:T(8,128)(2,1)S(1)}, u32[]{:S(2)}, u32[]{:S(2)}) collective-permute-start(bf16[2,2,32,256]{3,2,1,0:T(8,128)(2,1)S(1)} %add_out.1.refs_2_), channel_id=1, source_target_pairs={{0,24},{1,25},{2,26},{3,27},{4,28},{5,29},{6,30},{7,31},{8,16},{9,... | collective-permute-start | bytes 196616 | tf_op jit(solution)/shard_map/ppermute | solution.py:62
  57.9 5.2 %collective-permute-start.24 = (bf16[2,2,32,256]{3,2,1,0:T(8,128)(2,1)S(1)}, bf16[2,2,32,256]{3,2,1,0:T(8,128)(2,1)S(1)}, u32[]{:S(2)}, u32[]{:S(2)}) collective-permute-start(bf16[2,2,32,256]{3,2,1,0:T(8,128)(2,1)S(1)} %add_out.1.refs_2_), channel_id=1, source_target_pairs={{0,16},{1,17},{2,18},{3,19},{4,20},{5,21},{6,22},{7,23},{8,24},{9,... | collective-permute-start | bytes 196616 | tf_op jit(solution)/shard_map/ppermute | solution.py:62
  57.9 5.2 %collective-permute-start.23 = (bf16[2,2,32,256]{3,2,1,0:T(8,128)(2,1)S(1)}, bf16[2,2,32,256]{3,2,1,0:T(8,128)(2,1)S(1)}, u32[]{:S(2)}, u32[]{:S(2)}) collective-permute-start(bf16[2,2,32,256]{3,2,1,0:T(8,128)(2,1)S(1)} %add_out.1.refs_2_), channel_id=1, source_target_pairs={{0,8},{1,9},{2,10},{3,11},{4,12},{5,13},{6,14},{7,15},{8,0},{9,1},... | collective-permute-start | bytes 196616 | tf_op jit(solution)/shard_map/ppermute | solution.py:62
  64.0 5.0 %collective-permute-start.26 = (bf16[64,1024]{1,0:T(8,128)(2,1)S(1)}, bf16[64,1024]{1,0:T(8,128)(2,1)S(1)}, u32[]{:S(2)}, u32[]{:S(2)}) collective-permute-start(bf16[64,1024]{1,0:T(8,128)(2,1)S(1)} %get-tuple-element.78.refs_0_), channel_id=1, source_target_pairs={{0,2},{1,3},{2,0},{3,1},{4,6},{5,7},{6,4},{7,5},{8,10},{9,11},{10,... | collective-permute-start | bytes 393224 | tf_op jit(solution)/shard_map/ppermute | solution.py:62
  69.6 4.3 %collective-permute-start.27 = (bf16[64,512]{1,0:T(8,128)(2,1)S(1)}, bf16[64,512]{1,0:T(8,128)(2,1)S(1)}, u32[]{:S(2)}, u32[]{:S(2)}) collective-permute-start(bf16[64,512]{1,0:T(8,128)(2,1)S(1)} %get-tuple-element.81), channel_id=1, source_target_pairs={{0,4},{1,5},{2,6},{3,7},{4,0},{5,1},{6,2},{7,3},{8,12},{9,13},{10,... | collective-permute-start | bytes 196616 | tf_op jit(solution)/shard_map/ppermute | solution.py:62
  73.9 6.1 %collective-permute-start.30 = (bf16[64,512]{1,0:T(8,128)(2,1)S(1)}, bf16[64,512]{1,0:T(8,128)(2,1)S(1)}, u32[]{:S(2)}, u32[]{:S(2)}) collective-permute-start(bf16[64,512]{1,0:T(8,128)(2,1)S(1)} %add_x.1.refs_0_), channel_id=1, source_target_pairs={{0,24},{1,25},{2,26},{3,27},{4,28},{5,29},{6,30},{7,31},{8,16},{9,... | collective-permute-start | bytes 196616 | tf_op jit(solution)/shard_map/ppermute | solution.py:62
  76.3 5.6 %collective-permute-start.29 = (bf16[64,512]{1,0:T(8,128)(2,1)S(1)}, bf16[64,512]{1,0:T(8,128)(2,1)S(1)}, u32[]{:S(2)}, u32[]{:S(2)}) collective-permute-start(bf16[64,512]{1,0:T(8,128)(2,1)S(1)} %add_x.1.refs_0_), channel_id=1, source_target_pairs={{0,16},{1,17},{2,18},{3,19},{4,20},{5,21},{6,22},{7,23},{8,24},{9,... | collective-permute-start | bytes 196616 | tf_op jit(solution)/shard_map/ppermute | solution.py:62
  76.6 5.2 %collective-permute-start.28 = (bf16[64,512]{1,0:T(8,128)(2,1)S(1)}, bf16[64,512]{1,0:T(8,128)(2,1)S(1)}, u32[]{:S(2)}, u32[]{:S(2)}) collective-permute-start(bf16[64,512]{1,0:T(8,128)(2,1)S(1)} %add_x.1.refs_0_), channel_id=1, source_target_pairs={{0,8},{1,9},{2,10},{3,11},{4,12},{5,13},{6,14},{7,15},{8,0},{9,1},... | collective-permute-start | bytes 196616 | tf_op jit(solution)/shard_map/ppermute | solution.py:62
  81.9 4.0 %collective-permute-start.32 = (bf16[32,512]{1,0:T(8,128)(2,1)S(1)}, bf16[32,512]{1,0:T(8,128)(2,1)S(1)}, u32[]{:S(2)}, u32[]{:S(2)}) collective-permute-start(bf16[32,512]{1,0:T(8,128)(2,1)S(1)} %get-tuple-element.82.refs_0_), channel_id=1, source_target_pairs={{0,4},{1,5},{2,6},{3,7},{4,0},{5,1},{6,2},{7,3},{8,12},{9,13},{10,... | collective-permute-start | bytes 98312 | tf_op jit(solution)/shard_map/ppermute | solution.py:62
  83.5 4.8 %collective-permute-start.33 = (bf16[32,512]{1,0:T(8,128)(2,1)S(1)}, bf16[32,512]{1,0:T(8,128)(2,1)S(1)}, u32[]{:S(2)}, u32[]{:S(2)}) collective-permute-start(bf16[32,512]{1,0:T(8,128)(2,1)S(1)} %get-tuple-element.83), channel_id=1, source_target_pairs={{0,6},{1,7},{2,4},{3,5},{4,2},{5,3},{6,0},{7,1},{8,14},{9,15},{10,... | collective-permute-start | bytes 98312 | tf_op jit(solution)/shard_map/ppermute | solution.py:62
  (14 other events, 264.9 us)
